TPU v7x, 32 devices: a whole 2x2x4 slice. The times are simulated.
32 devices in a mesh: grp: 2 (over x), seq: 16 (over z, y, core).
Axes of the slice: x: 2, y: 2, z: 4, core: 2. Of those that a mesh axis runs over, the one named last changes fastest.
Arguments:
- activations: bfloat16 [1024, 2, 2048], P('seq', 'grp'), parts along dimension 1, may hold values from -6 to 6
- queries: bfloat16 [1024, 2, 4096], P('seq', 'grp'), parts along dimension 1, may hold values from -160 to 160
- keys: bfloat16 [1024, 2, 256], P('seq', 'grp'), parts along dimension 1, may hold values from -4 to 4
- norm_gain: float32 [2048], replicated, may hold values from 0.5 to 1.5
- value_weight: bfloat16 [2048, 256], P('seq'), may hold values from -0.125 to 0.125
- expert_ids: int32 [1024, 2, 4], P('seq', 'grp'), parts along dimension 1, may hold values from 0 to 15, all different within a row; in each aligned block of 64 rows (0 to 63, 64 to 127, ..., all dimensions but the last counted through in order) at most 24 rows name the same one
- gate_weights: float32 [1024, 2, 4], P('seq', 'grp'), parts along dimension 1, may hold values from 0.05 to 0.5
- w_gate_up: bfloat16 [16, 2048, 1536], P('seq'), may hold values from -0.125 to 0.125
- w_down: bfloat16 [16, 768, 2048], P('seq'), may hold values from -0.21875 to 0.21875
Outputs:
- context: bfloat16 [1024, 2, 4096], P('seq', 'grp'), parts along dimension 1
- layer_out: bfloat16 [1024, 2, 2048], P('seq', 'grp'), parts along dimension 1
There are 2 independent parts, one for each index of `grp`. A program takes and returns all parts, laid end to end along the dimension named above; an argument that names none is the same for every part. Nothing has to cross between parts.
Inputs may be any that keep to these rules, and one draw needn't show every extreme that they name: `expert_ids`: each row names 4 different experts. Of the 64 rows of one device (64 positions of the one sequence), at most 24 name any one expert, a bound that some block reaches of them.
All inputs are finite; a program needn't handle non-finite values.
Results may differ from a plain program's by a relative error of at most 0.006.
Values may be sent and summed in bfloat16 or wider, within the bound.
No kernel may reach another device: no remote copies, remote signals or barrier semaphores. Data moves between devices by JAX's collectives and lax.ppermute only.
A program may use at most 128 MiB of HBM per device.

v0:
```python
import math

import jax
import jax.numpy as jnp
from jax import lax
from jax.sharding import PartitionSpec as P

QUERY_HEADS = 32
KEY_VALUE_HEADS = 2
HEAD_DIMENSION = 128


def normalize(activations, norm_gain):
    features = activations.astype(jnp.float32)
    inverse = lax.rsqrt(jnp.mean(features * features, axis=-1, keepdims=True) + 1e-06)
    return (features * inverse * norm_gain).astype(jnp.bfloat16)


def empty_state(count_of_rows, sequence_count):
    query_group = QUERY_HEADS // KEY_VALUE_HEADS
    return (
        jnp.full(
            (count_of_rows, sequence_count, KEY_VALUE_HEADS, query_group), -1e30, dtype=jnp.float32
        ),
        jnp.zeros((count_of_rows, sequence_count, KEY_VALUE_HEADS, query_group), dtype=jnp.float32),
        jnp.zeros(
            (count_of_rows, sequence_count, KEY_VALUE_HEADS, query_group, HEAD_DIMENSION),
            dtype=jnp.float32,
        ),
    )


def attend(carry_state, grouped_queries, q_start, key_block_size, value_block_size, key_start):
    run_max, run_sum, run_acc = carry_state
    query_count, sequence_count = (grouped_queries.shape[0], grouped_queries.shape[1])
    key_count = key_block_size.shape[0]
    grouped_rows = grouped_queries.reshape(
        query_count, sequence_count, KEY_VALUE_HEADS, QUERY_HEADS // KEY_VALUE_HEADS, HEAD_DIMENSION
    )
    key_head_rows = key_block_size.reshape(
        key_count, sequence_count, KEY_VALUE_HEADS, HEAD_DIMENSION
    )
    value_head_rows = value_block_size.reshape(
        key_count, sequence_count, KEY_VALUE_HEADS, HEAD_DIMENSION
    )
    scores = jnp.einsum(
        "rskgd,pskd->rskgp", grouped_rows, key_head_rows, preferred_element_type=jnp.float32
    ) * (1.0 / math.sqrt(HEAD_DIMENSION))
    query_positions = q_start + jnp.arange(query_count, dtype=jnp.int32)
    key_positions = key_start + jnp.arange(key_count, dtype=jnp.int32)
    visible = (query_positions[:, None] >= key_positions[None, :])[:, None, None, None, :]
    scores = jnp.where(visible, scores, -1e30)
    new_max = jnp.maximum(run_max, jnp.max(scores, axis=-1))
    rescale = jnp.exp(run_max - new_max)
    weights = jnp.where(visible, jnp.exp(scores - new_max[..., None]), 0.0)
    run_sum = run_sum * rescale + jnp.sum(weights, axis=-1)
    added = jnp.einsum(
        "rskgp,pskd->rskgd",
        weights.astype(jnp.bfloat16),
        value_head_rows,
        preferred_element_type=jnp.float32,
    )
    run_acc = run_acc * rescale[..., None] + added
    return (new_max, run_sum, run_acc)


def maybe_attend(current, grouped_queries, q_start, key_block_size, value_block_size, block_start):
    last_query = q_start + grouped_queries.shape[0] - 1
    return lax.cond(
        block_start <= last_query,
        lambda kept: attend(
            kept, grouped_queries, q_start, key_block_size, value_block_size, block_start
        ),
        lambda kept: kept,
        current,
    )


def finish(carry_state):
    run_max, run_sum, run_acc = carry_state
    count_of_rows, sequence_count = (run_acc.shape[0], run_acc.shape[1])
    return (
        (run_acc / run_sum[..., None])
        .reshape(count_of_rows, sequence_count, QUERY_HEADS * HEAD_DIMENSION)
        .astype(jnp.bfloat16)
    )


def per_device(
    activations, queries, keys, norm_gain, value_weight, expert_ids, gate_weights, w_gate_up, w_down
):
    pos_rows, sequence_count, model_width = activations.shape
    tok_rows = pos_rows * sequence_count
    top_count = expert_ids.shape[2]
    local_experts = w_down.shape[0]
    hidden_units = w_down.shape[1]
    devices = lax.axis_size("seq")
    experts = local_experts * devices
    capacity = max(2, 3 * tok_rows * top_count // (2 * experts))
    my_index = lax.axis_index("seq")
    normed = normalize(activations, norm_gain)
    flat_normed = normed.reshape(tok_rows, model_width)
    value_tensor = jnp.dot(
        flat_normed,
        lax.all_gather(value_weight, "seq", axis=0, tiled=True),
        preferred_element_type=jnp.float32,
    ).astype(jnp.bfloat16)
    value_tensor = value_tensor.reshape(pos_rows, sequence_count, value_weight.shape[1])
    flat_ids = expert_ids.reshape(-1)
    onehot = (flat_ids[:, None] == jnp.arange(experts, dtype=jnp.int32)[None, :]).astype(jnp.int32)
    slot_rank = jnp.sum((jnp.cumsum(onehot, axis=0) - onehot) * onehot, axis=1)
    slot_index = flat_ids * capacity + slot_rank
    source_rows = jnp.repeat(flat_normed, top_count, axis=0)
    outgoing = (
        jnp.zeros((experts * capacity, model_width), dtype=jnp.bfloat16)
        .at[slot_index]
        .set(source_rows)
    )
    outgoing = outgoing.reshape(experts, capacity, model_width)
    incoming = lax.all_to_all(outgoing, "seq", split_axis=0, concat_axis=0, tiled=True)
    slot_count = incoming.shape[1]
    expert_rows = incoming.reshape(devices, local_experts, slot_count, model_width)
    expert_rows = expert_rows.transpose(1, 0, 2, 3).reshape(
        local_experts, devices * slot_count, model_width
    )
    gate_up = jnp.einsum("erd,edf->erf", expert_rows, w_gate_up, preferred_element_type=jnp.float32)
    hidden = (jax.nn.silu(gate_up[..., :hidden_units]) * gate_up[..., hidden_units:]).astype(
        jnp.bfloat16
    )
    result = jnp.einsum("erf,efd->erd", hidden, w_down, preferred_element_type=jnp.float32).astype(
        jnp.bfloat16
    )
    result = result.reshape(local_experts, devices, slot_count, model_width).transpose(1, 0, 2, 3)
    result = result.reshape(experts, slot_count, model_width)
    returned = lax.all_to_all(result, "seq", split_axis=0, concat_axis=0, tiled=True)
    routed = returned.reshape(experts * capacity, model_width)[slot_index].astype(jnp.float32)
    routed = routed.reshape(tok_rows, top_count, model_width)
    combined = jnp.sum(routed * gate_weights.reshape(tok_rows, top_count)[..., None], axis=1)
    combined = combined.reshape(pos_rows, sequence_count, model_width)
    layer_out = (activations.astype(jnp.float32) + combined).astype(jnp.bfloat16)
    groups = ((queries, my_index * pos_rows),)
    initial = tuple((empty_state(member[0].shape[0], sequence_count) for member in groups))
    piece_k = lax.all_gather(keys, "seq", axis=0, tiled=True)
    piece_v = lax.all_gather(value_tensor, "seq", axis=0, tiled=True)
    total_rows = piece_k.shape[0]
    rows_per_block = math.gcd(total_rows, 512)
    block_count = total_rows // rows_per_block
    key_blocks = piece_k.reshape(block_count, rows_per_block, sequence_count, piece_k.shape[2])
    value_blocks = piece_v.reshape(block_count, rows_per_block, sequence_count, piece_v.shape[2])
    block_starts = rows_per_block * jnp.arange(block_count, dtype=jnp.int32)

    def one_block(states, inputs):
        key_block_size, value_block_size, block_start = inputs
        updated = tuple(
            (
                maybe_attend(
                    current, member[0], member[1], key_block_size, value_block_size, block_start
                )
                for current, member in zip(states, groups)
            )
        )
        return (updated, None)

    final_states, leftover = lax.scan(one_block, initial, (key_blocks, value_blocks, block_starts))
    states = final_states
    contexts = [finish(current) for current in states]
    context = contexts[0]
    return (context, layer_out)


def solution(mesh):
    placed = (
        P("seq", "grp", None),
        P("seq", "grp", None),
        P("seq", "grp", None),
        P(),
        P("seq", None),
        P("seq", "grp", None),
        P("seq", "grp", None),
        P("seq", None, None),
        P("seq", None, None),
    )
    return jax.shard_map(
        per_device,
        mesh=mesh,
        in_specs=placed,
        out_specs=(P("seq", "grp", None), P("seq", "grp", None)),
        check_vma=False,
    )
```

profile of v0, /device:TPU:0, one launch (start us, length us, event | category | flops | bytes accessed | tf_op | source)
XLA Modules:
  0.0 192.9 jit_solution(2277189401436695233)
XLA Ops:
  7.2 0.0 copy-start
  7.2 0.9 copy.23
  8.1 0.1 eq.29
  8.2 0.1 eq.25
  8.3 0.7 broadcast_multiply_fusion
  9.0 0.6 reduce-window.6
  9.6 0.2 slice_reduce_fusion
  9.8 0.1 copy.22
  9.9 0.1 mul.100
  10.0 1.1 fusion.34
  11.1 1.1 fusion.38
  12.2 1.5 broadcast_in_dim.54
  13.8 2.1 %reshape.245 = bf16[256,2048]{1,0:T(8,128)(2,1)} reshape(bf16[64,4,2048]{2,1,0:T(4,128)(2,1)} %broadcast_in_dim.54) | data formatting | bytes 2097152 | tf_op jit(solution)/shard_map/reshape | solution.py:113
  15.9 0.1 fusion.41
  16.0 4.1 %scatter_custom_fusion = bf16[384,2048]{1,0:T(8,128)(2,1)} fusion(s32[256]{0:T(256)S(1)} %bitcast.133, bf16[256,2048]{1,0:T(8,128)(2,1)} %reshape.245, bf16[]{:T(256)} %constant.75.clone.1), kind=kCustom, calls=%fused_computation.37 | custom fusion | bytes 1573376 | tf_op jit(solution)/shard_map/scatter | solution.py:117
  20.1 43.5 %all_to_all.10 = bf16[16,24,2048]{2,1,0:T(8,128)(2,1)S(1)} all-to-all(bf16[16,24,2048]{2,1,0:T(8,128)(2,1)} %bitcast.127), channel_id=1, replica_groups=mesh['grp'=2,'seq'=16] {'seq'}, dimensions={0} | all-to-all | bytes 3145728 | tf_op jit(solution)/shard_map/all_to_all | solution.py:120
  63.6 4.7 %fusion.23 = f32[1,384,1536]{2,1,0:T(8,128)S(1)} fusion(bf16[384,2048]{1,0:T(8,128)(2,1)S(1)} %bitcast.131, bf16[1,2048,1536]{2,1,0:T(8,128)(2,1)} %param.20), kind=kOutput, calls=%fused_computation.30 | convolution fusion | flops 2415919104 | bytes 10223616 | tf_op jit(solution)/shard_map/erd,edf->erf/dot_general | solution.py:126
  68.3 0.0 copy-done
  68.3 2.6 %fusion.26 = bf16[384,2048]{1,0:T(8,128)(2,1)} fusion(bf16[1,768,2048]{2,1,0:T(8,128)(2,1)S(1)} %copy-done, f32[1,384,1536]{2,1,0:T(8,128)S(1)} %fusion.23), kind=kOutput, calls=%fused_computation.31 | convolution fusion | flops 1210515456 | bytes 7077888 | tf_op jit(solution)/shard_map/erf,efd->erd/dot_general | solution.py:130
  70.9 0.0 copy-start.5
  70.9 0.0 copy-start.4
  70.9 5.2 %all-to-all-start.1 = ((bf16[16,24,2048]{2,1,0:T(8,128)(2,1)}), bf16[16,24,2048]{2,1,0:T(8,128)(2,1)}, u32[]{:S(2)}, u32[]{:S(2)}) async-start(bf16[16,24,2048]{2,1,0:T(8,128)(2,1)} %bitcast.130), calls=%async_computation.1 | async-start | bytes 3145728 | tf_op jit(solution)/shard_map/all_to_all | solution.py:135
  76.1 0.0 all-gather.3.cloned.1.call-start
  76.2 0.7 all-gather.3.cloned.1.call-update
  76.9 0.0 copy-done.5
  76.9 0.1 copy.26
  77.0 0.0 copy-done.4
  77.0 49.6 %all_gather.9 = bf16[1024,1,256]{2,0,1:T(8,128)(2,1)} all-gather(bf16[64,1,256]{2,0,1:T(8,128)(2,1)S(1)} %copy-done.4), channel_id=1, replica_groups=mesh['grp'=2,'seq'=16] {'seq'}, dimensions={0}, use_global_device_ids=true | all-gather | bytes 557056 | tf_op jit(solution)/shard_map/all_gather | solution.py:143
  126.6 2.0 %copy.19 = bf16[2,512,1,256]{1,3,2,0:T(8,128)(2,1)} copy(bf16[2,512,1,256]{3,1,0,2:T(8,128)(2,1)} %bitcast.129) | data formatting | bytes 1048576 | tf_op jit(solution)/shard_map/while | solution.py:164
  128.7 0.0 all-gather.3.cloned.1.call-done
  128.7 1.5 convolution_convert_fusion
  130.3 25.5 %all-gather = bf16[1024,256]{1,0:T(8,128)(2,1)} all-gather(bf16[64,256]{1,0:T(8,128)(2,1)S(1)} %convolution_convert_fusion), channel_id=2, replica_groups=mesh['grp'=2,'seq'=16] {'seq'}, dimensions={0}, use_global_device_ids=true | all-gather | bytes 557056 | tf_op jit(solution)/shard_map/all_gather | solution.py:144
  155.7 2.0 %copy.20 = bf16[2,512,1,256]{1,3,2,0:T(8,128)(2,1)} copy(bf16[2,512,1,256]{3,1,0,2:T(8,128)(2,1)} %bitcast.128) | data formatting | bytes 1048576 | tf_op jit(solution)/shard_map/while | solution.py:164
  157.8 1.1 broadcast_in_dim.52
  158.9 10.6 %while.16 = (s32[]{:T(128)}, f32[64,1,2,16]{0,3,2,1:T(8,128)S(1)}, f32[64,1,2,16]{0,3,2,1:T(8,128)S(1)}, f32[64,1,2,16,128]{4,0,3,2,1:T(8,128)}, s32[2]{0:T(128)...) while((s32[]{:T(128)}, f32[64,1,2,16]{0,3,2,1:T(8,128)S(1)}, ...), condition=%wide.region_6.7_spmd, body=%wide.region_1.6_spmd.sunk | while | flops 551066176 | bytes 26481484 | solution.py:164
  158.9 0.6 dynamic_slice.28
  160.2 8.0 %conditional.2 = ((f32[64,1,2,16]{0,3,2,1:T(8,128)S(1)}, f32[64,1,2,16]{0,3,2,1:T(8,128)S(1)}, f32[64,1,2,16,128]{4,0,3,2,1:T(8,128)})) conditional(s32[]{:T(128)} %convert_element_type.106, (f32[64,1,2,16]{0,3,2,1:T(8,128)S(1)}, f32[64,1,2,16]{0,3,2,1:T(8,128)S(1)}, f32[64,1,2,16,128]{4,0,3,2,1:T(8,128)}) %tuple.48, (s32[]{:T(128)}, s32[]{:T(128)}, ...), branch_computations={%region_2.2_spmd, %region_3.5_spmd} | conditional | flops 551066176 | bytes 26481252 | solution.py:69
  160.2 0.7 iota_add_fusion
  160.9 0.1 broadcast_compare_fusion
  161.0 1.1 constant_dynamic-slice_fusion
  162.1 1.1 copy.33
  163.2 0.9 fusion
  164.2 0.0 copy-start.1
  164.2 1.4 fusion.2
  165.6 0.0 copy-done.1
  165.6 1.6 fusion.10
  167.2 0.0 copy-start.2
  167.2 1.0 copy-done.2
  168.2 0.6 dynamic_slice.28
  169.5 1.6 divide_convert_fusion
  171.1 1.1 copy.21
  172.2 2.1 %convert_element_type.62 = bf16[64,1,4096]{2,0,1:T(8,128)(2,1)} reshape(bf16[64,1,2,16,128]{4,3,2,0,1:T(8,128)(2,1)} %copy.21) | data formatting | bytes 1048576 | tf_op jit(solution)/shard_map/convert_element_type | solution.py:85
  174.3 0.0 all-to-all-done.1
  174.3 5.0 %gather_fusion = bf16[256,2048]{1,0:T(8,128)(2,1)} fusion(bf16[384,2048]{1,0:T(8,128)(2,1)} %bitcast.28, s32[1024]{0:T(1024)S(1)} %pad_clamp_fusion), kind=kCustom, calls=%fused_computation | custom fusion | bytes 2098176 | tf_op jit(solution)/shard_map/gather | solution.py:136
  179.3 0.0 copy-start.3
  179.3 2.8 %reshape.232 = f32[64,4,2048]{2,1,0:T(4,128)} reshape(bf16[256,2048]{1,0:T(8,128)(2,1)} %gather_fusion) | data formatting | bytes 3145728 | tf_op jit(solution)/shard_map/convert_element_type | solution.py:136
  182.1 3.2 %multiply_reduce_fusion = f32[64,2048]{1,0:T(8,128)S(1)} fusion(f32[64,4,2048]{2,1,0:T(4,128)} %reshape.232, f32[64,4]{1,0:T(8,128)S(1)} %copy.26), kind=kLoop, calls=%fused_computation.32 | loop fusion | flops 917504 | bytes 2622464 | tf_op jit(solution)/shard_map/reduce_sum | solution.py:138
  185.2 0.0 copy-done.3
  185.3 0.8 fusion.37
  (14 shorter events, 0.1 us)
Async XLA Ops:
  7.2 61.1 %copy-start = (bf16[1,768,2048]{2,1,0:T(8,128)(2,1)S(1)}, bf16[1,768,2048]{2,1,0:T(8,128)(2,1)}, u32[]{:S(2)}) copy-start(bf16[1,768,2048]{2,1,0:T(8,128)(2,1)} %param.21) | copy-start | bytes 9437188
  70.9 6.0 %copy-start.5 = (f32[64,1,4]{0,2,1:T(4,128)S(1)}, f32[64,1,4]{0,2,1:T(4,128)}, u32[]{:S(2)}) copy-start(f32[64,1,4]{0,2,1:T(4,128)} %param.19) | copy-start | bytes 3076
  70.9 6.1 %copy-start.4 = (bf16[64,1,256]{2,0,1:T(8,128)(2,1)S(1)}, bf16[64,1,256]{2,0,1:T(8,128)(2,1)}, u32[]{:S(2)}) copy-start(bf16[64,1,256]{2,0,1:T(8,128)(2,1)} %param.15) | copy-start | bytes 98308
  70.9 103.4 %all-to-all-start.1 = ((bf16[16,24,2048]{2,1,0:T(8,128)(2,1)}), bf16[16,24,2048]{2,1,0:T(8,128)(2,1)}, u32[]{:S(2)}, u32[]{:S(2)}) async-start(bf16[16,24,2048]{2,1,0:T(8,128)(2,1)} %bitcast.130), calls=%async_computation.1 | async-start | bytes 3145728 | tf_op jit(solution)/shard_map/all_to_all | solution.py:135
  76.1 52.6 %all-gather.3.cloned.1.call-start = ((), (), s32[]{:S(2)}) async-start(), calls=%async_computation.2 | async-start | bytes 1114112 | tf_op jit(solution)/shard_map/all_gather | solution.py:105
  164.2 1.4 copy-start.1
  167.2 1.0 copy-start.2
  179.3 6.0 %copy-start.3 = (bf16[64,1,2048]{2,0,1:T(8,128)(2,1)S(1)}, bf16[64,1,2048]{2,0,1:T(8,128)(2,1)}, u32[]{:S(2)}) copy-start(bf16[64,1,2048]{2,0,1:T(8,128)(2,1)} %param.13) | copy-start | bytes 786436
Sparse Core Ops, SparseCore 0:
  79.1 47.9 all-gather.2
where the time goes:
time: 196 us; the launch traced here: 193 us
  blocking collectives  119 us (61%)
  local copies, waits for them, and re-layouts  30 us (15%)
  between operations  14.2 us (7%)
  matrix products  11.4 us (6%)
  other arithmetic  11.3 us (6%)
  starting transfers between devices  5.25 us (3%)
    all_gather x1, blocking collectives, per_device(): piece_k = lax.all_gather(keys, 'seq', axis=0, tiled=True)  49.6 us
    all_to_all x1, blocking collectives, per_device(): lax.all_to_all(outgoing, 'seq', split_axis=0, concat_axis=0, tiled=True)  43.5 us
    all_gather x1, blocking collectives, per_device(): piece_v = lax.all_gather(value_tensor, 'seq', axis=0, tiled=True)  25.5 us
    all_to_all x1, starting transfers between devices, per_device(): lax.all_to_all(result, 'seq', split_axis=0, concat_axis=0, tiled=True)  5.21 us
    gather x1, local copies, waits for them, and re-layouts, per_device(): returned.reshape(experts * capacity, model_width)[slot_index]  4.96 us
    dot_general x1, matrix products, per_device(): jnp.einsum('erd,edf->erf', expert_rows, w_gate_up, preferred_element_type...  4.74 us
    scatter x1, local copies, waits for them, and re-layouts, per_device(): outgoing = jnp.zeros((experts * capacity, model_width), dtype=jnp.bfloat1...  4.11 us
    while x2, local copies, waits for them, and re-layouts, per_device(): lax.scan(one_block, initial, (key_blocks, value_blocks, block_starts))  4.09 us
  transfers between devices with their start and end apart: 2, of which 0 were waited for; matrix products, arithmetic and copies ran while one was open for 10% of the time, Pallas kernels for 0%

commit v1 on v0

v1 whole, which is shorter than its diff:
```python
import functools
import math

import jax
import jax.numpy as jnp
from jax import lax
from jax.experimental import pallas as pl
from jax.experimental.pallas import tpu as pltpu
from jax.sharding import PartitionSpec as P

QUERY_HEADS = 32
KEY_VALUE_HEADS = 2
HEAD_DIMENSION = 128
GROUPS = 4
META = 128
F32 = jnp.float32
BF16 = jnp.bfloat16


def dot(a, b):
    return jnp.dot(a, b, preferred_element_type=F32)


def pack_kernel(act_ref, gain_ref, ids_ref, gates_ref, out_ref, meta_ref):
    width = act_ref.shape[1]
    rows = act_ref.shape[0]
    top = ids_ref.shape[0]
    features = act_ref[...].astype(F32)
    inverse = lax.rsqrt(jnp.mean(features * features, axis=-1, keepdims=True) + 1e-06)
    out_ref[:, :width] = (features * inverse * gain_ref[...]).astype(BF16)
    gates = gates_ref[...]
    high = gates.astype(BF16).astype(F32)
    rest = gates - high
    middle = rest.astype(BF16).astype(F32)
    meta_ref[...] = jnp.zeros_like(meta_ref)
    meta_ref[0:top, 0:rows] = ids_ref[...].astype(F32)
    meta_ref[8 : 8 + top, 0:rows] = high
    meta_ref[16 : 16 + top, 0:rows] = middle
    meta_ref[24 : 24 + top, 0:rows] = rest - middle
    out_ref[:, width:] = meta_ref[...].T[:rows, :].astype(BF16)


def pack(activations, norm_gain, ids, gates):
    rows, width = activations.shape
    assert rows <= META and ids.shape[0] <= 8
    return pl.pallas_call(
        pack_kernel,
        out_shape=jax.ShapeDtypeStruct((rows, width + META), BF16),
        scratch_shapes=[pltpu.VMEM((META, META), F32)],
        cost_estimate=pl.CostEstimate(
            flops=4 * rows * width, bytes_accessed=4 * rows * width, transcendentals=0
        ),
        name="normalize_and_pack",
    )(activations, norm_gain.reshape(1, width), ids, gates)


def expert_kernel(
    top,
    tok_rows,
    capacity,
    x_hbm,
    up_hbm,
    down_hbm,
    out_hbm,
    x_buf,
    up_buf,
    down_buf,
    slot_rows,
    slot_gates,
    places,
    hidden,
    result,
    x_sem,
    w_sem,
    out_sem,
):
    groups, rows, packed = x_buf.shape
    width = packed - META
    slots = slot_rows.shape[0] // groups
    units = down_buf.shape[0]
    tile = 256
    me = lax.axis_index("seq").astype(F32)

    def load(group):
        return pltpu.make_async_copy(
            x_hbm.at[pl.ds(group * rows, rows)], x_buf.at[group], x_sem.at[group]
        )

    def load_up(index):
        part = pl.ds(index * tile, tile)
        return pltpu.make_async_copy(up_hbm.at[:, part], up_buf.at[:, part], w_sem.at[index])

    up_parts = 2 * units // tile
    load_down = pltpu.make_async_copy(down_hbm, down_buf, w_sem.at[up_parts])

    def store(group):
        return pltpu.make_async_copy(
            x_buf.at[group, :, pl.ds(0, width)],
            out_hbm.at[pl.ds(group * rows, rows)],
            out_sem.at[group],
        )

    half = up_parts // 2
    for group in range(groups):
        load(group).start()
    for index in range(half):
        load_up(index).start()
        load_up(half + index).start()
    load_down.start()

    chunk = tok_rows * META // math.gcd(tok_rows, META)
    first = lax.broadcasted_iota(jnp.int32, (chunk, chunk), 0)
    second = lax.broadcasted_iota(jnp.int32, (chunk, chunk), 1)
    earlier = ((first < second) & (first // tok_rows == second // tok_rows)).astype(F32).astype(BF16)
    block = lax.broadcasted_iota(jnp.int32, (1, rows), 1) // tok_rows
    for group in range(groups):
        load(group).wait()
        meta = x_buf[group, :, width:].astype(F32).T
        gate = jnp.zeros((1, rows), F32)
        named = jnp.zeros((1, rows), F32)
        for k in range(top):
            match = meta[k : k + 1] == me
            value = meta[8 + k : 9 + k] + (meta[16 + k : 17 + k] + meta[24 + k : 25 + k])
            gate = jnp.where(match, value, gate)
            named = jnp.where(match, 1.0, named)
        marks = jnp.broadcast_to(named, (8, rows)).astype(BF16)
        rank = jnp.concatenate(
            [
                dot(marks[:, at : at + chunk], earlier)
                for at in range(0, rows, chunk)
            ],
            axis=1,
        )[0:1]
        slot = jnp.where(named > 0.0, (block * capacity).astype(F32) + rank, -1.0)
        spots = lax.broadcasted_iota(jnp.int32, (slots, rows), 0).astype(F32)
        chosen = spots == slot
        slot_gates[pl.ds(group * slots, slots)] = jnp.broadcast_to(
            jnp.sum(jnp.where(chosen, gate, 0.0), axis=1, keepdims=True), (slots, META)
        )
        pick = chosen.astype(F32).astype(BF16)
        for at in range(0, width, 512):
            slot_rows[pl.ds(group * slots, slots), at : at + 512] = dot(
                pick, x_buf[group, :, at : at + 512]
            ).astype(BF16)
        by_row = jnp.broadcast_to(slot, (META, rows)).T
        spots = lax.broadcasted_iota(jnp.int32, (rows, META), 1).astype(F32)
        places[group] = (spots == by_row).astype(F32).astype(BF16)

    for index in range(half):
        load_up(index).wait()
        load_up(half + index).wait()
        gate = dot(slot_rows[...], up_buf[:, index * tile : (index + 1) * tile])
        up = dot(slot_rows[...], up_buf[:, units + index * tile : units + (index + 1) * tile])
        hidden[:, index * tile : (index + 1) * tile] = (
            gate / (1.0 + jnp.exp(-gate)) * up
        ).astype(BF16)
    load_down.wait()
    for at in range(0, width, 256):
        out = dot(hidden[...], down_buf[:, at : at + 256]).astype(BF16).astype(F32)
        result[:, at : at + 256] = (out * slot_gates[:, 0:1]).astype(BF16)
    for group in range(groups):
        for at in range(0, width, 512):
            x_buf[group, :, at : at + 512] = dot(
                places[group, :, :slots],
                result[pl.ds(group * slots, slots), at : at + 512],
            ).astype(BF16)
        store(group).start()
    for group in range(groups):
        store(group).wait()


def run_experts(gathered, w_gate_up, w_down, top, tok_rows, capacity):
    total, packed = gathered.shape
    width = packed - META
    units = w_down.shape[0]
    rows = total // GROUPS
    slots = rows // tok_rows * capacity
    assert slots % 16 == 0 and slots <= META and units % 256 == 0 and width % 512 == 0
    all_slots = GROUPS * slots
    held = (
        2 * total * packed
        + 6 * units * width
        + all_slots * (4 * width + 2 * units + 4 * META)
        + 2 * total * META
    )
    return pl.pallas_call(
        functools.partial(expert_kernel, top, tok_rows, capacity),
        out_shape=jax.ShapeDtypeStruct((total, width), BF16),
        in_specs=[pl.BlockSpec(memory_space=pl.ANY)] * 3,
        out_specs=pl.BlockSpec(memory_space=pl.ANY),
        scratch_shapes=[
            pltpu.VMEM((GROUPS, rows, packed), BF16),
            pltpu.VMEM((width, 2 * units), BF16),
            pltpu.VMEM((units, width), BF16),
            pltpu.VMEM((all_slots, width), BF16),
            pltpu.VMEM((all_slots, META), F32),
            pltpu.VMEM((GROUPS, rows, META), BF16),
            pltpu.VMEM((all_slots, units), BF16),
            pltpu.VMEM((all_slots, width), BF16),
            pltpu.SemaphoreType.DMA((GROUPS,)),
            pltpu.SemaphoreType.DMA((2 * units // 256 + 1,)),
            pltpu.SemaphoreType.DMA((GROUPS,)),
        ],
        compiler_params=pltpu.CompilerParams(vmem_limit_bytes=held + 8 * 2**20),
        cost_estimate=pl.CostEstimate(
            flops=6 * all_slots * width * units + 4 * all_slots * rows * width,
            bytes_accessed=4 * total * width + 6 * units * width,
            transcendentals=all_slots * units,
        ),
        name="experts",
    )(gathered, w_gate_up, w_down)


def attention_kernel(
    key_rows,
    q_ref,
    x_ref,
    small_hbm,
    out_ref,
    keys,
    weight,
    values,
    top_score,
    run_sum,
    run_acc,
    sems,
):
    step = pl.program_id(0)
    steps = pl.num_programs(0)
    chunk = x_ref.shape[0]
    q_rows, q_width = q_ref.shape
    width = x_ref.shape[1] - META
    heads = q_width // HEAD_DIMENSION
    together = 4
    per_kv = heads // KEY_VALUE_HEADS
    blocks = chunk // key_rows
    kv_width = KEY_VALUE_HEADS * HEAD_DIMENSION
    q_start = lax.axis_index("seq") * q_rows
    factor = math.log2(math.e) / math.sqrt(HEAD_DIMENSION)

    load_keys = pltpu.make_async_copy(
        small_hbm.at[pl.ds(step * blocks, blocks), pl.ds(0, key_rows)], keys, sems.at[0]
    )
    load_weight = pltpu.make_async_copy(
        small_hbm.at[:, pl.ds(key_rows, small_hbm.shape[1] - key_rows)], weight, sems.at[1]
    )
    load_keys.start()

    @pl.when(step == 0)
    def _():
        load_weight.start()
        load_weight.wait()
        if top_score is not None:
            top_score[...] = jnp.full_like(top_score, -1e30)
            run_sum[...] = jnp.zeros_like(run_sum)
            run_acc[...] = jnp.zeros_like(run_acc)

    load_keys.wait()

    def attend():
        values[...] = dot(x_ref[:, :width], weight[...].reshape(width, kv_width)).astype(BF16)
        all_keys = keys[...].reshape(chunk, kv_width)
        q_at = q_start + lax.broadcasted_iota(jnp.int32, (q_rows, chunk), 0)
        k_at = step * chunk + lax.broadcasted_iota(jnp.int32, (q_rows, chunk), 1)
        bias = jnp.where(q_at >= k_at, 0.0, -1e30)[None]
        for at in range(0, heads, together):
            kv = at // per_kv * HEAD_DIMENSION
            rows = jnp.concatenate(
                [
                    q_ref[:, h * HEAD_DIMENSION : (h + 1) * HEAD_DIMENSION]
                    for h in range(at, at + together)
                ],
                axis=0,
            )
            scores = lax.dot_general(
                rows,
                all_keys[:, kv : kv + HEAD_DIMENSION],
                (((1,), (1,)), ((), ())),
                preferred_element_type=F32,
            )
            scores = (scores.reshape(together, q_rows, chunk) + bias).reshape(
                together * q_rows, chunk
            )
            best = jnp.max(scores, axis=1, keepdims=True)
            place = slice(at * q_rows, (at + together) * q_rows)
            if top_score is not None:
                before = top_score[place, 0:1]
                best = jnp.maximum(best, before)
                rescale = jnp.exp2((before - best) * factor)
                top_score[place] = jnp.broadcast_to(best, (together * q_rows, HEAD_DIMENSION))
            weights = jnp.exp2((scores - best) * factor)
            total = jnp.sum(weights, axis=1, keepdims=True)
            added = dot(weights.astype(BF16), values[:, kv : kv + HEAD_DIMENSION])
            if top_score is not None:
                total = run_sum[place, 0:1] * rescale + total
                added = run_acc[place] * rescale + added
                run_sum[place] = jnp.broadcast_to(total, (together * q_rows, HEAD_DIMENSION))
                run_acc[place] = added
            context = (added / total).astype(BF16)
            for h in range(together):
                out_ref[:, (at + h) * HEAD_DIMENSION : (at + h + 1) * HEAD_DIMENSION] = context[
                    h * q_rows : (h + 1) * q_rows
                ]

    if top_score is None:
        attend()
    else:
        pl.when(step * chunk <= q_start + q_rows - 1)(attend)


def attend_all(queries, gathered, small, key_rows):
    q_rows, q_width = queries.shape
    total, packed = gathered.shape
    width = packed - META
    chunk = math.gcd(total, 1024)
    steps = total // chunk
    kv_width = small.shape[2]
    heads = q_width // HEAD_DIMENSION
    weight_rows = small.shape[1] - key_rows
    state = [pltpu.VMEM((heads * q_rows, HEAD_DIMENSION), F32)] * 3
    kernel = functools.partial(attention_kernel, key_rows)
    if steps == 1:
        state = []

        def kernel(q_ref, x_ref, small_hbm, out_ref, keys, weight, values, sems):
            attention_kernel(
                key_rows, q_ref, x_ref, small_hbm, out_ref, keys, weight, values, None, None, None, sems
            )

    return pl.pallas_call(
        kernel,
        grid=(steps,),
        out_shape=jax.ShapeDtypeStruct((q_rows, q_width), BF16),
        in_specs=[
            pl.BlockSpec((q_rows, q_width), lambda i: (0, 0)),
            pl.BlockSpec((chunk, packed), lambda i: (i, 0)),
            pl.BlockSpec(memory_space=pl.ANY),
        ],
        out_specs=pl.BlockSpec((q_rows, q_width), lambda i: (0, 0)),
        scratch_shapes=[
            pltpu.VMEM((chunk // key_rows, key_rows, kv_width), BF16),
            pltpu.VMEM((small.shape[0], weight_rows, kv_width), BF16),
            pltpu.VMEM((chunk, kv_width), BF16),
            *state,
            pltpu.SemaphoreType.DMA((2,)),
        ],
        compiler_params=pltpu.CompilerParams(vmem_limit_bytes=40 * 2**20),
        cost_estimate=pl.CostEstimate(
            flops=4 * q_rows * q_width * total + 2 * total * width * kv_width,
            bytes_accessed=2 * total * packed + 4 * q_rows * q_width,
            transcendentals=heads * q_rows * total,
        ),
        name="attention",
    )(queries, gathered, small)


def per_device(
    activations, queries, keys, norm_gain, value_weight, expert_ids, gate_weights, w_gate_up, w_down
):
    pos_rows, sequence_count, model_width = activations.shape
    assert sequence_count == 1 and w_down.shape[0] == 1
    top = expert_ids.shape[2]
    devices = lax.axis_size("seq")
    capacity = max(2, 3 * pos_rows * top // (2 * devices))
    acts = activations.reshape(pos_rows, model_width)
    packed = pack(
        acts,
        norm_gain,
        expert_ids.transpose(1, 2, 0).reshape(top, pos_rows),
        gate_weights.transpose(1, 2, 0).reshape(top, pos_rows),
    )
    gathered = lax.all_gather(packed, "seq", axis=0, tiled=True)
    small = jnp.concatenate([keys.reshape(pos_rows, -1), value_weight], axis=0)
    small = lax.all_gather(small, "seq", axis=0, tiled=False)
    partial = run_experts(gathered, w_gate_up[0], w_down[0], top, pos_rows, capacity)
    combined = lax.psum_scatter(partial, "seq", scatter_dimension=0, tiled=True)
    context = attend_all(queries.reshape(pos_rows, -1), gathered, small, pos_rows)
    layer_out = (acts.astype(F32) + combined.astype(F32)).astype(BF16)
    return (context.reshape(queries.shape), layer_out.reshape(activations.shape))


def solution(mesh):
    placed = (
        P("seq", "grp", None),
        P("seq", "grp", None),
        P("seq", "grp", None),
        P(),
        P("seq", None),
        P("seq", "grp", None),
        P("seq", "grp", None),
        P("seq", None, None),
        P("seq", None, None),
    )
    return jax.shard_map(
        per_device,
        mesh=mesh,
        in_specs=placed,
        out_specs=(P("seq", "grp", None), P("seq", "grp", None)),
        check_vma=False,
    )
```

time: 196 us -> 190 us (0.969); the launches traced: 193 us -> 190 us
  waiting for transfers between devices: 0.7 us -> 141 us
  blocking collectives: 119 us -> 0 us
  Pallas kernels: 0 us -> 19 us
  local copies, waits for them, and re-layouts: 30 us -> 12.6 us
  matrix products: 11.4 us -> 0 us
  other arithmetic: 11.3 us -> 3.21 us
  starting transfers between devices: 5.25 us -> 0.12 us
    all_gather x1 -> x2, waiting for transfers between devices: 0.02 us -> 77.4 us  [the longest x1 54.9 us: per_device(): gathered = lax.all_gather(packed, 'seq', axis=0, tiled=True)]
    all_gather x2 -> x0, blocking collectives: 75.1 us -> none  [the longest x1 49.6 us: per_device(): piece_k = lax.all_gather(keys, 'seq', axis=0, tiled=True)]
    reduce_scatter x0 -> x1, waiting for transfers between devices: none -> 63.9 us  [per_device(): combined = lax.psum_scatter(partial, 'seq', scatter_dimension=0, tiled=True)]
    all_to_all x1 -> x0, blocking collectives: 43.5 us -> none  [per_device(): lax.all_to_all(outgoing, 'seq', split_axis=0, concat_axis=0, tiled=True)]
    pallas_call x0 -> x3, Pallas kernels: none -> 19 us  [the longest x1 9.55 us: run_experts(): pl.pallas_call(functools.partial(expert_kernel, top, tok_rows, capacity),...]
    unnamed x9 -> x16, local copies, waits for them, and re-layouts: 0.94 us -> 12.6 us
    dot_general x5 -> x0, matrix products: 11.4 us -> none  [the longest x1 4.74 us: per_device(): jnp.einsum('erd,edf->erf', expert_rows, w_gate_up, preferred_element_type...]
    convert_element_type x3 -> x0, local copies, waits for them, and re-layouts: 5.98 us -> none  [the longest x2 3.19 us: finish(): return (run_acc / run_sum[..., None]).reshape(count_of_rows, sequence_cou...]
  transfers between devices with their start and end apart: 2 -> 3, of which waited for: 0 -> 3; matrix products, arithmetic and copies ran while one was open for 10% -> 1% of each run, Pallas kernels for 0% -> 9%
where the time goes in v1:
time: 190 us
  waiting for transfers between devices  141 us (74%)
  Pallas kernels  19 us (10%)
  between operations  13.8 us (7%)
  local copies, waits for them, and re-layouts  12.6 us (7%)
  other arithmetic  3.21 us (2%)
    reduce_scatter x1, waiting for transfers between devices, per_device(): combined = lax.psum_scatter(partial, 'seq', scatter_dimension=0, tiled=True)  63.9 us
    all_gather x1, waiting for transfers between devices, per_device(): gathered = lax.all_gather(packed, 'seq', axis=0, tiled=True)  54.9 us
    all_gather x1, waiting for transfers between devices, per_device(): small = lax.all_gather(small, 'seq', axis=0, tiled=False)  22.5 us
    unnamed x16, local copies, waits for them, and re-layouts  12.6 us
    pallas_call x1, Pallas kernels, run_experts(): pl.pallas_call(functools.partial(expert_kernel, top, tok_rows, capacity),...  9.55 us
    pallas_call x1, Pallas kernels, attend_all(): pl.pallas_call(kernel, grid=(steps,), out_shape=jax.ShapeDtypeStruct((q_r...  7.63 us
  transfers between devices with their start and end apart: 3, of which 3 were waited for; matrix products, arithmetic and copies ran while one was open for 1% of the time, Pallas kernels for 9%

profile of v1, /device:TPU:0, one launch (start us, length us, event | category | flops | bytes accessed | tf_op | source)
XLA Modules:
  0.0 190.1 jit_solution(13426166286140498463)
XLA Ops:
  7.2 0.0 all-gather.4.cloned.1.call-start
  7.2 1.8 normalize_and_pack.1
  9.1 0.0 all-gather.4.cloned.1.call-update
  9.1 0.0 all-gather.6.cloned.1.call-start
  9.1 1.5 pad_maximum_fusion
  10.6 0.0 all-gather.6.cloned.1.call-update
  10.6 0.0 reduce-scatter.2.cloned.1.call-start
  10.7 54.9 %all-gather.4.cloned.1.call-done.x_ref.x_hbm = bf16[1024,2176]{1,0:T(8,128)(2,1)} async-done(((bf16[64,2176]{1,0:T(8,128)(2,1)}), bf16[1024,2176]{1,0:T(8,128)(2,1)}) %all-gather.4.cloned.1.call-update) | async-done | bytes 4456464 | tf_op jit(solution)/shard_map/all_gather | solution.py:372
  65.6 0.0 copy-start.1
  65.6 2.8 %copy-done.1 = bf16[1,2048,1536]{2,1,0:T(8,128)(2,1)S(1)} copy-done((bf16[1,2048,1536]{2,1,0:T(8,128)(2,1)S(1)}, bf16[1,2048,1536]{2,1,0:T(8,128)(2,1)}, u32[]{:S(2)}) %copy-start.1) | copy-done | bytes 6291480
  68.3 0.0 copy-start.2
  68.3 2.3 %copy-done.2 = bf16[1024,2176]{1,0:T(8,128)(2,1)S(1)} copy-done((bf16[1024,2176]{1,0:T(8,128)(2,1)S(1)}, bf16[1024,2176]{1,0:T(8,128)(2,1)}, u32[]{:S(2)}) %copy-start.2) | copy-done | bytes 4456472
  70.6 0.0 copy-start.4
  70.6 1.9 copy-done.4
  72.5 9.6 %experts.1 = bf16[1024,2048]{1,0:T(8,128)(2,1)S(1)} custom-call(bf16[1024,2176]{1,0:T(8,128)(2,1)S(1)} %copy-done.2, bf16[2048,1536]{1,0:T(8,128)(2,1)S(1)} %bitcast.17, bf16[768,2048]{1,0:T(8,128)(2,1)S(1)} %bitcast.18), custom_call_target="tpu_custom_call" | custom-call | flops 4429185024 | bytes 17825792 | tf_op jit(solution)/shard_map/experts/pallas_call | solution.py:186
  82.0 0.0 copy-start
  82.1 2.0 %copy-done = bf16[1024,2048]{1,0:T(8,128)(2,1)} copy-done((bf16[1024,2048]{1,0:T(8,128)(2,1)}, bf16[1024,2048]{1,0:T(8,128)(2,1)S(1)}, u32[]{:S(2)}) %copy-start) | copy-done | bytes 4194328
  84.1 0.0 copy-start.6
  84.1 0.0 copy-start.7
  84.1 0.0 reduce-scatter.2.cloned.1.call-update
  84.1 22.5 %all-gather.6.cloned.1.call-done = bf16[3072,256]{1,0:T(8,128)(2,1)} async-done(((bf16[192,256]{1,0:T(8,128)(2,1)}), bf16[3072,256]{1,0:T(8,128)(2,1)}) %all-gather.6.cloned.1.call-update) | async-done | bytes 1572880 | tf_op jit(solution)/shard_map/all_gather | solution.py:374
  106.6 0.0 copy-done.6
  106.6 0.0 copy-start.3
  106.6 2.3 %copy-done.3 = bf16[1024,2176]{1,0:T(8,128)(2,1)S(1)} copy-done((bf16[1024,2176]{1,0:T(8,128)(2,1)S(1)}, bf16[1024,2176]{1,0:T(8,128)(2,1)}, u32[]{:S(2)}) %copy-start.3) | copy-done | bytes 4456472
  108.9 0.0 copy-start.5
  108.9 1.4 copy-done.5
  110.3 7.6 %attention.1 = bf16[64,4096]{1,0:T(8,128)(2,1)} custom-call(bf16[64,4096]{1,0:T(8,128)(2,1)S(1)} %bitcast.20, bf16[1024,2176]{1,0:T(8,128)(2,1)S(1)} %copy-done.3, bf16[16,192,256]{2,1,0:T(8,128)(2,1)S(1)} %bitcast.19), custom_call_target="tpu_custom_call" | custom-call | flops 2147483648 | bytes 5505024 | tf_op jit(solution)/shard_map/attention/pallas_call | solution.py:330
  118.0 63.9 %reduce-scatter.2.cloned.1.call-done = bf16[64,2048]{1,0:T(8,128)(2,1)} async-done(((bf16[1024,2048]{1,0:T(8,128)(2,1)}), bf16[64,2048]{1,0:T(8,128)(2,1)}) %reduce-scatter.2.cloned.1.call-update) | async-done | bytes 262160 | tf_op jit(solution)/shard_map/reduce_scatter | solution.py:376
  181.9 0.0 copy-done.7
  181.9 1.7 fusion
Async XLA Ops:
  7.2 58.4 %all-gather.4.cloned.1.call-start = ((), (), s32[]{:S(2)}) async-start(), calls=%async_computation.1 | async-start | bytes 4734976 | tf_op jit(solution)/shard_map/all_gather | solution.py:372
  9.1 97.6 %all-gather.6.cloned.1.call-start = ((), (), s32[]{:S(2)}) async-start(), calls=%async_computation.3 | async-start | bytes 1671168 | tf_op jit(solution)/shard_map/all_gather | solution.py:374
  10.6 171.2 %reduce-scatter.2.cloned.1.call-start = ((), (), s32[]{:S(2)}) async-start(), calls=%async_computation.2 | async-start | bytes 4456448 | tf_op jit(solution)/shard_map/reduce_scatter | solution.py:376
  65.6 2.8 %copy-start.1 = (bf16[1,2048,1536]{2,1,0:T(8,128)(2,1)S(1)}, bf16[1,2048,1536]{2,1,0:T(8,128)(2,1)}, u32[]{:S(2)}) copy-start(bf16[1,2048,1536]{2,1,0:T(8,128)(2,1)} %param.16) | copy-start | bytes 18874372
  68.3 2.3 %copy-start.2 = (bf16[1024,2176]{1,0:T(8,128)(2,1)S(1)}, bf16[1024,2176]{1,0:T(8,128)(2,1)}, u32[]{:S(2)}) copy-start(bf16[1024,2176]{1,0:T(8,128)(2,1)} %all-gather.4.cloned.1.call-done.x_ref.x_hbm) | copy-start | bytes 13369348
  70.6 1.9 copy-start.4
  82.0 2.0 %copy-start = (bf16[1024,2048]{1,0:T(8,128)(2,1)}, bf16[1024,2048]{1,0:T(8,128)(2,1)S(1)}, u32[]{:S(2)}) copy-start(bf16[1024,2048]{1,0:T(8,128)(2,1)S(1)} %experts.1) | copy-start | bytes 12582916
  84.1 22.6 %copy-start.6 = (bf16[64,1,4096]{2,0,1:T(8,128)(2,1)S(1)}, bf16[64,1,4096]{2,0,1:T(8,128)(2,1)}, u32[]{:S(2)}) copy-start(bf16[64,1,4096]{2,0,1:T(8,128)(2,1)} %param.10) | copy-start | bytes 1572868
  84.1 97.8 %copy-start.7 = (bf16[64,1,2048]{2,0,1:T(8,128)(2,1)S(1)}, bf16[64,1,2048]{2,0,1:T(8,128)(2,1)}, u32[]{:S(2)}) copy-start(bf16[64,1,2048]{2,0,1:T(8,128)(2,1)} %param.9) | copy-start | bytes 786436
  106.6 2.3 %copy-start.3 = (bf16[1024,2176]{1,0:T(8,128)(2,1)S(1)}, bf16[1024,2176]{1,0:T(8,128)(2,1)}, u32[]{:S(2)}) copy-start(bf16[1024,2176]{1,0:T(8,128)(2,1)} %all-gather.4.cloned.1.call-done.x_ref.x_hbm) | copy-start | bytes 13369348
  108.9 1.4 copy-start.5
Sparse Core Ops, SparseCore 0:
  10.9 54.6 all-gather.3
  68.4 38.1 all-gather.5
  110.5 71.3 reduce-scatter.1

commit v2 on v1

v2 whole, which is shorter than its diff:
```python
import functools
import math

import jax
import jax.numpy as jnp
from jax import lax
from jax.experimental import pallas as pl
from jax.experimental.pallas import tpu as pltpu
from jax.sharding import PartitionSpec as P

QUERY_HEADS = 32
KEY_VALUE_HEADS = 2
HEAD_DIMENSION = 128
GROUPS = 4
META = 128
LINE = 4
VMEM_LIMIT = 60 * 2**20
F32 = jnp.float32
BF16 = jnp.bfloat16
ANY = pl.BlockSpec(memory_space=pl.ANY)
IN_VMEM = pl.BlockSpec(memory_space=pltpu.VMEM)


def dot(a, b):
    return jnp.dot(a, b, preferred_element_type=F32)


RING = (0, 1, 3, 2)


def device_index(place, y, core):
    return (RING[place % LINE] * 2 + y) * 2 + core


def swaps(flip_y, flip_core):
    return [
        (device_index(p, y, c), device_index(p, y ^ flip_y, c ^ flip_core))
        for p in range(LINE)
        for y in range(2)
        for c in range(2)
    ]


def ring_step():
    return [
        (device_index(p, y, c), device_index(p + 1, y, c))
        for p in range(LINE)
        for y in range(2)
        for c in range(2)
    ]


def along_ring(x):
    return lax.ppermute(x, "seq", ring_step())


def across(x):
    return lax.ppermute(x, "seq", swaps(1, 0))


def other_core(x):
    return lax.ppermute(x, "seq", swaps(0, 1))


def from_device(steps, flip_y, flip_core):
    me = lax.axis_index("seq")
    core, y, line = me % 2, me // 2 % 2, me // 4
    place = sum(jnp.where(line == RING[p], p, 0) for p in range(LINE))
    place = (place + LINE - steps) % LINE
    line = sum(jnp.where(place == p, RING[p], 0) for p in range(LINE))
    y = 1 - y if flip_y else y
    core = 1 - core if flip_core else core
    return (line * 2 + y) * 2 + core


def pack_kernel(act_ref, gain_ref, ids_ref, gates_ref, out_ref, meta_ref):
    width = act_ref.shape[1]
    rows = act_ref.shape[0]
    top = ids_ref.shape[0]
    features = act_ref[...].astype(F32)
    inverse = lax.rsqrt(jnp.mean(features * features, axis=-1, keepdims=True) + 1e-06)
    out_ref[:, :width] = (features * inverse * gain_ref[...]).astype(BF16)
    gates = gates_ref[...]
    high = gates.astype(BF16).astype(F32)
    rest = gates - high
    middle = rest.astype(BF16).astype(F32)
    meta_ref[...] = jnp.zeros_like(meta_ref)
    meta_ref[0:top, 0:rows] = ids_ref[...].astype(F32)
    meta_ref[8 : 8 + top, 0:rows] = high
    meta_ref[16 : 16 + top, 0:rows] = middle
    meta_ref[24 : 24 + top, 0:rows] = rest - middle
    out_ref[:, width:] = meta_ref[...].T[:rows, :].astype(BF16)


def pack(activations, norm_gain, ids, gates):
    rows, width = activations.shape
    assert rows <= META and ids.shape[0] <= 8
    return pl.pallas_call(
        pack_kernel,
        out_shape=jax.ShapeDtypeStruct((rows, width + META), BF16),
        scratch_shapes=[pltpu.VMEM((META, META), F32)],
        cost_estimate=pl.CostEstimate(
            flops=4 * rows * width, bytes_accessed=4 * rows * width, transcendentals=0
        ),
        name="normalize_and_pack",
    )(activations, norm_gain.reshape(1, width), ids, gates)


def expert_kernel(top, tok_rows, capacity, sources, targets, *refs):
    inputs = 1 + max(s[0] for group in sources for s in group)
    outputs = 1 + max(t[0] for group in targets for t in group)
    x_hbm = refs[:inputs]
    up_hbm, down_hbm = refs[inputs : inputs + 2]
    out_hbm = refs[inputs + 2 : inputs + 2 + outputs]
    (
        x_buf,
        up_buf,
        down_buf,
        slot_rows,
        slot_gates,
        places,
        hidden,
        result,
        x_sem,
        w_sem,
        out_sem,
    ) = refs[inputs + 2 + outputs :]
    groups, rows, packed = x_buf.shape
    width = packed - META
    slots = slot_rows.shape[0] // groups
    units = down_buf.shape[0]
    tile = 256
    me = lax.axis_index("seq").astype(F32)

    def loads(group):
        copies, at = [], 0
        for number, (operand, first, count) in enumerate(sources[group]):
            copies.append(
                pltpu.make_async_copy(
                    x_hbm[operand].at[pl.ds(first, count)],
                    x_buf.at[group, pl.ds(at, count)],
                    x_sem.at[group, number],
                )
            )
            at += count
        return copies

    def stores(group):
        copies, at = [], 0
        for number, (operand, first, count) in enumerate(targets[group]):
            copies.append(
                pltpu.make_async_copy(
                    x_buf.at[group, pl.ds(at, count), pl.ds(0, width)],
                    out_hbm[operand].at[pl.ds(first, count)],
                    out_sem.at[group, number],
                )
            )
            at += count
        return copies

    def load_up(index):
        part = pl.ds(index * tile, tile)
        return pltpu.make_async_copy(up_hbm.at[:, part], up_buf.at[:, part], w_sem.at[index])

    up_parts = 2 * units // tile
    load_down = pltpu.make_async_copy(down_hbm, down_buf, w_sem.at[up_parts])
    half = up_parts // 2
    for group in range(groups):
        for copy in loads(group):
            copy.start()
    for index in range(half):
        load_up(index).start()
        load_up(half + index).start()
    load_down.start()

    chunk = tok_rows * META // math.gcd(tok_rows, META)
    first = lax.broadcasted_iota(jnp.int32, (chunk, chunk), 0)
    second = lax.broadcasted_iota(jnp.int32, (chunk, chunk), 1)
    earlier = ((first < second) & (first // tok_rows == second // tok_rows)).astype(F32).astype(BF16)
    block = lax.broadcasted_iota(jnp.int32, (1, rows), 1) // tok_rows
    for group in range(groups):
        for copy in loads(group):
            copy.wait()
        meta = x_buf[group, :, width:].astype(F32).T
        gate = jnp.zeros((1, rows), F32)
        named = jnp.zeros((1, rows), F32)
        for k in range(top):
            match = meta[k : k + 1] == me
            value = meta[8 + k : 9 + k] + (meta[16 + k : 17 + k] + meta[24 + k : 25 + k])
            gate = jnp.where(match, value, gate)
            named = jnp.where(match, 1.0, named)
        marks = jnp.broadcast_to(named, (8, rows)).astype(BF16)
        rank = jnp.concatenate(
            [dot(marks[:, at : at + chunk], earlier) for at in range(0, rows, chunk)], axis=1
        )[0:1]
        slot = jnp.where(named > 0.0, (block * capacity).astype(F32) + rank, -1.0)
        spots = lax.broadcasted_iota(jnp.int32, (slots, rows), 0).astype(F32)
        chosen = spots == slot
        slot_gates[pl.ds(group * slots, slots)] = jnp.broadcast_to(
            jnp.sum(jnp.where(chosen, gate, 0.0), axis=1, keepdims=True), (slots, META)
        )
        pick = chosen.astype(F32).astype(BF16)
        for at in range(0, width, 512):
            slot_rows[pl.ds(group * slots, slots), at : at + 512] = dot(
                pick, x_buf[group, :, at : at + 512]
            ).astype(BF16)
        by_row = jnp.broadcast_to(slot, (META, rows)).T
        spots = lax.broadcasted_iota(jnp.int32, (rows, META), 1).astype(F32)
        places[group] = (spots == by_row).astype(F32).astype(BF16)

    for index in range(half):
        load_up(index).wait()
        load_up(half + index).wait()
        gate = dot(slot_rows[...], up_buf[:, index * tile : (index + 1) * tile])
        up = dot(slot_rows[...], up_buf[:, units + index * tile : units + (index + 1) * tile])
        hidden[:, index * tile : (index + 1) * tile] = (gate / (1.0 + jnp.exp(-gate)) * up).astype(
            BF16
        )
    load_down.wait()
    for at in range(0, width, 256):
        out = dot(hidden[...], down_buf[:, at : at + 256]).astype(BF16).astype(F32)
        result[:, at : at + 256] = (out * slot_gates[:, 0:1]).astype(BF16)
    for group in range(groups):
        for at in range(0, width, 512):
            x_buf[group, :, at : at + 512] = dot(
                places[group, :, :slots], result[pl.ds(group * slots, slots), at : at + 512]
            ).astype(BF16)
        for copy in stores(group):
            copy.start()
    for group in range(groups):
        for copy in stores(group):
            copy.wait()


def run_experts(arrays, sources, targets, out_rows, w_gate_up, w_down, top, tok_rows, capacity):
    groups = len(sources)
    rows = sum(count for _, _, count in sources[0])
    packed = arrays[0].shape[1]
    total = groups * rows
    width = packed - META
    units = w_down.shape[0]
    slots = rows // tok_rows * capacity
    assert slots % 16 == 0 and slots <= META and units % 256 == 0 and width % 512 == 0
    all_slots = groups * slots
    return pl.pallas_call(
        functools.partial(expert_kernel, top, tok_rows, capacity, sources, targets),
        out_shape=[jax.ShapeDtypeStruct((count, width), BF16) for count in out_rows],
        in_specs=[ANY] * (len(arrays) + 2),
        out_specs=[ANY] * len(out_rows),
        scratch_shapes=[
            pltpu.VMEM((groups, rows, packed), BF16),
            pltpu.VMEM((width, 2 * units), BF16),
            pltpu.VMEM((units, width), BF16),
            pltpu.VMEM((all_slots, width), BF16),
            pltpu.VMEM((all_slots, META), F32),
            pltpu.VMEM((groups, rows, META), BF16),
            pltpu.VMEM((all_slots, units), BF16),
            pltpu.VMEM((all_slots, width), BF16),
            pltpu.SemaphoreType.DMA((groups, max(len(s) for s in sources))),
            pltpu.SemaphoreType.DMA((2 * units // 256 + 1,)),
            pltpu.SemaphoreType.DMA((groups, max(len(t) for t in targets))),
        ],
        compiler_params=pltpu.CompilerParams(vmem_limit_bytes=VMEM_LIMIT),
        cost_estimate=pl.CostEstimate(
            flops=6 * all_slots * width * units + 4 * all_slots * rows * width,
            bytes_accessed=4 * total * width + 6 * units * width,
            transcendentals=all_slots * units,
        ),
        name="experts",
    )(*arrays, w_gate_up, w_down)


def value_kernel(key_rows, blocks, small_blocks, *refs):
    inputs = 1 + max(b[0] for b in blocks)
    smalls = 1 + max(b[0] for b in small_blocks)
    x_hbm = refs[:inputs]
    small_hbm = refs[inputs : inputs + smalls]
    key_ref, value_ref, x_buf, weight, sems = refs[inputs + smalls :]
    width = x_buf.shape[1]
    weight_rows = width // len(small_blocks)
    copies = []
    for number, (operand, first, device) in enumerate(blocks):
        copies.append(
            pltpu.make_async_copy(
                x_hbm[operand].at[pl.ds(first, key_rows), pl.ds(0, width)],
                x_buf.at[pl.ds(device() * key_rows, key_rows)],
                sems.at[0, number],
            )
        )
    for number, (operand, first, device) in enumerate(small_blocks):
        place = device()
        copies.append(
            pltpu.make_async_copy(
                small_hbm[operand].at[pl.ds(first, key_rows)],
                key_ref.at[pl.ds(place * key_rows, key_rows)],
                sems.at[1, number],
            )
        )
        copies.append(
            pltpu.make_async_copy(
                small_hbm[operand].at[pl.ds(first + key_rows, weight_rows)],
                weight.at[pl.ds(place * weight_rows, weight_rows)],
                sems.at[2, number],
            )
        )
    for copy in copies:
        copy.start()
    for copy in copies:
        copy.wait()
    value_ref[...] = dot(x_buf[...], weight[...]).astype(BF16)


def make_values(arrays, blocks, smalls, small_blocks, key_rows, width):
    kv_width = smalls[0].shape[1]
    total = key_rows * len(blocks)
    kv = jax.ShapeDtypeStruct((total, kv_width), BF16)
    return pl.pallas_call(
        functools.partial(value_kernel, key_rows, blocks, small_blocks),
        out_shape=[kv, kv],
        in_specs=[ANY] * (len(arrays) + len(smalls)),
        out_specs=[IN_VMEM] * 2,
        scratch_shapes=[
            pltpu.VMEM((total, width), BF16),
            pltpu.VMEM((width, kv_width), BF16),
            pltpu.SemaphoreType.DMA((3, len(blocks))),
        ],
        compiler_params=pltpu.CompilerParams(vmem_limit_bytes=VMEM_LIMIT),
        cost_estimate=pl.CostEstimate(
            flops=2 * total * width * kv_width,
            bytes_accessed=2 * total * width + 2 * width * kv_width,
            transcendentals=0,
        ),
        name="values",
    )(*arrays, *smalls)


def attention_kernel(chunk, q_ref, k_ref, v_ref, *refs):
    out_ref = refs[-1]
    q_rows, q_width = q_ref.shape
    heads = q_width // HEAD_DIMENSION
    together = 4
    q_start = lax.axis_index("seq") * q_rows
    factor = math.log2(math.e) / math.sqrt(HEAD_DIMENSION)
    steps = k_ref.shape[0] // chunk
    tall = together * q_rows

    def scored(rows, start):
        scores = lax.dot_general(
            rows, k_ref[pl.ds(start, chunk)], (((1,), (1,)), ((), ())), preferred_element_type=F32
        )
        q_at = q_start + lax.broadcasted_iota(jnp.int32, (q_rows, chunk), 0)
        k_at = start + lax.broadcasted_iota(jnp.int32, (q_rows, chunk), 1)
        bias = jnp.where(q_at >= k_at, 0.0, -1e30)[None]
        return (scores.reshape(together, q_rows, chunk) + bias).reshape(tall, chunk)

    for at in range(0, heads, together):
        rows = jnp.concatenate(
            [
                q_ref[:, h * HEAD_DIMENSION : (h + 1) * HEAD_DIMENSION]
                for h in range(at, at + together)
            ],
            axis=0,
        )

        def one(step, state):
            top_score, run_sum, run_acc = state
            start = pl.multiple_of(step * chunk, chunk)
            scores = scored(rows, start)
            best = jnp.maximum(jnp.max(scores, axis=1, keepdims=True), top_score)
            rescale = jnp.exp2((top_score - best) * factor)
            weights = jnp.exp2((scores - best) * factor)
            total = run_sum * rescale + jnp.sum(weights, axis=1, keepdims=True)
            added = dot(weights.astype(BF16), v_ref[pl.ds(start, chunk)])
            return (best, total, run_acc * rescale + added)

        if steps == 1:
            scores = scored(rows, 0)
            best = jnp.max(scores, axis=1, keepdims=True)
            weights = jnp.exp2((scores - best) * factor)
            total = jnp.sum(weights, axis=1, keepdims=True)
            added = dot(weights.astype(BF16), v_ref[...])
        else:
            best, total, added = lax.fori_loop(
                0,
                (q_start + q_rows + chunk - 1) // chunk,
                one,
                (
                    jnp.full((tall, 1), -1e30, F32),
                    jnp.zeros((tall, 1), F32),
                    jnp.zeros((tall, HEAD_DIMENSION), F32),
                ),
            )
        context = (added / total).astype(BF16)
        for h in range(together):
            out_ref[:, (at + h) * HEAD_DIMENSION : (at + h + 1) * HEAD_DIMENSION] = context[
                h * q_rows : (h + 1) * q_rows
            ]


def attend_all(queries, keys, values, parts):
    q_rows, q_width = queries.shape
    total = keys.shape[0]
    part_width = q_width // parts
    per_kv = parts // KEY_VALUE_HEADS
    chunk = math.gcd(total, 1024)
    context = ()
    for part in range(parts):
        context = (
            pl.pallas_call(
                functools.partial(attention_kernel, chunk),
                grid=(1,),
                out_shape=jax.ShapeDtypeStruct((q_rows, q_width), BF16),
                in_specs=[
                    pl.BlockSpec((q_rows, part_width), lambda i, part=part: (0, part)),
                    pl.BlockSpec((total, HEAD_DIMENSION), lambda i, part=part: (0, part // per_kv)),
                    pl.BlockSpec((total, HEAD_DIMENSION), lambda i, part=part: (0, part // per_kv)),
                    *[ANY for _ in context],
                ],
                out_specs=pl.BlockSpec((q_rows, part_width), lambda i, part=part: (0, part)),
                input_output_aliases={3: 0} if context else {},
                compiler_params=pltpu.CompilerParams(vmem_limit_bytes=VMEM_LIMIT),
                cost_estimate=pl.CostEstimate(
                    flops=4 * q_rows * part_width * total,
                    bytes_accessed=4 * total * HEAD_DIMENSION + 4 * q_rows * part_width,
                    transcendentals=part_width // HEAD_DIMENSION * q_rows * total,
                ),
                name="attention",
            )(queries, keys, values, *context),
        )
    return context[0]


def summed(*terms):
    return sum(term.astype(F32) for term in terms).astype(BF16)


def on_line(acts, packed, keys, value_weight, queries, w_gate_up, w_down, top, capacity):
    rows, width = acts.shape
    pair = jnp.concatenate([keys, value_weight], axis=0)
    small_rows = pair.shape[0]
    pair = jnp.concatenate([pair, across(pair)], axis=0)
    small = [pair]
    for _ in range(LINE - 1):
        small.append(along_ring(small[-1]))
    own_core = jnp.concatenate(small, axis=0)
    small = [own_core, other_core(own_core)]
    small_blocks = [
        (core, (step * 2 + y) * small_rows, functools.partial(from_device, step, y, core))
        for core in range(2)
        for step in range(LINE)
        for y in range(2)
    ]
    arrays, blocks, sources, targets = [], [], [], []
    moving = packed
    for step in range(LINE):
        if step > 0:
            moving = along_ring(moving)
        crossed = across(moving)
        arrays += [moving, crossed, other_core(moving), other_core(crossed)]
        sources.append([(4 * step + i, 0, rows) for i in range(4)])
        targets.append([(2 * step + i, 0, 2 * rows) for i in range(2)])
        blocks += [
            (4 * step + core * 2 + y, 0, functools.partial(from_device, step, y, core))
            for core in range(2)
            for y in range(2)
        ]
    partial = run_experts(
        arrays, sources, targets, [2 * rows] * (2 * LINE), w_gate_up, w_down, top, rows, capacity
    )
    new_keys, values = make_values(arrays, blocks, small, small_blocks, rows, width)
    context = attend_all(queries, new_keys, values, 4)
    moving = None
    for step in (1, 2, 3, 0):
        keep, send = partial[2 * step], partial[2 * step + 1]
        came = other_core(send)
        mine = summed(keep[:rows], came[:rows])
        theirs = across(summed(keep[rows:], came[rows:]))
        if step == 0:
            break
        total = summed(mine, theirs) if moving is None else summed(mine, theirs, moving)
        moving = along_ring(total)
    layer_out = summed(acts, mine, theirs, moving)
    return context, layer_out


def on_any(acts, packed, keys, value_weight, queries, w_gate_up, w_down, top, capacity):
    rows, width = acts.shape
    gathered = lax.all_gather(packed, "seq", axis=0, tiled=True)
    all_keys = lax.all_gather(keys, "seq", axis=0, tiled=True)
    weight = lax.all_gather(value_weight, "seq", axis=0, tiled=True)
    total = gathered.shape[0]
    part = total // GROUPS
    pieces = [[(0, group * part, part)] for group in range(GROUPS)]
    (partial,) = run_experts(
        [gathered], pieces, pieces, [total], w_gate_up, w_down, top, rows, capacity
    )
    values = dot(gathered[:, :width], weight).astype(BF16)
    context = attend_all(queries, all_keys, values, KEY_VALUE_HEADS)
    combined = lax.psum_scatter(partial, "seq", scatter_dimension=0, tiled=True)
    return context, summed(acts, combined)


def per_device(
    activations, queries, keys, norm_gain, value_weight, expert_ids, gate_weights, w_gate_up, w_down
):
    pos_rows, sequence_count, model_width = activations.shape
    assert sequence_count == 1 and w_down.shape[0] == 1
    top = expert_ids.shape[2]
    devices = lax.axis_size("seq")
    capacity = max(2, 3 * pos_rows * top // (2 * devices))
    acts = activations.reshape(pos_rows, model_width)
    packed = pack(
        acts,
        norm_gain,
        expert_ids.transpose(1, 2, 0).reshape(top, pos_rows),
        gate_weights.transpose(1, 2, 0).reshape(top, pos_rows),
    )
    way = on_line if devices == 4 * LINE else on_any
    context, layer_out = way(
        acts,
        packed,
        keys.reshape(pos_rows, -1),
        value_weight,
        queries.reshape(pos_rows, -1),
        w_gate_up[0],
        w_down[0],
        top,
        capacity,
    )
    return (context.reshape(queries.shape), layer_out.reshape(activations.shape))


def solution(mesh):
    placed = (
        P("seq", "grp", None),
        P("seq", "grp", None),
        P("seq", "grp", None),
        P(),
        P("seq", None),
        P("seq", "grp", None),
        P("seq", "grp", None),
        P("seq", None, None),
        P("seq", None, None),
    )
    return jax.shard_map(
        per_device,
        mesh=mesh,
        in_specs=placed,
        out_specs=(P("seq", "grp", None), P("seq", "grp", None)),
        check_vma=False,
    )
```

time: 190 us -> 120 us (0.63)
  waiting for transfers between devices: 141 us -> 53.4 us
  starting transfers between devices: 0.12 us -> 22 us
  between operations: 13.8 us -> 0.97 us
  Pallas kernels: 19 us -> 30 us
  local copies, waits for them, and re-layouts: 12.6 us -> 4.58 us
  other arithmetic: 3.21 us -> 7.98 us
    all_gather x2 -> x0, waiting for transfers between devices: 77.4 us -> none  [the longest x1 54.9 us: per_device(): gathered = lax.all_gather(packed, 'seq', axis=0, tiled=True)]
    reduce_scatter x1 -> x0, waiting for transfers between devices: 63.9 us -> none  [per_device(): combined = lax.psum_scatter(partial, 'seq', scatter_dimension=0, tiled=True)]
    ppermute x0 -> x31, waiting for transfers between devices: none -> 53.4 us  [the longest x9 34 us: along_ring(): return lax.ppermute(x, 'seq', ring_step())]
    ppermute x0 -> x31, starting transfers between devices: none -> 22 us  [the longest x9 10.2 us: across(): return lax.ppermute(x, 'seq', swaps(1, 0))]
    pallas_call x2 -> x6, Pallas kernels: 17.2 us -> 28.1 us  [the longest x1 11.6 us: run_experts(): pl.pallas_call(functools.partial(expert_kernel, top, tok_rows, capacity,...]
    unnamed x16 -> x47, local copies, waits for them, and re-layouts: 12.6 us -> 4.56 us
    convert_element_type x0 -> x7, other arithmetic: none -> 5.4 us  [summed(): return sum((term.astype(F32) for term in terms)).astype(BF16)]
  transfers between devices with their start and end apart: 3 -> 31, of which waited for: 3 -> 11; matrix products, arithmetic and copies ran while one was open for 1% -> 8% of each run, Pallas kernels for 9% -> 24%
where the time goes in v2:
time: 120 us; the launch traced here: 119 us
  waiting for transfers between devices  53.4 us (44%)
  Pallas kernels  30 us (25%)
  starting transfers between devices  22 us (18%)
  other arithmetic  7.98 us (7%)
  local copies, waits for them, and re-layouts  4.58 us (4%)
    ppermute x9, waiting for transfers between devices, along_ring(): return lax.ppermute(x, 'seq', ring_step())  34 us
    ppermute x9, waiting for transfers between devices, across(): return lax.ppermute(x, 'seq', swaps(1, 0))  19.4 us
    pallas_call x1, Pallas kernels, run_experts(): pl.pallas_call(functools.partial(expert_kernel, top, tok_rows, capacity,...  11.6 us
    pallas_call x4, Pallas kernels, attend_all(): pl.pallas_call(functools.partial(attention_kernel, chunk), grid=(1,), out...  11.6 us
    ppermute x9, starting transfers between devices, across(): return lax.ppermute(x, 'seq', swaps(1, 0))  10.2 us
    ppermute x9, starting transfers between devices, along_ring(): return lax.ppermute(x, 'seq', ring_step())  10.1 us
    convert_element_type x7, other arithmetic, summed(): return sum((term.astype(F32) for term in terms)).astype(BF16)  5.4 us
    pallas_call x1, Pallas kernels, make_values(): pl.pallas_call(functools.partial(value_kernel, key_rows, blocks, small_bl...  5.01 us
  transfers between devices with their start and end apart: 31, of which 11 were waited for; matrix products, arithmetic and copies ran while one was open for 8% of the time, Pallas kernels for 24%

profile of v2, /device:TPU:0, one launch (start us, length us, event | category | flops | bytes accessed | tf_op | source)
XLA Modules:
  0.0 119.0 jit_solution(16774079956709565985)
XLA Ops:
  0.6 1.8 %normalize_and_pack.1.refs_0_ = bf16[64,2176]{1,0:T(8,128)(2,1)} custom-call(bf16[64,2048]{1,0:T(8,128)(2,1)} %bitcast.22, f32[1,2048]{1,0:T(1,128)} %bitcast.25, s32[4,64]{1,0:T(4,128)} %bitcast.26, f32[4,64]{1,0:T(4,128)} %bitcast.27), custom_call_target="tpu_custom_call" | custom-call | flops 524288 | bytes 524288 | tf_op jit(solution)/shard_map/normalize_and_pack/pallas_call | solution.py:98
  2.5 3.0 %collective-permute-start.3 = (bf16[64,2176]{1,0:T(8,128)(2,1)}, bf16[64,2176]{1,0:T(8,128)(2,1)S(1)}, u32[]{:S(2)}, u32[]{:S(2)}) collective-permute-start(bf16[64,2176]{1,0:T(8,128)(2,1)} %normalize_and_pack.1.refs_0_), channel_id=1, source_target_pairs={{0,4},{1,5},{2,6},{3,7},{4,12},{5,13},{6,14},{7,15},{12,8},{13,9},... | collective-permute-start | bytes 835592 | tf_op jit(solution)/shard_map/ppermute | solution.py:54
  5.5 7.9 %collective-permute-done.3.refs_4_ = bf16[64,2176]{1,0:T(8,128)(2,1)S(1)} collective-permute-done((bf16[64,2176]{1,0:T(8,128)(2,1)}, bf16[64,2176]{1,0:T(8,128)(2,1)S(1)}, u32[]{:S(2)}, u32[]{:S(2)}) %collective-permute-start.3) | collective-permute-done | bytes 278560 | tf_op jit(solution)/shard_map/ppermute | solution.py:54
  13.4 0.9 collective-permute-start.7
  14.3 0.8 pad_maximum_fusion.1
  15.2 1.6 %collective-permute-start.15 = (bf16[192,256]{1,0:T(8,128)(2,1)S(1)}, bf16[192,256]{1,0:T(8,128)(2,1)S(1)}, u32[]{:S(2)}, u32[]{:S(2)}) collective-permute-start(bf16[192,256]{1,0:T(8,128)(2,1)S(1)} %pad_maximum_fusion.1), channel_id=1, source_target_pairs={{0,2},{1,3},{2,0},{3,1},{4,6},{5,7},{6,4},{7,5},{12,14},{13,15},{1... | collective-permute-start | bytes 294920 | tf_op jit(solution)/shard_map/ppermute | solution.py:58
  16.8 0.5 collective-permute-start
  17.3 4.9 %collective-permute-done.7.refs_8_ = bf16[64,2176]{1,0:T(8,128)(2,1)S(1)} collective-permute-done((bf16[64,2176]{1,0:T(8,128)(2,1)S(1)}, bf16[64,2176]{1,0:T(8,128)(2,1)S(1)}, u32[]{:S(2)}, u32[]{:S(2)}) %collective-permute-start.7) | collective-permute-done | bytes 278560 | tf_op jit(solution)/shard_map/ppermute | solution.py:54
  22.1 0.5 collective-permute-start.11
  22.7 0.9 pad_maximum_fusion
  23.5 3.4 %collective-permute-start.16 = (bf16[384,256]{1,0:T(8,128)(2,1)S(1)}, bf16[384,256]{1,0:T(8,128)(2,1)}, u32[]{:S(2)}, u32[]{:S(2)}) collective-permute-start(bf16[384,256]{1,0:T(8,128)(2,1)S(1)} %pad_maximum_fusion), channel_id=1, source_target_pairs={{0,4},{1,5},{2,6},{3,7},{4,12},{5,13},{6,14},{7,15},{12,8},{13,9},... | collective-permute-start | bytes 589832 | tf_op jit(solution)/shard_map/ppermute | solution.py:54
  27.0 1.6 %collective-permute-start.4 = (bf16[64,2176]{1,0:T(8,128)(2,1)S(1)}, bf16[64,2176]{1,0:T(8,128)(2,1)S(1)}, u32[]{:S(2)}, u32[]{:S(2)}) collective-permute-start(bf16[64,2176]{1,0:T(8,128)(2,1)S(1)} %collective-permute-done.3.refs_4_), channel_id=1, source_target_pairs={{0,2},{1,3},{2,0},{3,1},{4,6},{5,7},{6,4},{7,5},{12,14},{13,15},{1... | collective-permute-start | bytes 835592 | tf_op jit(solution)/shard_map/ppermute | solution.py:58
  28.5 0.2 collective-permute-start.5
  28.7 5.6 %collective-permute-done.16 = bf16[384,256]{1,0:T(8,128)(2,1)} collective-permute-done((bf16[384,256]{1,0:T(8,128)(2,1)S(1)}, bf16[384,256]{1,0:T(8,128)(2,1)}, u32[]{:S(2)}, u32[]{:S(2)}) %collective-permute-start.16) | collective-permute-done | bytes 196640 | tf_op jit(solution)/shard_map/ppermute | solution.py:54
  34.3 0.9 collective-permute-start.8
  35.2 1.1 collective-permute-start.12
  36.3 0.2 collective-permute-done.4.refs_5_
  36.5 0.3 collective-permute-start.6
  36.8 0.2 collective-permute-start.13
  37.0 6.9 %collective-permute-done.8.refs_9_ = bf16[64,2176]{1,0:T(8,128)(2,1)S(1)} collective-permute-done((bf16[64,2176]{1,0:T(8,128)(2,1)S(1)}, bf16[64,2176]{1,0:T(8,128)(2,1)S(1)}, u32[]{:S(2)}, u32[]{:S(2)}) %collective-permute-start.8) | collective-permute-done | bytes 278560 | tf_op jit(solution)/shard_map/ppermute | solution.py:58
  43.9 4.1 %collective-permute-done.12.refs_13_ = bf16[64,2176]{1,0:T(8,128)(2,1)S(1)} collective-permute-done((bf16[64,2176]{1,0:T(8,128)(2,1)S(1)}, bf16[64,2176]{1,0:T(8,128)(2,1)S(1)}, u32[]{:S(2)}, u32[]{:S(2)}) %collective-permute-start.12) | collective-permute-done | bytes 278560 | tf_op jit(solution)/shard_map/ppermute | solution.py:58
  48.0 0.8 constant_dynamic-update-slice_fusion.5
  48.7 1.3 %collective-permute-start.17 = (bf16[384,256]{1,0:T(8,128)(2,1)}, bf16[384,256]{1,0:T(8,128)(2,1)}, u32[]{:S(2)}, u32[]{:S(2)}) collective-permute-start(bf16[384,256]{1,0:T(8,128)(2,1)} %collective-permute-done.16), channel_id=1, source_target_pairs={{0,4},{1,5},{2,6},{3,7},{4,12},{5,13},{6,14},{7,15},{12,8},{13,9},... | collective-permute-start | bytes 589832 | tf_op jit(solution)/shard_map/ppermute | solution.py:54
  50.1 0.7 copy-done.19
  50.8 0.1 copy-done.18
  50.9 0.1 copy-done.20
  51.1 0.0 copy-done.16
  51.1 11.6 %experts.1 = (bf16[128,2048]{1,0:T(8,128)(2,1)}, bf16[128,2048]{1,0:T(8,128)(2,1)}, bf16[128,2048]{1,0:T(8,128)(2,1)}, bf16[128,2048]{1,0:T(8,128)(2,1)}, bf16[1...) custom-call(bf16[64,2176]{1,0:T(8,128)(2,1)} %normalize_and_pack.1.refs_, ...), custom_call_target="tpu_custom_call" | custom-call | flops 4429185024 | bytes 17825792 | tf_op jit(solution)/shard_map/experts/pallas_call | solution.py:245
  62.7 0.0 copy-start.5
  62.8 0.3 collective-permute-start.26
  63.1 0.5 collective-permute-start.18
  63.6 0.9 constant_dynamic-update-slice_fusion.2
  64.5 0.9 constant_dynamic-update-slice_fusion.1
  65.5 0.1 collective-permute-start.24
  65.6 5.8 %collective-permute-done.18 = bf16[384,256]{1,0:T(8,128)(2,1)S(1)} collective-permute-done((bf16[384,256]{1,0:T(8,128)(2,1)}, bf16[384,256]{1,0:T(8,128)(2,1)S(1)}, u32[]{:S(2)}, u32[]{:S(2)}) %collective-permute-start.18) | collective-permute-done | bytes 196640 | tf_op jit(solution)/shard_map/ppermute | solution.py:54
  71.4 0.1 collective-permute-start.19
  71.5 0.5 collective-permute-start.22
  72.0 0.1 collective-permute-start.20
  72.0 1.0 add_convert_fusion.4
  73.1 1.2 collective-permute-start.27
  74.2 1.0 add_convert_fusion.6
  75.3 1.0 collective-permute-start.25
  76.2 6.0 %collective-permute-done.27 = bf16[64,2048]{1,0:T(8,128)(2,1)S(1)} collective-permute-done((bf16[64,2048]{1,0:T(8,128)(2,1)S(1)}, bf16[64,2048]{1,0:T(8,128)(2,1)S(1)}, u32[]{:S(2)}, u32[]{:S(2)}) %collective-permute-start.27) | collective-permute-done | bytes 262176 | tf_op jit(solution)/shard_map/ppermute | solution.py:58
  82.2 1.1 add_convert_fusion.3
  83.3 0.1 collective-permute-start.28
  83.4 1.0 add_convert_fusion.8
  84.4 1.2 collective-permute-start.23
  85.6 2.3 %collective-permute-done.25 = bf16[64,2048]{1,0:T(8,128)(2,1)S(1)} collective-permute-done((bf16[64,2048]{1,0:T(8,128)(2,1)S(1)}, bf16[64,2048]{1,0:T(8,128)(2,1)S(1)}, u32[]{:S(2)}, u32[]{:S(2)}) %collective-permute-start.25) | collective-permute-done | bytes 262176 | tf_op jit(solution)/shard_map/ppermute | solution.py:58
  87.8 3.8 %collective-permute-done.28 = bf16[64,2048]{1,0:T(8,128)(2,1)S(1)} collective-permute-done((bf16[64,2048]{1,0:T(8,128)(2,1)S(1)}, bf16[64,2048]{1,0:T(8,128)(2,1)S(1)}, u32[]{:S(2)}, u32[]{:S(2)}) %collective-permute-start.28) | collective-permute-done | bytes 262176 | tf_op jit(solution)/shard_map/ppermute | solution.py:54
  91.7 1.1 add_convert_fusion.2
  92.7 0.1 collective-permute-start.29
  92.8 0.1 add_convert_fusion.10
  92.9 1.2 collective-permute-start.21
  94.1 6.1 %collective-permute-done.29 = bf16[64,2048]{1,0:T(8,128)(2,1)S(1)} collective-permute-done((bf16[64,2048]{1,0:T(8,128)(2,1)S(1)}, bf16[64,2048]{1,0:T(8,128)(2,1)S(1)}, u32[]{:S(2)}, u32[]{:S(2)}) %collective-permute-start.29) | collective-permute-done | bytes 262176 | tf_op jit(solution)/shard_map/ppermute | solution.py:54
  100.2 0.1 add_convert_fusion.1
  100.3 0.2 collective-permute-start.30
  100.6 0.9 copy-done.2
  101.5 5.0 %values.1 = (bf16[1024,256]{1,0:T(8,128)(2,1)}, bf16[1024,256]{1,0:T(8,128)(2,1)}) custom-call(bf16[64,2176]{1,0:T(8,128)(2,1)} %normalize_and_pack.1.refs_0_, bf16[64,2176]{1,0:T(8,128)(2,1)} %copy-done.8, bf16[64,2176]{1,0:T(8,128)(2,1)} %copy-done.9, bf16[64,2176]{1,0:T(8,128)(2,1)} %copy-done.11, bf16[64,2176]{1,0:T(8,128)(2,1)} %copy-done.6, ...), custom_call_target="tpu_custom_call" | custom-call | flops 1073741824 | bytes 5242880 | tf_op jit(solution)/shard_map/values/pallas_call | solution.py:317
  106.5 0.0 copy-start
  106.5 2.9 %attention.4.refs_0_ = bf16[64,4096]{1,0:T(8,128)(2,1)} custom-call(bf16[64,4096]{1,0:T(8,128)(2,1)} %bitcast.17, bf16[1024,256]{1,0:T(8,128)(2,1)} %get-tuple-element.12.k_ref, bf16[1024,256]{1,0:T(8,128)(2,1)} %get-tuple-element.13.v_ref), custom_call_target="tpu_custom_call" | custom-call | flops 268435456 | bytes 786432 | tf_op jit(solution)/shard_map/attention/pallas_call | solution.py:409
  109.5 2.9 %attention.5.refs_0_ = bf16[64,4096]{1,0:T(8,128)(2,1)} custom-call(bf16[64,4096]{1,0:T(8,128)(2,1)} %bitcast.18, bf16[1024,256]{1,0:T(8,128)(2,1)} %get-tuple-element.12.k_ref, bf16[1024,256]{1,0:T(8,128)(2,1)} %get-tuple-element.13.v_ref, bf16[64,4096]{1,0:T(8,128)(2,1)} %attention.4.refs_0_), custom_call_target="tpu_custom_call", output_to_operand_aliasing={{}: (3, {})} | custom-call | flops 268435456 | bytes 786432 | tf_op jit(solution)/shard_map/attention/pallas_call | solution.py:409
  112.3 2.9 %attention.6.refs_0_ = bf16[64,4096]{1,0:T(8,128)(2,1)} custom-call(bf16[64,4096]{1,0:T(8,128)(2,1)} %bitcast.19, bf16[1024,256]{1,0:T(8,128)(2,1)} %get-tuple-element.12.k_ref, bf16[1024,256]{1,0:T(8,128)(2,1)} %get-tuple-element.13.v_ref, bf16[64,4096]{1,0:T(8,128)(2,1)} %attention.5.refs_0_), custom_call_target="tpu_custom_call", output_to_operand_aliasing={{}: (3, {})} | custom-call | flops 268435456 | bytes 786432 | tf_op jit(solution)/shard_map/attention/pallas_call | solution.py:409
  115.2 2.9 %attention.7 = bf16[64,4096]{1,0:T(8,128)(2,1)} custom-call(bf16[64,4096]{1,0:T(8,128)(2,1)} %bitcast.20, bf16[1024,256]{1,0:T(8,128)(2,1)} %get-tuple-element.12.k_ref, bf16[1024,256]{1,0:T(8,128)(2,1)} %get-tuple-element.13.v_ref, bf16[64,4096]{1,0:T(8,128)(2,1)} %attention.6.refs_0_), custom_call_target="tpu_custom_call", output_to_operand_aliasing={{}: (3, {})} | custom-call | flops 268435456 | bytes 786432 | tf_op jit(solution)/shard_map/attention/pallas_call | solution.py:409
  118.1 0.9 fusion
  (63 shorter events, 0.2 us)
Async XLA Ops:
  2.5 10.9 %collective-permute-start.3 = (bf16[64,2176]{1,0:T(8,128)(2,1)}, bf16[64,2176]{1,0:T(8,128)(2,1)S(1)}, u32[]{:S(2)}, u32[]{:S(2)}) collective-permute-start(bf16[64,2176]{1,0:T(8,128)(2,1)} %normalize_and_pack.1.refs_0_), channel_id=1, source_target_pairs={{0,4},{1,5},{2,6},{3,7},{4,12},{5,13},{6,14},{7,15},{12,8},{13,9},... | collective-permute-start | bytes 835592 | tf_op jit(solution)/shard_map/ppermute | solution.py:54
  13.4 37.7 %copy-start.6 = (bf16[64,2176]{1,0:T(8,128)(2,1)}, bf16[64,2176]{1,0:T(8,128)(2,1)S(1)}, u32[]{:S(2)}) copy-start(bf16[64,2176]{1,0:T(8,128)(2,1)S(1)} %collective-permute-done.3.refs_4_) | copy-start | bytes 835588
  13.4 8.7 %collective-permute-start.7 = (bf16[64,2176]{1,0:T(8,128)(2,1)S(1)}, bf16[64,2176]{1,0:T(8,128)(2,1)S(1)}, u32[]{:S(2)}, u32[]{:S(2)}) collective-permute-start(bf16[64,2176]{1,0:T(8,128)(2,1)S(1)} %collective-permute-done.3.refs_4_), channel_id=1, source_target_pairs={{0,4},{1,5},{2,6},{3,7},{4,12},{5,13},{6,14},{7,15},{12,8},{13,9},... | collective-permute-start | bytes 835592 | tf_op jit(solution)/shard_map/ppermute | solution.py:54
  15.2 7.5 %collective-permute-start.15 = (bf16[192,256]{1,0:T(8,128)(2,1)S(1)}, bf16[192,256]{1,0:T(8,128)(2,1)S(1)}, u32[]{:S(2)}, u32[]{:S(2)}) collective-permute-start(bf16[192,256]{1,0:T(8,128)(2,1)S(1)} %pad_maximum_fusion.1), channel_id=1, source_target_pairs={{0,2},{1,3},{2,0},{3,1},{4,6},{5,7},{6,4},{7,5},{12,14},{13,15},{1... | collective-permute-start | bytes 294920 | tf_op jit(solution)/shard_map/ppermute | solution.py:58
  16.8 10.2 %collective-permute-start = (bf16[64,2176]{1,0:T(8,128)(2,1)}, bf16[64,2176]{1,0:T(8,128)(2,1)S(1)}, u32[]{:S(2)}, u32[]{:S(2)}) collective-permute-start(bf16[64,2176]{1,0:T(8,128)(2,1)} %normalize_and_pack.1.refs_0_), channel_id=1, source_target_pairs={{0,2},{1,3},{2,0},{3,1},{4,6},{5,7},{6,4},{7,5},{12,14},{13,15},{1... | collective-permute-start | bytes 835592 | tf_op jit(solution)/shard_map/ppermute | solution.py:58
  17.3 11.3 %collective-permute-start.1 = (bf16[64,2176]{1,0:T(8,128)(2,1)}, bf16[64,2176]{1,0:T(8,128)(2,1)S(1)}, u32[]{:S(2)}, u32[]{:S(2)}) collective-permute-start(bf16[64,2176]{1,0:T(8,128)(2,1)} %normalize_and_pack.1.refs_0_), channel_id=1, source_target_pairs={{0,1},{1,0},{2,3},{3,2},{4,5},{5,4},{6,7},{7,6},{12,13},{13,12},{1... | collective-permute-start | bytes 835592 | tf_op jit(solution)/shard_map/ppermute | solution.py:62
  22.1 28.9 %copy-start.7 = (bf16[64,2176]{1,0:T(8,128)(2,1)}, bf16[64,2176]{1,0:T(8,128)(2,1)S(1)}, u32[]{:S(2)}) copy-start(bf16[64,2176]{1,0:T(8,128)(2,1)S(1)} %collective-permute-done.7.refs_8_) | copy-start | bytes 835588
  22.1 13.1 %collective-permute-start.11 = (bf16[64,2176]{1,0:T(8,128)(2,1)S(1)}, bf16[64,2176]{1,0:T(8,128)(2,1)S(1)}, u32[]{:S(2)}, u32[]{:S(2)}) collective-permute-start(bf16[64,2176]{1,0:T(8,128)(2,1)S(1)} %collective-permute-done.7.refs_8_), channel_id=1, source_target_pairs={{0,4},{1,5},{2,6},{3,7},{4,12},{5,13},{6,14},{7,15},{12,8},{13,9},... | collective-permute-start | bytes 835592 | tf_op jit(solution)/shard_map/ppermute | solution.py:54
  23.5 10.8 %collective-permute-start.16 = (bf16[384,256]{1,0:T(8,128)(2,1)S(1)}, bf16[384,256]{1,0:T(8,128)(2,1)}, u32[]{:S(2)}, u32[]{:S(2)}) collective-permute-start(bf16[384,256]{1,0:T(8,128)(2,1)S(1)} %pad_maximum_fusion), channel_id=1, source_target_pairs={{0,4},{1,5},{2,6},{3,7},{4,12},{5,13},{6,14},{7,15},{12,8},{13,9},... | collective-permute-start | bytes 589832 | tf_op jit(solution)/shard_map/ppermute | solution.py:54
  26.9 24.1 %copy-start.8 = (bf16[64,2176]{1,0:T(8,128)(2,1)}, bf16[64,2176]{1,0:T(8,128)(2,1)S(1)}, u32[]{:S(2)}) copy-start(bf16[64,2176]{1,0:T(8,128)(2,1)S(1)} %collective-permute-done.refs_1_) | copy-start | bytes 835588
  26.9 9.4 %collective-permute-start.2 = (bf16[64,2176]{1,0:T(8,128)(2,1)S(1)}, bf16[64,2176]{1,0:T(8,128)(2,1)S(1)}, u32[]{:S(2)}, u32[]{:S(2)}) collective-permute-start(bf16[64,2176]{1,0:T(8,128)(2,1)S(1)} %collective-permute-done.refs_1_), channel_id=1, source_target_pairs={{0,1},{1,0},{2,3},{3,2},{4,5},{5,4},{6,7},{7,6},{12,13},{13,12},{1... | collective-permute-start | bytes 835592 | tf_op jit(solution)/shard_map/ppermute | solution.py:62
  27.0 9.5 %collective-permute-start.4 = (bf16[64,2176]{1,0:T(8,128)(2,1)S(1)}, bf16[64,2176]{1,0:T(8,128)(2,1)S(1)}, u32[]{:S(2)}, u32[]{:S(2)}) collective-permute-start(bf16[64,2176]{1,0:T(8,128)(2,1)S(1)} %collective-permute-done.3.refs_4_), channel_id=1, source_target_pairs={{0,2},{1,3},{2,0},{3,1},{4,6},{5,7},{6,4},{7,5},{12,14},{13,15},{1... | collective-permute-start | bytes 835592 | tf_op jit(solution)/shard_map/ppermute | solution.py:58
  28.5 22.5 %copy-start.9 = (bf16[64,2176]{1,0:T(8,128)(2,1)}, bf16[64,2176]{1,0:T(8,128)(2,1)S(1)}, u32[]{:S(2)}) copy-start(bf16[64,2176]{1,0:T(8,128)(2,1)S(1)} %collective-permute-done.1.refs_2_) | copy-start | bytes 835588
  28.5 8.3 %collective-permute-start.5 = (bf16[64,2176]{1,0:T(8,128)(2,1)S(1)}, bf16[64,2176]{1,0:T(8,128)(2,1)S(1)}, u32[]{:S(2)}, u32[]{:S(2)}) collective-permute-start(bf16[64,2176]{1,0:T(8,128)(2,1)S(1)} %collective-permute-done.3.refs_4_), channel_id=1, source_target_pairs={{0,1},{1,0},{2,3},{3,2},{4,5},{5,4},{6,7},{7,6},{12,13},{13,12},{1... | collective-permute-start | bytes 835592 | tf_op jit(solution)/shard_map/ppermute | solution.py:62
  34.3 9.6 %collective-permute-start.8 = (bf16[64,2176]{1,0:T(8,128)(2,1)S(1)}, bf16[64,2176]{1,0:T(8,128)(2,1)S(1)}, u32[]{:S(2)}, u32[]{:S(2)}) collective-permute-start(bf16[64,2176]{1,0:T(8,128)(2,1)S(1)} %collective-permute-done.7.refs_8_), channel_id=1, source_target_pairs={{0,2},{1,3},{2,0},{3,1},{4,6},{5,7},{6,4},{7,5},{12,14},{13,15},{1... | collective-permute-start | bytes 835592 | tf_op jit(solution)/shard_map/ppermute | solution.py:58
  35.2 15.9 %copy-start.10 = (bf16[64,2176]{1,0:T(8,128)(2,1)}, bf16[64,2176]{1,0:T(8,128)(2,1)S(1)}, u32[]{:S(2)}) copy-start(bf16[64,2176]{1,0:T(8,128)(2,1)S(1)} %collective-permute-done.11.refs_12_) | copy-start | bytes 835588
  35.2 12.8 %collective-permute-start.12 = (bf16[64,2176]{1,0:T(8,128)(2,1)S(1)}, bf16[64,2176]{1,0:T(8,128)(2,1)S(1)}, u32[]{:S(2)}, u32[]{:S(2)}) collective-permute-start(bf16[64,2176]{1,0:T(8,128)(2,1)S(1)} %collective-permute-done.11.refs_12_), channel_id=1, source_target_pairs={{0,2},{1,3},{2,0},{3,1},{4,6},{5,7},{6,4},{7,5},{12,14},{13,15},{1... | collective-permute-start | bytes 835592 | tf_op jit(solution)/shard_map/ppermute | solution.py:58
  36.3 14.8 %copy-start.11 = (bf16[64,2176]{1,0:T(8,128)(2,1)}, bf16[64,2176]{1,0:T(8,128)(2,1)S(1)}, u32[]{:S(2)}) copy-start(bf16[64,2176]{1,0:T(8,128)(2,1)S(1)} %collective-permute-done.2.refs_3_) | copy-start | bytes 835588
  36.3 13.7 %collective-permute-start.9 = (bf16[64,2176]{1,0:T(8,128)(2,1)S(1)}, bf16[64,2176]{1,0:T(8,128)(2,1)S(1)}, u32[]{:S(2)}, u32[]{:S(2)}) collective-permute-start(bf16[64,2176]{1,0:T(8,128)(2,1)S(1)} %collective-permute-done.7.refs_8_), channel_id=1, source_target_pairs={{0,1},{1,0},{2,3},{3,2},{4,5},{5,4},{6,7},{7,6},{12,13},{13,12},{1... | collective-permute-start | bytes 835592 | tf_op jit(solution)/shard_map/ppermute | solution.py:62
  36.5 14.6 %copy-start.12 = (bf16[64,2176]{1,0:T(8,128)(2,1)}, bf16[64,2176]{1,0:T(8,128)(2,1)S(1)}, u32[]{:S(2)}) copy-start(bf16[64,2176]{1,0:T(8,128)(2,1)S(1)} %collective-permute-done.4.refs_5_) | copy-start | bytes 835588
  36.5 12.2 %collective-permute-start.6 = (bf16[64,2176]{1,0:T(8,128)(2,1)S(1)}, bf16[64,2176]{1,0:T(8,128)(2,1)S(1)}, u32[]{:S(2)}, u32[]{:S(2)}) collective-permute-start(bf16[64,2176]{1,0:T(8,128)(2,1)S(1)} %collective-permute-done.4.refs_5_), channel_id=1, source_target_pairs={{0,1},{1,0},{2,3},{3,2},{4,5},{5,4},{6,7},{7,6},{12,13},{13,12},{1... | collective-permute-start | bytes 835592 | tf_op jit(solution)/shard_map/ppermute | solution.py:62
  36.8 14.3 %copy-start.13 = (bf16[64,2176]{1,0:T(8,128)(2,1)}, bf16[64,2176]{1,0:T(8,128)(2,1)S(1)}, u32[]{:S(2)}) copy-start(bf16[64,2176]{1,0:T(8,128)(2,1)S(1)} %collective-permute-done.5.refs_6_) | copy-start | bytes 835588
  36.8 13.2 %collective-permute-start.13 = (bf16[64,2176]{1,0:T(8,128)(2,1)S(1)}, bf16[64,2176]{1,0:T(8,128)(2,1)S(1)}, u32[]{:S(2)}, u32[]{:S(2)}) collective-permute-start(bf16[64,2176]{1,0:T(8,128)(2,1)S(1)} %collective-permute-done.11.refs_12_), channel_id=1, source_target_pairs={{0,1},{1,0},{2,3},{3,2},{4,5},{5,4},{6,7},{7,6},{12,13},{13,12},{1... | collective-permute-start | bytes 835592 | tf_op jit(solution)/shard_map/ppermute | solution.py:62
  43.9 7.2 %copy-start.14 = (bf16[64,2176]{1,0:T(8,128)(2,1)}, bf16[64,2176]{1,0:T(8,128)(2,1)S(1)}, u32[]{:S(2)}) copy-start(bf16[64,2176]{1,0:T(8,128)(2,1)S(1)} %collective-permute-done.8.refs_9_) | copy-start | bytes 835588
  43.9 6.2 %collective-permute-start.10 = (bf16[64,2176]{1,0:T(8,128)(2,1)S(1)}, bf16[64,2176]{1,0:T(8,128)(2,1)S(1)}, u32[]{:S(2)}, u32[]{:S(2)}) collective-permute-start(bf16[64,2176]{1,0:T(8,128)(2,1)S(1)} %collective-permute-done.8.refs_9_), channel_id=1, source_target_pairs={{0,1},{1,0},{2,3},{3,2},{4,5},{5,4},{6,7},{7,6},{12,13},{13,12},{1... | collective-permute-start | bytes 835592 | tf_op jit(solution)/shard_map/ppermute | solution.py:62
  48.0 3.2 %copy-start.15 = (bf16[64,2176]{1,0:T(8,128)(2,1)}, bf16[64,2176]{1,0:T(8,128)(2,1)S(1)}, u32[]{:S(2)}) copy-start(bf16[64,2176]{1,0:T(8,128)(2,1)S(1)} %collective-permute-done.12.refs_13_) | copy-start | bytes 835588
  48.0 2.1 %collective-permute-start.14 = (bf16[64,2176]{1,0:T(8,128)(2,1)S(1)}, bf16[64,2176]{1,0:T(8,128)(2,1)S(1)}, u32[]{:S(2)}, u32[]{:S(2)}) collective-permute-start(bf16[64,2176]{1,0:T(8,128)(2,1)S(1)} %collective-permute-done.12.refs_13_), channel_id=1, source_target_pairs={{0,1},{1,0},{2,3},{3,2},{4,5},{5,4},{6,7},{7,6},{12,13},{13,12},{1... | collective-permute-start | bytes 835592 | tf_op jit(solution)/shard_map/ppermute | solution.py:62
  48.7 1.4 %copy-start.17 = (bf16[64,2176]{1,0:T(8,128)(2,1)}, bf16[64,2176]{1,0:T(8,128)(2,1)S(1)}, u32[]{:S(2)}) copy-start(bf16[64,2176]{1,0:T(8,128)(2,1)S(1)} %collective-permute-done.6.refs_7_) | copy-start | bytes 835588
  48.7 14.4 %collective-permute-start.17 = (bf16[384,256]{1,0:T(8,128)(2,1)}, bf16[384,256]{1,0:T(8,128)(2,1)}, u32[]{:S(2)}, u32[]{:S(2)}) collective-permute-start(bf16[384,256]{1,0:T(8,128)(2,1)} %collective-permute-done.16), channel_id=1, source_target_pairs={{0,4},{1,5},{2,6},{3,7},{4,12},{5,13},{6,14},{7,15},{12,8},{13,9},... | collective-permute-start | bytes 589832 | tf_op jit(solution)/shard_map/ppermute | solution.py:54
  50.1 1.1 copy-start.16
  50.1 0.8 copy-start.19
  50.1 0.9 copy-start.18
  50.1 0.9 copy-start.20
  51.1 11.9 %copy-start.3 = (bf16[128,256]{1,0:T(8,128)(2,1)S(1)}, bf16[128,256]{1,0:T(8,128)(2,1)}, u32[]{:S(2)}) copy-start(bf16[128,256]{1,0:T(8,128)(2,1)} %param.13) | copy-start | bytes 196612
  62.7 30.1 %copy-start.5 = (bf16[128,2048]{1,0:T(8,128)(2,1)S(1)}, bf16[128,2048]{1,0:T(8,128)(2,1)}, u32[]{:S(2)}) copy-start(bf16[128,2048]{1,0:T(8,128)(2,1)} %get-tuple-element.14) | copy-start | bytes 1572868
  62.8 37.4 %copy-start.4 = (bf16[128,2048]{1,0:T(8,128)(2,1)S(1)}, bf16[128,2048]{1,0:T(8,128)(2,1)}, u32[]{:S(2)}) copy-start(bf16[128,2048]{1,0:T(8,128)(2,1)} %get-tuple-element.16) | copy-start | bytes 1572868
  62.8 9.3 %collective-permute-start.26 = (bf16[128,2048]{1,0:T(8,128)(2,1)}, bf16[128,2048]{1,0:T(8,128)(2,1)S(1)}, u32[]{:S(2)}, u32[]{:S(2)}) collective-permute-start(bf16[128,2048]{1,0:T(8,128)(2,1)} %get-tuple-element.21), channel_id=1, source_target_pairs={{0,1},{1,0},{2,3},{3,2},{4,5},{5,4},{6,7},{7,6},{12,13},{13,12},{1... | collective-permute-start | bytes 1572872 | tf_op jit(solution)/shard_map/ppermute | solution.py:62
  63.1 8.2 %collective-permute-start.18 = (bf16[384,256]{1,0:T(8,128)(2,1)}, bf16[384,256]{1,0:T(8,128)(2,1)S(1)}, u32[]{:S(2)}, u32[]{:S(2)}) collective-permute-start(bf16[384,256]{1,0:T(8,128)(2,1)} %collective-permute-done.17), channel_id=1, source_target_pairs={{0,4},{1,5},{2,6},{3,7},{4,12},{5,13},{6,14},{7,15},{12,8},{13,9},... | collective-permute-start | bytes 589832 | tf_op jit(solution)/shard_map/ppermute | solution.py:54
  65.5 8.8 %collective-permute-start.24 = (bf16[128,2048]{1,0:T(8,128)(2,1)}, bf16[128,2048]{1,0:T(8,128)(2,1)S(1)}, u32[]{:S(2)}, u32[]{:S(2)}) collective-permute-start(bf16[128,2048]{1,0:T(8,128)(2,1)} %get-tuple-element.19), channel_id=1, source_target_pairs={{0,1},{1,0},{2,3},{3,2},{4,5},{5,4},{6,7},{7,6},{12,13},{13,12},{1... | collective-permute-start | bytes 1572872 | tf_op jit(solution)/shard_map/ppermute | solution.py:62
  71.4 29.2 %copy-start.1 = (bf16[1536,256]{1,0:T(8,128)(2,1)}, bf16[1536,256]{1,0:T(8,128)(2,1)S(1)}, u32[]{:S(2)}) copy-start(bf16[1536,256]{1,0:T(8,128)(2,1)S(1)} %constant_dynamic-update-slice_fusion.refs_16_) | copy-start | bytes 2359300
  71.4 29.2 %collective-permute-start.19 = (bf16[1536,256]{1,0:T(8,128)(2,1)S(1)}, bf16[1536,256]{1,0:T(8,128)(2,1)S(1)}, u32[]{:S(2)}, u32[]{:S(2)}) collective-permute-start(bf16[1536,256]{1,0:T(8,128)(2,1)S(1)} %constant_dynamic-update-slice_fusion.refs_16_), channel_id=1, source_target_pairs={{0,1},{1,0},{2,3},{3,2},{4,5},{5,4},{6,7},{7,6},{12,13},{13,12},{1... | collective-permute-start | bytes 2359304 | tf_op jit(solution)/shard_map/ppermute | solution.py:62
  71.5 11.9 %collective-permute-start.22 = (bf16[128,2048]{1,0:T(8,128)(2,1)}, bf16[128,2048]{1,0:T(8,128)(2,1)S(1)}, u32[]{:S(2)}, u32[]{:S(2)}) collective-permute-start(bf16[128,2048]{1,0:T(8,128)(2,1)} %get-tuple-element.17), channel_id=1, source_target_pairs={{0,1},{1,0},{2,3},{3,2},{4,5},{5,4},{6,7},{7,6},{12,13},{13,12},{1... | collective-permute-start | bytes 1572872 | tf_op jit(solution)/shard_map/ppermute | solution.py:62
  72.0 20.9 %collective-permute-start.20 = (bf16[128,2048]{1,0:T(8,128)(2,1)}, bf16[128,2048]{1,0:T(8,128)(2,1)S(1)}, u32[]{:S(2)}, u32[]{:S(2)}) collective-permute-start(bf16[128,2048]{1,0:T(8,128)(2,1)} %get-tuple-element.15), channel_id=1, source_target_pairs={{0,1},{1,0},{2,3},{3,2},{4,5},{5,4},{6,7},{7,6},{12,13},{13,12},{1... | collective-permute-start | bytes 1572872 | tf_op jit(solution)/shard_map/ppermute | solution.py:62
  73.1 9.2 %collective-permute-start.27 = (bf16[64,2048]{1,0:T(8,128)(2,1)S(1)}, bf16[64,2048]{1,0:T(8,128)(2,1)S(1)}, u32[]{:S(2)}, u32[]{:S(2)}) collective-permute-start(bf16[64,2048]{1,0:T(8,128)(2,1)S(1)} %add_convert_fusion.4), channel_id=1, source_target_pairs={{0,2},{1,3},{2,0},{3,1},{4,6},{5,7},{6,4},{7,5},{12,14},{13,15},{1... | collective-permute-start | bytes 786440 | tf_op jit(solution)/shard_map/ppermute | solution.py:58
  75.3 12.6 %collective-permute-start.25 = (bf16[64,2048]{1,0:T(8,128)(2,1)S(1)}, bf16[64,2048]{1,0:T(8,128)(2,1)S(1)}, u32[]{:S(2)}, u32[]{:S(2)}) collective-permute-start(bf16[64,2048]{1,0:T(8,128)(2,1)S(1)} %add_convert_fusion.6), channel_id=1, source_target_pairs={{0,2},{1,3},{2,0},{3,1},{4,6},{5,7},{6,4},{7,5},{12,14},{13,15},{1... | collective-permute-start | bytes 786440 | tf_op jit(solution)/shard_map/ppermute | solution.py:58
  83.3 8.4 %collective-permute-start.28 = (bf16[64,2048]{1,0:T(8,128)(2,1)S(1)}, bf16[64,2048]{1,0:T(8,128)(2,1)S(1)}, u32[]{:S(2)}, u32[]{:S(2)}) collective-permute-start(bf16[64,2048]{1,0:T(8,128)(2,1)S(1)} %add_convert_fusion.3), channel_id=1, source_target_pairs={{0,4},{1,5},{2,6},{3,7},{4,12},{5,13},{6,14},{7,15},{12,8},{13,9},... | collective-permute-start | bytes 786440 | tf_op jit(solution)/shard_map/ppermute | solution.py:54
  84.4 9.7 %collective-permute-start.23 = (bf16[64,2048]{1,0:T(8,128)(2,1)S(1)}, bf16[64,2048]{1,0:T(8,128)(2,1)S(1)}, u32[]{:S(2)}, u32[]{:S(2)}) collective-permute-start(bf16[64,2048]{1,0:T(8,128)(2,1)S(1)} %add_convert_fusion.8), channel_id=1, source_target_pairs={{0,2},{1,3},{2,0},{3,1},{4,6},{5,7},{6,4},{7,5},{12,14},{13,15},{1... | collective-permute-start | bytes 786440 | tf_op jit(solution)/shard_map/ppermute | solution.py:58
  92.7 7.5 %collective-permute-start.29 = (bf16[64,2048]{1,0:T(8,128)(2,1)S(1)}, bf16[64,2048]{1,0:T(8,128)(2,1)S(1)}, u32[]{:S(2)}, u32[]{:S(2)}) collective-permute-start(bf16[64,2048]{1,0:T(8,128)(2,1)S(1)} %add_convert_fusion.2), channel_id=1, source_target_pairs={{0,4},{1,5},{2,6},{3,7},{4,12},{5,13},{6,14},{7,15},{12,8},{13,9},... | collective-permute-start | bytes 786440 | tf_op jit(solution)/shard_map/ppermute | solution.py:54
  92.9 25.2 %collective-permute-start.21 = (bf16[64,2048]{1,0:T(8,128)(2,1)S(1)}, bf16[64,2048]{1,0:T(8,128)(2,1)S(1)}, u32[]{:S(2)}, u32[]{:S(2)}) collective-permute-start(bf16[64,2048]{1,0:T(8,128)(2,1)S(1)} %add_convert_fusion.10), channel_id=1, source_target_pairs={{0,2},{1,3},{2,0},{3,1},{4,6},{5,7},{6,4},{7,5},{12,14},{13,15},{1... | collective-permute-start | bytes 786440 | tf_op jit(solution)/shard_map/ppermute | solution.py:58
  100.3 17.8 %collective-permute-start.30 = (bf16[64,2048]{1,0:T(8,128)(2,1)S(1)}, bf16[64,2048]{1,0:T(8,128)(2,1)S(1)}, u32[]{:S(2)}, u32[]{:S(2)}) collective-permute-start(bf16[64,2048]{1,0:T(8,128)(2,1)S(1)} %add_convert_fusion.1), channel_id=1, source_target_pairs={{0,4},{1,5},{2,6},{3,7},{4,12},{5,13},{6,14},{7,15},{12,8},{13,9},... | collective-permute-start | bytes 786440 | tf_op jit(solution)/shard_map/ppermute | solution.py:54
  100.6 0.9 copy-start.2
  106.5 11.6 %copy-start = (bf16[64,1,2048]{2,0,1:T(8,128)(2,1)S(1)}, bf16[64,1,2048]{2,0,1:T(8,128)(2,1)}, u32[]{:S(2)}) copy-start(bf16[64,1,2048]{2,0,1:T(8,128)(2,1)} %param.9) | copy-start | bytes 786436

commit v3 on v2

--- a/solution.py
+++ b/solution.py
@@ -73,7 +73,9 @@
     return (line * 2 + y) * 2 + core
 
 
-def pack_kernel(act_ref, gain_ref, ids_ref, gates_ref, out_ref, meta_ref):
+def pack_kernel(
+    act_ref, gain_ref, ids_ref, gates_ref, key_ref, weight_ref, out_ref, small_ref, meta_ref
+):
     width = act_ref.shape[1]
     rows = act_ref.shape[0]
     top = ids_ref.shape[0]
@@ -90,20 +92,26 @@
     meta_ref[16 : 16 + top, 0:rows] = middle
     meta_ref[24 : 24 + top, 0:rows] = rest - middle
     out_ref[:, width:] = meta_ref[...].T[:rows, :].astype(BF16)
-
-
-def pack(activations, norm_gain, ids, gates):
+    small_ref[:rows] = key_ref[...]
+    small_ref[rows:] = weight_ref[...]
+
+
+def pack(activations, norm_gain, ids, gates, keys, value_weight):
     rows, width = activations.shape
+    small_rows = rows + value_weight.shape[0]
     assert rows <= META and ids.shape[0] <= 8
     return pl.pallas_call(
         pack_kernel,
-        out_shape=jax.ShapeDtypeStruct((rows, width + META), BF16),
+        out_shape=[
+            jax.ShapeDtypeStruct((rows, width + META), BF16),
+            jax.ShapeDtypeStruct((small_rows, keys.shape[1]), BF16),
+        ],
         scratch_shapes=[pltpu.VMEM((META, META), F32)],
         cost_estimate=pl.CostEstimate(
             flops=4 * rows * width, bytes_accessed=4 * rows * width, transcendentals=0
         ),
         name="normalize_and_pack",
-    )(activations, norm_gain.reshape(1, width), ids, gates)
+    )(activations, norm_gain.reshape(1, width), ids, gates, keys, value_weight)
 
 
 def expert_kernel(top, tok_rows, capacity, sources, targets, *refs):
@@ -310,7 +318,8 @@
     value_ref[...] = dot(x_buf[...], weight[...]).astype(BF16)
 
 
-def make_values(arrays, blocks, smalls, small_blocks, key_rows, width):
+def make_values(arrays, blocks, smalls, small_blocks, key_rows, width, earlier):
+    smalls = [after(smalls[0], earlier), *smalls[1:]]
     kv_width = smalls[0].shape[1]
     total = key_rows * len(blocks)
     kv = jax.ShapeDtypeStruct((total, kv_width), BF16)
@@ -397,94 +406,113 @@
             ]
 
 
-def attend_all(queries, keys, values, parts):
+def attend_part(queries, keys, values, part, parts, context=None):
     q_rows, q_width = queries.shape
     total = keys.shape[0]
     part_width = q_width // parts
     per_kv = parts // KEY_VALUE_HEADS
     chunk = math.gcd(total, 1024)
-    context = ()
-    for part in range(parts):
-        context = (
-            pl.pallas_call(
-                functools.partial(attention_kernel, chunk),
-                grid=(1,),
-                out_shape=jax.ShapeDtypeStruct((q_rows, q_width), BF16),
-                in_specs=[
-                    pl.BlockSpec((q_rows, part_width), lambda i, part=part: (0, part)),
-                    pl.BlockSpec((total, HEAD_DIMENSION), lambda i, part=part: (0, part // per_kv)),
-                    pl.BlockSpec((total, HEAD_DIMENSION), lambda i, part=part: (0, part // per_kv)),
-                    *[ANY for _ in context],
-                ],
-                out_specs=pl.BlockSpec((q_rows, part_width), lambda i, part=part: (0, part)),
-                input_output_aliases={3: 0} if context else {},
-                compiler_params=pltpu.CompilerParams(vmem_limit_bytes=VMEM_LIMIT),
-                cost_estimate=pl.CostEstimate(
-                    flops=4 * q_rows * part_width * total,
-                    bytes_accessed=4 * total * HEAD_DIMENSION + 4 * q_rows * part_width,
-                    transcendentals=part_width // HEAD_DIMENSION * q_rows * total,
-                ),
-                name="attention",
-            )(queries, keys, values, *context),
-        )
-    return context[0]
+    before = () if context is None else (context,)
+    return pl.pallas_call(
+        functools.partial(attention_kernel, chunk),
+        grid=(1,),
+        out_shape=jax.ShapeDtypeStruct((q_rows, q_width), BF16),
+        in_specs=[
+            pl.BlockSpec((q_rows, part_width), lambda i: (0, part)),
+            pl.BlockSpec((total, HEAD_DIMENSION), lambda i: (0, part // per_kv)),
+            pl.BlockSpec((total, HEAD_DIMENSION), lambda i: (0, part // per_kv)),
+            *[ANY for _ in before],
+        ],
+        out_specs=pl.BlockSpec((q_rows, part_width), lambda i: (0, part)),
+        input_output_aliases={3: 0} if before else {},
+        compiler_params=pltpu.CompilerParams(vmem_limit_bytes=VMEM_LIMIT),
+        cost_estimate=pl.CostEstimate(
+            flops=4 * q_rows * part_width * total,
+            bytes_accessed=4 * total * HEAD_DIMENSION + 4 * q_rows * part_width,
+            transcendentals=part_width // HEAD_DIMENSION * q_rows * total,
+        ),
+        name="attention",
+    )(queries, keys, values, *before)
 
 
 def summed(*terms):
     return sum(term.astype(F32) for term in terms).astype(BF16)
 
 
-def on_line(acts, packed, keys, value_weight, queries, w_gate_up, w_down, top, capacity):
+def after(x, *others):
+    return lax.optimization_barrier((x, *others))[0]
+
+
+def on_line(acts, packed, small, queries, w_gate_up, w_down, top, capacity):
     rows, width = acts.shape
-    pair = jnp.concatenate([keys, value_weight], axis=0)
-    small_rows = pair.shape[0]
-    pair = jnp.concatenate([pair, across(pair)], axis=0)
-    small = [pair]
-    for _ in range(LINE - 1):
-        small.append(along_ring(small[-1]))
-    own_core = jnp.concatenate(small, axis=0)
-    small = [own_core, other_core(own_core)]
-    small_blocks = [
-        (core, (step * 2 + y) * small_rows, functools.partial(from_device, step, y, core))
-        for core in range(2)
-        for step in range(LINE)
-        for y in range(2)
-    ]
-    arrays, blocks, sources, targets = [], [], [], []
+    arrays, blocks, sources = [], [], []
     moving = packed
+    pair = jnp.concatenate([small, across(small)], axis=0)
     for step in range(LINE):
-        if step > 0:
+        if step == 1:
             moving = along_ring(moving)
+        elif step == 2:
+            moving = along_ring(after(moving, pair, arrays[1]))
+        elif step > 2:
+            moving = along_ring(after(moving, arrays[4 * step - 7], *arrays[4 * step - 10 : 4 * step - 8]))
         crossed = across(moving)
         arrays += [moving, crossed, other_core(moving), other_core(crossed)]
         sources.append([(4 * step + i, 0, rows) for i in range(4)])
-        targets.append([(2 * step + i, 0, 2 * rows) for i in range(2)])
         blocks += [
             (4 * step + core * 2 + y, 0, functools.partial(from_device, step, y, core))
             for core in range(2)
             for y in range(2)
         ]
-    partial = run_experts(
-        arrays, sources, targets, [2 * rows] * (2 * LINE), w_gate_up, w_down, top, rows, capacity
-    )
-    new_keys, values = make_values(arrays, blocks, small, small_blocks, rows, width)
-    context = attend_all(queries, new_keys, values, 4)
-    moving = None
-    for step in (1, 2, 3, 0):
-        keep, send = partial[2 * step], partial[2 * step + 1]
-        came = other_core(send)
-        mine = summed(keep[:rows], came[:rows])
-        theirs = across(summed(keep[rows:], came[rows:]))
-        if step == 0:
-            break
-        total = summed(mine, theirs) if moving is None else summed(mine, theirs, moving)
-        moving = along_ring(total)
-    layer_out = summed(acts, mine, theirs, moving)
+    small_rows = small.shape[0]
+    pair = after(pair, moving, arrays[-7], *arrays[-10:-8])
+    smalls, small_blocks = [], []
+    for step in range(LINE):
+        if step > 0:
+            pair = along_ring(pair if step != 2 else after(pair, *arrays[-6:-4]))
+        if step == LINE - 2:
+            arrays[0] = after(arrays[0], pair)
+        smalls += [pair, other_core(pair)]
+        small_blocks += [
+            (2 * step + core, y * small_rows, functools.partial(from_device, step, y, core))
+            for core in range(2)
+            for y in range(2)
+        ]
+    targets = [
+        [(0, 0, 2 * rows), (5, 4 * rows, 2 * rows)],
+        [(1, 0, 2 * rows), (4, 0, 2 * rows)],
+        [(2, 0, 2 * rows), (5, 0, 2 * rows)],
+        [(3, 0, 2 * rows), (5, 2 * rows, 2 * rows)],
+    ]
+    out_rows = [2 * rows] * 5 + [6 * rows]
+    *keep, send_first, send_rest = run_experts(
+        arrays, sources, targets, out_rows, w_gate_up, w_down, top, rows, capacity
+    )
+    came_first = other_core(send_first)
+    came_rest = other_core(after(send_rest, came_first))
+    came = [came_rest[4 * rows :], came_first, came_rest[: 2 * rows], came_rest[2 * rows : 4 * rows]]
+    crossing = [summed(keep[step][rows:], came[step][rows:]) for step in range(LINE)]
+    theirs = [across(crossing[step]) for step in (1, 2, 3, 0)]
+    theirs = [theirs[3], *theirs[:3]]
+    new_keys, values = make_values(
+        arrays, blocks, smalls, small_blocks, rows, width, crossing[0]
+    )
+    total = summed(keep[1][:rows], came[1][:rows], after(theirs[1], values))
+    moving = along_ring(total)
+    context = attend_part(after(queries, total), new_keys, values, 0, 4)
+    context = attend_part(queries, new_keys, values, 1, 4, context)
+    total = summed(keep[2][:rows], came[2][:rows], theirs[2], after(moving, context))
+    moving = along_ring(total)
+    context = attend_part(after(queries, total), new_keys, values, 2, 4, context)
+    total = summed(keep[3][:rows], came[3][:rows], theirs[3], after(moving, context))
+    moving = along_ring(total)
+    context = attend_part(after(queries, total), new_keys, values, 3, 4, context)
+    layer_out = summed(acts, keep[0][:rows], came[0][:rows], theirs[0], after(moving, context))
     return context, layer_out
 
 
-def on_any(acts, packed, keys, value_weight, queries, w_gate_up, w_down, top, capacity):
+def on_any(acts, packed, small, queries, w_gate_up, w_down, top, capacity):
     rows, width = acts.shape
+    keys, value_weight = small[:rows], small[rows:]
     gathered = lax.all_gather(packed, "seq", axis=0, tiled=True)
     all_keys = lax.all_gather(keys, "seq", axis=0, tiled=True)
     weight = lax.all_gather(value_weight, "seq", axis=0, tiled=True)
@@ -495,7 +523,9 @@
         [gathered], pieces, pieces, [total], w_gate_up, w_down, top, rows, capacity
     )
     values = dot(gathered[:, :width], weight).astype(BF16)
-    context = attend_all(queries, all_keys, values, KEY_VALUE_HEADS)
+    context = None
+    for part in range(KEY_VALUE_HEADS):
+        context = attend_part(queries, all_keys, values, part, KEY_VALUE_HEADS, context)
     combined = lax.psum_scatter(partial, "seq", scatter_dimension=0, tiled=True)
     return context, summed(acts, combined)
 
@@ -509,18 +539,19 @@
     devices = lax.axis_size("seq")
     capacity = max(2, 3 * pos_rows * top // (2 * devices))
     acts = activations.reshape(pos_rows, model_width)
-    packed = pack(
+    packed, small = pack(
         acts,
         norm_gain,
         expert_ids.transpose(1, 2, 0).reshape(top, pos_rows),
         gate_weights.transpose(1, 2, 0).reshape(top, pos_rows),
+        keys.reshape(pos_rows, -1),
+        value_weight,
     )
     way = on_line if devices == 4 * LINE else on_any
     context, layer_out = way(
         acts,
         packed,
-        keys.reshape(pos_rows, -1),
-        value_weight,
+        small,
         queries.reshape(pos_rows, -1),
         w_gate_up[0],
         w_down[0],

time: 120 us -> 114 us (0.950)
  other arithmetic: 7.98 us -> 3.69 us
  starting transfers between devices: 22 us -> 20.2 us
    ppermute x9, waiting for transfers between devices: 19.4 us -> 12.6 us  [across(): return lax.ppermute(x, 'seq', swaps(1, 0))]
    ppermute x9, waiting for transfers between devices: 34 us -> 39.4 us  [along_ring(): return lax.ppermute(x, 'seq', ring_step())]
    ppermute x9, starting transfers between devices: 10.1 us -> 7.22 us  [along_ring(): return lax.ppermute(x, 'seq', ring_step())]
    convert_element_type x7 -> x5, other arithmetic: 5.4 us -> 2.82 us  [summed(): return sum((term.astype(F32) for term in terms)).astype(BF16)]
    ppermute x13 -> x14, waiting for transfers between devices: 0.03 us -> 2.14 us  [other_core(): return lax.ppermute(x, 'seq', swaps(0, 1))]
    concatenate x2 -> x0, other arithmetic: 1.7 us -> none  [the longest x1 0.86 us: on_line(): pair = jnp.concatenate([pair, across(pair)], axis=0)]
    unnamed x47 -> x51, local copies, waits for them, and re-layouts: 4.56 us -> 4.54 us
  transfers between devices with their start and end apart: 31 -> 32, of which waited for: 11 -> 12; matrix products, arithmetic and copies ran while one was open for 8% -> 3% of each run, Pallas kernels for 24% -> 15%
where the time goes in v3:
time: 114 us
  waiting for transfers between devices  54.1 us (47%)
  Pallas kernels  30 us (26%)
  starting transfers between devices  20.2 us (18%)
  local copies, waits for them, and re-layouts  4.55 us (4%)
  other arithmetic  3.69 us (3%)
    ppermute x9, waiting for transfers between devices, along_ring(): return lax.ppermute(x, 'seq', ring_step())  39.4 us
    ppermute x9, waiting for transfers between devices, across(): return lax.ppermute(x, 'seq', swaps(1, 0))  12.6 us
    pallas_call x4, Pallas kernels, attend_part(): pl.pallas_call(functools.partial(attention_kernel, chunk), grid=(1,), out...  11.6 us
    pallas_call x1, Pallas kernels, run_experts(): pl.pallas_call(functools.partial(expert_kernel, top, tok_rows, capacity,...  11.6 us
    ppermute x9, starting transfers between devices, across(): return lax.ppermute(x, 'seq', swaps(1, 0))  10.6 us
    ppermute x9, starting transfers between devices, along_ring(): return lax.ppermute(x, 'seq', ring_step())  7.22 us
    pallas_call x1, Pallas kernels, make_values(): pl.pallas_call(functools.partial(value_kernel, key_rows, blocks, small_bl...  5.01 us
    unnamed x51, local copies, waits for them, and re-layouts  4.54 us
  transfers between devices with their start and end apart: 32, of which 12 were waited for; matrix products, arithmetic and copies ran while one was open for 3% of the time, Pallas kernels for 15%

profile of v3, /device:TPU:0, one launch (start us, length us, event | category | flops | bytes accessed | tf_op | source)
XLA Modules:
  0.0 113.5 jit_solution(13002238369891179287)
XLA Ops:
  0.6 1.9 %normalize_and_pack.1 = (bf16[64,2176]{1,0:T(8,128)(2,1)}, bf16[192,256]{1,0:T(8,128)(2,1)}) custom-call(bf16[64,2048]{1,0:T(8,128)(2,1)} %bitcast.21, f32[1,2048]{1,0:T(1,128)} %bitcast.23, s32[4,64]{1,0:T(4,128)} %bitcast.24, f32[4,64]{1,0:T(4,128)} %bitcast.25, bf16[64,256]{1,0:T(8,128)(2,1)} %bitcast.22, bf16[128,256]{1,0:T(8,128)(2,1)} %weight_ref.1), custom_call_target="tpu_custom_call" | custom-call | flops 524288 | bytes 524288 | tf_op jit(solution)/shard_map/normalize_and_pack/pallas_call | solution.py:103
  2.5 3.0 %collective-permute-start.1 = (bf16[64,2176]{1,0:T(8,128)(2,1)}, bf16[64,2176]{1,0:T(8,128)(2,1)S(1)}, u32[]{:S(2)}, u32[]{:S(2)}) collective-permute-start(bf16[64,2176]{1,0:T(8,128)(2,1)} %get-tuple-element.32.refs_0_), channel_id=1, source_target_pairs={{0,4},{1,5},{2,6},{3,7},{4,12},{5,13},{6,14},{7,15},{12,8},{13,9},... | collective-permute-start | bytes 835592 | tf_op jit(solution)/shard_map/ppermute | solution.py:54
  5.5 1.5 %collective-permute-start.2 = (bf16[64,2176]{1,0:T(8,128)(2,1)}, bf16[64,2176]{1,0:T(8,128)(2,1)S(1)}, u32[]{:S(2)}, u32[]{:S(2)}) collective-permute-start(bf16[64,2176]{1,0:T(8,128)(2,1)} %get-tuple-element.32.refs_0_), channel_id=1, source_target_pairs={{0,2},{1,3},{2,0},{3,1},{4,6},{5,7},{6,4},{7,5},{12,14},{13,15},{1... | collective-permute-start | bytes 835592 | tf_op jit(solution)/shard_map/ppermute | solution.py:58
  7.0 0.0 collective-permute-start.5
  7.0 0.5 collective-permute-start
  7.6 0.9 constant_dynamic-update-slice_fusion.1
  8.5 7.5 %collective-permute-done = bf16[192,256]{1,0:T(8,128)(2,1)S(1)} collective-permute-done((bf16[192,256]{1,0:T(8,128)(2,1)}, bf16[192,256]{1,0:T(8,128)(2,1)S(1)}, u32[]{:S(2)}, u32[]{:S(2)}) %collective-permute-start) | collective-permute-done | bytes 98336 | tf_op jit(solution)/shard_map/ppermute | solution.py:58
  16.0 0.0 copy-start.5
  16.0 0.0 collective-permute-done.1.refs_4_
  16.0 2.6 %collective-permute-start.3 = (bf16[64,2176]{1,0:T(8,128)(2,1)S(1)}, bf16[64,2176]{1,0:T(8,128)(2,1)S(1)}, u32[]{:S(2)}, u32[]{:S(2)}) collective-permute-start(bf16[64,2176]{1,0:T(8,128)(2,1)S(1)} %collective-permute-done.1.refs_4_), channel_id=1, source_target_pairs={{0,4},{1,5},{2,6},{3,7},{4,12},{5,13},{6,14},{7,15},{12,8},{13,9},... | collective-permute-start | bytes 835592 | tf_op jit(solution)/shard_map/ppermute | solution.py:54
  18.7 1.5 %collective-permute-start.4 = (bf16[64,2176]{1,0:T(8,128)(2,1)S(1)}, bf16[64,2176]{1,0:T(8,128)(2,1)S(1)}, u32[]{:S(2)}, u32[]{:S(2)}) collective-permute-start(bf16[64,2176]{1,0:T(8,128)(2,1)S(1)} %collective-permute-done.1.refs_4_), channel_id=1, source_target_pairs={{0,2},{1,3},{2,0},{3,1},{4,6},{5,7},{6,4},{7,5},{12,14},{13,15},{1... | collective-permute-start | bytes 835592 | tf_op jit(solution)/shard_map/ppermute | solution.py:58
  20.2 0.0 collective-permute-start.6
  20.2 0.0 collective-permute-done.5.refs_2_
  20.2 4.0 %collective-permute-done.3.refs_8_ = bf16[64,2176]{1,0:T(8,128)(2,1)S(1)} collective-permute-done((bf16[64,2176]{1,0:T(8,128)(2,1)S(1)}, bf16[64,2176]{1,0:T(8,128)(2,1)S(1)}, u32[]{:S(2)}, u32[]{:S(2)}) %collective-permute-start.3) | collective-permute-done | bytes 278560 | tf_op jit(solution)/shard_map/ppermute | solution.py:54
  24.2 1.4 %collective-permute-done.4.refs_5_ = bf16[64,2176]{1,0:T(8,128)(2,1)S(1)} collective-permute-done((bf16[64,2176]{1,0:T(8,128)(2,1)S(1)}, bf16[64,2176]{1,0:T(8,128)(2,1)S(1)}, u32[]{:S(2)}, u32[]{:S(2)}) %collective-permute-start.4) | collective-permute-done | bytes 278560 | tf_op jit(solution)/shard_map/ppermute | solution.py:58
  25.6 0.0 collective-permute-done.6.refs_3_
  25.6 0.5 collective-permute-start.7
  26.1 1.5 %collective-permute-start.8 = (bf16[64,2176]{1,0:T(8,128)(2,1)S(1)}, bf16[64,2176]{1,0:T(8,128)(2,1)S(1)}, u32[]{:S(2)}, u32[]{:S(2)}) collective-permute-start(bf16[64,2176]{1,0:T(8,128)(2,1)S(1)} %collective-permute-done.3.refs_8_), channel_id=1, source_target_pairs={{0,2},{1,3},{2,0},{3,1},{4,6},{5,7},{6,4},{7,5},{12,14},{13,15},{1... | collective-permute-start | bytes 835592 | tf_op jit(solution)/shard_map/ppermute | solution.py:58
  27.6 0.5 collective-permute-start.10
  28.1 5.0 %collective-permute-done.7.refs_12_ = bf16[64,2176]{1,0:T(8,128)(2,1)S(1)} collective-permute-done((bf16[64,2176]{1,0:T(8,128)(2,1)S(1)}, bf16[64,2176]{1,0:T(8,128)(2,1)S(1)}, u32[]{:S(2)}, u32[]{:S(2)}) %collective-permute-start.7) | collective-permute-done | bytes 278560 | tf_op jit(solution)/shard_map/ppermute | solution.py:54
  33.1 1.5 %collective-permute-start.15 = (bf16[64,2176]{1,0:T(8,128)(2,1)S(1)}, bf16[64,2176]{1,0:T(8,128)(2,1)S(1)}, u32[]{:S(2)}, u32[]{:S(2)}) collective-permute-start(bf16[64,2176]{1,0:T(8,128)(2,1)S(1)} %collective-permute-done.7.refs_12_), channel_id=1, source_target_pairs={{0,2},{1,3},{2,0},{3,1},{4,6},{5,7},{6,4},{7,5},{12,14},{13,15},{1... | collective-permute-start | bytes 835592 | tf_op jit(solution)/shard_map/ppermute | solution.py:58
  34.6 0.5 collective-permute-start.13
  35.2 0.6 collective-permute-start.11
  35.8 0.2 collective-permute-start.16
  36.0 3.7 %collective-permute-done.15.refs_13_ = bf16[64,2176]{1,0:T(8,128)(2,1)S(1)} collective-permute-done((bf16[64,2176]{1,0:T(8,128)(2,1)S(1)}, bf16[64,2176]{1,0:T(8,128)(2,1)S(1)}, u32[]{:S(2)}, u32[]{:S(2)}) %collective-permute-start.15) | collective-permute-done | bytes 278560 | tf_op jit(solution)/shard_map/ppermute | solution.py:58
  39.7 3.4 %collective-permute-done.11.refs_18_ = bf16[384,256]{1,0:T(8,128)(2,1)} collective-permute-done((bf16[384,256]{1,0:T(8,128)(2,1)S(1)}, bf16[384,256]{1,0:T(8,128)(2,1)}, u32[]{:S(2)}, u32[]{:S(2)}) %collective-permute-start.11) | collective-permute-done | bytes 196640 | tf_op jit(solution)/shard_map/ppermute | solution.py:54
  43.1 0.1 collective-permute-start.14
  43.2 7.2 %collective-permute-done.14.refs_20_ = bf16[384,256]{1,0:T(8,128)(2,1)} collective-permute-done((bf16[384,256]{1,0:T(8,128)(2,1)}, bf16[384,256]{1,0:T(8,128)(2,1)}, u32[]{:S(2)}, u32[]{:S(2)}) %collective-permute-start.14) | collective-permute-done | bytes 196640 | tf_op jit(solution)/shard_map/ppermute | solution.py:54
  50.4 0.7 copy-done.19
  51.1 0.7 copy-done.20
  51.9 11.6 %experts.1 = (bf16[128,2048]{1,0:T(8,128)(2,1)}, bf16[128,2048]{1,0:T(8,128)(2,1)}, bf16[128,2048]{1,0:T(8,128)(2,1)}, bf16[128,2048]{1,0:T(8,128)(2,1)}, bf16[1...) custom-call(bf16[64,2176]{1,0:T(8,128)(2,1)} %get-tuple-element.32.refs_0_, bf16[64,2176]{1,0:T(8,128)(2,1)} %copy-done.7, ...), custom_call_target="tpu_custom_call" | custom-call | flops 4429185024 | bytes 17825792 | tf_op jit(solution)/shard_map/experts/pallas_call | solution.py:253
  63.5 0.1 collective-permute-start.18
  63.6 2.1 %collective-permute-done.18 = bf16[128,2048]{1,0:T(8,128)(2,1)S(1)} collective-permute-done((bf16[128,2048]{1,0:T(8,128)(2,1)}, bf16[128,2048]{1,0:T(8,128)(2,1)S(1)}, u32[]{:S(2)}, u32[]{:S(2)}) %collective-permute-start.18) | collective-permute-done | bytes 524320 | tf_op jit(solution)/shard_map/ppermute | solution.py:62
  65.7 0.1 collective-permute-start.19
  65.8 0.4 collective-permute-start.23
  66.2 0.1 collective-permute-start.24
  66.3 0.4 collective-permute-start.25
  66.7 7.4 %collective-permute-done.26.refs_22_ = bf16[384,256]{1,0:T(8,128)(2,1)S(1)} collective-permute-done((bf16[384,256]{1,0:T(8,128)(2,1)}, bf16[384,256]{1,0:T(8,128)(2,1)S(1)}, u32[]{:S(2)}, u32[]{:S(2)}) %collective-permute-start.26) | collective-permute-done | bytes 196640 | tf_op jit(solution)/shard_map/ppermute | solution.py:54
  74.1 1.1 add_convert_fusion.5
  75.2 2.9 %collective-permute-start.22 = (bf16[64,2048]{1,0:T(8,128)(2,1)S(1)}, bf16[64,2048]{1,0:T(8,128)(2,1)S(1)}, u32[]{:S(2)}, u32[]{:S(2)}) collective-permute-start(bf16[64,2048]{1,0:T(8,128)(2,1)S(1)} %add_convert_fusion.5), channel_id=1, source_target_pairs={{0,2},{1,3},{2,0},{3,1},{4,6},{5,7},{6,4},{7,5},{12,14},{13,15},{1... | collective-permute-start | bytes 786440 | tf_op jit(solution)/shard_map/ppermute | solution.py:58
  78.1 1.4 %add_convert_fusion.7 = (bf16[64,2048]{1,0:T(8,128)(2,1)S(1)}, bf16[64,2048]{1,0:T(8,128)(2,1)S(1)}, bf16[64,2048]{1,0:T(8,128)(2,1)S(1)}) fusion(bf16[384,2048]{1,0:T(8,128)(2,1)S(1)} %collective-permute-done.19, bf16[128,2048]{1,0:T(8,128)(2,1)} %get-tuple-element.33, bf16[128,2048]{1,0:T(8,128)(2,1)} %get-tuple-element.39, ...), kind=kLoop, calls=%fused_computation.7 | loop fusion | flops 1572864 | bytes 2359296 | tf_op jit(solution)/shard_map/convert_element_type | solution.py:439
  79.5 0.0 copy-start.4
  79.6 0.7 copy-done.22
  80.2 0.7 copy-done.23
  80.9 0.7 copy-done.24
  81.6 5.0 %values.1 = (bf16[1024,256]{1,0:T(8,128)(2,1)}, bf16[1024,256]{1,0:T(8,128)(2,1)}) custom-call(bf16[64,2176]{1,0:T(8,128)(2,1)} %get-tuple-element.32.refs_0_, bf16[64,2176]{1,0:T(8,128)(2,1)} %copy-done.7, bf16[64,2176]{1,0:T(8,128)(2,1)} %copy-done.8, bf16[64,2176]{1,0:T(8,128)(2,1)} %copy-done.11, bf16[64,2176]{1,0:T(8,128)(2,1)} %copy-done.6, ...), custom_call_target="tpu_custom_call" | custom-call | flops 1073741824 | bytes 5242880 | tf_op jit(solution)/shard_map/values/pallas_call | solution.py:326
  86.6 0.1 add_convert_fusion.3
  86.8 0.2 collective-permute-start.28
  87.0 0.2 collective-permute-start.21
  87.2 2.9 %attention.4.refs_0_ = bf16[64,4096]{1,0:T(8,128)(2,1)} custom-call(bf16[64,4096]{1,0:T(8,128)(2,1)} %bitcast.16, bf16[1024,256]{1,0:T(8,128)(2,1)} %get-tuple-element.43.k_ref, bf16[1024,256]{1,0:T(8,128)(2,1)} %get-tuple-element.41.v_ref), custom_call_target="tpu_custom_call" | custom-call | flops 268435456 | bytes 786432 | tf_op jit(solution)/shard_map/attention/pallas_call | solution.py:416
  90.1 2.9 %attention.5.refs_0_ = bf16[64,4096]{1,0:T(8,128)(2,1)} custom-call(bf16[64,4096]{1,0:T(8,128)(2,1)} %bitcast.17, bf16[1024,256]{1,0:T(8,128)(2,1)} %get-tuple-element.43.k_ref, bf16[1024,256]{1,0:T(8,128)(2,1)} %get-tuple-element.41.v_ref, bf16[64,4096]{1,0:T(8,128)(2,1)} %attention.4.refs_0_), custom_call_target="tpu_custom_call", output_to_operand_aliasing={{}: (3, {})} | custom-call | flops 268435456 | bytes 786432 | tf_op jit(solution)/shard_map/attention/pallas_call | solution.py:416
  93.0 3.2 %collective-permute-done.28 = bf16[64,2048]{1,0:T(8,128)(2,1)S(1)} collective-permute-done((bf16[64,2048]{1,0:T(8,128)(2,1)S(1)}, bf16[64,2048]{1,0:T(8,128)(2,1)S(1)}, u32[]{:S(2)}, u32[]{:S(2)}) %collective-permute-start.28) | collective-permute-done | bytes 262176 | tf_op jit(solution)/shard_map/ppermute | solution.py:54
  96.3 0.1 add_convert_fusion.2
  96.4 0.1 collective-permute-start.29
  96.5 0.4 collective-permute-start.20
  96.8 2.9 %attention.6.refs_0_ = bf16[64,4096]{1,0:T(8,128)(2,1)} custom-call(bf16[64,4096]{1,0:T(8,128)(2,1)} %bitcast.18, bf16[1024,256]{1,0:T(8,128)(2,1)} %get-tuple-element.43.k_ref, bf16[1024,256]{1,0:T(8,128)(2,1)} %get-tuple-element.41.v_ref, bf16[64,4096]{1,0:T(8,128)(2,1)} %attention.5.refs_0_), custom_call_target="tpu_custom_call", output_to_operand_aliasing={{}: (3, {})} | custom-call | flops 268435456 | bytes 786432 | tf_op jit(solution)/shard_map/attention/pallas_call | solution.py:416
  99.7 5.2 %collective-permute-done.29 = bf16[64,2048]{1,0:T(8,128)(2,1)S(1)} collective-permute-done((bf16[64,2048]{1,0:T(8,128)(2,1)S(1)}, bf16[64,2048]{1,0:T(8,128)(2,1)S(1)}, u32[]{:S(2)}, u32[]{:S(2)}) %collective-permute-start.29) | collective-permute-done | bytes 262176 | tf_op jit(solution)/shard_map/ppermute | solution.py:54
  104.9 0.1 add_convert_fusion.1
  105.0 0.0 copy-start
  105.1 0.1 collective-permute-start.31
  105.1 0.5 collective-permute-start.30
  105.7 2.9 %attention.7 = bf16[64,4096]{1,0:T(8,128)(2,1)} custom-call(bf16[64,4096]{1,0:T(8,128)(2,1)} %bitcast.19, bf16[1024,256]{1,0:T(8,128)(2,1)} %get-tuple-element.43.k_ref, bf16[1024,256]{1,0:T(8,128)(2,1)} %get-tuple-element.41.v_ref, bf16[64,4096]{1,0:T(8,128)(2,1)} %attention.6.refs_0_), custom_call_target="tpu_custom_call", output_to_operand_aliasing={{}: (3, {})} | custom-call | flops 268435456 | bytes 786432 | tf_op jit(solution)/shard_map/attention/pallas_call | solution.py:416
  108.5 4.1 %collective-permute-done.31 = bf16[64,2048]{1,0:T(8,128)(2,1)S(1)} collective-permute-done((bf16[64,2048]{1,0:T(8,128)(2,1)S(1)}, bf16[64,2048]{1,0:T(8,128)(2,1)S(1)}, u32[]{:S(2)}, u32[]{:S(2)}) %collective-permute-start.31) | collective-permute-done | bytes 262176 | tf_op jit(solution)/shard_map/ppermute | solution.py:54
  112.6 0.9 fusion
  (65 shorter events, 0.1 us)
Async XLA Ops:
  2.5 13.5 %collective-permute-start.1 = (bf16[64,2176]{1,0:T(8,128)(2,1)}, bf16[64,2176]{1,0:T(8,128)(2,1)S(1)}, u32[]{:S(2)}, u32[]{:S(2)}) collective-permute-start(bf16[64,2176]{1,0:T(8,128)(2,1)} %get-tuple-element.32.refs_0_), channel_id=1, source_target_pairs={{0,4},{1,5},{2,6},{3,7},{4,12},{5,13},{6,14},{7,15},{12,8},{13,9},... | collective-permute-start | bytes 835592 | tf_op jit(solution)/shard_map/ppermute | solution.py:54
  5.5 10.5 %collective-permute-start.2 = (bf16[64,2176]{1,0:T(8,128)(2,1)}, bf16[64,2176]{1,0:T(8,128)(2,1)S(1)}, u32[]{:S(2)}, u32[]{:S(2)}) collective-permute-start(bf16[64,2176]{1,0:T(8,128)(2,1)} %get-tuple-element.32.refs_0_), channel_id=1, source_target_pairs={{0,2},{1,3},{2,0},{3,1},{4,6},{5,7},{6,4},{7,5},{12,14},{13,15},{1... | collective-permute-start | bytes 835592 | tf_op jit(solution)/shard_map/ppermute | solution.py:58
  7.0 13.1 %collective-permute-start.5 = (bf16[64,2176]{1,0:T(8,128)(2,1)}, bf16[64,2176]{1,0:T(8,128)(2,1)S(1)}, u32[]{:S(2)}, u32[]{:S(2)}) collective-permute-start(bf16[64,2176]{1,0:T(8,128)(2,1)} %get-tuple-element.32.refs_0_), channel_id=1, source_target_pairs={{0,1},{1,0},{2,3},{3,2},{4,5},{5,4},{6,7},{7,6},{12,13},{13,12},{1... | collective-permute-start | bytes 835592 | tf_op jit(solution)/shard_map/ppermute | solution.py:62
  7.0 8.9 %collective-permute-start = (bf16[192,256]{1,0:T(8,128)(2,1)}, bf16[192,256]{1,0:T(8,128)(2,1)S(1)}, u32[]{:S(2)}, u32[]{:S(2)}) collective-permute-start(bf16[192,256]{1,0:T(8,128)(2,1)} %get-tuple-element.27), channel_id=1, source_target_pairs={{0,2},{1,3},{2,0},{3,1},{4,6},{5,7},{6,4},{7,5},{12,14},{13,15},{1... | collective-permute-start | bytes 294920 | tf_op jit(solution)/shard_map/ppermute | solution.py:58
  16.0 49.9 %copy-start.5 = (bf16[384,256]{1,0:T(8,128)(2,1)}, bf16[384,256]{1,0:T(8,128)(2,1)S(1)}, u32[]{:S(2)}) copy-start(bf16[384,256]{1,0:T(8,128)(2,1)S(1)} %constant_dynamic-update-slice_fusion.refs_16_) | copy-start | bytes 589828
  16.0 35.9 %copy-start.6 = (bf16[64,2176]{1,0:T(8,128)(2,1)}, bf16[64,2176]{1,0:T(8,128)(2,1)S(1)}, u32[]{:S(2)}) copy-start(bf16[64,2176]{1,0:T(8,128)(2,1)S(1)} %collective-permute-done.1.refs_4_) | copy-start | bytes 835588
  16.0 35.8 %copy-start.7 = (bf16[64,2176]{1,0:T(8,128)(2,1)}, bf16[64,2176]{1,0:T(8,128)(2,1)S(1)}, u32[]{:S(2)}) copy-start(bf16[64,2176]{1,0:T(8,128)(2,1)S(1)} %collective-permute-done.2.refs_1_) | copy-start | bytes 835588
  16.0 8.2 %collective-permute-start.3 = (bf16[64,2176]{1,0:T(8,128)(2,1)S(1)}, bf16[64,2176]{1,0:T(8,128)(2,1)S(1)}, u32[]{:S(2)}, u32[]{:S(2)}) collective-permute-start(bf16[64,2176]{1,0:T(8,128)(2,1)S(1)} %collective-permute-done.1.refs_4_), channel_id=1, source_target_pairs={{0,4},{1,5},{2,6},{3,7},{4,12},{5,13},{6,14},{7,15},{12,8},{13,9},... | collective-permute-start | bytes 835592 | tf_op jit(solution)/shard_map/ppermute | solution.py:54
  18.7 6.9 %collective-permute-start.4 = (bf16[64,2176]{1,0:T(8,128)(2,1)S(1)}, bf16[64,2176]{1,0:T(8,128)(2,1)S(1)}, u32[]{:S(2)}, u32[]{:S(2)}) collective-permute-start(bf16[64,2176]{1,0:T(8,128)(2,1)S(1)} %collective-permute-done.1.refs_4_), channel_id=1, source_target_pairs={{0,2},{1,3},{2,0},{3,1},{4,6},{5,7},{6,4},{7,5},{12,14},{13,15},{1... | collective-permute-start | bytes 835592 | tf_op jit(solution)/shard_map/ppermute | solution.py:58
  20.2 5.4 %collective-permute-start.6 = (bf16[64,2176]{1,0:T(8,128)(2,1)S(1)}, bf16[64,2176]{1,0:T(8,128)(2,1)S(1)}, u32[]{:S(2)}, u32[]{:S(2)}) collective-permute-start(bf16[64,2176]{1,0:T(8,128)(2,1)S(1)} %collective-permute-done.2.refs_1_), channel_id=1, source_target_pairs={{0,1},{1,0},{2,3},{3,2},{4,5},{5,4},{6,7},{7,6},{12,13},{13,12},{1... | collective-permute-start | bytes 835592 | tf_op jit(solution)/shard_map/ppermute | solution.py:62
  20.2 31.7 %copy-start.8 = (bf16[64,2176]{1,0:T(8,128)(2,1)}, bf16[64,2176]{1,0:T(8,128)(2,1)S(1)}, u32[]{:S(2)}) copy-start(bf16[64,2176]{1,0:T(8,128)(2,1)S(1)} %collective-permute-done.5.refs_2_) | copy-start | bytes 835588
  24.2 27.7 %copy-start.9 = (bf16[64,2176]{1,0:T(8,128)(2,1)}, bf16[64,2176]{1,0:T(8,128)(2,1)S(1)}, u32[]{:S(2)}) copy-start(bf16[64,2176]{1,0:T(8,128)(2,1)S(1)} %collective-permute-done.3.refs_8_) | copy-start | bytes 835588
  25.6 26.3 %copy-start.10 = (bf16[64,2176]{1,0:T(8,128)(2,1)}, bf16[64,2176]{1,0:T(8,128)(2,1)S(1)}, u32[]{:S(2)}) copy-start(bf16[64,2176]{1,0:T(8,128)(2,1)S(1)} %collective-permute-done.4.refs_5_) | copy-start | bytes 835588
  25.6 26.3 %copy-start.11 = (bf16[64,2176]{1,0:T(8,128)(2,1)}, bf16[64,2176]{1,0:T(8,128)(2,1)S(1)}, u32[]{:S(2)}) copy-start(bf16[64,2176]{1,0:T(8,128)(2,1)S(1)} %collective-permute-done.6.refs_3_) | copy-start | bytes 835588
  25.6 7.5 %collective-permute-start.7 = (bf16[64,2176]{1,0:T(8,128)(2,1)S(1)}, bf16[64,2176]{1,0:T(8,128)(2,1)S(1)}, u32[]{:S(2)}, u32[]{:S(2)}) collective-permute-start(bf16[64,2176]{1,0:T(8,128)(2,1)S(1)} %collective-permute-done.3.refs_8_), channel_id=1, source_target_pairs={{0,4},{1,5},{2,6},{3,7},{4,12},{5,13},{6,14},{7,15},{12,8},{13,9},... | collective-permute-start | bytes 835592 | tf_op jit(solution)/shard_map/ppermute | solution.py:54
  26.1 8.5 %collective-permute-start.8 = (bf16[64,2176]{1,0:T(8,128)(2,1)S(1)}, bf16[64,2176]{1,0:T(8,128)(2,1)S(1)}, u32[]{:S(2)}, u32[]{:S(2)}) collective-permute-start(bf16[64,2176]{1,0:T(8,128)(2,1)S(1)} %collective-permute-done.3.refs_8_), channel_id=1, source_target_pairs={{0,2},{1,3},{2,0},{3,1},{4,6},{5,7},{6,4},{7,5},{12,14},{13,15},{1... | collective-permute-start | bytes 835592 | tf_op jit(solution)/shard_map/ppermute | solution.py:58
  27.6 7.5 %collective-permute-start.9 = (bf16[64,2176]{1,0:T(8,128)(2,1)S(1)}, bf16[64,2176]{1,0:T(8,128)(2,1)S(1)}, u32[]{:S(2)}, u32[]{:S(2)}) collective-permute-start(bf16[64,2176]{1,0:T(8,128)(2,1)S(1)} %collective-permute-done.1.refs_4_), channel_id=1, source_target_pairs={{0,1},{1,0},{2,3},{3,2},{4,5},{5,4},{6,7},{7,6},{12,13},{13,12},{1... | collective-permute-start | bytes 835592 | tf_op jit(solution)/shard_map/ppermute | solution.py:62
  27.6 7.5 %collective-permute-start.10 = (bf16[64,2176]{1,0:T(8,128)(2,1)S(1)}, bf16[64,2176]{1,0:T(8,128)(2,1)S(1)}, u32[]{:S(2)}, u32[]{:S(2)}) collective-permute-start(bf16[64,2176]{1,0:T(8,128)(2,1)S(1)} %collective-permute-done.4.refs_5_), channel_id=1, source_target_pairs={{0,1},{1,0},{2,3},{3,2},{4,5},{5,4},{6,7},{7,6},{12,13},{13,12},{1... | collective-permute-start | bytes 835592 | tf_op jit(solution)/shard_map/ppermute | solution.py:62
  33.1 18.8 %copy-start.12 = (bf16[64,2176]{1,0:T(8,128)(2,1)}, bf16[64,2176]{1,0:T(8,128)(2,1)S(1)}, u32[]{:S(2)}) copy-start(bf16[64,2176]{1,0:T(8,128)(2,1)S(1)} %collective-permute-done.7.refs_12_) | copy-start | bytes 835588
  33.1 6.5 %collective-permute-start.15 = (bf16[64,2176]{1,0:T(8,128)(2,1)S(1)}, bf16[64,2176]{1,0:T(8,128)(2,1)S(1)}, u32[]{:S(2)}, u32[]{:S(2)}) collective-permute-start(bf16[64,2176]{1,0:T(8,128)(2,1)S(1)} %collective-permute-done.7.refs_12_), channel_id=1, source_target_pairs={{0,2},{1,3},{2,0},{3,1},{4,6},{5,7},{6,4},{7,5},{12,14},{13,15},{1... | collective-permute-start | bytes 835592 | tf_op jit(solution)/shard_map/ppermute | solution.py:58
  34.6 5.0 %collective-permute-start.12 = (bf16[64,2176]{1,0:T(8,128)(2,1)S(1)}, bf16[64,2176]{1,0:T(8,128)(2,1)S(1)}, u32[]{:S(2)}, u32[]{:S(2)}) collective-permute-start(bf16[64,2176]{1,0:T(8,128)(2,1)S(1)} %collective-permute-done.3.refs_8_), channel_id=1, source_target_pairs={{0,1},{1,0},{2,3},{3,2},{4,5},{5,4},{6,7},{7,6},{12,13},{13,12},{1... | collective-permute-start | bytes 835592 | tf_op jit(solution)/shard_map/ppermute | solution.py:62
  34.6 17.3 %copy-start.13 = (bf16[64,2176]{1,0:T(8,128)(2,1)}, bf16[64,2176]{1,0:T(8,128)(2,1)S(1)}, u32[]{:S(2)}) copy-start(bf16[64,2176]{1,0:T(8,128)(2,1)S(1)} %collective-permute-done.8.refs_9_) | copy-start | bytes 835588
  34.6 8.5 %collective-permute-start.13 = (bf16[64,2176]{1,0:T(8,128)(2,1)S(1)}, bf16[64,2176]{1,0:T(8,128)(2,1)S(1)}, u32[]{:S(2)}, u32[]{:S(2)}) collective-permute-start(bf16[64,2176]{1,0:T(8,128)(2,1)S(1)} %collective-permute-done.8.refs_9_), channel_id=1, source_target_pairs={{0,1},{1,0},{2,3},{3,2},{4,5},{5,4},{6,7},{7,6},{12,13},{13,12},{1... | collective-permute-start | bytes 835592 | tf_op jit(solution)/shard_map/ppermute | solution.py:62
  35.1 16.8 %copy-start.14 = (bf16[64,2176]{1,0:T(8,128)(2,1)}, bf16[64,2176]{1,0:T(8,128)(2,1)S(1)}, u32[]{:S(2)}) copy-start(bf16[64,2176]{1,0:T(8,128)(2,1)S(1)} %collective-permute-done.9.refs_6_) | copy-start | bytes 835588
  35.1 16.8 %copy-start.15 = (bf16[64,2176]{1,0:T(8,128)(2,1)}, bf16[64,2176]{1,0:T(8,128)(2,1)S(1)}, u32[]{:S(2)}) copy-start(bf16[64,2176]{1,0:T(8,128)(2,1)S(1)} %collective-permute-done.10.refs_7_) | copy-start | bytes 835588
  35.2 7.9 %collective-permute-start.11 = (bf16[384,256]{1,0:T(8,128)(2,1)S(1)}, bf16[384,256]{1,0:T(8,128)(2,1)}, u32[]{:S(2)}, u32[]{:S(2)}) collective-permute-start(bf16[384,256]{1,0:T(8,128)(2,1)S(1)} %constant_dynamic-update-slice_fusion.refs_16_), channel_id=1, source_target_pairs={{0,4},{1,5},{2,6},{3,7},{4,12},{5,13},{6,14},{7,15},{12,8},{13,9},... | collective-permute-start | bytes 589832 | tf_op jit(solution)/shard_map/ppermute | solution.py:54
  35.8 14.6 %collective-permute-start.16 = (bf16[64,2176]{1,0:T(8,128)(2,1)S(1)}, bf16[64,2176]{1,0:T(8,128)(2,1)S(1)}, u32[]{:S(2)}, u32[]{:S(2)}) collective-permute-start(bf16[64,2176]{1,0:T(8,128)(2,1)S(1)} %collective-permute-done.7.refs_12_), channel_id=1, source_target_pairs={{0,1},{1,0},{2,3},{3,2},{4,5},{5,4},{6,7},{7,6},{12,13},{13,12},{1... | collective-permute-start | bytes 835592 | tf_op jit(solution)/shard_map/ppermute | solution.py:62
  39.6 12.3 %copy-start.16 = (bf16[64,2176]{1,0:T(8,128)(2,1)}, bf16[64,2176]{1,0:T(8,128)(2,1)S(1)}, u32[]{:S(2)}) copy-start(bf16[64,2176]{1,0:T(8,128)(2,1)S(1)} %collective-permute-done.15.refs_13_) | copy-start | bytes 835588
  39.6 10.7 %collective-permute-start.17 = (bf16[64,2176]{1,0:T(8,128)(2,1)S(1)}, bf16[64,2176]{1,0:T(8,128)(2,1)S(1)}, u32[]{:S(2)}, u32[]{:S(2)}) collective-permute-start(bf16[64,2176]{1,0:T(8,128)(2,1)S(1)} %collective-permute-done.15.refs_13_), channel_id=1, source_target_pairs={{0,1},{1,0},{2,3},{3,2},{4,5},{5,4},{6,7},{7,6},{12,13},{13,12},{1... | collective-permute-start | bytes 835592 | tf_op jit(solution)/shard_map/ppermute | solution.py:62
  39.7 12.3 %copy-start.17 = (bf16[64,2176]{1,0:T(8,128)(2,1)}, bf16[64,2176]{1,0:T(8,128)(2,1)S(1)}, u32[]{:S(2)}) copy-start(bf16[64,2176]{1,0:T(8,128)(2,1)S(1)} %collective-permute-done.12.refs_10_) | copy-start | bytes 835588
  43.1 8.8 %copy-start.18 = (bf16[64,2176]{1,0:T(8,128)(2,1)}, bf16[64,2176]{1,0:T(8,128)(2,1)S(1)}, u32[]{:S(2)}) copy-start(bf16[64,2176]{1,0:T(8,128)(2,1)S(1)} %collective-permute-done.13.refs_11_) | copy-start | bytes 835588
  43.1 7.2 %collective-permute-start.14 = (bf16[384,256]{1,0:T(8,128)(2,1)}, bf16[384,256]{1,0:T(8,128)(2,1)}, u32[]{:S(2)}, u32[]{:S(2)}) collective-permute-start(bf16[384,256]{1,0:T(8,128)(2,1)} %collective-permute-done.11.refs_18_), channel_id=1, source_target_pairs={{0,4},{1,5},{2,6},{3,7},{4,12},{5,13},{6,14},{7,15},{12,8},{13,9},... | collective-permute-start | bytes 589832 | tf_op jit(solution)/shard_map/ppermute | solution.py:54
  50.3 0.8 copy-start.19
  51.1 0.7 copy-start.20
  63.5 2.2 %collective-permute-start.18 = (bf16[128,2048]{1,0:T(8,128)(2,1)}, bf16[128,2048]{1,0:T(8,128)(2,1)S(1)}, u32[]{:S(2)}, u32[]{:S(2)}) collective-permute-start(bf16[128,2048]{1,0:T(8,128)(2,1)} %get-tuple-element.35), channel_id=1, source_target_pairs={{0,1},{1,0},{2,3},{3,2},{4,5},{5,4},{6,7},{7,6},{12,13},{13,12},{1... | collective-permute-start | bytes 1572872 | tf_op jit(solution)/shard_map/ppermute | solution.py:62
  65.7 9.5 %collective-permute-start.19 = (bf16[384,2048]{1,0:T(8,128)(2,1)}, bf16[384,2048]{1,0:T(8,128)(2,1)S(1)}, u32[]{:S(2)}, u32[]{:S(2)}) collective-permute-start(bf16[384,2048]{1,0:T(8,128)(2,1)} %get-tuple-element.36), channel_id=1, source_target_pairs={{0,1},{1,0},{2,3},{3,2},{4,5},{5,4},{6,7},{7,6},{12,13},{13,12},{1... | collective-permute-start | bytes 4718600 | tf_op jit(solution)/shard_map/ppermute | solution.py:62
  65.8 8.3 %collective-permute-start.26 = (bf16[384,256]{1,0:T(8,128)(2,1)}, bf16[384,256]{1,0:T(8,128)(2,1)S(1)}, u32[]{:S(2)}, u32[]{:S(2)}) collective-permute-start(bf16[384,256]{1,0:T(8,128)(2,1)} %collective-permute-done.14.refs_20_), channel_id=1, source_target_pairs={{0,4},{1,5},{2,6},{3,7},{4,12},{5,13},{6,14},{7,15},{12,8},{13,9},... | collective-permute-start | bytes 589832 | tf_op jit(solution)/shard_map/ppermute | solution.py:54
  65.8 13.7 %collective-permute-start.23 = (bf16[384,256]{1,0:T(8,128)(2,1)S(1)}, bf16[384,256]{1,0:T(8,128)(2,1)S(1)}, u32[]{:S(2)}, u32[]{:S(2)}) collective-permute-start(bf16[384,256]{1,0:T(8,128)(2,1)S(1)} %constant_dynamic-update-slice_fusion.refs_16_), channel_id=1, source_target_pairs={{0,1},{1,0},{2,3},{3,2},{4,5},{5,4},{6,7},{7,6},{12,13},{13,12},{1... | collective-permute-start | bytes 589832 | tf_op jit(solution)/shard_map/ppermute | solution.py:62
  66.2 14.0 %collective-permute-start.24 = (bf16[384,256]{1,0:T(8,128)(2,1)}, bf16[384,256]{1,0:T(8,128)(2,1)S(1)}, u32[]{:S(2)}, u32[]{:S(2)}) collective-permute-start(bf16[384,256]{1,0:T(8,128)(2,1)} %collective-permute-done.11.refs_18_), channel_id=1, source_target_pairs={{0,1},{1,0},{2,3},{3,2},{4,5},{5,4},{6,7},{7,6},{12,13},{13,12},{1... | collective-permute-start | bytes 589832 | tf_op jit(solution)/shard_map/ppermute | solution.py:62
  66.3 14.6 %collective-permute-start.25 = (bf16[384,256]{1,0:T(8,128)(2,1)}, bf16[384,256]{1,0:T(8,128)(2,1)S(1)}, u32[]{:S(2)}, u32[]{:S(2)}) collective-permute-start(bf16[384,256]{1,0:T(8,128)(2,1)} %collective-permute-done.14.refs_20_), channel_id=1, source_target_pairs={{0,1},{1,0},{2,3},{3,2},{4,5},{5,4},{6,7},{7,6},{12,13},{13,12},{1... | collective-permute-start | bytes 589832 | tf_op jit(solution)/shard_map/ppermute | solution.py:62
  74.1 5.4 %copy-start.21 = (bf16[384,256]{1,0:T(8,128)(2,1)}, bf16[384,256]{1,0:T(8,128)(2,1)S(1)}, u32[]{:S(2)}) copy-start(bf16[384,256]{1,0:T(8,128)(2,1)S(1)} %collective-permute-done.26.refs_22_) | copy-start | bytes 589828
  74.1 7.5 %collective-permute-start.27 = (bf16[384,256]{1,0:T(8,128)(2,1)S(1)}, bf16[384,256]{1,0:T(8,128)(2,1)}, u32[]{:S(2)}, u32[]{:S(2)}) collective-permute-start(bf16[384,256]{1,0:T(8,128)(2,1)S(1)} %collective-permute-done.26.refs_22_), channel_id=1, source_target_pairs={{0,1},{1,0},{2,3},{3,2},{4,5},{5,4},{6,7},{7,6},{12,13},{13,12},{1... | collective-permute-start | bytes 589832 | tf_op jit(solution)/shard_map/ppermute | solution.py:62
  75.2 11.4 %collective-permute-start.22 = (bf16[64,2048]{1,0:T(8,128)(2,1)S(1)}, bf16[64,2048]{1,0:T(8,128)(2,1)S(1)}, u32[]{:S(2)}, u32[]{:S(2)}) collective-permute-start(bf16[64,2048]{1,0:T(8,128)(2,1)S(1)} %add_convert_fusion.5), channel_id=1, source_target_pairs={{0,2},{1,3},{2,0},{3,1},{4,6},{5,7},{6,4},{7,5},{12,14},{13,15},{1... | collective-permute-start | bytes 786440 | tf_op jit(solution)/shard_map/ppermute | solution.py:58
  79.5 7.1 %copy-start.4 = (bf16[128,2048]{1,0:T(8,128)(2,1)S(1)}, bf16[128,2048]{1,0:T(8,128)(2,1)}, u32[]{:S(2)}) copy-start(bf16[128,2048]{1,0:T(8,128)(2,1)} %get-tuple-element.38) | copy-start | bytes 1572868
  79.5 0.7 copy-start.22
  80.2 0.7 copy-start.23
  80.9 0.7 copy-start.24
  86.8 9.5 %collective-permute-start.28 = (bf16[64,2048]{1,0:T(8,128)(2,1)S(1)}, bf16[64,2048]{1,0:T(8,128)(2,1)S(1)}, u32[]{:S(2)}, u32[]{:S(2)}) collective-permute-start(bf16[64,2048]{1,0:T(8,128)(2,1)S(1)} %add_convert_fusion.3), channel_id=1, source_target_pairs={{0,4},{1,5},{2,6},{3,7},{4,12},{5,13},{6,14},{7,15},{12,8},{13,9},... | collective-permute-start | bytes 786440 | tf_op jit(solution)/shard_map/ppermute | solution.py:54
  87.0 9.3 %collective-permute-start.21 = (bf16[64,2048]{1,0:T(8,128)(2,1)S(1)}, bf16[64,2048]{1,0:T(8,128)(2,1)S(1)}, u32[]{:S(2)}, u32[]{:S(2)}) collective-permute-start(bf16[64,2048]{1,0:T(8,128)(2,1)S(1)} %get-tuple-element.52), channel_id=1, source_target_pairs={{0,2},{1,3},{2,0},{3,1},{4,6},{5,7},{6,4},{7,5},{12,14},{13,15},{1... | collective-permute-start | bytes 786440 | tf_op jit(solution)/shard_map/ppermute | solution.py:58
  90.1 6.2 %copy-start.2 = (bf16[128,2048]{1,0:T(8,128)(2,1)S(1)}, bf16[128,2048]{1,0:T(8,128)(2,1)}, u32[]{:S(2)}) copy-start(bf16[128,2048]{1,0:T(8,128)(2,1)} %get-tuple-element.37) | copy-start | bytes 1572868
  96.4 8.5 %copy-start.1 = (bf16[128,2048]{1,0:T(8,128)(2,1)S(1)}, bf16[128,2048]{1,0:T(8,128)(2,1)}, u32[]{:S(2)}) copy-start(bf16[128,2048]{1,0:T(8,128)(2,1)} %get-tuple-element.33) | copy-start | bytes 1572868
  96.4 8.5 %collective-permute-start.29 = (bf16[64,2048]{1,0:T(8,128)(2,1)S(1)}, bf16[64,2048]{1,0:T(8,128)(2,1)S(1)}, u32[]{:S(2)}, u32[]{:S(2)}) collective-permute-start(bf16[64,2048]{1,0:T(8,128)(2,1)S(1)} %add_convert_fusion.2), channel_id=1, source_target_pairs={{0,4},{1,5},{2,6},{3,7},{4,12},{5,13},{6,14},{7,15},{12,8},{13,9},... | collective-permute-start | bytes 786440 | tf_op jit(solution)/shard_map/ppermute | solution.py:54
  96.5 8.4 %collective-permute-start.20 = (bf16[64,2048]{1,0:T(8,128)(2,1)S(1)}, bf16[64,2048]{1,0:T(8,128)(2,1)S(1)}, u32[]{:S(2)}, u32[]{:S(2)}) collective-permute-start(bf16[64,2048]{1,0:T(8,128)(2,1)S(1)} %get-tuple-element.50), channel_id=1, source_target_pairs={{0,2},{1,3},{2,0},{3,1},{4,6},{5,7},{6,4},{7,5},{12,14},{13,15},{1... | collective-permute-start | bytes 786440 | tf_op jit(solution)/shard_map/ppermute | solution.py:58
  105.0 7.6 %copy-start = (bf16[64,1,2048]{2,0,1:T(8,128)(2,1)S(1)}, bf16[64,1,2048]{2,0,1:T(8,128)(2,1)}, u32[]{:S(2)}) copy-start(bf16[64,1,2048]{2,0,1:T(8,128)(2,1)} %param.9) | copy-start | bytes 786436
  105.1 7.6 %copy-start.3 = (bf16[128,2048]{1,0:T(8,128)(2,1)S(1)}, bf16[128,2048]{1,0:T(8,128)(2,1)}, u32[]{:S(2)}) copy-start(bf16[128,2048]{1,0:T(8,128)(2,1)} %get-tuple-element.39) | copy-start | bytes 1572868
  105.1 7.6 %collective-permute-start.31 = (bf16[64,2048]{1,0:T(8,128)(2,1)S(1)}, bf16[64,2048]{1,0:T(8,128)(2,1)S(1)}, u32[]{:S(2)}, u32[]{:S(2)}) collective-permute-start(bf16[64,2048]{1,0:T(8,128)(2,1)S(1)} %add_convert_fusion.1), channel_id=1, source_target_pairs={{0,4},{1,5},{2,6},{3,7},{4,12},{5,13},{6,14},{7,15},{12,8},{13,9},... | collective-permute-start | bytes 786440 | tf_op jit(solution)/shard_map/ppermute | solution.py:54
  105.1 7.5 %collective-permute-start.30 = (bf16[64,2048]{1,0:T(8,128)(2,1)S(1)}, bf16[64,2048]{1,0:T(8,128)(2,1)S(1)}, u32[]{:S(2)}, u32[]{:S(2)}) collective-permute-start(bf16[64,2048]{1,0:T(8,128)(2,1)S(1)} %get-tuple-element.51), channel_id=1, source_target_pairs={{0,2},{1,3},{2,0},{3,1},{4,6},{5,7},{6,4},{7,5},{12,14},{13,15},{1... | collective-permute-start | bytes 786440 | tf_op jit(solution)/shard_map/ppermute | solution.py:58

commit v4 on v3

--- a/solution.py
+++ b/solution.py
@@ -18,6 +18,7 @@
 F32 = jnp.float32
 BF16 = jnp.bfloat16
 ANY = pl.BlockSpec(memory_space=pl.ANY)
+SHORT = pl.CostEstimate(flops=1, bytes_accessed=1, transcendentals=0)
 IN_VMEM = pl.BlockSpec(memory_space=pltpu.VMEM)
 
 
@@ -41,17 +42,21 @@
     ]
 
 
-def ring_step():
+def ring_steps(steps):
     return [
-        (device_index(p, y, c), device_index(p + 1, y, c))
+        (device_index(p, y, c), device_index(p + steps, y, c))
         for p in range(LINE)
         for y in range(2)
         for c in range(2)
     ]
 
 
-def along_ring(x):
-    return lax.ppermute(x, "seq", ring_step())
+def forward(x):
+    return lax.ppermute(x, "seq", ring_steps(1))
+
+
+def backward(x):
+    return lax.ppermute(x, "seq", ring_steps(LINE - 1))
 
 
 def across(x):
@@ -107,9 +112,7 @@
             jax.ShapeDtypeStruct((small_rows, keys.shape[1]), BF16),
         ],
         scratch_shapes=[pltpu.VMEM((META, META), F32)],
-        cost_estimate=pl.CostEstimate(
-            flops=4 * rows * width, bytes_accessed=4 * rows * width, transcendentals=0
-        ),
+        cost_estimate=SHORT,
         name="normalize_and_pack",
     )(activations, norm_gain.reshape(1, width), ids, gates, keys, value_weight)
 
@@ -269,11 +272,7 @@
             pltpu.SemaphoreType.DMA((groups, max(len(t) for t in targets))),
         ],
         compiler_params=pltpu.CompilerParams(vmem_limit_bytes=VMEM_LIMIT),
-        cost_estimate=pl.CostEstimate(
-            flops=6 * all_slots * width * units + 4 * all_slots * rows * width,
-            bytes_accessed=4 * total * width + 6 * units * width,
-            transcendentals=all_slots * units,
-        ),
+        cost_estimate=SHORT,
         name="experts",
     )(*arrays, w_gate_up, w_down)
 
@@ -319,7 +318,7 @@
 
 
 def make_values(arrays, blocks, smalls, small_blocks, key_rows, width, earlier):
-    smalls = [after(smalls[0], earlier), *smalls[1:]]
+    smalls = [after(smalls[0], *earlier), *smalls[1:]]
     kv_width = smalls[0].shape[1]
     total = key_rows * len(blocks)
     kv = jax.ShapeDtypeStruct((total, kv_width), BF16)
@@ -334,11 +333,7 @@
             pltpu.SemaphoreType.DMA((3, len(blocks))),
         ],
         compiler_params=pltpu.CompilerParams(vmem_limit_bytes=VMEM_LIMIT),
-        cost_estimate=pl.CostEstimate(
-            flops=2 * total * width * kv_width,
-            bytes_accessed=2 * total * width + 2 * width * kv_width,
-            transcendentals=0,
-        ),
+        cost_estimate=SHORT,
         name="values",
     )(*arrays, *smalls)
 
@@ -426,11 +421,7 @@
         out_specs=pl.BlockSpec((q_rows, part_width), lambda i: (0, part)),
         input_output_aliases={3: 0} if before else {},
         compiler_params=pltpu.CompilerParams(vmem_limit_bytes=VMEM_LIMIT),
-        cost_estimate=pl.CostEstimate(
-            flops=4 * q_rows * part_width * total,
-            bytes_accessed=4 * total * HEAD_DIMENSION + 4 * q_rows * part_width,
-            transcendentals=part_width // HEAD_DIMENSION * q_rows * total,
-        ),
+        cost_estimate=SHORT,
         name="attention",
     )(queries, keys, values, *before)
 
@@ -445,68 +436,79 @@
 
 def on_line(acts, packed, small, queries, w_gate_up, w_down, top, capacity):
     rows, width = acts.shape
-    arrays, blocks, sources = [], [], []
-    moving = packed
+    line = [packed, forward(packed), None, backward(packed)]
+    crossed = [across(packed), across(line[1]), None, across(line[3])]
     pair = jnp.concatenate([small, across(small)], axis=0)
+    line[2] = forward(after(line[1], pair, crossed[0]))
+    crossed[2] = across(line[2])
+    arrays = [
+        [line[step], crossed[step], other_core(line[step]), other_core(crossed[step])]
+        for step in range(LINE)
+    ]
+    blocks = [
+        (4 * step + core * 2 + y, 0, functools.partial(from_device, step, y, core))
+        for step in range(LINE)
+        for core in range(2)
+        for y in range(2)
+    ]
+    pair = after(pair, line[3])
+    pairs = [pair, forward(pair), None, backward(pair)]
+    pairs[2] = forward(pairs[1])
+    small_rows = small.shape[0]
+    small_blocks = [
+        (2 * step + core, y * small_rows, functools.partial(from_device, step, y, core))
+        for step in range(LINE)
+        for core in range(2)
+        for y in range(2)
+    ]
+
+    keep, mine, crossing = [None] * LINE, [None] * LINE, [None] * LINE
+
+    def experts(first, second, before, beside):
+        ready = arrays[first] + arrays[second]
+        ready = [after(ready[0], *before), *ready[1:]]
+        sources = [[(4 * group + i, 0, rows) for i in range(4)] for group in range(2)]
+        targets = [[(group, 0, 2 * rows), (2, group * 2 * rows, 2 * rows)] for group in range(2)]
+        keep[first], keep[second], send = run_experts(
+            ready,
+            sources,
+            targets,
+            [2 * rows, 2 * rows, 4 * rows],
+            w_gate_up,
+            w_down,
+            top,
+            rows,
+            capacity,
+        )
+        came = other_core(after(send, *beside))
+        for at, step in ((0, first), (2 * rows, second)):
+            mine[step] = (keep[step][:rows], came[at : at + rows])
+            crossing[step] = summed(keep[step][rows:], came[at + rows : at + 2 * rows])
+        return send
+
+    theirs = [None] * LINE
+    experts(1, 0, [line[2], crossed[3]], [crossed[2], pairs[1]])
+    theirs[1] = across(crossing[1])
+    send = experts(2, 3, [crossing[0], crossing[1]], [theirs[1], pairs[2], pairs[3]])
+    total = summed(*mine[1], after(theirs[1], send))
+    moving = forward(total)
+    smalls = []
     for step in range(LINE):
-        if step == 1:
-            moving = along_ring(moving)
-        elif step == 2:
-            moving = along_ring(after(moving, pair, arrays[1]))
-        elif step > 2:
-            moving = along_ring(after(moving, arrays[4 * step - 7], *arrays[4 * step - 10 : 4 * step - 8]))
-        crossed = across(moving)
-        arrays += [moving, crossed, other_core(moving), other_core(crossed)]
-        sources.append([(4 * step + i, 0, rows) for i in range(4)])
-        blocks += [
-            (4 * step + core * 2 + y, 0, functools.partial(from_device, step, y, core))
-            for core in range(2)
-            for y in range(2)
-        ]
-    small_rows = small.shape[0]
-    pair = after(pair, moving, arrays[-7], *arrays[-10:-8])
-    smalls, small_blocks = [], []
-    for step in range(LINE):
-        if step > 0:
-            pair = along_ring(pair if step != 2 else after(pair, *arrays[-6:-4]))
-        if step == LINE - 2:
-            arrays[0] = after(arrays[0], pair)
-        smalls += [pair, other_core(pair)]
-        small_blocks += [
-            (2 * step + core, y * small_rows, functools.partial(from_device, step, y, core))
-            for core in range(2)
-            for y in range(2)
-        ]
-    targets = [
-        [(0, 0, 2 * rows), (5, 4 * rows, 2 * rows)],
-        [(1, 0, 2 * rows), (4, 0, 2 * rows)],
-        [(2, 0, 2 * rows), (5, 0, 2 * rows)],
-        [(3, 0, 2 * rows), (5, 2 * rows, 2 * rows)],
-    ]
-    out_rows = [2 * rows] * 5 + [6 * rows]
-    *keep, send_first, send_rest = run_experts(
-        arrays, sources, targets, out_rows, w_gate_up, w_down, top, rows, capacity
+        smalls += [pairs[step], other_core(after(pairs[step], total))]
+    theirs[2], theirs[3] = across(crossing[2]), across(crossing[3])
+    new_keys, values = make_values(
+        sum(arrays, []), blocks, smalls, small_blocks, rows, width, crossing[2:]
     )
-    came_first = other_core(send_first)
-    came_rest = other_core(after(send_rest, came_first))
-    came = [came_rest[4 * rows :], came_first, came_rest[: 2 * rows], came_rest[2 * rows : 4 * rows]]
-    crossing = [summed(keep[step][rows:], came[step][rows:]) for step in range(LINE)]
-    theirs = [across(crossing[step]) for step in (1, 2, 3, 0)]
-    theirs = [theirs[3], *theirs[:3]]
-    new_keys, values = make_values(
-        arrays, blocks, smalls, small_blocks, rows, width, crossing[0]
-    )
-    total = summed(keep[1][:rows], came[1][:rows], after(theirs[1], values))
-    moving = along_ring(total)
+    total = summed(*mine[2], theirs[2], after(moving, values))
+    moving = forward(total)
+    theirs[0] = across(after(crossing[0], total))
     context = attend_part(after(queries, total), new_keys, values, 0, 4)
     context = attend_part(queries, new_keys, values, 1, 4, context)
-    total = summed(keep[2][:rows], came[2][:rows], theirs[2], after(moving, context))
-    moving = along_ring(total)
+    total = summed(*mine[3], theirs[3], after(moving, context))
+    moving = forward(total)
     context = attend_part(after(queries, total), new_keys, values, 2, 4, context)
-    total = summed(keep[3][:rows], came[3][:rows], theirs[3], after(moving, context))
-    moving = along_ring(total)
-    context = attend_part(after(queries, total), new_keys, values, 3, 4, context)
-    layer_out = summed(acts, keep[0][:rows], came[0][:rows], theirs[0], after(moving, context))
+    context = attend_part(queries, new_keys, values, 3, 4, context)
+    layer_out = summed(acts, *mine[0], theirs[0], after(moving, context))
     return context, layer_out
 
 

time: 114 us -> 99.5 us (0.87)
  waiting for transfers between devices: 54.1 us -> 19.2 us
  starting transfers between devices: 20.2 us -> 29.5 us
  other arithmetic: 3.69 us -> 9.54 us
  Pallas kernels: 30 us -> 35.1 us
    ppermute x9, waiting for transfers between devices: 39.4 us -> 9.09 us  [the longest x7 9.08 us: forward(): return lax.ppermute(x, 'seq', ring_steps(1))]
    ppermute x9, starting transfers between devices: 7.22 us -> 19.9 us  [the longest x7 18.5 us: forward(): return lax.ppermute(x, 'seq', ring_steps(1))]
    ppermute x9, waiting for transfers between devices: 12.6 us -> 5.02 us  [across(): return lax.ppermute(x, 'seq', swaps(1, 0))]
    convert_element_type x5, other arithmetic: 2.82 us -> 8.67 us  [summed(): return sum((term.astype(F32) for term in terms)).astype(BF16)]
    pallas_call x1 -> x2, Pallas kernels: 11.6 us -> 16.7 us  [run_experts(): pl.pallas_call(functools.partial(expert_kernel, top, tok_rows, capacity,...]
    ppermute x9, starting transfers between devices: 10.6 us -> 7.21 us  [across(): return lax.ppermute(x, 'seq', swaps(1, 0))]
    ppermute x14, waiting for transfers between devices: 2.14 us -> 5.09 us  [other_core(): return lax.ppermute(x, 'seq', swaps(0, 1))]
    unnamed x51 -> x55, local copies, waits for them, and re-layouts: 4.54 us -> 4.84 us
  transfers between devices with their start and end apart: 32 -> 32, of which waited for: 12 -> 13; matrix products, arithmetic and copies ran while one was open for 3% -> 7% of each run, Pallas kernels for 15% -> 34%
where the time goes in v4:
time: 99.5 us; the launch traced here: 99.1 us
  Pallas kernels  35.1 us (35%)
  starting transfers between devices  29.5 us (30%)
  waiting for transfers between devices  19.2 us (19%)
  other arithmetic  9.54 us (10%)
  local copies, waits for them, and re-layouts  4.85 us (5%)
    ppermute x7, starting transfers between devices, forward(): return lax.ppermute(x, 'seq', ring_steps(1))  18.5 us
    pallas_call x2, Pallas kernels, run_experts(): pl.pallas_call(functools.partial(expert_kernel, top, tok_rows, capacity,...  16.7 us
    pallas_call x4, Pallas kernels, attend_part(): pl.pallas_call(functools.partial(attention_kernel, chunk), grid=(1,), out...  11.5 us
    ppermute x7, waiting for transfers between devices, forward(): return lax.ppermute(x, 'seq', ring_steps(1))  9.08 us
    convert_element_type x5, other arithmetic, summed(): return sum((term.astype(F32) for term in terms)).astype(BF16)  8.67 us
    ppermute x9, starting transfers between devices, across(): return lax.ppermute(x, 'seq', swaps(1, 0))  7.21 us
    ppermute x14, waiting for transfers between devices, other_core(): return lax.ppermute(x, 'seq', swaps(0, 1))  5.09 us
    pallas_call x1, Pallas kernels, make_values(): pl.pallas_call(functools.partial(value_kernel, key_rows, blocks, small_bl...  5.02 us
  transfers between devices with their start and end apart: 32, of which 13 were waited for; matrix products, arithmetic and copies ran while one was open for 7% of the time, Pallas kernels for 34%

profile of v4, /device:TPU:0, one launch (start us, length us, event | category | flops | bytes accessed | tf_op | source)
XLA Modules:
  0.0 99.1 jit_solution(11879996019805813084)
XLA Ops:
  0.6 1.9 %normalize_and_pack.1 = (bf16[64,2176]{1,0:T(8,128)(2,1)}, bf16[192,256]{1,0:T(8,128)(2,1)}) custom-call(bf16[64,2048]{1,0:T(8,128)(2,1)} %bitcast.25, f32[1,2048]{1,0:T(1,128)} %bitcast.27, s32[4,64]{1,0:T(4,128)} %bitcast.28, f32[4,64]{1,0:T(4,128)} %bitcast.29, bf16[64,256]{1,0:T(8,128)(2,1)} %bitcast.26, bf16[128,256]{1,0:T(8,128)(2,1)} %weight_ref.1), custom_call_target="tpu_custom_call" | custom-call | flops 1 | bytes 1 | tf_op jit(solution)/shard_map/normalize_and_pack/pallas_call | solution.py:108
  2.5 3.0 %collective-permute-start.3 = (bf16[64,2176]{1,0:T(8,128)(2,1)}, bf16[64,2176]{1,0:T(8,128)(2,1)S(1)}, u32[]{:S(2)}, u32[]{:S(2)}) collective-permute-start(bf16[64,2176]{1,0:T(8,128)(2,1)} %get-tuple-element.30.refs_4_.refs_0_), channel_id=1, source_target_pairs={{0,4},{1,5},{2,6},{3,7},{4,12},{5,13},{6,14},{7,15},{12,8},{13,9},... | collective-permute-start | bytes 835592 | tf_op jit(solution)/shard_map/ppermute | solution.py:55
  5.5 1.5 %collective-permute-start = (bf16[64,2176]{1,0:T(8,128)(2,1)}, bf16[64,2176]{1,0:T(8,128)(2,1)S(1)}, u32[]{:S(2)}, u32[]{:S(2)}) collective-permute-start(bf16[64,2176]{1,0:T(8,128)(2,1)} %get-tuple-element.30.refs_4_.refs_0_), channel_id=1, source_target_pairs={{0,2},{1,3},{2,0},{3,1},{4,6},{5,7},{6,4},{7,5},{12,14},{13,15},{1... | collective-permute-start | bytes 835592 | tf_op jit(solution)/shard_map/ppermute | solution.py:63
  7.0 1.3 %collective-permute-start.12 = (bf16[64,2176]{1,0:T(8,128)(2,1)}, bf16[64,2176]{1,0:T(8,128)(2,1)S(1)}, u32[]{:S(2)}, u32[]{:S(2)}) collective-permute-start(bf16[64,2176]{1,0:T(8,128)(2,1)} %get-tuple-element.30.refs_4_.refs_0_), channel_id=1, source_target_pairs={{0,8},{1,9},{2,10},{3,11},{4,0},{5,1},{6,2},{7,3},{12,4},{13,5},{1... | collective-permute-start | bytes 835592 | tf_op jit(solution)/shard_map/ppermute | solution.py:59
  8.4 0.2 collective-permute-start.7
  8.6 0.9 constant_dynamic-update-slice_fusion.1
  9.5 4.0 %collective-permute-done.3.refs_0_.refs_4_ = bf16[64,2176]{1,0:T(8,128)(2,1)S(1)} collective-permute-done((bf16[64,2176]{1,0:T(8,128)(2,1)}, bf16[64,2176]{1,0:T(8,128)(2,1)S(1)}, u32[]{:S(2)}, u32[]{:S(2)}) %collective-permute-start.3) | collective-permute-done | bytes 278560 | tf_op jit(solution)/shard_map/ppermute | solution.py:55
  13.5 1.6 %collective-permute-start.4 = (bf16[64,2176]{1,0:T(8,128)(2,1)S(1)}, bf16[64,2176]{1,0:T(8,128)(2,1)S(1)}, u32[]{:S(2)}, u32[]{:S(2)}) collective-permute-start(bf16[64,2176]{1,0:T(8,128)(2,1)S(1)} %collective-permute-done.3.refs_0_.refs_4_), channel_id=1, source_target_pairs={{0,2},{1,3},{2,0},{3,1},{4,6},{5,7},{6,4},{7,5},{12,14},{13,15},{1... | collective-permute-start | bytes 835592 | tf_op jit(solution)/shard_map/ppermute | solution.py:63
  15.1 1.4 %collective-permute-done.7 = bf16[192,256]{1,0:T(8,128)(2,1)S(1)} collective-permute-done((bf16[192,256]{1,0:T(8,128)(2,1)}, bf16[192,256]{1,0:T(8,128)(2,1)S(1)}, u32[]{:S(2)}, u32[]{:S(2)}) %collective-permute-start.7) | collective-permute-done | bytes 98336 | tf_op jit(solution)/shard_map/ppermute | solution.py:63
  16.6 6.4 %collective-permute-start.8 = (bf16[64,2176]{1,0:T(8,128)(2,1)S(1)}, bf16[64,2176]{1,0:T(8,128)(2,1)S(1)}, u32[]{:S(2)}, u32[]{:S(2)}) collective-permute-start(bf16[64,2176]{1,0:T(8,128)(2,1)S(1)} %collective-permute-done.3.refs_0_.refs_4_), channel_id=1, source_target_pairs={{0,4},{1,5},{2,6},{3,7},{4,12},{5,13},{6,14},{7,15},{12,8},{13,9},... | collective-permute-start | bytes 835592 | tf_op jit(solution)/shard_map/ppermute | solution.py:55
  23.0 0.4 collective-permute-start.13
  23.4 0.5 collective-permute-start.2
  23.9 0.1 collective-permute-start.6
  24.0 3.1 %collective-permute-done.8.refs_0_.refs_8_ = bf16[64,2176]{1,0:T(8,128)(2,1)S(1)} collective-permute-done((bf16[64,2176]{1,0:T(8,128)(2,1)S(1)}, bf16[64,2176]{1,0:T(8,128)(2,1)S(1)}, u32[]{:S(2)}, u32[]{:S(2)}) %collective-permute-start.8) | collective-permute-done | bytes 278560 | tf_op jit(solution)/shard_map/ppermute | solution.py:55
  27.0 1.0 collective-permute-start.9
  28.0 2.6 %collective-permute-done.13.refs_5_.refs_13_ = bf16[64,2176]{1,0:T(8,128)(2,1)S(1)} collective-permute-done((bf16[64,2176]{1,0:T(8,128)(2,1)S(1)}, bf16[64,2176]{1,0:T(8,128)(2,1)S(1)}, u32[]{:S(2)}, u32[]{:S(2)}) %collective-permute-start.13) | collective-permute-done | bytes 278560 | tf_op jit(solution)/shard_map/ppermute | solution.py:63
  30.6 3.2 %collective-permute-start.16 = (bf16[384,256]{1,0:T(8,128)(2,1)S(1)}, bf16[384,256]{1,0:T(8,128)(2,1)S(1)}, u32[]{:S(2)}, u32[]{:S(2)}) collective-permute-start(bf16[384,256]{1,0:T(8,128)(2,1)S(1)} %constant_dynamic-update-slice_fusion.refs_16_), channel_id=1, source_target_pairs={{0,4},{1,5},{2,6},{3,7},{4,12},{5,13},{6,14},{7,15},{12,8},{13,9},... | collective-permute-start | bytes 589832 | tf_op jit(solution)/shard_map/ppermute | solution.py:55
  33.9 0.6 copy-done.7
  34.5 0.1 copy-done.8
  34.6 0.1 copy-done.9
  34.7 8.3 %experts.2 = (bf16[128,2048]{1,0:T(8,128)(2,1)}, bf16[128,2048]{1,0:T(8,128)(2,1)}, bf16[256,2048]{1,0:T(8,128)(2,1)}) custom-call(bf16[64,2176]{1,0:T(8,128)(2,1)} %copy-done, bf16[64,2176]{1,0:T(8,128)(2,1)} %copy-done.4, bf16[64,2176]{1,0:T(8,128)(2,1)} %copy-done.7, bf16[64,2176]{1,0:T(8,128)(2,1)} %copy-done.9, ...), custom_call_target="tpu_custom_call" | custom-call | flops 1 | bytes 1 | tf_op jit(solution)/shard_map/experts/pallas_call | solution.py:256
  43.1 0.7 copy-done.21
  43.8 0.5 collective-permute-start.14
  44.3 0.0 collective-permute-start.15
  44.3 0.5 collective-permute-start.10
  44.8 3.3 %collective-permute-done.17 = bf16[256,2048]{1,0:T(8,128)(2,1)S(1)} collective-permute-done((bf16[256,2048]{1,0:T(8,128)(2,1)}, bf16[256,2048]{1,0:T(8,128)(2,1)S(1)}, u32[]{:S(2)}, u32[]{:S(2)}) %collective-permute-start.17) | collective-permute-done | bytes 1048608 | tf_op jit(solution)/shard_map/ppermute | solution.py:67
  48.1 2.0 %add_convert_fusion.6 = (bf16[64,2048]{1,0:T(8,128)(2,1)}, bf16[64,2048]{1,0:T(8,128)(2,1)}) fusion(bf16[256,2048]{1,0:T(8,128)(2,1)S(1)} %collective-permute-done.17, bf16[128,2048]{1,0:T(8,128)(2,1)} %get-tuple-element.38, bf16[128,2048]{1,0:T(8,128)(2,1)} %get-tuple-element.35), kind=kLoop, calls=%fused_computation.6 | loop fusion | flops 1048576 | bytes 1572864 | tf_op jit(solution)/shard_map/convert_element_type | solution.py:430
  50.1 0.1 collective-permute-start.18
  50.2 0.1 collective-permute-start.20
  50.3 2.0 %collective-permute-start.19 = (bf16[384,256]{1,0:T(8,128)(2,1)}, bf16[384,256]{1,0:T(8,128)(2,1)S(1)}, u32[]{:S(2)}, u32[]{:S(2)}) collective-permute-start(bf16[384,256]{1,0:T(8,128)(2,1)} %copy-done.21), channel_id=1, source_target_pairs={{0,4},{1,5},{2,6},{3,7},{4,12},{5,13},{6,14},{7,15},{12,8},{13,9},... | collective-permute-start | bytes 589832 | tf_op jit(solution)/shard_map/ppermute | solution.py:55
  52.4 0.7 copy-done.13
  53.0 0.7 copy-done.14
  53.8 8.4 %experts.3 = (bf16[128,2048]{1,0:T(8,128)(2,1)}, bf16[128,2048]{1,0:T(8,128)(2,1)}, bf16[256,2048]{1,0:T(8,128)(2,1)}) custom-call(bf16[64,2176]{1,0:T(8,128)(2,1)} %copy-done.5, bf16[64,2176]{1,0:T(8,128)(2,1)} %copy-done.10, bf16[64,2176]{1,0:T(8,128)(2,1)} %copy-done.13, bf16[64,2176]{1,0:T(8,128)(2,1)} %copy-done.14, bf16[64,2176]{1,0:T(8,128)(2,1)} %copy-done.2, ...), custom_call_target="tpu_custom_call" | custom-call | flops 1 | bytes 1 | tf_op jit(solution)/shard_map/experts/pallas_call | solution.py:256
  62.1 0.5 collective-permute-done.19.refs_20_
  62.6 0.2 copy-done.22
  62.8 0.5 copy-done.23
  63.3 1.7 %add_convert_fusion.3 = bf16[64,2048]{1,0:T(8,128)(2,1)} fusion(bf16[64,2048]{1,0:T(8,128)(2,1)} %collective-permute-done.18, bf16[256,2048]{1,0:T(8,128)(2,1)S(1)} %collective-permute-done.17, bf16[128,2048]{1,0:T(8,128)(2,1)S(1)} %copy-done.19), kind=kLoop, calls=%fused_computation.3 | loop fusion | flops 786432 | bytes 1048576 | tf_op jit(solution)/shard_map/convert_element_type | solution.py:430
  65.1 2.3 %collective-permute-start.28 = (bf16[64,2048]{1,0:T(8,128)(2,1)}, bf16[64,2048]{1,0:T(8,128)(2,1)}, u32[]{:S(2)}, u32[]{:S(2)}) collective-permute-start(bf16[64,2048]{1,0:T(8,128)(2,1)} %add_convert_fusion.3), channel_id=1, source_target_pairs={{0,4},{1,5},{2,6},{3,7},{4,12},{5,13},{6,14},{7,15},{12,8},{13,9},... | collective-permute-start | bytes 786440 | tf_op jit(solution)/shard_map/ppermute | solution.py:55
  67.4 0.2 collective-permute-start.22
  67.6 1.9 %add_convert_fusion.4 = (bf16[64,2048]{1,0:T(8,128)(2,1)}, bf16[64,2048]{1,0:T(8,128)(2,1)}) fusion(bf16[256,2048]{1,0:T(8,128)(2,1)S(1)} %collective-permute-done.21, bf16[128,2048]{1,0:T(8,128)(2,1)} %get-tuple-element.43, bf16[128,2048]{1,0:T(8,128)(2,1)} %get-tuple-element.40), kind=kLoop, calls=%fused_computation.4 | loop fusion | flops 1048576 | bytes 1572864 | tf_op jit(solution)/shard_map/convert_element_type | solution.py:430
  69.6 0.4 collective-permute-start.27
  69.9 0.5 collective-permute-start.24
  70.5 0.1 collective-permute-start.25
  70.5 1.1 %collective-permute-done.23.refs_19_ = bf16[384,256]{1,0:T(8,128)(2,1)S(1)} collective-permute-done((bf16[384,256]{1,0:T(8,128)(2,1)}, bf16[384,256]{1,0:T(8,128)(2,1)S(1)}, u32[]{:S(2)}, u32[]{:S(2)}) %collective-permute-start.23) | collective-permute-done | bytes 196640 | tf_op jit(solution)/shard_map/ppermute | solution.py:67
  71.6 0.3 collective-permute-done.24.refs_21_
  71.9 0.4 collective-permute-done.25.refs_23_
  72.3 0.3 copy-done.26
  72.5 5.0 %values.1 = (bf16[1024,256]{1,0:T(8,128)(2,1)}, bf16[1024,256]{1,0:T(8,128)(2,1)}) custom-call(bf16[64,2176]{1,0:T(8,128)(2,1)} %get-tuple-element.30.refs_4_.refs_0_, bf16[64,2176]{1,0:T(8,128)(2,1)} %copy-done.1, bf16[64,2176]{1,0:T(8,128)(2,1)} %copy-done.3, bf16[64,2176]{1,0:T(8,128)(2,1)} %copy-done.8, bf16[64,2176]{1,0:T(8,128)(2,1)} %copy-done, ...), custom_call_target="tpu_custom_call" | custom-call | flops 1 | bytes 1 | tf_op jit(solution)/shard_map/values/pallas_call | solution.py:325
  77.6 0.0 copy-start.15
  77.6 0.8 collective-permute-done.27
  78.4 1.9 %add_convert_fusion.2 = bf16[64,2048]{1,0:T(8,128)(2,1)} fusion(bf16[64,2048]{1,0:T(8,128)(2,1)} %collective-permute-done.28, bf16[64,2048]{1,0:T(8,128)(2,1)} %collective-permute-done.27, bf16[256,2048]{1,0:T(8,128)(2,1)S(1)} %collective-permute-done.21, bf16[128,2048]{1,0:T(8,128)(2,1)S(1)} %copy-done.17), kind=kLoop, calls=%fused_computation.2 | loop fusion | flops 1048576 | bytes 1310720 | tf_op jit(solution)/shard_map/convert_element_type | solution.py:430
  80.2 0.7 collective-permute-start.29
  81.0 1.1 %collective-permute-start.26 = (bf16[64,2048]{1,0:T(8,128)(2,1)}, bf16[64,2048]{1,0:T(8,128)(2,1)}, u32[]{:S(2)}, u32[]{:S(2)}) collective-permute-start(bf16[64,2048]{1,0:T(8,128)(2,1)} %get-tuple-element.58), channel_id=1, source_target_pairs={{0,2},{1,3},{2,0},{3,1},{4,6},{5,7},{6,4},{7,5},{12,14},{13,15},{1... | collective-permute-start | bytes 786440 | tf_op jit(solution)/shard_map/ppermute | solution.py:63
  82.1 2.9 %attention.4.refs_0_ = bf16[64,4096]{1,0:T(8,128)(2,1)} custom-call(bf16[64,4096]{1,0:T(8,128)(2,1)} %bitcast.20, bf16[1024,256]{1,0:T(8,128)(2,1)} %get-tuple-element.50.k_ref, bf16[1024,256]{1,0:T(8,128)(2,1)} %get-tuple-element.51.v_ref), custom_call_target="tpu_custom_call" | custom-call | flops 1 | bytes 1 | tf_op jit(solution)/shard_map/attention/pallas_call | solution.py:411
  85.0 2.9 %attention.5.refs_0_ = bf16[64,4096]{1,0:T(8,128)(2,1)} custom-call(bf16[64,4096]{1,0:T(8,128)(2,1)} %bitcast.21, bf16[1024,256]{1,0:T(8,128)(2,1)} %get-tuple-element.50.k_ref, bf16[1024,256]{1,0:T(8,128)(2,1)} %get-tuple-element.51.v_ref, bf16[64,4096]{1,0:T(8,128)(2,1)} %attention.4.refs_0_), custom_call_target="tpu_custom_call", output_to_operand_aliasing={{}: (3, {})} | custom-call | flops 1 | bytes 1 | tf_op jit(solution)/shard_map/attention/pallas_call | solution.py:411
  87.9 1.3 %collective-permute-done.29 = bf16[64,2048]{1,0:T(8,128)(2,1)S(1)} collective-permute-done((bf16[64,2048]{1,0:T(8,128)(2,1)}, bf16[64,2048]{1,0:T(8,128)(2,1)S(1)}, u32[]{:S(2)}, u32[]{:S(2)}) %collective-permute-start.29) | collective-permute-done | bytes 262176 | tf_op jit(solution)/shard_map/ppermute | solution.py:55
  89.1 1.1 %add_convert_fusion.1 = bf16[64,2048]{1,0:T(8,128)(2,1)S(1)} fusion(bf16[64,2048]{1,0:T(8,128)(2,1)S(1)} %collective-permute-done.29, bf16[64,2048]{1,0:T(8,128)(2,1)} %collective-permute-done.26, bf16[256,2048]{1,0:T(8,128)(2,1)S(1)} %collective-permute-done.21, bf16[128,2048]{1,0:T(8,128)(2,1)S(1)} %copy-done.16), kind=kLoop, calls=%fused_computation.1 | loop fusion | flops 1048576 | bytes 1310720 | tf_op jit(solution)/shard_map/convert_element_type | solution.py:430
  90.2 0.8 collective-permute-start.31
  91.0 1.0 %collective-permute-start.30 = (bf16[64,2048]{1,0:T(8,128)(2,1)}, bf16[64,2048]{1,0:T(8,128)(2,1)S(1)}, u32[]{:S(2)}, u32[]{:S(2)}) collective-permute-start(bf16[64,2048]{1,0:T(8,128)(2,1)} %get-tuple-element.56), channel_id=1, source_target_pairs={{0,2},{1,3},{2,0},{3,1},{4,6},{5,7},{6,4},{7,5},{12,14},{13,15},{1... | collective-permute-start | bytes 786440 | tf_op jit(solution)/shard_map/ppermute | solution.py:63
  92.0 2.9 %attention.6.refs_0_ = bf16[64,4096]{1,0:T(8,128)(2,1)} custom-call(bf16[64,4096]{1,0:T(8,128)(2,1)} %bitcast.22, bf16[1024,256]{1,0:T(8,128)(2,1)} %get-tuple-element.50.k_ref, bf16[1024,256]{1,0:T(8,128)(2,1)} %get-tuple-element.51.v_ref, bf16[64,4096]{1,0:T(8,128)(2,1)} %attention.5.refs_0_), custom_call_target="tpu_custom_call", output_to_operand_aliasing={{}: (3, {})} | custom-call | flops 1 | bytes 1 | tf_op jit(solution)/shard_map/attention/pallas_call | solution.py:411
  94.9 2.9 %attention.7 = bf16[64,4096]{1,0:T(8,128)(2,1)} custom-call(bf16[64,4096]{1,0:T(8,128)(2,1)} %bitcast.23, bf16[1024,256]{1,0:T(8,128)(2,1)} %get-tuple-element.50.k_ref, bf16[1024,256]{1,0:T(8,128)(2,1)} %get-tuple-element.51.v_ref, bf16[64,4096]{1,0:T(8,128)(2,1)} %attention.6.refs_0_), custom_call_target="tpu_custom_call", output_to_operand_aliasing={{}: (3, {})} | custom-call | flops 1 | bytes 1 | tf_op jit(solution)/shard_map/attention/pallas_call | solution.py:411
  97.8 0.3 collective-permute-done.31
  98.0 0.2 collective-permute-done.30
  98.2 0.9 fusion
  (70 shorter events, 0.2 us)
Async XLA Ops:
  2.5 11.0 %collective-permute-start.3 = (bf16[64,2176]{1,0:T(8,128)(2,1)}, bf16[64,2176]{1,0:T(8,128)(2,1)S(1)}, u32[]{:S(2)}, u32[]{:S(2)}) collective-permute-start(bf16[64,2176]{1,0:T(8,128)(2,1)} %get-tuple-element.30.refs_4_.refs_0_), channel_id=1, source_target_pairs={{0,4},{1,5},{2,6},{3,7},{4,12},{5,13},{6,14},{7,15},{12,8},{13,9},... | collective-permute-start | bytes 835592 | tf_op jit(solution)/shard_map/ppermute | solution.py:55
  5.5 11.0 %collective-permute-start = (bf16[64,2176]{1,0:T(8,128)(2,1)}, bf16[64,2176]{1,0:T(8,128)(2,1)S(1)}, u32[]{:S(2)}, u32[]{:S(2)}) collective-permute-start(bf16[64,2176]{1,0:T(8,128)(2,1)} %get-tuple-element.30.refs_4_.refs_0_), channel_id=1, source_target_pairs={{0,2},{1,3},{2,0},{3,1},{4,6},{5,7},{6,4},{7,5},{12,14},{13,15},{1... | collective-permute-start | bytes 835592 | tf_op jit(solution)/shard_map/ppermute | solution.py:63
  7.0 15.9 %collective-permute-start.12 = (bf16[64,2176]{1,0:T(8,128)(2,1)}, bf16[64,2176]{1,0:T(8,128)(2,1)S(1)}, u32[]{:S(2)}, u32[]{:S(2)}) collective-permute-start(bf16[64,2176]{1,0:T(8,128)(2,1)} %get-tuple-element.30.refs_4_.refs_0_), channel_id=1, source_target_pairs={{0,8},{1,9},{2,10},{3,11},{4,0},{5,1},{6,2},{7,3},{12,4},{13,5},{1... | collective-permute-start | bytes 835592 | tf_op jit(solution)/shard_map/ppermute | solution.py:59
  8.4 15.0 %collective-permute-start.1 = (bf16[64,2176]{1,0:T(8,128)(2,1)}, bf16[64,2176]{1,0:T(8,128)(2,1)S(1)}, u32[]{:S(2)}, u32[]{:S(2)}) collective-permute-start(bf16[64,2176]{1,0:T(8,128)(2,1)} %get-tuple-element.30.refs_4_.refs_0_), channel_id=1, source_target_pairs={{0,1},{1,0},{2,3},{3,2},{4,5},{5,4},{6,7},{7,6},{12,13},{13,12},{1... | collective-permute-start | bytes 835592 | tf_op jit(solution)/shard_map/ppermute | solution.py:67
  8.4 8.1 %collective-permute-start.7 = (bf16[192,256]{1,0:T(8,128)(2,1)}, bf16[192,256]{1,0:T(8,128)(2,1)S(1)}, u32[]{:S(2)}, u32[]{:S(2)}) collective-permute-start(bf16[192,256]{1,0:T(8,128)(2,1)} %get-tuple-element.31), channel_id=1, source_target_pairs={{0,2},{1,3},{2,0},{3,1},{4,6},{5,7},{6,4},{7,5},{12,14},{13,15},{1... | collective-permute-start | bytes 294920 | tf_op jit(solution)/shard_map/ppermute | solution.py:63
  13.5 20.3 %copy-start = (bf16[64,2176]{1,0:T(8,128)(2,1)}, bf16[64,2176]{1,0:T(8,128)(2,1)S(1)}, u32[]{:S(2)}) copy-start(bf16[64,2176]{1,0:T(8,128)(2,1)S(1)} %collective-permute-done.3.refs_0_.refs_4_) | copy-start | bytes 835588
  13.5 10.4 %collective-permute-start.4 = (bf16[64,2176]{1,0:T(8,128)(2,1)S(1)}, bf16[64,2176]{1,0:T(8,128)(2,1)S(1)}, u32[]{:S(2)}, u32[]{:S(2)}) collective-permute-start(bf16[64,2176]{1,0:T(8,128)(2,1)S(1)} %collective-permute-done.3.refs_0_.refs_4_), channel_id=1, source_target_pairs={{0,2},{1,3},{2,0},{3,1},{4,6},{5,7},{6,4},{7,5},{12,14},{13,15},{1... | collective-permute-start | bytes 835592 | tf_op jit(solution)/shard_map/ppermute | solution.py:63
  16.5 55.8 %copy-start.20 = (bf16[384,256]{1,0:T(8,128)(2,1)}, bf16[384,256]{1,0:T(8,128)(2,1)S(1)}, u32[]{:S(2)}) copy-start(bf16[384,256]{1,0:T(8,128)(2,1)S(1)} %constant_dynamic-update-slice_fusion.refs_16_) | copy-start | bytes 589828
  16.5 17.3 %copy-start.1 = (bf16[64,2176]{1,0:T(8,128)(2,1)}, bf16[64,2176]{1,0:T(8,128)(2,1)S(1)}, u32[]{:S(2)}) copy-start(bf16[64,2176]{1,0:T(8,128)(2,1)S(1)} %collective-permute-done.refs_5_.refs_1_) | copy-start | bytes 835588
  16.6 10.5 %collective-permute-start.8 = (bf16[64,2176]{1,0:T(8,128)(2,1)S(1)}, bf16[64,2176]{1,0:T(8,128)(2,1)S(1)}, u32[]{:S(2)}, u32[]{:S(2)}) collective-permute-start(bf16[64,2176]{1,0:T(8,128)(2,1)S(1)} %collective-permute-done.3.refs_0_.refs_4_), channel_id=1, source_target_pairs={{0,4},{1,5},{2,6},{3,7},{4,12},{5,13},{6,14},{7,15},{12,8},{13,9},... | collective-permute-start | bytes 835592 | tf_op jit(solution)/shard_map/ppermute | solution.py:55
  23.0 27.1 %copy-start.2 = (bf16[64,2176]{1,0:T(8,128)(2,1)}, bf16[64,2176]{1,0:T(8,128)(2,1)S(1)}, u32[]{:S(2)}) copy-start(bf16[64,2176]{1,0:T(8,128)(2,1)S(1)} %collective-permute-done.12.refs_4_.refs_12_) | copy-start | bytes 835588
  23.0 7.6 %collective-permute-start.13 = (bf16[64,2176]{1,0:T(8,128)(2,1)S(1)}, bf16[64,2176]{1,0:T(8,128)(2,1)S(1)}, u32[]{:S(2)}, u32[]{:S(2)}) collective-permute-start(bf16[64,2176]{1,0:T(8,128)(2,1)S(1)} %collective-permute-done.12.refs_4_.refs_12_), channel_id=1, source_target_pairs={{0,2},{1,3},{2,0},{3,1},{4,6},{5,7},{6,4},{7,5},{12,14},{13,15},{1... | collective-permute-start | bytes 835592 | tf_op jit(solution)/shard_map/ppermute | solution.py:63
  23.4 10.4 %collective-permute-start.5 = (bf16[64,2176]{1,0:T(8,128)(2,1)S(1)}, bf16[64,2176]{1,0:T(8,128)(2,1)S(1)}, u32[]{:S(2)}, u32[]{:S(2)}) collective-permute-start(bf16[64,2176]{1,0:T(8,128)(2,1)S(1)} %collective-permute-done.3.refs_0_.refs_4_), channel_id=1, source_target_pairs={{0,1},{1,0},{2,3},{3,2},{4,5},{5,4},{6,7},{7,6},{12,13},{13,12},{1... | collective-permute-start | bytes 835592 | tf_op jit(solution)/shard_map/ppermute | solution.py:67
  23.4 10.5 %copy-start.3 = (bf16[64,2176]{1,0:T(8,128)(2,1)}, bf16[64,2176]{1,0:T(8,128)(2,1)S(1)}, u32[]{:S(2)}) copy-start(bf16[64,2176]{1,0:T(8,128)(2,1)S(1)} %collective-permute-done.1.refs_6_.refs_2_) | copy-start | bytes 835588
  23.4 10.4 %collective-permute-start.2 = (bf16[64,2176]{1,0:T(8,128)(2,1)S(1)}, bf16[64,2176]{1,0:T(8,128)(2,1)S(1)}, u32[]{:S(2)}, u32[]{:S(2)}) collective-permute-start(bf16[64,2176]{1,0:T(8,128)(2,1)S(1)} %collective-permute-done.refs_5_.refs_1_), channel_id=1, source_target_pairs={{0,1},{1,0},{2,3},{3,2},{4,5},{5,4},{6,7},{7,6},{12,13},{13,12},{1... | collective-permute-start | bytes 835592 | tf_op jit(solution)/shard_map/ppermute | solution.py:67
  23.9 10.0 %copy-start.4 = (bf16[64,2176]{1,0:T(8,128)(2,1)}, bf16[64,2176]{1,0:T(8,128)(2,1)S(1)}, u32[]{:S(2)}) copy-start(bf16[64,2176]{1,0:T(8,128)(2,1)S(1)} %collective-permute-done.4.refs_1_.refs_5_) | copy-start | bytes 835588
  23.9 9.9 %collective-permute-start.6 = (bf16[64,2176]{1,0:T(8,128)(2,1)S(1)}, bf16[64,2176]{1,0:T(8,128)(2,1)S(1)}, u32[]{:S(2)}, u32[]{:S(2)}) collective-permute-start(bf16[64,2176]{1,0:T(8,128)(2,1)S(1)} %collective-permute-done.4.refs_1_.refs_5_), channel_id=1, source_target_pairs={{0,1},{1,0},{2,3},{3,2},{4,5},{5,4},{6,7},{7,6},{12,13},{13,12},{1... | collective-permute-start | bytes 835592 | tf_op jit(solution)/shard_map/ppermute | solution.py:67
  27.0 23.1 %copy-start.5 = (bf16[64,2176]{1,0:T(8,128)(2,1)}, bf16[64,2176]{1,0:T(8,128)(2,1)S(1)}, u32[]{:S(2)}) copy-start(bf16[64,2176]{1,0:T(8,128)(2,1)S(1)} %collective-permute-done.8.refs_0_.refs_8_) | copy-start | bytes 835588
  27.0 16.0 %collective-permute-start.9 = (bf16[64,2176]{1,0:T(8,128)(2,1)S(1)}, bf16[64,2176]{1,0:T(8,128)(2,1)S(1)}, u32[]{:S(2)}, u32[]{:S(2)}) collective-permute-start(bf16[64,2176]{1,0:T(8,128)(2,1)S(1)} %collective-permute-done.8.refs_0_.refs_8_), channel_id=1, source_target_pairs={{0,2},{1,3},{2,0},{3,1},{4,6},{5,7},{6,4},{7,5},{12,14},{13,15},{1... | collective-permute-start | bytes 835592 | tf_op jit(solution)/shard_map/ppermute | solution.py:63
  30.6 19.5 %copy-start.6 = (bf16[64,2176]{1,0:T(8,128)(2,1)}, bf16[64,2176]{1,0:T(8,128)(2,1)S(1)}, u32[]{:S(2)}) copy-start(bf16[64,2176]{1,0:T(8,128)(2,1)S(1)} %collective-permute-done.13.refs_5_.refs_13_) | copy-start | bytes 835588
  30.6 12.4 %collective-permute-start.16 = (bf16[384,256]{1,0:T(8,128)(2,1)S(1)}, bf16[384,256]{1,0:T(8,128)(2,1)S(1)}, u32[]{:S(2)}, u32[]{:S(2)}) collective-permute-start(bf16[384,256]{1,0:T(8,128)(2,1)S(1)} %constant_dynamic-update-slice_fusion.refs_16_), channel_id=1, source_target_pairs={{0,4},{1,5},{2,6},{3,7},{4,12},{5,13},{6,14},{7,15},{12,8},{13,9},... | collective-permute-start | bytes 589832 | tf_op jit(solution)/shard_map/ppermute | solution.py:55
  33.8 0.7 copy-start.7
  33.8 0.8 copy-start.8
  33.8 0.9 copy-start.9
  43.1 0.7 copy-start.21
  43.7 8.6 %copy-start.10 = (bf16[64,2176]{1,0:T(8,128)(2,1)}, bf16[64,2176]{1,0:T(8,128)(2,1)S(1)}, u32[]{:S(2)}) copy-start(bf16[64,2176]{1,0:T(8,128)(2,1)S(1)} %collective-permute-done.9.refs_1_.refs_9_) | copy-start | bytes 835588
  43.7 4.3 %collective-permute-start.17 = (bf16[256,2048]{1,0:T(8,128)(2,1)}, bf16[256,2048]{1,0:T(8,128)(2,1)S(1)}, u32[]{:S(2)}, u32[]{:S(2)}) collective-permute-start(bf16[256,2048]{1,0:T(8,128)(2,1)} %get-tuple-element.37), channel_id=1, source_target_pairs={{0,1},{1,0},{2,3},{3,2},{4,5},{5,4},{6,7},{7,6},{12,13},{13,12},{1... | collective-permute-start | bytes 3145736 | tf_op jit(solution)/shard_map/ppermute | solution.py:67
  43.8 6.5 %collective-permute-start.14 = (bf16[64,2176]{1,0:T(8,128)(2,1)S(1)}, bf16[64,2176]{1,0:T(8,128)(2,1)S(1)}, u32[]{:S(2)}, u32[]{:S(2)}) collective-permute-start(bf16[64,2176]{1,0:T(8,128)(2,1)S(1)} %collective-permute-done.12.refs_4_.refs_12_), channel_id=1, source_target_pairs={{0,1},{1,0},{2,3},{3,2},{4,5},{5,4},{6,7},{7,6},{12,13},{13,12},{1... | collective-permute-start | bytes 835592 | tf_op jit(solution)/shard_map/ppermute | solution.py:67
  44.3 6.0 %collective-permute-start.15 = (bf16[64,2176]{1,0:T(8,128)(2,1)S(1)}, bf16[64,2176]{1,0:T(8,128)(2,1)S(1)}, u32[]{:S(2)}, u32[]{:S(2)}) collective-permute-start(bf16[64,2176]{1,0:T(8,128)(2,1)S(1)} %collective-permute-done.13.refs_5_.refs_13_), channel_id=1, source_target_pairs={{0,1},{1,0},{2,3},{3,2},{4,5},{5,4},{6,7},{7,6},{12,13},{13,12},{1... | collective-permute-start | bytes 835592 | tf_op jit(solution)/shard_map/ppermute | solution.py:67
  44.3 8.1 %collective-permute-start.10 = (bf16[64,2176]{1,0:T(8,128)(2,1)S(1)}, bf16[64,2176]{1,0:T(8,128)(2,1)S(1)}, u32[]{:S(2)}, u32[]{:S(2)}) collective-permute-start(bf16[64,2176]{1,0:T(8,128)(2,1)S(1)} %collective-permute-done.8.refs_0_.refs_8_), channel_id=1, source_target_pairs={{0,1},{1,0},{2,3},{3,2},{4,5},{5,4},{6,7},{7,6},{12,13},{13,12},{1... | collective-permute-start | bytes 835592 | tf_op jit(solution)/shard_map/ppermute | solution.py:67
  44.8 7.5 %collective-permute-start.11 = (bf16[64,2176]{1,0:T(8,128)(2,1)S(1)}, bf16[64,2176]{1,0:T(8,128)(2,1)S(1)}, u32[]{:S(2)}, u32[]{:S(2)}) collective-permute-start(bf16[64,2176]{1,0:T(8,128)(2,1)S(1)} %collective-permute-done.9.refs_1_.refs_9_), channel_id=1, source_target_pairs={{0,1},{1,0},{2,3},{3,2},{4,5},{5,4},{6,7},{7,6},{12,13},{13,12},{1... | collective-permute-start | bytes 835592 | tf_op jit(solution)/shard_map/ppermute | solution.py:67
  48.1 15.2 %copy-start.19 = (bf16[128,2048]{1,0:T(8,128)(2,1)S(1)}, bf16[128,2048]{1,0:T(8,128)(2,1)}, u32[]{:S(2)}) copy-start(bf16[128,2048]{1,0:T(8,128)(2,1)} %get-tuple-element.38) | copy-start | bytes 1572868
  50.1 12.5 %collective-permute-start.18 = (bf16[64,2048]{1,0:T(8,128)(2,1)}, bf16[64,2048]{1,0:T(8,128)(2,1)}, u32[]{:S(2)}, u32[]{:S(2)}) collective-permute-start(bf16[64,2048]{1,0:T(8,128)(2,1)} %get-tuple-element.60), channel_id=1, source_target_pairs={{0,2},{1,3},{2,0},{3,1},{4,6},{5,7},{6,4},{7,5},{12,14},{13,15},{1... | collective-permute-start | bytes 786440 | tf_op jit(solution)/shard_map/ppermute | solution.py:63
  50.2 2.1 %copy-start.11 = (bf16[64,2176]{1,0:T(8,128)(2,1)}, bf16[64,2176]{1,0:T(8,128)(2,1)S(1)}, u32[]{:S(2)}) copy-start(bf16[64,2176]{1,0:T(8,128)(2,1)S(1)} %collective-permute-done.14.refs_6_.refs_14_) | copy-start | bytes 835588
  50.2 11.9 %collective-permute-start.20 = (bf16[384,256]{1,0:T(8,128)(2,1)S(1)}, bf16[384,256]{1,0:T(8,128)(2,1)S(1)}, u32[]{:S(2)}, u32[]{:S(2)}) collective-permute-start(bf16[384,256]{1,0:T(8,128)(2,1)S(1)} %constant_dynamic-update-slice_fusion.refs_16_), channel_id=1, source_target_pairs={{0,8},{1,9},{2,10},{3,11},{4,0},{5,1},{6,2},{7,3},{12,4},{13,5},{1... | collective-permute-start | bytes 589832 | tf_op jit(solution)/shard_map/ppermute | solution.py:59
  50.3 2.0 %copy-start.12 = (bf16[64,2176]{1,0:T(8,128)(2,1)}, bf16[64,2176]{1,0:T(8,128)(2,1)S(1)}, u32[]{:S(2)}) copy-start(bf16[64,2176]{1,0:T(8,128)(2,1)S(1)} %collective-permute-done.15.refs_7_.refs_15_) | copy-start | bytes 835588
  50.3 12.3 %collective-permute-start.19 = (bf16[384,256]{1,0:T(8,128)(2,1)}, bf16[384,256]{1,0:T(8,128)(2,1)S(1)}, u32[]{:S(2)}, u32[]{:S(2)}) collective-permute-start(bf16[384,256]{1,0:T(8,128)(2,1)} %copy-done.21), channel_id=1, source_target_pairs={{0,4},{1,5},{2,6},{3,7},{4,12},{5,13},{6,14},{7,15},{12,8},{13,9},... | collective-permute-start | bytes 589832 | tf_op jit(solution)/shard_map/ppermute | solution.py:55
  52.3 0.7 copy-start.13
  53.0 0.7 copy-start.14
  62.1 16.3 %copy-start.17 = (bf16[128,2048]{1,0:T(8,128)(2,1)S(1)}, bf16[128,2048]{1,0:T(8,128)(2,1)}, u32[]{:S(2)}) copy-start(bf16[128,2048]{1,0:T(8,128)(2,1)} %get-tuple-element.40) | copy-start | bytes 1572868
  62.1 0.7 copy-start.22
  62.6 0.7 copy-start.23
  63.3 4.3 %collective-permute-start.21 = (bf16[256,2048]{1,0:T(8,128)(2,1)}, bf16[256,2048]{1,0:T(8,128)(2,1)S(1)}, u32[]{:S(2)}, u32[]{:S(2)}) collective-permute-start(bf16[256,2048]{1,0:T(8,128)(2,1)} %get-tuple-element.42), channel_id=1, source_target_pairs={{0,1},{1,0},{2,3},{3,2},{4,5},{5,4},{6,7},{7,6},{12,13},{13,12},{1... | collective-permute-start | bytes 3145736 | tf_op jit(solution)/shard_map/ppermute | solution.py:67
  65.1 12.5 %collective-permute-start.28 = (bf16[64,2048]{1,0:T(8,128)(2,1)}, bf16[64,2048]{1,0:T(8,128)(2,1)}, u32[]{:S(2)}, u32[]{:S(2)}) collective-permute-start(bf16[64,2048]{1,0:T(8,128)(2,1)} %add_convert_fusion.3), channel_id=1, source_target_pairs={{0,4},{1,5},{2,6},{3,7},{4,12},{5,13},{6,14},{7,15},{12,8},{13,9},... | collective-permute-start | bytes 786440 | tf_op jit(solution)/shard_map/ppermute | solution.py:55
  67.4 3.1 %collective-permute-start.22 = (bf16[384,256]{1,0:T(8,128)(2,1)S(1)}, bf16[384,256]{1,0:T(8,128)(2,1)S(1)}, u32[]{:S(2)}, u32[]{:S(2)}) collective-permute-start(bf16[384,256]{1,0:T(8,128)(2,1)S(1)} %constant_dynamic-update-slice_fusion.refs_16_), channel_id=1, source_target_pairs={{0,1},{1,0},{2,3},{3,2},{4,5},{5,4},{6,7},{7,6},{12,13},{13,12},{1... | collective-permute-start | bytes 589832 | tf_op jit(solution)/shard_map/ppermute | solution.py:67
  69.6 19.6 %copy-start.16 = (bf16[128,2048]{1,0:T(8,128)(2,1)S(1)}, bf16[128,2048]{1,0:T(8,128)(2,1)}, u32[]{:S(2)}) copy-start(bf16[128,2048]{1,0:T(8,128)(2,1)} %get-tuple-element.43) | copy-start | bytes 1572868
  69.6 8.8 %collective-permute-start.27 = (bf16[64,2048]{1,0:T(8,128)(2,1)}, bf16[64,2048]{1,0:T(8,128)(2,1)}, u32[]{:S(2)}, u32[]{:S(2)}) collective-permute-start(bf16[64,2048]{1,0:T(8,128)(2,1)} %get-tuple-element.59), channel_id=1, source_target_pairs={{0,2},{1,3},{2,0},{3,1},{4,6},{5,7},{6,4},{7,5},{12,14},{13,15},{1... | collective-permute-start | bytes 786440 | tf_op jit(solution)/shard_map/ppermute | solution.py:63
  69.9 1.7 %collective-permute-start.23 = (bf16[384,256]{1,0:T(8,128)(2,1)}, bf16[384,256]{1,0:T(8,128)(2,1)S(1)}, u32[]{:S(2)}, u32[]{:S(2)}) collective-permute-start(bf16[384,256]{1,0:T(8,128)(2,1)} %copy-done.21), channel_id=1, source_target_pairs={{0,1},{1,0},{2,3},{3,2},{4,5},{5,4},{6,7},{7,6},{12,13},{13,12},{1... | collective-permute-start | bytes 589832 | tf_op jit(solution)/shard_map/ppermute | solution.py:67
  69.9 1.9 %collective-permute-start.24 = (bf16[384,256]{1,0:T(8,128)(2,1)}, bf16[384,256]{1,0:T(8,128)(2,1)S(1)}, u32[]{:S(2)}, u32[]{:S(2)}) collective-permute-start(bf16[384,256]{1,0:T(8,128)(2,1)} %copy-done.23), channel_id=1, source_target_pairs={{0,1},{1,0},{2,3},{3,2},{4,5},{5,4},{6,7},{7,6},{12,13},{13,12},{1... | collective-permute-start | bytes 589832 | tf_op jit(solution)/shard_map/ppermute | solution.py:67
  70.5 1.8 %copy-start.24 = (bf16[384,256]{1,0:T(8,128)(2,1)}, bf16[384,256]{1,0:T(8,128)(2,1)S(1)}, u32[]{:S(2)}) copy-start(bf16[384,256]{1,0:T(8,128)(2,1)S(1)} %collective-permute-done.22.refs_17_) | copy-start | bytes 589828
  70.5 1.8 %collective-permute-start.25 = (bf16[384,256]{1,0:T(8,128)(2,1)}, bf16[384,256]{1,0:T(8,128)(2,1)}, u32[]{:S(2)}, u32[]{:S(2)}) collective-permute-start(bf16[384,256]{1,0:T(8,128)(2,1)} %copy-done.22), channel_id=1, source_target_pairs={{0,1},{1,0},{2,3},{3,2},{4,5},{5,4},{6,7},{7,6},{12,13},{13,12},{1... | collective-permute-start | bytes 589832 | tf_op jit(solution)/shard_map/ppermute | solution.py:67
  71.6 0.7 copy-start.25
  71.9 0.7 copy-start.26
  77.6 20.6 %copy-start.15 = (bf16[64,1,2048]{2,0,1:T(8,128)(2,1)S(1)}, bf16[64,1,2048]{2,0,1:T(8,128)(2,1)}, u32[]{:S(2)}) copy-start(bf16[64,1,2048]{2,0,1:T(8,128)(2,1)} %param.9) | copy-start | bytes 786436
  77.6 20.6 %copy-start.18 = (bf16[128,2048]{1,0:T(8,128)(2,1)S(1)}, bf16[128,2048]{1,0:T(8,128)(2,1)}, u32[]{:S(2)}) copy-start(bf16[128,2048]{1,0:T(8,128)(2,1)} %get-tuple-element.35) | copy-start | bytes 1572868
  80.2 8.9 %collective-permute-start.29 = (bf16[64,2048]{1,0:T(8,128)(2,1)}, bf16[64,2048]{1,0:T(8,128)(2,1)S(1)}, u32[]{:S(2)}, u32[]{:S(2)}) collective-permute-start(bf16[64,2048]{1,0:T(8,128)(2,1)} %add_convert_fusion.2), channel_id=1, source_target_pairs={{0,4},{1,5},{2,6},{3,7},{4,12},{5,13},{6,14},{7,15},{12,8},{13,9},... | collective-permute-start | bytes 786440 | tf_op jit(solution)/shard_map/ppermute | solution.py:55
  81.0 8.1 %collective-permute-start.26 = (bf16[64,2048]{1,0:T(8,128)(2,1)}, bf16[64,2048]{1,0:T(8,128)(2,1)}, u32[]{:S(2)}, u32[]{:S(2)}) collective-permute-start(bf16[64,2048]{1,0:T(8,128)(2,1)} %get-tuple-element.58), channel_id=1, source_target_pairs={{0,2},{1,3},{2,0},{3,1},{4,6},{5,7},{6,4},{7,5},{12,14},{13,15},{1... | collective-permute-start | bytes 786440 | tf_op jit(solution)/shard_map/ppermute | solution.py:63
  90.2 7.8 %collective-permute-start.31 = (bf16[64,2048]{1,0:T(8,128)(2,1)S(1)}, bf16[64,2048]{1,0:T(8,128)(2,1)S(1)}, u32[]{:S(2)}, u32[]{:S(2)}) collective-permute-start(bf16[64,2048]{1,0:T(8,128)(2,1)S(1)} %add_convert_fusion.1), channel_id=1, source_target_pairs={{0,4},{1,5},{2,6},{3,7},{4,12},{5,13},{6,14},{7,15},{12,8},{13,9},... | collective-permute-start | bytes 786440 | tf_op jit(solution)/shard_map/ppermute | solution.py:55
  91.0 7.2 %collective-permute-start.30 = (bf16[64,2048]{1,0:T(8,128)(2,1)}, bf16[64,2048]{1,0:T(8,128)(2,1)S(1)}, u32[]{:S(2)}, u32[]{:S(2)}) collective-permute-start(bf16[64,2048]{1,0:T(8,128)(2,1)} %get-tuple-element.56), channel_id=1, source_target_pairs={{0,2},{1,3},{2,0},{3,1},{4,6},{5,7},{6,4},{7,5},{12,14},{13,15},{1... | collective-permute-start | bytes 786440 | tf_op jit(solution)/shard_map/ppermute | solution.py:63

commit v5 on v4

--- a/solution.py
+++ b/solution.py
@@ -14,7 +14,7 @@
 GROUPS = 4
 META = 128
 LINE = 4
-VMEM_LIMIT = 60 * 2**20
+VMEM_LIMIT = 24 * 2**20
 F32 = jnp.float32
 BF16 = jnp.bfloat16
 ANY = pl.BlockSpec(memory_space=pl.ANY)
@@ -117,29 +117,46 @@
     )(activations, norm_gain.reshape(1, width), ids, gates, keys, value_weight)
 
 
+def hold_kernel(small_ref, up_ref, down_ref, out_ref):
+    out_ref[...] = small_ref[...]
+
+
+def hold(small, weights):
+    return pl.pallas_call(
+        hold_kernel,
+        out_shape=jax.ShapeDtypeStruct(small.shape, small.dtype),
+        in_specs=[IN_VMEM] * 3,
+        out_specs=IN_VMEM,
+        compiler_params=pltpu.CompilerParams(vmem_limit_bytes=4 * 2**20),
+        cost_estimate=SHORT,
+        name="hold_weights",
+    )(small, *weights)
+
+
+def in_vmem(*arrays):
+    return [pltpu.with_memory_space_constraint(x, pltpu.VMEM) for x in arrays]
+
+
 def expert_kernel(top, tok_rows, capacity, sources, targets, *refs):
     inputs = 1 + max(s[0] for group in sources for s in group)
     outputs = 1 + max(t[0] for group in targets for t in group)
     x_hbm = refs[:inputs]
-    up_hbm, down_hbm = refs[inputs : inputs + 2]
+    up_ref, down_ref = refs[inputs : inputs + 2]
     out_hbm = refs[inputs + 2 : inputs + 2 + outputs]
     (
         x_buf,
-        up_buf,
-        down_buf,
         slot_rows,
         slot_gates,
         places,
         hidden,
         result,
         x_sem,
-        w_sem,
         out_sem,
     ) = refs[inputs + 2 + outputs :]
     groups, rows, packed = x_buf.shape
     width = packed - META
     slots = slot_rows.shape[0] // groups
-    units = down_buf.shape[0]
+    units = down_ref.shape[0]
     tile = 256
     me = lax.axis_index("seq").astype(F32)
 
@@ -169,20 +186,9 @@
             at += count
         return copies
 
-    def load_up(index):
-        part = pl.ds(index * tile, tile)
-        return pltpu.make_async_copy(up_hbm.at[:, part], up_buf.at[:, part], w_sem.at[index])
-
-    up_parts = 2 * units // tile
-    load_down = pltpu.make_async_copy(down_hbm, down_buf, w_sem.at[up_parts])
-    half = up_parts // 2
     for group in range(groups):
         for copy in loads(group):
             copy.start()
-    for index in range(half):
-        load_up(index).start()
-        load_up(half + index).start()
-    load_down.start()
 
     chunk = tok_rows * META // math.gcd(tok_rows, META)
     first = lax.broadcasted_iota(jnp.int32, (chunk, chunk), 0)
@@ -219,18 +225,13 @@
         spots = lax.broadcasted_iota(jnp.int32, (rows, META), 1).astype(F32)
         places[group] = (spots == by_row).astype(F32).astype(BF16)
 
-    for index in range(half):
-        load_up(index).wait()
-        load_up(half + index).wait()
-        gate = dot(slot_rows[...], up_buf[:, index * tile : (index + 1) * tile])
-        up = dot(slot_rows[...], up_buf[:, units + index * tile : units + (index + 1) * tile])
-        hidden[:, index * tile : (index + 1) * tile] = (gate / (1.0 + jnp.exp(-gate)) * up).astype(
-            BF16
-        )
-    load_down.wait()
-    for at in range(0, width, 256):
-        out = dot(hidden[...], down_buf[:, at : at + 256]).astype(BF16).astype(F32)
-        result[:, at : at + 256] = (out * slot_gates[:, 0:1]).astype(BF16)
+    for at in range(0, units, tile):
+        gate = dot(slot_rows[...], up_ref[:, at : at + tile])
+        up = dot(slot_rows[...], up_ref[:, units + at : units + at + tile])
+        hidden[:, at : at + tile] = (gate / (1.0 + jnp.exp(-gate)) * up).astype(BF16)
+    for at in range(0, width, tile):
+        out = dot(hidden[...], down_ref[:, at : at + tile]).astype(BF16).astype(F32)
+        result[:, at : at + tile] = (out * slot_gates[:, 0:1]).astype(BF16)
     for group in range(groups):
         for at in range(0, width, 512):
             x_buf[group, :, at : at + 512] = dot(
@@ -253,28 +254,27 @@
     slots = rows // tok_rows * capacity
     assert slots % 16 == 0 and slots <= META and units % 256 == 0 and width % 512 == 0
     all_slots = groups * slots
+    weights = in_vmem(w_gate_up, w_down)
+    held = 2 * total * (packed + META) + all_slots * (4 * width + 2 * units + 4 * META)
     return pl.pallas_call(
         functools.partial(expert_kernel, top, tok_rows, capacity, sources, targets),
         out_shape=[jax.ShapeDtypeStruct((count, width), BF16) for count in out_rows],
-        in_specs=[ANY] * (len(arrays) + 2),
+        in_specs=[ANY] * len(arrays) + [IN_VMEM] * 2,
         out_specs=[ANY] * len(out_rows),
         scratch_shapes=[
             pltpu.VMEM((groups, rows, packed), BF16),
-            pltpu.VMEM((width, 2 * units), BF16),
-            pltpu.VMEM((units, width), BF16),
             pltpu.VMEM((all_slots, width), BF16),
             pltpu.VMEM((all_slots, META), F32),
             pltpu.VMEM((groups, rows, META), BF16),
             pltpu.VMEM((all_slots, units), BF16),
             pltpu.VMEM((all_slots, width), BF16),
             pltpu.SemaphoreType.DMA((groups, max(len(s) for s in sources))),
-            pltpu.SemaphoreType.DMA((2 * units // 256 + 1,)),
             pltpu.SemaphoreType.DMA((groups, max(len(t) for t in targets))),
         ],
-        compiler_params=pltpu.CompilerParams(vmem_limit_bytes=VMEM_LIMIT),
+        compiler_params=pltpu.CompilerParams(vmem_limit_bytes=held + 8 * 2**20),
         cost_estimate=SHORT,
         name="experts",
-    )(*arrays, w_gate_up, w_down)
+    )(*arrays, *weights)
 
 
 def value_kernel(key_rows, blocks, small_blocks, *refs):
@@ -438,11 +438,18 @@
     rows, width = acts.shape
     line = [packed, forward(packed), None, backward(packed)]
     crossed = [across(packed), across(line[1]), None, across(line[3])]
+    to_core = other_core(packed)
+    small = hold(after(small, to_core), in_vmem(w_gate_up, w_down))
     pair = jnp.concatenate([small, across(small)], axis=0)
     line[2] = forward(after(line[1], pair, crossed[0]))
     crossed[2] = across(line[2])
     arrays = [
-        [line[step], crossed[step], other_core(line[step]), other_core(crossed[step])]
+        [
+            line[step],
+            crossed[step],
+            other_core(line[step]) if step else to_core,
+            other_core(crossed[step]),
+        ]
         for step in range(LINE)
     ]
     blocks = [

time: 99.5 us -> 84.9 us (0.85)
  Pallas kernels: 35.1 us -> 22 us
  waiting for transfers between devices: 19.2 us -> 27.5 us
  other arithmetic: 9.54 us -> 1.5 us
  starting transfers between devices: 29.5 us -> 27.3 us
    pallas_call x2, Pallas kernels: 16.7 us -> 8.25 us  [run_experts(): pl.pallas_call(functools.partial(expert_kernel, top, tok_rows, capacity,...]
    convert_element_type x5, other arithmetic: 8.67 us -> 0.62 us  [summed(): return sum((term.astype(F32) for term in terms)).astype(BF16)]
    ppermute x7, waiting for transfers between devices: 9.08 us -> 16.9 us  [forward(): return lax.ppermute(x, 'seq', ring_steps(1))]
    ppermute x7, starting transfers between devices: 18.5 us -> 11.6 us  [forward(): return lax.ppermute(x, 'seq', ring_steps(1))]
    pallas_call x4, Pallas kernels: 11.5 us -> 7.33 us  [attend_part(): pl.pallas_call(functools.partial(attention_kernel, chunk), grid=(1,), out...]
    ppermute x2, waiting for transfers between devices: 0.01 us -> 3.29 us  [backward(): return lax.ppermute(x, 'seq', ring_steps(LINE - 1))]
    ppermute x9, starting transfers between devices: 7.21 us -> 10.3 us  [across(): return lax.ppermute(x, 'seq', swaps(1, 0))]
    ppermute x9, waiting for transfers between devices: 5.02 us -> 2.2 us  [across(): return lax.ppermute(x, 'seq', swaps(1, 0))]
  transfers between devices with their start and end apart: 32 -> 32, of which waited for: 13 -> 14; matrix products, arithmetic and copies ran while one was open for 7% -> 0% of each run, Pallas kernels for 34% -> 24%
where the time goes in v5:
time: 84.9 us; the launch traced here: 84.6 us
  waiting for transfers between devices  27.5 us (32%)
  starting transfers between devices  27.3 us (32%)
  Pallas kernels  22 us (26%)
  local copies, waits for them, and re-layouts  5.59 us (7%)
  other arithmetic  1.5 us (2%)
    ppermute x7, waiting for transfers between devices, forward(): return lax.ppermute(x, 'seq', ring_steps(1))  16.9 us
    ppermute x7, starting transfers between devices, forward(): return lax.ppermute(x, 'seq', ring_steps(1))  11.6 us
    ppermute x9, starting transfers between devices, across(): return lax.ppermute(x, 'seq', swaps(1, 0))  10.3 us
    pallas_call x2, Pallas kernels, run_experts(): pl.pallas_call(functools.partial(expert_kernel, top, tok_rows, capacity,...  8.25 us
    pallas_call x4, Pallas kernels, attend_part(): pl.pallas_call(functools.partial(attention_kernel, chunk), grid=(1,), out...  7.33 us
    unnamed x16, local copies, waits for them, and re-layouts  5.59 us
    ppermute x14, waiting for transfers between devices, other_core(): return lax.ppermute(x, 'seq', swaps(0, 1))  5.06 us
    pallas_call x1, Pallas kernels, make_values(): pl.pallas_call(functools.partial(value_kernel, key_rows, blocks, small_bl...  4.58 us
  transfers between devices with their start and end apart: 32, of which 14 were waited for; matrix products, arithmetic and copies ran while one was open for 0% of the time, Pallas kernels for 24%

profile of v5, /device:TPU:0, one launch (start us, length us, event | category | flops | bytes accessed | tf_op | source)
XLA Modules:
  0.0 84.6 jit_solution(8609434690189947935)
XLA Ops:
  0.6 1.9 %normalize_and_pack.1 = (bf16[64,2176]{1,0:T(8,128)(2,1)}, bf16[192,256]{1,0:T(8,128)(2,1)}) custom-call(bf16[64,2048]{1,0:T(8,128)(2,1)} %bitcast.27, f32[1,2048]{1,0:T(1,128)} %bitcast.29, s32[4,64]{1,0:T(4,128)} %bitcast.30, f32[4,64]{1,0:T(4,128)} %bitcast.31, bf16[64,256]{1,0:T(8,128)(2,1)} %bitcast.28, bf16[128,256]{1,0:T(8,128)(2,1)} %weight_ref.1), custom_call_target="tpu_custom_call" | custom-call | flops 1 | bytes 1 | tf_op jit(solution)/shard_map/normalize_and_pack/pallas_call | solution.py:108
  2.5 0.5 collective-permute-start.1
  2.9 2.6 %collective-permute-start.3 = (bf16[64,2176]{1,0:T(8,128)(2,1)}, bf16[64,2176]{1,0:T(8,128)(2,1)S(1)}, u32[]{:S(2)}, u32[]{:S(2)}) collective-permute-start(bf16[64,2176]{1,0:T(8,128)(2,1)} %get-tuple-element.31.refs_4_.refs_0_), channel_id=1, source_target_pairs={{0,4},{1,5},{2,6},{3,7},{4,12},{5,13},{6,14},{7,15},{12,8},{13,9},... | collective-permute-start | bytes 835592 | tf_op jit(solution)/shard_map/ppermute | solution.py:55
  5.5 1.5 %collective-permute-start = (bf16[64,2176]{1,0:T(8,128)(2,1)}, bf16[64,2176]{1,0:T(8,128)(2,1)S(1)}, u32[]{:S(2)}, u32[]{:S(2)}) collective-permute-start(bf16[64,2176]{1,0:T(8,128)(2,1)} %get-tuple-element.31.refs_4_.refs_0_), channel_id=1, source_target_pairs={{0,2},{1,3},{2,0},{3,1},{4,6},{5,7},{6,4},{7,5},{12,14},{13,15},{1... | collective-permute-start | bytes 835592 | tf_op jit(solution)/shard_map/ppermute | solution.py:63
  7.0 2.8 %copy-done = bf16[1,2048,1536]{2,1,0:T(8,128)(2,1)S(1)} copy-done((bf16[1,2048,1536]{2,1,0:T(8,128)(2,1)S(1)}, bf16[1,2048,1536]{2,1,0:T(8,128)(2,1)}, u32[]{:S(2)}) %copy-start) | copy-done | bytes 6291480
  9.8 1.9 %copy-done.2 = bf16[1,768,2048]{2,1,0:T(8,128)(2,1)S(1)} copy-done((bf16[1,768,2048]{2,1,0:T(8,128)(2,1)S(1)}, bf16[1,768,2048]{2,1,0:T(8,128)(2,1)}, u32[]{:S(2)}) %copy-start.2) | copy-done | bytes 3145752
  11.7 0.9 %copy-done.6 = bf16[192,256]{1,0:T(8,128)(2,1)S(1)} copy-done((bf16[192,256]{1,0:T(8,128)(2,1)S(1)}, bf16[192,256]{1,0:T(8,128)(2,1)}, u32[]{:S(2)}) %copy-start.6) | copy-done | bytes 98328
  12.6 0.6 collective-permute-start.7
  13.2 2.3 %collective-permute-start.12 = (bf16[64,2176]{1,0:T(8,128)(2,1)}, bf16[64,2176]{1,0:T(8,128)(2,1)S(1)}, u32[]{:S(2)}, u32[]{:S(2)}) collective-permute-start(bf16[64,2176]{1,0:T(8,128)(2,1)} %get-tuple-element.31.refs_4_.refs_0_), channel_id=1, source_target_pairs={{0,8},{1,9},{2,10},{3,11},{4,0},{5,1},{6,2},{7,3},{12,4},{13,5},{1... | collective-permute-start | bytes 835592 | tf_op jit(solution)/shard_map/ppermute | solution.py:59
  15.5 0.6 collective-permute-start.4
  16.1 1.3 %collective-permute-done.7 = bf16[192,256]{1,0:T(8,128)(2,1)S(1)} collective-permute-done((bf16[192,256]{1,0:T(8,128)(2,1)S(1)}, bf16[192,256]{1,0:T(8,128)(2,1)S(1)}, u32[]{:S(2)}, u32[]{:S(2)}) %collective-permute-start.7) | collective-permute-done | bytes 98336 | tf_op jit(solution)/shard_map/ppermute | solution.py:63
  17.4 0.0 collective-permute-done.refs_5_.refs_1_
  17.4 3.7 %collective-permute-start.8 = (bf16[64,2176]{1,0:T(8,128)(2,1)S(1)}, bf16[64,2176]{1,0:T(8,128)(2,1)S(1)}, u32[]{:S(2)}, u32[]{:S(2)}) collective-permute-start(bf16[64,2176]{1,0:T(8,128)(2,1)S(1)} %collective-permute-done.3.refs_0_.refs_4_), channel_id=1, source_target_pairs={{0,4},{1,5},{2,6},{3,7},{4,12},{5,13},{6,14},{7,15},{12,8},{13,9},... | collective-permute-start | bytes 835592 | tf_op jit(solution)/shard_map/ppermute | solution.py:55
  21.0 1.9 %collective-permute-done.12.refs_4_.refs_12_ = bf16[64,2176]{1,0:T(8,128)(2,1)S(1)} collective-permute-done((bf16[64,2176]{1,0:T(8,128)(2,1)}, bf16[64,2176]{1,0:T(8,128)(2,1)S(1)}, u32[]{:S(2)}, u32[]{:S(2)}) %collective-permute-start.12) | collective-permute-done | bytes 278560 | tf_op jit(solution)/shard_map/ppermute | solution.py:59
  22.9 1.2 %collective-permute-start.13 = (bf16[64,2176]{1,0:T(8,128)(2,1)S(1)}, bf16[64,2176]{1,0:T(8,128)(2,1)S(1)}, u32[]{:S(2)}, u32[]{:S(2)}) collective-permute-start(bf16[64,2176]{1,0:T(8,128)(2,1)S(1)} %collective-permute-done.12.refs_4_.refs_12_), channel_id=1, source_target_pairs={{0,2},{1,3},{2,0},{3,1},{4,6},{5,7},{6,4},{7,5},{12,14},{13,15},{1... | collective-permute-start | bytes 835592 | tf_op jit(solution)/shard_map/ppermute | solution.py:63
  24.1 0.0 collective-permute-start.5
  24.1 0.5 collective-permute-start.2
  24.6 0.0 collective-permute-done.4.refs_1_.refs_5_
  24.6 0.0 collective-permute-start.6
  24.6 5.9 %collective-permute-done.8.refs_0_.refs_8_ = bf16[64,2176]{1,0:T(8,128)(2,1)S(1)} collective-permute-done((bf16[64,2176]{1,0:T(8,128)(2,1)S(1)}, bf16[64,2176]{1,0:T(8,128)(2,1)S(1)}, u32[]{:S(2)}, u32[]{:S(2)}) %collective-permute-start.8) | collective-permute-done | bytes 278560 | tf_op jit(solution)/shard_map/ppermute | solution.py:55
  30.5 1.5 %collective-permute-start.9 = (bf16[64,2176]{1,0:T(8,128)(2,1)S(1)}, bf16[64,2176]{1,0:T(8,128)(2,1)S(1)}, u32[]{:S(2)}, u32[]{:S(2)}) collective-permute-start(bf16[64,2176]{1,0:T(8,128)(2,1)S(1)} %collective-permute-done.8.refs_0_.refs_8_), channel_id=1, source_target_pairs={{0,2},{1,3},{2,0},{3,1},{4,6},{5,7},{6,4},{7,5},{12,14},{13,15},{1... | collective-permute-start | bytes 835592 | tf_op jit(solution)/shard_map/ppermute | solution.py:63
  32.1 0.0 collective-permute-done.13.refs_5_.refs_13_
  32.1 2.5 %collective-permute-start.16 = (bf16[384,256]{1,0:T(8,128)(2,1)S(1)}, bf16[384,256]{1,0:T(8,128)(2,1)S(1)}, u32[]{:S(2)}, u32[]{:S(2)}) collective-permute-start(bf16[384,256]{1,0:T(8,128)(2,1)S(1)} %pad_maximum_fusion.refs_16_), channel_id=1, source_target_pairs={{0,4},{1,5},{2,6},{3,7},{4,12},{5,13},{6,14},{7,15},{12,8},{13,9},... | collective-permute-start | bytes 589832 | tf_op jit(solution)/shard_map/ppermute | solution.py:55
  34.6 4.1 %experts.2 = (bf16[128,2048]{1,0:T(8,128)(2,1)S(1)}, bf16[128,2048]{1,0:T(8,128)(2,1)S(1)}, bf16[256,2048]{1,0:T(8,128)(2,1)S(1)}) custom-call(bf16[64,2176]{1,0:T(8,128)(2,1)S(1)} %collective-permute-done.3.refs_0_.refs_4_, bf16[64,2176]{1,0:T(8,128)(2,1)S(1)} %collective-permute-done.4.refs_1_.refs_5_, ...), custom_call_target="tpu_custom_call" | custom-call | flops 1 | bytes 1 | tf_op jit(solution)/shard_map/experts/pallas_call | solution.py:259
  38.8 0.7 collective-permute-done.16.refs_18_
  39.5 0.5 collective-permute-start.14
  40.0 0.0 collective-permute-start.15
  40.0 0.5 collective-permute-start.10
  40.5 0.0 collective-permute-start.11
  40.5 1.6 %collective-permute-done.17 = bf16[256,2048]{1,0:T(8,128)(2,1)S(1)} collective-permute-done((bf16[256,2048]{1,0:T(8,128)(2,1)S(1)}, bf16[256,2048]{1,0:T(8,128)(2,1)S(1)}, u32[]{:S(2)}, u32[]{:S(2)}) %collective-permute-start.17) | collective-permute-done | bytes 1048608 | tf_op jit(solution)/shard_map/ppermute | solution.py:67
  42.2 0.1 add_convert_fusion.6
  42.3 1.9 %collective-permute-start.18 = (bf16[64,2048]{1,0:T(8,128)(2,1)S(1)}, bf16[64,2048]{1,0:T(8,128)(2,1)S(1)}, u32[]{:S(2)}, u32[]{:S(2)}) collective-permute-start(bf16[64,2048]{1,0:T(8,128)(2,1)S(1)} %get-tuple-element.62), channel_id=1, source_target_pairs={{0,2},{1,3},{2,0},{3,1},{4,6},{5,7},{6,4},{7,5},{12,14},{13,15},{1... | collective-permute-start | bytes 786440 | tf_op jit(solution)/shard_map/ppermute | solution.py:63
  44.2 2.0 %collective-permute-start.19 = (bf16[384,256]{1,0:T(8,128)(2,1)S(1)}, bf16[384,256]{1,0:T(8,128)(2,1)S(1)}, u32[]{:S(2)}, u32[]{:S(2)}) collective-permute-start(bf16[384,256]{1,0:T(8,128)(2,1)S(1)} %collective-permute-done.16.refs_18_), channel_id=1, source_target_pairs={{0,4},{1,5},{2,6},{3,7},{4,12},{5,13},{6,14},{7,15},{12,8},{13,9},... | collective-permute-start | bytes 589832 | tf_op jit(solution)/shard_map/ppermute | solution.py:55
  46.2 4.1 %experts.3 = (bf16[128,2048]{1,0:T(8,128)(2,1)S(1)}, bf16[128,2048]{1,0:T(8,128)(2,1)S(1)}, bf16[256,2048]{1,0:T(8,128)(2,1)S(1)}) custom-call(bf16[64,2176]{1,0:T(8,128)(2,1)S(1)} %collective-permute-done.8.refs_0_.refs_8_, bf16[64,2176]{1,0:T(8,128)(2,1)S(1)} %collective-permute-done.9.refs_1_.refs_9_, ...), custom_call_target="tpu_custom_call" | custom-call | flops 1 | bytes 1 | tf_op jit(solution)/shard_map/experts/pallas_call | solution.py:259
  50.4 0.0 copy-start.4
  50.4 1.4 %collective-permute-done.20.refs_22_ = bf16[384,256]{1,0:T(8,128)(2,1)S(1)} collective-permute-done((bf16[384,256]{1,0:T(8,128)(2,1)S(1)}, bf16[384,256]{1,0:T(8,128)(2,1)S(1)}, u32[]{:S(2)}, u32[]{:S(2)}) %collective-permute-start.20) | collective-permute-done | bytes 196640 | tf_op jit(solution)/shard_map/ppermute | solution.py:59
  51.8 4.2 %collective-permute-done.19.refs_20_ = bf16[384,256]{1,0:T(8,128)(2,1)S(1)} collective-permute-done((bf16[384,256]{1,0:T(8,128)(2,1)S(1)}, bf16[384,256]{1,0:T(8,128)(2,1)S(1)}, u32[]{:S(2)}, u32[]{:S(2)}) %collective-permute-start.19) | collective-permute-done | bytes 196640 | tf_op jit(solution)/shard_map/ppermute | solution.py:55
  56.0 0.1 add_convert_fusion.3
  56.1 0.1 collective-permute-start.28
  56.2 0.6 collective-permute-start.22
  56.8 1.9 %collective-permute-done.21 = bf16[256,2048]{1,0:T(8,128)(2,1)S(1)} collective-permute-done((bf16[256,2048]{1,0:T(8,128)(2,1)S(1)}, bf16[256,2048]{1,0:T(8,128)(2,1)S(1)}, u32[]{:S(2)}, u32[]{:S(2)}) %collective-permute-start.21) | collective-permute-done | bytes 1048608 | tf_op jit(solution)/shard_map/ppermute | solution.py:67
  58.7 0.1 add_convert_fusion.4
  58.8 0.9 %collective-permute-start.27 = (bf16[64,2048]{1,0:T(8,128)(2,1)S(1)}, bf16[64,2048]{1,0:T(8,128)(2,1)S(1)}, u32[]{:S(2)}, u32[]{:S(2)}) collective-permute-start(bf16[64,2048]{1,0:T(8,128)(2,1)S(1)} %get-tuple-element.61), channel_id=1, source_target_pairs={{0,2},{1,3},{2,0},{3,1},{4,6},{5,7},{6,4},{7,5},{12,14},{13,15},{1... | collective-permute-start | bytes 786440 | tf_op jit(solution)/shard_map/ppermute | solution.py:63
  59.7 0.5 collective-permute-start.24
  60.2 0.0 collective-permute-start.25
  60.2 0.9 %collective-permute-done.23.refs_19_ = bf16[384,256]{1,0:T(8,128)(2,1)S(1)} collective-permute-done((bf16[384,256]{1,0:T(8,128)(2,1)S(1)}, bf16[384,256]{1,0:T(8,128)(2,1)S(1)}, u32[]{:S(2)}, u32[]{:S(2)}) %collective-permute-start.23) | collective-permute-done | bytes 196640 | tf_op jit(solution)/shard_map/ppermute | solution.py:67
  61.1 0.3 collective-permute-done.24.refs_21_
  61.4 0.3 collective-permute-done.25.refs_23_
  61.7 4.6 %values.1 = (bf16[1024,256]{1,0:T(8,128)(2,1)S(1)}, bf16[1024,256]{1,0:T(8,128)(2,1)S(1)}) custom-call(bf16[64,2176]{1,0:T(8,128)(2,1)S(1)} %copy-done.5, bf16[64,2176]{1,0:T(8,128)(2,1)S(1)} %collective-permute-done.refs_5_.refs_1_, bf16[64,2176]{1,0:T(8,128)(2,1)S(1)} %collective-permute-done.1.refs_6_.refs_2_, ...), custom_call_target="tpu_custom_call" | custom-call | flops 1 | bytes 1 | tf_op jit(solution)/shard_map/values/pallas_call | solution.py:325
  66.3 0.0 copy-start.7
  66.3 0.9 %collective-permute-done.27 = bf16[64,2048]{1,0:T(8,128)(2,1)S(1)} collective-permute-done((bf16[64,2048]{1,0:T(8,128)(2,1)S(1)}, bf16[64,2048]{1,0:T(8,128)(2,1)S(1)}, u32[]{:S(2)}, u32[]{:S(2)}) %collective-permute-start.27) | collective-permute-done | bytes 262176 | tf_op jit(solution)/shard_map/ppermute | solution.py:63
  67.2 0.1 add_convert_fusion.2
  67.4 0.2 collective-permute-start.29
  67.6 0.9 %collective-permute-start.26 = (bf16[64,2048]{1,0:T(8,128)(2,1)S(1)}, bf16[64,2048]{1,0:T(8,128)(2,1)S(1)}, u32[]{:S(2)}, u32[]{:S(2)}) collective-permute-start(bf16[64,2048]{1,0:T(8,128)(2,1)S(1)} %get-tuple-element.60), channel_id=1, source_target_pairs={{0,2},{1,3},{2,0},{3,1},{4,6},{5,7},{6,4},{7,5},{12,14},{13,15},{1... | collective-permute-start | bytes 786440 | tf_op jit(solution)/shard_map/ppermute | solution.py:63
  68.5 1.8 %attention.4.refs_0_ = bf16[64,4096]{1,0:T(8,128)(2,1)} custom-call(bf16[64,4096]{1,0:T(8,128)(2,1)S(1)} %bitcast.22, bf16[1024,256]{1,0:T(8,128)(2,1)S(1)} %get-tuple-element.52.k_ref, bf16[1024,256]{1,0:T(8,128)(2,1)S(1)} %get-tuple-element.53.v_ref), custom_call_target="tpu_custom_call" | custom-call | flops 1 | bytes 1 | tf_op jit(solution)/shard_map/attention/pallas_call | solution.py:411
  70.3 1.8 %attention.5.refs_0_ = bf16[64,4096]{1,0:T(8,128)(2,1)} custom-call(bf16[64,4096]{1,0:T(8,128)(2,1)S(1)} %bitcast.23, bf16[1024,256]{1,0:T(8,128)(2,1)S(1)} %get-tuple-element.52.k_ref, bf16[1024,256]{1,0:T(8,128)(2,1)S(1)} %get-tuple-element.53.v_ref, bf16[64,4096]{1,0:T(8,128)(2,1)} %attention.4.refs_0_), custom_call_target="tpu_custom_call", output_to_operand_aliasing={{}: (3, {})} | custom-call | flops 1 | bytes 1 | tf_op jit(solution)/shard_map/attention/pallas_call | solution.py:411
  72.2 3.9 %collective-permute-done.29 = bf16[64,2048]{1,0:T(8,128)(2,1)S(1)} collective-permute-done((bf16[64,2048]{1,0:T(8,128)(2,1)S(1)}, bf16[64,2048]{1,0:T(8,128)(2,1)S(1)}, u32[]{:S(2)}, u32[]{:S(2)}) %collective-permute-start.29) | collective-permute-done | bytes 262176 | tf_op jit(solution)/shard_map/ppermute | solution.py:55
  76.1 0.1 add_convert_fusion.1
  76.2 0.5 collective-permute-start.31
  76.7 1.2 %collective-permute-start.30 = (bf16[64,2048]{1,0:T(8,128)(2,1)S(1)}, bf16[64,2048]{1,0:T(8,128)(2,1)S(1)}, u32[]{:S(2)}, u32[]{:S(2)}) collective-permute-start(bf16[64,2048]{1,0:T(8,128)(2,1)S(1)} %get-tuple-element.58), channel_id=1, source_target_pairs={{0,2},{1,3},{2,0},{3,1},{4,6},{5,7},{6,4},{7,5},{12,14},{13,15},{1... | collective-permute-start | bytes 786440 | tf_op jit(solution)/shard_map/ppermute | solution.py:63
  78.0 1.8 %attention.6.refs_0_ = bf16[64,4096]{1,0:T(8,128)(2,1)} custom-call(bf16[64,4096]{1,0:T(8,128)(2,1)S(1)} %bitcast.24, bf16[1024,256]{1,0:T(8,128)(2,1)S(1)} %get-tuple-element.52.k_ref, bf16[1024,256]{1,0:T(8,128)(2,1)S(1)} %get-tuple-element.53.v_ref, bf16[64,4096]{1,0:T(8,128)(2,1)} %attention.5.refs_0_), custom_call_target="tpu_custom_call", output_to_operand_aliasing={{}: (3, {})} | custom-call | flops 1 | bytes 1 | tf_op jit(solution)/shard_map/attention/pallas_call | solution.py:411
  79.8 1.8 %attention.7 = bf16[64,4096]{1,0:T(8,128)(2,1)} custom-call(bf16[64,4096]{1,0:T(8,128)(2,1)S(1)} %bitcast.25, bf16[1024,256]{1,0:T(8,128)(2,1)S(1)} %get-tuple-element.52.k_ref, bf16[1024,256]{1,0:T(8,128)(2,1)S(1)} %get-tuple-element.53.v_ref, bf16[64,4096]{1,0:T(8,128)(2,1)} %attention.6.refs_0_), custom_call_target="tpu_custom_call", output_to_operand_aliasing={{}: (3, {})} | custom-call | flops 1 | bytes 1 | tf_op jit(solution)/shard_map/attention/pallas_call | solution.py:411
  81.6 2.1 %collective-permute-done.31 = bf16[64,2048]{1,0:T(8,128)(2,1)S(1)} collective-permute-done((bf16[64,2048]{1,0:T(8,128)(2,1)S(1)}, bf16[64,2048]{1,0:T(8,128)(2,1)S(1)}, u32[]{:S(2)}, u32[]{:S(2)}) %collective-permute-start.31) | collective-permute-done | bytes 262176 | tf_op jit(solution)/shard_map/ppermute | solution.py:55
  83.8 0.9 %fusion = bf16[64,1,2048]{2,0,1:T(8,128)(2,1)} fusion(bf16[64,2048]{1,0:T(8,128)(2,1)S(1)} %collective-permute-done.31, bf16[64,2048]{1,0:T(8,128)(2,1)S(1)} %collective-permute-done.30, bf16[256,2048]{1,0:T(8,128)(2,1)S(1)} %collective-permute-done.17, bf16[128,2048]{1,0:T(8,128)(2,1)S(1)} %get-tuple-element.37, bf16[64,1,2048]{2,0,1:T(8,128)(2,1)S(1)} %copy-done.7), kind=kLoop, calls=%fused_computation.8 | loop fusion | flops 1310720 | bytes 1572864 | tf_op jit(solution)/shard_map/reshape | solution.py:570
  (32 shorter events, 0.1 us)
Async XLA Ops:
  2.5 4.6 %collective-permute-start.1 = (bf16[64,2176]{1,0:T(8,128)(2,1)}, bf16[64,2176]{1,0:T(8,128)(2,1)S(1)}, u32[]{:S(2)}, u32[]{:S(2)}) collective-permute-start(bf16[64,2176]{1,0:T(8,128)(2,1)} %get-tuple-element.31.refs_4_.refs_0_), channel_id=1, source_target_pairs={{0,1},{1,0},{2,3},{3,2},{4,5},{5,4},{6,7},{7,6},{12,13},{13,12},{1... | collective-permute-start | bytes 835592 | tf_op jit(solution)/shard_map/ppermute | solution.py:67
  2.9 12.5 %collective-permute-start.3 = (bf16[64,2176]{1,0:T(8,128)(2,1)}, bf16[64,2176]{1,0:T(8,128)(2,1)S(1)}, u32[]{:S(2)}, u32[]{:S(2)}) collective-permute-start(bf16[64,2176]{1,0:T(8,128)(2,1)} %get-tuple-element.31.refs_4_.refs_0_), channel_id=1, source_target_pairs={{0,4},{1,5},{2,6},{3,7},{4,12},{5,13},{6,14},{7,15},{12,8},{13,9},... | collective-permute-start | bytes 835592 | tf_op jit(solution)/shard_map/ppermute | solution.py:55
  5.5 11.8 %collective-permute-start = (bf16[64,2176]{1,0:T(8,128)(2,1)}, bf16[64,2176]{1,0:T(8,128)(2,1)S(1)}, u32[]{:S(2)}, u32[]{:S(2)}) collective-permute-start(bf16[64,2176]{1,0:T(8,128)(2,1)} %get-tuple-element.31.refs_4_.refs_0_), channel_id=1, source_target_pairs={{0,2},{1,3},{2,0},{3,1},{4,6},{5,7},{6,4},{7,5},{12,14},{13,15},{1... | collective-permute-start | bytes 835592 | tf_op jit(solution)/shard_map/ppermute | solution.py:63
  7.0 2.8 %copy-start = (bf16[1,2048,1536]{2,1,0:T(8,128)(2,1)S(1)}, bf16[1,2048,1536]{2,1,0:T(8,128)(2,1)}, u32[]{:S(2)}) copy-start(bf16[1,2048,1536]{2,1,0:T(8,128)(2,1)} %param.16) | copy-start | bytes 18874372
  9.8 1.9 %copy-start.2 = (bf16[1,768,2048]{2,1,0:T(8,128)(2,1)S(1)}, bf16[1,768,2048]{2,1,0:T(8,128)(2,1)}, u32[]{:S(2)}) copy-start(bf16[1,768,2048]{2,1,0:T(8,128)(2,1)} %param.17) | copy-start | bytes 9437188
  11.7 0.9 %copy-start.6 = (bf16[192,256]{1,0:T(8,128)(2,1)S(1)}, bf16[192,256]{1,0:T(8,128)(2,1)}, u32[]{:S(2)}) copy-start(bf16[192,256]{1,0:T(8,128)(2,1)} %get-tuple-element.33.small_ref) | copy-start | bytes 294916
  12.6 22.0 %copy-start.1 = (bf16[1,2048,1536]{2,1,0:T(8,128)(2,1)S(1)}, bf16[1,2048,1536]{2,1,0:T(8,128)(2,1)}, u32[]{:S(2)}) copy-start(bf16[1,2048,1536]{2,1,0:T(8,128)(2,1)} %param.16) | copy-start | bytes 18874372
  12.6 22.0 %copy-start.3 = (bf16[1,768,2048]{2,1,0:T(8,128)(2,1)S(1)}, bf16[1,768,2048]{2,1,0:T(8,128)(2,1)}, u32[]{:S(2)}) copy-start(bf16[1,768,2048]{2,1,0:T(8,128)(2,1)} %param.17) | copy-start | bytes 9437188
  12.6 22.0 %copy-start.5 = (bf16[64,2176]{1,0:T(8,128)(2,1)S(1)}, bf16[64,2176]{1,0:T(8,128)(2,1)}, u32[]{:S(2)}) copy-start(bf16[64,2176]{1,0:T(8,128)(2,1)} %get-tuple-element.31.refs_4_.refs_0_) | copy-start | bytes 835588
  12.6 4.7 %collective-permute-start.7 = (bf16[192,256]{1,0:T(8,128)(2,1)S(1)}, bf16[192,256]{1,0:T(8,128)(2,1)S(1)}, u32[]{:S(2)}, u32[]{:S(2)}) collective-permute-start(bf16[192,256]{1,0:T(8,128)(2,1)S(1)} %hold_weights.1), channel_id=1, source_target_pairs={{0,2},{1,3},{2,0},{3,1},{4,6},{5,7},{6,4},{7,5},{12,14},{13,15},{1... | collective-permute-start | bytes 294920 | tf_op jit(solution)/shard_map/ppermute | solution.py:63
  13.2 9.7 %collective-permute-start.12 = (bf16[64,2176]{1,0:T(8,128)(2,1)}, bf16[64,2176]{1,0:T(8,128)(2,1)S(1)}, u32[]{:S(2)}, u32[]{:S(2)}) collective-permute-start(bf16[64,2176]{1,0:T(8,128)(2,1)} %get-tuple-element.31.refs_4_.refs_0_), channel_id=1, source_target_pairs={{0,8},{1,9},{2,10},{3,11},{4,0},{5,1},{6,2},{7,3},{12,4},{13,5},{1... | collective-permute-start | bytes 835592 | tf_op jit(solution)/shard_map/ppermute | solution.py:59
  15.5 9.1 %collective-permute-start.4 = (bf16[64,2176]{1,0:T(8,128)(2,1)S(1)}, bf16[64,2176]{1,0:T(8,128)(2,1)S(1)}, u32[]{:S(2)}, u32[]{:S(2)}) collective-permute-start(bf16[64,2176]{1,0:T(8,128)(2,1)S(1)} %collective-permute-done.3.refs_0_.refs_4_), channel_id=1, source_target_pairs={{0,2},{1,3},{2,0},{3,1},{4,6},{5,7},{6,4},{7,5},{12,14},{13,15},{1... | collective-permute-start | bytes 835592 | tf_op jit(solution)/shard_map/ppermute | solution.py:63
  17.4 13.2 %collective-permute-start.8 = (bf16[64,2176]{1,0:T(8,128)(2,1)S(1)}, bf16[64,2176]{1,0:T(8,128)(2,1)S(1)}, u32[]{:S(2)}, u32[]{:S(2)}) collective-permute-start(bf16[64,2176]{1,0:T(8,128)(2,1)S(1)} %collective-permute-done.3.refs_0_.refs_4_), channel_id=1, source_target_pairs={{0,4},{1,5},{2,6},{3,7},{4,12},{5,13},{6,14},{7,15},{12,8},{13,9},... | collective-permute-start | bytes 835592 | tf_op jit(solution)/shard_map/ppermute | solution.py:55
  22.9 9.2 %collective-permute-start.13 = (bf16[64,2176]{1,0:T(8,128)(2,1)S(1)}, bf16[64,2176]{1,0:T(8,128)(2,1)S(1)}, u32[]{:S(2)}, u32[]{:S(2)}) collective-permute-start(bf16[64,2176]{1,0:T(8,128)(2,1)S(1)} %collective-permute-done.12.refs_4_.refs_12_), channel_id=1, source_target_pairs={{0,2},{1,3},{2,0},{3,1},{4,6},{5,7},{6,4},{7,5},{12,14},{13,15},{1... | collective-permute-start | bytes 835592 | tf_op jit(solution)/shard_map/ppermute | solution.py:63
  24.1 10.5 %collective-permute-start.5 = (bf16[64,2176]{1,0:T(8,128)(2,1)S(1)}, bf16[64,2176]{1,0:T(8,128)(2,1)S(1)}, u32[]{:S(2)}, u32[]{:S(2)}) collective-permute-start(bf16[64,2176]{1,0:T(8,128)(2,1)S(1)} %collective-permute-done.3.refs_0_.refs_4_), channel_id=1, source_target_pairs={{0,1},{1,0},{2,3},{3,2},{4,5},{5,4},{6,7},{7,6},{12,13},{13,12},{1... | collective-permute-start | bytes 835592 | tf_op jit(solution)/shard_map/ppermute | solution.py:67
  24.1 10.5 %collective-permute-start.2 = (bf16[64,2176]{1,0:T(8,128)(2,1)S(1)}, bf16[64,2176]{1,0:T(8,128)(2,1)S(1)}, u32[]{:S(2)}, u32[]{:S(2)}) collective-permute-start(bf16[64,2176]{1,0:T(8,128)(2,1)S(1)} %collective-permute-done.refs_5_.refs_1_), channel_id=1, source_target_pairs={{0,1},{1,0},{2,3},{3,2},{4,5},{5,4},{6,7},{7,6},{12,13},{13,12},{1... | collective-permute-start | bytes 835592 | tf_op jit(solution)/shard_map/ppermute | solution.py:67
  24.6 10.0 %collective-permute-start.6 = (bf16[64,2176]{1,0:T(8,128)(2,1)S(1)}, bf16[64,2176]{1,0:T(8,128)(2,1)S(1)}, u32[]{:S(2)}, u32[]{:S(2)}) collective-permute-start(bf16[64,2176]{1,0:T(8,128)(2,1)S(1)} %collective-permute-done.4.refs_1_.refs_5_), channel_id=1, source_target_pairs={{0,1},{1,0},{2,3},{3,2},{4,5},{5,4},{6,7},{7,6},{12,13},{13,12},{1... | collective-permute-start | bytes 835592 | tf_op jit(solution)/shard_map/ppermute | solution.py:67
  30.5 9.0 %collective-permute-start.9 = (bf16[64,2176]{1,0:T(8,128)(2,1)S(1)}, bf16[64,2176]{1,0:T(8,128)(2,1)S(1)}, u32[]{:S(2)}, u32[]{:S(2)}) collective-permute-start(bf16[64,2176]{1,0:T(8,128)(2,1)S(1)} %collective-permute-done.8.refs_0_.refs_8_), channel_id=1, source_target_pairs={{0,2},{1,3},{2,0},{3,1},{4,6},{5,7},{6,4},{7,5},{12,14},{13,15},{1... | collective-permute-start | bytes 835592 | tf_op jit(solution)/shard_map/ppermute | solution.py:63
  32.1 7.4 %collective-permute-start.16 = (bf16[384,256]{1,0:T(8,128)(2,1)S(1)}, bf16[384,256]{1,0:T(8,128)(2,1)S(1)}, u32[]{:S(2)}, u32[]{:S(2)}) collective-permute-start(bf16[384,256]{1,0:T(8,128)(2,1)S(1)} %pad_maximum_fusion.refs_16_), channel_id=1, source_target_pairs={{0,4},{1,5},{2,6},{3,7},{4,12},{5,13},{6,14},{7,15},{12,8},{13,9},... | collective-permute-start | bytes 589832 | tf_op jit(solution)/shard_map/ppermute | solution.py:55
  39.5 2.7 %collective-permute-start.17 = (bf16[256,2048]{1,0:T(8,128)(2,1)S(1)}, bf16[256,2048]{1,0:T(8,128)(2,1)S(1)}, u32[]{:S(2)}, u32[]{:S(2)}) collective-permute-start(bf16[256,2048]{1,0:T(8,128)(2,1)S(1)} %get-tuple-element.39), channel_id=1, source_target_pairs={{0,1},{1,0},{2,3},{3,2},{4,5},{5,4},{6,7},{7,6},{12,13},{13,12},{1... | collective-permute-start | bytes 3145736 | tf_op jit(solution)/shard_map/ppermute | solution.py:67
  39.5 4.7 %collective-permute-start.14 = (bf16[64,2176]{1,0:T(8,128)(2,1)S(1)}, bf16[64,2176]{1,0:T(8,128)(2,1)S(1)}, u32[]{:S(2)}, u32[]{:S(2)}) collective-permute-start(bf16[64,2176]{1,0:T(8,128)(2,1)S(1)} %collective-permute-done.12.refs_4_.refs_12_), channel_id=1, source_target_pairs={{0,1},{1,0},{2,3},{3,2},{4,5},{5,4},{6,7},{7,6},{12,13},{13,12},{1... | collective-permute-start | bytes 835592 | tf_op jit(solution)/shard_map/ppermute | solution.py:67
  40.0 4.2 %collective-permute-start.15 = (bf16[64,2176]{1,0:T(8,128)(2,1)S(1)}, bf16[64,2176]{1,0:T(8,128)(2,1)S(1)}, u32[]{:S(2)}, u32[]{:S(2)}) collective-permute-start(bf16[64,2176]{1,0:T(8,128)(2,1)S(1)} %collective-permute-done.13.refs_5_.refs_13_), channel_id=1, source_target_pairs={{0,1},{1,0},{2,3},{3,2},{4,5},{5,4},{6,7},{7,6},{12,13},{13,12},{1... | collective-permute-start | bytes 835592 | tf_op jit(solution)/shard_map/ppermute | solution.py:67
  40.0 6.2 %collective-permute-start.10 = (bf16[64,2176]{1,0:T(8,128)(2,1)S(1)}, bf16[64,2176]{1,0:T(8,128)(2,1)S(1)}, u32[]{:S(2)}, u32[]{:S(2)}) collective-permute-start(bf16[64,2176]{1,0:T(8,128)(2,1)S(1)} %collective-permute-done.8.refs_0_.refs_8_), channel_id=1, source_target_pairs={{0,1},{1,0},{2,3},{3,2},{4,5},{5,4},{6,7},{7,6},{12,13},{13,12},{1... | collective-permute-start | bytes 835592 | tf_op jit(solution)/shard_map/ppermute | solution.py:67
  40.5 5.7 %collective-permute-start.11 = (bf16[64,2176]{1,0:T(8,128)(2,1)S(1)}, bf16[64,2176]{1,0:T(8,128)(2,1)S(1)}, u32[]{:S(2)}, u32[]{:S(2)}) collective-permute-start(bf16[64,2176]{1,0:T(8,128)(2,1)S(1)} %collective-permute-done.9.refs_1_.refs_9_), channel_id=1, source_target_pairs={{0,1},{1,0},{2,3},{3,2},{4,5},{5,4},{6,7},{7,6},{12,13},{13,12},{1... | collective-permute-start | bytes 835592 | tf_op jit(solution)/shard_map/ppermute | solution.py:67
  42.3 13.7 %collective-permute-start.18 = (bf16[64,2048]{1,0:T(8,128)(2,1)S(1)}, bf16[64,2048]{1,0:T(8,128)(2,1)S(1)}, u32[]{:S(2)}, u32[]{:S(2)}) collective-permute-start(bf16[64,2048]{1,0:T(8,128)(2,1)S(1)} %get-tuple-element.62), channel_id=1, source_target_pairs={{0,2},{1,3},{2,0},{3,1},{4,6},{5,7},{6,4},{7,5},{12,14},{13,15},{1... | collective-permute-start | bytes 786440 | tf_op jit(solution)/shard_map/ppermute | solution.py:63
  44.2 7.6 %collective-permute-start.20 = (bf16[384,256]{1,0:T(8,128)(2,1)S(1)}, bf16[384,256]{1,0:T(8,128)(2,1)S(1)}, u32[]{:S(2)}, u32[]{:S(2)}) collective-permute-start(bf16[384,256]{1,0:T(8,128)(2,1)S(1)} %pad_maximum_fusion.refs_16_), channel_id=1, source_target_pairs={{0,8},{1,9},{2,10},{3,11},{4,0},{5,1},{6,2},{7,3},{12,4},{13,5},{1... | collective-permute-start | bytes 589832 | tf_op jit(solution)/shard_map/ppermute | solution.py:59
  44.2 11.8 %collective-permute-start.19 = (bf16[384,256]{1,0:T(8,128)(2,1)S(1)}, bf16[384,256]{1,0:T(8,128)(2,1)S(1)}, u32[]{:S(2)}, u32[]{:S(2)}) collective-permute-start(bf16[384,256]{1,0:T(8,128)(2,1)S(1)} %collective-permute-done.16.refs_18_), channel_id=1, source_target_pairs={{0,4},{1,5},{2,6},{3,7},{4,12},{5,13},{6,14},{7,15},{12,8},{13,9},... | collective-permute-start | bytes 589832 | tf_op jit(solution)/shard_map/ppermute | solution.py:55
  50.4 18.1 %copy-start.4 = (bf16[64,1,4096]{2,0,1:T(8,128)(2,1)S(1)}, bf16[64,1,4096]{2,0,1:T(8,128)(2,1)}, u32[]{:S(2)}) copy-start(bf16[64,1,4096]{2,0,1:T(8,128)(2,1)} %param.10) | copy-start | bytes 1572868
  56.0 2.7 %collective-permute-start.21 = (bf16[256,2048]{1,0:T(8,128)(2,1)S(1)}, bf16[256,2048]{1,0:T(8,128)(2,1)S(1)}, u32[]{:S(2)}, u32[]{:S(2)}) collective-permute-start(bf16[256,2048]{1,0:T(8,128)(2,1)S(1)} %get-tuple-element.44), channel_id=1, source_target_pairs={{0,1},{1,0},{2,3},{3,2},{4,5},{5,4},{6,7},{7,6},{12,13},{13,12},{1... | collective-permute-start | bytes 3145736 | tf_op jit(solution)/shard_map/ppermute | solution.py:67
  56.1 10.2 %collective-permute-start.28 = (bf16[64,2048]{1,0:T(8,128)(2,1)S(1)}, bf16[64,2048]{1,0:T(8,128)(2,1)S(1)}, u32[]{:S(2)}, u32[]{:S(2)}) collective-permute-start(bf16[64,2048]{1,0:T(8,128)(2,1)S(1)} %add_convert_fusion.3), channel_id=1, source_target_pairs={{0,4},{1,5},{2,6},{3,7},{4,12},{5,13},{6,14},{7,15},{12,8},{13,9},... | collective-permute-start | bytes 786440 | tf_op jit(solution)/shard_map/ppermute | solution.py:55
  56.2 4.0 %collective-permute-start.22 = (bf16[384,256]{1,0:T(8,128)(2,1)S(1)}, bf16[384,256]{1,0:T(8,128)(2,1)S(1)}, u32[]{:S(2)}, u32[]{:S(2)}) collective-permute-start(bf16[384,256]{1,0:T(8,128)(2,1)S(1)} %pad_maximum_fusion.refs_16_), channel_id=1, source_target_pairs={{0,1},{1,0},{2,3},{3,2},{4,5},{5,4},{6,7},{7,6},{12,13},{13,12},{1... | collective-permute-start | bytes 589832 | tf_op jit(solution)/shard_map/ppermute | solution.py:67
  58.8 8.4 %collective-permute-start.27 = (bf16[64,2048]{1,0:T(8,128)(2,1)S(1)}, bf16[64,2048]{1,0:T(8,128)(2,1)S(1)}, u32[]{:S(2)}, u32[]{:S(2)}) collective-permute-start(bf16[64,2048]{1,0:T(8,128)(2,1)S(1)} %get-tuple-element.61), channel_id=1, source_target_pairs={{0,2},{1,3},{2,0},{3,1},{4,6},{5,7},{6,4},{7,5},{12,14},{13,15},{1... | collective-permute-start | bytes 786440 | tf_op jit(solution)/shard_map/ppermute | solution.py:63
  59.7 1.4 %collective-permute-start.23 = (bf16[384,256]{1,0:T(8,128)(2,1)S(1)}, bf16[384,256]{1,0:T(8,128)(2,1)S(1)}, u32[]{:S(2)}, u32[]{:S(2)}) collective-permute-start(bf16[384,256]{1,0:T(8,128)(2,1)S(1)} %collective-permute-done.16.refs_18_), channel_id=1, source_target_pairs={{0,1},{1,0},{2,3},{3,2},{4,5},{5,4},{6,7},{7,6},{12,13},{13,12},{1... | collective-permute-start | bytes 589832 | tf_op jit(solution)/shard_map/ppermute | solution.py:67
  59.7 1.7 %collective-permute-start.24 = (bf16[384,256]{1,0:T(8,128)(2,1)S(1)}, bf16[384,256]{1,0:T(8,128)(2,1)S(1)}, u32[]{:S(2)}, u32[]{:S(2)}) collective-permute-start(bf16[384,256]{1,0:T(8,128)(2,1)S(1)} %collective-permute-done.19.refs_20_), channel_id=1, source_target_pairs={{0,1},{1,0},{2,3},{3,2},{4,5},{5,4},{6,7},{7,6},{12,13},{13,12},{1... | collective-permute-start | bytes 589832 | tf_op jit(solution)/shard_map/ppermute | solution.py:67
  60.2 1.5 %collective-permute-start.25 = (bf16[384,256]{1,0:T(8,128)(2,1)S(1)}, bf16[384,256]{1,0:T(8,128)(2,1)S(1)}, u32[]{:S(2)}, u32[]{:S(2)}) collective-permute-start(bf16[384,256]{1,0:T(8,128)(2,1)S(1)} %collective-permute-done.20.refs_22_), channel_id=1, source_target_pairs={{0,1},{1,0},{2,3},{3,2},{4,5},{5,4},{6,7},{7,6},{12,13},{13,12},{1... | collective-permute-start | bytes 589832 | tf_op jit(solution)/shard_map/ppermute | solution.py:67
  66.3 17.5 %copy-start.7 = (bf16[64,1,2048]{2,0,1:T(8,128)(2,1)S(1)}, bf16[64,1,2048]{2,0,1:T(8,128)(2,1)}, u32[]{:S(2)}) copy-start(bf16[64,1,2048]{2,0,1:T(8,128)(2,1)} %param.9) | copy-start | bytes 786436
  67.4 8.7 %collective-permute-start.29 = (bf16[64,2048]{1,0:T(8,128)(2,1)S(1)}, bf16[64,2048]{1,0:T(8,128)(2,1)S(1)}, u32[]{:S(2)}, u32[]{:S(2)}) collective-permute-start(bf16[64,2048]{1,0:T(8,128)(2,1)S(1)} %add_convert_fusion.2), channel_id=1, source_target_pairs={{0,4},{1,5},{2,6},{3,7},{4,12},{5,13},{6,14},{7,15},{12,8},{13,9},... | collective-permute-start | bytes 786440 | tf_op jit(solution)/shard_map/ppermute | solution.py:55
  67.6 8.4 %collective-permute-start.26 = (bf16[64,2048]{1,0:T(8,128)(2,1)S(1)}, bf16[64,2048]{1,0:T(8,128)(2,1)S(1)}, u32[]{:S(2)}, u32[]{:S(2)}) collective-permute-start(bf16[64,2048]{1,0:T(8,128)(2,1)S(1)} %get-tuple-element.60), channel_id=1, source_target_pairs={{0,2},{1,3},{2,0},{3,1},{4,6},{5,7},{6,4},{7,5},{12,14},{13,15},{1... | collective-permute-start | bytes 786440 | tf_op jit(solution)/shard_map/ppermute | solution.py:63
  76.2 7.6 %collective-permute-start.31 = (bf16[64,2048]{1,0:T(8,128)(2,1)S(1)}, bf16[64,2048]{1,0:T(8,128)(2,1)S(1)}, u32[]{:S(2)}, u32[]{:S(2)}) collective-permute-start(bf16[64,2048]{1,0:T(8,128)(2,1)S(1)} %add_convert_fusion.1), channel_id=1, source_target_pairs={{0,4},{1,5},{2,6},{3,7},{4,12},{5,13},{6,14},{7,15},{12,8},{13,9},... | collective-permute-start | bytes 786440 | tf_op jit(solution)/shard_map/ppermute | solution.py:55
  76.7 7.0 %collective-permute-start.30 = (bf16[64,2048]{1,0:T(8,128)(2,1)S(1)}, bf16[64,2048]{1,0:T(8,128)(2,1)S(1)}, u32[]{:S(2)}, u32[]{:S(2)}) collective-permute-start(bf16[64,2048]{1,0:T(8,128)(2,1)S(1)} %get-tuple-element.58), channel_id=1, source_target_pairs={{0,2},{1,3},{2,0},{3,1},{4,6},{5,7},{6,4},{7,5},{12,14},{13,15},{1... | collective-permute-start | bytes 786440 | tf_op jit(solution)/shard_map/ppermute | solution.py:63

commit v6 on v5

--- a/solution.py
+++ b/solution.py
@@ -79,8 +79,21 @@
 
 
 def pack_kernel(
-    act_ref, gain_ref, ids_ref, gates_ref, key_ref, weight_ref, out_ref, small_ref, meta_ref
+    act_ref,
+    gain_ref,
+    ids_ref,
+    gates_ref,
+    key_ref,
+    weight_ref,
+    up_hbm,
+    out_ref,
+    small_ref,
+    up_ref,
+    meta_ref,
+    up_sem,
 ):
+    fetch = pltpu.make_async_copy(up_hbm, up_ref, up_sem)
+    fetch.start()
     width = act_ref.shape[1]
     rows = act_ref.shape[0]
     top = ids_ref.shape[0]
@@ -99,38 +112,28 @@
     out_ref[:, width:] = meta_ref[...].T[:rows, :].astype(BF16)
     small_ref[:rows] = key_ref[...]
     small_ref[rows:] = weight_ref[...]
-
-
-def pack(activations, norm_gain, ids, gates, keys, value_weight):
+    fetch.wait()
+
+
+def pack(activations, norm_gain, ids, gates, keys, value_weight, w_gate_up):
     rows, width = activations.shape
     small_rows = rows + value_weight.shape[0]
+    from_hbm = pltpu.with_memory_space_constraint(w_gate_up, pltpu.HBM)
     assert rows <= META and ids.shape[0] <= 8
     return pl.pallas_call(
         pack_kernel,
         out_shape=[
             jax.ShapeDtypeStruct((rows, width + META), BF16),
             jax.ShapeDtypeStruct((small_rows, keys.shape[1]), BF16),
+            pltpu.VMEM(w_gate_up.shape, BF16),
         ],
-        scratch_shapes=[pltpu.VMEM((META, META), F32)],
+        in_specs=[IN_VMEM] * 6 + [ANY],
+        out_specs=[IN_VMEM] * 3,
+        scratch_shapes=[pltpu.VMEM((META, META), F32), pltpu.SemaphoreType.DMA(())],
+        compiler_params=pltpu.CompilerParams(vmem_limit_bytes=VMEM_LIMIT),
         cost_estimate=SHORT,
         name="normalize_and_pack",
-    )(activations, norm_gain.reshape(1, width), ids, gates, keys, value_weight)
-
-
-def hold_kernel(small_ref, up_ref, down_ref, out_ref):
-    out_ref[...] = small_ref[...]
-
-
-def hold(small, weights):
-    return pl.pallas_call(
-        hold_kernel,
-        out_shape=jax.ShapeDtypeStruct(small.shape, small.dtype),
-        in_specs=[IN_VMEM] * 3,
-        out_specs=IN_VMEM,
-        compiler_params=pltpu.CompilerParams(vmem_limit_bytes=4 * 2**20),
-        cost_estimate=SHORT,
-        name="hold_weights",
-    )(small, *weights)
+    )(activations, norm_gain.reshape(1, width), ids, gates, keys, value_weight, from_hbm)
 
 
 def in_vmem(*arrays):
@@ -141,22 +144,24 @@
     inputs = 1 + max(s[0] for group in sources for s in group)
     outputs = 1 + max(t[0] for group in targets for t in group)
     x_hbm = refs[:inputs]
-    up_ref, down_ref = refs[inputs : inputs + 2]
+    up_ref, down_hbm = refs[inputs : inputs + 2]
     out_hbm = refs[inputs + 2 : inputs + 2 + outputs]
     (
         x_buf,
+        down_buf,
         slot_rows,
         slot_gates,
         places,
         hidden,
         result,
         x_sem,
+        down_sem,
         out_sem,
     ) = refs[inputs + 2 + outputs :]
     groups, rows, packed = x_buf.shape
     width = packed - META
     slots = slot_rows.shape[0] // groups
-    units = down_ref.shape[0]
+    units = down_buf.shape[0]
     tile = 256
     me = lax.axis_index("seq").astype(F32)
 
@@ -189,6 +194,8 @@
     for group in range(groups):
         for copy in loads(group):
             copy.start()
+    load_down = pltpu.make_async_copy(down_hbm, down_buf, down_sem)
+    load_down.start()
 
     chunk = tok_rows * META // math.gcd(tok_rows, META)
     first = lax.broadcasted_iota(jnp.int32, (chunk, chunk), 0)
@@ -229,8 +236,9 @@
         gate = dot(slot_rows[...], up_ref[:, at : at + tile])
         up = dot(slot_rows[...], up_ref[:, units + at : units + at + tile])
         hidden[:, at : at + tile] = (gate / (1.0 + jnp.exp(-gate)) * up).astype(BF16)
+    load_down.wait()
     for at in range(0, width, tile):
-        out = dot(hidden[...], down_ref[:, at : at + tile]).astype(BF16).astype(F32)
+        out = dot(hidden[...], down_buf[:, at : at + tile]).astype(BF16).astype(F32)
         result[:, at : at + tile] = (out * slot_gates[:, 0:1]).astype(BF16)
     for group in range(groups):
         for at in range(0, width, 512):
@@ -254,27 +262,29 @@
     slots = rows // tok_rows * capacity
     assert slots % 16 == 0 and slots <= META and units % 256 == 0 and width % 512 == 0
     all_slots = groups * slots
-    weights = in_vmem(w_gate_up, w_down)
-    held = 2 * total * (packed + META) + all_slots * (4 * width + 2 * units + 4 * META)
+    (w_gate_up,) = in_vmem(w_gate_up)
+    held = 2 * units * width + 2 * total * (packed + META) + all_slots * (4 * width + 2 * units + 4 * META)
     return pl.pallas_call(
         functools.partial(expert_kernel, top, tok_rows, capacity, sources, targets),
         out_shape=[jax.ShapeDtypeStruct((count, width), BF16) for count in out_rows],
-        in_specs=[ANY] * len(arrays) + [IN_VMEM] * 2,
+        in_specs=[ANY] * len(arrays) + [IN_VMEM, ANY],
         out_specs=[ANY] * len(out_rows),
         scratch_shapes=[
             pltpu.VMEM((groups, rows, packed), BF16),
+            pltpu.VMEM(w_down.shape, BF16),
             pltpu.VMEM((all_slots, width), BF16),
             pltpu.VMEM((all_slots, META), F32),
             pltpu.VMEM((groups, rows, META), BF16),
             pltpu.VMEM((all_slots, units), BF16),
             pltpu.VMEM((all_slots, width), BF16),
             pltpu.SemaphoreType.DMA((groups, max(len(s) for s in sources))),
+            pltpu.SemaphoreType.DMA(()),
             pltpu.SemaphoreType.DMA((groups, max(len(t) for t in targets))),
         ],
         compiler_params=pltpu.CompilerParams(vmem_limit_bytes=held + 8 * 2**20),
         cost_estimate=SHORT,
         name="experts",
-    )(*arrays, *weights)
+    )(*arrays, w_gate_up, w_down)
 
 
 def value_kernel(key_rows, blocks, small_blocks, *refs):
@@ -437,21 +447,22 @@
 def on_line(acts, packed, small, queries, w_gate_up, w_down, top, capacity):
     rows, width = acts.shape
     line = [packed, forward(packed), None, backward(packed)]
-    crossed = [across(packed), across(line[1]), None, across(line[3])]
-    to_core = other_core(packed)
-    small = hold(after(small, to_core), in_vmem(w_gate_up, w_down))
-    pair = jnp.concatenate([small, across(small)], axis=0)
-    line[2] = forward(after(line[1], pair, crossed[0]))
-    crossed[2] = across(line[2])
-    arrays = [
-        [
+    small_across = across(small)
+    crossed = [across(after(packed, small_across)), across(line[1]), None, across(line[3])]
+    pair = jnp.concatenate([small, small_across], axis=0)
+    line[2] = forward(line[1])
+    arrays = [None] * LINE
+
+    def complete(step):
+        arrays[step] = [
             line[step],
             crossed[step],
-            other_core(line[step]) if step else to_core,
+            other_core(line[step]),
             other_core(crossed[step]),
         ]
-        for step in range(LINE)
-    ]
+
+    for step in (0, 1, 3):
+        complete(step)
     blocks = [
         (4 * step + core * 2 + y, 0, functools.partial(from_device, step, y, core))
         for step in range(LINE)
@@ -494,7 +505,9 @@
         return send
 
     theirs = [None] * LINE
-    experts(1, 0, [line[2], crossed[3]], [crossed[2], pairs[1]])
+    crossed[2] = across(line[2])
+    complete(2)
+    send = experts(1, 0, [line[2], pairs[0]], [crossed[3], crossed[2], pairs[1]])
     theirs[1] = across(crossing[1])
     send = experts(2, 3, [crossing[0], crossing[1]], [theirs[1], pairs[2], pairs[3]])
     total = summed(*mine[1], after(theirs[1], send))
@@ -548,13 +561,14 @@
     devices = lax.axis_size("seq")
     capacity = max(2, 3 * pos_rows * top // (2 * devices))
     acts = activations.reshape(pos_rows, model_width)
-    packed, small = pack(
+    packed, small, up_weights = pack(
         acts,
         norm_gain,
         expert_ids.transpose(1, 2, 0).reshape(top, pos_rows),
         gate_weights.transpose(1, 2, 0).reshape(top, pos_rows),
         keys.reshape(pos_rows, -1),
         value_weight,
+        w_gate_up[0],
     )
     way = on_line if devices == 4 * LINE else on_any
     context, layer_out = way(
@@ -562,7 +576,7 @@
         packed,
         small,
         queries.reshape(pos_rows, -1),
-        w_gate_up[0],
+        up_weights,
         w_down[0],
         top,
         capacity,

time: 84.9 us -> 91.4 us (1.077)
  starting transfers between devices: 27.3 us -> 32 us
  Pallas kernels: 22 us -> 23.7 us
    ppermute x9, waiting for transfers between devices: 2.2 us -> 6.85 us  [across(): return lax.ppermute(x, 'seq', swaps(1, 0))]
    ppermute x7, starting transfers between devices: 11.6 us -> 14.9 us  [forward(): return lax.ppermute(x, 'seq', ring_steps(1))]
    ppermute x2, waiting for transfers between devices: 3.29 us -> 0.37 us  [backward(): return lax.ppermute(x, 'seq', ring_steps(LINE - 1))]
    ppermute x2, starting transfers between devices: 2.27 us -> 4.11 us  [backward(): return lax.ppermute(x, 'seq', ring_steps(LINE - 1))]
    ppermute x7, waiting for transfers between devices: 16.9 us -> 16 us  [forward(): return lax.ppermute(x, 'seq', ring_steps(1))]
    pallas_call x1, Pallas kernels: 1.86 us -> 2.79 us  [pack(): pl.pallas_call(pack_kernel, out_shape=[jax.ShapeDtypeStruct((rows, width...]
    unnamed x16 -> x18, local copies, waits for them, and re-layouts: 5.59 us -> 4.77 us
  transfers between devices with their start and end apart: 32 -> 32, of which waited for: 14 -> 16; matrix products, arithmetic and copies ran while one was open for 0% -> 0% of each run, Pallas kernels for 24% -> 23%
where the time goes in v6:
time: 91.4 us; the launch traced here: 91.1 us
  starting transfers between devices  32 us (35%)
  waiting for transfers between devices  28.3 us (31%)
  Pallas kernels  23.7 us (26%)
  local copies, waits for them, and re-layouts  4.77 us (5%)
  other arithmetic  1.5 us (2%)
    ppermute x7, waiting for transfers between devices, forward(): return lax.ppermute(x, 'seq', ring_steps(1))  16 us
    ppermute x7, starting transfers between devices, forward(): return lax.ppermute(x, 'seq', ring_steps(1))  14.9 us
    ppermute x9, starting transfers between devices, across(): return lax.ppermute(x, 'seq', swaps(1, 0))  10.4 us
    pallas_call x2, Pallas kernels, run_experts(): pl.pallas_call(functools.partial(expert_kernel, top, tok_rows, capacity,...  9.03 us
    pallas_call x4, Pallas kernels, attend_part(): pl.pallas_call(functools.partial(attention_kernel, chunk), grid=(1,), out...  7.34 us
    ppermute x9, waiting for transfers between devices, across(): return lax.ppermute(x, 'seq', swaps(1, 0))  6.85 us
    ppermute x14, waiting for transfers between devices, other_core(): return lax.ppermute(x, 'seq', swaps(0, 1))  5.06 us
    unnamed x18, local copies, waits for them, and re-layouts  4.77 us
  transfers between devices with their start and end apart: 32, of which 16 were waited for; matrix products, arithmetic and copies ran while one was open for 0% of the time, Pallas kernels for 23%

profile of v6, /device:TPU:0, one launch (start us, length us, event | category | flops | bytes accessed | tf_op | source)
XLA Modules:
  0.0 91.1 jit_solution(1792455064018162089)
XLA Ops:
  0.6 0.0 copy-start.2
  0.7 1.1 %copy-done.2 = bf16[64,1,2048]{2,0,1:T(8,128)(2,1)S(1)} copy-done((bf16[64,1,2048]{2,0,1:T(8,128)(2,1)S(1)}, bf16[64,1,2048]{2,0,1:T(8,128)(2,1)}, u32[]{:S(2)}) %copy-start.2) | copy-done | bytes 262168
  1.7 0.8 copy-done.4
  2.6 0.8 copy-done.5
  3.3 0.7 copy-done.6
  4.0 0.7 copy-done.7
  4.7 0.7 copy-done.8
  5.4 2.8 %normalize_and_pack.1 = (bf16[64,2176]{1,0:T(8,128)(2,1)S(1)}, bf16[192,256]{1,0:T(8,128)(2,1)S(1)}, bf16[2048,1536]{1,0:T(8,128)(2,1)S(1)}) custom-call(bf16[64,2048]{1,0:T(8,128)(2,1)S(1)} %bitcast.22, f32[1,2048]{1,0:T(1,128)S(1)} %bitcast.24, s32[4,64]{1,0:T(4,128)S(1)} %bitcast.25, f32[4,64]{1,0:T(4,128)S(1)} %bitcast.26, bf16[64,256]{1,0:T(8,128)(2,1)S(1)} %bitcast.23, ...), custom_call_target="tpu_custom_call" | custom-call | flops 1 | bytes 1 | tf_op jit(solution)/shard_map/normalize_and_pack/pallas_call | solution.py:123
  8.2 3.1 %collective-permute-start.4 = (bf16[64,2176]{1,0:T(8,128)(2,1)S(1)}, bf16[64,2176]{1,0:T(8,128)(2,1)S(1)}, u32[]{:S(2)}, u32[]{:S(2)}) collective-permute-start(bf16[64,2176]{1,0:T(8,128)(2,1)S(1)} %get-tuple-element.33.refs_4_.refs_0_), channel_id=1, source_target_pairs={{0,4},{1,5},{2,6},{3,7},{4,12},{5,13},{6,14},{7,15},{12,8},{13,9},... | collective-permute-start | bytes 835592 | tf_op jit(solution)/shard_map/ppermute | solution.py:55
  11.3 1.1 %collective-permute-start.12 = (bf16[64,2176]{1,0:T(8,128)(2,1)S(1)}, bf16[64,2176]{1,0:T(8,128)(2,1)S(1)}, u32[]{:S(2)}, u32[]{:S(2)}) collective-permute-start(bf16[64,2176]{1,0:T(8,128)(2,1)S(1)} %get-tuple-element.33.refs_4_.refs_0_), channel_id=1, source_target_pairs={{0,8},{1,9},{2,10},{3,11},{4,0},{5,1},{6,2},{7,3},{12,4},{13,5},{1... | collective-permute-start | bytes 835592 | tf_op jit(solution)/shard_map/ppermute | solution.py:59
  12.4 1.8 %collective-permute-start = (bf16[192,256]{1,0:T(8,128)(2,1)S(1)}, bf16[192,256]{1,0:T(8,128)(2,1)S(1)}, u32[]{:S(2)}, u32[]{:S(2)}) collective-permute-start(bf16[192,256]{1,0:T(8,128)(2,1)S(1)} %get-tuple-element.32), channel_id=1, source_target_pairs={{0,2},{1,3},{2,0},{3,1},{4,6},{5,7},{6,4},{7,5},{12,14},{13,15},{1... | collective-permute-start | bytes 294920 | tf_op jit(solution)/shard_map/ppermute | solution.py:63
  14.2 2.8 %collective-permute-done = bf16[192,256]{1,0:T(8,128)(2,1)S(1)} collective-permute-done((bf16[192,256]{1,0:T(8,128)(2,1)S(1)}, bf16[192,256]{1,0:T(8,128)(2,1)S(1)}, u32[]{:S(2)}, u32[]{:S(2)}) %collective-permute-start) | collective-permute-done | bytes 98336 | tf_op jit(solution)/shard_map/ppermute | solution.py:63
  17.0 1.8 %collective-permute-start.1 = (bf16[64,2176]{1,0:T(8,128)(2,1)S(1)}, bf16[64,2176]{1,0:T(8,128)(2,1)S(1)}, u32[]{:S(2)}, u32[]{:S(2)}) collective-permute-start(bf16[64,2176]{1,0:T(8,128)(2,1)S(1)} %get-tuple-element.33.refs_4_.refs_0_), channel_id=1, source_target_pairs={{0,2},{1,3},{2,0},{3,1},{4,6},{5,7},{6,4},{7,5},{12,14},{13,15},{1... | collective-permute-start | bytes 835592 | tf_op jit(solution)/shard_map/ppermute | solution.py:63
  18.8 0.3 collective-permute-done.4.refs_0_.refs_4_
  19.1 1.6 %collective-permute-start.5 = (bf16[64,2176]{1,0:T(8,128)(2,1)S(1)}, bf16[64,2176]{1,0:T(8,128)(2,1)S(1)}, u32[]{:S(2)}, u32[]{:S(2)}) collective-permute-start(bf16[64,2176]{1,0:T(8,128)(2,1)S(1)} %collective-permute-done.4.refs_0_.refs_4_), channel_id=1, source_target_pairs={{0,2},{1,3},{2,0},{3,1},{4,6},{5,7},{6,4},{7,5},{12,14},{13,15},{1... | collective-permute-start | bytes 835592 | tf_op jit(solution)/shard_map/ppermute | solution.py:63
  20.6 7.6 %collective-permute-start.8 = (bf16[64,2176]{1,0:T(8,128)(2,1)S(1)}, bf16[64,2176]{1,0:T(8,128)(2,1)S(1)}, u32[]{:S(2)}, u32[]{:S(2)}) collective-permute-start(bf16[64,2176]{1,0:T(8,128)(2,1)S(1)} %collective-permute-done.4.refs_0_.refs_4_), channel_id=1, source_target_pairs={{0,4},{1,5},{2,6},{3,7},{4,12},{5,13},{6,14},{7,15},{12,8},{13,9},... | collective-permute-start | bytes 835592 | tf_op jit(solution)/shard_map/ppermute | solution.py:55
  28.3 0.1 collective-permute-start.13
  28.4 0.5 collective-permute-start.3
  28.9 1.3 %collective-permute-done.5.refs_1_.refs_5_ = bf16[64,2176]{1,0:T(8,128)(2,1)S(1)} collective-permute-done((bf16[64,2176]{1,0:T(8,128)(2,1)S(1)}, bf16[64,2176]{1,0:T(8,128)(2,1)S(1)}, u32[]{:S(2)}, u32[]{:S(2)}) %collective-permute-start.5) | collective-permute-done | bytes 278560 | tf_op jit(solution)/shard_map/ppermute | solution.py:63
  30.2 2.1 %collective-permute-done.8.refs_0_.refs_8_ = bf16[64,2176]{1,0:T(8,128)(2,1)S(1)} collective-permute-done((bf16[64,2176]{1,0:T(8,128)(2,1)S(1)}, bf16[64,2176]{1,0:T(8,128)(2,1)S(1)}, u32[]{:S(2)}, u32[]{:S(2)}) %collective-permute-start.8) | collective-permute-done | bytes 278560 | tf_op jit(solution)/shard_map/ppermute | solution.py:55
  32.3 1.2 %collective-permute-start.9 = (bf16[64,2176]{1,0:T(8,128)(2,1)S(1)}, bf16[64,2176]{1,0:T(8,128)(2,1)S(1)}, u32[]{:S(2)}, u32[]{:S(2)}) collective-permute-start(bf16[64,2176]{1,0:T(8,128)(2,1)S(1)} %collective-permute-done.8.refs_0_.refs_8_), channel_id=1, source_target_pairs={{0,2},{1,3},{2,0},{3,1},{4,6},{5,7},{6,4},{7,5},{12,14},{13,15},{1... | collective-permute-start | bytes 835592 | tf_op jit(solution)/shard_map/ppermute | solution.py:63
  33.6 2.2 %collective-permute-start.16 = (bf16[384,256]{1,0:T(8,128)(2,1)S(1)}, bf16[384,256]{1,0:T(8,128)(2,1)S(1)}, u32[]{:S(2)}, u32[]{:S(2)}) collective-permute-start(bf16[384,256]{1,0:T(8,128)(2,1)S(1)} %pad_maximum_fusion.refs_16_), channel_id=1, source_target_pairs={{0,4},{1,5},{2,6},{3,7},{4,12},{5,13},{6,14},{7,15},{12,8},{13,9},... | collective-permute-start | bytes 589832 | tf_op jit(solution)/shard_map/ppermute | solution.py:55
  35.8 4.5 %experts.2 = (bf16[128,2048]{1,0:T(8,128)(2,1)S(1)}, bf16[128,2048]{1,0:T(8,128)(2,1)S(1)}, bf16[256,2048]{1,0:T(8,128)(2,1)S(1)}) custom-call(bf16[64,2176]{1,0:T(8,128)(2,1)S(1)} %collective-permute-done.4.refs_0_.refs_4_, bf16[64,2176]{1,0:T(8,128)(2,1)S(1)} %collective-permute-done.5.refs_1_.refs_5_, ...), custom_call_target="tpu_custom_call" | custom-call | flops 1 | bytes 1 | tf_op jit(solution)/shard_map/experts/pallas_call | solution.py:267
  40.4 0.8 collective-permute-done.16.refs_18_
  41.1 2.2 %collective-permute-done.9.refs_1_.refs_9_ = bf16[64,2176]{1,0:T(8,128)(2,1)S(1)} collective-permute-done((bf16[64,2176]{1,0:T(8,128)(2,1)S(1)}, bf16[64,2176]{1,0:T(8,128)(2,1)S(1)}, u32[]{:S(2)}, u32[]{:S(2)}) %collective-permute-start.9) | collective-permute-done | bytes 278560 | tf_op jit(solution)/shard_map/ppermute | solution.py:63
  43.3 0.5 collective-permute-start.14
  43.8 0.5 collective-permute-start.15
  44.4 1.6 %collective-permute-done.17 = bf16[256,2048]{1,0:T(8,128)(2,1)S(1)} collective-permute-done((bf16[256,2048]{1,0:T(8,128)(2,1)S(1)}, bf16[256,2048]{1,0:T(8,128)(2,1)S(1)}, u32[]{:S(2)}, u32[]{:S(2)}) %collective-permute-start.17) | collective-permute-done | bytes 1048608 | tf_op jit(solution)/shard_map/ppermute | solution.py:67
  46.0 0.1 add_convert_fusion.6
  46.1 0.4 collective-permute-start.18
  46.5 3.0 %collective-permute-start.20 = (bf16[384,256]{1,0:T(8,128)(2,1)S(1)}, bf16[384,256]{1,0:T(8,128)(2,1)S(1)}, u32[]{:S(2)}, u32[]{:S(2)}) collective-permute-start(bf16[384,256]{1,0:T(8,128)(2,1)S(1)} %pad_maximum_fusion.refs_16_), channel_id=1, source_target_pairs={{0,8},{1,9},{2,10},{3,11},{4,0},{5,1},{6,2},{7,3},{12,4},{13,5},{1... | collective-permute-start | bytes 589832 | tf_op jit(solution)/shard_map/ppermute | solution.py:59
  49.6 0.6 collective-permute-start.19
  50.2 4.5 %experts.3 = (bf16[128,2048]{1,0:T(8,128)(2,1)S(1)}, bf16[128,2048]{1,0:T(8,128)(2,1)S(1)}, bf16[256,2048]{1,0:T(8,128)(2,1)S(1)}) custom-call(bf16[64,2176]{1,0:T(8,128)(2,1)S(1)} %collective-permute-done.8.refs_0_.refs_8_, bf16[64,2176]{1,0:T(8,128)(2,1)S(1)} %collective-permute-done.9.refs_1_.refs_9_, ...), custom_call_target="tpu_custom_call" | custom-call | flops 1 | bytes 1 | tf_op jit(solution)/shard_map/experts/pallas_call | solution.py:267
  54.7 0.0 copy-start.1
  54.7 0.4 collective-permute-done.20.refs_22_
  55.1 6.5 %collective-permute-done.19.refs_20_ = bf16[384,256]{1,0:T(8,128)(2,1)S(1)} collective-permute-done((bf16[384,256]{1,0:T(8,128)(2,1)S(1)}, bf16[384,256]{1,0:T(8,128)(2,1)S(1)}, u32[]{:S(2)}, u32[]{:S(2)}) %collective-permute-start.19) | collective-permute-done | bytes 196640 | tf_op jit(solution)/shard_map/ppermute | solution.py:55
  61.5 0.0 collective-permute-start.21
  61.6 0.1 add_convert_fusion.3
  61.7 0.1 collective-permute-start.28
  61.7 0.6 collective-permute-start.25
  62.3 1.9 %collective-permute-done.21 = bf16[256,2048]{1,0:T(8,128)(2,1)S(1)} collective-permute-done((bf16[256,2048]{1,0:T(8,128)(2,1)S(1)}, bf16[256,2048]{1,0:T(8,128)(2,1)S(1)}, u32[]{:S(2)}, u32[]{:S(2)}) %collective-permute-start.21) | collective-permute-done | bytes 1048608 | tf_op jit(solution)/shard_map/ppermute | solution.py:67
  64.2 0.1 add_convert_fusion.4
  64.3 1.3 %collective-permute-start.27 = (bf16[64,2048]{1,0:T(8,128)(2,1)S(1)}, bf16[64,2048]{1,0:T(8,128)(2,1)S(1)}, u32[]{:S(2)}, u32[]{:S(2)}) collective-permute-start(bf16[64,2048]{1,0:T(8,128)(2,1)S(1)} %get-tuple-element.61), channel_id=1, source_target_pairs={{0,2},{1,3},{2,0},{3,1},{4,6},{5,7},{6,4},{7,5},{12,14},{13,15},{1... | collective-permute-start | bytes 786440 | tf_op jit(solution)/shard_map/ppermute | solution.py:63
  65.7 0.5 collective-permute-start.23
  66.2 0.0 collective-permute-start.22
  66.2 0.9 %collective-permute-done.24.refs_21_ = bf16[384,256]{1,0:T(8,128)(2,1)S(1)} collective-permute-done((bf16[384,256]{1,0:T(8,128)(2,1)S(1)}, bf16[384,256]{1,0:T(8,128)(2,1)S(1)}, u32[]{:S(2)}, u32[]{:S(2)}) %collective-permute-start.24) | collective-permute-done | bytes 196640 | tf_op jit(solution)/shard_map/ppermute | solution.py:67
  67.1 0.3 collective-permute-done.23.refs_19_
  67.4 0.3 collective-permute-done.22.refs_17_
  67.7 4.6 %values.1 = (bf16[1024,256]{1,0:T(8,128)(2,1)S(1)}, bf16[1024,256]{1,0:T(8,128)(2,1)S(1)}) custom-call(bf16[64,2176]{1,0:T(8,128)(2,1)S(1)} %get-tuple-element.33.refs_4_.refs_0_, bf16[64,2176]{1,0:T(8,128)(2,1)S(1)} %collective-permute-done.1.refs_5_.refs_1_, bf16[64,2176]{1,0:T(8,128)(2,1)S(1)} %collective-permute-done.2.refs_6_.refs_2_, ...), custom_call_target="tpu_custom_call" | custom-call | flops 1 | bytes 1 | tf_op jit(solution)/shard_map/values/pallas_call | solution.py:335
  72.3 0.0 copy-start.3
  72.3 0.5 collective-permute-done.27
  72.7 0.1 add_convert_fusion.2
  72.9 0.4 collective-permute-start.29
  73.3 1.2 %collective-permute-start.26 = (bf16[64,2048]{1,0:T(8,128)(2,1)S(1)}, bf16[64,2048]{1,0:T(8,128)(2,1)S(1)}, u32[]{:S(2)}, u32[]{:S(2)}) collective-permute-start(bf16[64,2048]{1,0:T(8,128)(2,1)S(1)} %get-tuple-element.60), channel_id=1, source_target_pairs={{0,2},{1,3},{2,0},{3,1},{4,6},{5,7},{6,4},{7,5},{12,14},{13,15},{1... | collective-permute-start | bytes 786440 | tf_op jit(solution)/shard_map/ppermute | solution.py:63
  74.5 1.8 %attention.4.refs_0_ = bf16[64,4096]{1,0:T(8,128)(2,1)} custom-call(bf16[64,4096]{1,0:T(8,128)(2,1)S(1)} %bitcast.18, bf16[1024,256]{1,0:T(8,128)(2,1)S(1)} %get-tuple-element.52.k_ref, bf16[1024,256]{1,0:T(8,128)(2,1)S(1)} %get-tuple-element.53.v_ref), custom_call_target="tpu_custom_call" | custom-call | flops 1 | bytes 1 | tf_op jit(solution)/shard_map/attention/pallas_call | solution.py:421
  76.3 1.8 %attention.5.refs_0_ = bf16[64,4096]{1,0:T(8,128)(2,1)} custom-call(bf16[64,4096]{1,0:T(8,128)(2,1)S(1)} %bitcast.19, bf16[1024,256]{1,0:T(8,128)(2,1)S(1)} %get-tuple-element.52.k_ref, bf16[1024,256]{1,0:T(8,128)(2,1)S(1)} %get-tuple-element.53.v_ref, bf16[64,4096]{1,0:T(8,128)(2,1)} %attention.4.refs_0_), custom_call_target="tpu_custom_call", output_to_operand_aliasing={{}: (3, {})} | custom-call | flops 1 | bytes 1 | tf_op jit(solution)/shard_map/attention/pallas_call | solution.py:421
  78.1 3.9 %collective-permute-done.29 = bf16[64,2048]{1,0:T(8,128)(2,1)S(1)} collective-permute-done((bf16[64,2048]{1,0:T(8,128)(2,1)S(1)}, bf16[64,2048]{1,0:T(8,128)(2,1)S(1)}, u32[]{:S(2)}, u32[]{:S(2)}) %collective-permute-start.29) | collective-permute-done | bytes 262176 | tf_op jit(solution)/shard_map/ppermute | solution.py:55
  82.0 0.1 add_convert_fusion.1
  82.2 0.9 collective-permute-start.31
  83.0 1.0 %collective-permute-start.30 = (bf16[64,2048]{1,0:T(8,128)(2,1)S(1)}, bf16[64,2048]{1,0:T(8,128)(2,1)S(1)}, u32[]{:S(2)}, u32[]{:S(2)}) collective-permute-start(bf16[64,2048]{1,0:T(8,128)(2,1)S(1)} %get-tuple-element.58), channel_id=1, source_target_pairs={{0,2},{1,3},{2,0},{3,1},{4,6},{5,7},{6,4},{7,5},{12,14},{13,15},{1... | collective-permute-start | bytes 786440 | tf_op jit(solution)/shard_map/ppermute | solution.py:63
  84.1 1.8 %attention.6.refs_0_ = bf16[64,4096]{1,0:T(8,128)(2,1)} custom-call(bf16[64,4096]{1,0:T(8,128)(2,1)S(1)} %bitcast.20, bf16[1024,256]{1,0:T(8,128)(2,1)S(1)} %get-tuple-element.52.k_ref, bf16[1024,256]{1,0:T(8,128)(2,1)S(1)} %get-tuple-element.53.v_ref, bf16[64,4096]{1,0:T(8,128)(2,1)} %attention.5.refs_0_), custom_call_target="tpu_custom_call", output_to_operand_aliasing={{}: (3, {})} | custom-call | flops 1 | bytes 1 | tf_op jit(solution)/shard_map/attention/pallas_call | solution.py:421
  85.9 1.8 %attention.7 = bf16[64,4096]{1,0:T(8,128)(2,1)} custom-call(bf16[64,4096]{1,0:T(8,128)(2,1)S(1)} %bitcast.21, bf16[1024,256]{1,0:T(8,128)(2,1)S(1)} %get-tuple-element.52.k_ref, bf16[1024,256]{1,0:T(8,128)(2,1)S(1)} %get-tuple-element.53.v_ref, bf16[64,4096]{1,0:T(8,128)(2,1)} %attention.6.refs_0_), custom_call_target="tpu_custom_call", output_to_operand_aliasing={{}: (3, {})} | custom-call | flops 1 | bytes 1 | tf_op jit(solution)/shard_map/attention/pallas_call | solution.py:421
  87.8 2.5 %collective-permute-done.31 = bf16[64,2048]{1,0:T(8,128)(2,1)S(1)} collective-permute-done((bf16[64,2048]{1,0:T(8,128)(2,1)S(1)}, bf16[64,2048]{1,0:T(8,128)(2,1)S(1)}, u32[]{:S(2)}, u32[]{:S(2)}) %collective-permute-start.31) | collective-permute-done | bytes 262176 | tf_op jit(solution)/shard_map/ppermute | solution.py:55
  90.2 0.9 fusion
  (33 shorter events, 0.1 us)
Async XLA Ops:
  0.6 35.2 %copy-start = (bf16[1,768,2048]{2,1,0:T(8,128)(2,1)S(1)}, bf16[1,768,2048]{2,1,0:T(8,128)(2,1)}, u32[]{:S(2)}) copy-start(bf16[1,768,2048]{2,1,0:T(8,128)(2,1)} %param.17) | copy-start | bytes 9437188
  0.6 1.1 %copy-start.2 = (bf16[64,1,2048]{2,0,1:T(8,128)(2,1)S(1)}, bf16[64,1,2048]{2,0,1:T(8,128)(2,1)}, u32[]{:S(2)}) copy-start(bf16[64,1,2048]{2,0,1:T(8,128)(2,1)} %param.9) | copy-start | bytes 786436
  1.7 0.8 copy-start.4
  2.6 0.8 copy-start.5
  3.3 0.7 copy-start.6
  4.0 0.7 copy-start.7
  4.7 0.7 copy-start.8
  8.2 10.8 %collective-permute-start.4 = (bf16[64,2176]{1,0:T(8,128)(2,1)S(1)}, bf16[64,2176]{1,0:T(8,128)(2,1)S(1)}, u32[]{:S(2)}, u32[]{:S(2)}) collective-permute-start(bf16[64,2176]{1,0:T(8,128)(2,1)S(1)} %get-tuple-element.33.refs_4_.refs_0_), channel_id=1, source_target_pairs={{0,4},{1,5},{2,6},{3,7},{4,12},{5,13},{6,14},{7,15},{12,8},{13,9},... | collective-permute-start | bytes 835592 | tf_op jit(solution)/shard_map/ppermute | solution.py:55
  11.3 17.0 %collective-permute-start.12 = (bf16[64,2176]{1,0:T(8,128)(2,1)S(1)}, bf16[64,2176]{1,0:T(8,128)(2,1)S(1)}, u32[]{:S(2)}, u32[]{:S(2)}) collective-permute-start(bf16[64,2176]{1,0:T(8,128)(2,1)S(1)} %get-tuple-element.33.refs_4_.refs_0_), channel_id=1, source_target_pairs={{0,8},{1,9},{2,10},{3,11},{4,0},{5,1},{6,2},{7,3},{12,4},{13,5},{1... | collective-permute-start | bytes 835592 | tf_op jit(solution)/shard_map/ppermute | solution.py:59
  12.4 4.6 %collective-permute-start = (bf16[192,256]{1,0:T(8,128)(2,1)S(1)}, bf16[192,256]{1,0:T(8,128)(2,1)S(1)}, u32[]{:S(2)}, u32[]{:S(2)}) collective-permute-start(bf16[192,256]{1,0:T(8,128)(2,1)S(1)} %get-tuple-element.32), channel_id=1, source_target_pairs={{0,2},{1,3},{2,0},{3,1},{4,6},{5,7},{6,4},{7,5},{12,14},{13,15},{1... | collective-permute-start | bytes 294920 | tf_op jit(solution)/shard_map/ppermute | solution.py:63
  14.2 14.1 %collective-permute-start.2 = (bf16[64,2176]{1,0:T(8,128)(2,1)S(1)}, bf16[64,2176]{1,0:T(8,128)(2,1)S(1)}, u32[]{:S(2)}, u32[]{:S(2)}) collective-permute-start(bf16[64,2176]{1,0:T(8,128)(2,1)S(1)} %get-tuple-element.33.refs_4_.refs_0_), channel_id=1, source_target_pairs={{0,1},{1,0},{2,3},{3,2},{4,5},{5,4},{6,7},{7,6},{12,13},{13,12},{1... | collective-permute-start | bytes 835592 | tf_op jit(solution)/shard_map/ppermute | solution.py:67
  17.0 11.4 %collective-permute-start.1 = (bf16[64,2176]{1,0:T(8,128)(2,1)S(1)}, bf16[64,2176]{1,0:T(8,128)(2,1)S(1)}, u32[]{:S(2)}, u32[]{:S(2)}) collective-permute-start(bf16[64,2176]{1,0:T(8,128)(2,1)S(1)} %get-tuple-element.33.refs_4_.refs_0_), channel_id=1, source_target_pairs={{0,2},{1,3},{2,0},{3,1},{4,6},{5,7},{6,4},{7,5},{12,14},{13,15},{1... | collective-permute-start | bytes 835592 | tf_op jit(solution)/shard_map/ppermute | solution.py:63
  19.1 11.2 %collective-permute-start.5 = (bf16[64,2176]{1,0:T(8,128)(2,1)S(1)}, bf16[64,2176]{1,0:T(8,128)(2,1)S(1)}, u32[]{:S(2)}, u32[]{:S(2)}) collective-permute-start(bf16[64,2176]{1,0:T(8,128)(2,1)S(1)} %collective-permute-done.4.refs_0_.refs_4_), channel_id=1, source_target_pairs={{0,2},{1,3},{2,0},{3,1},{4,6},{5,7},{6,4},{7,5},{12,14},{13,15},{1... | collective-permute-start | bytes 835592 | tf_op jit(solution)/shard_map/ppermute | solution.py:63
  20.6 11.7 %collective-permute-start.8 = (bf16[64,2176]{1,0:T(8,128)(2,1)S(1)}, bf16[64,2176]{1,0:T(8,128)(2,1)S(1)}, u32[]{:S(2)}, u32[]{:S(2)}) collective-permute-start(bf16[64,2176]{1,0:T(8,128)(2,1)S(1)} %collective-permute-done.4.refs_0_.refs_4_), channel_id=1, source_target_pairs={{0,4},{1,5},{2,6},{3,7},{4,12},{5,13},{6,14},{7,15},{12,8},{13,9},... | collective-permute-start | bytes 835592 | tf_op jit(solution)/shard_map/ppermute | solution.py:55
  28.3 5.3 %collective-permute-start.6 = (bf16[64,2176]{1,0:T(8,128)(2,1)S(1)}, bf16[64,2176]{1,0:T(8,128)(2,1)S(1)}, u32[]{:S(2)}, u32[]{:S(2)}) collective-permute-start(bf16[64,2176]{1,0:T(8,128)(2,1)S(1)} %collective-permute-done.4.refs_0_.refs_4_), channel_id=1, source_target_pairs={{0,1},{1,0},{2,3},{3,2},{4,5},{5,4},{6,7},{7,6},{12,13},{13,12},{1... | collective-permute-start | bytes 835592 | tf_op jit(solution)/shard_map/ppermute | solution.py:67
  28.3 12.8 %collective-permute-start.13 = (bf16[64,2176]{1,0:T(8,128)(2,1)S(1)}, bf16[64,2176]{1,0:T(8,128)(2,1)S(1)}, u32[]{:S(2)}, u32[]{:S(2)}) collective-permute-start(bf16[64,2176]{1,0:T(8,128)(2,1)S(1)} %collective-permute-done.12.refs_4_.refs_12_), channel_id=1, source_target_pairs={{0,2},{1,3},{2,0},{3,1},{4,6},{5,7},{6,4},{7,5},{12,14},{13,15},{1... | collective-permute-start | bytes 835592 | tf_op jit(solution)/shard_map/ppermute | solution.py:63
  28.4 7.4 %collective-permute-start.3 = (bf16[64,2176]{1,0:T(8,128)(2,1)S(1)}, bf16[64,2176]{1,0:T(8,128)(2,1)S(1)}, u32[]{:S(2)}, u32[]{:S(2)}) collective-permute-start(bf16[64,2176]{1,0:T(8,128)(2,1)S(1)} %collective-permute-done.1.refs_5_.refs_1_), channel_id=1, source_target_pairs={{0,1},{1,0},{2,3},{3,2},{4,5},{5,4},{6,7},{7,6},{12,13},{13,12},{1... | collective-permute-start | bytes 835592 | tf_op jit(solution)/shard_map/ppermute | solution.py:67
  30.2 5.6 %collective-permute-start.7 = (bf16[64,2176]{1,0:T(8,128)(2,1)S(1)}, bf16[64,2176]{1,0:T(8,128)(2,1)S(1)}, u32[]{:S(2)}, u32[]{:S(2)}) collective-permute-start(bf16[64,2176]{1,0:T(8,128)(2,1)S(1)} %collective-permute-done.5.refs_1_.refs_5_), channel_id=1, source_target_pairs={{0,1},{1,0},{2,3},{3,2},{4,5},{5,4},{6,7},{7,6},{12,13},{13,12},{1... | collective-permute-start | bytes 835592 | tf_op jit(solution)/shard_map/ppermute | solution.py:67
  32.3 11.0 %collective-permute-start.9 = (bf16[64,2176]{1,0:T(8,128)(2,1)S(1)}, bf16[64,2176]{1,0:T(8,128)(2,1)S(1)}, u32[]{:S(2)}, u32[]{:S(2)}) collective-permute-start(bf16[64,2176]{1,0:T(8,128)(2,1)S(1)} %collective-permute-done.8.refs_0_.refs_8_), channel_id=1, source_target_pairs={{0,2},{1,3},{2,0},{3,1},{4,6},{5,7},{6,4},{7,5},{12,14},{13,15},{1... | collective-permute-start | bytes 835592 | tf_op jit(solution)/shard_map/ppermute | solution.py:63
  33.6 7.5 %collective-permute-start.16 = (bf16[384,256]{1,0:T(8,128)(2,1)S(1)}, bf16[384,256]{1,0:T(8,128)(2,1)S(1)}, u32[]{:S(2)}, u32[]{:S(2)}) collective-permute-start(bf16[384,256]{1,0:T(8,128)(2,1)S(1)} %pad_maximum_fusion.refs_16_), channel_id=1, source_target_pairs={{0,4},{1,5},{2,6},{3,7},{4,12},{5,13},{6,14},{7,15},{12,8},{13,9},... | collective-permute-start | bytes 589832 | tf_op jit(solution)/shard_map/ppermute | solution.py:55
  43.3 2.7 %collective-permute-start.17 = (bf16[256,2048]{1,0:T(8,128)(2,1)S(1)}, bf16[256,2048]{1,0:T(8,128)(2,1)S(1)}, u32[]{:S(2)}, u32[]{:S(2)}) collective-permute-start(bf16[256,2048]{1,0:T(8,128)(2,1)S(1)} %get-tuple-element.39), channel_id=1, source_target_pairs={{0,1},{1,0},{2,3},{3,2},{4,5},{5,4},{6,7},{7,6},{12,13},{13,12},{1... | collective-permute-start | bytes 3145736 | tf_op jit(solution)/shard_map/ppermute | solution.py:67
  43.3 3.2 %collective-permute-start.14 = (bf16[64,2176]{1,0:T(8,128)(2,1)S(1)}, bf16[64,2176]{1,0:T(8,128)(2,1)S(1)}, u32[]{:S(2)}, u32[]{:S(2)}) collective-permute-start(bf16[64,2176]{1,0:T(8,128)(2,1)S(1)} %collective-permute-done.12.refs_4_.refs_12_), channel_id=1, source_target_pairs={{0,1},{1,0},{2,3},{3,2},{4,5},{5,4},{6,7},{7,6},{12,13},{13,12},{1... | collective-permute-start | bytes 835592 | tf_op jit(solution)/shard_map/ppermute | solution.py:67
  43.8 5.7 %collective-permute-start.10 = (bf16[64,2176]{1,0:T(8,128)(2,1)S(1)}, bf16[64,2176]{1,0:T(8,128)(2,1)S(1)}, u32[]{:S(2)}, u32[]{:S(2)}) collective-permute-start(bf16[64,2176]{1,0:T(8,128)(2,1)S(1)} %collective-permute-done.8.refs_0_.refs_8_), channel_id=1, source_target_pairs={{0,1},{1,0},{2,3},{3,2},{4,5},{5,4},{6,7},{7,6},{12,13},{13,12},{1... | collective-permute-start | bytes 835592 | tf_op jit(solution)/shard_map/ppermute | solution.py:67
  43.8 6.3 %collective-permute-start.15 = (bf16[64,2176]{1,0:T(8,128)(2,1)S(1)}, bf16[64,2176]{1,0:T(8,128)(2,1)S(1)}, u32[]{:S(2)}, u32[]{:S(2)}) collective-permute-start(bf16[64,2176]{1,0:T(8,128)(2,1)S(1)} %collective-permute-done.13.refs_5_.refs_13_), channel_id=1, source_target_pairs={{0,1},{1,0},{2,3},{3,2},{4,5},{5,4},{6,7},{7,6},{12,13},{13,12},{1... | collective-permute-start | bytes 835592 | tf_op jit(solution)/shard_map/ppermute | solution.py:67
  44.4 5.8 %collective-permute-start.11 = (bf16[64,2176]{1,0:T(8,128)(2,1)S(1)}, bf16[64,2176]{1,0:T(8,128)(2,1)S(1)}, u32[]{:S(2)}, u32[]{:S(2)}) collective-permute-start(bf16[64,2176]{1,0:T(8,128)(2,1)S(1)} %collective-permute-done.9.refs_1_.refs_9_), channel_id=1, source_target_pairs={{0,1},{1,0},{2,3},{3,2},{4,5},{5,4},{6,7},{7,6},{12,13},{13,12},{1... | collective-permute-start | bytes 835592 | tf_op jit(solution)/shard_map/ppermute | solution.py:67
  46.1 15.4 %collective-permute-start.18 = (bf16[64,2048]{1,0:T(8,128)(2,1)S(1)}, bf16[64,2048]{1,0:T(8,128)(2,1)S(1)}, u32[]{:S(2)}, u32[]{:S(2)}) collective-permute-start(bf16[64,2048]{1,0:T(8,128)(2,1)S(1)} %get-tuple-element.62), channel_id=1, source_target_pairs={{0,2},{1,3},{2,0},{3,1},{4,6},{5,7},{6,4},{7,5},{12,14},{13,15},{1... | collective-permute-start | bytes 786440 | tf_op jit(solution)/shard_map/ppermute | solution.py:63
  46.5 8.5 %collective-permute-start.20 = (bf16[384,256]{1,0:T(8,128)(2,1)S(1)}, bf16[384,256]{1,0:T(8,128)(2,1)S(1)}, u32[]{:S(2)}, u32[]{:S(2)}) collective-permute-start(bf16[384,256]{1,0:T(8,128)(2,1)S(1)} %pad_maximum_fusion.refs_16_), channel_id=1, source_target_pairs={{0,8},{1,9},{2,10},{3,11},{4,0},{5,1},{6,2},{7,3},{12,4},{13,5},{1... | collective-permute-start | bytes 589832 | tf_op jit(solution)/shard_map/ppermute | solution.py:59
  49.6 12.0 %collective-permute-start.19 = (bf16[384,256]{1,0:T(8,128)(2,1)S(1)}, bf16[384,256]{1,0:T(8,128)(2,1)S(1)}, u32[]{:S(2)}, u32[]{:S(2)}) collective-permute-start(bf16[384,256]{1,0:T(8,128)(2,1)S(1)} %collective-permute-done.16.refs_18_), channel_id=1, source_target_pairs={{0,4},{1,5},{2,6},{3,7},{4,12},{5,13},{6,14},{7,15},{12,8},{13,9},... | collective-permute-start | bytes 589832 | tf_op jit(solution)/shard_map/ppermute | solution.py:55
  54.7 19.8 %copy-start.1 = (bf16[64,1,4096]{2,0,1:T(8,128)(2,1)S(1)}, bf16[64,1,4096]{2,0,1:T(8,128)(2,1)}, u32[]{:S(2)}) copy-start(bf16[64,1,4096]{2,0,1:T(8,128)(2,1)} %param.10) | copy-start | bytes 1572868
  61.5 2.7 %collective-permute-start.21 = (bf16[256,2048]{1,0:T(8,128)(2,1)S(1)}, bf16[256,2048]{1,0:T(8,128)(2,1)S(1)}, u32[]{:S(2)}, u32[]{:S(2)}) collective-permute-start(bf16[256,2048]{1,0:T(8,128)(2,1)S(1)} %get-tuple-element.44), channel_id=1, source_target_pairs={{0,1},{1,0},{2,3},{3,2},{4,5},{5,4},{6,7},{7,6},{12,13},{13,12},{1... | collective-permute-start | bytes 3145736 | tf_op jit(solution)/shard_map/ppermute | solution.py:67
  61.7 10.6 %collective-permute-start.28 = (bf16[64,2048]{1,0:T(8,128)(2,1)S(1)}, bf16[64,2048]{1,0:T(8,128)(2,1)S(1)}, u32[]{:S(2)}, u32[]{:S(2)}) collective-permute-start(bf16[64,2048]{1,0:T(8,128)(2,1)S(1)} %add_convert_fusion.3), channel_id=1, source_target_pairs={{0,4},{1,5},{2,6},{3,7},{4,12},{5,13},{6,14},{7,15},{12,8},{13,9},... | collective-permute-start | bytes 786440 | tf_op jit(solution)/shard_map/ppermute | solution.py:55
  61.7 4.5 %collective-permute-start.25 = (bf16[384,256]{1,0:T(8,128)(2,1)S(1)}, bf16[384,256]{1,0:T(8,128)(2,1)S(1)}, u32[]{:S(2)}, u32[]{:S(2)}) collective-permute-start(bf16[384,256]{1,0:T(8,128)(2,1)S(1)} %collective-permute-done.20.refs_22_), channel_id=1, source_target_pairs={{0,1},{1,0},{2,3},{3,2},{4,5},{5,4},{6,7},{7,6},{12,13},{13,12},{1... | collective-permute-start | bytes 589832 | tf_op jit(solution)/shard_map/ppermute | solution.py:67
  64.3 8.4 %collective-permute-start.27 = (bf16[64,2048]{1,0:T(8,128)(2,1)S(1)}, bf16[64,2048]{1,0:T(8,128)(2,1)S(1)}, u32[]{:S(2)}, u32[]{:S(2)}) collective-permute-start(bf16[64,2048]{1,0:T(8,128)(2,1)S(1)} %get-tuple-element.61), channel_id=1, source_target_pairs={{0,2},{1,3},{2,0},{3,1},{4,6},{5,7},{6,4},{7,5},{12,14},{13,15},{1... | collective-permute-start | bytes 786440 | tf_op jit(solution)/shard_map/ppermute | solution.py:63
  65.7 1.4 %collective-permute-start.24 = (bf16[384,256]{1,0:T(8,128)(2,1)S(1)}, bf16[384,256]{1,0:T(8,128)(2,1)S(1)}, u32[]{:S(2)}, u32[]{:S(2)}) collective-permute-start(bf16[384,256]{1,0:T(8,128)(2,1)S(1)} %collective-permute-done.19.refs_20_), channel_id=1, source_target_pairs={{0,1},{1,0},{2,3},{3,2},{4,5},{5,4},{6,7},{7,6},{12,13},{13,12},{1... | collective-permute-start | bytes 589832 | tf_op jit(solution)/shard_map/ppermute | solution.py:67
  65.7 1.7 %collective-permute-start.23 = (bf16[384,256]{1,0:T(8,128)(2,1)S(1)}, bf16[384,256]{1,0:T(8,128)(2,1)S(1)}, u32[]{:S(2)}, u32[]{:S(2)}) collective-permute-start(bf16[384,256]{1,0:T(8,128)(2,1)S(1)} %collective-permute-done.16.refs_18_), channel_id=1, source_target_pairs={{0,1},{1,0},{2,3},{3,2},{4,5},{5,4},{6,7},{7,6},{12,13},{13,12},{1... | collective-permute-start | bytes 589832 | tf_op jit(solution)/shard_map/ppermute | solution.py:67
  66.2 1.5 %collective-permute-start.22 = (bf16[384,256]{1,0:T(8,128)(2,1)S(1)}, bf16[384,256]{1,0:T(8,128)(2,1)S(1)}, u32[]{:S(2)}, u32[]{:S(2)}) collective-permute-start(bf16[384,256]{1,0:T(8,128)(2,1)S(1)} %pad_maximum_fusion.refs_16_), channel_id=1, source_target_pairs={{0,1},{1,0},{2,3},{3,2},{4,5},{5,4},{6,7},{7,6},{12,13},{13,12},{1... | collective-permute-start | bytes 589832 | tf_op jit(solution)/shard_map/ppermute | solution.py:67
  72.3 18.0 %copy-start.3 = (bf16[64,1,2048]{2,0,1:T(8,128)(2,1)S(1)}, bf16[64,1,2048]{2,0,1:T(8,128)(2,1)}, u32[]{:S(2)}) copy-start(bf16[64,1,2048]{2,0,1:T(8,128)(2,1)} %param.9) | copy-start | bytes 786436
  72.9 9.1 %collective-permute-start.29 = (bf16[64,2048]{1,0:T(8,128)(2,1)S(1)}, bf16[64,2048]{1,0:T(8,128)(2,1)S(1)}, u32[]{:S(2)}, u32[]{:S(2)}) collective-permute-start(bf16[64,2048]{1,0:T(8,128)(2,1)S(1)} %add_convert_fusion.2), channel_id=1, source_target_pairs={{0,4},{1,5},{2,6},{3,7},{4,12},{5,13},{6,14},{7,15},{12,8},{13,9},... | collective-permute-start | bytes 786440 | tf_op jit(solution)/shard_map/ppermute | solution.py:55
  73.3 8.7 %collective-permute-start.26 = (bf16[64,2048]{1,0:T(8,128)(2,1)S(1)}, bf16[64,2048]{1,0:T(8,128)(2,1)S(1)}, u32[]{:S(2)}, u32[]{:S(2)}) collective-permute-start(bf16[64,2048]{1,0:T(8,128)(2,1)S(1)} %get-tuple-element.60), channel_id=1, source_target_pairs={{0,2},{1,3},{2,0},{3,1},{4,6},{5,7},{6,4},{7,5},{12,14},{13,15},{1... | collective-permute-start | bytes 786440 | tf_op jit(solution)/shard_map/ppermute | solution.py:63
  82.2 8.1 %collective-permute-start.31 = (bf16[64,2048]{1,0:T(8,128)(2,1)S(1)}, bf16[64,2048]{1,0:T(8,128)(2,1)S(1)}, u32[]{:S(2)}, u32[]{:S(2)}) collective-permute-start(bf16[64,2048]{1,0:T(8,128)(2,1)S(1)} %add_convert_fusion.1), channel_id=1, source_target_pairs={{0,4},{1,5},{2,6},{3,7},{4,12},{5,13},{6,14},{7,15},{12,8},{13,9},... | collective-permute-start | bytes 786440 | tf_op jit(solution)/shard_map/ppermute | solution.py:55
  83.0 7.2 %collective-permute-start.30 = (bf16[64,2048]{1,0:T(8,128)(2,1)S(1)}, bf16[64,2048]{1,0:T(8,128)(2,1)S(1)}, u32[]{:S(2)}, u32[]{:S(2)}) collective-permute-start(bf16[64,2048]{1,0:T(8,128)(2,1)S(1)} %get-tuple-element.58), channel_id=1, source_target_pairs={{0,2},{1,3},{2,0},{3,1},{4,6},{5,7},{6,4},{7,5},{12,14},{13,15},{1... | collective-permute-start | bytes 786440 | tf_op jit(solution)/shard_map/ppermute | solution.py:63

commit v7 on v6

--- a/solution.py
+++ b/solution.py
@@ -78,22 +78,20 @@
     return (line * 2 + y) * 2 + core
 
 
-def pack_kernel(
-    act_ref,
-    gain_ref,
-    ids_ref,
-    gates_ref,
-    key_ref,
-    weight_ref,
-    up_hbm,
-    out_ref,
-    small_ref,
-    up_ref,
-    meta_ref,
-    up_sem,
-):
-    fetch = pltpu.make_async_copy(up_hbm, up_ref, up_sem)
-    fetch.start()
+def pack_kernel(*refs):
+    sources, targets = refs[:7], refs[10:17]
+    out_ref, small_ref, up_ref = refs[7:10]
+    meta_ref, sems = refs[17:]
+    act_ref, gain_ref, ids_ref, gates_ref = targets[:4]
+    copies = [
+        pltpu.make_async_copy(source, target, sems.at[number])
+        for number, (source, target) in enumerate(zip(sources, targets))
+    ]
+    for copy in copies:
+        copy.start()
+    meta_ref[...] = jnp.zeros_like(meta_ref)
+    for copy in copies[:4]:
+        copy.wait()
     width = act_ref.shape[1]
     rows = act_ref.shape[0]
     top = ids_ref.shape[0]
@@ -104,40 +102,48 @@
     high = gates.astype(BF16).astype(F32)
     rest = gates - high
     middle = rest.astype(BF16).astype(F32)
-    meta_ref[...] = jnp.zeros_like(meta_ref)
     meta_ref[0:top, 0:rows] = ids_ref[...].astype(F32)
     meta_ref[8 : 8 + top, 0:rows] = high
     meta_ref[16 : 16 + top, 0:rows] = middle
     meta_ref[24 : 24 + top, 0:rows] = rest - middle
     out_ref[:, width:] = meta_ref[...].T[:rows, :].astype(BF16)
-    small_ref[:rows] = key_ref[...]
-    small_ref[rows:] = weight_ref[...]
-    fetch.wait()
+    for copy in copies[4:]:
+        copy.wait()
+
+
+def in_vmem(*arrays):
+    return [pltpu.with_memory_space_constraint(x, pltpu.VMEM) for x in arrays]
 
 
 def pack(activations, norm_gain, ids, gates, keys, value_weight, w_gate_up):
     rows, width = activations.shape
     small_rows = rows + value_weight.shape[0]
-    from_hbm = pltpu.with_memory_space_constraint(w_gate_up, pltpu.HBM)
     assert rows <= META and ids.shape[0] <= 8
+    operands = (activations, norm_gain.reshape(1, width), ids, gates, keys, value_weight, w_gate_up)
+
+    def kernel(*refs):
+        small_ref, up_ref = refs[8:10]
+        loaded = (*refs[10:14], small_ref.at[pl.ds(0, rows)], small_ref.at[pl.ds(rows, small_rows - rows)], up_ref)
+        pack_kernel(*refs[:10], *loaded, *refs[14:])
+
     return pl.pallas_call(
-        pack_kernel,
+        kernel,
         out_shape=[
             jax.ShapeDtypeStruct((rows, width + META), BF16),
             jax.ShapeDtypeStruct((small_rows, keys.shape[1]), BF16),
             pltpu.VMEM(w_gate_up.shape, BF16),
         ],
-        in_specs=[IN_VMEM] * 6 + [ANY],
+        in_specs=[ANY] * 7,
         out_specs=[IN_VMEM] * 3,
-        scratch_shapes=[pltpu.VMEM((META, META), F32), pltpu.SemaphoreType.DMA(())],
+        scratch_shapes=[
+            *(pltpu.VMEM(x.shape, x.dtype) for x in operands[:4]),
+            pltpu.VMEM((META, META), F32),
+            pltpu.SemaphoreType.DMA((7,)),
+        ],
         compiler_params=pltpu.CompilerParams(vmem_limit_bytes=VMEM_LIMIT),
         cost_estimate=SHORT,
         name="normalize_and_pack",
-    )(activations, norm_gain.reshape(1, width), ids, gates, keys, value_weight, from_hbm)
-
-
-def in_vmem(*arrays):
-    return [pltpu.with_memory_space_constraint(x, pltpu.VMEM) for x in arrays]
+    )(*(pltpu.with_memory_space_constraint(x, pltpu.HBM) for x in operands))
 
 
 def expert_kernel(top, tok_rows, capacity, sources, targets, *refs):
@@ -448,30 +454,37 @@
     rows, width = acts.shape
     line = [packed, forward(packed), None, backward(packed)]
     small_across = across(small)
-    crossed = [across(after(packed, small_across)), across(line[1]), None, across(line[3])]
     pair = jnp.concatenate([small, small_across], axis=0)
-    line[2] = forward(line[1])
+    line, crossed = [packed, forward(packed)], [across(after(packed, small_across))]
+    line.append(None)
+    line.append(backward(after(packed, line[1])))
+    line[2] = forward(after(line[1], line[3]))
+    crossed.append(across(line[1]))
+    crossed.append(None)
+    crossed.append(across(after(line[3], crossed[1])))
+    crossed[2] = across(after(line[2], crossed[3]))
     arrays = [None] * LINE
 
-    def complete(step):
+    def complete(step, crossed_rows):
         arrays[step] = [
             line[step],
-            crossed[step],
+            crossed_rows,
             other_core(line[step]),
-            other_core(crossed[step]),
+            other_core(crossed_rows),
         ]
 
-    for step in (0, 1, 3):
-        complete(step)
     blocks = [
         (4 * step + core * 2 + y, 0, functools.partial(from_device, step, y, core))
         for step in range(LINE)
         for core in range(2)
         for y in range(2)
     ]
-    pair = after(pair, line[3])
-    pairs = [pair, forward(pair), None, backward(pair)]
-    pairs[2] = forward(pairs[1])
+    pair = after(pair, line[2])
+    pairs = [pair, forward(pair), None, None]
+    pairs[3] = backward(after(pair, pairs[1]))
+    for step in (0, 1, 3):
+        complete(step, crossed[step])
+    complete(2, after(crossed[2], pairs[1]))
     small_rows = small.shape[0]
     small_blocks = [
         (2 * step + core, y * small_rows, functools.partial(from_device, step, y, core))
@@ -480,54 +493,47 @@
         for y in range(2)
     ]
 
-    keep, mine, crossing = [None] * LINE, [None] * LINE, [None] * LINE
+    mine, crossing = [None] * LINE, [None] * LINE
 
     def experts(first, second, before, beside):
         ready = arrays[first] + arrays[second]
         ready = [after(ready[0], *before), *ready[1:]]
         sources = [[(4 * group + i, 0, rows) for i in range(4)] for group in range(2)]
-        targets = [[(group, 0, 2 * rows), (2, group * 2 * rows, 2 * rows)] for group in range(2)]
-        keep[first], keep[second], send = run_experts(
-            ready,
-            sources,
-            targets,
-            [2 * rows, 2 * rows, 4 * rows],
-            w_gate_up,
-            w_down,
-            top,
-            rows,
-            capacity,
+        targets = [[(group, 0, 2 * rows), (2 + group, 0, 2 * rows)] for group in range(2)]
+        *keep, send_first, send_second = run_experts(
+            ready, sources, targets, [2 * rows] * 4, w_gate_up, w_down, top, rows, capacity
         )
-        came = other_core(after(send, *beside))
-        for at, step in ((0, first), (2 * rows, second)):
-            mine[step] = (keep[step][:rows], came[at : at + rows])
-            crossing[step] = summed(keep[step][rows:], came[at + rows : at + 2 * rows])
-        return send
+        came = other_core(after(send_first, *beside))
+        mine[first] = (keep[0][:rows], came[:rows])
+        crossing[first] = summed(keep[0][rows:], came[rows:])
+        came = other_core(after(send_second, crossing[first]))
+        mine[second] = (keep[1][:rows], came[:rows])
+        crossing[second] = summed(keep[1][rows:], came[rows:])
+        return send_first
 
     theirs = [None] * LINE
-    crossed[2] = across(line[2])
-    complete(2)
-    send = experts(1, 0, [line[2], pairs[0]], [crossed[3], crossed[2], pairs[1]])
+    experts(1, 0, [line[3]], [crossed[3]])
     theirs[1] = across(crossing[1])
-    send = experts(2, 3, [crossing[0], crossing[1]], [theirs[1], pairs[2], pairs[3]])
+    send = experts(2, 3, [], [theirs[1], pairs[3]])
+    pairs[2] = forward(after(pairs[1], send))
     total = summed(*mine[1], after(theirs[1], send))
     moving = forward(total)
     smalls = []
     for step in range(LINE):
         smalls += [pairs[step], other_core(after(pairs[step], total))]
     theirs[2], theirs[3] = across(crossing[2]), across(crossing[3])
-    new_keys, values = make_values(
-        sum(arrays, []), blocks, smalls, small_blocks, rows, width, crossing[2:]
-    )
-    total = summed(*mine[2], theirs[2], after(moving, values))
+    total = summed(*mine[2], theirs[2], moving)
     moving = forward(total)
     theirs[0] = across(after(crossing[0], total))
-    context = attend_part(after(queries, total), new_keys, values, 0, 4)
-    context = attend_part(queries, new_keys, values, 1, 4, context)
-    total = summed(*mine[3], theirs[3], after(moving, context))
+    new_keys, values = make_values(
+        sum(arrays, []), blocks, smalls, small_blocks, rows, width, [total]
+    )
+    total = summed(*mine[3], theirs[3], after(moving, values))
     moving = forward(total)
-    context = attend_part(after(queries, total), new_keys, values, 2, 4, context)
-    context = attend_part(queries, new_keys, values, 3, 4, context)
+    queries = after(queries, total)
+    context = None
+    for part in range(4):
+        context = attend_part(queries, new_keys, values, part, 4, context)
     layer_out = summed(acts, *mine[0], theirs[0], after(moving, context))
     return context, layer_out
 

time: 91.4 us -> 89 us (0.974)
  local copies, waits for them, and re-layouts: 4.77 us -> 0.02 us
  waiting for transfers between devices: 28.3 us -> 32.1 us
  starting transfers between devices: 32 us -> 30.2 us
    ppermute x14 -> x16, waiting for transfers between devices: 5.06 us -> 0.17 us  [other_core(): return lax.ppermute(x, 'seq', swaps(0, 1))]
    unnamed x18 -> x6, local copies, waits for them, and re-layouts: 4.77 us -> 0.02 us
    ppermute x9, waiting for transfers between devices: 6.85 us -> 11 us  [across(): return lax.ppermute(x, 'seq', swaps(1, 0))]
    ppermute x7, waiting for transfers between devices: 16 us -> 19 us  [forward(): return lax.ppermute(x, 'seq', ring_steps(1))]
    ppermute x2, starting transfers between devices: 4.11 us -> 2.07 us  [backward(): return lax.ppermute(x, 'seq', ring_steps(LINE - 1))]
    ppermute x2, waiting for transfers between devices: 0.37 us -> 1.97 us  [backward(): return lax.ppermute(x, 'seq', ring_steps(LINE - 1))]
    ppermute x14 -> x16, starting transfers between devices: 2.61 us -> 2.63 us  [other_core(): return lax.ppermute(x, 'seq', swaps(0, 1))]
  transfers between devices with their start and end apart: 32 -> 34, of which waited for: 16 -> 14; matrix products, arithmetic and copies ran while one was open for 0% -> 1% of each run, Pallas kernels for 23% -> 24%
where the time goes in v7:
time: 89 us; the launch traced here: 88.9 us
  waiting for transfers between devices  32.1 us (36%)
  starting transfers between devices  30.2 us (34%)
  Pallas kernels  24.2 us (27%)
  other arithmetic  1.51 us (2%)
    ppermute x7, waiting for transfers between devices, forward(): return lax.ppermute(x, 'seq', ring_steps(1))  19 us
    ppermute x7, starting transfers between devices, forward(): return lax.ppermute(x, 'seq', ring_steps(1))  14.8 us
    ppermute x9, waiting for transfers between devices, across(): return lax.ppermute(x, 'seq', swaps(1, 0))  11 us
    ppermute x9, starting transfers between devices, across(): return lax.ppermute(x, 'seq', swaps(1, 0))  10.8 us
    pallas_call x2, Pallas kernels, run_experts(): pl.pallas_call(functools.partial(expert_kernel, top, tok_rows, capacity,...  9.04 us
    pallas_call x4, Pallas kernels, attend_part(): pl.pallas_call(functools.partial(attention_kernel, chunk), grid=(1,), out...  7.34 us
    pallas_call x1, Pallas kernels, make_values(): pl.pallas_call(functools.partial(value_kernel, key_rows, blocks, small_bl...  4.66 us
    pallas_call x1, Pallas kernels, pack(): pl.pallas_call(kernel, out_shape=[jax.ShapeDtypeStruct((rows, width + MET...  3.17 us
  transfers between devices with their start and end apart: 34, of which 14 were waited for; matrix products, arithmetic and copies ran while one was open for 1% of the time, Pallas kernels for 24%

profile of v7, /device:TPU:0, one launch (start us, length us, event | category | flops | bytes accessed | tf_op | source)
XLA Modules:
  0.0 88.9 jit_solution(17899614947120810584)
XLA Ops:
  0.6 3.2 %normalize_and_pack.1 = (bf16[64,2176]{1,0:T(8,128)(2,1)S(1)}, bf16[192,256]{1,0:T(8,128)(2,1)S(1)}, bf16[2048,1536]{1,0:T(8,128)(2,1)S(1)}) custom-call(bf16[64,2048]{1,0:T(8,128)(2,1)} %bitcast.24, f32[1,2048]{1,0:T(1,128)} %bitcast.26, s32[4,64]{1,0:T(4,128)} %bitcast.27, f32[4,64]{1,0:T(4,128)} %bitcast.28, bf16[64,256]{1,0:T(8,128)(2,1)} %bitcast.25, ...), custom_call_target="tpu_custom_call" | custom-call | flops 1 | bytes 1 | tf_op jit(solution)/shard_map/normalize_and_pack/pallas_call | solution.py:129
  3.8 3.1 %collective-permute-start = (bf16[64,2176]{1,0:T(8,128)(2,1)S(1)}, bf16[64,2176]{1,0:T(8,128)(2,1)S(1)}, u32[]{:S(2)}, u32[]{:S(2)}) collective-permute-start(bf16[64,2176]{1,0:T(8,128)(2,1)S(1)} %get-tuple-element.51.refs_4_.refs_0_), channel_id=1, source_target_pairs={{0,4},{1,5},{2,6},{3,7},{4,12},{5,13},{6,14},{7,15},{12,8},{13,9},... | collective-permute-start | bytes 835592 | tf_op jit(solution)/shard_map/ppermute | solution.py:55
  6.9 1.5 %collective-permute-start.6 = (bf16[192,256]{1,0:T(8,128)(2,1)S(1)}, bf16[192,256]{1,0:T(8,128)(2,1)S(1)}, u32[]{:S(2)}, u32[]{:S(2)}) collective-permute-start(bf16[192,256]{1,0:T(8,128)(2,1)S(1)} %get-tuple-element.43), channel_id=1, source_target_pairs={{0,2},{1,3},{2,0},{3,1},{4,6},{5,7},{6,4},{7,5},{12,14},{13,15},{1... | collective-permute-start | bytes 294920 | tf_op jit(solution)/shard_map/ppermute | solution.py:63
  8.4 3.1 %collective-permute-done.6 = bf16[192,256]{1,0:T(8,128)(2,1)S(1)} collective-permute-done((bf16[192,256]{1,0:T(8,128)(2,1)S(1)}, bf16[192,256]{1,0:T(8,128)(2,1)S(1)}, u32[]{:S(2)}, u32[]{:S(2)}) %collective-permute-start.6) | collective-permute-done | bytes 98336 | tf_op jit(solution)/shard_map/ppermute | solution.py:63
  11.5 1.5 %collective-permute-start.14 = (bf16[64,2176]{1,0:T(8,128)(2,1)S(1)}, bf16[64,2176]{1,0:T(8,128)(2,1)S(1)}, u32[]{:S(2)}, u32[]{:S(2)}) collective-permute-start(bf16[64,2176]{1,0:T(8,128)(2,1)S(1)} %get-tuple-element.51.refs_4_.refs_0_), channel_id=1, source_target_pairs={{0,2},{1,3},{2,0},{3,1},{4,6},{5,7},{6,4},{7,5},{12,14},{13,15},{1... | collective-permute-start | bytes 835592 | tf_op jit(solution)/shard_map/ppermute | solution.py:63
  13.0 1.5 %collective-permute-done.refs_0_.refs_4_ = bf16[64,2176]{1,0:T(8,128)(2,1)S(1)} collective-permute-done((bf16[64,2176]{1,0:T(8,128)(2,1)S(1)}, bf16[64,2176]{1,0:T(8,128)(2,1)S(1)}, u32[]{:S(2)}, u32[]{:S(2)}) %collective-permute-start) | collective-permute-done | bytes 278560 | tf_op jit(solution)/shard_map/ppermute | solution.py:55
  14.6 1.6 %collective-permute-start.3 = (bf16[64,2176]{1,0:T(8,128)(2,1)S(1)}, bf16[64,2176]{1,0:T(8,128)(2,1)S(1)}, u32[]{:S(2)}, u32[]{:S(2)}) collective-permute-start(bf16[64,2176]{1,0:T(8,128)(2,1)S(1)} %collective-permute-done.refs_0_.refs_4_), channel_id=1, source_target_pairs={{0,2},{1,3},{2,0},{3,1},{4,6},{5,7},{6,4},{7,5},{12,14},{13,15},{1... | collective-permute-start | bytes 835592 | tf_op jit(solution)/shard_map/ppermute | solution.py:63
  16.1 1.7 %collective-permute-start.1 = (bf16[64,2176]{1,0:T(8,128)(2,1)S(1)}, bf16[64,2176]{1,0:T(8,128)(2,1)S(1)}, u32[]{:S(2)}, u32[]{:S(2)}) collective-permute-start(bf16[64,2176]{1,0:T(8,128)(2,1)S(1)} %get-tuple-element.51.refs_4_.refs_0_), channel_id=1, source_target_pairs={{0,8},{1,9},{2,10},{3,11},{4,0},{5,1},{6,2},{7,3},{12,4},{13,5},{1... | collective-permute-start | bytes 835592 | tf_op jit(solution)/shard_map/ppermute | solution.py:59
  17.8 0.5 collective-permute-start.12
  18.3 2.7 %collective-permute-done.14.refs_5_.refs_1_ = bf16[64,2176]{1,0:T(8,128)(2,1)S(1)} collective-permute-done((bf16[64,2176]{1,0:T(8,128)(2,1)S(1)}, bf16[64,2176]{1,0:T(8,128)(2,1)S(1)}, u32[]{:S(2)}, u32[]{:S(2)}) %collective-permute-start.14) | collective-permute-done | bytes 278560 | tf_op jit(solution)/shard_map/ppermute | solution.py:63
  21.1 0.0 collective-permute-start.16
  21.1 3.7 %collective-permute-done.3.refs_1_.refs_5_ = bf16[64,2176]{1,0:T(8,128)(2,1)S(1)} collective-permute-done((bf16[64,2176]{1,0:T(8,128)(2,1)S(1)}, bf16[64,2176]{1,0:T(8,128)(2,1)S(1)}, u32[]{:S(2)}, u32[]{:S(2)}) %collective-permute-start.3) | collective-permute-done | bytes 278560 | tf_op jit(solution)/shard_map/ppermute | solution.py:63
  24.7 0.0 collective-permute-start.13
  24.8 0.0 collective-permute-done.1.refs_4_.refs_12_
  24.8 1.5 %collective-permute-start.4 = (bf16[64,2176]{1,0:T(8,128)(2,1)S(1)}, bf16[64,2176]{1,0:T(8,128)(2,1)S(1)}, u32[]{:S(2)}, u32[]{:S(2)}) collective-permute-start(bf16[64,2176]{1,0:T(8,128)(2,1)S(1)} %collective-permute-done.1.refs_4_.refs_12_), channel_id=1, source_target_pairs={{0,2},{1,3},{2,0},{3,1},{4,6},{5,7},{6,4},{7,5},{12,14},{13,15},{1... | collective-permute-start | bytes 835592 | tf_op jit(solution)/shard_map/ppermute | solution.py:63
  26.3 0.0 collective-permute-done.15.refs_6_.refs_2_
  26.3 2.6 %collective-permute-start.2 = (bf16[64,2176]{1,0:T(8,128)(2,1)S(1)}, bf16[64,2176]{1,0:T(8,128)(2,1)S(1)}, u32[]{:S(2)}, u32[]{:S(2)}) collective-permute-start(bf16[64,2176]{1,0:T(8,128)(2,1)S(1)} %collective-permute-done.refs_0_.refs_4_), channel_id=1, source_target_pairs={{0,4},{1,5},{2,6},{3,7},{4,12},{5,13},{6,14},{7,15},{12,8},{13,9},... | collective-permute-start | bytes 835592 | tf_op jit(solution)/shard_map/ppermute | solution.py:55
  28.9 4.5 %experts.3 = (bf16[128,2048]{1,0:T(8,128)(2,1)S(1)}, bf16[128,2048]{1,0:T(8,128)(2,1)S(1)}, bf16[128,2048]{1,0:T(8,128)(2,1)S(1)}, bf16[128,2048]{1,0:T(8,128)(2,1)S(1)}) custom-call(bf16[64,2176]{1,0:T(8,128)(2,1)S(1)} %collective-permute-done.refs_0_.refs_4_, bf16[64,2176]{1,0:T(8,128)(2,1)S(1)} %collective-permute-done.3.refs_1_.refs_5_, ...), custom_call_target="tpu_custom_call" | custom-call | flops 1 | bytes 1 | tf_op jit(solution)/shard_map/experts/pallas_call | solution.py:273
  33.4 0.4 collective-permute-done.4.refs_5_.refs_13_
  33.8 0.0 collective-permute-start.17
  33.8 2.1 %collective-permute-done.2.refs_0_.refs_8_ = bf16[64,2176]{1,0:T(8,128)(2,1)S(1)} collective-permute-done((bf16[64,2176]{1,0:T(8,128)(2,1)S(1)}, bf16[64,2176]{1,0:T(8,128)(2,1)S(1)}, u32[]{:S(2)}, u32[]{:S(2)}) %collective-permute-start.2) | collective-permute-done | bytes 278560 | tf_op jit(solution)/shard_map/ppermute | solution.py:55
  36.0 0.5 collective-permute-start.5
  36.5 1.7 %collective-permute-start.7 = (bf16[384,256]{1,0:T(8,128)(2,1)S(1)}, bf16[384,256]{1,0:T(8,128)(2,1)S(1)}, u32[]{:S(2)}, u32[]{:S(2)}) collective-permute-start(bf16[384,256]{1,0:T(8,128)(2,1)S(1)} %pad_maximum_fusion.refs_16_), channel_id=1, source_target_pairs={{0,4},{1,5},{2,6},{3,7},{4,12},{5,13},{6,14},{7,15},{12,8},{13,9},... | collective-permute-start | bytes 589832 | tf_op jit(solution)/shard_map/ppermute | solution.py:55
  38.2 0.0 collective-permute-start.10
  38.2 0.5 collective-permute-start.8
  38.7 4.6 %collective-permute-done.7.refs_18_ = bf16[384,256]{1,0:T(8,128)(2,1)S(1)} collective-permute-done((bf16[384,256]{1,0:T(8,128)(2,1)S(1)}, bf16[384,256]{1,0:T(8,128)(2,1)S(1)}, u32[]{:S(2)}, u32[]{:S(2)}) %collective-permute-start.7) | collective-permute-done | bytes 196640 | tf_op jit(solution)/shard_map/ppermute | solution.py:55
  43.4 0.0 collective-permute-start.11
  43.4 0.6 collective-permute-done.5.refs_1_.refs_9_
  43.9 0.0 collective-permute-start.9
  43.9 0.1 add_convert_fusion.7
  44.0 1.5 %collective-permute-start.18 = (bf16[64,2048]{1,0:T(8,128)(2,1)S(1)}, bf16[64,2048]{1,0:T(8,128)(2,1)S(1)}, u32[]{:S(2)}, u32[]{:S(2)}) collective-permute-start(bf16[64,2048]{1,0:T(8,128)(2,1)S(1)} %add_convert_fusion.7), channel_id=1, source_target_pairs={{0,2},{1,3},{2,0},{3,1},{4,6},{5,7},{6,4},{7,5},{12,14},{13,15},{1... | collective-permute-start | bytes 786440 | tf_op jit(solution)/shard_map/ppermute | solution.py:63
  45.6 0.4 collective-permute-start.19
  45.9 4.5 %experts.2 = (bf16[128,2048]{1,0:T(8,128)(2,1)S(1)}, bf16[128,2048]{1,0:T(8,128)(2,1)S(1)}, bf16[128,2048]{1,0:T(8,128)(2,1)S(1)}, bf16[128,2048]{1,0:T(8,128)(2,1)S(1)}) custom-call(bf16[64,2176]{1,0:T(8,128)(2,1)S(1)} %collective-permute-done.2.refs_0_.refs_8_, bf16[64,2176]{1,0:T(8,128)(2,1)S(1)} %collective-permute-done.5.refs_1_.refs_9_, ...), custom_call_target="tpu_custom_call" | custom-call | flops 1 | bytes 1 | tf_op jit(solution)/shard_map/experts/pallas_call | solution.py:273
  50.5 0.0 copy-start.1
  50.5 2.0 %collective-permute-done.19.refs_22_ = bf16[384,256]{1,0:T(8,128)(2,1)S(1)} collective-permute-done((bf16[384,256]{1,0:T(8,128)(2,1)S(1)}, bf16[384,256]{1,0:T(8,128)(2,1)S(1)}, u32[]{:S(2)}, u32[]{:S(2)}) %collective-permute-start.19) | collective-permute-done | bytes 196640 | tf_op jit(solution)/shard_map/ppermute | solution.py:59
  52.4 0.3 collective-permute-done.18
  52.8 0.1 add_convert_fusion.4
  52.9 2.3 %collective-permute-start.24 = (bf16[64,2048]{1,0:T(8,128)(2,1)S(1)}, bf16[64,2048]{1,0:T(8,128)(2,1)S(1)}, u32[]{:S(2)}, u32[]{:S(2)}) collective-permute-start(bf16[64,2048]{1,0:T(8,128)(2,1)S(1)} %add_convert_fusion.4), channel_id=1, source_target_pairs={{0,4},{1,5},{2,6},{3,7},{4,12},{5,13},{6,14},{7,15},{12,8},{13,9},... | collective-permute-start | bytes 786440 | tf_op jit(solution)/shard_map/ppermute | solution.py:55
  55.3 0.1 add_convert_fusion.6
  55.3 0.8 collective-permute-start.23
  56.2 1.7 %collective-permute-start.28 = (bf16[384,256]{1,0:T(8,128)(2,1)S(1)}, bf16[384,256]{1,0:T(8,128)(2,1)S(1)}, u32[]{:S(2)}, u32[]{:S(2)}) collective-permute-start(bf16[384,256]{1,0:T(8,128)(2,1)S(1)} %collective-permute-done.7.refs_18_), channel_id=1, source_target_pairs={{0,4},{1,5},{2,6},{3,7},{4,12},{5,13},{6,14},{7,15},{12,8},{13,9},... | collective-permute-start | bytes 589832 | tf_op jit(solution)/shard_map/ppermute | solution.py:55
  57.9 0.5 collective-permute-start.31
  58.4 8.4 %collective-permute-done.28.refs_20_ = bf16[384,256]{1,0:T(8,128)(2,1)S(1)} collective-permute-done((bf16[384,256]{1,0:T(8,128)(2,1)S(1)}, bf16[384,256]{1,0:T(8,128)(2,1)S(1)}, u32[]{:S(2)}, u32[]{:S(2)}) %collective-permute-start.28) | collective-permute-done | bytes 196640 | tf_op jit(solution)/shard_map/ppermute | solution.py:55
  66.8 0.5 collective-permute-start.27
  67.3 0.1 collective-permute-start.29
  67.4 0.1 add_convert_fusion.3
  67.5 0.5 collective-permute-start.30
  68.0 0.1 add_convert_fusion.5
  68.1 0.1 collective-permute-done.26.refs_17_
  68.2 1.4 %collective-permute-start.25 = (bf16[64,2048]{1,0:T(8,128)(2,1)S(1)}, bf16[64,2048]{1,0:T(8,128)(2,1)S(1)}, u32[]{:S(2)}, u32[]{:S(2)}) collective-permute-start(bf16[64,2048]{1,0:T(8,128)(2,1)S(1)} %add_convert_fusion.3), channel_id=1, source_target_pairs={{0,4},{1,5},{2,6},{3,7},{4,12},{5,13},{6,14},{7,15},{12,8},{13,9},... | collective-permute-start | bytes 786440 | tf_op jit(solution)/shard_map/ppermute | solution.py:55
  69.6 0.8 collective-permute-start.22
  70.4 0.1 add_convert_fusion.1
  70.5 4.7 %values.1 = (bf16[1024,256]{1,0:T(8,128)(2,1)S(1)}, bf16[1024,256]{1,0:T(8,128)(2,1)S(1)}) custom-call(bf16[64,2176]{1,0:T(8,128)(2,1)S(1)} %get-tuple-element.51.refs_4_.refs_0_, bf16[64,2176]{1,0:T(8,128)(2,1)S(1)} %collective-permute-done.14.refs_5_.refs_1_, bf16[64,2176]{1,0:T(8,128)(2,1)S(1)} %collective-permute-done.15.refs_6_.refs_2_, ...), custom_call_target="tpu_custom_call" | custom-call | flops 1 | bytes 1 | tf_op jit(solution)/shard_map/values/pallas_call | solution.py:341
  75.2 0.0 copy-start.2
  75.2 2.3 %collective-permute-done.25 = bf16[64,2048]{1,0:T(8,128)(2,1)S(1)} collective-permute-done((bf16[64,2048]{1,0:T(8,128)(2,1)S(1)}, bf16[64,2048]{1,0:T(8,128)(2,1)S(1)}, u32[]{:S(2)}, u32[]{:S(2)}) %collective-permute-start.25) | collective-permute-done | bytes 262176 | tf_op jit(solution)/shard_map/ppermute | solution.py:55
  77.5 0.2 collective-permute-done.22
  77.7 0.1 add_convert_fusion.2
  77.8 1.9 %collective-permute-start.33 = (bf16[64,2048]{1,0:T(8,128)(2,1)S(1)}, bf16[64,2048]{1,0:T(8,128)(2,1)S(1)}, u32[]{:S(2)}, u32[]{:S(2)}) collective-permute-start(bf16[64,2048]{1,0:T(8,128)(2,1)S(1)} %add_convert_fusion.2), channel_id=1, source_target_pairs={{0,4},{1,5},{2,6},{3,7},{4,12},{5,13},{6,14},{7,15},{12,8},{13,9},... | collective-permute-start | bytes 786440 | tf_op jit(solution)/shard_map/ppermute | solution.py:55
  79.7 1.0 %collective-permute-start.32 = (bf16[64,2048]{1,0:T(8,128)(2,1)S(1)}, bf16[64,2048]{1,0:T(8,128)(2,1)S(1)}, u32[]{:S(2)}, u32[]{:S(2)}) collective-permute-start(bf16[64,2048]{1,0:T(8,128)(2,1)S(1)} %add_convert_fusion.1), channel_id=1, source_target_pairs={{0,2},{1,3},{2,0},{3,1},{4,6},{5,7},{6,4},{7,5},{12,14},{13,15},{1... | collective-permute-start | bytes 786440 | tf_op jit(solution)/shard_map/ppermute | solution.py:63
  80.7 1.8 %attention.4.refs_0_ = bf16[64,4096]{1,0:T(8,128)(2,1)} custom-call(bf16[64,4096]{1,0:T(8,128)(2,1)S(1)} %bitcast.18, bf16[1024,256]{1,0:T(8,128)(2,1)S(1)} %get-tuple-element.68.k_ref, bf16[1024,256]{1,0:T(8,128)(2,1)S(1)} %get-tuple-element.65.v_ref), custom_call_target="tpu_custom_call" | custom-call | flops 1 | bytes 1 | tf_op jit(solution)/shard_map/attention/pallas_call | solution.py:427
  82.5 1.8 %attention.5.refs_0_ = bf16[64,4096]{1,0:T(8,128)(2,1)} custom-call(bf16[64,4096]{1,0:T(8,128)(2,1)S(1)} %bitcast.19, bf16[1024,256]{1,0:T(8,128)(2,1)S(1)} %get-tuple-element.68.k_ref, bf16[1024,256]{1,0:T(8,128)(2,1)S(1)} %get-tuple-element.65.v_ref, bf16[64,4096]{1,0:T(8,128)(2,1)} %attention.4.refs_0_), custom_call_target="tpu_custom_call", output_to_operand_aliasing={{}: (3, {})} | custom-call | flops 1 | bytes 1 | tf_op jit(solution)/shard_map/attention/pallas_call | solution.py:427
  84.3 1.8 %attention.6.refs_0_ = bf16[64,4096]{1,0:T(8,128)(2,1)} custom-call(bf16[64,4096]{1,0:T(8,128)(2,1)S(1)} %bitcast.20, bf16[1024,256]{1,0:T(8,128)(2,1)S(1)} %get-tuple-element.68.k_ref, bf16[1024,256]{1,0:T(8,128)(2,1)S(1)} %get-tuple-element.65.v_ref, bf16[64,4096]{1,0:T(8,128)(2,1)} %attention.5.refs_0_), custom_call_target="tpu_custom_call", output_to_operand_aliasing={{}: (3, {})} | custom-call | flops 1 | bytes 1 | tf_op jit(solution)/shard_map/attention/pallas_call | solution.py:427
  86.2 1.8 %attention.7 = bf16[64,4096]{1,0:T(8,128)(2,1)} custom-call(bf16[64,4096]{1,0:T(8,128)(2,1)S(1)} %bitcast.21, bf16[1024,256]{1,0:T(8,128)(2,1)S(1)} %get-tuple-element.68.k_ref, bf16[1024,256]{1,0:T(8,128)(2,1)S(1)} %get-tuple-element.65.v_ref, bf16[64,4096]{1,0:T(8,128)(2,1)} %attention.6.refs_0_), custom_call_target="tpu_custom_call", output_to_operand_aliasing={{}: (3, {})} | custom-call | flops 1 | bytes 1 | tf_op jit(solution)/shard_map/attention/pallas_call | solution.py:427
  88.0 0.9 fusion
  (27 shorter events, 0.1 us)
Async XLA Ops:
  0.6 28.3 %copy-start = (bf16[1,768,2048]{2,1,0:T(8,128)(2,1)S(1)}, bf16[1,768,2048]{2,1,0:T(8,128)(2,1)}, u32[]{:S(2)}) copy-start(bf16[1,768,2048]{2,1,0:T(8,128)(2,1)} %param.17) | copy-start | bytes 9437188
  3.8 10.7 %collective-permute-start = (bf16[64,2176]{1,0:T(8,128)(2,1)S(1)}, bf16[64,2176]{1,0:T(8,128)(2,1)S(1)}, u32[]{:S(2)}, u32[]{:S(2)}) collective-permute-start(bf16[64,2176]{1,0:T(8,128)(2,1)S(1)} %get-tuple-element.51.refs_4_.refs_0_), channel_id=1, source_target_pairs={{0,4},{1,5},{2,6},{3,7},{4,12},{5,13},{6,14},{7,15},{12,8},{13,9},... | collective-permute-start | bytes 835592 | tf_op jit(solution)/shard_map/ppermute | solution.py:55
  6.9 4.6 %collective-permute-start.6 = (bf16[192,256]{1,0:T(8,128)(2,1)S(1)}, bf16[192,256]{1,0:T(8,128)(2,1)S(1)}, u32[]{:S(2)}, u32[]{:S(2)}) collective-permute-start(bf16[192,256]{1,0:T(8,128)(2,1)S(1)} %get-tuple-element.43), channel_id=1, source_target_pairs={{0,2},{1,3},{2,0},{3,1},{4,6},{5,7},{6,4},{7,5},{12,14},{13,15},{1... | collective-permute-start | bytes 294920 | tf_op jit(solution)/shard_map/ppermute | solution.py:63
  11.5 9.5 %collective-permute-start.14 = (bf16[64,2176]{1,0:T(8,128)(2,1)S(1)}, bf16[64,2176]{1,0:T(8,128)(2,1)S(1)}, u32[]{:S(2)}, u32[]{:S(2)}) collective-permute-start(bf16[64,2176]{1,0:T(8,128)(2,1)S(1)} %get-tuple-element.51.refs_4_.refs_0_), channel_id=1, source_target_pairs={{0,2},{1,3},{2,0},{3,1},{4,6},{5,7},{6,4},{7,5},{12,14},{13,15},{1... | collective-permute-start | bytes 835592 | tf_op jit(solution)/shard_map/ppermute | solution.py:63
  14.6 10.2 %collective-permute-start.3 = (bf16[64,2176]{1,0:T(8,128)(2,1)S(1)}, bf16[64,2176]{1,0:T(8,128)(2,1)S(1)}, u32[]{:S(2)}, u32[]{:S(2)}) collective-permute-start(bf16[64,2176]{1,0:T(8,128)(2,1)S(1)} %collective-permute-done.refs_0_.refs_4_), channel_id=1, source_target_pairs={{0,2},{1,3},{2,0},{3,1},{4,6},{5,7},{6,4},{7,5},{12,14},{13,15},{1... | collective-permute-start | bytes 835592 | tf_op jit(solution)/shard_map/ppermute | solution.py:63
  16.1 8.6 %collective-permute-start.1 = (bf16[64,2176]{1,0:T(8,128)(2,1)S(1)}, bf16[64,2176]{1,0:T(8,128)(2,1)S(1)}, u32[]{:S(2)}, u32[]{:S(2)}) collective-permute-start(bf16[64,2176]{1,0:T(8,128)(2,1)S(1)} %get-tuple-element.51.refs_4_.refs_0_), channel_id=1, source_target_pairs={{0,8},{1,9},{2,10},{3,11},{4,0},{5,1},{6,2},{7,3},{12,4},{13,5},{1... | collective-permute-start | bytes 835592 | tf_op jit(solution)/shard_map/ppermute | solution.py:59
  17.8 8.4 %collective-permute-start.15 = (bf16[64,2176]{1,0:T(8,128)(2,1)S(1)}, bf16[64,2176]{1,0:T(8,128)(2,1)S(1)}, u32[]{:S(2)}, u32[]{:S(2)}) collective-permute-start(bf16[64,2176]{1,0:T(8,128)(2,1)S(1)} %get-tuple-element.51.refs_4_.refs_0_), channel_id=1, source_target_pairs={{0,1},{1,0},{2,3},{3,2},{4,5},{5,4},{6,7},{7,6},{12,13},{13,12},{1... | collective-permute-start | bytes 835592 | tf_op jit(solution)/shard_map/ppermute | solution.py:67
  17.8 11.0 %collective-permute-start.12 = (bf16[64,2176]{1,0:T(8,128)(2,1)S(1)}, bf16[64,2176]{1,0:T(8,128)(2,1)S(1)}, u32[]{:S(2)}, u32[]{:S(2)}) collective-permute-start(bf16[64,2176]{1,0:T(8,128)(2,1)S(1)} %collective-permute-done.refs_0_.refs_4_), channel_id=1, source_target_pairs={{0,1},{1,0},{2,3},{3,2},{4,5},{5,4},{6,7},{7,6},{12,13},{13,12},{1... | collective-permute-start | bytes 835592 | tf_op jit(solution)/shard_map/ppermute | solution.py:67
  21.1 7.8 %collective-permute-start.16 = (bf16[64,2176]{1,0:T(8,128)(2,1)S(1)}, bf16[64,2176]{1,0:T(8,128)(2,1)S(1)}, u32[]{:S(2)}, u32[]{:S(2)}) collective-permute-start(bf16[64,2176]{1,0:T(8,128)(2,1)S(1)} %collective-permute-done.14.refs_5_.refs_1_), channel_id=1, source_target_pairs={{0,1},{1,0},{2,3},{3,2},{4,5},{5,4},{6,7},{7,6},{12,13},{13,12},{1... | collective-permute-start | bytes 835592 | tf_op jit(solution)/shard_map/ppermute | solution.py:67
  24.7 4.1 %collective-permute-start.13 = (bf16[64,2176]{1,0:T(8,128)(2,1)S(1)}, bf16[64,2176]{1,0:T(8,128)(2,1)S(1)}, u32[]{:S(2)}, u32[]{:S(2)}) collective-permute-start(bf16[64,2176]{1,0:T(8,128)(2,1)S(1)} %collective-permute-done.3.refs_1_.refs_5_), channel_id=1, source_target_pairs={{0,1},{1,0},{2,3},{3,2},{4,5},{5,4},{6,7},{7,6},{12,13},{13,12},{1... | collective-permute-start | bytes 835592 | tf_op jit(solution)/shard_map/ppermute | solution.py:67
  24.8 9.1 %collective-permute-start.4 = (bf16[64,2176]{1,0:T(8,128)(2,1)S(1)}, bf16[64,2176]{1,0:T(8,128)(2,1)S(1)}, u32[]{:S(2)}, u32[]{:S(2)}) collective-permute-start(bf16[64,2176]{1,0:T(8,128)(2,1)S(1)} %collective-permute-done.1.refs_4_.refs_12_), channel_id=1, source_target_pairs={{0,2},{1,3},{2,0},{3,1},{4,6},{5,7},{6,4},{7,5},{12,14},{13,15},{1... | collective-permute-start | bytes 835592 | tf_op jit(solution)/shard_map/ppermute | solution.py:63
  26.3 9.7 %collective-permute-start.2 = (bf16[64,2176]{1,0:T(8,128)(2,1)S(1)}, bf16[64,2176]{1,0:T(8,128)(2,1)S(1)}, u32[]{:S(2)}, u32[]{:S(2)}) collective-permute-start(bf16[64,2176]{1,0:T(8,128)(2,1)S(1)} %collective-permute-done.refs_0_.refs_4_), channel_id=1, source_target_pairs={{0,4},{1,5},{2,6},{3,7},{4,12},{5,13},{6,14},{7,15},{12,8},{13,9},... | collective-permute-start | bytes 835592 | tf_op jit(solution)/shard_map/ppermute | solution.py:55
  33.8 10.1 %collective-permute-start.17 = (bf16[128,2048]{1,0:T(8,128)(2,1)S(1)}, bf16[128,2048]{1,0:T(8,128)(2,1)S(1)}, u32[]{:S(2)}, u32[]{:S(2)}) collective-permute-start(bf16[128,2048]{1,0:T(8,128)(2,1)S(1)} %get-tuple-element.54), channel_id=1, source_target_pairs={{0,1},{1,0},{2,3},{3,2},{4,5},{5,4},{6,7},{7,6},{12,13},{13,12},{1... | collective-permute-start | bytes 1572872 | tf_op jit(solution)/shard_map/ppermute | solution.py:67
  36.0 8.0 %collective-permute-start.5 = (bf16[64,2176]{1,0:T(8,128)(2,1)S(1)}, bf16[64,2176]{1,0:T(8,128)(2,1)S(1)}, u32[]{:S(2)}, u32[]{:S(2)}) collective-permute-start(bf16[64,2176]{1,0:T(8,128)(2,1)S(1)} %collective-permute-done.2.refs_0_.refs_8_), channel_id=1, source_target_pairs={{0,2},{1,3},{2,0},{3,1},{4,6},{5,7},{6,4},{7,5},{12,14},{13,15},{1... | collective-permute-start | bytes 835592 | tf_op jit(solution)/shard_map/ppermute | solution.py:63
  36.5 6.9 %collective-permute-start.7 = (bf16[384,256]{1,0:T(8,128)(2,1)S(1)}, bf16[384,256]{1,0:T(8,128)(2,1)S(1)}, u32[]{:S(2)}, u32[]{:S(2)}) collective-permute-start(bf16[384,256]{1,0:T(8,128)(2,1)S(1)} %pad_maximum_fusion.refs_16_), channel_id=1, source_target_pairs={{0,4},{1,5},{2,6},{3,7},{4,12},{5,13},{6,14},{7,15},{12,8},{13,9},... | collective-permute-start | bytes 589832 | tf_op jit(solution)/shard_map/ppermute | solution.py:55
  38.2 7.3 %collective-permute-start.10 = (bf16[64,2176]{1,0:T(8,128)(2,1)S(1)}, bf16[64,2176]{1,0:T(8,128)(2,1)S(1)}, u32[]{:S(2)}, u32[]{:S(2)}) collective-permute-start(bf16[64,2176]{1,0:T(8,128)(2,1)S(1)} %collective-permute-done.1.refs_4_.refs_12_), channel_id=1, source_target_pairs={{0,1},{1,0},{2,3},{3,2},{4,5},{5,4},{6,7},{7,6},{12,13},{13,12},{1... | collective-permute-start | bytes 835592 | tf_op jit(solution)/shard_map/ppermute | solution.py:67
  38.2 7.7 %collective-permute-start.8 = (bf16[64,2176]{1,0:T(8,128)(2,1)S(1)}, bf16[64,2176]{1,0:T(8,128)(2,1)S(1)}, u32[]{:S(2)}, u32[]{:S(2)}) collective-permute-start(bf16[64,2176]{1,0:T(8,128)(2,1)S(1)} %collective-permute-done.2.refs_0_.refs_8_), channel_id=1, source_target_pairs={{0,1},{1,0},{2,3},{3,2},{4,5},{5,4},{6,7},{7,6},{12,13},{13,12},{1... | collective-permute-start | bytes 835592 | tf_op jit(solution)/shard_map/ppermute | solution.py:67
  43.4 2.6 %collective-permute-start.11 = (bf16[64,2176]{1,0:T(8,128)(2,1)S(1)}, bf16[64,2176]{1,0:T(8,128)(2,1)S(1)}, u32[]{:S(2)}, u32[]{:S(2)}) collective-permute-start(bf16[64,2176]{1,0:T(8,128)(2,1)S(1)} %collective-permute-done.4.refs_5_.refs_13_), channel_id=1, source_target_pairs={{0,1},{1,0},{2,3},{3,2},{4,5},{5,4},{6,7},{7,6},{12,13},{13,12},{1... | collective-permute-start | bytes 835592 | tf_op jit(solution)/shard_map/ppermute | solution.py:67
  43.9 2.0 %collective-permute-start.9 = (bf16[64,2176]{1,0:T(8,128)(2,1)S(1)}, bf16[64,2176]{1,0:T(8,128)(2,1)S(1)}, u32[]{:S(2)}, u32[]{:S(2)}) collective-permute-start(bf16[64,2176]{1,0:T(8,128)(2,1)S(1)} %collective-permute-done.5.refs_1_.refs_9_), channel_id=1, source_target_pairs={{0,1},{1,0},{2,3},{3,2},{4,5},{5,4},{6,7},{7,6},{12,13},{13,12},{1... | collective-permute-start | bytes 835592 | tf_op jit(solution)/shard_map/ppermute | solution.py:67
  44.0 8.8 %collective-permute-start.18 = (bf16[64,2048]{1,0:T(8,128)(2,1)S(1)}, bf16[64,2048]{1,0:T(8,128)(2,1)S(1)}, u32[]{:S(2)}, u32[]{:S(2)}) collective-permute-start(bf16[64,2048]{1,0:T(8,128)(2,1)S(1)} %add_convert_fusion.7), channel_id=1, source_target_pairs={{0,2},{1,3},{2,0},{3,1},{4,6},{5,7},{6,4},{7,5},{12,14},{13,15},{1... | collective-permute-start | bytes 786440 | tf_op jit(solution)/shard_map/ppermute | solution.py:63
  45.6 6.9 %collective-permute-start.19 = (bf16[384,256]{1,0:T(8,128)(2,1)S(1)}, bf16[384,256]{1,0:T(8,128)(2,1)S(1)}, u32[]{:S(2)}, u32[]{:S(2)}) collective-permute-start(bf16[384,256]{1,0:T(8,128)(2,1)S(1)} %pad_maximum_fusion.refs_16_), channel_id=1, source_target_pairs={{0,8},{1,9},{2,10},{3,11},{4,0},{5,1},{6,2},{7,3},{12,4},{13,5},{1... | collective-permute-start | bytes 589832 | tf_op jit(solution)/shard_map/ppermute | solution.py:59
  50.5 30.2 %copy-start.1 = (bf16[64,1,4096]{2,0,1:T(8,128)(2,1)S(1)}, bf16[64,1,4096]{2,0,1:T(8,128)(2,1)}, u32[]{:S(2)}) copy-start(bf16[64,1,4096]{2,0,1:T(8,128)(2,1)} %param.10) | copy-start | bytes 1572868
  52.8 2.5 %collective-permute-start.20 = (bf16[128,2048]{1,0:T(8,128)(2,1)S(1)}, bf16[128,2048]{1,0:T(8,128)(2,1)S(1)}, u32[]{:S(2)}, u32[]{:S(2)}) collective-permute-start(bf16[128,2048]{1,0:T(8,128)(2,1)S(1)} %get-tuple-element.56), channel_id=1, source_target_pairs={{0,1},{1,0},{2,3},{3,2},{4,5},{5,4},{6,7},{7,6},{12,13},{13,12},{1... | collective-permute-start | bytes 1572872 | tf_op jit(solution)/shard_map/ppermute | solution.py:67
  52.9 13.9 %collective-permute-start.24 = (bf16[64,2048]{1,0:T(8,128)(2,1)S(1)}, bf16[64,2048]{1,0:T(8,128)(2,1)S(1)}, u32[]{:S(2)}, u32[]{:S(2)}) collective-permute-start(bf16[64,2048]{1,0:T(8,128)(2,1)S(1)} %add_convert_fusion.4), channel_id=1, source_target_pairs={{0,4},{1,5},{2,6},{3,7},{4,12},{5,13},{6,14},{7,15},{12,8},{13,9},... | collective-permute-start | bytes 786440 | tf_op jit(solution)/shard_map/ppermute | solution.py:55
  55.3 12.0 %collective-permute-start.23 = (bf16[64,2048]{1,0:T(8,128)(2,1)S(1)}, bf16[64,2048]{1,0:T(8,128)(2,1)S(1)}, u32[]{:S(2)}, u32[]{:S(2)}) collective-permute-start(bf16[64,2048]{1,0:T(8,128)(2,1)S(1)} %add_convert_fusion.6), channel_id=1, source_target_pairs={{0,2},{1,3},{2,0},{3,1},{4,6},{5,7},{6,4},{7,5},{12,14},{13,15},{1... | collective-permute-start | bytes 786440 | tf_op jit(solution)/shard_map/ppermute | solution.py:63
  56.2 10.6 %collective-permute-start.28 = (bf16[384,256]{1,0:T(8,128)(2,1)S(1)}, bf16[384,256]{1,0:T(8,128)(2,1)S(1)}, u32[]{:S(2)}, u32[]{:S(2)}) collective-permute-start(bf16[384,256]{1,0:T(8,128)(2,1)S(1)} %collective-permute-done.7.refs_18_), channel_id=1, source_target_pairs={{0,4},{1,5},{2,6},{3,7},{4,12},{5,13},{6,14},{7,15},{12,8},{13,9},... | collective-permute-start | bytes 589832 | tf_op jit(solution)/shard_map/ppermute | solution.py:55
  57.9 9.6 %collective-permute-start.21 = (bf16[128,2048]{1,0:T(8,128)(2,1)S(1)}, bf16[128,2048]{1,0:T(8,128)(2,1)S(1)}, u32[]{:S(2)}, u32[]{:S(2)}) collective-permute-start(bf16[128,2048]{1,0:T(8,128)(2,1)S(1)} %get-tuple-element.57), channel_id=1, source_target_pairs={{0,1},{1,0},{2,3},{3,2},{4,5},{5,4},{6,7},{7,6},{12,13},{13,12},{1... | collective-permute-start | bytes 1572872 | tf_op jit(solution)/shard_map/ppermute | solution.py:67
  57.9 11.7 %collective-permute-start.31 = (bf16[128,2048]{1,0:T(8,128)(2,1)S(1)}, bf16[128,2048]{1,0:T(8,128)(2,1)S(1)}, u32[]{:S(2)}, u32[]{:S(2)}) collective-permute-start(bf16[128,2048]{1,0:T(8,128)(2,1)S(1)} %get-tuple-element.71), channel_id=1, source_target_pairs={{0,1},{1,0},{2,3},{3,2},{4,5},{5,4},{6,7},{7,6},{12,13},{13,12},{1... | collective-permute-start | bytes 1572872 | tf_op jit(solution)/shard_map/ppermute | solution.py:67
  66.8 1.4 %collective-permute-start.26 = (bf16[384,256]{1,0:T(8,128)(2,1)S(1)}, bf16[384,256]{1,0:T(8,128)(2,1)S(1)}, u32[]{:S(2)}, u32[]{:S(2)}) collective-permute-start(bf16[384,256]{1,0:T(8,128)(2,1)S(1)} %pad_maximum_fusion.refs_16_), channel_id=1, source_target_pairs={{0,1},{1,0},{2,3},{3,2},{4,5},{5,4},{6,7},{7,6},{12,13},{13,12},{1... | collective-permute-start | bytes 589832 | tf_op jit(solution)/shard_map/ppermute | solution.py:67
  66.8 3.7 %collective-permute-start.27 = (bf16[384,256]{1,0:T(8,128)(2,1)S(1)}, bf16[384,256]{1,0:T(8,128)(2,1)S(1)}, u32[]{:S(2)}, u32[]{:S(2)}) collective-permute-start(bf16[384,256]{1,0:T(8,128)(2,1)S(1)} %collective-permute-done.7.refs_18_), channel_id=1, source_target_pairs={{0,1},{1,0},{2,3},{3,2},{4,5},{5,4},{6,7},{7,6},{12,13},{13,12},{1... | collective-permute-start | bytes 589832 | tf_op jit(solution)/shard_map/ppermute | solution.py:67
  67.3 3.2 %collective-permute-start.29 = (bf16[384,256]{1,0:T(8,128)(2,1)S(1)}, bf16[384,256]{1,0:T(8,128)(2,1)S(1)}, u32[]{:S(2)}, u32[]{:S(2)}) collective-permute-start(bf16[384,256]{1,0:T(8,128)(2,1)S(1)} %collective-permute-done.28.refs_20_), channel_id=1, source_target_pairs={{0,1},{1,0},{2,3},{3,2},{4,5},{5,4},{6,7},{7,6},{12,13},{13,12},{1... | collective-permute-start | bytes 589832 | tf_op jit(solution)/shard_map/ppermute | solution.py:67
  67.5 3.0 %collective-permute-start.30 = (bf16[384,256]{1,0:T(8,128)(2,1)S(1)}, bf16[384,256]{1,0:T(8,128)(2,1)S(1)}, u32[]{:S(2)}, u32[]{:S(2)}) collective-permute-start(bf16[384,256]{1,0:T(8,128)(2,1)S(1)} %collective-permute-done.19.refs_22_), channel_id=1, source_target_pairs={{0,1},{1,0},{2,3},{3,2},{4,5},{5,4},{6,7},{7,6},{12,13},{13,12},{1... | collective-permute-start | bytes 589832 | tf_op jit(solution)/shard_map/ppermute | solution.py:67
  68.2 9.2 %collective-permute-start.25 = (bf16[64,2048]{1,0:T(8,128)(2,1)S(1)}, bf16[64,2048]{1,0:T(8,128)(2,1)S(1)}, u32[]{:S(2)}, u32[]{:S(2)}) collective-permute-start(bf16[64,2048]{1,0:T(8,128)(2,1)S(1)} %add_convert_fusion.3), channel_id=1, source_target_pairs={{0,4},{1,5},{2,6},{3,7},{4,12},{5,13},{6,14},{7,15},{12,8},{13,9},... | collective-permute-start | bytes 786440 | tf_op jit(solution)/shard_map/ppermute | solution.py:55
  69.6 8.1 %collective-permute-start.22 = (bf16[64,2048]{1,0:T(8,128)(2,1)S(1)}, bf16[64,2048]{1,0:T(8,128)(2,1)S(1)}, u32[]{:S(2)}, u32[]{:S(2)}) collective-permute-start(bf16[64,2048]{1,0:T(8,128)(2,1)S(1)} %add_convert_fusion.5), channel_id=1, source_target_pairs={{0,2},{1,3},{2,0},{3,1},{4,6},{5,7},{6,4},{7,5},{12,14},{13,15},{1... | collective-permute-start | bytes 786440 | tf_op jit(solution)/shard_map/ppermute | solution.py:63
  75.2 12.8 %copy-start.2 = (bf16[64,1,2048]{2,0,1:T(8,128)(2,1)S(1)}, bf16[64,1,2048]{2,0,1:T(8,128)(2,1)}, u32[]{:S(2)}) copy-start(bf16[64,1,2048]{2,0,1:T(8,128)(2,1)} %param.9) | copy-start | bytes 786436
  77.8 10.2 %collective-permute-start.33 = (bf16[64,2048]{1,0:T(8,128)(2,1)S(1)}, bf16[64,2048]{1,0:T(8,128)(2,1)S(1)}, u32[]{:S(2)}, u32[]{:S(2)}) collective-permute-start(bf16[64,2048]{1,0:T(8,128)(2,1)S(1)} %add_convert_fusion.2), channel_id=1, source_target_pairs={{0,4},{1,5},{2,6},{3,7},{4,12},{5,13},{6,14},{7,15},{12,8},{13,9},... | collective-permute-start | bytes 786440 | tf_op jit(solution)/shard_map/ppermute | solution.py:55
  79.7 8.3 %collective-permute-start.32 = (bf16[64,2048]{1,0:T(8,128)(2,1)S(1)}, bf16[64,2048]{1,0:T(8,128)(2,1)S(1)}, u32[]{:S(2)}, u32[]{:S(2)}) collective-permute-start(bf16[64,2048]{1,0:T(8,128)(2,1)S(1)} %add_convert_fusion.1), channel_id=1, source_target_pairs={{0,2},{1,3},{2,0},{3,1},{4,6},{5,7},{6,4},{7,5},{12,14},{13,15},{1... | collective-permute-start | bytes 786440 | tf_op jit(solution)/shard_map/ppermute | solution.py:63

commit v8 on v7

--- a/solution.py
+++ b/solution.py
@@ -452,27 +452,15 @@
 
 def on_line(acts, packed, small, queries, w_gate_up, w_down, top, capacity):
     rows, width = acts.shape
-    line = [packed, forward(packed), None, backward(packed)]
     small_across = across(small)
     pair = jnp.concatenate([small, small_across], axis=0)
-    line, crossed = [packed, forward(packed)], [across(after(packed, small_across))]
-    line.append(None)
-    line.append(backward(after(packed, line[1])))
-    line[2] = forward(after(line[1], line[3]))
-    crossed.append(across(line[1]))
-    crossed.append(None)
-    crossed.append(across(after(line[3], crossed[1])))
-    crossed[2] = across(after(line[2], crossed[3]))
-    arrays = [None] * LINE
-
-    def complete(step, crossed_rows):
-        arrays[step] = [
-            line[step],
-            crossed_rows,
-            other_core(line[step]),
-            other_core(crossed_rows),
-        ]
-
+    line = [packed, forward(packed), None, backward(packed)]
+    line[2] = forward(line[1])
+    crossed = [across(after(packed, small_across)), *map(across, line[1:])]
+    arrays = [
+        [line[step], crossed[step], other_core(line[step]), other_core(crossed[step])]
+        for step in range(LINE)
+    ]
     blocks = [
         (4 * step + core * 2 + y, 0, functools.partial(from_device, step, y, core))
         for step in range(LINE)
@@ -482,9 +470,6 @@
     pair = after(pair, line[2])
     pairs = [pair, forward(pair), None, None]
     pairs[3] = backward(after(pair, pairs[1]))
-    for step in (0, 1, 3):
-        complete(step, crossed[step])
-    complete(2, after(crossed[2], pairs[1]))
     small_rows = small.shape[0]
     small_blocks = [
         (2 * step + core, y * small_rows, functools.partial(from_device, step, y, core))
@@ -493,8 +478,6 @@
         for y in range(2)
     ]
 
-    mine, crossing = [None] * LINE, [None] * LINE
-
     def experts(first, second, before, beside):
         ready = arrays[first] + arrays[second]
         ready = [after(ready[0], *before), *ready[1:]]
@@ -503,38 +486,39 @@
         *keep, send_first, send_second = run_experts(
             ready, sources, targets, [2 * rows] * 4, w_gate_up, w_down, top, rows, capacity
         )
-        came = other_core(after(send_first, *beside))
-        mine[first] = (keep[0][:rows], came[:rows])
-        crossing[first] = summed(keep[0][rows:], came[rows:])
-        came = other_core(after(send_second, crossing[first]))
-        mine[second] = (keep[1][:rows], came[:rows])
-        crossing[second] = summed(keep[1][rows:], came[rows:])
-        return send_first
-
-    theirs = [None] * LINE
-    experts(1, 0, [line[3]], [crossed[3]])
-    theirs[1] = across(crossing[1])
-    send = experts(2, 3, [], [theirs[1], pairs[3]])
+        came_first = other_core(after(send_first, *beside))
+        crossing = summed(keep[0][rows:], came_first[rows:])
+        came_second = other_core(after(send_second, crossing))
+        return keep, (came_first, came_second), send_first
+
+    beside = [crossed[3], crossed[2], pairs[1], arrays[3][2], arrays[2][2]]
+    keep, came, send = experts(1, 0, [line[2]], beside)
+    near = [(keep[i][:rows], came[i][:rows]) for i in range(2)]
+    crossing = [summed(keep[i][rows:], came[i][rows:]) for i in range(2)]
+    theirs_near = across(crossing[0])
+    keep, came, send = experts(2, 3, [crossing[0]], [theirs_near, pairs[3]])
     pairs[2] = forward(after(pairs[1], send))
-    total = summed(*mine[1], after(theirs[1], send))
+    total = summed(*near[0], after(theirs_near, send))
     moving = forward(total)
+    far = [summed(keep[i][rows:], came[i][rows:]) for i in range(2)]
+    theirs = across(far[0])
     smalls = []
     for step in range(LINE):
-        smalls += [pairs[step], other_core(after(pairs[step], total))]
-    theirs[2], theirs[3] = across(crossing[2]), across(crossing[3])
-    total = summed(*mine[2], theirs[2], moving)
+        smalls += [pairs[step], other_core(after(pairs[step], far[0]))]
+    total = summed(keep[0][:rows], came[0][:rows], theirs, moving)
     moving = forward(total)
-    theirs[0] = across(after(crossing[0], total))
     new_keys, values = make_values(
         sum(arrays, []), blocks, smalls, small_blocks, rows, width, [total]
     )
-    total = summed(*mine[3], theirs[3], after(moving, values))
+    theirs = across(after(far[1], theirs))
+    total = summed(keep[1][:rows], came[1][:rows], theirs, after(moving, values))
     moving = forward(total)
+    theirs = across(after(crossing[1], theirs))
     queries = after(queries, total)
     context = None
-    for part in range(4):
-        context = attend_part(queries, new_keys, values, part, 4, context)
-    layer_out = summed(acts, *mine[0], theirs[0], after(moving, context))
+    for number in range(4):
+        context = attend_part(queries, new_keys, values, number, 4, context)
+    layer_out = summed(acts, *near[1], theirs, after(moving, context))
     return context, layer_out
 
 

time: 89 us -> 90.5 us (1.017)
  starting transfers between devices: 30.2 us -> 38.5 us
  waiting for transfers between devices: 32.1 us -> 25.3 us
    ppermute x9, waiting for transfers between devices: 11 us -> 4.18 us  [across(): return lax.ppermute(x, 'seq', swaps(1, 0))]
    ppermute x7, starting transfers between devices: 14.8 us -> 19.4 us  [forward(): return lax.ppermute(x, 'seq', ring_steps(1))]
    ppermute x7, waiting for transfers between devices: 19 us -> 14.7 us  [forward(): return lax.ppermute(x, 'seq', ring_steps(1))]
    ppermute x2, waiting for transfers between devices: 1.97 us -> 5.06 us  [backward(): return lax.ppermute(x, 'seq', ring_steps(LINE - 1))]
    ppermute x2, starting transfers between devices: 2.07 us -> 3.68 us  [backward(): return lax.ppermute(x, 'seq', ring_steps(LINE - 1))]
    ppermute x9, starting transfers between devices: 10.8 us -> 12.3 us  [across(): return lax.ppermute(x, 'seq', swaps(1, 0))]
    ppermute x16, waiting for transfers between devices: 0.17 us -> 1.44 us  [other_core(): return lax.ppermute(x, 'seq', swaps(0, 1))]
  transfers between devices with their start and end apart: 34 -> 34, of which waited for: 14 -> 12; matrix products, arithmetic and copies ran while one was open for 1% -> 1% of each run, Pallas kernels for 24% -> 23%
where the time goes in v8:
time: 90.5 us; the launch traced here: 90.3 us
  starting transfers between devices  38.5 us (43%)
  waiting for transfers between devices  25.3 us (28%)
  Pallas kernels  24.2 us (27%)
  other arithmetic  1.51 us (2%)
    ppermute x7, starting transfers between devices, forward(): return lax.ppermute(x, 'seq', ring_steps(1))  19.4 us
    ppermute x7, waiting for transfers between devices, forward(): return lax.ppermute(x, 'seq', ring_steps(1))  14.7 us
    ppermute x9, starting transfers between devices, across(): return lax.ppermute(x, 'seq', swaps(1, 0))  12.3 us
    pallas_call x2, Pallas kernels, run_experts(): pl.pallas_call(functools.partial(expert_kernel, top, tok_rows, capacity,...  9.01 us
    pallas_call x4, Pallas kernels, attend_part(): pl.pallas_call(functools.partial(attention_kernel, chunk), grid=(1,), out...  7.34 us
    ppermute x2, waiting for transfers between devices, backward(): return lax.ppermute(x, 'seq', ring_steps(LINE - 1))  5.06 us
    pallas_call x1, Pallas kernels, make_values(): pl.pallas_call(functools.partial(value_kernel, key_rows, blocks, small_bl...  4.66 us
    ppermute x9, waiting for transfers between devices, across(): return lax.ppermute(x, 'seq', swaps(1, 0))  4.18 us
  transfers between devices with their start and end apart: 34, of which 12 were waited for; matrix products, arithmetic and copies ran while one was open for 1% of the time, Pallas kernels for 23%

profile of v8, /device:TPU:0, one launch (start us, length us, event | category | flops | bytes accessed | tf_op | source)
XLA Modules:
  0.0 90.3 jit_solution(18086508930423418097)
XLA Ops:
  0.6 3.2 %normalize_and_pack.1 = (bf16[64,2176]{1,0:T(8,128)(2,1)S(1)}, bf16[192,256]{1,0:T(8,128)(2,1)S(1)}, bf16[2048,1536]{1,0:T(8,128)(2,1)S(1)}) custom-call(bf16[64,2048]{1,0:T(8,128)(2,1)} %bitcast.24, f32[1,2048]{1,0:T(1,128)} %bitcast.26, s32[4,64]{1,0:T(4,128)} %bitcast.27, f32[4,64]{1,0:T(4,128)} %bitcast.28, bf16[64,256]{1,0:T(8,128)(2,1)} %bitcast.25, ...), custom_call_target="tpu_custom_call" | custom-call | flops 1 | bytes 1 | tf_op jit(solution)/shard_map/normalize_and_pack/pallas_call | solution.py:129
  3.8 3.1 %collective-permute-start = (bf16[64,2176]{1,0:T(8,128)(2,1)S(1)}, bf16[64,2176]{1,0:T(8,128)(2,1)S(1)}, u32[]{:S(2)}, u32[]{:S(2)}) collective-permute-start(bf16[64,2176]{1,0:T(8,128)(2,1)S(1)} %get-tuple-element.39.refs_4_.refs_0_), channel_id=1, source_target_pairs={{0,4},{1,5},{2,6},{3,7},{4,12},{5,13},{6,14},{7,15},{12,8},{13,9},... | collective-permute-start | bytes 835592 | tf_op jit(solution)/shard_map/ppermute | solution.py:55
  6.9 1.5 %collective-permute-start.5 = (bf16[192,256]{1,0:T(8,128)(2,1)S(1)}, bf16[192,256]{1,0:T(8,128)(2,1)S(1)}, u32[]{:S(2)}, u32[]{:S(2)}) collective-permute-start(bf16[192,256]{1,0:T(8,128)(2,1)S(1)} %get-tuple-element.38), channel_id=1, source_target_pairs={{0,2},{1,3},{2,0},{3,1},{4,6},{5,7},{6,4},{7,5},{12,14},{13,15},{1... | collective-permute-start | bytes 294920 | tf_op jit(solution)/shard_map/ppermute | solution.py:63
  8.4 1.3 %collective-permute-start.9 = (bf16[64,2176]{1,0:T(8,128)(2,1)S(1)}, bf16[64,2176]{1,0:T(8,128)(2,1)S(1)}, u32[]{:S(2)}, u32[]{:S(2)}) collective-permute-start(bf16[64,2176]{1,0:T(8,128)(2,1)S(1)} %get-tuple-element.39.refs_4_.refs_0_), channel_id=1, source_target_pairs={{0,8},{1,9},{2,10},{3,11},{4,0},{5,1},{6,2},{7,3},{12,4},{13,5},{1... | collective-permute-start | bytes 835592 | tf_op jit(solution)/shard_map/ppermute | solution.py:59
  9.8 1.7 %collective-permute-done.5 = bf16[192,256]{1,0:T(8,128)(2,1)S(1)} collective-permute-done((bf16[192,256]{1,0:T(8,128)(2,1)S(1)}, bf16[192,256]{1,0:T(8,128)(2,1)S(1)}, u32[]{:S(2)}, u32[]{:S(2)}) %collective-permute-start.5) | collective-permute-done | bytes 98336 | tf_op jit(solution)/shard_map/ppermute | solution.py:63
  11.5 1.5 %collective-permute-start.6 = (bf16[64,2176]{1,0:T(8,128)(2,1)S(1)}, bf16[64,2176]{1,0:T(8,128)(2,1)S(1)}, u32[]{:S(2)}, u32[]{:S(2)}) collective-permute-start(bf16[64,2176]{1,0:T(8,128)(2,1)S(1)} %get-tuple-element.39.refs_4_.refs_0_), channel_id=1, source_target_pairs={{0,2},{1,3},{2,0},{3,1},{4,6},{5,7},{6,4},{7,5},{12,14},{13,15},{1... | collective-permute-start | bytes 835592 | tf_op jit(solution)/shard_map/ppermute | solution.py:63
  13.0 1.6 %collective-permute-done.refs_0_.refs_4_ = bf16[64,2176]{1,0:T(8,128)(2,1)S(1)} collective-permute-done((bf16[64,2176]{1,0:T(8,128)(2,1)S(1)}, bf16[64,2176]{1,0:T(8,128)(2,1)S(1)}, u32[]{:S(2)}, u32[]{:S(2)}) %collective-permute-start) | collective-permute-done | bytes 278560 | tf_op jit(solution)/shard_map/ppermute | solution.py:55
  14.7 1.6 %collective-permute-start.2 = (bf16[64,2176]{1,0:T(8,128)(2,1)S(1)}, bf16[64,2176]{1,0:T(8,128)(2,1)S(1)}, u32[]{:S(2)}, u32[]{:S(2)}) collective-permute-start(bf16[64,2176]{1,0:T(8,128)(2,1)S(1)} %collective-permute-done.refs_0_.refs_4_), channel_id=1, source_target_pairs={{0,2},{1,3},{2,0},{3,1},{4,6},{5,7},{6,4},{7,5},{12,14},{13,15},{1... | collective-permute-start | bytes 835592 | tf_op jit(solution)/shard_map/ppermute | solution.py:63
  16.2 0.0 collective-permute-start.7
  16.3 0.5 collective-permute-start.3
  16.8 3.8 %collective-permute-done.9.refs_4_.refs_12_ = bf16[64,2176]{1,0:T(8,128)(2,1)S(1)} collective-permute-done((bf16[64,2176]{1,0:T(8,128)(2,1)S(1)}, bf16[64,2176]{1,0:T(8,128)(2,1)S(1)}, u32[]{:S(2)}, u32[]{:S(2)}) %collective-permute-start.9) | collective-permute-done | bytes 278560 | tf_op jit(solution)/shard_map/ppermute | solution.py:59
  20.5 2.9 %collective-permute-start.1 = (bf16[64,2176]{1,0:T(8,128)(2,1)S(1)}, bf16[64,2176]{1,0:T(8,128)(2,1)S(1)}, u32[]{:S(2)}, u32[]{:S(2)}) collective-permute-start(bf16[64,2176]{1,0:T(8,128)(2,1)S(1)} %collective-permute-done.refs_0_.refs_4_), channel_id=1, source_target_pairs={{0,4},{1,5},{2,6},{3,7},{4,12},{5,13},{6,14},{7,15},{12,8},{13,9},... | collective-permute-start | bytes 835592 | tf_op jit(solution)/shard_map/ppermute | solution.py:55
  23.5 0.0 collective-permute-done.6.refs_5_.refs_1_
  23.5 0.0 collective-permute-start.8
  23.5 1.3 %collective-permute-done.2.refs_1_.refs_5_ = bf16[64,2176]{1,0:T(8,128)(2,1)S(1)} collective-permute-done((bf16[64,2176]{1,0:T(8,128)(2,1)S(1)}, bf16[64,2176]{1,0:T(8,128)(2,1)S(1)}, u32[]{:S(2)}, u32[]{:S(2)}) %collective-permute-start.2) | collective-permute-done | bytes 278560 | tf_op jit(solution)/shard_map/ppermute | solution.py:63
  24.7 0.0 collective-permute-start.4
  24.8 0.5 collective-permute-start.13
  25.3 1.5 %collective-permute-start.10 = (bf16[64,2176]{1,0:T(8,128)(2,1)S(1)}, bf16[64,2176]{1,0:T(8,128)(2,1)S(1)}, u32[]{:S(2)}, u32[]{:S(2)}) collective-permute-start(bf16[64,2176]{1,0:T(8,128)(2,1)S(1)} %collective-permute-done.9.refs_4_.refs_12_), channel_id=1, source_target_pairs={{0,2},{1,3},{2,0},{3,1},{4,6},{5,7},{6,4},{7,5},{12,14},{13,15},{1... | collective-permute-start | bytes 835592 | tf_op jit(solution)/shard_map/ppermute | solution.py:63
  26.8 3.2 %collective-permute-done.1.refs_0_.refs_8_ = bf16[64,2176]{1,0:T(8,128)(2,1)S(1)} collective-permute-done((bf16[64,2176]{1,0:T(8,128)(2,1)S(1)}, bf16[64,2176]{1,0:T(8,128)(2,1)S(1)}, u32[]{:S(2)}, u32[]{:S(2)}) %collective-permute-start.1) | collective-permute-done | bytes 278560 | tf_op jit(solution)/shard_map/ppermute | solution.py:55
  30.0 0.0 collective-permute-start.14
  30.0 0.0 collective-permute-done.8.refs_7_.refs_3_
  30.0 1.6 %collective-permute-start.11 = (bf16[64,2176]{1,0:T(8,128)(2,1)S(1)}, bf16[64,2176]{1,0:T(8,128)(2,1)S(1)}, u32[]{:S(2)}, u32[]{:S(2)}) collective-permute-start(bf16[64,2176]{1,0:T(8,128)(2,1)S(1)} %collective-permute-done.1.refs_0_.refs_8_), channel_id=1, source_target_pairs={{0,2},{1,3},{2,0},{3,1},{4,6},{5,7},{6,4},{7,5},{12,14},{13,15},{1... | collective-permute-start | bytes 835592 | tf_op jit(solution)/shard_map/ppermute | solution.py:63
  31.6 0.0 collective-permute-done.4.refs_3_.refs_7_
  31.6 1.9 %collective-permute-start.12 = (bf16[384,256]{1,0:T(8,128)(2,1)S(1)}, bf16[384,256]{1,0:T(8,128)(2,1)S(1)}, u32[]{:S(2)}, u32[]{:S(2)}) collective-permute-start(bf16[384,256]{1,0:T(8,128)(2,1)S(1)} %pad_maximum_fusion.refs_16_), channel_id=1, source_target_pairs={{0,4},{1,5},{2,6},{3,7},{4,12},{5,13},{6,14},{7,15},{12,8},{13,9},... | collective-permute-start | bytes 589832 | tf_op jit(solution)/shard_map/ppermute | solution.py:55
  33.5 4.5 %experts.2 = (bf16[128,2048]{1,0:T(8,128)(2,1)S(1)}, bf16[128,2048]{1,0:T(8,128)(2,1)S(1)}, bf16[128,2048]{1,0:T(8,128)(2,1)S(1)}, bf16[128,2048]{1,0:T(8,128)(2,1)S(1)}) custom-call(bf16[64,2176]{1,0:T(8,128)(2,1)S(1)} %collective-permute-done.refs_0_.refs_4_, bf16[64,2176]{1,0:T(8,128)(2,1)S(1)} %collective-permute-done.2.refs_1_.refs_5_, ...), custom_call_target="tpu_custom_call" | custom-call | flops 1 | bytes 1 | tf_op jit(solution)/shard_map/experts/pallas_call | solution.py:273
  38.0 0.0 collective-permute-done.10.refs_5_.refs_13_
  38.0 1.6 %collective-permute-done.12.refs_18_ = bf16[384,256]{1,0:T(8,128)(2,1)S(1)} collective-permute-done((bf16[384,256]{1,0:T(8,128)(2,1)S(1)}, bf16[384,256]{1,0:T(8,128)(2,1)S(1)}, u32[]{:S(2)}, u32[]{:S(2)}) %collective-permute-start.12) | collective-permute-done | bytes 196640 | tf_op jit(solution)/shard_map/ppermute | solution.py:55
  39.6 0.3 collective-permute-done.11.refs_1_.refs_9_
  39.9 0.5 collective-permute-start.17
  40.4 0.0 collective-permute-start.16
  40.4 1.4 %collective-permute-done.15 = bf16[128,2048]{1,0:T(8,128)(2,1)S(1)} collective-permute-done((bf16[128,2048]{1,0:T(8,128)(2,1)S(1)}, bf16[128,2048]{1,0:T(8,128)(2,1)S(1)}, u32[]{:S(2)}, u32[]{:S(2)}) %collective-permute-start.15) | collective-permute-done | bytes 524320 | tf_op jit(solution)/shard_map/ppermute | solution.py:67
  41.8 0.1 add_convert_fusion.7
  41.8 1.6 %collective-permute-start.18 = (bf16[64,2048]{1,0:T(8,128)(2,1)S(1)}, bf16[64,2048]{1,0:T(8,128)(2,1)S(1)}, u32[]{:S(2)}, u32[]{:S(2)}) collective-permute-start(bf16[64,2048]{1,0:T(8,128)(2,1)S(1)} %add_convert_fusion.7), channel_id=1, source_target_pairs={{0,2},{1,3},{2,0},{3,1},{4,6},{5,7},{6,4},{7,5},{12,14},{13,15},{1... | collective-permute-start | bytes 786440 | tf_op jit(solution)/shard_map/ppermute | solution.py:63
  43.4 2.3 %collective-permute-start.19 = (bf16[384,256]{1,0:T(8,128)(2,1)S(1)}, bf16[384,256]{1,0:T(8,128)(2,1)S(1)}, u32[]{:S(2)}, u32[]{:S(2)}) collective-permute-start(bf16[384,256]{1,0:T(8,128)(2,1)S(1)} %pad_maximum_fusion.refs_16_), channel_id=1, source_target_pairs={{0,8},{1,9},{2,10},{3,11},{4,0},{5,1},{6,2},{7,3},{12,4},{13,5},{1... | collective-permute-start | bytes 589832 | tf_op jit(solution)/shard_map/ppermute | solution.py:59
  45.8 4.5 %experts.3 = (bf16[128,2048]{1,0:T(8,128)(2,1)S(1)}, bf16[128,2048]{1,0:T(8,128)(2,1)S(1)}, bf16[128,2048]{1,0:T(8,128)(2,1)S(1)}, bf16[128,2048]{1,0:T(8,128)(2,1)S(1)}) custom-call(bf16[64,2176]{1,0:T(8,128)(2,1)S(1)} %collective-permute-done.1.refs_0_.refs_8_, bf16[64,2176]{1,0:T(8,128)(2,1)S(1)} %collective-permute-done.11.refs_1_.refs_9_, ...), custom_call_target="tpu_custom_call" | custom-call | flops 1 | bytes 1 | tf_op jit(solution)/shard_map/experts/pallas_call | solution.py:273
  50.3 0.0 copy-start.1
  50.3 1.3 %collective-permute-done.19.refs_22_ = bf16[384,256]{1,0:T(8,128)(2,1)S(1)} collective-permute-done((bf16[384,256]{1,0:T(8,128)(2,1)S(1)}, bf16[384,256]{1,0:T(8,128)(2,1)S(1)}, u32[]{:S(2)}, u32[]{:S(2)}) %collective-permute-start.19) | collective-permute-done | bytes 196640 | tf_op jit(solution)/shard_map/ppermute | solution.py:59
  51.6 0.1 add_convert_fusion.4
  51.7 3.4 %collective-permute-start.24 = (bf16[64,2048]{1,0:T(8,128)(2,1)S(1)}, bf16[64,2048]{1,0:T(8,128)(2,1)S(1)}, u32[]{:S(2)}, u32[]{:S(2)}) collective-permute-start(bf16[64,2048]{1,0:T(8,128)(2,1)S(1)} %add_convert_fusion.4), channel_id=1, source_target_pairs={{0,4},{1,5},{2,6},{3,7},{4,12},{5,13},{6,14},{7,15},{12,8},{13,9},... | collective-permute-start | bytes 786440 | tf_op jit(solution)/shard_map/ppermute | solution.py:55
  55.1 0.1 add_convert_fusion.6
  55.2 0.6 collective-permute-start.22
  55.8 2.9 %collective-permute-start.28 = (bf16[384,256]{1,0:T(8,128)(2,1)S(1)}, bf16[384,256]{1,0:T(8,128)(2,1)S(1)}, u32[]{:S(2)}, u32[]{:S(2)}) collective-permute-start(bf16[384,256]{1,0:T(8,128)(2,1)S(1)} %collective-permute-done.12.refs_18_), channel_id=1, source_target_pairs={{0,4},{1,5},{2,6},{3,7},{4,12},{5,13},{6,14},{7,15},{12,8},{13,9},... | collective-permute-start | bytes 589832 | tf_op jit(solution)/shard_map/ppermute | solution.py:55
  58.7 0.5 collective-permute-start.31
  59.2 6.8 %collective-permute-done.28.refs_20_ = bf16[384,256]{1,0:T(8,128)(2,1)S(1)} collective-permute-done((bf16[384,256]{1,0:T(8,128)(2,1)S(1)}, bf16[384,256]{1,0:T(8,128)(2,1)S(1)}, u32[]{:S(2)}, u32[]{:S(2)}) %collective-permute-start.28) | collective-permute-done | bytes 196640 | tf_op jit(solution)/shard_map/ppermute | solution.py:55
  66.0 0.5 collective-permute-start.27
  66.5 0.1 collective-permute-start.29
  66.6 0.1 add_convert_fusion.3
  66.7 0.5 collective-permute-start.30
  67.2 0.1 add_convert_fusion.5
  67.3 2.1 %collective-permute-start.25 = (bf16[64,2048]{1,0:T(8,128)(2,1)S(1)}, bf16[64,2048]{1,0:T(8,128)(2,1)S(1)}, u32[]{:S(2)}, u32[]{:S(2)}) collective-permute-start(bf16[64,2048]{1,0:T(8,128)(2,1)S(1)} %add_convert_fusion.3), channel_id=1, source_target_pairs={{0,4},{1,5},{2,6},{3,7},{4,12},{5,13},{6,14},{7,15},{12,8},{13,9},... | collective-permute-start | bytes 786440 | tf_op jit(solution)/shard_map/ppermute | solution.py:55
  69.4 0.9 %collective-permute-start.23 = (bf16[64,2048]{1,0:T(8,128)(2,1)S(1)}, bf16[64,2048]{1,0:T(8,128)(2,1)S(1)}, u32[]{:S(2)}, u32[]{:S(2)}) collective-permute-start(bf16[64,2048]{1,0:T(8,128)(2,1)S(1)} %add_convert_fusion.5), channel_id=1, source_target_pairs={{0,2},{1,3},{2,0},{3,1},{4,6},{5,7},{6,4},{7,5},{12,14},{13,15},{1... | collective-permute-start | bytes 786440 | tf_op jit(solution)/shard_map/ppermute | solution.py:63
  70.4 0.1 add_convert_fusion.1
  70.5 4.7 %values.1 = (bf16[1024,256]{1,0:T(8,128)(2,1)S(1)}, bf16[1024,256]{1,0:T(8,128)(2,1)S(1)}) custom-call(bf16[64,2176]{1,0:T(8,128)(2,1)S(1)} %get-tuple-element.39.refs_4_.refs_0_, bf16[64,2176]{1,0:T(8,128)(2,1)S(1)} %collective-permute-done.6.refs_5_.refs_1_, bf16[64,2176]{1,0:T(8,128)(2,1)S(1)} %collective-permute-done.7.refs_6_.refs_2_, ...), custom_call_target="tpu_custom_call" | custom-call | flops 1 | bytes 1 | tf_op jit(solution)/shard_map/values/pallas_call | solution.py:341
  75.1 0.0 copy-start.2
  75.1 1.4 %collective-permute-done.25 = bf16[64,2048]{1,0:T(8,128)(2,1)S(1)} collective-permute-done((bf16[64,2048]{1,0:T(8,128)(2,1)S(1)}, bf16[64,2048]{1,0:T(8,128)(2,1)S(1)}, u32[]{:S(2)}, u32[]{:S(2)}) %collective-permute-start.25) | collective-permute-done | bytes 262176 | tf_op jit(solution)/shard_map/ppermute | solution.py:55
  76.6 0.9 collective-permute-done.23
  77.4 0.1 add_convert_fusion.2
  77.6 3.0 %collective-permute-start.33 = (bf16[64,2048]{1,0:T(8,128)(2,1)S(1)}, bf16[64,2048]{1,0:T(8,128)(2,1)S(1)}, u32[]{:S(2)}, u32[]{:S(2)}) collective-permute-start(bf16[64,2048]{1,0:T(8,128)(2,1)S(1)} %add_convert_fusion.2), channel_id=1, source_target_pairs={{0,4},{1,5},{2,6},{3,7},{4,12},{5,13},{6,14},{7,15},{12,8},{13,9},... | collective-permute-start | bytes 786440 | tf_op jit(solution)/shard_map/ppermute | solution.py:55
  80.6 1.5 %collective-permute-start.32 = (bf16[64,2048]{1,0:T(8,128)(2,1)S(1)}, bf16[64,2048]{1,0:T(8,128)(2,1)S(1)}, u32[]{:S(2)}, u32[]{:S(2)}) collective-permute-start(bf16[64,2048]{1,0:T(8,128)(2,1)S(1)} %add_convert_fusion.1), channel_id=1, source_target_pairs={{0,2},{1,3},{2,0},{3,1},{4,6},{5,7},{6,4},{7,5},{12,14},{13,15},{1... | collective-permute-start | bytes 786440 | tf_op jit(solution)/shard_map/ppermute | solution.py:63
  82.1 1.8 %attention.4.refs_0_ = bf16[64,4096]{1,0:T(8,128)(2,1)} custom-call(bf16[64,4096]{1,0:T(8,128)(2,1)S(1)} %bitcast.18, bf16[1024,256]{1,0:T(8,128)(2,1)S(1)} %get-tuple-element.64.k_ref, bf16[1024,256]{1,0:T(8,128)(2,1)S(1)} %get-tuple-element.61.v_ref), custom_call_target="tpu_custom_call" | custom-call | flops 1 | bytes 1 | tf_op jit(solution)/shard_map/attention/pallas_call | solution.py:427
  84.0 1.8 %attention.5.refs_0_ = bf16[64,4096]{1,0:T(8,128)(2,1)} custom-call(bf16[64,4096]{1,0:T(8,128)(2,1)S(1)} %bitcast.19, bf16[1024,256]{1,0:T(8,128)(2,1)S(1)} %get-tuple-element.64.k_ref, bf16[1024,256]{1,0:T(8,128)(2,1)S(1)} %get-tuple-element.61.v_ref, bf16[64,4096]{1,0:T(8,128)(2,1)} %attention.4.refs_0_), custom_call_target="tpu_custom_call", output_to_operand_aliasing={{}: (3, {})} | custom-call | flops 1 | bytes 1 | tf_op jit(solution)/shard_map/attention/pallas_call | solution.py:427
  85.8 1.8 %attention.6.refs_0_ = bf16[64,4096]{1,0:T(8,128)(2,1)} custom-call(bf16[64,4096]{1,0:T(8,128)(2,1)S(1)} %bitcast.20, bf16[1024,256]{1,0:T(8,128)(2,1)S(1)} %get-tuple-element.64.k_ref, bf16[1024,256]{1,0:T(8,128)(2,1)S(1)} %get-tuple-element.61.v_ref, bf16[64,4096]{1,0:T(8,128)(2,1)} %attention.5.refs_0_), custom_call_target="tpu_custom_call", output_to_operand_aliasing={{}: (3, {})} | custom-call | flops 1 | bytes 1 | tf_op jit(solution)/shard_map/attention/pallas_call | solution.py:427
  87.6 1.8 %attention.7 = bf16[64,4096]{1,0:T(8,128)(2,1)} custom-call(bf16[64,4096]{1,0:T(8,128)(2,1)S(1)} %bitcast.21, bf16[1024,256]{1,0:T(8,128)(2,1)S(1)} %get-tuple-element.64.k_ref, bf16[1024,256]{1,0:T(8,128)(2,1)S(1)} %get-tuple-element.61.v_ref, bf16[64,4096]{1,0:T(8,128)(2,1)} %attention.6.refs_0_), custom_call_target="tpu_custom_call", output_to_operand_aliasing={{}: (3, {})} | custom-call | flops 1 | bytes 1 | tf_op jit(solution)/shard_map/attention/pallas_call | solution.py:427
  89.5 0.9 fusion
  (27 shorter events, 0.1 us)
Async XLA Ops:
  0.6 32.9 %copy-start = (bf16[1,768,2048]{2,1,0:T(8,128)(2,1)S(1)}, bf16[1,768,2048]{2,1,0:T(8,128)(2,1)}, u32[]{:S(2)}) copy-start(bf16[1,768,2048]{2,1,0:T(8,128)(2,1)} %param.17) | copy-start | bytes 9437188
  3.8 10.8 %collective-permute-start = (bf16[64,2176]{1,0:T(8,128)(2,1)S(1)}, bf16[64,2176]{1,0:T(8,128)(2,1)S(1)}, u32[]{:S(2)}, u32[]{:S(2)}) collective-permute-start(bf16[64,2176]{1,0:T(8,128)(2,1)S(1)} %get-tuple-element.39.refs_4_.refs_0_), channel_id=1, source_target_pairs={{0,4},{1,5},{2,6},{3,7},{4,12},{5,13},{6,14},{7,15},{12,8},{13,9},... | collective-permute-start | bytes 835592 | tf_op jit(solution)/shard_map/ppermute | solution.py:55
  6.9 4.6 %collective-permute-start.5 = (bf16[192,256]{1,0:T(8,128)(2,1)S(1)}, bf16[192,256]{1,0:T(8,128)(2,1)S(1)}, u32[]{:S(2)}, u32[]{:S(2)}) collective-permute-start(bf16[192,256]{1,0:T(8,128)(2,1)S(1)} %get-tuple-element.38), channel_id=1, source_target_pairs={{0,2},{1,3},{2,0},{3,1},{4,6},{5,7},{6,4},{7,5},{12,14},{13,15},{1... | collective-permute-start | bytes 294920 | tf_op jit(solution)/shard_map/ppermute | solution.py:63
  8.4 12.1 %collective-permute-start.9 = (bf16[64,2176]{1,0:T(8,128)(2,1)S(1)}, bf16[64,2176]{1,0:T(8,128)(2,1)S(1)}, u32[]{:S(2)}, u32[]{:S(2)}) collective-permute-start(bf16[64,2176]{1,0:T(8,128)(2,1)S(1)} %get-tuple-element.39.refs_4_.refs_0_), channel_id=1, source_target_pairs={{0,8},{1,9},{2,10},{3,11},{4,0},{5,1},{6,2},{7,3},{12,4},{13,5},{1... | collective-permute-start | bytes 835592 | tf_op jit(solution)/shard_map/ppermute | solution.py:59
  11.5 11.9 %collective-permute-start.6 = (bf16[64,2176]{1,0:T(8,128)(2,1)S(1)}, bf16[64,2176]{1,0:T(8,128)(2,1)S(1)}, u32[]{:S(2)}, u32[]{:S(2)}) collective-permute-start(bf16[64,2176]{1,0:T(8,128)(2,1)S(1)} %get-tuple-element.39.refs_4_.refs_0_), channel_id=1, source_target_pairs={{0,2},{1,3},{2,0},{3,1},{4,6},{5,7},{6,4},{7,5},{12,14},{13,15},{1... | collective-permute-start | bytes 835592 | tf_op jit(solution)/shard_map/ppermute | solution.py:63
  14.7 10.1 %collective-permute-start.2 = (bf16[64,2176]{1,0:T(8,128)(2,1)S(1)}, bf16[64,2176]{1,0:T(8,128)(2,1)S(1)}, u32[]{:S(2)}, u32[]{:S(2)}) collective-permute-start(bf16[64,2176]{1,0:T(8,128)(2,1)S(1)} %collective-permute-done.refs_0_.refs_4_), channel_id=1, source_target_pairs={{0,2},{1,3},{2,0},{3,1},{4,6},{5,7},{6,4},{7,5},{12,14},{13,15},{1... | collective-permute-start | bytes 835592 | tf_op jit(solution)/shard_map/ppermute | solution.py:63
  16.2 8.5 %collective-permute-start.7 = (bf16[64,2176]{1,0:T(8,128)(2,1)S(1)}, bf16[64,2176]{1,0:T(8,128)(2,1)S(1)}, u32[]{:S(2)}, u32[]{:S(2)}) collective-permute-start(bf16[64,2176]{1,0:T(8,128)(2,1)S(1)} %get-tuple-element.39.refs_4_.refs_0_), channel_id=1, source_target_pairs={{0,1},{1,0},{2,3},{3,2},{4,5},{5,4},{6,7},{7,6},{12,13},{13,12},{1... | collective-permute-start | bytes 835592 | tf_op jit(solution)/shard_map/ppermute | solution.py:67
  16.3 9.0 %collective-permute-start.3 = (bf16[64,2176]{1,0:T(8,128)(2,1)S(1)}, bf16[64,2176]{1,0:T(8,128)(2,1)S(1)}, u32[]{:S(2)}, u32[]{:S(2)}) collective-permute-start(bf16[64,2176]{1,0:T(8,128)(2,1)S(1)} %collective-permute-done.refs_0_.refs_4_), channel_id=1, source_target_pairs={{0,1},{1,0},{2,3},{3,2},{4,5},{5,4},{6,7},{7,6},{12,13},{13,12},{1... | collective-permute-start | bytes 835592 | tf_op jit(solution)/shard_map/ppermute | solution.py:67
  20.5 9.5 %collective-permute-start.1 = (bf16[64,2176]{1,0:T(8,128)(2,1)S(1)}, bf16[64,2176]{1,0:T(8,128)(2,1)S(1)}, u32[]{:S(2)}, u32[]{:S(2)}) collective-permute-start(bf16[64,2176]{1,0:T(8,128)(2,1)S(1)} %collective-permute-done.refs_0_.refs_4_), channel_id=1, source_target_pairs={{0,4},{1,5},{2,6},{3,7},{4,12},{5,13},{6,14},{7,15},{12,8},{13,9},... | collective-permute-start | bytes 835592 | tf_op jit(solution)/shard_map/ppermute | solution.py:55
  23.5 6.6 %collective-permute-start.8 = (bf16[64,2176]{1,0:T(8,128)(2,1)S(1)}, bf16[64,2176]{1,0:T(8,128)(2,1)S(1)}, u32[]{:S(2)}, u32[]{:S(2)}) collective-permute-start(bf16[64,2176]{1,0:T(8,128)(2,1)S(1)} %collective-permute-done.6.refs_5_.refs_1_), channel_id=1, source_target_pairs={{0,1},{1,0},{2,3},{3,2},{4,5},{5,4},{6,7},{7,6},{12,13},{13,12},{1... | collective-permute-start | bytes 835592 | tf_op jit(solution)/shard_map/ppermute | solution.py:67
  24.7 6.9 %collective-permute-start.4 = (bf16[64,2176]{1,0:T(8,128)(2,1)S(1)}, bf16[64,2176]{1,0:T(8,128)(2,1)S(1)}, u32[]{:S(2)}, u32[]{:S(2)}) collective-permute-start(bf16[64,2176]{1,0:T(8,128)(2,1)S(1)} %collective-permute-done.2.refs_1_.refs_5_), channel_id=1, source_target_pairs={{0,1},{1,0},{2,3},{3,2},{4,5},{5,4},{6,7},{7,6},{12,13},{13,12},{1... | collective-permute-start | bytes 835592 | tf_op jit(solution)/shard_map/ppermute | solution.py:67
  24.8 13.3 %collective-permute-start.13 = (bf16[64,2176]{1,0:T(8,128)(2,1)S(1)}, bf16[64,2176]{1,0:T(8,128)(2,1)S(1)}, u32[]{:S(2)}, u32[]{:S(2)}) collective-permute-start(bf16[64,2176]{1,0:T(8,128)(2,1)S(1)} %collective-permute-done.9.refs_4_.refs_12_), channel_id=1, source_target_pairs={{0,1},{1,0},{2,3},{3,2},{4,5},{5,4},{6,7},{7,6},{12,13},{13,12},{1... | collective-permute-start | bytes 835592 | tf_op jit(solution)/shard_map/ppermute | solution.py:67
  25.3 12.8 %collective-permute-start.10 = (bf16[64,2176]{1,0:T(8,128)(2,1)S(1)}, bf16[64,2176]{1,0:T(8,128)(2,1)S(1)}, u32[]{:S(2)}, u32[]{:S(2)}) collective-permute-start(bf16[64,2176]{1,0:T(8,128)(2,1)S(1)} %collective-permute-done.9.refs_4_.refs_12_), channel_id=1, source_target_pairs={{0,2},{1,3},{2,0},{3,1},{4,6},{5,7},{6,4},{7,5},{12,14},{13,15},{1... | collective-permute-start | bytes 835592 | tf_op jit(solution)/shard_map/ppermute | solution.py:63
  30.0 9.6 %collective-permute-start.14 = (bf16[64,2176]{1,0:T(8,128)(2,1)S(1)}, bf16[64,2176]{1,0:T(8,128)(2,1)S(1)}, u32[]{:S(2)}, u32[]{:S(2)}) collective-permute-start(bf16[64,2176]{1,0:T(8,128)(2,1)S(1)} %collective-permute-done.1.refs_0_.refs_8_), channel_id=1, source_target_pairs={{0,1},{1,0},{2,3},{3,2},{4,5},{5,4},{6,7},{7,6},{12,13},{13,12},{1... | collective-permute-start | bytes 835592 | tf_op jit(solution)/shard_map/ppermute | solution.py:67
  30.0 9.8 %collective-permute-start.11 = (bf16[64,2176]{1,0:T(8,128)(2,1)S(1)}, bf16[64,2176]{1,0:T(8,128)(2,1)S(1)}, u32[]{:S(2)}, u32[]{:S(2)}) collective-permute-start(bf16[64,2176]{1,0:T(8,128)(2,1)S(1)} %collective-permute-done.1.refs_0_.refs_8_), channel_id=1, source_target_pairs={{0,2},{1,3},{2,0},{3,1},{4,6},{5,7},{6,4},{7,5},{12,14},{13,15},{1... | collective-permute-start | bytes 835592 | tf_op jit(solution)/shard_map/ppermute | solution.py:63
  31.6 8.0 %collective-permute-start.12 = (bf16[384,256]{1,0:T(8,128)(2,1)S(1)}, bf16[384,256]{1,0:T(8,128)(2,1)S(1)}, u32[]{:S(2)}, u32[]{:S(2)}) collective-permute-start(bf16[384,256]{1,0:T(8,128)(2,1)S(1)} %pad_maximum_fusion.refs_16_), channel_id=1, source_target_pairs={{0,4},{1,5},{2,6},{3,7},{4,12},{5,13},{6,14},{7,15},{12,8},{13,9},... | collective-permute-start | bytes 589832 | tf_op jit(solution)/shard_map/ppermute | solution.py:55
  39.9 1.9 %collective-permute-start.15 = (bf16[128,2048]{1,0:T(8,128)(2,1)S(1)}, bf16[128,2048]{1,0:T(8,128)(2,1)S(1)}, u32[]{:S(2)}, u32[]{:S(2)}) collective-permute-start(bf16[128,2048]{1,0:T(8,128)(2,1)S(1)} %get-tuple-element.44), channel_id=1, source_target_pairs={{0,1},{1,0},{2,3},{3,2},{4,5},{5,4},{6,7},{7,6},{12,13},{13,12},{1... | collective-permute-start | bytes 1572872 | tf_op jit(solution)/shard_map/ppermute | solution.py:67
  39.9 5.9 %collective-permute-start.17 = (bf16[64,2176]{1,0:T(8,128)(2,1)S(1)}, bf16[64,2176]{1,0:T(8,128)(2,1)S(1)}, u32[]{:S(2)}, u32[]{:S(2)}) collective-permute-start(bf16[64,2176]{1,0:T(8,128)(2,1)S(1)} %collective-permute-done.10.refs_5_.refs_13_), channel_id=1, source_target_pairs={{0,1},{1,0},{2,3},{3,2},{4,5},{5,4},{6,7},{7,6},{12,13},{13,12},{1... | collective-permute-start | bytes 835592 | tf_op jit(solution)/shard_map/ppermute | solution.py:67
  40.4 5.4 %collective-permute-start.16 = (bf16[64,2176]{1,0:T(8,128)(2,1)S(1)}, bf16[64,2176]{1,0:T(8,128)(2,1)S(1)}, u32[]{:S(2)}, u32[]{:S(2)}) collective-permute-start(bf16[64,2176]{1,0:T(8,128)(2,1)S(1)} %collective-permute-done.11.refs_1_.refs_9_), channel_id=1, source_target_pairs={{0,1},{1,0},{2,3},{3,2},{4,5},{5,4},{6,7},{7,6},{12,13},{13,12},{1... | collective-permute-start | bytes 835592 | tf_op jit(solution)/shard_map/ppermute | solution.py:67
  41.8 9.7 %collective-permute-start.18 = (bf16[64,2048]{1,0:T(8,128)(2,1)S(1)}, bf16[64,2048]{1,0:T(8,128)(2,1)S(1)}, u32[]{:S(2)}, u32[]{:S(2)}) collective-permute-start(bf16[64,2048]{1,0:T(8,128)(2,1)S(1)} %add_convert_fusion.7), channel_id=1, source_target_pairs={{0,2},{1,3},{2,0},{3,1},{4,6},{5,7},{6,4},{7,5},{12,14},{13,15},{1... | collective-permute-start | bytes 786440 | tf_op jit(solution)/shard_map/ppermute | solution.py:63
  43.4 8.1 %collective-permute-start.19 = (bf16[384,256]{1,0:T(8,128)(2,1)S(1)}, bf16[384,256]{1,0:T(8,128)(2,1)S(1)}, u32[]{:S(2)}, u32[]{:S(2)}) collective-permute-start(bf16[384,256]{1,0:T(8,128)(2,1)S(1)} %pad_maximum_fusion.refs_16_), channel_id=1, source_target_pairs={{0,8},{1,9},{2,10},{3,11},{4,0},{5,1},{6,2},{7,3},{12,4},{13,5},{1... | collective-permute-start | bytes 589832 | tf_op jit(solution)/shard_map/ppermute | solution.py:59
  50.3 31.8 %copy-start.1 = (bf16[64,1,4096]{2,0,1:T(8,128)(2,1)S(1)}, bf16[64,1,4096]{2,0,1:T(8,128)(2,1)}, u32[]{:S(2)}) copy-start(bf16[64,1,4096]{2,0,1:T(8,128)(2,1)} %param.10) | copy-start | bytes 1572868
  51.6 3.5 %collective-permute-start.20 = (bf16[128,2048]{1,0:T(8,128)(2,1)S(1)}, bf16[128,2048]{1,0:T(8,128)(2,1)S(1)}, u32[]{:S(2)}, u32[]{:S(2)}) collective-permute-start(bf16[128,2048]{1,0:T(8,128)(2,1)S(1)} %get-tuple-element.51), channel_id=1, source_target_pairs={{0,1},{1,0},{2,3},{3,2},{4,5},{5,4},{6,7},{7,6},{12,13},{13,12},{1... | collective-permute-start | bytes 1572872 | tf_op jit(solution)/shard_map/ppermute | solution.py:67
  51.7 14.3 %collective-permute-start.24 = (bf16[64,2048]{1,0:T(8,128)(2,1)S(1)}, bf16[64,2048]{1,0:T(8,128)(2,1)S(1)}, u32[]{:S(2)}, u32[]{:S(2)}) collective-permute-start(bf16[64,2048]{1,0:T(8,128)(2,1)S(1)} %add_convert_fusion.4), channel_id=1, source_target_pairs={{0,4},{1,5},{2,6},{3,7},{4,12},{5,13},{6,14},{7,15},{12,8},{13,9},... | collective-permute-start | bytes 786440 | tf_op jit(solution)/shard_map/ppermute | solution.py:55
  55.2 11.3 %collective-permute-start.22 = (bf16[64,2048]{1,0:T(8,128)(2,1)S(1)}, bf16[64,2048]{1,0:T(8,128)(2,1)S(1)}, u32[]{:S(2)}, u32[]{:S(2)}) collective-permute-start(bf16[64,2048]{1,0:T(8,128)(2,1)S(1)} %add_convert_fusion.6), channel_id=1, source_target_pairs={{0,2},{1,3},{2,0},{3,1},{4,6},{5,7},{6,4},{7,5},{12,14},{13,15},{1... | collective-permute-start | bytes 786440 | tf_op jit(solution)/shard_map/ppermute | solution.py:63
  55.8 10.2 %collective-permute-start.28 = (bf16[384,256]{1,0:T(8,128)(2,1)S(1)}, bf16[384,256]{1,0:T(8,128)(2,1)S(1)}, u32[]{:S(2)}, u32[]{:S(2)}) collective-permute-start(bf16[384,256]{1,0:T(8,128)(2,1)S(1)} %collective-permute-done.12.refs_18_), channel_id=1, source_target_pairs={{0,4},{1,5},{2,6},{3,7},{4,12},{5,13},{6,14},{7,15},{12,8},{13,9},... | collective-permute-start | bytes 589832 | tf_op jit(solution)/shard_map/ppermute | solution.py:55
  58.7 8.1 %collective-permute-start.21 = (bf16[128,2048]{1,0:T(8,128)(2,1)S(1)}, bf16[128,2048]{1,0:T(8,128)(2,1)S(1)}, u32[]{:S(2)}, u32[]{:S(2)}) collective-permute-start(bf16[128,2048]{1,0:T(8,128)(2,1)S(1)} %get-tuple-element.52), channel_id=1, source_target_pairs={{0,1},{1,0},{2,3},{3,2},{4,5},{5,4},{6,7},{7,6},{12,13},{13,12},{1... | collective-permute-start | bytes 1572872 | tf_op jit(solution)/shard_map/ppermute | solution.py:67
  58.7 8.6 %collective-permute-start.31 = (bf16[128,2048]{1,0:T(8,128)(2,1)S(1)}, bf16[128,2048]{1,0:T(8,128)(2,1)S(1)}, u32[]{:S(2)}, u32[]{:S(2)}) collective-permute-start(bf16[128,2048]{1,0:T(8,128)(2,1)S(1)} %get-tuple-element.67), channel_id=1, source_target_pairs={{0,1},{1,0},{2,3},{3,2},{4,5},{5,4},{6,7},{7,6},{12,13},{13,12},{1... | collective-permute-start | bytes 1572872 | tf_op jit(solution)/shard_map/ppermute | solution.py:67
  66.0 3.4 %collective-permute-start.26 = (bf16[384,256]{1,0:T(8,128)(2,1)S(1)}, bf16[384,256]{1,0:T(8,128)(2,1)S(1)}, u32[]{:S(2)}, u32[]{:S(2)}) collective-permute-start(bf16[384,256]{1,0:T(8,128)(2,1)S(1)} %pad_maximum_fusion.refs_16_), channel_id=1, source_target_pairs={{0,1},{1,0},{2,3},{3,2},{4,5},{5,4},{6,7},{7,6},{12,13},{13,12},{1... | collective-permute-start | bytes 589832 | tf_op jit(solution)/shard_map/ppermute | solution.py:67
  66.0 4.4 %collective-permute-start.27 = (bf16[384,256]{1,0:T(8,128)(2,1)S(1)}, bf16[384,256]{1,0:T(8,128)(2,1)S(1)}, u32[]{:S(2)}, u32[]{:S(2)}) collective-permute-start(bf16[384,256]{1,0:T(8,128)(2,1)S(1)} %collective-permute-done.12.refs_18_), channel_id=1, source_target_pairs={{0,1},{1,0},{2,3},{3,2},{4,5},{5,4},{6,7},{7,6},{12,13},{13,12},{1... | collective-permute-start | bytes 589832 | tf_op jit(solution)/shard_map/ppermute | solution.py:67
  66.5 3.9 %collective-permute-start.29 = (bf16[384,256]{1,0:T(8,128)(2,1)S(1)}, bf16[384,256]{1,0:T(8,128)(2,1)S(1)}, u32[]{:S(2)}, u32[]{:S(2)}) collective-permute-start(bf16[384,256]{1,0:T(8,128)(2,1)S(1)} %collective-permute-done.28.refs_20_), channel_id=1, source_target_pairs={{0,1},{1,0},{2,3},{3,2},{4,5},{5,4},{6,7},{7,6},{12,13},{13,12},{1... | collective-permute-start | bytes 589832 | tf_op jit(solution)/shard_map/ppermute | solution.py:67
  66.7 3.7 %collective-permute-start.30 = (bf16[384,256]{1,0:T(8,128)(2,1)S(1)}, bf16[384,256]{1,0:T(8,128)(2,1)S(1)}, u32[]{:S(2)}, u32[]{:S(2)}) collective-permute-start(bf16[384,256]{1,0:T(8,128)(2,1)S(1)} %collective-permute-done.19.refs_22_), channel_id=1, source_target_pairs={{0,1},{1,0},{2,3},{3,2},{4,5},{5,4},{6,7},{7,6},{12,13},{13,12},{1... | collective-permute-start | bytes 589832 | tf_op jit(solution)/shard_map/ppermute | solution.py:67
  67.3 9.2 %collective-permute-start.25 = (bf16[64,2048]{1,0:T(8,128)(2,1)S(1)}, bf16[64,2048]{1,0:T(8,128)(2,1)S(1)}, u32[]{:S(2)}, u32[]{:S(2)}) collective-permute-start(bf16[64,2048]{1,0:T(8,128)(2,1)S(1)} %add_convert_fusion.3), channel_id=1, source_target_pairs={{0,4},{1,5},{2,6},{3,7},{4,12},{5,13},{6,14},{7,15},{12,8},{13,9},... | collective-permute-start | bytes 786440 | tf_op jit(solution)/shard_map/ppermute | solution.py:55
  69.4 8.0 %collective-permute-start.23 = (bf16[64,2048]{1,0:T(8,128)(2,1)S(1)}, bf16[64,2048]{1,0:T(8,128)(2,1)S(1)}, u32[]{:S(2)}, u32[]{:S(2)}) collective-permute-start(bf16[64,2048]{1,0:T(8,128)(2,1)S(1)} %add_convert_fusion.5), channel_id=1, source_target_pairs={{0,2},{1,3},{2,0},{3,1},{4,6},{5,7},{6,4},{7,5},{12,14},{13,15},{1... | collective-permute-start | bytes 786440 | tf_op jit(solution)/shard_map/ppermute | solution.py:63
  75.1 14.3 %copy-start.2 = (bf16[64,1,2048]{2,0,1:T(8,128)(2,1)S(1)}, bf16[64,1,2048]{2,0,1:T(8,128)(2,1)}, u32[]{:S(2)}) copy-start(bf16[64,1,2048]{2,0,1:T(8,128)(2,1)} %param.9) | copy-start | bytes 786436
  77.6 11.9 %collective-permute-start.33 = (bf16[64,2048]{1,0:T(8,128)(2,1)S(1)}, bf16[64,2048]{1,0:T(8,128)(2,1)S(1)}, u32[]{:S(2)}, u32[]{:S(2)}) collective-permute-start(bf16[64,2048]{1,0:T(8,128)(2,1)S(1)} %add_convert_fusion.2), channel_id=1, source_target_pairs={{0,4},{1,5},{2,6},{3,7},{4,12},{5,13},{6,14},{7,15},{12,8},{13,9},... | collective-permute-start | bytes 786440 | tf_op jit(solution)/shard_map/ppermute | solution.py:55
  80.6 8.9 %collective-permute-start.32 = (bf16[64,2048]{1,0:T(8,128)(2,1)S(1)}, bf16[64,2048]{1,0:T(8,128)(2,1)S(1)}, u32[]{:S(2)}, u32[]{:S(2)}) collective-permute-start(bf16[64,2048]{1,0:T(8,128)(2,1)S(1)} %add_convert_fusion.1), channel_id=1, source_target_pairs={{0,2},{1,3},{2,0},{3,1},{4,6},{5,7},{6,4},{7,5},{12,14},{13,15},{1... | collective-permute-start | bytes 786440 | tf_op jit(solution)/shard_map/ppermute | solution.py:63

commit v9 on v8

--- a/solution.py
+++ b/solution.py
@@ -78,23 +78,33 @@
     return (line * 2 + y) * 2 + core
 
 
-def pack_kernel(*refs):
-    sources, targets = refs[:7], refs[10:17]
-    out_ref, small_ref, up_ref = refs[7:10]
-    meta_ref, sems = refs[17:]
-    act_ref, gain_ref, ids_ref, gates_ref = targets[:4]
+def pack_kernel(act_hbm, gain_hbm, ids_hbm, gates_hbm, up_hbm, *refs):
+    *extra, out_ref, up_ref, act_ref, gain_ref, ids_ref, gates_ref, meta_ref, sems = refs
+    rows, width = act_ref.shape
+    top = ids_ref.shape[0]
+    pairs = [
+        (act_hbm, act_ref),
+        (gain_hbm, gain_ref),
+        (ids_hbm, ids_ref),
+        (gates_hbm, gates_ref),
+        (up_hbm, up_ref),
+    ]
+    at = width + META
+    for source in extra:
+        for first in range(0, source.shape[0], rows):
+            pairs.append(
+                (source.at[pl.ds(first, rows)], out_ref.at[:, pl.ds(at, source.shape[1])])
+            )
+            at += source.shape[1]
     copies = [
         pltpu.make_async_copy(source, target, sems.at[number])
-        for number, (source, target) in enumerate(zip(sources, targets))
+        for number, (source, target) in enumerate(pairs)
     ]
     for copy in copies:
         copy.start()
     meta_ref[...] = jnp.zeros_like(meta_ref)
     for copy in copies[:4]:
         copy.wait()
-    width = act_ref.shape[1]
-    rows = act_ref.shape[0]
-    top = ids_ref.shape[0]
     features = act_ref[...].astype(F32)
     inverse = lax.rsqrt(jnp.mean(features * features, axis=-1, keepdims=True) + 1e-06)
     out_ref[:, :width] = (features * inverse * gain_ref[...]).astype(BF16)
@@ -106,44 +116,37 @@
     meta_ref[8 : 8 + top, 0:rows] = high
     meta_ref[16 : 16 + top, 0:rows] = middle
     meta_ref[24 : 24 + top, 0:rows] = rest - middle
-    out_ref[:, width:] = meta_ref[...].T[:rows, :].astype(BF16)
+    out_ref[:, width : width + META] = meta_ref[...].T[:rows, :].astype(BF16)
     for copy in copies[4:]:
         copy.wait()
 
 
-def in_vmem(*arrays):
-    return [pltpu.with_memory_space_constraint(x, pltpu.VMEM) for x in arrays]
-
-
-def pack(activations, norm_gain, ids, gates, keys, value_weight, w_gate_up):
+def pack(activations, norm_gain, ids, gates, w_gate_up, *extra):
     rows, width = activations.shape
-    small_rows = rows + value_weight.shape[0]
     assert rows <= META and ids.shape[0] <= 8
-    operands = (activations, norm_gain.reshape(1, width), ids, gates, keys, value_weight, w_gate_up)
-
-    def kernel(*refs):
-        small_ref, up_ref = refs[8:10]
-        loaded = (*refs[10:14], small_ref.at[pl.ds(0, rows)], small_ref.at[pl.ds(rows, small_rows - rows)], up_ref)
-        pack_kernel(*refs[:10], *loaded, *refs[14:])
-
+    operands = (activations, norm_gain.reshape(1, width), ids, gates, w_gate_up, *extra)
+    columns = width + META + sum(x.shape[0] // rows * x.shape[1] for x in extra)
     return pl.pallas_call(
-        kernel,
+        pack_kernel,
         out_shape=[
-            jax.ShapeDtypeStruct((rows, width + META), BF16),
-            jax.ShapeDtypeStruct((small_rows, keys.shape[1]), BF16),
+            jax.ShapeDtypeStruct((rows, columns), BF16),
             pltpu.VMEM(w_gate_up.shape, BF16),
         ],
-        in_specs=[ANY] * 7,
-        out_specs=[IN_VMEM] * 3,
+        in_specs=[ANY] * len(operands),
+        out_specs=[IN_VMEM] * 2,
         scratch_shapes=[
             *(pltpu.VMEM(x.shape, x.dtype) for x in operands[:4]),
             pltpu.VMEM((META, META), F32),
-            pltpu.SemaphoreType.DMA((7,)),
+            pltpu.SemaphoreType.DMA((5 + sum(x.shape[0] // rows for x in extra),)),
         ],
         compiler_params=pltpu.CompilerParams(vmem_limit_bytes=VMEM_LIMIT),
         cost_estimate=SHORT,
         name="normalize_and_pack",
     )(*(pltpu.with_memory_space_constraint(x, pltpu.HBM) for x in operands))
+
+
+def in_vmem(*arrays):
+    return [pltpu.with_memory_space_constraint(x, pltpu.VMEM) for x in arrays]
 
 
 def expert_kernel(top, tok_rows, capacity, sources, targets, *refs):
@@ -176,7 +179,7 @@
         for number, (operand, first, count) in enumerate(sources[group]):
             copies.append(
                 pltpu.make_async_copy(
-                    x_hbm[operand].at[pl.ds(first, count)],
+                    x_hbm[operand].at[pl.ds(first, count), pl.ds(0, packed)],
                     x_buf.at[group, pl.ds(at, count)],
                     x_sem.at[group, number],
                 )
@@ -261,10 +264,9 @@
 def run_experts(arrays, sources, targets, out_rows, w_gate_up, w_down, top, tok_rows, capacity):
     groups = len(sources)
     rows = sum(count for _, _, count in sources[0])
-    packed = arrays[0].shape[1]
     total = groups * rows
-    width = packed - META
-    units = w_down.shape[0]
+    units, width = w_down.shape
+    packed = width + META
     slots = rows // tok_rows * capacity
     assert slots % 16 == 0 and slots <= META and units % 256 == 0 and width % 512 == 0
     all_slots = groups * slots
@@ -293,39 +295,29 @@
     )(*arrays, w_gate_up, w_down)
 
 
-def value_kernel(key_rows, blocks, small_blocks, *refs):
-    inputs = 1 + max(b[0] for b in blocks)
-    smalls = 1 + max(b[0] for b in small_blocks)
-    x_hbm = refs[:inputs]
-    small_hbm = refs[inputs : inputs + smalls]
-    key_ref, value_ref, x_buf, weight, sems = refs[inputs + smalls :]
+def value_kernel(kv_width, devices, *refs):
+    x_hbm = refs[: len(devices)]
+    key_ref, value_ref, x_buf, weight, sems = refs[len(devices) :]
+    rows = x_hbm[0].shape[0]
     width = x_buf.shape[1]
-    weight_rows = width // len(small_blocks)
+    weight_rows = width // len(devices)
     copies = []
-    for number, (operand, first, device) in enumerate(blocks):
-        copies.append(
-            pltpu.make_async_copy(
-                x_hbm[operand].at[pl.ds(first, key_rows), pl.ds(0, width)],
-                x_buf.at[pl.ds(device() * key_rows, key_rows)],
-                sems.at[0, number],
+    for number, device in enumerate(devices):
+        place = device()
+        block = x_hbm[number]
+        pairs = [
+            (block.at[:, pl.ds(0, width)], x_buf.at[pl.ds(place * rows, rows)]),
+            (block.at[:, pl.ds(width + META, kv_width)], key_ref.at[pl.ds(place * rows, rows)]),
+        ]
+        for part in range(weight_rows // rows):
+            pairs.append(
+                (
+                    block.at[:, pl.ds(width + META + (1 + part) * kv_width, kv_width)],
+                    weight.at[pl.ds(place * weight_rows + part * rows, rows)],
+                )
             )
-        )
-    for number, (operand, first, device) in enumerate(small_blocks):
-        place = device()
-        copies.append(
-            pltpu.make_async_copy(
-                small_hbm[operand].at[pl.ds(first, key_rows)],
-                key_ref.at[pl.ds(place * key_rows, key_rows)],
-                sems.at[1, number],
-            )
-        )
-        copies.append(
-            pltpu.make_async_copy(
-                small_hbm[operand].at[pl.ds(first + key_rows, weight_rows)],
-                weight.at[pl.ds(place * weight_rows, weight_rows)],
-                sems.at[2, number],
-            )
-        )
+        for kind, (source, target) in enumerate(pairs):
+            copies.append(pltpu.make_async_copy(source, target, sems.at[kind, number]))
     for copy in copies:
         copy.start()
     for copy in copies:
@@ -333,25 +325,25 @@
     value_ref[...] = dot(x_buf[...], weight[...]).astype(BF16)
 
 
-def make_values(arrays, blocks, smalls, small_blocks, key_rows, width, earlier):
-    smalls = [after(smalls[0], *earlier), *smalls[1:]]
-    kv_width = smalls[0].shape[1]
-    total = key_rows * len(blocks)
+def make_values(arrays, devices, width, kv_width):
+    rows = arrays[0].shape[0]
+    total = rows * len(devices)
+    kinds = 2 + width // total
     kv = jax.ShapeDtypeStruct((total, kv_width), BF16)
     return pl.pallas_call(
-        functools.partial(value_kernel, key_rows, blocks, small_blocks),
+        functools.partial(value_kernel, kv_width, devices),
         out_shape=[kv, kv],
-        in_specs=[ANY] * (len(arrays) + len(smalls)),
+        in_specs=[ANY] * len(arrays),
         out_specs=[IN_VMEM] * 2,
         scratch_shapes=[
             pltpu.VMEM((total, width), BF16),
             pltpu.VMEM((width, kv_width), BF16),
-            pltpu.SemaphoreType.DMA((3, len(blocks))),
+            pltpu.SemaphoreType.DMA((kinds, len(devices))),
         ],
         compiler_params=pltpu.CompilerParams(vmem_limit_bytes=VMEM_LIMIT),
         cost_estimate=SHORT,
         name="values",
-    )(*arrays, *smalls)
+    )(*arrays)
 
 
 def attention_kernel(chunk, q_ref, k_ref, v_ref, *refs):
@@ -450,29 +442,18 @@
     return lax.optimization_barrier((x, *others))[0]
 
 
-def on_line(acts, packed, small, queries, w_gate_up, w_down, top, capacity):
+def on_line(acts, packed, kv_width, queries, w_gate_up, w_down, top, capacity):
     rows, width = acts.shape
-    small_across = across(small)
-    pair = jnp.concatenate([small, small_across], axis=0)
-    line = [packed, forward(packed), None, backward(packed)]
+    line = [packed, forward(packed), None, None]
     line[2] = forward(line[1])
-    crossed = [across(after(packed, small_across)), *map(across, line[1:])]
+    line[3] = backward(after(packed, line[1]))
+    crossed = [across(x) for x in line]
     arrays = [
         [line[step], crossed[step], other_core(line[step]), other_core(crossed[step])]
         for step in range(LINE)
     ]
-    blocks = [
-        (4 * step + core * 2 + y, 0, functools.partial(from_device, step, y, core))
-        for step in range(LINE)
-        for core in range(2)
-        for y in range(2)
-    ]
-    pair = after(pair, line[2])
-    pairs = [pair, forward(pair), None, None]
-    pairs[3] = backward(after(pair, pairs[1]))
-    small_rows = small.shape[0]
-    small_blocks = [
-        (2 * step + core, y * small_rows, functools.partial(from_device, step, y, core))
+    devices = [
+        functools.partial(from_device, step, y, core)
         for step in range(LINE)
         for core in range(2)
         for y in range(2)
@@ -491,25 +472,21 @@
         came_second = other_core(after(send_second, crossing))
         return keep, (came_first, came_second), send_first
 
-    beside = [crossed[3], crossed[2], pairs[1], arrays[3][2], arrays[2][2]]
+    beside = [crossed[3], crossed[2], arrays[3][2], arrays[2][2]]
     keep, came, send = experts(1, 0, [line[2]], beside)
     near = [(keep[i][:rows], came[i][:rows]) for i in range(2)]
     crossing = [summed(keep[i][rows:], came[i][rows:]) for i in range(2)]
     theirs_near = across(crossing[0])
-    keep, came, send = experts(2, 3, [crossing[0]], [theirs_near, pairs[3]])
-    pairs[2] = forward(after(pairs[1], send))
-    total = summed(*near[0], after(theirs_near, send))
-    moving = forward(total)
+    keep, came, _ = experts(2, 3, [crossing[0]], [theirs_near])
     far = [summed(keep[i][rows:], came[i][rows:]) for i in range(2)]
     theirs = across(far[0])
-    smalls = []
-    for step in range(LINE):
-        smalls += [pairs[step], other_core(after(pairs[step], far[0]))]
+    total = summed(*near[0], after(theirs_near, far[0]))
+    moving = forward(total)
     total = summed(keep[0][:rows], came[0][:rows], theirs, moving)
     moving = forward(total)
-    new_keys, values = make_values(
-        sum(arrays, []), blocks, smalls, small_blocks, rows, width, [total]
-    )
+    blocks = sum(arrays, [])
+    blocks[0] = after(blocks[0], total)
+    new_keys, values = make_values(blocks, devices, width, kv_width)
     theirs = across(after(far[1], theirs))
     total = summed(keep[1][:rows], came[1][:rows], theirs, after(moving, values))
     moving = forward(total)
@@ -522,9 +499,10 @@
     return context, layer_out
 
 
-def on_any(acts, packed, small, queries, w_gate_up, w_down, top, capacity):
+def on_any(
+    acts, packed, keys, value_weight, queries, w_gate_up, w_down, top, capacity
+):
     rows, width = acts.shape
-    keys, value_weight = small[:rows], small[rows:]
     gathered = lax.all_gather(packed, "seq", axis=0, tiled=True)
     all_keys = lax.all_gather(keys, "seq", axis=0, tiled=True)
     weight = lax.all_gather(value_weight, "seq", axis=0, tiled=True)
@@ -551,26 +529,21 @@
     devices = lax.axis_size("seq")
     capacity = max(2, 3 * pos_rows * top // (2 * devices))
     acts = activations.reshape(pos_rows, model_width)
-    packed, small, up_weights = pack(
+    keys = keys.reshape(pos_rows, -1)
+    line = devices == 4 * LINE and value_weight.shape[0] % pos_rows == 0
+    packed, up_weights = pack(
         acts,
         norm_gain,
         expert_ids.transpose(1, 2, 0).reshape(top, pos_rows),
         gate_weights.transpose(1, 2, 0).reshape(top, pos_rows),
-        keys.reshape(pos_rows, -1),
-        value_weight,
         w_gate_up[0],
+        *((keys, value_weight) if line else ()),
     )
-    way = on_line if devices == 4 * LINE else on_any
-    context, layer_out = way(
-        acts,
-        packed,
-        small,
-        queries.reshape(pos_rows, -1),
-        up_weights,
-        w_down[0],
-        top,
-        capacity,
-    )
+    rest = (queries.reshape(pos_rows, -1), up_weights, w_down[0], top, capacity)
+    if line:
+        context, layer_out = on_line(acts, packed, keys.shape[1], *rest)
+    else:
+        context, layer_out = on_any(acts, packed, keys, value_weight, *rest)
     return (context.reshape(queries.shape), layer_out.reshape(activations.shape))
 
 

time: 90.5 us -> 97.7 us (1.080)
  waiting for transfers between devices: 25.3 us -> 48.3 us
  starting transfers between devices: 38.5 us -> 24.9 us
  Pallas kernels: 24.2 us -> 22 us
    ppermute x9 -> x8, waiting for transfers between devices: 4.18 us -> 18.7 us  [across(): return lax.ppermute(x, 'seq', swaps(1, 0))]
    ppermute x7 -> x5, waiting for transfers between devices: 14.7 us -> 23.3 us  [forward(): return lax.ppermute(x, 'seq', ring_steps(1))]
    ppermute x9 -> x8, starting transfers between devices: 12.3 us -> 6.26 us  [across(): return lax.ppermute(x, 'seq', swaps(1, 0))]
    ppermute x7 -> x5, starting transfers between devices: 19.4 us -> 15.7 us  [forward(): return lax.ppermute(x, 'seq', ring_steps(1))]
    ppermute x2 -> x1, waiting for transfers between devices: 5.06 us -> 2.57 us  [backward(): return lax.ppermute(x, 'seq', ring_steps(LINE - 1))]
    ppermute x16 -> x12, waiting for transfers between devices: 1.44 us -> 3.76 us  [other_core(): return lax.ppermute(x, 'seq', swaps(0, 1))]
    ppermute x2 -> x1, starting transfers between devices: 3.68 us -> 1.69 us  [backward(): return lax.ppermute(x, 'seq', ring_steps(LINE - 1))]
    pallas_call x2, Pallas kernels: 7.83 us -> 5.91 us  [the longest x1 3.14 us: pack(): pl.pallas_call(pack_kernel, out_shape=[jax.ShapeDtypeStruct((rows, column...]
  transfers between devices with their start and end apart: 34 -> 26, of which waited for: 12 -> 13; matrix products, arithmetic and copies ran while one was open for 1% -> 0% of each run, Pallas kernels for 23% -> 19%
where the time goes in v9:
time: 97.7 us; the launch traced here: 97.5 us
  waiting for transfers between devices  48.3 us (49%)
  starting transfers between devices  24.9 us (25%)
  Pallas kernels  22 us (23%)
  other arithmetic  1.5 us (2%)
    ppermute x5, waiting for transfers between devices, forward(): return lax.ppermute(x, 'seq', ring_steps(1))  23.3 us
    ppermute x8, waiting for transfers between devices, across(): return lax.ppermute(x, 'seq', swaps(1, 0))  18.7 us
    ppermute x5, starting transfers between devices, forward(): return lax.ppermute(x, 'seq', ring_steps(1))  15.7 us
    pallas_call x2, Pallas kernels, run_experts(): pl.pallas_call(functools.partial(expert_kernel, top, tok_rows, capacity,...  8.73 us
    pallas_call x4, Pallas kernels, attend_part(): pl.pallas_call(functools.partial(attention_kernel, chunk), grid=(1,), out...  7.33 us
    ppermute x8, starting transfers between devices, across(): return lax.ppermute(x, 'seq', swaps(1, 0))  6.26 us
    ppermute x12, waiting for transfers between devices, other_core(): return lax.ppermute(x, 'seq', swaps(0, 1))  3.76 us
    pallas_call x1, Pallas kernels, pack(): pl.pallas_call(pack_kernel, out_shape=[jax.ShapeDtypeStruct((rows, column...  3.14 us
  transfers between devices with their start and end apart: 26, of which 13 were waited for; matrix products, arithmetic and copies ran while one was open for 0% of the time, Pallas kernels for 19%

profile of v9, /device:TPU:0, one launch (start us, length us, event | category | flops | bytes accessed | tf_op | source)
XLA Modules:
  0.0 97.5 jit_solution(1409544963896296014)
XLA Ops:
  0.6 3.1 %normalize_and_pack.1 = (bf16[64,2944]{1,0:T(8,128)(2,1)S(1)}, bf16[2048,1536]{1,0:T(8,128)(2,1)S(1)}) custom-call(bf16[64,2048]{1,0:T(8,128)(2,1)} %bitcast.24, f32[1,2048]{1,0:T(1,128)} %bitcast.26, s32[4,64]{1,0:T(4,128)} %bitcast.27, f32[4,64]{1,0:T(4,128)} %bitcast.28, bf16[2048,1536]{1,0:T(8,128)(2,1)} %bitcast.23, bf16[64,256]{1,0:T(8,128)(2,1)} %bitcast.25, ...), custom_call_target="tpu_custom_call" | custom-call | flops 1 | bytes 1 | tf_op jit(solution)/shard_map/normalize_and_pack/pallas_call | solution.py:129
  3.8 3.1 %collective-permute-start = (bf16[64,2944]{1,0:T(8,128)(2,1)S(1)}, bf16[64,2944]{1,0:T(8,128)(2,1)S(1)}, u32[]{:S(2)}, u32[]{:S(2)}) collective-permute-start(bf16[64,2944]{1,0:T(8,128)(2,1)S(1)} %get-tuple-element.44.refs_4_.refs_0_), channel_id=1, source_target_pairs={{0,4},{1,5},{2,6},{3,7},{4,12},{5,13},{6,14},{7,15},{12,8},{13,9},... | collective-permute-start | bytes 1130504 | tf_op jit(solution)/shard_map/ppermute | solution.py:55
  6.9 1.5 %collective-permute-start.5 = (bf16[64,2944]{1,0:T(8,128)(2,1)S(1)}, bf16[64,2944]{1,0:T(8,128)(2,1)S(1)}, u32[]{:S(2)}, u32[]{:S(2)}) collective-permute-start(bf16[64,2944]{1,0:T(8,128)(2,1)S(1)} %get-tuple-element.44.refs_4_.refs_0_), channel_id=1, source_target_pairs={{0,2},{1,3},{2,0},{3,1},{4,6},{5,7},{6,4},{7,5},{12,14},{13,15},{1... | collective-permute-start | bytes 1130504 | tf_op jit(solution)/shard_map/ppermute | solution.py:63
  8.4 0.0 collective-permute-start.6
  8.4 8.3 %collective-permute-done.refs_0_.refs_4_ = bf16[64,2944]{1,0:T(8,128)(2,1)S(1)} collective-permute-done((bf16[64,2944]{1,0:T(8,128)(2,1)S(1)}, bf16[64,2944]{1,0:T(8,128)(2,1)S(1)}, u32[]{:S(2)}, u32[]{:S(2)}) %collective-permute-start) | collective-permute-done | bytes 376864 | tf_op jit(solution)/shard_map/ppermute | solution.py:55
  16.6 1.6 %collective-permute-start.2 = (bf16[64,2944]{1,0:T(8,128)(2,1)S(1)}, bf16[64,2944]{1,0:T(8,128)(2,1)S(1)}, u32[]{:S(2)}, u32[]{:S(2)}) collective-permute-start(bf16[64,2944]{1,0:T(8,128)(2,1)S(1)} %collective-permute-done.refs_0_.refs_4_), channel_id=1, source_target_pairs={{0,2},{1,3},{2,0},{3,1},{4,6},{5,7},{6,4},{7,5},{12,14},{13,15},{1... | collective-permute-start | bytes 1130504 | tf_op jit(solution)/shard_map/ppermute | solution.py:63
  18.2 1.7 %collective-permute-start.8 = (bf16[64,2944]{1,0:T(8,128)(2,1)S(1)}, bf16[64,2944]{1,0:T(8,128)(2,1)S(1)}, u32[]{:S(2)}, u32[]{:S(2)}) collective-permute-start(bf16[64,2944]{1,0:T(8,128)(2,1)S(1)} %get-tuple-element.44.refs_4_.refs_0_), channel_id=1, source_target_pairs={{0,8},{1,9},{2,10},{3,11},{4,0},{5,1},{6,2},{7,3},{12,4},{13,5},{1... | collective-permute-start | bytes 1130504 | tf_op jit(solution)/shard_map/ppermute | solution.py:59
  19.9 0.0 collective-permute-done.5.refs_5_.refs_1_
  19.9 0.0 collective-permute-start.7
  19.9 0.3 collective-permute-start.1
  20.3 0.0 collective-permute-done.6.refs_6_.refs_2_
  20.3 0.2 collective-permute-start.3
  20.5 6.1 %collective-permute-done.2.refs_1_.refs_5_ = bf16[64,2944]{1,0:T(8,128)(2,1)S(1)} collective-permute-done((bf16[64,2944]{1,0:T(8,128)(2,1)S(1)}, bf16[64,2944]{1,0:T(8,128)(2,1)S(1)}, u32[]{:S(2)}, u32[]{:S(2)}) %collective-permute-start.2) | collective-permute-done | bytes 376864 | tf_op jit(solution)/shard_map/ppermute | solution.py:63
  26.6 0.0 collective-permute-start.4
  26.6 2.6 %collective-permute-done.8.refs_4_.refs_12_ = bf16[64,2944]{1,0:T(8,128)(2,1)S(1)} collective-permute-done((bf16[64,2944]{1,0:T(8,128)(2,1)S(1)}, bf16[64,2944]{1,0:T(8,128)(2,1)S(1)}, u32[]{:S(2)}, u32[]{:S(2)}) %collective-permute-start.8) | collective-permute-done | bytes 376864 | tf_op jit(solution)/shard_map/ppermute | solution.py:59
  29.2 0.0 collective-permute-start.11
  29.2 0.0 collective-permute-done.7.refs_7_.refs_3_
  29.2 0.5 collective-permute-start.9
  29.7 7.8 %collective-permute-done.1.refs_0_.refs_8_ = bf16[64,2944]{1,0:T(8,128)(2,1)S(1)} collective-permute-done((bf16[64,2944]{1,0:T(8,128)(2,1)S(1)}, bf16[64,2944]{1,0:T(8,128)(2,1)S(1)}, u32[]{:S(2)}, u32[]{:S(2)}) %collective-permute-start.1) | collective-permute-done | bytes 376864 | tf_op jit(solution)/shard_map/ppermute | solution.py:55
  37.5 0.1 collective-permute-start.12
  37.6 0.5 collective-permute-start.10
  38.1 0.0 collective-permute-done.4.refs_3_.refs_7_
  38.1 4.4 %experts.2 = (bf16[128,2048]{1,0:T(8,128)(2,1)S(1)}, bf16[128,2048]{1,0:T(8,128)(2,1)S(1)}, bf16[128,2048]{1,0:T(8,128)(2,1)S(1)}, bf16[128,2048]{1,0:T(8,128)(2,1)S(1)}) custom-call(bf16[64,2944]{1,0:T(8,128)(2,1)S(1)} %collective-permute-done.refs_0_.refs_4_, bf16[64,2944]{1,0:T(8,128)(2,1)S(1)} %collective-permute-done.2.refs_1_.refs_5_, ...), custom_call_target="tpu_custom_call" | custom-call | flops 1 | bytes 1 | tf_op jit(solution)/shard_map/experts/pallas_call | solution.py:275
  42.5 0.0 collective-permute-done.9.refs_5_.refs_13_
  42.5 0.0 collective-permute-done.12.refs_2_.refs_10_
  42.5 6.2 %collective-permute-done.10.refs_1_.refs_9_ = bf16[64,2944]{1,0:T(8,128)(2,1)S(1)} collective-permute-done((bf16[64,2944]{1,0:T(8,128)(2,1)S(1)}, bf16[64,2944]{1,0:T(8,128)(2,1)S(1)}, u32[]{:S(2)}, u32[]{:S(2)}) %collective-permute-start.10) | collective-permute-done | bytes 376864 | tf_op jit(solution)/shard_map/ppermute | solution.py:63
  48.7 0.5 collective-permute-start.15
  49.2 0.0 collective-permute-start.14
  49.2 1.4 %collective-permute-done.13 = bf16[128,2048]{1,0:T(8,128)(2,1)S(1)} collective-permute-done((bf16[128,2048]{1,0:T(8,128)(2,1)S(1)}, bf16[128,2048]{1,0:T(8,128)(2,1)S(1)}, u32[]{:S(2)}, u32[]{:S(2)}) %collective-permute-start.13) | collective-permute-done | bytes 524320 | tf_op jit(solution)/shard_map/ppermute | solution.py:67
  50.6 0.1 add_convert_fusion.7
  50.7 0.6 collective-permute-start.16
  51.2 0.0 collective-permute-done.15.refs_7_.refs_15_
  51.2 0.4 collective-permute-done.14.refs_3_.refs_11_
  51.7 4.4 %experts.3 = (bf16[128,2048]{1,0:T(8,128)(2,1)S(1)}, bf16[128,2048]{1,0:T(8,128)(2,1)S(1)}, bf16[128,2048]{1,0:T(8,128)(2,1)S(1)}, bf16[128,2048]{1,0:T(8,128)(2,1)S(1)}) custom-call(bf16[64,2944]{1,0:T(8,128)(2,1)S(1)} %collective-permute-done.1.refs_0_.refs_8_, bf16[64,2944]{1,0:T(8,128)(2,1)S(1)} %collective-permute-done.10.refs_1_.refs_9_, ...), custom_call_target="tpu_custom_call" | custom-call | flops 1 | bytes 1 | tf_op jit(solution)/shard_map/experts/pallas_call | solution.py:275
  56.0 0.0 copy-start.1
  56.1 3.0 %collective-permute-done.16 = bf16[64,2048]{1,0:T(8,128)(2,1)S(1)} collective-permute-done((bf16[64,2048]{1,0:T(8,128)(2,1)S(1)}, bf16[64,2048]{1,0:T(8,128)(2,1)S(1)}, u32[]{:S(2)}, u32[]{:S(2)}) %collective-permute-start.16) | collective-permute-done | bytes 262176 | tf_op jit(solution)/shard_map/ppermute | solution.py:63
  59.1 1.9 %collective-permute-done.17 = bf16[128,2048]{1,0:T(8,128)(2,1)S(1)} collective-permute-done((bf16[128,2048]{1,0:T(8,128)(2,1)S(1)}, bf16[128,2048]{1,0:T(8,128)(2,1)S(1)}, u32[]{:S(2)}, u32[]{:S(2)}) %collective-permute-start.17) | collective-permute-done | bytes 524320 | tf_op jit(solution)/shard_map/ppermute | solution.py:67
  61.0 0.1 add_convert_fusion.6
  61.1 0.1 add_convert_fusion.4
  61.2 2.7 %collective-permute-start.21 = (bf16[64,2048]{1,0:T(8,128)(2,1)S(1)}, bf16[64,2048]{1,0:T(8,128)(2,1)S(1)}, u32[]{:S(2)}, u32[]{:S(2)}) collective-permute-start(bf16[64,2048]{1,0:T(8,128)(2,1)S(1)} %add_convert_fusion.4), channel_id=1, source_target_pairs={{0,4},{1,5},{2,6},{3,7},{4,12},{5,13},{6,14},{7,15},{12,8},{13,9},... | collective-permute-start | bytes 786440 | tf_op jit(solution)/shard_map/ppermute | solution.py:55
  63.9 0.5 collective-permute-start.19
  64.4 0.0 collective-permute-start.18
  64.4 0.5 collective-permute-start.23
  64.9 6.0 %collective-permute-done.21 = bf16[64,2048]{1,0:T(8,128)(2,1)S(1)} collective-permute-done((bf16[64,2048]{1,0:T(8,128)(2,1)S(1)}, bf16[64,2048]{1,0:T(8,128)(2,1)S(1)}, u32[]{:S(2)}, u32[]{:S(2)}) %collective-permute-start.21) | collective-permute-done | bytes 262176 | tf_op jit(solution)/shard_map/ppermute | solution.py:55
  70.9 1.0 %collective-permute-done.19 = bf16[64,2048]{1,0:T(8,128)(2,1)S(1)} collective-permute-done((bf16[64,2048]{1,0:T(8,128)(2,1)S(1)}, bf16[64,2048]{1,0:T(8,128)(2,1)S(1)}, u32[]{:S(2)}, u32[]{:S(2)}) %collective-permute-start.19) | collective-permute-done | bytes 262176 | tf_op jit(solution)/shard_map/ppermute | solution.py:63
  72.0 0.1 add_convert_fusion.3
  72.1 7.8 %collective-permute-start.22 = (bf16[64,2048]{1,0:T(8,128)(2,1)S(1)}, bf16[64,2048]{1,0:T(8,128)(2,1)S(1)}, u32[]{:S(2)}, u32[]{:S(2)}) collective-permute-start(bf16[64,2048]{1,0:T(8,128)(2,1)S(1)} %add_convert_fusion.3), channel_id=1, source_target_pairs={{0,4},{1,5},{2,6},{3,7},{4,12},{5,13},{6,14},{7,15},{12,8},{13,9},... | collective-permute-start | bytes 786440 | tf_op jit(solution)/shard_map/ppermute | solution.py:55
  79.9 0.0 collective-permute-done.18
  79.9 0.1 add_convert_fusion.5
  79.9 0.6 collective-permute-start.20
  80.5 0.0 collective-permute-done.23
  80.5 0.1 add_convert_fusion.1
  80.6 2.8 %values.1 = (bf16[1024,256]{1,0:T(8,128)(2,1)S(1)}, bf16[1024,256]{1,0:T(8,128)(2,1)S(1)}) custom-call(bf16[64,2944]{1,0:T(8,128)(2,1)S(1)} %get-tuple-element.44.refs_4_.refs_0_, bf16[64,2944]{1,0:T(8,128)(2,1)S(1)} %collective-permute-done.5.refs_5_.refs_1_, bf16[64,2944]{1,0:T(8,128)(2,1)S(1)} %collective-permute-done.6.refs_6_.refs_2_, ...), custom_call_target="tpu_custom_call" | custom-call | flops 1 | bytes 1 | tf_op jit(solution)/shard_map/values/pallas_call | solution.py:333
  83.3 0.0 copy-start.2
  83.4 1.2 %collective-permute-done.22 = bf16[64,2048]{1,0:T(8,128)(2,1)S(1)} collective-permute-done((bf16[64,2048]{1,0:T(8,128)(2,1)S(1)}, bf16[64,2048]{1,0:T(8,128)(2,1)S(1)}, u32[]{:S(2)}, u32[]{:S(2)}) %collective-permute-start.22) | collective-permute-done | bytes 262176 | tf_op jit(solution)/shard_map/ppermute | solution.py:55
  84.6 2.3 %collective-permute-done.20 = bf16[64,2048]{1,0:T(8,128)(2,1)S(1)} collective-permute-done((bf16[64,2048]{1,0:T(8,128)(2,1)S(1)}, bf16[64,2048]{1,0:T(8,128)(2,1)S(1)}, u32[]{:S(2)}, u32[]{:S(2)}) %collective-permute-start.20) | collective-permute-done | bytes 262176 | tf_op jit(solution)/shard_map/ppermute | solution.py:63
  86.9 0.1 add_convert_fusion.2
  87.0 1.7 %collective-permute-start.25 = (bf16[64,2048]{1,0:T(8,128)(2,1)S(1)}, bf16[64,2048]{1,0:T(8,128)(2,1)S(1)}, u32[]{:S(2)}, u32[]{:S(2)}) collective-permute-start(bf16[64,2048]{1,0:T(8,128)(2,1)S(1)} %add_convert_fusion.2), channel_id=1, source_target_pairs={{0,4},{1,5},{2,6},{3,7},{4,12},{5,13},{6,14},{7,15},{12,8},{13,9},... | collective-permute-start | bytes 786440 | tf_op jit(solution)/shard_map/ppermute | solution.py:55
  88.8 0.5 collective-permute-start.24
  89.3 1.8 %attention.4.refs_0_ = bf16[64,4096]{1,0:T(8,128)(2,1)} custom-call(bf16[64,4096]{1,0:T(8,128)(2,1)S(1)} %bitcast.18, bf16[1024,256]{1,0:T(8,128)(2,1)S(1)} %get-tuple-element.48.k_ref, bf16[1024,256]{1,0:T(8,128)(2,1)S(1)} %get-tuple-element.45.v_ref), custom_call_target="tpu_custom_call" | custom-call | flops 1 | bytes 1 | tf_op jit(solution)/shard_map/attention/pallas_call | solution.py:419
  91.1 1.8 %attention.5.refs_0_ = bf16[64,4096]{1,0:T(8,128)(2,1)} custom-call(bf16[64,4096]{1,0:T(8,128)(2,1)S(1)} %bitcast.19, bf16[1024,256]{1,0:T(8,128)(2,1)S(1)} %get-tuple-element.48.k_ref, bf16[1024,256]{1,0:T(8,128)(2,1)S(1)} %get-tuple-element.45.v_ref, bf16[64,4096]{1,0:T(8,128)(2,1)} %attention.4.refs_0_), custom_call_target="tpu_custom_call", output_to_operand_aliasing={{}: (3, {})} | custom-call | flops 1 | bytes 1 | tf_op jit(solution)/shard_map/attention/pallas_call | solution.py:419
  93.0 1.8 %attention.6.refs_0_ = bf16[64,4096]{1,0:T(8,128)(2,1)} custom-call(bf16[64,4096]{1,0:T(8,128)(2,1)S(1)} %bitcast.20, bf16[1024,256]{1,0:T(8,128)(2,1)S(1)} %get-tuple-element.48.k_ref, bf16[1024,256]{1,0:T(8,128)(2,1)S(1)} %get-tuple-element.45.v_ref, bf16[64,4096]{1,0:T(8,128)(2,1)} %attention.5.refs_0_), custom_call_target="tpu_custom_call", output_to_operand_aliasing={{}: (3, {})} | custom-call | flops 1 | bytes 1 | tf_op jit(solution)/shard_map/attention/pallas_call | solution.py:419
  94.8 1.8 %attention.7 = bf16[64,4096]{1,0:T(8,128)(2,1)} custom-call(bf16[64,4096]{1,0:T(8,128)(2,1)S(1)} %bitcast.21, bf16[1024,256]{1,0:T(8,128)(2,1)S(1)} %get-tuple-element.48.k_ref, bf16[1024,256]{1,0:T(8,128)(2,1)S(1)} %get-tuple-element.45.v_ref, bf16[64,4096]{1,0:T(8,128)(2,1)} %attention.6.refs_0_), custom_call_target="tpu_custom_call", output_to_operand_aliasing={{}: (3, {})} | custom-call | flops 1 | bytes 1 | tf_op jit(solution)/shard_map/attention/pallas_call | solution.py:419
  96.6 0.9 fusion
  (10 shorter events, 0.0 us)
Async XLA Ops:
  0.6 37.5 %copy-start = (bf16[1,768,2048]{2,1,0:T(8,128)(2,1)S(1)}, bf16[1,768,2048]{2,1,0:T(8,128)(2,1)}, u32[]{:S(2)}) copy-start(bf16[1,768,2048]{2,1,0:T(8,128)(2,1)} %param.17) | copy-start | bytes 9437188
  3.8 12.9 %collective-permute-start = (bf16[64,2944]{1,0:T(8,128)(2,1)S(1)}, bf16[64,2944]{1,0:T(8,128)(2,1)S(1)}, u32[]{:S(2)}, u32[]{:S(2)}) collective-permute-start(bf16[64,2944]{1,0:T(8,128)(2,1)S(1)} %get-tuple-element.44.refs_4_.refs_0_), channel_id=1, source_target_pairs={{0,4},{1,5},{2,6},{3,7},{4,12},{5,13},{6,14},{7,15},{12,8},{13,9},... | collective-permute-start | bytes 1130504 | tf_op jit(solution)/shard_map/ppermute | solution.py:55
  6.9 13.0 %collective-permute-start.5 = (bf16[64,2944]{1,0:T(8,128)(2,1)S(1)}, bf16[64,2944]{1,0:T(8,128)(2,1)S(1)}, u32[]{:S(2)}, u32[]{:S(2)}) collective-permute-start(bf16[64,2944]{1,0:T(8,128)(2,1)S(1)} %get-tuple-element.44.refs_4_.refs_0_), channel_id=1, source_target_pairs={{0,2},{1,3},{2,0},{3,1},{4,6},{5,7},{6,4},{7,5},{12,14},{13,15},{1... | collective-permute-start | bytes 1130504 | tf_op jit(solution)/shard_map/ppermute | solution.py:63
  8.4 11.9 %collective-permute-start.6 = (bf16[64,2944]{1,0:T(8,128)(2,1)S(1)}, bf16[64,2944]{1,0:T(8,128)(2,1)S(1)}, u32[]{:S(2)}, u32[]{:S(2)}) collective-permute-start(bf16[64,2944]{1,0:T(8,128)(2,1)S(1)} %get-tuple-element.44.refs_4_.refs_0_), channel_id=1, source_target_pairs={{0,1},{1,0},{2,3},{3,2},{4,5},{5,4},{6,7},{7,6},{12,13},{13,12},{1... | collective-permute-start | bytes 1130504 | tf_op jit(solution)/shard_map/ppermute | solution.py:67
  16.6 9.9 %collective-permute-start.2 = (bf16[64,2944]{1,0:T(8,128)(2,1)S(1)}, bf16[64,2944]{1,0:T(8,128)(2,1)S(1)}, u32[]{:S(2)}, u32[]{:S(2)}) collective-permute-start(bf16[64,2944]{1,0:T(8,128)(2,1)S(1)} %collective-permute-done.refs_0_.refs_4_), channel_id=1, source_target_pairs={{0,2},{1,3},{2,0},{3,1},{4,6},{5,7},{6,4},{7,5},{12,14},{13,15},{1... | collective-permute-start | bytes 1130504 | tf_op jit(solution)/shard_map/ppermute | solution.py:63
  18.2 11.0 %collective-permute-start.8 = (bf16[64,2944]{1,0:T(8,128)(2,1)S(1)}, bf16[64,2944]{1,0:T(8,128)(2,1)S(1)}, u32[]{:S(2)}, u32[]{:S(2)}) collective-permute-start(bf16[64,2944]{1,0:T(8,128)(2,1)S(1)} %get-tuple-element.44.refs_4_.refs_0_), channel_id=1, source_target_pairs={{0,8},{1,9},{2,10},{3,11},{4,0},{5,1},{6,2},{7,3},{12,4},{13,5},{1... | collective-permute-start | bytes 1130504 | tf_op jit(solution)/shard_map/ppermute | solution.py:59
  19.9 9.3 %collective-permute-start.7 = (bf16[64,2944]{1,0:T(8,128)(2,1)S(1)}, bf16[64,2944]{1,0:T(8,128)(2,1)S(1)}, u32[]{:S(2)}, u32[]{:S(2)}) collective-permute-start(bf16[64,2944]{1,0:T(8,128)(2,1)S(1)} %collective-permute-done.5.refs_5_.refs_1_), channel_id=1, source_target_pairs={{0,1},{1,0},{2,3},{3,2},{4,5},{5,4},{6,7},{7,6},{12,13},{13,12},{1... | collective-permute-start | bytes 1130504 | tf_op jit(solution)/shard_map/ppermute | solution.py:67
  19.9 17.6 %collective-permute-start.1 = (bf16[64,2944]{1,0:T(8,128)(2,1)S(1)}, bf16[64,2944]{1,0:T(8,128)(2,1)S(1)}, u32[]{:S(2)}, u32[]{:S(2)}) collective-permute-start(bf16[64,2944]{1,0:T(8,128)(2,1)S(1)} %collective-permute-done.refs_0_.refs_4_), channel_id=1, source_target_pairs={{0,4},{1,5},{2,6},{3,7},{4,12},{5,13},{6,14},{7,15},{12,8},{13,9},... | collective-permute-start | bytes 1130504 | tf_op jit(solution)/shard_map/ppermute | solution.py:55
  20.3 17.3 %collective-permute-start.3 = (bf16[64,2944]{1,0:T(8,128)(2,1)S(1)}, bf16[64,2944]{1,0:T(8,128)(2,1)S(1)}, u32[]{:S(2)}, u32[]{:S(2)}) collective-permute-start(bf16[64,2944]{1,0:T(8,128)(2,1)S(1)} %collective-permute-done.refs_0_.refs_4_), channel_id=1, source_target_pairs={{0,1},{1,0},{2,3},{3,2},{4,5},{5,4},{6,7},{7,6},{12,13},{13,12},{1... | collective-permute-start | bytes 1130504 | tf_op jit(solution)/shard_map/ppermute | solution.py:67
  26.6 11.5 %collective-permute-start.4 = (bf16[64,2944]{1,0:T(8,128)(2,1)S(1)}, bf16[64,2944]{1,0:T(8,128)(2,1)S(1)}, u32[]{:S(2)}, u32[]{:S(2)}) collective-permute-start(bf16[64,2944]{1,0:T(8,128)(2,1)S(1)} %collective-permute-done.2.refs_1_.refs_5_), channel_id=1, source_target_pairs={{0,1},{1,0},{2,3},{3,2},{4,5},{5,4},{6,7},{7,6},{12,13},{13,12},{1... | collective-permute-start | bytes 1130504 | tf_op jit(solution)/shard_map/ppermute | solution.py:67
  29.2 13.3 %collective-permute-start.11 = (bf16[64,2944]{1,0:T(8,128)(2,1)S(1)}, bf16[64,2944]{1,0:T(8,128)(2,1)S(1)}, u32[]{:S(2)}, u32[]{:S(2)}) collective-permute-start(bf16[64,2944]{1,0:T(8,128)(2,1)S(1)} %collective-permute-done.8.refs_4_.refs_12_), channel_id=1, source_target_pairs={{0,1},{1,0},{2,3},{3,2},{4,5},{5,4},{6,7},{7,6},{12,13},{13,12},{1... | collective-permute-start | bytes 1130504 | tf_op jit(solution)/shard_map/ppermute | solution.py:67
  29.2 13.3 %collective-permute-start.9 = (bf16[64,2944]{1,0:T(8,128)(2,1)S(1)}, bf16[64,2944]{1,0:T(8,128)(2,1)S(1)}, u32[]{:S(2)}, u32[]{:S(2)}) collective-permute-start(bf16[64,2944]{1,0:T(8,128)(2,1)S(1)} %collective-permute-done.8.refs_4_.refs_12_), channel_id=1, source_target_pairs={{0,2},{1,3},{2,0},{3,1},{4,6},{5,7},{6,4},{7,5},{12,14},{13,15},{1... | collective-permute-start | bytes 1130504 | tf_op jit(solution)/shard_map/ppermute | solution.py:63
  37.5 5.0 %collective-permute-start.12 = (bf16[64,2944]{1,0:T(8,128)(2,1)S(1)}, bf16[64,2944]{1,0:T(8,128)(2,1)S(1)}, u32[]{:S(2)}, u32[]{:S(2)}) collective-permute-start(bf16[64,2944]{1,0:T(8,128)(2,1)S(1)} %collective-permute-done.1.refs_0_.refs_8_), channel_id=1, source_target_pairs={{0,1},{1,0},{2,3},{3,2},{4,5},{5,4},{6,7},{7,6},{12,13},{13,12},{1... | collective-permute-start | bytes 1130504 | tf_op jit(solution)/shard_map/ppermute | solution.py:67
  37.6 11.1 %collective-permute-start.10 = (bf16[64,2944]{1,0:T(8,128)(2,1)S(1)}, bf16[64,2944]{1,0:T(8,128)(2,1)S(1)}, u32[]{:S(2)}, u32[]{:S(2)}) collective-permute-start(bf16[64,2944]{1,0:T(8,128)(2,1)S(1)} %collective-permute-done.1.refs_0_.refs_8_), channel_id=1, source_target_pairs={{0,2},{1,3},{2,0},{3,1},{4,6},{5,7},{6,4},{7,5},{12,14},{13,15},{1... | collective-permute-start | bytes 1130504 | tf_op jit(solution)/shard_map/ppermute | solution.py:63
  48.7 1.9 %collective-permute-start.13 = (bf16[128,2048]{1,0:T(8,128)(2,1)S(1)}, bf16[128,2048]{1,0:T(8,128)(2,1)S(1)}, u32[]{:S(2)}, u32[]{:S(2)}) collective-permute-start(bf16[128,2048]{1,0:T(8,128)(2,1)S(1)} %get-tuple-element.34), channel_id=1, source_target_pairs={{0,1},{1,0},{2,3},{3,2},{4,5},{5,4},{6,7},{7,6},{12,13},{13,12},{1... | collective-permute-start | bytes 1572872 | tf_op jit(solution)/shard_map/ppermute | solution.py:67
  48.7 2.5 %collective-permute-start.15 = (bf16[64,2944]{1,0:T(8,128)(2,1)S(1)}, bf16[64,2944]{1,0:T(8,128)(2,1)S(1)}, u32[]{:S(2)}, u32[]{:S(2)}) collective-permute-start(bf16[64,2944]{1,0:T(8,128)(2,1)S(1)} %collective-permute-done.9.refs_5_.refs_13_), channel_id=1, source_target_pairs={{0,1},{1,0},{2,3},{3,2},{4,5},{5,4},{6,7},{7,6},{12,13},{13,12},{1... | collective-permute-start | bytes 1130504 | tf_op jit(solution)/shard_map/ppermute | solution.py:67
  49.2 2.5 %collective-permute-start.14 = (bf16[64,2944]{1,0:T(8,128)(2,1)S(1)}, bf16[64,2944]{1,0:T(8,128)(2,1)S(1)}, u32[]{:S(2)}, u32[]{:S(2)}) collective-permute-start(bf16[64,2944]{1,0:T(8,128)(2,1)S(1)} %collective-permute-done.10.refs_1_.refs_9_), channel_id=1, source_target_pairs={{0,1},{1,0},{2,3},{3,2},{4,5},{5,4},{6,7},{7,6},{12,13},{13,12},{1... | collective-permute-start | bytes 1130504 | tf_op jit(solution)/shard_map/ppermute | solution.py:67
  50.7 8.4 %collective-permute-start.16 = (bf16[64,2048]{1,0:T(8,128)(2,1)S(1)}, bf16[64,2048]{1,0:T(8,128)(2,1)S(1)}, u32[]{:S(2)}, u32[]{:S(2)}) collective-permute-start(bf16[64,2048]{1,0:T(8,128)(2,1)S(1)} %add_convert_fusion.7), channel_id=1, source_target_pairs={{0,2},{1,3},{2,0},{3,1},{4,6},{5,7},{6,4},{7,5},{12,14},{13,15},{1... | collective-permute-start | bytes 786440 | tf_op jit(solution)/shard_map/ppermute | solution.py:63
  56.0 33.2 %copy-start.1 = (bf16[64,1,4096]{2,0,1:T(8,128)(2,1)S(1)}, bf16[64,1,4096]{2,0,1:T(8,128)(2,1)}, u32[]{:S(2)}) copy-start(bf16[64,1,4096]{2,0,1:T(8,128)(2,1)} %param.10) | copy-start | bytes 1572868
  59.1 1.9 %collective-permute-start.17 = (bf16[128,2048]{1,0:T(8,128)(2,1)S(1)}, bf16[128,2048]{1,0:T(8,128)(2,1)S(1)}, u32[]{:S(2)}, u32[]{:S(2)}) collective-permute-start(bf16[128,2048]{1,0:T(8,128)(2,1)S(1)} %get-tuple-element.40), channel_id=1, source_target_pairs={{0,1},{1,0},{2,3},{3,2},{4,5},{5,4},{6,7},{7,6},{12,13},{13,12},{1... | collective-permute-start | bytes 1572872 | tf_op jit(solution)/shard_map/ppermute | solution.py:67
  61.2 9.8 %collective-permute-start.21 = (bf16[64,2048]{1,0:T(8,128)(2,1)S(1)}, bf16[64,2048]{1,0:T(8,128)(2,1)S(1)}, u32[]{:S(2)}, u32[]{:S(2)}) collective-permute-start(bf16[64,2048]{1,0:T(8,128)(2,1)S(1)} %add_convert_fusion.4), channel_id=1, source_target_pairs={{0,4},{1,5},{2,6},{3,7},{4,12},{5,13},{6,14},{7,15},{12,8},{13,9},... | collective-permute-start | bytes 786440 | tf_op jit(solution)/shard_map/ppermute | solution.py:55
  63.9 8.1 %collective-permute-start.19 = (bf16[64,2048]{1,0:T(8,128)(2,1)S(1)}, bf16[64,2048]{1,0:T(8,128)(2,1)S(1)}, u32[]{:S(2)}, u32[]{:S(2)}) collective-permute-start(bf16[64,2048]{1,0:T(8,128)(2,1)S(1)} %add_convert_fusion.6), channel_id=1, source_target_pairs={{0,2},{1,3},{2,0},{3,1},{4,6},{5,7},{6,4},{7,5},{12,14},{13,15},{1... | collective-permute-start | bytes 786440 | tf_op jit(solution)/shard_map/ppermute | solution.py:63
  64.4 15.5 %collective-permute-start.18 = (bf16[128,2048]{1,0:T(8,128)(2,1)S(1)}, bf16[128,2048]{1,0:T(8,128)(2,1)S(1)}, u32[]{:S(2)}, u32[]{:S(2)}) collective-permute-start(bf16[128,2048]{1,0:T(8,128)(2,1)S(1)} %get-tuple-element.41), channel_id=1, source_target_pairs={{0,1},{1,0},{2,3},{3,2},{4,5},{5,4},{6,7},{7,6},{12,13},{13,12},{1... | collective-permute-start | bytes 1572872 | tf_op jit(solution)/shard_map/ppermute | solution.py:67
  64.4 16.1 %collective-permute-start.23 = (bf16[128,2048]{1,0:T(8,128)(2,1)S(1)}, bf16[128,2048]{1,0:T(8,128)(2,1)S(1)}, u32[]{:S(2)}, u32[]{:S(2)}) collective-permute-start(bf16[128,2048]{1,0:T(8,128)(2,1)S(1)} %get-tuple-element.51), channel_id=1, source_target_pairs={{0,1},{1,0},{2,3},{3,2},{4,5},{5,4},{6,7},{7,6},{12,13},{13,12},{1... | collective-permute-start | bytes 1572872 | tf_op jit(solution)/shard_map/ppermute | solution.py:67
  72.1 12.5 %collective-permute-start.22 = (bf16[64,2048]{1,0:T(8,128)(2,1)S(1)}, bf16[64,2048]{1,0:T(8,128)(2,1)S(1)}, u32[]{:S(2)}, u32[]{:S(2)}) collective-permute-start(bf16[64,2048]{1,0:T(8,128)(2,1)S(1)} %add_convert_fusion.3), channel_id=1, source_target_pairs={{0,4},{1,5},{2,6},{3,7},{4,12},{5,13},{6,14},{7,15},{12,8},{13,9},... | collective-permute-start | bytes 786440 | tf_op jit(solution)/shard_map/ppermute | solution.py:55
  79.9 7.0 %collective-permute-start.20 = (bf16[64,2048]{1,0:T(8,128)(2,1)S(1)}, bf16[64,2048]{1,0:T(8,128)(2,1)S(1)}, u32[]{:S(2)}, u32[]{:S(2)}) collective-permute-start(bf16[64,2048]{1,0:T(8,128)(2,1)S(1)} %add_convert_fusion.5), channel_id=1, source_target_pairs={{0,2},{1,3},{2,0},{3,1},{4,6},{5,7},{6,4},{7,5},{12,14},{13,15},{1... | collective-permute-start | bytes 786440 | tf_op jit(solution)/shard_map/ppermute | solution.py:63
  83.3 13.3 %copy-start.2 = (bf16[64,1,2048]{2,0,1:T(8,128)(2,1)S(1)}, bf16[64,1,2048]{2,0,1:T(8,128)(2,1)}, u32[]{:S(2)}) copy-start(bf16[64,1,2048]{2,0,1:T(8,128)(2,1)} %param.9) | copy-start | bytes 786436
  87.0 9.6 %collective-permute-start.25 = (bf16[64,2048]{1,0:T(8,128)(2,1)S(1)}, bf16[64,2048]{1,0:T(8,128)(2,1)S(1)}, u32[]{:S(2)}, u32[]{:S(2)}) collective-permute-start(bf16[64,2048]{1,0:T(8,128)(2,1)S(1)} %add_convert_fusion.2), channel_id=1, source_target_pairs={{0,4},{1,5},{2,6},{3,7},{4,12},{5,13},{6,14},{7,15},{12,8},{13,9},... | collective-permute-start | bytes 786440 | tf_op jit(solution)/shard_map/ppermute | solution.py:55
  88.8 7.8 %collective-permute-start.24 = (bf16[64,2048]{1,0:T(8,128)(2,1)S(1)}, bf16[64,2048]{1,0:T(8,128)(2,1)S(1)}, u32[]{:S(2)}, u32[]{:S(2)}) collective-permute-start(bf16[64,2048]{1,0:T(8,128)(2,1)S(1)} %add_convert_fusion.1), channel_id=1, source_target_pairs={{0,2},{1,3},{2,0},{3,1},{4,6},{5,7},{6,4},{7,5},{12,14},{13,15},{1... | collective-permute-start | bytes 786440 | tf_op jit(solution)/shard_map/ppermute | solution.py:63

commit v10 on v5

--- a/solution.py
+++ b/solution.py
@@ -436,7 +436,8 @@
 
 def on_line(acts, packed, small, queries, w_gate_up, w_down, top, capacity):
     rows, width = acts.shape
-    line = [packed, forward(packed), None, backward(packed)]
+    line = [packed, forward(packed), None, None]
+    line[3] = backward(after(packed, line[1]))
     crossed = [across(packed), across(line[1]), None, across(line[3])]
     to_core = other_core(packed)
     small = hold(after(small, to_core), in_vmem(w_gate_up, w_down))
@@ -494,7 +495,8 @@
         return send
 
     theirs = [None] * LINE
-    experts(1, 0, [line[2], crossed[3]], [crossed[2], pairs[1]])
+    ready = [line[2], crossed[3], arrays[3][2], arrays[2][2]]
+    experts(1, 0, ready, [crossed[2], pairs[1]])
     theirs[1] = across(crossing[1])
     send = experts(2, 3, [crossing[0], crossing[1]], [theirs[1], pairs[2], pairs[3]])
     total = summed(*mine[1], after(theirs[1], send))

time: 84.9 us -> 92.1 us (1.085)
  waiting for transfers between devices: 27.5 us -> 32.3 us
  starting transfers between devices: 27.3 us -> 29.7 us
    ppermute x2, starting transfers between devices: 2.27 us -> 7.53 us  [backward(): return lax.ppermute(x, 'seq', ring_steps(LINE - 1))]
    ppermute x7, starting transfers between devices: 11.6 us -> 9.54 us  [forward(): return lax.ppermute(x, 'seq', ring_steps(1))]
    ppermute x7, waiting for transfers between devices: 16.9 us -> 18.9 us  [forward(): return lax.ppermute(x, 'seq', ring_steps(1))]
    ppermute x9, waiting for transfers between devices: 2.2 us -> 4.16 us  [across(): return lax.ppermute(x, 'seq', swaps(1, 0))]
  transfers between devices with their start and end apart: 32 -> 32, of which waited for: 14 -> 16; matrix products, arithmetic and copies ran while one was open for 0% -> 0% of each run, Pallas kernels for 24% -> 22%
where the time goes in v10:
time: 92.1 us; the launch traced here: 91.9 us
  waiting for transfers between devices  32.3 us (35%)
  starting transfers between devices  29.7 us (32%)
  Pallas kernels  22 us (24%)
  local copies, waits for them, and re-layouts  5.59 us (6%)
  other arithmetic  1.5 us (2%)
    ppermute x7, waiting for transfers between devices, forward(): return lax.ppermute(x, 'seq', ring_steps(1))  18.9 us
    ppermute x7, starting transfers between devices, forward(): return lax.ppermute(x, 'seq', ring_steps(1))  9.54 us
    ppermute x9, starting transfers between devices, across(): return lax.ppermute(x, 'seq', swaps(1, 0))  9.52 us
    pallas_call x2, Pallas kernels, run_experts(): pl.pallas_call(functools.partial(expert_kernel, top, tok_rows, capacity,...  8.26 us
    ppermute x2, starting transfers between devices, backward(): return lax.ppermute(x, 'seq', ring_steps(LINE - 1))  7.53 us
    pallas_call x4, Pallas kernels, attend_part(): pl.pallas_call(functools.partial(attention_kernel, chunk), grid=(1,), out...  7.33 us
    unnamed x16, local copies, waits for them, and re-layouts  5.59 us
    ppermute x14, waiting for transfers between devices, other_core(): return lax.ppermute(x, 'seq', swaps(0, 1))  5.57 us
  transfers between devices with their start and end apart: 32, of which 16 were waited for; matrix products, arithmetic and copies ran while one was open for 0% of the time, Pallas kernels for 22%

profile of v10, /device:TPU:0, one launch (start us, length us, event | category | flops | bytes accessed | tf_op | source)
XLA Modules:
  0.0 91.9 jit_solution(7175227808166765111)
XLA Ops:
  0.6 1.9 %normalize_and_pack.1 = (bf16[64,2176]{1,0:T(8,128)(2,1)}, bf16[192,256]{1,0:T(8,128)(2,1)}) custom-call(bf16[64,2048]{1,0:T(8,128)(2,1)} %bitcast.27, f32[1,2048]{1,0:T(1,128)} %bitcast.29, s32[4,64]{1,0:T(4,128)} %bitcast.30, f32[4,64]{1,0:T(4,128)} %bitcast.31, bf16[64,256]{1,0:T(8,128)(2,1)} %bitcast.28, bf16[128,256]{1,0:T(8,128)(2,1)} %weight_ref.1), custom_call_target="tpu_custom_call" | custom-call | flops 1 | bytes 1 | tf_op jit(solution)/shard_map/normalize_and_pack/pallas_call | solution.py:108
  2.5 0.5 collective-permute-start.1
  2.9 2.6 %collective-permute-start.3 = (bf16[64,2176]{1,0:T(8,128)(2,1)}, bf16[64,2176]{1,0:T(8,128)(2,1)S(1)}, u32[]{:S(2)}, u32[]{:S(2)}) collective-permute-start(bf16[64,2176]{1,0:T(8,128)(2,1)} %get-tuple-element.36.refs_4_.refs_0_), channel_id=1, source_target_pairs={{0,4},{1,5},{2,6},{3,7},{4,12},{5,13},{6,14},{7,15},{12,8},{13,9},... | collective-permute-start | bytes 835592 | tf_op jit(solution)/shard_map/ppermute | solution.py:55
  5.5 1.5 %collective-permute-start = (bf16[64,2176]{1,0:T(8,128)(2,1)}, bf16[64,2176]{1,0:T(8,128)(2,1)S(1)}, u32[]{:S(2)}, u32[]{:S(2)}) collective-permute-start(bf16[64,2176]{1,0:T(8,128)(2,1)} %get-tuple-element.36.refs_4_.refs_0_), channel_id=1, source_target_pairs={{0,2},{1,3},{2,0},{3,1},{4,6},{5,7},{6,4},{7,5},{12,14},{13,15},{1... | collective-permute-start | bytes 835592 | tf_op jit(solution)/shard_map/ppermute | solution.py:63
  7.0 0.0 collective-permute-done.1.refs_6_.refs_2_
  7.0 2.8 %copy-done = bf16[1,2048,1536]{2,1,0:T(8,128)(2,1)S(1)} copy-done((bf16[1,2048,1536]{2,1,0:T(8,128)(2,1)S(1)}, bf16[1,2048,1536]{2,1,0:T(8,128)(2,1)}, u32[]{:S(2)}) %copy-start) | copy-done | bytes 6291480
  9.8 1.9 %copy-done.2 = bf16[1,768,2048]{2,1,0:T(8,128)(2,1)S(1)} copy-done((bf16[1,768,2048]{2,1,0:T(8,128)(2,1)S(1)}, bf16[1,768,2048]{2,1,0:T(8,128)(2,1)}, u32[]{:S(2)}) %copy-start.2) | copy-done | bytes 3145752
  11.7 0.9 copy-done.6
  12.6 0.6 collective-permute-start.7
  13.2 0.9 collective-permute-done.3.refs_0_.refs_4_
  14.1 1.7 %collective-permute-start.12 = (bf16[64,2176]{1,0:T(8,128)(2,1)}, bf16[64,2176]{1,0:T(8,128)(2,1)S(1)}, u32[]{:S(2)}, u32[]{:S(2)}) collective-permute-start(bf16[64,2176]{1,0:T(8,128)(2,1)} %get-tuple-element.36.refs_4_.refs_0_), channel_id=1, source_target_pairs={{0,8},{1,9},{2,10},{3,11},{4,0},{5,1},{6,2},{7,3},{12,4},{13,5},{1... | collective-permute-start | bytes 835592 | tf_op jit(solution)/shard_map/ppermute | solution.py:59
  15.8 1.5 %collective-permute-done.7 = bf16[192,256]{1,0:T(8,128)(2,1)S(1)} collective-permute-done((bf16[192,256]{1,0:T(8,128)(2,1)S(1)}, bf16[192,256]{1,0:T(8,128)(2,1)S(1)}, u32[]{:S(2)}, u32[]{:S(2)}) %collective-permute-start.7) | collective-permute-done | bytes 98336 | tf_op jit(solution)/shard_map/ppermute | solution.py:63
  17.4 2.6 %collective-permute-start.8 = (bf16[64,2176]{1,0:T(8,128)(2,1)S(1)}, bf16[64,2176]{1,0:T(8,128)(2,1)S(1)}, u32[]{:S(2)}, u32[]{:S(2)}) collective-permute-start(bf16[64,2176]{1,0:T(8,128)(2,1)S(1)} %collective-permute-done.3.refs_0_.refs_4_), channel_id=1, source_target_pairs={{0,4},{1,5},{2,6},{3,7},{4,12},{5,13},{6,14},{7,15},{12,8},{13,9},... | collective-permute-start | bytes 835592 | tf_op jit(solution)/shard_map/ppermute | solution.py:55
  20.0 0.8 collective-permute-start.4
  20.8 2.4 %collective-permute-done.12.refs_4_.refs_12_ = bf16[64,2176]{1,0:T(8,128)(2,1)S(1)} collective-permute-done((bf16[64,2176]{1,0:T(8,128)(2,1)}, bf16[64,2176]{1,0:T(8,128)(2,1)S(1)}, u32[]{:S(2)}, u32[]{:S(2)}) %collective-permute-start.12) | collective-permute-done | bytes 278560 | tf_op jit(solution)/shard_map/ppermute | solution.py:59
  23.3 1.5 %collective-permute-start.13 = (bf16[64,2176]{1,0:T(8,128)(2,1)S(1)}, bf16[64,2176]{1,0:T(8,128)(2,1)S(1)}, u32[]{:S(2)}, u32[]{:S(2)}) collective-permute-start(bf16[64,2176]{1,0:T(8,128)(2,1)S(1)} %collective-permute-done.12.refs_4_.refs_12_), channel_id=1, source_target_pairs={{0,2},{1,3},{2,0},{3,1},{4,6},{5,7},{6,4},{7,5},{12,14},{13,15},{1... | collective-permute-start | bytes 835592 | tf_op jit(solution)/shard_map/ppermute | solution.py:63
  24.8 5.8 %collective-permute-done.8.refs_0_.refs_8_ = bf16[64,2176]{1,0:T(8,128)(2,1)S(1)} collective-permute-done((bf16[64,2176]{1,0:T(8,128)(2,1)S(1)}, bf16[64,2176]{1,0:T(8,128)(2,1)S(1)}, u32[]{:S(2)}, u32[]{:S(2)}) %collective-permute-start.8) | collective-permute-done | bytes 278560 | tf_op jit(solution)/shard_map/ppermute | solution.py:55
  30.5 0.0 collective-permute-start.10
  30.6 0.5 collective-permute-start.5
  31.1 0.0 collective-permute-start.2
  31.1 0.5 collective-permute-start.6
  31.6 1.8 %collective-permute-done.13.refs_5_.refs_13_ = bf16[64,2176]{1,0:T(8,128)(2,1)S(1)} collective-permute-done((bf16[64,2176]{1,0:T(8,128)(2,1)S(1)}, bf16[64,2176]{1,0:T(8,128)(2,1)S(1)}, u32[]{:S(2)}, u32[]{:S(2)}) %collective-permute-start.13) | collective-permute-done | bytes 278560 | tf_op jit(solution)/shard_map/ppermute | solution.py:63
  33.4 1.1 %collective-permute-start.9 = (bf16[64,2176]{1,0:T(8,128)(2,1)S(1)}, bf16[64,2176]{1,0:T(8,128)(2,1)S(1)}, u32[]{:S(2)}, u32[]{:S(2)}) collective-permute-start(bf16[64,2176]{1,0:T(8,128)(2,1)S(1)} %collective-permute-done.8.refs_0_.refs_8_), channel_id=1, source_target_pairs={{0,2},{1,3},{2,0},{3,1},{4,6},{5,7},{6,4},{7,5},{12,14},{13,15},{1... | collective-permute-start | bytes 835592 | tf_op jit(solution)/shard_map/ppermute | solution.py:63
  34.5 2.7 %collective-permute-start.16 = (bf16[384,256]{1,0:T(8,128)(2,1)S(1)}, bf16[384,256]{1,0:T(8,128)(2,1)S(1)}, u32[]{:S(2)}, u32[]{:S(2)}) collective-permute-start(bf16[384,256]{1,0:T(8,128)(2,1)S(1)} %pad_maximum_fusion.refs_16_), channel_id=1, source_target_pairs={{0,4},{1,5},{2,6},{3,7},{4,12},{5,13},{6,14},{7,15},{12,8},{13,9},... | collective-permute-start | bytes 589832 | tf_op jit(solution)/shard_map/ppermute | solution.py:55
  37.2 4.1 %experts.2 = (bf16[128,2048]{1,0:T(8,128)(2,1)S(1)}, bf16[128,2048]{1,0:T(8,128)(2,1)S(1)}, bf16[256,2048]{1,0:T(8,128)(2,1)S(1)}) custom-call(bf16[64,2176]{1,0:T(8,128)(2,1)S(1)} %collective-permute-done.3.refs_0_.refs_4_, bf16[64,2176]{1,0:T(8,128)(2,1)S(1)} %collective-permute-done.4.refs_1_.refs_5_, ...), custom_call_target="tpu_custom_call" | custom-call | flops 1 | bytes 1 | tf_op jit(solution)/shard_map/experts/pallas_call | solution.py:259
  41.3 0.3 collective-permute-done.16.refs_18_
  41.6 0.5 collective-permute-start.15
  42.2 0.0 collective-permute-start.11
  42.2 2.1 %collective-permute-done.17 = bf16[256,2048]{1,0:T(8,128)(2,1)S(1)} collective-permute-done((bf16[256,2048]{1,0:T(8,128)(2,1)S(1)}, bf16[256,2048]{1,0:T(8,128)(2,1)S(1)}, u32[]{:S(2)}, u32[]{:S(2)}) %collective-permute-start.17) | collective-permute-done | bytes 1048608 | tf_op jit(solution)/shard_map/ppermute | solution.py:67
  44.3 0.1 add_convert_fusion.6
  44.4 1.0 %collective-permute-start.18 = (bf16[64,2048]{1,0:T(8,128)(2,1)S(1)}, bf16[64,2048]{1,0:T(8,128)(2,1)S(1)}, u32[]{:S(2)}, u32[]{:S(2)}) collective-permute-start(bf16[64,2048]{1,0:T(8,128)(2,1)S(1)} %get-tuple-element.64), channel_id=1, source_target_pairs={{0,2},{1,3},{2,0},{3,1},{4,6},{5,7},{6,4},{7,5},{12,14},{13,15},{1... | collective-permute-start | bytes 786440 | tf_op jit(solution)/shard_map/ppermute | solution.py:63
  45.4 5.8 %collective-permute-start.20 = (bf16[384,256]{1,0:T(8,128)(2,1)S(1)}, bf16[384,256]{1,0:T(8,128)(2,1)S(1)}, u32[]{:S(2)}, u32[]{:S(2)}) collective-permute-start(bf16[384,256]{1,0:T(8,128)(2,1)S(1)} %pad_maximum_fusion.refs_16_), channel_id=1, source_target_pairs={{0,8},{1,9},{2,10},{3,11},{4,0},{5,1},{6,2},{7,3},{12,4},{13,5},{1... | collective-permute-start | bytes 589832 | tf_op jit(solution)/shard_map/ppermute | solution.py:59
  51.2 4.1 %experts.3 = (bf16[128,2048]{1,0:T(8,128)(2,1)S(1)}, bf16[128,2048]{1,0:T(8,128)(2,1)S(1)}, bf16[256,2048]{1,0:T(8,128)(2,1)S(1)}) custom-call(bf16[64,2176]{1,0:T(8,128)(2,1)S(1)} %collective-permute-done.8.refs_0_.refs_8_, bf16[64,2176]{1,0:T(8,128)(2,1)S(1)} %collective-permute-done.9.refs_1_.refs_9_, ...), custom_call_target="tpu_custom_call" | custom-call | flops 1 | bytes 1 | tf_op jit(solution)/shard_map/experts/pallas_call | solution.py:259
  55.4 0.0 copy-start.4
  55.4 1.1 %collective-permute-done.20.refs_22_ = bf16[384,256]{1,0:T(8,128)(2,1)S(1)} collective-permute-done((bf16[384,256]{1,0:T(8,128)(2,1)S(1)}, bf16[384,256]{1,0:T(8,128)(2,1)S(1)}, u32[]{:S(2)}, u32[]{:S(2)}) %collective-permute-start.20) | collective-permute-done | bytes 196640 | tf_op jit(solution)/shard_map/ppermute | solution.py:59
  56.5 6.5 %collective-permute-done.19.refs_20_ = bf16[384,256]{1,0:T(8,128)(2,1)S(1)} collective-permute-done((bf16[384,256]{1,0:T(8,128)(2,1)S(1)}, bf16[384,256]{1,0:T(8,128)(2,1)S(1)}, u32[]{:S(2)}, u32[]{:S(2)}) %collective-permute-start.19) | collective-permute-done | bytes 196640 | tf_op jit(solution)/shard_map/ppermute | solution.py:55
  63.1 0.0 collective-permute-start.21
  63.1 0.1 add_convert_fusion.3
  63.2 0.1 collective-permute-start.28
  63.3 0.6 collective-permute-start.22
  63.8 1.9 %collective-permute-done.21 = bf16[256,2048]{1,0:T(8,128)(2,1)S(1)} collective-permute-done((bf16[256,2048]{1,0:T(8,128)(2,1)S(1)}, bf16[256,2048]{1,0:T(8,128)(2,1)S(1)}, u32[]{:S(2)}, u32[]{:S(2)}) %collective-permute-start.21) | collective-permute-done | bytes 1048608 | tf_op jit(solution)/shard_map/ppermute | solution.py:67
  65.7 0.1 add_convert_fusion.4
  65.9 1.0 %collective-permute-start.27 = (bf16[64,2048]{1,0:T(8,128)(2,1)S(1)}, bf16[64,2048]{1,0:T(8,128)(2,1)S(1)}, u32[]{:S(2)}, u32[]{:S(2)}) collective-permute-start(bf16[64,2048]{1,0:T(8,128)(2,1)S(1)} %get-tuple-element.63), channel_id=1, source_target_pairs={{0,2},{1,3},{2,0},{3,1},{4,6},{5,7},{6,4},{7,5},{12,14},{13,15},{1... | collective-permute-start | bytes 786440 | tf_op jit(solution)/shard_map/ppermute | solution.py:63
  66.8 0.5 collective-permute-start.24
  67.3 0.0 collective-permute-start.25
  67.3 0.9 %collective-permute-done.23.refs_19_ = bf16[384,256]{1,0:T(8,128)(2,1)S(1)} collective-permute-done((bf16[384,256]{1,0:T(8,128)(2,1)S(1)}, bf16[384,256]{1,0:T(8,128)(2,1)S(1)}, u32[]{:S(2)}, u32[]{:S(2)}) %collective-permute-start.23) | collective-permute-done | bytes 196640 | tf_op jit(solution)/shard_map/ppermute | solution.py:67
  68.3 0.3 collective-permute-done.24.refs_21_
  68.6 0.3 collective-permute-done.25.refs_23_
  68.8 4.6 %values.1 = (bf16[1024,256]{1,0:T(8,128)(2,1)S(1)}, bf16[1024,256]{1,0:T(8,128)(2,1)S(1)}) custom-call(bf16[64,2176]{1,0:T(8,128)(2,1)S(1)} %copy-done.5, bf16[64,2176]{1,0:T(8,128)(2,1)S(1)} %collective-permute-done.refs_5_.refs_1_, bf16[64,2176]{1,0:T(8,128)(2,1)S(1)} %collective-permute-done.1.refs_6_.refs_2_, ...), custom_call_target="tpu_custom_call" | custom-call | flops 1 | bytes 1 | tf_op jit(solution)/shard_map/values/pallas_call | solution.py:325
  73.4 0.0 copy-start.7
  73.4 0.8 collective-permute-done.27
  74.3 0.1 add_convert_fusion.2
  74.4 0.4 collective-permute-start.29
  74.8 0.9 collective-permute-start.26
  75.7 1.8 %attention.4.refs_0_ = bf16[64,4096]{1,0:T(8,128)(2,1)} custom-call(bf16[64,4096]{1,0:T(8,128)(2,1)S(1)} %bitcast.22, bf16[1024,256]{1,0:T(8,128)(2,1)S(1)} %get-tuple-element.54.k_ref, bf16[1024,256]{1,0:T(8,128)(2,1)S(1)} %get-tuple-element.55.v_ref), custom_call_target="tpu_custom_call" | custom-call | flops 1 | bytes 1 | tf_op jit(solution)/shard_map/attention/pallas_call | solution.py:411
  77.6 1.8 %attention.5.refs_0_ = bf16[64,4096]{1,0:T(8,128)(2,1)} custom-call(bf16[64,4096]{1,0:T(8,128)(2,1)S(1)} %bitcast.23, bf16[1024,256]{1,0:T(8,128)(2,1)S(1)} %get-tuple-element.54.k_ref, bf16[1024,256]{1,0:T(8,128)(2,1)S(1)} %get-tuple-element.55.v_ref, bf16[64,4096]{1,0:T(8,128)(2,1)} %attention.4.refs_0_), custom_call_target="tpu_custom_call", output_to_operand_aliasing={{}: (3, {})} | custom-call | flops 1 | bytes 1 | tf_op jit(solution)/shard_map/attention/pallas_call | solution.py:411
  79.4 3.8 %collective-permute-done.29 = bf16[64,2048]{1,0:T(8,128)(2,1)S(1)} collective-permute-done((bf16[64,2048]{1,0:T(8,128)(2,1)S(1)}, bf16[64,2048]{1,0:T(8,128)(2,1)S(1)}, u32[]{:S(2)}, u32[]{:S(2)}) %collective-permute-start.29) | collective-permute-done | bytes 262176 | tf_op jit(solution)/shard_map/ppermute | solution.py:55
  83.2 0.1 add_convert_fusion.1
  83.3 1.2 %collective-permute-start.31 = (bf16[64,2048]{1,0:T(8,128)(2,1)S(1)}, bf16[64,2048]{1,0:T(8,128)(2,1)S(1)}, u32[]{:S(2)}, u32[]{:S(2)}) collective-permute-start(bf16[64,2048]{1,0:T(8,128)(2,1)S(1)} %add_convert_fusion.1), channel_id=1, source_target_pairs={{0,4},{1,5},{2,6},{3,7},{4,12},{5,13},{6,14},{7,15},{12,8},{13,9},... | collective-permute-start | bytes 786440 | tf_op jit(solution)/shard_map/ppermute | solution.py:55
  84.5 1.1 %collective-permute-start.30 = (bf16[64,2048]{1,0:T(8,128)(2,1)S(1)}, bf16[64,2048]{1,0:T(8,128)(2,1)S(1)}, u32[]{:S(2)}, u32[]{:S(2)}) collective-permute-start(bf16[64,2048]{1,0:T(8,128)(2,1)S(1)} %get-tuple-element.60), channel_id=1, source_target_pairs={{0,2},{1,3},{2,0},{3,1},{4,6},{5,7},{6,4},{7,5},{12,14},{13,15},{1... | collective-permute-start | bytes 786440 | tf_op jit(solution)/shard_map/ppermute | solution.py:63
  85.6 1.8 %attention.6.refs_0_ = bf16[64,4096]{1,0:T(8,128)(2,1)} custom-call(bf16[64,4096]{1,0:T(8,128)(2,1)S(1)} %bitcast.24, bf16[1024,256]{1,0:T(8,128)(2,1)S(1)} %get-tuple-element.54.k_ref, bf16[1024,256]{1,0:T(8,128)(2,1)S(1)} %get-tuple-element.55.v_ref, bf16[64,4096]{1,0:T(8,128)(2,1)} %attention.5.refs_0_), custom_call_target="tpu_custom_call", output_to_operand_aliasing={{}: (3, {})} | custom-call | flops 1 | bytes 1 | tf_op jit(solution)/shard_map/attention/pallas_call | solution.py:411
  87.5 1.8 %attention.7 = bf16[64,4096]{1,0:T(8,128)(2,1)} custom-call(bf16[64,4096]{1,0:T(8,128)(2,1)S(1)} %bitcast.25, bf16[1024,256]{1,0:T(8,128)(2,1)S(1)} %get-tuple-element.54.k_ref, bf16[1024,256]{1,0:T(8,128)(2,1)S(1)} %get-tuple-element.55.v_ref, bf16[64,4096]{1,0:T(8,128)(2,1)} %attention.6.refs_0_), custom_call_target="tpu_custom_call", output_to_operand_aliasing={{}: (3, {})} | custom-call | flops 1 | bytes 1 | tf_op jit(solution)/shard_map/attention/pallas_call | solution.py:411
  89.3 1.7 %collective-permute-done.31 = bf16[64,2048]{1,0:T(8,128)(2,1)S(1)} collective-permute-done((bf16[64,2048]{1,0:T(8,128)(2,1)S(1)}, bf16[64,2048]{1,0:T(8,128)(2,1)S(1)}, u32[]{:S(2)}, u32[]{:S(2)}) %collective-permute-start.31) | collective-permute-done | bytes 262176 | tf_op jit(solution)/shard_map/ppermute | solution.py:55
  91.0 0.9 fusion
  (32 shorter events, 0.1 us)
Async XLA Ops:
  2.5 4.6 %collective-permute-start.1 = (bf16[64,2176]{1,0:T(8,128)(2,1)}, bf16[64,2176]{1,0:T(8,128)(2,1)S(1)}, u32[]{:S(2)}, u32[]{:S(2)}) collective-permute-start(bf16[64,2176]{1,0:T(8,128)(2,1)} %get-tuple-element.36.refs_4_.refs_0_), channel_id=1, source_target_pairs={{0,1},{1,0},{2,3},{3,2},{4,5},{5,4},{6,7},{7,6},{12,13},{13,12},{1... | collective-permute-start | bytes 835592 | tf_op jit(solution)/shard_map/ppermute | solution.py:67
  2.9 11.1 %collective-permute-start.3 = (bf16[64,2176]{1,0:T(8,128)(2,1)}, bf16[64,2176]{1,0:T(8,128)(2,1)S(1)}, u32[]{:S(2)}, u32[]{:S(2)}) collective-permute-start(bf16[64,2176]{1,0:T(8,128)(2,1)} %get-tuple-element.36.refs_4_.refs_0_), channel_id=1, source_target_pairs={{0,4},{1,5},{2,6},{3,7},{4,12},{5,13},{6,14},{7,15},{12,8},{13,9},... | collective-permute-start | bytes 835592 | tf_op jit(solution)/shard_map/ppermute | solution.py:55
  5.5 11.8 %collective-permute-start = (bf16[64,2176]{1,0:T(8,128)(2,1)}, bf16[64,2176]{1,0:T(8,128)(2,1)S(1)}, u32[]{:S(2)}, u32[]{:S(2)}) collective-permute-start(bf16[64,2176]{1,0:T(8,128)(2,1)} %get-tuple-element.36.refs_4_.refs_0_), channel_id=1, source_target_pairs={{0,2},{1,3},{2,0},{3,1},{4,6},{5,7},{6,4},{7,5},{12,14},{13,15},{1... | collective-permute-start | bytes 835592 | tf_op jit(solution)/shard_map/ppermute | solution.py:63
  7.0 2.8 %copy-start = (bf16[1,2048,1536]{2,1,0:T(8,128)(2,1)S(1)}, bf16[1,2048,1536]{2,1,0:T(8,128)(2,1)}, u32[]{:S(2)}) copy-start(bf16[1,2048,1536]{2,1,0:T(8,128)(2,1)} %param.16) | copy-start | bytes 18874372
  9.8 1.9 %copy-start.2 = (bf16[1,768,2048]{2,1,0:T(8,128)(2,1)S(1)}, bf16[1,768,2048]{2,1,0:T(8,128)(2,1)}, u32[]{:S(2)}) copy-start(bf16[1,768,2048]{2,1,0:T(8,128)(2,1)} %param.17) | copy-start | bytes 9437188
  11.7 0.9 copy-start.6
  12.6 24.5 %copy-start.1 = (bf16[1,2048,1536]{2,1,0:T(8,128)(2,1)S(1)}, bf16[1,2048,1536]{2,1,0:T(8,128)(2,1)}, u32[]{:S(2)}) copy-start(bf16[1,2048,1536]{2,1,0:T(8,128)(2,1)} %param.16) | copy-start | bytes 18874372
  12.6 24.5 %copy-start.3 = (bf16[1,768,2048]{2,1,0:T(8,128)(2,1)S(1)}, bf16[1,768,2048]{2,1,0:T(8,128)(2,1)}, u32[]{:S(2)}) copy-start(bf16[1,768,2048]{2,1,0:T(8,128)(2,1)} %param.17) | copy-start | bytes 9437188
  12.6 24.5 %copy-start.5 = (bf16[64,2176]{1,0:T(8,128)(2,1)S(1)}, bf16[64,2176]{1,0:T(8,128)(2,1)}, u32[]{:S(2)}) copy-start(bf16[64,2176]{1,0:T(8,128)(2,1)} %get-tuple-element.36.refs_4_.refs_0_) | copy-start | bytes 835588
  12.6 4.7 %collective-permute-start.7 = (bf16[192,256]{1,0:T(8,128)(2,1)S(1)}, bf16[192,256]{1,0:T(8,128)(2,1)S(1)}, u32[]{:S(2)}, u32[]{:S(2)}) collective-permute-start(bf16[192,256]{1,0:T(8,128)(2,1)S(1)} %hold_weights.1), channel_id=1, source_target_pairs={{0,2},{1,3},{2,0},{3,1},{4,6},{5,7},{6,4},{7,5},{12,14},{13,15},{1... | collective-permute-start | bytes 294920 | tf_op jit(solution)/shard_map/ppermute | solution.py:63
  14.1 9.2 %collective-permute-start.12 = (bf16[64,2176]{1,0:T(8,128)(2,1)}, bf16[64,2176]{1,0:T(8,128)(2,1)S(1)}, u32[]{:S(2)}, u32[]{:S(2)}) collective-permute-start(bf16[64,2176]{1,0:T(8,128)(2,1)} %get-tuple-element.36.refs_4_.refs_0_), channel_id=1, source_target_pairs={{0,8},{1,9},{2,10},{3,11},{4,0},{5,1},{6,2},{7,3},{12,4},{13,5},{1... | collective-permute-start | bytes 835592 | tf_op jit(solution)/shard_map/ppermute | solution.py:59
  17.4 13.2 %collective-permute-start.8 = (bf16[64,2176]{1,0:T(8,128)(2,1)S(1)}, bf16[64,2176]{1,0:T(8,128)(2,1)S(1)}, u32[]{:S(2)}, u32[]{:S(2)}) collective-permute-start(bf16[64,2176]{1,0:T(8,128)(2,1)S(1)} %collective-permute-done.3.refs_0_.refs_4_), channel_id=1, source_target_pairs={{0,4},{1,5},{2,6},{3,7},{4,12},{5,13},{6,14},{7,15},{12,8},{13,9},... | collective-permute-start | bytes 835592 | tf_op jit(solution)/shard_map/ppermute | solution.py:55
  20.0 11.0 %collective-permute-start.4 = (bf16[64,2176]{1,0:T(8,128)(2,1)S(1)}, bf16[64,2176]{1,0:T(8,128)(2,1)S(1)}, u32[]{:S(2)}, u32[]{:S(2)}) collective-permute-start(bf16[64,2176]{1,0:T(8,128)(2,1)S(1)} %collective-permute-done.3.refs_0_.refs_4_), channel_id=1, source_target_pairs={{0,2},{1,3},{2,0},{3,1},{4,6},{5,7},{6,4},{7,5},{12,14},{13,15},{1... | collective-permute-start | bytes 835592 | tf_op jit(solution)/shard_map/ppermute | solution.py:63
  23.3 7.8 %collective-permute-start.14 = (bf16[64,2176]{1,0:T(8,128)(2,1)S(1)}, bf16[64,2176]{1,0:T(8,128)(2,1)S(1)}, u32[]{:S(2)}, u32[]{:S(2)}) collective-permute-start(bf16[64,2176]{1,0:T(8,128)(2,1)S(1)} %collective-permute-done.12.refs_4_.refs_12_), channel_id=1, source_target_pairs={{0,1},{1,0},{2,3},{3,2},{4,5},{5,4},{6,7},{7,6},{12,13},{13,12},{1... | collective-permute-start | bytes 835592 | tf_op jit(solution)/shard_map/ppermute | solution.py:67
  23.3 10.1 %collective-permute-start.13 = (bf16[64,2176]{1,0:T(8,128)(2,1)S(1)}, bf16[64,2176]{1,0:T(8,128)(2,1)S(1)}, u32[]{:S(2)}, u32[]{:S(2)}) collective-permute-start(bf16[64,2176]{1,0:T(8,128)(2,1)S(1)} %collective-permute-done.12.refs_4_.refs_12_), channel_id=1, source_target_pairs={{0,2},{1,3},{2,0},{3,1},{4,6},{5,7},{6,4},{7,5},{12,14},{13,15},{1... | collective-permute-start | bytes 835592 | tf_op jit(solution)/shard_map/ppermute | solution.py:63
  30.5 3.9 %collective-permute-start.10 = (bf16[64,2176]{1,0:T(8,128)(2,1)S(1)}, bf16[64,2176]{1,0:T(8,128)(2,1)S(1)}, u32[]{:S(2)}, u32[]{:S(2)}) collective-permute-start(bf16[64,2176]{1,0:T(8,128)(2,1)S(1)} %collective-permute-done.8.refs_0_.refs_8_), channel_id=1, source_target_pairs={{0,1},{1,0},{2,3},{3,2},{4,5},{5,4},{6,7},{7,6},{12,13},{13,12},{1... | collective-permute-start | bytes 835592 | tf_op jit(solution)/shard_map/ppermute | solution.py:67
  30.6 6.6 %collective-permute-start.5 = (bf16[64,2176]{1,0:T(8,128)(2,1)S(1)}, bf16[64,2176]{1,0:T(8,128)(2,1)S(1)}, u32[]{:S(2)}, u32[]{:S(2)}) collective-permute-start(bf16[64,2176]{1,0:T(8,128)(2,1)S(1)} %collective-permute-done.3.refs_0_.refs_4_), channel_id=1, source_target_pairs={{0,1},{1,0},{2,3},{3,2},{4,5},{5,4},{6,7},{7,6},{12,13},{13,12},{1... | collective-permute-start | bytes 835592 | tf_op jit(solution)/shard_map/ppermute | solution.py:67
  31.1 6.1 %collective-permute-start.2 = (bf16[64,2176]{1,0:T(8,128)(2,1)S(1)}, bf16[64,2176]{1,0:T(8,128)(2,1)S(1)}, u32[]{:S(2)}, u32[]{:S(2)}) collective-permute-start(bf16[64,2176]{1,0:T(8,128)(2,1)S(1)} %collective-permute-done.refs_5_.refs_1_), channel_id=1, source_target_pairs={{0,1},{1,0},{2,3},{3,2},{4,5},{5,4},{6,7},{7,6},{12,13},{13,12},{1... | collective-permute-start | bytes 835592 | tf_op jit(solution)/shard_map/ppermute | solution.py:67
  31.1 6.0 %collective-permute-start.6 = (bf16[64,2176]{1,0:T(8,128)(2,1)S(1)}, bf16[64,2176]{1,0:T(8,128)(2,1)S(1)}, u32[]{:S(2)}, u32[]{:S(2)}) collective-permute-start(bf16[64,2176]{1,0:T(8,128)(2,1)S(1)} %collective-permute-done.4.refs_1_.refs_5_), channel_id=1, source_target_pairs={{0,1},{1,0},{2,3},{3,2},{4,5},{5,4},{6,7},{7,6},{12,13},{13,12},{1... | collective-permute-start | bytes 835592 | tf_op jit(solution)/shard_map/ppermute | solution.py:67
  33.4 8.3 %collective-permute-start.9 = (bf16[64,2176]{1,0:T(8,128)(2,1)S(1)}, bf16[64,2176]{1,0:T(8,128)(2,1)S(1)}, u32[]{:S(2)}, u32[]{:S(2)}) collective-permute-start(bf16[64,2176]{1,0:T(8,128)(2,1)S(1)} %collective-permute-done.8.refs_0_.refs_8_), channel_id=1, source_target_pairs={{0,2},{1,3},{2,0},{3,1},{4,6},{5,7},{6,4},{7,5},{12,14},{13,15},{1... | collective-permute-start | bytes 835592 | tf_op jit(solution)/shard_map/ppermute | solution.py:63
  34.5 7.2 %collective-permute-start.16 = (bf16[384,256]{1,0:T(8,128)(2,1)S(1)}, bf16[384,256]{1,0:T(8,128)(2,1)S(1)}, u32[]{:S(2)}, u32[]{:S(2)}) collective-permute-start(bf16[384,256]{1,0:T(8,128)(2,1)S(1)} %pad_maximum_fusion.refs_16_), channel_id=1, source_target_pairs={{0,4},{1,5},{2,6},{3,7},{4,12},{5,13},{6,14},{7,15},{12,8},{13,9},... | collective-permute-start | bytes 589832 | tf_op jit(solution)/shard_map/ppermute | solution.py:55
  41.6 2.7 %collective-permute-start.17 = (bf16[256,2048]{1,0:T(8,128)(2,1)S(1)}, bf16[256,2048]{1,0:T(8,128)(2,1)S(1)}, u32[]{:S(2)}, u32[]{:S(2)}) collective-permute-start(bf16[256,2048]{1,0:T(8,128)(2,1)S(1)} %get-tuple-element.41), channel_id=1, source_target_pairs={{0,1},{1,0},{2,3},{3,2},{4,5},{5,4},{6,7},{7,6},{12,13},{13,12},{1... | collective-permute-start | bytes 3145736 | tf_op jit(solution)/shard_map/ppermute | solution.py:67
  41.6 9.6 %collective-permute-start.15 = (bf16[64,2176]{1,0:T(8,128)(2,1)S(1)}, bf16[64,2176]{1,0:T(8,128)(2,1)S(1)}, u32[]{:S(2)}, u32[]{:S(2)}) collective-permute-start(bf16[64,2176]{1,0:T(8,128)(2,1)S(1)} %collective-permute-done.13.refs_5_.refs_13_), channel_id=1, source_target_pairs={{0,1},{1,0},{2,3},{3,2},{4,5},{5,4},{6,7},{7,6},{12,13},{13,12},{1... | collective-permute-start | bytes 835592 | tf_op jit(solution)/shard_map/ppermute | solution.py:67
  42.2 9.1 %collective-permute-start.11 = (bf16[64,2176]{1,0:T(8,128)(2,1)S(1)}, bf16[64,2176]{1,0:T(8,128)(2,1)S(1)}, u32[]{:S(2)}, u32[]{:S(2)}) collective-permute-start(bf16[64,2176]{1,0:T(8,128)(2,1)S(1)} %collective-permute-done.9.refs_1_.refs_9_), channel_id=1, source_target_pairs={{0,1},{1,0},{2,3},{3,2},{4,5},{5,4},{6,7},{7,6},{12,13},{13,12},{1... | collective-permute-start | bytes 835592 | tf_op jit(solution)/shard_map/ppermute | solution.py:67
  44.4 18.6 %collective-permute-start.18 = (bf16[64,2048]{1,0:T(8,128)(2,1)S(1)}, bf16[64,2048]{1,0:T(8,128)(2,1)S(1)}, u32[]{:S(2)}, u32[]{:S(2)}) collective-permute-start(bf16[64,2048]{1,0:T(8,128)(2,1)S(1)} %get-tuple-element.64), channel_id=1, source_target_pairs={{0,2},{1,3},{2,0},{3,1},{4,6},{5,7},{6,4},{7,5},{12,14},{13,15},{1... | collective-permute-start | bytes 786440 | tf_op jit(solution)/shard_map/ppermute | solution.py:63
  45.4 11.1 %collective-permute-start.20 = (bf16[384,256]{1,0:T(8,128)(2,1)S(1)}, bf16[384,256]{1,0:T(8,128)(2,1)S(1)}, u32[]{:S(2)}, u32[]{:S(2)}) collective-permute-start(bf16[384,256]{1,0:T(8,128)(2,1)S(1)} %pad_maximum_fusion.refs_16_), channel_id=1, source_target_pairs={{0,8},{1,9},{2,10},{3,11},{4,0},{5,1},{6,2},{7,3},{12,4},{13,5},{1... | collective-permute-start | bytes 589832 | tf_op jit(solution)/shard_map/ppermute | solution.py:59
  51.2 11.8 %collective-permute-start.19 = (bf16[384,256]{1,0:T(8,128)(2,1)S(1)}, bf16[384,256]{1,0:T(8,128)(2,1)S(1)}, u32[]{:S(2)}, u32[]{:S(2)}) collective-permute-start(bf16[384,256]{1,0:T(8,128)(2,1)S(1)} %collective-permute-done.16.refs_18_), channel_id=1, source_target_pairs={{0,4},{1,5},{2,6},{3,7},{4,12},{5,13},{6,14},{7,15},{12,8},{13,9},... | collective-permute-start | bytes 589832 | tf_op jit(solution)/shard_map/ppermute | solution.py:55
  55.4 20.4 %copy-start.4 = (bf16[64,1,4096]{2,0,1:T(8,128)(2,1)S(1)}, bf16[64,1,4096]{2,0,1:T(8,128)(2,1)}, u32[]{:S(2)}) copy-start(bf16[64,1,4096]{2,0,1:T(8,128)(2,1)} %param.10) | copy-start | bytes 1572868
  63.1 2.7 %collective-permute-start.21 = (bf16[256,2048]{1,0:T(8,128)(2,1)S(1)}, bf16[256,2048]{1,0:T(8,128)(2,1)S(1)}, u32[]{:S(2)}, u32[]{:S(2)}) collective-permute-start(bf16[256,2048]{1,0:T(8,128)(2,1)S(1)} %get-tuple-element.46), channel_id=1, source_target_pairs={{0,1},{1,0},{2,3},{3,2},{4,5},{5,4},{6,7},{7,6},{12,13},{13,12},{1... | collective-permute-start | bytes 3145736 | tf_op jit(solution)/shard_map/ppermute | solution.py:67
  63.2 10.2 %collective-permute-start.28 = (bf16[64,2048]{1,0:T(8,128)(2,1)S(1)}, bf16[64,2048]{1,0:T(8,128)(2,1)S(1)}, u32[]{:S(2)}, u32[]{:S(2)}) collective-permute-start(bf16[64,2048]{1,0:T(8,128)(2,1)S(1)} %add_convert_fusion.3), channel_id=1, source_target_pairs={{0,4},{1,5},{2,6},{3,7},{4,12},{5,13},{6,14},{7,15},{12,8},{13,9},... | collective-permute-start | bytes 786440 | tf_op jit(solution)/shard_map/ppermute | solution.py:55
  63.3 4.1 %collective-permute-start.22 = (bf16[384,256]{1,0:T(8,128)(2,1)S(1)}, bf16[384,256]{1,0:T(8,128)(2,1)S(1)}, u32[]{:S(2)}, u32[]{:S(2)}) collective-permute-start(bf16[384,256]{1,0:T(8,128)(2,1)S(1)} %pad_maximum_fusion.refs_16_), channel_id=1, source_target_pairs={{0,1},{1,0},{2,3},{3,2},{4,5},{5,4},{6,7},{7,6},{12,13},{13,12},{1... | collective-permute-start | bytes 589832 | tf_op jit(solution)/shard_map/ppermute | solution.py:67
  65.9 8.4 %collective-permute-start.27 = (bf16[64,2048]{1,0:T(8,128)(2,1)S(1)}, bf16[64,2048]{1,0:T(8,128)(2,1)S(1)}, u32[]{:S(2)}, u32[]{:S(2)}) collective-permute-start(bf16[64,2048]{1,0:T(8,128)(2,1)S(1)} %get-tuple-element.63), channel_id=1, source_target_pairs={{0,2},{1,3},{2,0},{3,1},{4,6},{5,7},{6,4},{7,5},{12,14},{13,15},{1... | collective-permute-start | bytes 786440 | tf_op jit(solution)/shard_map/ppermute | solution.py:63
  66.8 1.4 %collective-permute-start.23 = (bf16[384,256]{1,0:T(8,128)(2,1)S(1)}, bf16[384,256]{1,0:T(8,128)(2,1)S(1)}, u32[]{:S(2)}, u32[]{:S(2)}) collective-permute-start(bf16[384,256]{1,0:T(8,128)(2,1)S(1)} %collective-permute-done.16.refs_18_), channel_id=1, source_target_pairs={{0,1},{1,0},{2,3},{3,2},{4,5},{5,4},{6,7},{7,6},{12,13},{13,12},{1... | collective-permute-start | bytes 589832 | tf_op jit(solution)/shard_map/ppermute | solution.py:67
  66.8 1.7 %collective-permute-start.24 = (bf16[384,256]{1,0:T(8,128)(2,1)S(1)}, bf16[384,256]{1,0:T(8,128)(2,1)S(1)}, u32[]{:S(2)}, u32[]{:S(2)}) collective-permute-start(bf16[384,256]{1,0:T(8,128)(2,1)S(1)} %collective-permute-done.19.refs_20_), channel_id=1, source_target_pairs={{0,1},{1,0},{2,3},{3,2},{4,5},{5,4},{6,7},{7,6},{12,13},{13,12},{1... | collective-permute-start | bytes 589832 | tf_op jit(solution)/shard_map/ppermute | solution.py:67
  67.3 1.5 %collective-permute-start.25 = (bf16[384,256]{1,0:T(8,128)(2,1)S(1)}, bf16[384,256]{1,0:T(8,128)(2,1)S(1)}, u32[]{:S(2)}, u32[]{:S(2)}) collective-permute-start(bf16[384,256]{1,0:T(8,128)(2,1)S(1)} %collective-permute-done.20.refs_22_), channel_id=1, source_target_pairs={{0,1},{1,0},{2,3},{3,2},{4,5},{5,4},{6,7},{7,6},{12,13},{13,12},{1... | collective-permute-start | bytes 589832 | tf_op jit(solution)/shard_map/ppermute | solution.py:67
  73.4 17.5 %copy-start.7 = (bf16[64,1,2048]{2,0,1:T(8,128)(2,1)S(1)}, bf16[64,1,2048]{2,0,1:T(8,128)(2,1)}, u32[]{:S(2)}) copy-start(bf16[64,1,2048]{2,0,1:T(8,128)(2,1)} %param.9) | copy-start | bytes 786436
  74.4 8.8 %collective-permute-start.29 = (bf16[64,2048]{1,0:T(8,128)(2,1)S(1)}, bf16[64,2048]{1,0:T(8,128)(2,1)S(1)}, u32[]{:S(2)}, u32[]{:S(2)}) collective-permute-start(bf16[64,2048]{1,0:T(8,128)(2,1)S(1)} %add_convert_fusion.2), channel_id=1, source_target_pairs={{0,4},{1,5},{2,6},{3,7},{4,12},{5,13},{6,14},{7,15},{12,8},{13,9},... | collective-permute-start | bytes 786440 | tf_op jit(solution)/shard_map/ppermute | solution.py:55
  74.8 8.3 %collective-permute-start.26 = (bf16[64,2048]{1,0:T(8,128)(2,1)S(1)}, bf16[64,2048]{1,0:T(8,128)(2,1)S(1)}, u32[]{:S(2)}, u32[]{:S(2)}) collective-permute-start(bf16[64,2048]{1,0:T(8,128)(2,1)S(1)} %get-tuple-element.62), channel_id=1, source_target_pairs={{0,2},{1,3},{2,0},{3,1},{4,6},{5,7},{6,4},{7,5},{12,14},{13,15},{1... | collective-permute-start | bytes 786440 | tf_op jit(solution)/shard_map/ppermute | solution.py:63
  83.3 7.7 %collective-permute-start.31 = (bf16[64,2048]{1,0:T(8,128)(2,1)S(1)}, bf16[64,2048]{1,0:T(8,128)(2,1)S(1)}, u32[]{:S(2)}, u32[]{:S(2)}) collective-permute-start(bf16[64,2048]{1,0:T(8,128)(2,1)S(1)} %add_convert_fusion.1), channel_id=1, source_target_pairs={{0,4},{1,5},{2,6},{3,7},{4,12},{5,13},{6,14},{7,15},{12,8},{13,9},... | collective-permute-start | bytes 786440 | tf_op jit(solution)/shard_map/ppermute | solution.py:55
  84.5 6.5 %collective-permute-start.30 = (bf16[64,2048]{1,0:T(8,128)(2,1)S(1)}, bf16[64,2048]{1,0:T(8,128)(2,1)S(1)}, u32[]{:S(2)}, u32[]{:S(2)}) collective-permute-start(bf16[64,2048]{1,0:T(8,128)(2,1)S(1)} %get-tuple-element.60), channel_id=1, source_target_pairs={{0,2},{1,3},{2,0},{3,1},{4,6},{5,7},{6,4},{7,5},{12,14},{13,15},{1... | collective-permute-start | bytes 786440 | tf_op jit(solution)/shard_map/ppermute | solution.py:63

commit v11 on v5

--- a/solution.py
+++ b/solution.py
@@ -137,32 +137,44 @@
     return [pltpu.with_memory_space_constraint(x, pltpu.VMEM) for x in arrays]
 
 
-def expert_kernel(top, tok_rows, capacity, sources, targets, *refs):
+def expert_kernel(top, tok_rows, capacity, direct, sources, targets, *refs):
     inputs = 1 + max(s[0] for group in sources for s in group)
     outputs = 1 + max(t[0] for group in targets for t in group)
     x_hbm = refs[:inputs]
     up_ref, down_ref = refs[inputs : inputs + 2]
     out_hbm = refs[inputs + 2 : inputs + 2 + outputs]
-    (
-        x_buf,
-        slot_rows,
-        slot_gates,
-        places,
-        hidden,
-        result,
-        x_sem,
-        out_sem,
-    ) = refs[inputs + 2 + outputs :]
-    groups, rows, packed = x_buf.shape
-    width = packed - META
+    slot_rows, slot_gates, places, hidden, result, *rest = refs[inputs + 2 + outputs :]
+    groups, rows, _ = places.shape
+    units, width = down_ref.shape
+    packed = width + META
     slots = slot_rows.shape[0] // groups
-    units = down_ref.shape[0]
     tile = 256
     me = lax.axis_index("seq").astype(F32)
+    if direct:
+
+        def read(group, columns):
+            return jnp.concatenate(
+                [x_hbm[operand][:, columns] for operand, _, _ in sources[group]], axis=0
+            )
+
+        def write(group, columns, value):
+            at = 0
+            for operand, first, count in targets[group]:
+                out_hbm[operand][first : first + count, columns] = value[at : at + count]
+                at += count
+
+    else:
+        x_buf, x_sem, out_sem = rest
+
+        def read(group, columns):
+            return x_buf[group, :, columns]
+
+        def write(group, columns, value):
+            x_buf[group, :, columns] = value
 
     def loads(group):
         copies, at = [], 0
-        for number, (operand, first, count) in enumerate(sources[group]):
+        for number, (operand, first, count) in enumerate([] if direct else sources[group]):
             copies.append(
                 pltpu.make_async_copy(
                     x_hbm[operand].at[pl.ds(first, count)],
@@ -175,7 +187,7 @@
 
     def stores(group):
         copies, at = [], 0
-        for number, (operand, first, count) in enumerate(targets[group]):
+        for number, (operand, first, count) in enumerate([] if direct else targets[group]):
             copies.append(
                 pltpu.make_async_copy(
                     x_buf.at[group, pl.ds(at, count), pl.ds(0, width)],
@@ -198,7 +210,7 @@
     for group in range(groups):
         for copy in loads(group):
             copy.wait()
-        meta = x_buf[group, :, width:].astype(F32).T
+        meta = read(group, slice(width, packed)).astype(F32).T
         gate = jnp.zeros((1, rows), F32)
         named = jnp.zeros((1, rows), F32)
         for k in range(top):
@@ -219,7 +231,7 @@
         pick = chosen.astype(F32).astype(BF16)
         for at in range(0, width, 512):
             slot_rows[pl.ds(group * slots, slots), at : at + 512] = dot(
-                pick, x_buf[group, :, at : at + 512]
+                pick, read(group, slice(at, at + 512))
             ).astype(BF16)
         by_row = jnp.broadcast_to(slot, (META, rows)).T
         spots = lax.broadcasted_iota(jnp.int32, (rows, META), 1).astype(F32)
@@ -234,9 +246,10 @@
         result[:, at : at + tile] = (out * slot_gates[:, 0:1]).astype(BF16)
     for group in range(groups):
         for at in range(0, width, 512):
-            x_buf[group, :, at : at + 512] = dot(
+            placed = dot(
                 places[group, :, :slots], result[pl.ds(group * slots, slots), at : at + 512]
-            ).astype(BF16)
+            )
+            write(group, slice(at, at + 512), placed.astype(BF16))
         for copy in stores(group):
             copy.start()
     for group in range(groups):
@@ -245,36 +258,41 @@
 
 
 def run_experts(arrays, sources, targets, out_rows, w_gate_up, w_down, top, tok_rows, capacity):
+    direct = len(arrays) > 1
     groups = len(sources)
     rows = sum(count for _, _, count in sources[0])
-    packed = arrays[0].shape[1]
     total = groups * rows
-    width = packed - META
-    units = w_down.shape[0]
+    units, width = w_down.shape
+    packed = width + META
     slots = rows // tok_rows * capacity
     assert slots % 16 == 0 and slots <= META and units % 256 == 0 and width % 512 == 0
     all_slots = groups * slots
-    weights = in_vmem(w_gate_up, w_down)
     held = 2 * total * (packed + META) + all_slots * (4 * width + 2 * units + 4 * META)
-    return pl.pallas_call(
-        functools.partial(expert_kernel, top, tok_rows, capacity, sources, targets),
-        out_shape=[jax.ShapeDtypeStruct((count, width), BF16) for count in out_rows],
-        in_specs=[ANY] * len(arrays) + [IN_VMEM] * 2,
-        out_specs=[ANY] * len(out_rows),
-        scratch_shapes=[
+    scratch = [
+        pltpu.VMEM((all_slots, width), BF16),
+        pltpu.VMEM((all_slots, META), F32),
+        pltpu.VMEM((groups, rows, META), BF16),
+        pltpu.VMEM((all_slots, units), BF16),
+        pltpu.VMEM((all_slots, width), BF16),
+    ]
+    if not direct:
+        scratch += [
             pltpu.VMEM((groups, rows, packed), BF16),
-            pltpu.VMEM((all_slots, width), BF16),
-            pltpu.VMEM((all_slots, META), F32),
-            pltpu.VMEM((groups, rows, META), BF16),
-            pltpu.VMEM((all_slots, units), BF16),
-            pltpu.VMEM((all_slots, width), BF16),
             pltpu.SemaphoreType.DMA((groups, max(len(s) for s in sources))),
             pltpu.SemaphoreType.DMA((groups, max(len(t) for t in targets))),
-        ],
+        ]
+    shape = pltpu.VMEM if direct else jax.ShapeDtypeStruct
+    place = IN_VMEM if direct else ANY
+    return pl.pallas_call(
+        functools.partial(expert_kernel, top, tok_rows, capacity, direct, sources, targets),
+        out_shape=[shape((count, width), BF16) for count in out_rows],
+        in_specs=[place] * len(arrays) + [IN_VMEM] * 2,
+        out_specs=[place] * len(out_rows),
+        scratch_shapes=scratch,
         compiler_params=pltpu.CompilerParams(vmem_limit_bytes=held + 8 * 2**20),
         cost_estimate=SHORT,
         name="experts",
-    )(*arrays, *weights)
+    )(*(in_vmem(*arrays) if direct else arrays), *in_vmem(w_gate_up, w_down))
 
 
 def value_kernel(key_rows, blocks, small_blocks, *refs):
@@ -494,9 +512,9 @@
         return send
 
     theirs = [None] * LINE
-    experts(1, 0, [line[2], crossed[3]], [crossed[2], pairs[1]])
+    experts(1, 0, [line[2], crossed[3]], [crossed[2], pairs[1], pairs[3]])
     theirs[1] = across(crossing[1])
-    send = experts(2, 3, [crossing[0], crossing[1]], [theirs[1], pairs[2], pairs[3]])
+    send = experts(2, 3, [crossing[0], crossing[1]], [theirs[1], pairs[2]])
     total = summed(*mine[1], after(theirs[1], send))
     moving = forward(total)
     smalls = []

time: 84.9 us -> 83.8 us (0.987)
  Pallas kernels: 22 us -> 20.2 us
  waiting for transfers between devices: 27.5 us -> 29.1 us
    ppermute x2, waiting for transfers between devices: 3.29 us -> 6.87 us  [backward(): return lax.ppermute(x, 'seq', ring_steps(LINE - 1))]
    ppermute x7, waiting for transfers between devices: 16.9 us -> 14.6 us  [forward(): return lax.ppermute(x, 'seq', ring_steps(1))]
    pallas_call x2, Pallas kernels: 8.25 us -> 6.36 us  [run_experts(): pl.pallas_call(functools.partial(expert_kernel, top, tok_rows, capacity,...]
    ppermute x9, starting transfers between devices: 10.3 us -> 9.34 us  [across(): return lax.ppermute(x, 'seq', swaps(1, 0))]
  transfers between devices with their start and end apart: 32 -> 32, of which waited for: 14 -> 16; matrix products, arithmetic and copies ran while one was open for 0% -> 0% of each run, Pallas kernels for 24% -> 22%
where the time goes in v11:
time: 83.8 us; the launch traced here: 83.6 us
  waiting for transfers between devices  29.1 us (35%)
  starting transfers between devices  26.5 us (32%)
  Pallas kernels  20.2 us (24%)
  local copies, waits for them, and re-layouts  5.59 us (7%)
  other arithmetic  1.5 us (2%)
    ppermute x7, waiting for transfers between devices, forward(): return lax.ppermute(x, 'seq', ring_steps(1))  14.6 us
    ppermute x7, starting transfers between devices, forward(): return lax.ppermute(x, 'seq', ring_steps(1))  11.4 us
    ppermute x9, starting transfers between devices, across(): return lax.ppermute(x, 'seq', swaps(1, 0))  9.34 us
    pallas_call x4, Pallas kernels, attend_part(): pl.pallas_call(functools.partial(attention_kernel, chunk), grid=(1,), out...  7.34 us
    ppermute x2, waiting for transfers between devices, backward(): return lax.ppermute(x, 'seq', ring_steps(LINE - 1))  6.87 us
    pallas_call x2, Pallas kernels, run_experts(): pl.pallas_call(functools.partial(expert_kernel, top, tok_rows, capacity,...  6.36 us
    unnamed x16, local copies, waits for them, and re-layouts  5.59 us
    ppermute x14, waiting for transfers between devices, other_core(): return lax.ppermute(x, 'seq', swaps(0, 1))  5.55 us
  transfers between devices with their start and end apart: 32, of which 16 were waited for; matrix products, arithmetic and copies ran while one was open for 0% of the time, Pallas kernels for 22%

profile of v11, /device:TPU:0, one launch (start us, length us, event | category | flops | bytes accessed | tf_op | source)
XLA Modules:
  0.0 83.6 jit_solution(11884562124543389534)
XLA Ops:
  0.6 1.9 %normalize_and_pack.1 = (bf16[64,2176]{1,0:T(8,128)(2,1)}, bf16[192,256]{1,0:T(8,128)(2,1)}) custom-call(bf16[64,2048]{1,0:T(8,128)(2,1)} %bitcast.27, f32[1,2048]{1,0:T(1,128)} %bitcast.29, s32[4,64]{1,0:T(4,128)} %bitcast.30, f32[4,64]{1,0:T(4,128)} %bitcast.31, bf16[64,256]{1,0:T(8,128)(2,1)} %bitcast.28, bf16[128,256]{1,0:T(8,128)(2,1)} %weight_ref.1), custom_call_target="tpu_custom_call" | custom-call | flops 1 | bytes 1 | tf_op jit(solution)/shard_map/normalize_and_pack/pallas_call | solution.py:108
  2.5 0.5 collective-permute-start.1
  2.9 2.6 %collective-permute-start.3 = (bf16[64,2176]{1,0:T(8,128)(2,1)}, bf16[64,2176]{1,0:T(8,128)(2,1)S(1)}, u32[]{:S(2)}, u32[]{:S(2)}) collective-permute-start(bf16[64,2176]{1,0:T(8,128)(2,1)} %get-tuple-element.31.refs_4_.refs_0_), channel_id=1, source_target_pairs={{0,4},{1,5},{2,6},{3,7},{4,12},{5,13},{6,14},{7,15},{12,8},{13,9},... | collective-permute-start | bytes 835592 | tf_op jit(solution)/shard_map/ppermute | solution.py:55
  5.5 1.5 %collective-permute-start = (bf16[64,2176]{1,0:T(8,128)(2,1)}, bf16[64,2176]{1,0:T(8,128)(2,1)S(1)}, u32[]{:S(2)}, u32[]{:S(2)}) collective-permute-start(bf16[64,2176]{1,0:T(8,128)(2,1)} %get-tuple-element.31.refs_4_.refs_0_), channel_id=1, source_target_pairs={{0,2},{1,3},{2,0},{3,1},{4,6},{5,7},{6,4},{7,5},{12,14},{13,15},{1... | collective-permute-start | bytes 835592 | tf_op jit(solution)/shard_map/ppermute | solution.py:63
  7.0 2.8 %copy-done = bf16[1,2048,1536]{2,1,0:T(8,128)(2,1)S(1)} copy-done((bf16[1,2048,1536]{2,1,0:T(8,128)(2,1)S(1)}, bf16[1,2048,1536]{2,1,0:T(8,128)(2,1)}, u32[]{:S(2)}) %copy-start) | copy-done | bytes 6291480
  9.8 1.9 %copy-done.2 = bf16[1,768,2048]{2,1,0:T(8,128)(2,1)S(1)} copy-done((bf16[1,768,2048]{2,1,0:T(8,128)(2,1)S(1)}, bf16[1,768,2048]{2,1,0:T(8,128)(2,1)}, u32[]{:S(2)}) %copy-start.2) | copy-done | bytes 3145752
  11.7 0.9 %copy-done.6 = bf16[192,256]{1,0:T(8,128)(2,1)S(1)} copy-done((bf16[192,256]{1,0:T(8,128)(2,1)S(1)}, bf16[192,256]{1,0:T(8,128)(2,1)}, u32[]{:S(2)}) %copy-start.6) | copy-done | bytes 98328
  12.6 0.6 collective-permute-start.7
  13.2 2.3 %collective-permute-start.12 = (bf16[64,2176]{1,0:T(8,128)(2,1)}, bf16[64,2176]{1,0:T(8,128)(2,1)S(1)}, u32[]{:S(2)}, u32[]{:S(2)}) collective-permute-start(bf16[64,2176]{1,0:T(8,128)(2,1)} %get-tuple-element.31.refs_4_.refs_0_), channel_id=1, source_target_pairs={{0,8},{1,9},{2,10},{3,11},{4,0},{5,1},{6,2},{7,3},{12,4},{13,5},{1... | collective-permute-start | bytes 835592 | tf_op jit(solution)/shard_map/ppermute | solution.py:59
  15.5 0.6 collective-permute-start.4
  16.1 1.3 %collective-permute-done.7 = bf16[192,256]{1,0:T(8,128)(2,1)S(1)} collective-permute-done((bf16[192,256]{1,0:T(8,128)(2,1)S(1)}, bf16[192,256]{1,0:T(8,128)(2,1)S(1)}, u32[]{:S(2)}, u32[]{:S(2)}) %collective-permute-start.7) | collective-permute-done | bytes 98336 | tf_op jit(solution)/shard_map/ppermute | solution.py:63
  17.4 0.0 collective-permute-done.refs_5_.refs_1_
  17.4 3.7 %collective-permute-start.8 = (bf16[64,2176]{1,0:T(8,128)(2,1)S(1)}, bf16[64,2176]{1,0:T(8,128)(2,1)S(1)}, u32[]{:S(2)}, u32[]{:S(2)}) collective-permute-start(bf16[64,2176]{1,0:T(8,128)(2,1)S(1)} %collective-permute-done.3.refs_0_.refs_4_), channel_id=1, source_target_pairs={{0,4},{1,5},{2,6},{3,7},{4,12},{5,13},{6,14},{7,15},{12,8},{13,9},... | collective-permute-start | bytes 835592 | tf_op jit(solution)/shard_map/ppermute | solution.py:55
  21.0 1.9 %collective-permute-done.12.refs_4_.refs_12_ = bf16[64,2176]{1,0:T(8,128)(2,1)S(1)} collective-permute-done((bf16[64,2176]{1,0:T(8,128)(2,1)}, bf16[64,2176]{1,0:T(8,128)(2,1)S(1)}, u32[]{:S(2)}, u32[]{:S(2)}) %collective-permute-start.12) | collective-permute-done | bytes 278560 | tf_op jit(solution)/shard_map/ppermute | solution.py:59
  22.9 1.2 %collective-permute-start.13 = (bf16[64,2176]{1,0:T(8,128)(2,1)S(1)}, bf16[64,2176]{1,0:T(8,128)(2,1)S(1)}, u32[]{:S(2)}, u32[]{:S(2)}) collective-permute-start(bf16[64,2176]{1,0:T(8,128)(2,1)S(1)} %collective-permute-done.12.refs_4_.refs_12_), channel_id=1, source_target_pairs={{0,2},{1,3},{2,0},{3,1},{4,6},{5,7},{6,4},{7,5},{12,14},{13,15},{1... | collective-permute-start | bytes 835592 | tf_op jit(solution)/shard_map/ppermute | solution.py:63
  24.1 0.5 collective-permute-start.2
  24.6 0.0 collective-permute-start.6
  24.6 5.9 %collective-permute-done.8.refs_0_.refs_8_ = bf16[64,2176]{1,0:T(8,128)(2,1)S(1)} collective-permute-done((bf16[64,2176]{1,0:T(8,128)(2,1)S(1)}, bf16[64,2176]{1,0:T(8,128)(2,1)S(1)}, u32[]{:S(2)}, u32[]{:S(2)}) %collective-permute-start.8) | collective-permute-done | bytes 278560 | tf_op jit(solution)/shard_map/ppermute | solution.py:55
  30.5 1.5 %collective-permute-start.9 = (bf16[64,2176]{1,0:T(8,128)(2,1)S(1)}, bf16[64,2176]{1,0:T(8,128)(2,1)S(1)}, u32[]{:S(2)}, u32[]{:S(2)}) collective-permute-start(bf16[64,2176]{1,0:T(8,128)(2,1)S(1)} %collective-permute-done.8.refs_0_.refs_8_), channel_id=1, source_target_pairs={{0,2},{1,3},{2,0},{3,1},{4,6},{5,7},{6,4},{7,5},{12,14},{13,15},{1... | collective-permute-start | bytes 835592 | tf_op jit(solution)/shard_map/ppermute | solution.py:63
  32.1 0.7 collective-permute-start.17
  32.7 1.9 %collective-permute-start.16 = (bf16[384,256]{1,0:T(8,128)(2,1)S(1)}, bf16[384,256]{1,0:T(8,128)(2,1)S(1)}, u32[]{:S(2)}, u32[]{:S(2)}) collective-permute-start(bf16[384,256]{1,0:T(8,128)(2,1)S(1)} %pad_maximum_fusion.refs_16_), channel_id=1, source_target_pairs={{0,4},{1,5},{2,6},{3,7},{4,12},{5,13},{6,14},{7,15},{12,8},{13,9},... | collective-permute-start | bytes 589832 | tf_op jit(solution)/shard_map/ppermute | solution.py:55
  34.6 3.2 %experts.2 = (bf16[128,2048]{1,0:T(8,128)(2,1)S(1)}, bf16[128,2048]{1,0:T(8,128)(2,1)S(1)}, bf16[256,2048]{1,0:T(8,128)(2,1)S(1)}) custom-call(bf16[64,2176]{1,0:T(8,128)(2,1)S(1)} %collective-permute-done.3.refs_0_.refs_4_, bf16[64,2176]{1,0:T(8,128)(2,1)S(1)} %collective-permute-done.4.refs_1_.refs_5_, ...), custom_call_target="tpu_custom_call" | custom-call | flops 1 | bytes 1 | tf_op jit(solution)/shard_map/experts/pallas_call | solution.py:286
  37.8 5.0 %collective-permute-done.17.refs_22_ = bf16[384,256]{1,0:T(8,128)(2,1)S(1)} collective-permute-done((bf16[384,256]{1,0:T(8,128)(2,1)S(1)}, bf16[384,256]{1,0:T(8,128)(2,1)S(1)}, u32[]{:S(2)}, u32[]{:S(2)}) %collective-permute-start.17) | collective-permute-done | bytes 196640 | tf_op jit(solution)/shard_map/ppermute | solution.py:59
  42.8 0.5 collective-permute-start.14
  43.3 0.1 collective-permute-start.15
  43.4 0.4 collective-permute-start.10
  43.8 0.1 collective-permute-start.11
  43.9 1.6 %collective-permute-done.18 = bf16[256,2048]{1,0:T(8,128)(2,1)S(1)} collective-permute-done((bf16[256,2048]{1,0:T(8,128)(2,1)S(1)}, bf16[256,2048]{1,0:T(8,128)(2,1)S(1)}, u32[]{:S(2)}, u32[]{:S(2)}) %collective-permute-start.18) | collective-permute-done | bytes 1048608 | tf_op jit(solution)/shard_map/ppermute | solution.py:67
  45.5 0.1 add_convert_fusion.6
  45.6 0.6 collective-permute-start.19
  46.2 0.3 collective-permute-start.20
  46.5 0.2 collective-permute-done.10.refs_2_.refs_10_
  46.7 0.4 collective-permute-done.11.refs_3_.refs_11_
  47.1 3.2 %experts.3 = (bf16[128,2048]{1,0:T(8,128)(2,1)S(1)}, bf16[128,2048]{1,0:T(8,128)(2,1)S(1)}, bf16[256,2048]{1,0:T(8,128)(2,1)S(1)}) custom-call(bf16[64,2176]{1,0:T(8,128)(2,1)S(1)} %collective-permute-done.8.refs_0_.refs_8_, bf16[64,2176]{1,0:T(8,128)(2,1)S(1)} %collective-permute-done.9.refs_1_.refs_9_, ...), custom_call_target="tpu_custom_call" | custom-call | flops 1 | bytes 1 | tf_op jit(solution)/shard_map/experts/pallas_call | solution.py:286
  50.3 0.0 copy-start.4
  50.3 3.5 %collective-permute-done.20.refs_20_ = bf16[384,256]{1,0:T(8,128)(2,1)S(1)} collective-permute-done((bf16[384,256]{1,0:T(8,128)(2,1)S(1)}, bf16[384,256]{1,0:T(8,128)(2,1)S(1)}, u32[]{:S(2)}, u32[]{:S(2)}) %collective-permute-start.20) | collective-permute-done | bytes 196640 | tf_op jit(solution)/shard_map/ppermute | solution.py:55
  53.8 0.3 collective-permute-done.19
  54.0 0.1 add_convert_fusion.3
  54.1 0.4 collective-permute-start.28
  54.5 0.3 collective-permute-start.22
  54.8 1.9 %collective-permute-done.21 = bf16[256,2048]{1,0:T(8,128)(2,1)S(1)} collective-permute-done((bf16[256,2048]{1,0:T(8,128)(2,1)S(1)}, bf16[256,2048]{1,0:T(8,128)(2,1)S(1)}, u32[]{:S(2)}, u32[]{:S(2)}) %collective-permute-start.21) | collective-permute-done | bytes 1048608 | tf_op jit(solution)/shard_map/ppermute | solution.py:67
  56.7 0.1 add_convert_fusion.4
  56.8 1.3 %collective-permute-start.27 = (bf16[64,2048]{1,0:T(8,128)(2,1)S(1)}, bf16[64,2048]{1,0:T(8,128)(2,1)S(1)}, u32[]{:S(2)}, u32[]{:S(2)}) collective-permute-start(bf16[64,2048]{1,0:T(8,128)(2,1)S(1)} %get-tuple-element.61), channel_id=1, source_target_pairs={{0,2},{1,3},{2,0},{3,1},{4,6},{5,7},{6,4},{7,5},{12,14},{13,15},{1... | collective-permute-start | bytes 786440 | tf_op jit(solution)/shard_map/ppermute | solution.py:63
  58.1 0.5 collective-permute-start.24
  58.7 0.0 collective-permute-start.25
  58.7 0.9 %collective-permute-done.23.refs_19_ = bf16[384,256]{1,0:T(8,128)(2,1)S(1)} collective-permute-done((bf16[384,256]{1,0:T(8,128)(2,1)S(1)}, bf16[384,256]{1,0:T(8,128)(2,1)S(1)}, u32[]{:S(2)}, u32[]{:S(2)}) %collective-permute-start.23) | collective-permute-done | bytes 196640 | tf_op jit(solution)/shard_map/ppermute | solution.py:67
  59.6 0.3 collective-permute-done.24.refs_21_
  59.9 0.3 collective-permute-done.25.refs_23_
  60.1 4.6 %values.1 = (bf16[1024,256]{1,0:T(8,128)(2,1)S(1)}, bf16[1024,256]{1,0:T(8,128)(2,1)S(1)}) custom-call(bf16[64,2176]{1,0:T(8,128)(2,1)S(1)} %copy-done.5, bf16[64,2176]{1,0:T(8,128)(2,1)S(1)} %collective-permute-done.refs_5_.refs_1_, bf16[64,2176]{1,0:T(8,128)(2,1)S(1)} %collective-permute-done.1.refs_6_.refs_2_, ...), custom_call_target="tpu_custom_call" | custom-call | flops 1 | bytes 1 | tf_op jit(solution)/shard_map/values/pallas_call | solution.py:343
  64.7 0.0 copy-start.7
  64.8 0.5 collective-permute-done.27
  65.2 0.1 add_convert_fusion.2
  65.4 1.1 %collective-permute-start.29 = (bf16[64,2048]{1,0:T(8,128)(2,1)S(1)}, bf16[64,2048]{1,0:T(8,128)(2,1)S(1)}, u32[]{:S(2)}, u32[]{:S(2)}) collective-permute-start(bf16[64,2048]{1,0:T(8,128)(2,1)S(1)} %add_convert_fusion.2), channel_id=1, source_target_pairs={{0,4},{1,5},{2,6},{3,7},{4,12},{5,13},{6,14},{7,15},{12,8},{13,9},... | collective-permute-start | bytes 786440 | tf_op jit(solution)/shard_map/ppermute | solution.py:55
  66.4 0.9 %collective-permute-start.26 = (bf16[64,2048]{1,0:T(8,128)(2,1)S(1)}, bf16[64,2048]{1,0:T(8,128)(2,1)S(1)}, u32[]{:S(2)}, u32[]{:S(2)}) collective-permute-start(bf16[64,2048]{1,0:T(8,128)(2,1)S(1)} %get-tuple-element.60), channel_id=1, source_target_pairs={{0,2},{1,3},{2,0},{3,1},{4,6},{5,7},{6,4},{7,5},{12,14},{13,15},{1... | collective-permute-start | bytes 786440 | tf_op jit(solution)/shard_map/ppermute | solution.py:63
  67.4 1.8 %attention.4.refs_0_ = bf16[64,4096]{1,0:T(8,128)(2,1)} custom-call(bf16[64,4096]{1,0:T(8,128)(2,1)S(1)} %bitcast.22, bf16[1024,256]{1,0:T(8,128)(2,1)S(1)} %get-tuple-element.52.k_ref, bf16[1024,256]{1,0:T(8,128)(2,1)S(1)} %get-tuple-element.53.v_ref), custom_call_target="tpu_custom_call" | custom-call | flops 1 | bytes 1 | tf_op jit(solution)/shard_map/attention/pallas_call | solution.py:429
  69.2 1.8 %attention.5.refs_0_ = bf16[64,4096]{1,0:T(8,128)(2,1)} custom-call(bf16[64,4096]{1,0:T(8,128)(2,1)S(1)} %bitcast.23, bf16[1024,256]{1,0:T(8,128)(2,1)S(1)} %get-tuple-element.52.k_ref, bf16[1024,256]{1,0:T(8,128)(2,1)S(1)} %get-tuple-element.53.v_ref, bf16[64,4096]{1,0:T(8,128)(2,1)} %attention.4.refs_0_), custom_call_target="tpu_custom_call", output_to_operand_aliasing={{}: (3, {})} | custom-call | flops 1 | bytes 1 | tf_op jit(solution)/shard_map/attention/pallas_call | solution.py:429
  71.0 3.4 %collective-permute-done.29 = bf16[64,2048]{1,0:T(8,128)(2,1)S(1)} collective-permute-done((bf16[64,2048]{1,0:T(8,128)(2,1)S(1)}, bf16[64,2048]{1,0:T(8,128)(2,1)S(1)}, u32[]{:S(2)}, u32[]{:S(2)}) %collective-permute-start.29) | collective-permute-done | bytes 262176 | tf_op jit(solution)/shard_map/ppermute | solution.py:55
  74.5 0.1 add_convert_fusion.1
  74.6 1.5 %collective-permute-start.31 = (bf16[64,2048]{1,0:T(8,128)(2,1)S(1)}, bf16[64,2048]{1,0:T(8,128)(2,1)S(1)}, u32[]{:S(2)}, u32[]{:S(2)}) collective-permute-start(bf16[64,2048]{1,0:T(8,128)(2,1)S(1)} %add_convert_fusion.1), channel_id=1, source_target_pairs={{0,4},{1,5},{2,6},{3,7},{4,12},{5,13},{6,14},{7,15},{12,8},{13,9},... | collective-permute-start | bytes 786440 | tf_op jit(solution)/shard_map/ppermute | solution.py:55
  76.1 1.1 %collective-permute-start.30 = (bf16[64,2048]{1,0:T(8,128)(2,1)S(1)}, bf16[64,2048]{1,0:T(8,128)(2,1)S(1)}, u32[]{:S(2)}, u32[]{:S(2)}) collective-permute-start(bf16[64,2048]{1,0:T(8,128)(2,1)S(1)} %get-tuple-element.58), channel_id=1, source_target_pairs={{0,2},{1,3},{2,0},{3,1},{4,6},{5,7},{6,4},{7,5},{12,14},{13,15},{1... | collective-permute-start | bytes 786440 | tf_op jit(solution)/shard_map/ppermute | solution.py:63
  77.2 1.8 %attention.6.refs_0_ = bf16[64,4096]{1,0:T(8,128)(2,1)} custom-call(bf16[64,4096]{1,0:T(8,128)(2,1)S(1)} %bitcast.24, bf16[1024,256]{1,0:T(8,128)(2,1)S(1)} %get-tuple-element.52.k_ref, bf16[1024,256]{1,0:T(8,128)(2,1)S(1)} %get-tuple-element.53.v_ref, bf16[64,4096]{1,0:T(8,128)(2,1)} %attention.5.refs_0_), custom_call_target="tpu_custom_call", output_to_operand_aliasing={{}: (3, {})} | custom-call | flops 1 | bytes 1 | tf_op jit(solution)/shard_map/attention/pallas_call | solution.py:429
  79.1 1.8 %attention.7 = bf16[64,4096]{1,0:T(8,128)(2,1)} custom-call(bf16[64,4096]{1,0:T(8,128)(2,1)S(1)} %bitcast.25, bf16[1024,256]{1,0:T(8,128)(2,1)S(1)} %get-tuple-element.52.k_ref, bf16[1024,256]{1,0:T(8,128)(2,1)S(1)} %get-tuple-element.53.v_ref, bf16[64,4096]{1,0:T(8,128)(2,1)} %attention.6.refs_0_), custom_call_target="tpu_custom_call", output_to_operand_aliasing={{}: (3, {})} | custom-call | flops 1 | bytes 1 | tf_op jit(solution)/shard_map/attention/pallas_call | solution.py:429
  80.9 1.8 %collective-permute-done.31 = bf16[64,2048]{1,0:T(8,128)(2,1)S(1)} collective-permute-done((bf16[64,2048]{1,0:T(8,128)(2,1)S(1)}, bf16[64,2048]{1,0:T(8,128)(2,1)S(1)}, u32[]{:S(2)}, u32[]{:S(2)}) %collective-permute-start.31) | collective-permute-done | bytes 262176 | tf_op jit(solution)/shard_map/ppermute | solution.py:55
  82.7 0.9 %fusion = bf16[64,1,2048]{2,0,1:T(8,128)(2,1)} fusion(bf16[64,2048]{1,0:T(8,128)(2,1)S(1)} %collective-permute-done.31, bf16[64,2048]{1,0:T(8,128)(2,1)S(1)} %collective-permute-done.30, bf16[256,2048]{1,0:T(8,128)(2,1)S(1)} %collective-permute-done.18, bf16[128,2048]{1,0:T(8,128)(2,1)S(1)} %get-tuple-element.37, bf16[64,1,2048]{2,0,1:T(8,128)(2,1)S(1)} %copy-done.7), kind=kLoop, calls=%fused_computation.8 | loop fusion | flops 1310720 | bytes 1572864 | tf_op jit(solution)/shard_map/reshape | solution.py:588
  (32 shorter events, 0.1 us)
Async XLA Ops:
  2.5 4.6 %collective-permute-start.1 = (bf16[64,2176]{1,0:T(8,128)(2,1)}, bf16[64,2176]{1,0:T(8,128)(2,1)S(1)}, u32[]{:S(2)}, u32[]{:S(2)}) collective-permute-start(bf16[64,2176]{1,0:T(8,128)(2,1)} %get-tuple-element.31.refs_4_.refs_0_), channel_id=1, source_target_pairs={{0,1},{1,0},{2,3},{3,2},{4,5},{5,4},{6,7},{7,6},{12,13},{13,12},{1... | collective-permute-start | bytes 835592 | tf_op jit(solution)/shard_map/ppermute | solution.py:67
  2.9 12.5 %collective-permute-start.3 = (bf16[64,2176]{1,0:T(8,128)(2,1)}, bf16[64,2176]{1,0:T(8,128)(2,1)S(1)}, u32[]{:S(2)}, u32[]{:S(2)}) collective-permute-start(bf16[64,2176]{1,0:T(8,128)(2,1)} %get-tuple-element.31.refs_4_.refs_0_), channel_id=1, source_target_pairs={{0,4},{1,5},{2,6},{3,7},{4,12},{5,13},{6,14},{7,15},{12,8},{13,9},... | collective-permute-start | bytes 835592 | tf_op jit(solution)/shard_map/ppermute | solution.py:55
  5.5 11.8 %collective-permute-start = (bf16[64,2176]{1,0:T(8,128)(2,1)}, bf16[64,2176]{1,0:T(8,128)(2,1)S(1)}, u32[]{:S(2)}, u32[]{:S(2)}) collective-permute-start(bf16[64,2176]{1,0:T(8,128)(2,1)} %get-tuple-element.31.refs_4_.refs_0_), channel_id=1, source_target_pairs={{0,2},{1,3},{2,0},{3,1},{4,6},{5,7},{6,4},{7,5},{12,14},{13,15},{1... | collective-permute-start | bytes 835592 | tf_op jit(solution)/shard_map/ppermute | solution.py:63
  7.0 2.8 %copy-start = (bf16[1,2048,1536]{2,1,0:T(8,128)(2,1)S(1)}, bf16[1,2048,1536]{2,1,0:T(8,128)(2,1)}, u32[]{:S(2)}) copy-start(bf16[1,2048,1536]{2,1,0:T(8,128)(2,1)} %param.16) | copy-start | bytes 18874372
  9.8 1.9 %copy-start.2 = (bf16[1,768,2048]{2,1,0:T(8,128)(2,1)S(1)}, bf16[1,768,2048]{2,1,0:T(8,128)(2,1)}, u32[]{:S(2)}) copy-start(bf16[1,768,2048]{2,1,0:T(8,128)(2,1)} %param.17) | copy-start | bytes 9437188
  11.7 0.9 %copy-start.6 = (bf16[192,256]{1,0:T(8,128)(2,1)S(1)}, bf16[192,256]{1,0:T(8,128)(2,1)}, u32[]{:S(2)}) copy-start(bf16[192,256]{1,0:T(8,128)(2,1)} %get-tuple-element.33.small_ref) | copy-start | bytes 294916
  12.6 22.0 %copy-start.1 = (bf16[1,2048,1536]{2,1,0:T(8,128)(2,1)S(1)}, bf16[1,2048,1536]{2,1,0:T(8,128)(2,1)}, u32[]{:S(2)}) copy-start(bf16[1,2048,1536]{2,1,0:T(8,128)(2,1)} %param.16) | copy-start | bytes 18874372
  12.6 22.0 %copy-start.3 = (bf16[1,768,2048]{2,1,0:T(8,128)(2,1)S(1)}, bf16[1,768,2048]{2,1,0:T(8,128)(2,1)}, u32[]{:S(2)}) copy-start(bf16[1,768,2048]{2,1,0:T(8,128)(2,1)} %param.17) | copy-start | bytes 9437188
  12.6 22.0 %copy-start.5 = (bf16[64,2176]{1,0:T(8,128)(2,1)S(1)}, bf16[64,2176]{1,0:T(8,128)(2,1)}, u32[]{:S(2)}) copy-start(bf16[64,2176]{1,0:T(8,128)(2,1)} %get-tuple-element.31.refs_4_.refs_0_) | copy-start | bytes 835588
  12.6 4.7 %collective-permute-start.7 = (bf16[192,256]{1,0:T(8,128)(2,1)S(1)}, bf16[192,256]{1,0:T(8,128)(2,1)S(1)}, u32[]{:S(2)}, u32[]{:S(2)}) collective-permute-start(bf16[192,256]{1,0:T(8,128)(2,1)S(1)} %hold_weights.1), channel_id=1, source_target_pairs={{0,2},{1,3},{2,0},{3,1},{4,6},{5,7},{6,4},{7,5},{12,14},{13,15},{1... | collective-permute-start | bytes 294920 | tf_op jit(solution)/shard_map/ppermute | solution.py:63
  13.2 9.7 %collective-permute-start.12 = (bf16[64,2176]{1,0:T(8,128)(2,1)}, bf16[64,2176]{1,0:T(8,128)(2,1)S(1)}, u32[]{:S(2)}, u32[]{:S(2)}) collective-permute-start(bf16[64,2176]{1,0:T(8,128)(2,1)} %get-tuple-element.31.refs_4_.refs_0_), channel_id=1, source_target_pairs={{0,8},{1,9},{2,10},{3,11},{4,0},{5,1},{6,2},{7,3},{12,4},{13,5},{1... | collective-permute-start | bytes 835592 | tf_op jit(solution)/shard_map/ppermute | solution.py:59
  15.5 9.1 %collective-permute-start.4 = (bf16[64,2176]{1,0:T(8,128)(2,1)S(1)}, bf16[64,2176]{1,0:T(8,128)(2,1)S(1)}, u32[]{:S(2)}, u32[]{:S(2)}) collective-permute-start(bf16[64,2176]{1,0:T(8,128)(2,1)S(1)} %collective-permute-done.3.refs_0_.refs_4_), channel_id=1, source_target_pairs={{0,2},{1,3},{2,0},{3,1},{4,6},{5,7},{6,4},{7,5},{12,14},{13,15},{1... | collective-permute-start | bytes 835592 | tf_op jit(solution)/shard_map/ppermute | solution.py:63
  17.4 13.2 %collective-permute-start.8 = (bf16[64,2176]{1,0:T(8,128)(2,1)S(1)}, bf16[64,2176]{1,0:T(8,128)(2,1)S(1)}, u32[]{:S(2)}, u32[]{:S(2)}) collective-permute-start(bf16[64,2176]{1,0:T(8,128)(2,1)S(1)} %collective-permute-done.3.refs_0_.refs_4_), channel_id=1, source_target_pairs={{0,4},{1,5},{2,6},{3,7},{4,12},{5,13},{6,14},{7,15},{12,8},{13,9},... | collective-permute-start | bytes 835592 | tf_op jit(solution)/shard_map/ppermute | solution.py:55
  22.9 9.2 %collective-permute-start.13 = (bf16[64,2176]{1,0:T(8,128)(2,1)S(1)}, bf16[64,2176]{1,0:T(8,128)(2,1)S(1)}, u32[]{:S(2)}, u32[]{:S(2)}) collective-permute-start(bf16[64,2176]{1,0:T(8,128)(2,1)S(1)} %collective-permute-done.12.refs_4_.refs_12_), channel_id=1, source_target_pairs={{0,2},{1,3},{2,0},{3,1},{4,6},{5,7},{6,4},{7,5},{12,14},{13,15},{1... | collective-permute-start | bytes 835592 | tf_op jit(solution)/shard_map/ppermute | solution.py:63
  24.1 8.6 %collective-permute-start.5 = (bf16[64,2176]{1,0:T(8,128)(2,1)S(1)}, bf16[64,2176]{1,0:T(8,128)(2,1)S(1)}, u32[]{:S(2)}, u32[]{:S(2)}) collective-permute-start(bf16[64,2176]{1,0:T(8,128)(2,1)S(1)} %collective-permute-done.3.refs_0_.refs_4_), channel_id=1, source_target_pairs={{0,1},{1,0},{2,3},{3,2},{4,5},{5,4},{6,7},{7,6},{12,13},{13,12},{1... | collective-permute-start | bytes 835592 | tf_op jit(solution)/shard_map/ppermute | solution.py:67
  24.1 10.5 %collective-permute-start.2 = (bf16[64,2176]{1,0:T(8,128)(2,1)S(1)}, bf16[64,2176]{1,0:T(8,128)(2,1)S(1)}, u32[]{:S(2)}, u32[]{:S(2)}) collective-permute-start(bf16[64,2176]{1,0:T(8,128)(2,1)S(1)} %collective-permute-done.refs_5_.refs_1_), channel_id=1, source_target_pairs={{0,1},{1,0},{2,3},{3,2},{4,5},{5,4},{6,7},{7,6},{12,13},{13,12},{1... | collective-permute-start | bytes 835592 | tf_op jit(solution)/shard_map/ppermute | solution.py:67
  24.6 10.0 %collective-permute-start.6 = (bf16[64,2176]{1,0:T(8,128)(2,1)S(1)}, bf16[64,2176]{1,0:T(8,128)(2,1)S(1)}, u32[]{:S(2)}, u32[]{:S(2)}) collective-permute-start(bf16[64,2176]{1,0:T(8,128)(2,1)S(1)} %collective-permute-done.4.refs_1_.refs_5_), channel_id=1, source_target_pairs={{0,1},{1,0},{2,3},{3,2},{4,5},{5,4},{6,7},{7,6},{12,13},{13,12},{1... | collective-permute-start | bytes 835592 | tf_op jit(solution)/shard_map/ppermute | solution.py:67
  30.5 12.3 %collective-permute-start.9 = (bf16[64,2176]{1,0:T(8,128)(2,1)S(1)}, bf16[64,2176]{1,0:T(8,128)(2,1)S(1)}, u32[]{:S(2)}, u32[]{:S(2)}) collective-permute-start(bf16[64,2176]{1,0:T(8,128)(2,1)S(1)} %collective-permute-done.8.refs_0_.refs_8_), channel_id=1, source_target_pairs={{0,2},{1,3},{2,0},{3,1},{4,6},{5,7},{6,4},{7,5},{12,14},{13,15},{1... | collective-permute-start | bytes 835592 | tf_op jit(solution)/shard_map/ppermute | solution.py:63
  32.1 10.8 %collective-permute-start.17 = (bf16[384,256]{1,0:T(8,128)(2,1)S(1)}, bf16[384,256]{1,0:T(8,128)(2,1)S(1)}, u32[]{:S(2)}, u32[]{:S(2)}) collective-permute-start(bf16[384,256]{1,0:T(8,128)(2,1)S(1)} %pad_maximum_fusion.refs_16_), channel_id=1, source_target_pairs={{0,8},{1,9},{2,10},{3,11},{4,0},{5,1},{6,2},{7,3},{12,4},{13,5},{1... | collective-permute-start | bytes 589832 | tf_op jit(solution)/shard_map/ppermute | solution.py:59
  32.7 10.1 %collective-permute-start.16 = (bf16[384,256]{1,0:T(8,128)(2,1)S(1)}, bf16[384,256]{1,0:T(8,128)(2,1)S(1)}, u32[]{:S(2)}, u32[]{:S(2)}) collective-permute-start(bf16[384,256]{1,0:T(8,128)(2,1)S(1)} %pad_maximum_fusion.refs_16_), channel_id=1, source_target_pairs={{0,4},{1,5},{2,6},{3,7},{4,12},{5,13},{6,14},{7,15},{12,8},{13,9},... | collective-permute-start | bytes 589832 | tf_op jit(solution)/shard_map/ppermute | solution.py:55
  42.8 2.7 %collective-permute-start.18 = (bf16[256,2048]{1,0:T(8,128)(2,1)S(1)}, bf16[256,2048]{1,0:T(8,128)(2,1)S(1)}, u32[]{:S(2)}, u32[]{:S(2)}) collective-permute-start(bf16[256,2048]{1,0:T(8,128)(2,1)S(1)} %get-tuple-element.39), channel_id=1, source_target_pairs={{0,1},{1,0},{2,3},{3,2},{4,5},{5,4},{6,7},{7,6},{12,13},{13,12},{1... | collective-permute-start | bytes 3145736 | tf_op jit(solution)/shard_map/ppermute | solution.py:67
  42.8 3.4 %collective-permute-start.14 = (bf16[64,2176]{1,0:T(8,128)(2,1)S(1)}, bf16[64,2176]{1,0:T(8,128)(2,1)S(1)}, u32[]{:S(2)}, u32[]{:S(2)}) collective-permute-start(bf16[64,2176]{1,0:T(8,128)(2,1)S(1)} %collective-permute-done.12.refs_4_.refs_12_), channel_id=1, source_target_pairs={{0,1},{1,0},{2,3},{3,2},{4,5},{5,4},{6,7},{7,6},{12,13},{13,12},{1... | collective-permute-start | bytes 835592 | tf_op jit(solution)/shard_map/ppermute | solution.py:67
  43.3 3.2 %collective-permute-start.15 = (bf16[64,2176]{1,0:T(8,128)(2,1)S(1)}, bf16[64,2176]{1,0:T(8,128)(2,1)S(1)}, u32[]{:S(2)}, u32[]{:S(2)}) collective-permute-start(bf16[64,2176]{1,0:T(8,128)(2,1)S(1)} %collective-permute-done.13.refs_5_.refs_13_), channel_id=1, source_target_pairs={{0,1},{1,0},{2,3},{3,2},{4,5},{5,4},{6,7},{7,6},{12,13},{13,12},{1... | collective-permute-start | bytes 835592 | tf_op jit(solution)/shard_map/ppermute | solution.py:67
  43.4 3.3 %collective-permute-start.10 = (bf16[64,2176]{1,0:T(8,128)(2,1)S(1)}, bf16[64,2176]{1,0:T(8,128)(2,1)S(1)}, u32[]{:S(2)}, u32[]{:S(2)}) collective-permute-start(bf16[64,2176]{1,0:T(8,128)(2,1)S(1)} %collective-permute-done.8.refs_0_.refs_8_), channel_id=1, source_target_pairs={{0,1},{1,0},{2,3},{3,2},{4,5},{5,4},{6,7},{7,6},{12,13},{13,12},{1... | collective-permute-start | bytes 835592 | tf_op jit(solution)/shard_map/ppermute | solution.py:67
  43.8 3.2 %collective-permute-start.11 = (bf16[64,2176]{1,0:T(8,128)(2,1)S(1)}, bf16[64,2176]{1,0:T(8,128)(2,1)S(1)}, u32[]{:S(2)}, u32[]{:S(2)}) collective-permute-start(bf16[64,2176]{1,0:T(8,128)(2,1)S(1)} %collective-permute-done.9.refs_1_.refs_9_), channel_id=1, source_target_pairs={{0,1},{1,0},{2,3},{3,2},{4,5},{5,4},{6,7},{7,6},{12,13},{13,12},{1... | collective-permute-start | bytes 835592 | tf_op jit(solution)/shard_map/ppermute | solution.py:67
  45.6 8.4 %collective-permute-start.19 = (bf16[64,2048]{1,0:T(8,128)(2,1)S(1)}, bf16[64,2048]{1,0:T(8,128)(2,1)S(1)}, u32[]{:S(2)}, u32[]{:S(2)}) collective-permute-start(bf16[64,2048]{1,0:T(8,128)(2,1)S(1)} %get-tuple-element.62), channel_id=1, source_target_pairs={{0,2},{1,3},{2,0},{3,1},{4,6},{5,7},{6,4},{7,5},{12,14},{13,15},{1... | collective-permute-start | bytes 786440 | tf_op jit(solution)/shard_map/ppermute | solution.py:63
  46.2 7.6 %collective-permute-start.20 = (bf16[384,256]{1,0:T(8,128)(2,1)S(1)}, bf16[384,256]{1,0:T(8,128)(2,1)S(1)}, u32[]{:S(2)}, u32[]{:S(2)}) collective-permute-start(bf16[384,256]{1,0:T(8,128)(2,1)S(1)} %collective-permute-done.16.refs_18_), channel_id=1, source_target_pairs={{0,4},{1,5},{2,6},{3,7},{4,12},{5,13},{6,14},{7,15},{12,8},{13,9},... | collective-permute-start | bytes 589832 | tf_op jit(solution)/shard_map/ppermute | solution.py:55
  50.3 17.1 %copy-start.4 = (bf16[64,1,4096]{2,0,1:T(8,128)(2,1)S(1)}, bf16[64,1,4096]{2,0,1:T(8,128)(2,1)}, u32[]{:S(2)}) copy-start(bf16[64,1,4096]{2,0,1:T(8,128)(2,1)} %param.10) | copy-start | bytes 1572868
  54.0 2.7 %collective-permute-start.21 = (bf16[256,2048]{1,0:T(8,128)(2,1)S(1)}, bf16[256,2048]{1,0:T(8,128)(2,1)S(1)}, u32[]{:S(2)}, u32[]{:S(2)}) collective-permute-start(bf16[256,2048]{1,0:T(8,128)(2,1)S(1)} %get-tuple-element.44), channel_id=1, source_target_pairs={{0,1},{1,0},{2,3},{3,2},{4,5},{5,4},{6,7},{7,6},{12,13},{13,12},{1... | collective-permute-start | bytes 3145736 | tf_op jit(solution)/shard_map/ppermute | solution.py:67
  54.1 10.6 %collective-permute-start.28 = (bf16[64,2048]{1,0:T(8,128)(2,1)S(1)}, bf16[64,2048]{1,0:T(8,128)(2,1)S(1)}, u32[]{:S(2)}, u32[]{:S(2)}) collective-permute-start(bf16[64,2048]{1,0:T(8,128)(2,1)S(1)} %add_convert_fusion.3), channel_id=1, source_target_pairs={{0,4},{1,5},{2,6},{3,7},{4,12},{5,13},{6,14},{7,15},{12,8},{13,9},... | collective-permute-start | bytes 786440 | tf_op jit(solution)/shard_map/ppermute | solution.py:55
  54.5 4.1 %collective-permute-start.22 = (bf16[384,256]{1,0:T(8,128)(2,1)S(1)}, bf16[384,256]{1,0:T(8,128)(2,1)S(1)}, u32[]{:S(2)}, u32[]{:S(2)}) collective-permute-start(bf16[384,256]{1,0:T(8,128)(2,1)S(1)} %pad_maximum_fusion.refs_16_), channel_id=1, source_target_pairs={{0,1},{1,0},{2,3},{3,2},{4,5},{5,4},{6,7},{7,6},{12,13},{13,12},{1... | collective-permute-start | bytes 589832 | tf_op jit(solution)/shard_map/ppermute | solution.py:67
  56.8 8.4 %collective-permute-start.27 = (bf16[64,2048]{1,0:T(8,128)(2,1)S(1)}, bf16[64,2048]{1,0:T(8,128)(2,1)S(1)}, u32[]{:S(2)}, u32[]{:S(2)}) collective-permute-start(bf16[64,2048]{1,0:T(8,128)(2,1)S(1)} %get-tuple-element.61), channel_id=1, source_target_pairs={{0,2},{1,3},{2,0},{3,1},{4,6},{5,7},{6,4},{7,5},{12,14},{13,15},{1... | collective-permute-start | bytes 786440 | tf_op jit(solution)/shard_map/ppermute | solution.py:63
  58.1 1.4 %collective-permute-start.23 = (bf16[384,256]{1,0:T(8,128)(2,1)S(1)}, bf16[384,256]{1,0:T(8,128)(2,1)S(1)}, u32[]{:S(2)}, u32[]{:S(2)}) collective-permute-start(bf16[384,256]{1,0:T(8,128)(2,1)S(1)} %collective-permute-done.16.refs_18_), channel_id=1, source_target_pairs={{0,1},{1,0},{2,3},{3,2},{4,5},{5,4},{6,7},{7,6},{12,13},{13,12},{1... | collective-permute-start | bytes 589832 | tf_op jit(solution)/shard_map/ppermute | solution.py:67
  58.1 1.7 %collective-permute-start.24 = (bf16[384,256]{1,0:T(8,128)(2,1)S(1)}, bf16[384,256]{1,0:T(8,128)(2,1)S(1)}, u32[]{:S(2)}, u32[]{:S(2)}) collective-permute-start(bf16[384,256]{1,0:T(8,128)(2,1)S(1)} %collective-permute-done.20.refs_20_), channel_id=1, source_target_pairs={{0,1},{1,0},{2,3},{3,2},{4,5},{5,4},{6,7},{7,6},{12,13},{13,12},{1... | collective-permute-start | bytes 589832 | tf_op jit(solution)/shard_map/ppermute | solution.py:67
  58.7 1.5 %collective-permute-start.25 = (bf16[384,256]{1,0:T(8,128)(2,1)S(1)}, bf16[384,256]{1,0:T(8,128)(2,1)S(1)}, u32[]{:S(2)}, u32[]{:S(2)}) collective-permute-start(bf16[384,256]{1,0:T(8,128)(2,1)S(1)} %collective-permute-done.17.refs_22_), channel_id=1, source_target_pairs={{0,1},{1,0},{2,3},{3,2},{4,5},{5,4},{6,7},{7,6},{12,13},{13,12},{1... | collective-permute-start | bytes 589832 | tf_op jit(solution)/shard_map/ppermute | solution.py:67
  64.7 17.9 %copy-start.7 = (bf16[64,1,2048]{2,0,1:T(8,128)(2,1)S(1)}, bf16[64,1,2048]{2,0,1:T(8,128)(2,1)}, u32[]{:S(2)}) copy-start(bf16[64,1,2048]{2,0,1:T(8,128)(2,1)} %param.9) | copy-start | bytes 786436
  65.4 9.1 %collective-permute-start.29 = (bf16[64,2048]{1,0:T(8,128)(2,1)S(1)}, bf16[64,2048]{1,0:T(8,128)(2,1)S(1)}, u32[]{:S(2)}, u32[]{:S(2)}) collective-permute-start(bf16[64,2048]{1,0:T(8,128)(2,1)S(1)} %add_convert_fusion.2), channel_id=1, source_target_pairs={{0,4},{1,5},{2,6},{3,7},{4,12},{5,13},{6,14},{7,15},{12,8},{13,9},... | collective-permute-start | bytes 786440 | tf_op jit(solution)/shard_map/ppermute | solution.py:55
  66.4 8.0 %collective-permute-start.26 = (bf16[64,2048]{1,0:T(8,128)(2,1)S(1)}, bf16[64,2048]{1,0:T(8,128)(2,1)S(1)}, u32[]{:S(2)}, u32[]{:S(2)}) collective-permute-start(bf16[64,2048]{1,0:T(8,128)(2,1)S(1)} %get-tuple-element.60), channel_id=1, source_target_pairs={{0,2},{1,3},{2,0},{3,1},{4,6},{5,7},{6,4},{7,5},{12,14},{13,15},{1... | collective-permute-start | bytes 786440 | tf_op jit(solution)/shard_map/ppermute | solution.py:63
  74.6 8.0 %collective-permute-start.31 = (bf16[64,2048]{1,0:T(8,128)(2,1)S(1)}, bf16[64,2048]{1,0:T(8,128)(2,1)S(1)}, u32[]{:S(2)}, u32[]{:S(2)}) collective-permute-start(bf16[64,2048]{1,0:T(8,128)(2,1)S(1)} %add_convert_fusion.1), channel_id=1, source_target_pairs={{0,4},{1,5},{2,6},{3,7},{4,12},{5,13},{6,14},{7,15},{12,8},{13,9},... | collective-permute-start | bytes 786440 | tf_op jit(solution)/shard_map/ppermute | solution.py:55
  76.1 6.5 %collective-permute-start.30 = (bf16[64,2048]{1,0:T(8,128)(2,1)S(1)}, bf16[64,2048]{1,0:T(8,128)(2,1)S(1)}, u32[]{:S(2)}, u32[]{:S(2)}) collective-permute-start(bf16[64,2048]{1,0:T(8,128)(2,1)S(1)} %get-tuple-element.58), channel_id=1, source_target_pairs={{0,2},{1,3},{2,0},{3,1},{4,6},{5,7},{6,4},{7,5},{12,14},{13,15},{1... | collective-permute-start | bytes 786440 | tf_op jit(solution)/shard_map/ppermute | solution.py:63

commit v12 on v11

--- a/solution.py
+++ b/solution.py
@@ -98,12 +98,16 @@
     meta_ref[24 : 24 + top, 0:rows] = rest - middle
     out_ref[:, width:] = meta_ref[...].T[:rows, :].astype(BF16)
     small_ref[:rows] = key_ref[...]
-    small_ref[rows:] = weight_ref[...]
-
-
-def pack(activations, norm_gain, ids, gates, keys, value_weight):
+    share = small_ref.shape[0] - rows
+    first = 0
+    if share < weight_ref.shape[0]:
+        first = pl.multiple_of(lax.axis_index("grp") * share, share)
+    small_ref[rows:] = weight_ref[pl.ds(first, share)]
+
+
+def pack(activations, norm_gain, ids, gates, keys, value_weight, planes):
     rows, width = activations.shape
-    small_rows = rows + value_weight.shape[0]
+    small_rows = rows + value_weight.shape[0] // planes
     assert rows <= META and ids.shape[0] <= 8
     return pl.pallas_call(
         pack_kernel,
@@ -295,39 +299,32 @@
     )(*(in_vmem(*arrays) if direct else arrays), *in_vmem(w_gate_up, w_down))
 
 
-def value_kernel(key_rows, blocks, small_blocks, *refs):
-    inputs = 1 + max(b[0] for b in blocks)
-    smalls = 1 + max(b[0] for b in small_blocks)
-    x_hbm = refs[:inputs]
-    small_hbm = refs[inputs : inputs + smalls]
-    key_ref, value_ref, x_buf, weight, sems = refs[inputs + smalls :]
+def value_kernel(key_rows, blocks, *refs):
+    count = len(blocks)
+    x_hbm, smalls = refs[:count], refs[count : count + 4]
+    key_ref, value_ref, x_buf, weight, sems = refs[count + 4 :]
     width = x_buf.shape[1]
-    weight_rows = width // len(small_blocks)
+    share = width // count // 2
+    plane = lax.axis_index("grp")
     copies = []
-    for number, (operand, first, device) in enumerate(blocks):
-        copies.append(
-            pltpu.make_async_copy(
-                x_hbm[operand].at[pl.ds(first, key_rows), pl.ds(0, width)],
-                x_buf.at[pl.ds(device() * key_rows, key_rows)],
-                sems.at[0, number],
-            )
-        )
-    for number, (operand, first, device) in enumerate(small_blocks):
+    for number, (operand, at, device) in enumerate(blocks):
         place = device()
-        copies.append(
-            pltpu.make_async_copy(
-                small_hbm[operand].at[pl.ds(first, key_rows)],
-                key_ref.at[pl.ds(place * key_rows, key_rows)],
-                sems.at[1, number],
-            )
-        )
-        copies.append(
-            pltpu.make_async_copy(
-                small_hbm[operand].at[pl.ds(first + key_rows, weight_rows)],
-                weight.at[pl.ds(place * weight_rows, weight_rows)],
-                sems.at[2, number],
-            )
-        )
+        own, other = smalls[number * 2 // count * 2 : number * 2 // count * 2 + 2]
+        below = at * (key_rows + share)
+        pairs = [
+            (x_hbm[operand].at[:, pl.ds(0, width)], x_buf.at[pl.ds(place * key_rows, key_rows)]),
+            (own.at[pl.ds(below, key_rows)], key_ref.at[pl.ds(place * key_rows, key_rows)]),
+            (
+                own.at[pl.ds(below + key_rows, share)],
+                weight.at[pl.ds((2 * place + plane) * share, share)],
+            ),
+            (
+                other.at[pl.ds(at * share, share)],
+                weight.at[pl.ds((2 * place + 1 - plane) * share, share)],
+            ),
+        ]
+        for kind, (source, target) in enumerate(pairs):
+            copies.append(pltpu.make_async_copy(source, target, sems.at[kind, number]))
     for copy in copies:
         copy.start()
     for copy in copies:
@@ -335,20 +332,19 @@
     value_ref[...] = dot(x_buf[...], weight[...]).astype(BF16)
 
 
-def make_values(arrays, blocks, smalls, small_blocks, key_rows, width, earlier):
-    smalls = [after(smalls[0], *earlier), *smalls[1:]]
+def make_values(arrays, blocks, smalls, key_rows, width):
     kv_width = smalls[0].shape[1]
     total = key_rows * len(blocks)
     kv = jax.ShapeDtypeStruct((total, kv_width), BF16)
     return pl.pallas_call(
-        functools.partial(value_kernel, key_rows, blocks, small_blocks),
+        functools.partial(value_kernel, key_rows, blocks),
         out_shape=[kv, kv],
         in_specs=[ANY] * (len(arrays) + len(smalls)),
         out_specs=[IN_VMEM] * 2,
         scratch_shapes=[
             pltpu.VMEM((total, width), BF16),
             pltpu.VMEM((width, kv_width), BF16),
-            pltpu.SemaphoreType.DMA((3, len(blocks))),
+            pltpu.SemaphoreType.DMA((4, len(blocks))),
         ],
         compiler_params=pltpu.CompilerParams(vmem_limit_bytes=VMEM_LIMIT),
         cost_estimate=SHORT,
@@ -471,22 +467,14 @@
         for step in range(LINE)
     ]
     blocks = [
-        (4 * step + core * 2 + y, 0, functools.partial(from_device, step, y, core))
+        (4 * step + core * 2 + y, 2 * step + y, functools.partial(from_device, step, y, core))
+        for core in range(2)
         for step in range(LINE)
-        for core in range(2)
         for y in range(2)
     ]
     pair = after(pair, line[3])
     pairs = [pair, forward(pair), None, backward(pair)]
     pairs[2] = forward(pairs[1])
-    small_rows = small.shape[0]
-    small_blocks = [
-        (2 * step + core, y * small_rows, functools.partial(from_device, step, y, core))
-        for step in range(LINE)
-        for core in range(2)
-        for y in range(2)
-    ]
-
     keep, mine, crossing = [None] * LINE, [None] * LINE, [None] * LINE
 
     def experts(first, second, before, beside):
@@ -517,22 +505,22 @@
     send = experts(2, 3, [crossing[0], crossing[1]], [theirs[1], pairs[2]])
     total = summed(*mine[1], after(theirs[1], send))
     moving = forward(total)
-    smalls = []
-    for step in range(LINE):
-        smalls += [pairs[step], other_core(after(pairs[step], total))]
     theirs[2], theirs[3] = across(crossing[2]), across(crossing[3])
-    new_keys, values = make_values(
-        sum(arrays, []), blocks, smalls, small_blocks, rows, width, crossing[2:]
-    )
-    total = summed(*mine[2], theirs[2], after(moving, values))
+    own = jnp.concatenate(after(tuple(pairs), *crossing[2:], total), axis=0)
+    shares = own.reshape(2 * LINE, small.shape[0], -1)[:, rows:]
+    other = lax.ppermute(shares.reshape(-1, own.shape[1]), "grp", [(0, 1), (1, 0)])
+    total = summed(*mine[2], theirs[2], moving)
     moving = forward(total)
     theirs[0] = across(after(crossing[0], total))
-    context = attend_part(after(queries, total), new_keys, values, 0, 4)
-    context = attend_part(queries, new_keys, values, 1, 4, context)
-    total = summed(*mine[3], theirs[3], after(moving, context))
+    other = after(other, total)
+    smalls = [own, other, other_core(own), other_core(other)]
+    new_keys, values = make_values(sum(arrays, []), blocks, smalls, rows, width)
+    total = summed(*mine[3], theirs[3], after(moving, values))
     moving = forward(total)
-    context = attend_part(after(queries, total), new_keys, values, 2, 4, context)
-    context = attend_part(queries, new_keys, values, 3, 4, context)
+    queries = after(queries, total)
+    context = None
+    for part in range(4):
+        context = attend_part(queries, new_keys, values, part, 4, context)
     layer_out = summed(acts, *mine[0], theirs[0], after(moving, context))
     return context, layer_out
 
@@ -566,6 +554,8 @@
     devices = lax.axis_size("seq")
     capacity = max(2, 3 * pos_rows * top // (2 * devices))
     acts = activations.reshape(pos_rows, model_width)
+    halves = 2 * devices * pos_rows == model_width and value_weight.shape[0] % (2 * pos_rows) == 0
+    line = devices == 4 * LINE and lax.axis_size("grp") == 2 and halves
     packed, small = pack(
         acts,
         norm_gain,
@@ -573,8 +563,9 @@
         gate_weights.transpose(1, 2, 0).reshape(top, pos_rows),
         keys.reshape(pos_rows, -1),
         value_weight,
+        2 if line else 1,
     )
-    way = on_line if devices == 4 * LINE else on_any
+    way = on_line if line else on_any
     context, layer_out = way(
         acts,
         packed,

time: 83.8 us -> 86.4 us (1.031)
  starting transfers between devices: 26.5 us -> 31.5 us
  waiting for transfers between devices: 29.1 us -> 26.4 us
    ppermute x7, starting transfers between devices: 11.4 us -> 17.3 us  [forward(): return lax.ppermute(x, 'seq', ring_steps(1))]
    ppermute x14 -> x12, waiting for transfers between devices: 5.55 us -> 2.55 us  [other_core(): return lax.ppermute(x, 'seq', swaps(0, 1))]
    ppermute x2, waiting for transfers between devices: 6.87 us -> 4.77 us  [backward(): return lax.ppermute(x, 'seq', ring_steps(LINE - 1))]
    ppermute x9, starting transfers between devices: 9.34 us -> 7.54 us  [across(): return lax.ppermute(x, 'seq', swaps(1, 0))]
    ppermute x0 -> x1, starting transfers between devices: none -> 1.55 us  [on_line(): lax.ppermute(shares.reshape(-1, own.shape[1]), 'grp', [(0, 1), (1, 0)])]
    ppermute x9, waiting for transfers between devices: 2.04 us -> 3.33 us  [across(): return lax.ppermute(x, 'seq', swaps(1, 0))]
    ppermute x0 -> x1, waiting for transfers between devices: none -> 1.24 us  [on_line(): lax.ppermute(shares.reshape(-1, own.shape[1]), 'grp', [(0, 1), (1, 0)])]
    ppermute x14 -> x12, starting transfers between devices: 2.83 us -> 2.13 us  [other_core(): return lax.ppermute(x, 'seq', swaps(0, 1))]
  transfers between devices with their start and end apart: 32 -> 31, of which waited for: 16 -> 13; matrix products, arithmetic and copies ran while one was open for 0% -> 1% of each run, Pallas kernels for 22% -> 22%
where the time goes in v12:
time: 86.4 us; the launch traced here: 86.1 us
  starting transfers between devices  31.5 us (36%)
  waiting for transfers between devices  26.4 us (31%)
  Pallas kernels  20.4 us (24%)
  local copies, waits for them, and re-layouts  5.6 us (6%)
  other arithmetic  1.5 us (2%)
    ppermute x7, starting transfers between devices, forward(): return lax.ppermute(x, 'seq', ring_steps(1))  17.3 us
    ppermute x7, waiting for transfers between devices, forward(): return lax.ppermute(x, 'seq', ring_steps(1))  14.5 us
    ppermute x9, starting transfers between devices, across(): return lax.ppermute(x, 'seq', swaps(1, 0))  7.54 us
    pallas_call x4, Pallas kernels, attend_part(): pl.pallas_call(functools.partial(attention_kernel, chunk), grid=(1,), out...  7.33 us
    pallas_call x2, Pallas kernels, run_experts(): pl.pallas_call(functools.partial(expert_kernel, top, tok_rows, capacity,...  6.36 us
    unnamed x19, local copies, waits for them, and re-layouts  5.57 us
    pallas_call x1, Pallas kernels, make_values(): pl.pallas_call(functools.partial(value_kernel, key_rows, blocks), out_sha...  4.84 us
    ppermute x2, waiting for transfers between devices, backward(): return lax.ppermute(x, 'seq', ring_steps(LINE - 1))  4.77 us
  transfers between devices with their start and end apart: 31, of which 13 were waited for; matrix products, arithmetic and copies ran while one was open for 1% of the time, Pallas kernels for 22%

profile of v12, /device:TPU:0, one launch (start us, length us, event | category | flops | bytes accessed | tf_op | source)
XLA Modules:
  0.0 86.1 jit_solution(9797587783206374541)
XLA Ops:
  0.6 1.9 %normalize_and_pack.1 = (bf16[64,2176]{1,0:T(8,128)(2,1)}, bf16[128,256]{1,0:T(8,128)(2,1)}) custom-call(bf16[64,2048]{1,0:T(8,128)(2,1)} %bitcast.30, f32[1,2048]{1,0:T(1,128)} %bitcast.33, s32[4,64]{1,0:T(4,128)} %bitcast.34, f32[4,64]{1,0:T(4,128)} %bitcast.35, bf16[64,256]{1,0:T(8,128)(2,1)} %bitcast.32, bf16[128,256]{1,0:T(8,128)(2,1)} %weight_ref.1), custom_call_target="tpu_custom_call" | custom-call | flops 1 | bytes 1 | tf_op jit(solution)/shard_map/normalize_and_pack/pallas_call | solution.py:112
  2.5 0.5 collective-permute-start.1
  2.9 2.6 %collective-permute-start = (bf16[64,2176]{1,0:T(8,128)(2,1)}, bf16[64,2176]{1,0:T(8,128)(2,1)S(1)}, u32[]{:S(2)}, u32[]{:S(2)}) collective-permute-start(bf16[64,2176]{1,0:T(8,128)(2,1)} %get-tuple-element.29.refs_4_.refs_0_), channel_id=1, source_target_pairs={{0,4},{1,5},{2,6},{3,7},{4,12},{5,13},{6,14},{7,15},{12,8},{13,9},... | collective-permute-start | bytes 835592 | tf_op jit(solution)/shard_map/ppermute | solution.py:55
  5.5 1.5 %collective-permute-start.3 = (bf16[64,2176]{1,0:T(8,128)(2,1)}, bf16[64,2176]{1,0:T(8,128)(2,1)S(1)}, u32[]{:S(2)}, u32[]{:S(2)}) collective-permute-start(bf16[64,2176]{1,0:T(8,128)(2,1)} %get-tuple-element.29.refs_4_.refs_0_), channel_id=1, source_target_pairs={{0,2},{1,3},{2,0},{3,1},{4,6},{5,7},{6,4},{7,5},{12,14},{13,15},{1... | collective-permute-start | bytes 835592 | tf_op jit(solution)/shard_map/ppermute | solution.py:63
  7.0 0.0 collective-permute-done.1.refs_6_.refs_2_
  7.0 2.8 %copy-done = bf16[1,2048,1536]{2,1,0:T(8,128)(2,1)S(1)} copy-done((bf16[1,2048,1536]{2,1,0:T(8,128)(2,1)S(1)}, bf16[1,2048,1536]{2,1,0:T(8,128)(2,1)}, u32[]{:S(2)}) %copy-start) | copy-done | bytes 6291480
  9.8 1.9 %copy-done.2 = bf16[1,768,2048]{2,1,0:T(8,128)(2,1)S(1)} copy-done((bf16[1,768,2048]{2,1,0:T(8,128)(2,1)S(1)}, bf16[1,768,2048]{2,1,0:T(8,128)(2,1)}, u32[]{:S(2)}) %copy-start.2) | copy-done | bytes 3145752
  11.7 0.8 copy-done.6
  12.6 0.6 collective-permute-start.2
  13.2 2.3 %collective-permute-start.5 = (bf16[64,2176]{1,0:T(8,128)(2,1)}, bf16[64,2176]{1,0:T(8,128)(2,1)S(1)}, u32[]{:S(2)}, u32[]{:S(2)}) collective-permute-start(bf16[64,2176]{1,0:T(8,128)(2,1)} %get-tuple-element.29.refs_4_.refs_0_), channel_id=1, source_target_pairs={{0,8},{1,9},{2,10},{3,11},{4,0},{5,1},{6,2},{7,3},{12,4},{13,5},{1... | collective-permute-start | bytes 835592 | tf_op jit(solution)/shard_map/ppermute | solution.py:59
  15.4 0.0 collective-permute-done.refs_0_.refs_4_
  15.4 0.6 collective-permute-start.7
  16.0 0.9 %collective-permute-done.2 = bf16[128,256]{1,0:T(8,128)(2,1)S(1)} collective-permute-done((bf16[128,256]{1,0:T(8,128)(2,1)S(1)}, bf16[128,256]{1,0:T(8,128)(2,1)S(1)}, u32[]{:S(2)}, u32[]{:S(2)}) %collective-permute-start.2) | collective-permute-done | bytes 65568 | tf_op jit(solution)/shard_map/ppermute | solution.py:63
  16.9 3.3 %collective-permute-start.4 = (bf16[64,2176]{1,0:T(8,128)(2,1)S(1)}, bf16[64,2176]{1,0:T(8,128)(2,1)S(1)}, u32[]{:S(2)}, u32[]{:S(2)}) collective-permute-start(bf16[64,2176]{1,0:T(8,128)(2,1)S(1)} %collective-permute-done.refs_0_.refs_4_), channel_id=1, source_target_pairs={{0,4},{1,5},{2,6},{3,7},{4,12},{5,13},{6,14},{7,15},{12,8},{13,9},... | collective-permute-start | bytes 835592 | tf_op jit(solution)/shard_map/ppermute | solution.py:55
  20.3 2.6 %collective-permute-done.5.refs_4_.refs_12_ = bf16[64,2176]{1,0:T(8,128)(2,1)S(1)} collective-permute-done((bf16[64,2176]{1,0:T(8,128)(2,1)}, bf16[64,2176]{1,0:T(8,128)(2,1)S(1)}, u32[]{:S(2)}, u32[]{:S(2)}) %collective-permute-start.5) | collective-permute-done | bytes 278560 | tf_op jit(solution)/shard_map/ppermute | solution.py:59
  22.8 1.2 %collective-permute-start.6 = (bf16[64,2176]{1,0:T(8,128)(2,1)S(1)}, bf16[64,2176]{1,0:T(8,128)(2,1)S(1)}, u32[]{:S(2)}, u32[]{:S(2)}) collective-permute-start(bf16[64,2176]{1,0:T(8,128)(2,1)S(1)} %collective-permute-done.5.refs_4_.refs_12_), channel_id=1, source_target_pairs={{0,2},{1,3},{2,0},{3,1},{4,6},{5,7},{6,4},{7,5},{12,14},{13,15},{1... | collective-permute-start | bytes 835592 | tf_op jit(solution)/shard_map/ppermute | solution.py:63
  24.1 0.0 collective-permute-start.10
  24.1 0.5 collective-permute-start.8
  24.6 0.0 collective-permute-start.9
  24.6 5.9 %collective-permute-done.4.refs_0_.refs_8_ = bf16[64,2176]{1,0:T(8,128)(2,1)S(1)} collective-permute-done((bf16[64,2176]{1,0:T(8,128)(2,1)S(1)}, bf16[64,2176]{1,0:T(8,128)(2,1)S(1)}, u32[]{:S(2)}, u32[]{:S(2)}) %collective-permute-start.4) | collective-permute-done | bytes 278560 | tf_op jit(solution)/shard_map/ppermute | solution.py:55
  30.5 1.5 %collective-permute-start.11 = (bf16[64,2176]{1,0:T(8,128)(2,1)S(1)}, bf16[64,2176]{1,0:T(8,128)(2,1)S(1)}, u32[]{:S(2)}, u32[]{:S(2)}) collective-permute-start(bf16[64,2176]{1,0:T(8,128)(2,1)S(1)} %collective-permute-done.4.refs_0_.refs_8_), channel_id=1, source_target_pairs={{0,2},{1,3},{2,0},{3,1},{4,6},{5,7},{6,4},{7,5},{12,14},{13,15},{1... | collective-permute-start | bytes 835592 | tf_op jit(solution)/shard_map/ppermute | solution.py:63
  32.0 0.0 collective-permute-done.6.refs_5_.refs_13_
  32.0 0.7 collective-permute-start.13
  32.7 0.0 collective-permute-done.10.refs_7_.refs_3_
  32.7 1.9 %collective-permute-start.12 = (bf16[256,256]{1,0:T(8,128)(2,1)S(1)}, bf16[256,256]{1,0:T(8,128)(2,1)S(1)}, u32[]{:S(2)}, u32[]{:S(2)}) collective-permute-start(bf16[256,256]{1,0:T(8,128)(2,1)S(1)} %pad_maximum_fusion), channel_id=1, source_target_pairs={{0,4},{1,5},{2,6},{3,7},{4,12},{5,13},{6,14},{7,15},{12,8},{13,9},... | collective-permute-start | bytes 393224 | tf_op jit(solution)/shard_map/ppermute | solution.py:55
  34.6 3.2 %experts.2 = (bf16[128,2048]{1,0:T(8,128)(2,1)S(1)}, bf16[128,2048]{1,0:T(8,128)(2,1)S(1)}, bf16[256,2048]{1,0:T(8,128)(2,1)S(1)}) custom-call(bf16[64,2176]{1,0:T(8,128)(2,1)S(1)} %collective-permute-done.refs_0_.refs_4_, bf16[64,2176]{1,0:T(8,128)(2,1)S(1)} %collective-permute-done.7.refs_1_.refs_5_, ...), custom_call_target="tpu_custom_call" | custom-call | flops 1 | bytes 1 | tf_op jit(solution)/shard_map/experts/pallas_call | solution.py:290
  37.7 2.2 %collective-permute-done.13 = bf16[256,256]{1,0:T(8,128)(2,1)S(1)} collective-permute-done((bf16[256,256]{1,0:T(8,128)(2,1)S(1)}, bf16[256,256]{1,0:T(8,128)(2,1)S(1)}, u32[]{:S(2)}, u32[]{:S(2)}) %collective-permute-start.13) | collective-permute-done | bytes 131104 | tf_op jit(solution)/shard_map/ppermute | solution.py:59
  39.9 0.0 collective-permute-done.12
  40.0 0.5 collective-permute-start.17
  40.5 0.1 collective-permute-start.18
  40.5 0.4 collective-permute-start.15
  41.0 0.1 collective-permute-start.16
  41.1 1.6 %collective-permute-done.14 = bf16[256,2048]{1,0:T(8,128)(2,1)S(1)} collective-permute-done((bf16[256,2048]{1,0:T(8,128)(2,1)S(1)}, bf16[256,2048]{1,0:T(8,128)(2,1)S(1)}, u32[]{:S(2)}, u32[]{:S(2)}) %collective-permute-start.14) | collective-permute-done | bytes 1048608 | tf_op jit(solution)/shard_map/ppermute | solution.py:67
  42.6 0.1 add_convert_fusion.7
  42.8 0.7 collective-permute-start.19
  43.4 2.7 %collective-permute-start.20 = (bf16[256,256]{1,0:T(8,128)(2,1)S(1)}, bf16[256,256]{1,0:T(8,128)(2,1)S(1)}, u32[]{:S(2)}, u32[]{:S(2)}) collective-permute-start(bf16[256,256]{1,0:T(8,128)(2,1)S(1)} %collective-permute-done.12), channel_id=1, source_target_pairs={{0,4},{1,5},{2,6},{3,7},{4,12},{5,13},{6,14},{7,15},{12,8},{13,9},... | collective-permute-start | bytes 393224 | tf_op jit(solution)/shard_map/ppermute | solution.py:55
  46.1 3.2 %experts.3 = (bf16[128,2048]{1,0:T(8,128)(2,1)S(1)}, bf16[128,2048]{1,0:T(8,128)(2,1)S(1)}, bf16[256,2048]{1,0:T(8,128)(2,1)S(1)}) custom-call(bf16[64,2176]{1,0:T(8,128)(2,1)S(1)} %collective-permute-done.4.refs_0_.refs_8_, bf16[64,2176]{1,0:T(8,128)(2,1)S(1)} %collective-permute-done.11.refs_1_.refs_9_, ...), custom_call_target="tpu_custom_call" | custom-call | flops 1 | bytes 1 | tf_op jit(solution)/shard_map/experts/pallas_call | solution.py:290
  49.3 1.3 %collective-permute-done.20 = bf16[256,256]{1,0:T(8,128)(2,1)S(1)} collective-permute-done((bf16[256,256]{1,0:T(8,128)(2,1)S(1)}, bf16[256,256]{1,0:T(8,128)(2,1)S(1)}, u32[]{:S(2)}, u32[]{:S(2)}) %collective-permute-start.20) | collective-permute-done | bytes 131104 | tf_op jit(solution)/shard_map/ppermute | solution.py:55
  50.7 0.5 collective-permute-done.19
  51.2 0.1 add_convert_fusion.3
  51.3 1.6 %collective-permute-start.24 = (bf16[64,2048]{1,0:T(8,128)(2,1)S(1)}, bf16[64,2048]{1,0:T(8,128)(2,1)S(1)}, u32[]{:S(2)}, u32[]{:S(2)}) collective-permute-start(bf16[64,2048]{1,0:T(8,128)(2,1)S(1)} %add_convert_fusion.3), channel_id=1, source_target_pairs={{0,4},{1,5},{2,6},{3,7},{4,12},{5,13},{6,14},{7,15},{12,8},{13,9},... | collective-permute-start | bytes 786440 | tf_op jit(solution)/shard_map/ppermute | solution.py:55
  52.9 1.0 %collective-permute-done.21 = bf16[256,2048]{1,0:T(8,128)(2,1)S(1)} collective-permute-done((bf16[256,2048]{1,0:T(8,128)(2,1)S(1)}, bf16[256,2048]{1,0:T(8,128)(2,1)S(1)}, u32[]{:S(2)}, u32[]{:S(2)}) %collective-permute-start.21) | collective-permute-done | bytes 1048608 | tf_op jit(solution)/shard_map/ppermute | solution.py:67
  53.8 0.1 add_convert_fusion.5
  54.0 0.9 collective-permute-start.23
  54.9 0.1 collective-permute-start.27
  55.0 1.6 %collective-permute-start.26 = (bf16[512,256]{1,0:T(8,128)(2,1)S(1)}, bf16[512,256]{1,0:T(8,128)(2,1)S(1)}, u32[]{:S(2)}, u32[]{:S(2)}) collective-permute-start(bf16[512,256]{1,0:T(8,128)(2,1)S(1)} %bitcast.31), channel_id=1, source_target_pairs={{0,16},{16,0},{1,17},{17,1},{2,18},{18,2},{3,19},{19,3},{4,20},{20... | collective-permute-start | bytes 786440 | tf_op jit(solution)/shard_map/ppermute | solution.py:511
  56.5 4.4 %collective-permute-done.24 = bf16[64,2048]{1,0:T(8,128)(2,1)S(1)} collective-permute-done((bf16[64,2048]{1,0:T(8,128)(2,1)S(1)}, bf16[64,2048]{1,0:T(8,128)(2,1)S(1)}, u32[]{:S(2)}, u32[]{:S(2)}) %collective-permute-start.24) | collective-permute-done | bytes 262176 | tf_op jit(solution)/shard_map/ppermute | solution.py:55
  60.9 1.4 %collective-permute-done.23 = bf16[64,2048]{1,0:T(8,128)(2,1)S(1)} collective-permute-done((bf16[64,2048]{1,0:T(8,128)(2,1)S(1)}, bf16[64,2048]{1,0:T(8,128)(2,1)S(1)}, u32[]{:S(2)}, u32[]{:S(2)}) %collective-permute-start.23) | collective-permute-done | bytes 262176 | tf_op jit(solution)/shard_map/ppermute | solution.py:63
  62.4 0.1 add_convert_fusion.2
  62.5 1.2 %collective-permute-done.26.refs_17_ = bf16[512,256]{1,0:T(8,128)(2,1)S(1)} collective-permute-done((bf16[512,256]{1,0:T(8,128)(2,1)S(1)}, bf16[512,256]{1,0:T(8,128)(2,1)S(1)}, u32[]{:S(2)}, u32[]{:S(2)}) %collective-permute-start.26) | collective-permute-done | bytes 262176 | tf_op jit(solution)/shard_map/ppermute | solution.py:511
  63.8 2.6 %collective-permute-start.25 = (bf16[64,2048]{1,0:T(8,128)(2,1)S(1)}, bf16[64,2048]{1,0:T(8,128)(2,1)S(1)}, u32[]{:S(2)}, u32[]{:S(2)}) collective-permute-start(bf16[64,2048]{1,0:T(8,128)(2,1)S(1)} %add_convert_fusion.2), channel_id=1, source_target_pairs={{0,4},{1,5},{2,6},{3,7},{4,12},{5,13},{6,14},{7,15},{12,8},{13,9},... | collective-permute-start | bytes 786440 | tf_op jit(solution)/shard_map/ppermute | solution.py:55
  66.3 0.3 collective-permute-start.22
  66.6 4.8 %values.1 = (bf16[1024,256]{1,0:T(8,128)(2,1)S(1)}, bf16[1024,256]{1,0:T(8,128)(2,1)S(1)}) custom-call(bf16[64,2176]{1,0:T(8,128)(2,1)S(1)} %copy-done.5, bf16[64,2176]{1,0:T(8,128)(2,1)S(1)} %collective-permute-done.3.refs_5_.refs_1_, bf16[64,2176]{1,0:T(8,128)(2,1)S(1)} %collective-permute-done.1.refs_6_.refs_2_, ...), custom_call_target="tpu_custom_call" | custom-call | flops 1 | bytes 1 | tf_op jit(solution)/shard_map/values/pallas_call | solution.py:339
  71.5 0.0 copy-start.7
  71.5 2.8 %collective-permute-done.25 = bf16[64,2048]{1,0:T(8,128)(2,1)S(1)} collective-permute-done((bf16[64,2048]{1,0:T(8,128)(2,1)S(1)}, bf16[64,2048]{1,0:T(8,128)(2,1)S(1)}, u32[]{:S(2)}, u32[]{:S(2)}) %collective-permute-start.25) | collective-permute-done | bytes 262176 | tf_op jit(solution)/shard_map/ppermute | solution.py:55
  74.3 0.5 collective-permute-done.22
  74.7 0.1 add_convert_fusion.1
  74.9 2.7 %collective-permute-start.30 = (bf16[64,2048]{1,0:T(8,128)(2,1)S(1)}, bf16[64,2048]{1,0:T(8,128)(2,1)S(1)}, u32[]{:S(2)}, u32[]{:S(2)}) collective-permute-start(bf16[64,2048]{1,0:T(8,128)(2,1)S(1)} %add_convert_fusion.1), channel_id=1, source_target_pairs={{0,4},{1,5},{2,6},{3,7},{4,12},{5,13},{6,14},{7,15},{12,8},{13,9},... | collective-permute-start | bytes 786440 | tf_op jit(solution)/shard_map/ppermute | solution.py:55
  77.6 0.3 collective-permute-start.29
  77.9 1.8 %attention.4.refs_0_ = bf16[64,4096]{1,0:T(8,128)(2,1)} custom-call(bf16[64,4096]{1,0:T(8,128)(2,1)S(1)} %bitcast.24, bf16[1024,256]{1,0:T(8,128)(2,1)S(1)} %get-tuple-element.53.k_ref, bf16[1024,256]{1,0:T(8,128)(2,1)S(1)} %get-tuple-element.50.v_ref), custom_call_target="tpu_custom_call" | custom-call | flops 1 | bytes 1 | tf_op jit(solution)/shard_map/attention/pallas_call | solution.py:425
  79.7 1.8 %attention.5.refs_0_ = bf16[64,4096]{1,0:T(8,128)(2,1)} custom-call(bf16[64,4096]{1,0:T(8,128)(2,1)S(1)} %bitcast.25, bf16[1024,256]{1,0:T(8,128)(2,1)S(1)} %get-tuple-element.53.k_ref, bf16[1024,256]{1,0:T(8,128)(2,1)S(1)} %get-tuple-element.50.v_ref, bf16[64,4096]{1,0:T(8,128)(2,1)} %attention.4.refs_0_), custom_call_target="tpu_custom_call", output_to_operand_aliasing={{}: (3, {})} | custom-call | flops 1 | bytes 1 | tf_op jit(solution)/shard_map/attention/pallas_call | solution.py:425
  81.6 1.8 %attention.6.refs_0_ = bf16[64,4096]{1,0:T(8,128)(2,1)} custom-call(bf16[64,4096]{1,0:T(8,128)(2,1)S(1)} %bitcast.26, bf16[1024,256]{1,0:T(8,128)(2,1)S(1)} %get-tuple-element.53.k_ref, bf16[1024,256]{1,0:T(8,128)(2,1)S(1)} %get-tuple-element.50.v_ref, bf16[64,4096]{1,0:T(8,128)(2,1)} %attention.5.refs_0_), custom_call_target="tpu_custom_call", output_to_operand_aliasing={{}: (3, {})} | custom-call | flops 1 | bytes 1 | tf_op jit(solution)/shard_map/attention/pallas_call | solution.py:425
  83.4 1.8 %attention.7 = bf16[64,4096]{1,0:T(8,128)(2,1)} custom-call(bf16[64,4096]{1,0:T(8,128)(2,1)S(1)} %bitcast.27, bf16[1024,256]{1,0:T(8,128)(2,1)S(1)} %get-tuple-element.53.k_ref, bf16[1024,256]{1,0:T(8,128)(2,1)S(1)} %get-tuple-element.50.v_ref, bf16[64,4096]{1,0:T(8,128)(2,1)} %attention.6.refs_0_), custom_call_target="tpu_custom_call", output_to_operand_aliasing={{}: (3, {})} | custom-call | flops 1 | bytes 1 | tf_op jit(solution)/shard_map/attention/pallas_call | solution.py:425
  85.3 0.9 %fusion = bf16[64,1,2048]{2,0,1:T(8,128)(2,1)} fusion(bf16[64,2048]{1,0:T(8,128)(2,1)S(1)} %collective-permute-done.30, bf16[64,2048]{1,0:T(8,128)(2,1)S(1)} %collective-permute-done.29, bf16[256,2048]{1,0:T(8,128)(2,1)S(1)} %collective-permute-done.14, bf16[128,2048]{1,0:T(8,128)(2,1)S(1)} %get-tuple-element.34, bf16[64,1,2048]{2,0,1:T(8,128)(2,1)S(1)} %copy-done.7), kind=kLoop, calls=%fused_computation.8 | loop fusion | flops 1310720 | bytes 1572864 | tf_op jit(solution)/shard_map/reshape | solution.py:579
  (35 shorter events, 0.1 us)
Async XLA Ops:
  2.5 4.6 %collective-permute-start.1 = (bf16[64,2176]{1,0:T(8,128)(2,1)}, bf16[64,2176]{1,0:T(8,128)(2,1)S(1)}, u32[]{:S(2)}, u32[]{:S(2)}) collective-permute-start(bf16[64,2176]{1,0:T(8,128)(2,1)} %get-tuple-element.29.refs_4_.refs_0_), channel_id=1, source_target_pairs={{0,1},{1,0},{2,3},{3,2},{4,5},{5,4},{6,7},{7,6},{12,13},{13,12},{1... | collective-permute-start | bytes 835592 | tf_op jit(solution)/shard_map/ppermute | solution.py:67
  2.9 12.5 %collective-permute-start = (bf16[64,2176]{1,0:T(8,128)(2,1)}, bf16[64,2176]{1,0:T(8,128)(2,1)S(1)}, u32[]{:S(2)}, u32[]{:S(2)}) collective-permute-start(bf16[64,2176]{1,0:T(8,128)(2,1)} %get-tuple-element.29.refs_4_.refs_0_), channel_id=1, source_target_pairs={{0,4},{1,5},{2,6},{3,7},{4,12},{5,13},{6,14},{7,15},{12,8},{13,9},... | collective-permute-start | bytes 835592 | tf_op jit(solution)/shard_map/ppermute | solution.py:55
  5.5 11.4 %collective-permute-start.3 = (bf16[64,2176]{1,0:T(8,128)(2,1)}, bf16[64,2176]{1,0:T(8,128)(2,1)S(1)}, u32[]{:S(2)}, u32[]{:S(2)}) collective-permute-start(bf16[64,2176]{1,0:T(8,128)(2,1)} %get-tuple-element.29.refs_4_.refs_0_), channel_id=1, source_target_pairs={{0,2},{1,3},{2,0},{3,1},{4,6},{5,7},{6,4},{7,5},{12,14},{13,15},{1... | collective-permute-start | bytes 835592 | tf_op jit(solution)/shard_map/ppermute | solution.py:63
  7.0 2.8 %copy-start = (bf16[1,2048,1536]{2,1,0:T(8,128)(2,1)S(1)}, bf16[1,2048,1536]{2,1,0:T(8,128)(2,1)}, u32[]{:S(2)}) copy-start(bf16[1,2048,1536]{2,1,0:T(8,128)(2,1)} %param.16) | copy-start | bytes 18874372
  9.8 1.9 %copy-start.2 = (bf16[1,768,2048]{2,1,0:T(8,128)(2,1)S(1)}, bf16[1,768,2048]{2,1,0:T(8,128)(2,1)}, u32[]{:S(2)}) copy-start(bf16[1,768,2048]{2,1,0:T(8,128)(2,1)} %param.17) | copy-start | bytes 9437188
  11.7 0.8 copy-start.6
  12.6 22.0 %copy-start.1 = (bf16[1,2048,1536]{2,1,0:T(8,128)(2,1)S(1)}, bf16[1,2048,1536]{2,1,0:T(8,128)(2,1)}, u32[]{:S(2)}) copy-start(bf16[1,2048,1536]{2,1,0:T(8,128)(2,1)} %param.16) | copy-start | bytes 18874372
  12.6 22.0 %copy-start.3 = (bf16[1,768,2048]{2,1,0:T(8,128)(2,1)S(1)}, bf16[1,768,2048]{2,1,0:T(8,128)(2,1)}, u32[]{:S(2)}) copy-start(bf16[1,768,2048]{2,1,0:T(8,128)(2,1)} %param.17) | copy-start | bytes 9437188
  12.6 22.0 %copy-start.5 = (bf16[64,2176]{1,0:T(8,128)(2,1)S(1)}, bf16[64,2176]{1,0:T(8,128)(2,1)}, u32[]{:S(2)}) copy-start(bf16[64,2176]{1,0:T(8,128)(2,1)} %get-tuple-element.29.refs_4_.refs_0_) | copy-start | bytes 835588
  12.6 4.3 %collective-permute-start.2 = (bf16[128,256]{1,0:T(8,128)(2,1)S(1)}, bf16[128,256]{1,0:T(8,128)(2,1)S(1)}, u32[]{:S(2)}, u32[]{:S(2)}) collective-permute-start(bf16[128,256]{1,0:T(8,128)(2,1)S(1)} %hold_weights.1), channel_id=1, source_target_pairs={{0,2},{1,3},{2,0},{3,1},{4,6},{5,7},{6,4},{7,5},{12,14},{13,15},{1... | collective-permute-start | bytes 196616 | tf_op jit(solution)/shard_map/ppermute | solution.py:63
  13.2 9.7 %collective-permute-start.5 = (bf16[64,2176]{1,0:T(8,128)(2,1)}, bf16[64,2176]{1,0:T(8,128)(2,1)S(1)}, u32[]{:S(2)}, u32[]{:S(2)}) collective-permute-start(bf16[64,2176]{1,0:T(8,128)(2,1)} %get-tuple-element.29.refs_4_.refs_0_), channel_id=1, source_target_pairs={{0,8},{1,9},{2,10},{3,11},{4,0},{5,1},{6,2},{7,3},{12,4},{13,5},{1... | collective-permute-start | bytes 835592 | tf_op jit(solution)/shard_map/ppermute | solution.py:59
  15.4 9.1 %collective-permute-start.7 = (bf16[64,2176]{1,0:T(8,128)(2,1)S(1)}, bf16[64,2176]{1,0:T(8,128)(2,1)S(1)}, u32[]{:S(2)}, u32[]{:S(2)}) collective-permute-start(bf16[64,2176]{1,0:T(8,128)(2,1)S(1)} %collective-permute-done.refs_0_.refs_4_), channel_id=1, source_target_pairs={{0,2},{1,3},{2,0},{3,1},{4,6},{5,7},{6,4},{7,5},{12,14},{13,15},{1... | collective-permute-start | bytes 835592 | tf_op jit(solution)/shard_map/ppermute | solution.py:63
  16.9 13.5 %collective-permute-start.4 = (bf16[64,2176]{1,0:T(8,128)(2,1)S(1)}, bf16[64,2176]{1,0:T(8,128)(2,1)S(1)}, u32[]{:S(2)}, u32[]{:S(2)}) collective-permute-start(bf16[64,2176]{1,0:T(8,128)(2,1)S(1)} %collective-permute-done.refs_0_.refs_4_), channel_id=1, source_target_pairs={{0,4},{1,5},{2,6},{3,7},{4,12},{5,13},{6,14},{7,15},{12,8},{13,9},... | collective-permute-start | bytes 835592 | tf_op jit(solution)/shard_map/ppermute | solution.py:55
  22.8 9.2 %collective-permute-start.6 = (bf16[64,2176]{1,0:T(8,128)(2,1)S(1)}, bf16[64,2176]{1,0:T(8,128)(2,1)S(1)}, u32[]{:S(2)}, u32[]{:S(2)}) collective-permute-start(bf16[64,2176]{1,0:T(8,128)(2,1)S(1)} %collective-permute-done.5.refs_4_.refs_12_), channel_id=1, source_target_pairs={{0,2},{1,3},{2,0},{3,1},{4,6},{5,7},{6,4},{7,5},{12,14},{13,15},{1... | collective-permute-start | bytes 835592 | tf_op jit(solution)/shard_map/ppermute | solution.py:63
  24.1 8.6 %collective-permute-start.10 = (bf16[64,2176]{1,0:T(8,128)(2,1)S(1)}, bf16[64,2176]{1,0:T(8,128)(2,1)S(1)}, u32[]{:S(2)}, u32[]{:S(2)}) collective-permute-start(bf16[64,2176]{1,0:T(8,128)(2,1)S(1)} %collective-permute-done.3.refs_5_.refs_1_), channel_id=1, source_target_pairs={{0,1},{1,0},{2,3},{3,2},{4,5},{5,4},{6,7},{7,6},{12,13},{13,12},{1... | collective-permute-start | bytes 835592 | tf_op jit(solution)/shard_map/ppermute | solution.py:67
  24.1 10.5 %collective-permute-start.8 = (bf16[64,2176]{1,0:T(8,128)(2,1)S(1)}, bf16[64,2176]{1,0:T(8,128)(2,1)S(1)}, u32[]{:S(2)}, u32[]{:S(2)}) collective-permute-start(bf16[64,2176]{1,0:T(8,128)(2,1)S(1)} %collective-permute-done.refs_0_.refs_4_), channel_id=1, source_target_pairs={{0,1},{1,0},{2,3},{3,2},{4,5},{5,4},{6,7},{7,6},{12,13},{13,12},{1... | collective-permute-start | bytes 835592 | tf_op jit(solution)/shard_map/ppermute | solution.py:67
  24.6 10.0 %collective-permute-start.9 = (bf16[64,2176]{1,0:T(8,128)(2,1)S(1)}, bf16[64,2176]{1,0:T(8,128)(2,1)S(1)}, u32[]{:S(2)}, u32[]{:S(2)}) collective-permute-start(bf16[64,2176]{1,0:T(8,128)(2,1)S(1)} %collective-permute-done.7.refs_1_.refs_5_), channel_id=1, source_target_pairs={{0,1},{1,0},{2,3},{3,2},{4,5},{5,4},{6,7},{7,6},{12,13},{13,12},{1... | collective-permute-start | bytes 835592 | tf_op jit(solution)/shard_map/ppermute | solution.py:67
  30.5 9.5 %collective-permute-start.11 = (bf16[64,2176]{1,0:T(8,128)(2,1)S(1)}, bf16[64,2176]{1,0:T(8,128)(2,1)S(1)}, u32[]{:S(2)}, u32[]{:S(2)}) collective-permute-start(bf16[64,2176]{1,0:T(8,128)(2,1)S(1)} %collective-permute-done.4.refs_0_.refs_8_), channel_id=1, source_target_pairs={{0,2},{1,3},{2,0},{3,1},{4,6},{5,7},{6,4},{7,5},{12,14},{13,15},{1... | collective-permute-start | bytes 835592 | tf_op jit(solution)/shard_map/ppermute | solution.py:63
  32.0 7.9 %collective-permute-start.13 = (bf16[256,256]{1,0:T(8,128)(2,1)S(1)}, bf16[256,256]{1,0:T(8,128)(2,1)S(1)}, u32[]{:S(2)}, u32[]{:S(2)}) collective-permute-start(bf16[256,256]{1,0:T(8,128)(2,1)S(1)} %pad_maximum_fusion), channel_id=1, source_target_pairs={{0,8},{1,9},{2,10},{3,11},{4,0},{5,1},{6,2},{7,3},{12,4},{13,5},{1... | collective-permute-start | bytes 393224 | tf_op jit(solution)/shard_map/ppermute | solution.py:59
  32.7 7.3 %collective-permute-start.12 = (bf16[256,256]{1,0:T(8,128)(2,1)S(1)}, bf16[256,256]{1,0:T(8,128)(2,1)S(1)}, u32[]{:S(2)}, u32[]{:S(2)}) collective-permute-start(bf16[256,256]{1,0:T(8,128)(2,1)S(1)} %pad_maximum_fusion), channel_id=1, source_target_pairs={{0,4},{1,5},{2,6},{3,7},{4,12},{5,13},{6,14},{7,15},{12,8},{13,9},... | collective-permute-start | bytes 393224 | tf_op jit(solution)/shard_map/ppermute | solution.py:55
  40.0 2.7 %collective-permute-start.14 = (bf16[256,2048]{1,0:T(8,128)(2,1)S(1)}, bf16[256,2048]{1,0:T(8,128)(2,1)S(1)}, u32[]{:S(2)}, u32[]{:S(2)}) collective-permute-start(bf16[256,2048]{1,0:T(8,128)(2,1)S(1)} %get-tuple-element.37), channel_id=1, source_target_pairs={{0,1},{1,0},{2,3},{3,2},{4,5},{5,4},{6,7},{7,6},{12,13},{13,12},{1... | collective-permute-start | bytes 3145736 | tf_op jit(solution)/shard_map/ppermute | solution.py:67
  40.0 3.5 %collective-permute-start.17 = (bf16[64,2176]{1,0:T(8,128)(2,1)S(1)}, bf16[64,2176]{1,0:T(8,128)(2,1)S(1)}, u32[]{:S(2)}, u32[]{:S(2)}) collective-permute-start(bf16[64,2176]{1,0:T(8,128)(2,1)S(1)} %collective-permute-done.5.refs_4_.refs_12_), channel_id=1, source_target_pairs={{0,1},{1,0},{2,3},{3,2},{4,5},{5,4},{6,7},{7,6},{12,13},{13,12},{1... | collective-permute-start | bytes 835592 | tf_op jit(solution)/shard_map/ppermute | solution.py:67
  40.5 5.6 %collective-permute-start.18 = (bf16[64,2176]{1,0:T(8,128)(2,1)S(1)}, bf16[64,2176]{1,0:T(8,128)(2,1)S(1)}, u32[]{:S(2)}, u32[]{:S(2)}) collective-permute-start(bf16[64,2176]{1,0:T(8,128)(2,1)S(1)} %collective-permute-done.6.refs_5_.refs_13_), channel_id=1, source_target_pairs={{0,1},{1,0},{2,3},{3,2},{4,5},{5,4},{6,7},{7,6},{12,13},{13,12},{1... | collective-permute-start | bytes 835592 | tf_op jit(solution)/shard_map/ppermute | solution.py:67
  40.5 5.6 %collective-permute-start.15 = (bf16[64,2176]{1,0:T(8,128)(2,1)S(1)}, bf16[64,2176]{1,0:T(8,128)(2,1)S(1)}, u32[]{:S(2)}, u32[]{:S(2)}) collective-permute-start(bf16[64,2176]{1,0:T(8,128)(2,1)S(1)} %collective-permute-done.4.refs_0_.refs_8_), channel_id=1, source_target_pairs={{0,1},{1,0},{2,3},{3,2},{4,5},{5,4},{6,7},{7,6},{12,13},{13,12},{1... | collective-permute-start | bytes 835592 | tf_op jit(solution)/shard_map/ppermute | solution.py:67
  41.0 5.1 %collective-permute-start.16 = (bf16[64,2176]{1,0:T(8,128)(2,1)S(1)}, bf16[64,2176]{1,0:T(8,128)(2,1)S(1)}, u32[]{:S(2)}, u32[]{:S(2)}) collective-permute-start(bf16[64,2176]{1,0:T(8,128)(2,1)S(1)} %collective-permute-done.11.refs_1_.refs_9_), channel_id=1, source_target_pairs={{0,1},{1,0},{2,3},{3,2},{4,5},{5,4},{6,7},{7,6},{12,13},{13,12},{1... | collective-permute-start | bytes 835592 | tf_op jit(solution)/shard_map/ppermute | solution.py:67
  42.8 8.4 %collective-permute-start.19 = (bf16[64,2048]{1,0:T(8,128)(2,1)S(1)}, bf16[64,2048]{1,0:T(8,128)(2,1)S(1)}, u32[]{:S(2)}, u32[]{:S(2)}) collective-permute-start(bf16[64,2048]{1,0:T(8,128)(2,1)S(1)} %get-tuple-element.59), channel_id=1, source_target_pairs={{0,2},{1,3},{2,0},{3,1},{4,6},{5,7},{6,4},{7,5},{12,14},{13,15},{1... | collective-permute-start | bytes 786440 | tf_op jit(solution)/shard_map/ppermute | solution.py:63
  43.4 7.2 %collective-permute-start.20 = (bf16[256,256]{1,0:T(8,128)(2,1)S(1)}, bf16[256,256]{1,0:T(8,128)(2,1)S(1)}, u32[]{:S(2)}, u32[]{:S(2)}) collective-permute-start(bf16[256,256]{1,0:T(8,128)(2,1)S(1)} %collective-permute-done.12), channel_id=1, source_target_pairs={{0,4},{1,5},{2,6},{3,7},{4,12},{5,13},{6,14},{7,15},{12,8},{13,9},... | collective-permute-start | bytes 393224 | tf_op jit(solution)/shard_map/ppermute | solution.py:55
  51.2 26.7 %copy-start.4 = (bf16[64,1,4096]{2,0,1:T(8,128)(2,1)S(1)}, bf16[64,1,4096]{2,0,1:T(8,128)(2,1)}, u32[]{:S(2)}) copy-start(bf16[64,1,4096]{2,0,1:T(8,128)(2,1)} %param.10) | copy-start | bytes 1572868
  51.2 2.7 %collective-permute-start.21 = (bf16[256,2048]{1,0:T(8,128)(2,1)S(1)}, bf16[256,2048]{1,0:T(8,128)(2,1)S(1)}, u32[]{:S(2)}, u32[]{:S(2)}) collective-permute-start(bf16[256,2048]{1,0:T(8,128)(2,1)S(1)} %get-tuple-element.42), channel_id=1, source_target_pairs={{0,1},{1,0},{2,3},{3,2},{4,5},{5,4},{6,7},{7,6},{12,13},{13,12},{1... | collective-permute-start | bytes 3145736 | tf_op jit(solution)/shard_map/ppermute | solution.py:67
  51.3 9.7 %collective-permute-start.24 = (bf16[64,2048]{1,0:T(8,128)(2,1)S(1)}, bf16[64,2048]{1,0:T(8,128)(2,1)S(1)}, u32[]{:S(2)}, u32[]{:S(2)}) collective-permute-start(bf16[64,2048]{1,0:T(8,128)(2,1)S(1)} %add_convert_fusion.3), channel_id=1, source_target_pairs={{0,4},{1,5},{2,6},{3,7},{4,12},{5,13},{6,14},{7,15},{12,8},{13,9},... | collective-permute-start | bytes 786440 | tf_op jit(solution)/shard_map/ppermute | solution.py:55
  54.0 8.4 %collective-permute-start.23 = (bf16[64,2048]{1,0:T(8,128)(2,1)S(1)}, bf16[64,2048]{1,0:T(8,128)(2,1)S(1)}, u32[]{:S(2)}, u32[]{:S(2)}) collective-permute-start(bf16[64,2048]{1,0:T(8,128)(2,1)S(1)} %get-tuple-element.57), channel_id=1, source_target_pairs={{0,2},{1,3},{2,0},{3,1},{4,6},{5,7},{6,4},{7,5},{12,14},{13,15},{1... | collective-permute-start | bytes 786440 | tf_op jit(solution)/shard_map/ppermute | solution.py:63
  54.9 11.7 %collective-permute-start.27 = (bf16[1024,256]{1,0:T(8,128)(2,1)S(1)}, bf16[1024,256]{1,0:T(8,128)(2,1)S(1)}, u32[]{:S(2)}, u32[]{:S(2)}) collective-permute-start(bf16[1024,256]{1,0:T(8,128)(2,1)S(1)} %constant_dynamic-update-slice_fusion.refs_16_), channel_id=1, source_target_pairs={{0,1},{1,0},{2,3},{3,2},{4,5},{5,4},{6,7},{7,6},{12,13},{13,12},{1... | collective-permute-start | bytes 1572872 | tf_op jit(solution)/shard_map/ppermute | solution.py:67
  55.0 8.8 %collective-permute-start.26 = (bf16[512,256]{1,0:T(8,128)(2,1)S(1)}, bf16[512,256]{1,0:T(8,128)(2,1)S(1)}, u32[]{:S(2)}, u32[]{:S(2)}) collective-permute-start(bf16[512,256]{1,0:T(8,128)(2,1)S(1)} %bitcast.31), channel_id=1, source_target_pairs={{0,16},{16,0},{1,17},{17,1},{2,18},{18,2},{3,19},{19,3},{4,20},{20... | collective-permute-start | bytes 786440 | tf_op jit(solution)/shard_map/ppermute | solution.py:511
  63.8 2.8 %collective-permute-start.28 = (bf16[512,256]{1,0:T(8,128)(2,1)S(1)}, bf16[512,256]{1,0:T(8,128)(2,1)S(1)}, u32[]{:S(2)}, u32[]{:S(2)}) collective-permute-start(bf16[512,256]{1,0:T(8,128)(2,1)S(1)} %collective-permute-done.26.refs_17_), channel_id=1, source_target_pairs={{0,1},{1,0},{2,3},{3,2},{4,5},{5,4},{6,7},{7,6},{12,13},{13,12},{1... | collective-permute-start | bytes 786440 | tf_op jit(solution)/shard_map/ppermute | solution.py:67
  63.8 10.5 %collective-permute-start.25 = (bf16[64,2048]{1,0:T(8,128)(2,1)S(1)}, bf16[64,2048]{1,0:T(8,128)(2,1)S(1)}, u32[]{:S(2)}, u32[]{:S(2)}) collective-permute-start(bf16[64,2048]{1,0:T(8,128)(2,1)S(1)} %add_convert_fusion.2), channel_id=1, source_target_pairs={{0,4},{1,5},{2,6},{3,7},{4,12},{5,13},{6,14},{7,15},{12,8},{13,9},... | collective-permute-start | bytes 786440 | tf_op jit(solution)/shard_map/ppermute | solution.py:55
  66.3 8.4 %collective-permute-start.22 = (bf16[64,2048]{1,0:T(8,128)(2,1)S(1)}, bf16[64,2048]{1,0:T(8,128)(2,1)S(1)}, u32[]{:S(2)}, u32[]{:S(2)}) collective-permute-start(bf16[64,2048]{1,0:T(8,128)(2,1)S(1)} %get-tuple-element.56), channel_id=1, source_target_pairs={{0,2},{1,3},{2,0},{3,1},{4,6},{5,7},{6,4},{7,5},{12,14},{13,15},{1... | collective-permute-start | bytes 786440 | tf_op jit(solution)/shard_map/ppermute | solution.py:63
  71.5 13.8 %copy-start.7 = (bf16[64,1,2048]{2,0,1:T(8,128)(2,1)S(1)}, bf16[64,1,2048]{2,0,1:T(8,128)(2,1)}, u32[]{:S(2)}) copy-start(bf16[64,1,2048]{2,0,1:T(8,128)(2,1)} %param.9) | copy-start | bytes 786436
  74.9 10.4 %collective-permute-start.30 = (bf16[64,2048]{1,0:T(8,128)(2,1)S(1)}, bf16[64,2048]{1,0:T(8,128)(2,1)S(1)}, u32[]{:S(2)}, u32[]{:S(2)}) collective-permute-start(bf16[64,2048]{1,0:T(8,128)(2,1)S(1)} %add_convert_fusion.1), channel_id=1, source_target_pairs={{0,4},{1,5},{2,6},{3,7},{4,12},{5,13},{6,14},{7,15},{12,8},{13,9},... | collective-permute-start | bytes 786440 | tf_op jit(solution)/shard_map/ppermute | solution.py:55
  77.6 7.6 %collective-permute-start.29 = (bf16[64,2048]{1,0:T(8,128)(2,1)S(1)}, bf16[64,2048]{1,0:T(8,128)(2,1)S(1)}, u32[]{:S(2)}, u32[]{:S(2)}) collective-permute-start(bf16[64,2048]{1,0:T(8,128)(2,1)S(1)} %get-tuple-element.54), channel_id=1, source_target_pairs={{0,2},{1,3},{2,0},{3,1},{4,6},{5,7},{6,4},{7,5},{12,14},{13,15},{1... | collective-permute-start | bytes 786440 | tf_op jit(solution)/shard_map/ppermute | solution.py:63

commit v13 on v12

--- a/solution.py
+++ b/solution.py
@@ -506,20 +506,20 @@
     total = summed(*mine[1], after(theirs[1], send))
     moving = forward(total)
     theirs[2], theirs[3] = across(crossing[2]), across(crossing[3])
-    own = jnp.concatenate(after(tuple(pairs), *crossing[2:], total), axis=0)
+    own = jnp.concatenate(pairs, axis=0)
     shares = own.reshape(2 * LINE, small.shape[0], -1)[:, rows:]
     other = lax.ppermute(shares.reshape(-1, own.shape[1]), "grp", [(0, 1), (1, 0)])
     total = summed(*mine[2], theirs[2], moving)
     moving = forward(total)
     theirs[0] = across(after(crossing[0], total))
-    other = after(other, total)
-    smalls = [own, other, other_core(own), other_core(other)]
+    smalls = [own, other, other_core(own), other_core(after(other, crossing[3]))]
+    smalls[0] = after(own, total)
     new_keys, values = make_values(sum(arrays, []), blocks, smalls, rows, width)
-    total = summed(*mine[3], theirs[3], after(moving, values))
+    context = attend_part(queries, new_keys, values, 0, 4)
+    total = summed(*mine[3], theirs[3], after(moving, context))
     moving = forward(total)
     queries = after(queries, total)
-    context = None
-    for part in range(4):
+    for part in range(1, 4):
         context = attend_part(queries, new_keys, values, part, 4, context)
     layer_out = summed(acts, *mine[0], theirs[0], after(moving, context))
     return context, layer_out

time: 86.4 us -> 83.3 us (0.964)
  waiting for transfers between devices: 26.4 us -> 22.1 us
  starting transfers between devices: 31.5 us -> 32.7 us
    ppermute x7, waiting for transfers between devices: 14.5 us -> 10 us  [forward(): return lax.ppermute(x, 'seq', ring_steps(1))]
    ppermute x9, starting transfers between devices: 7.54 us -> 10.2 us  [across(): return lax.ppermute(x, 'seq', swaps(1, 0))]
    ppermute x1, waiting for transfers between devices: 1.24 us -> 3.58 us  [on_line(): lax.ppermute(shares.reshape(-1, own.shape[1]), 'grp', [(0, 1), (1, 0)])]
    ppermute x7, starting transfers between devices: 17.3 us -> 15.9 us  [forward(): return lax.ppermute(x, 'seq', ring_steps(1))]
    ppermute x9, waiting for transfers between devices: 3.33 us -> 2.1 us  [across(): return lax.ppermute(x, 'seq', swaps(1, 0))]
    ppermute x12, waiting for transfers between devices: 2.55 us -> 1.6 us  [other_core(): return lax.ppermute(x, 'seq', swaps(0, 1))]
  transfers between devices with their start and end apart: 31 -> 31, of which waited for: 13 -> 12; matrix products, arithmetic and copies ran while one was open for 1% -> 1% of each run, Pallas kernels for 22% -> 22%
where the time goes in v13:
time: 83.3 us; the launch traced here: 83.1 us
  starting transfers between devices  32.7 us (39%)
  waiting for transfers between devices  22.1 us (27%)
  Pallas kernels  20.4 us (24%)
  local copies, waits for them, and re-layouts  5.6 us (7%)
  other arithmetic  1.5 us (2%)
    ppermute x7, starting transfers between devices, forward(): return lax.ppermute(x, 'seq', ring_steps(1))  15.9 us
    ppermute x9, starting transfers between devices, across(): return lax.ppermute(x, 'seq', swaps(1, 0))  10.2 us
    ppermute x7, waiting for transfers between devices, forward(): return lax.ppermute(x, 'seq', ring_steps(1))  10 us
    pallas_call x4, Pallas kernels, attend_part(): pl.pallas_call(functools.partial(attention_kernel, chunk), grid=(1,), out...  7.34 us
    pallas_call x2, Pallas kernels, run_experts(): pl.pallas_call(functools.partial(expert_kernel, top, tok_rows, capacity,...  6.36 us
    unnamed x19, local copies, waits for them, and re-layouts  5.57 us
    pallas_call x1, Pallas kernels, make_values(): pl.pallas_call(functools.partial(value_kernel, key_rows, blocks), out_sha...  4.84 us
    ppermute x2, waiting for transfers between devices, backward(): return lax.ppermute(x, 'seq', ring_steps(LINE - 1))  4.77 us
  transfers between devices with their start and end apart: 31, of which 12 were waited for; matrix products, arithmetic and copies ran while one was open for 1% of the time, Pallas kernels for 22%

profile of v13, /device:TPU:0, one launch (start us, length us, event | category | flops | bytes accessed | tf_op | source)
XLA Modules:
  0.0 83.1 jit_solution(17243983897501580589)
XLA Ops:
  0.6 1.9 %normalize_and_pack.1 = (bf16[64,2176]{1,0:T(8,128)(2,1)}, bf16[128,256]{1,0:T(8,128)(2,1)}) custom-call(bf16[64,2048]{1,0:T(8,128)(2,1)} %bitcast.30, f32[1,2048]{1,0:T(1,128)} %bitcast.33, s32[4,64]{1,0:T(4,128)} %bitcast.34, f32[4,64]{1,0:T(4,128)} %bitcast.35, bf16[64,256]{1,0:T(8,128)(2,1)} %bitcast.32, bf16[128,256]{1,0:T(8,128)(2,1)} %weight_ref.1), custom_call_target="tpu_custom_call" | custom-call | flops 1 | bytes 1 | tf_op jit(solution)/shard_map/normalize_and_pack/pallas_call | solution.py:112
  2.5 0.5 collective-permute-start.1
  2.9 2.6 %collective-permute-start = (bf16[64,2176]{1,0:T(8,128)(2,1)}, bf16[64,2176]{1,0:T(8,128)(2,1)S(1)}, u32[]{:S(2)}, u32[]{:S(2)}) collective-permute-start(bf16[64,2176]{1,0:T(8,128)(2,1)} %get-tuple-element.26.refs_4_.refs_0_), channel_id=1, source_target_pairs={{0,4},{1,5},{2,6},{3,7},{4,12},{5,13},{6,14},{7,15},{12,8},{13,9},... | collective-permute-start | bytes 835592 | tf_op jit(solution)/shard_map/ppermute | solution.py:55
  5.5 1.5 %collective-permute-start.3 = (bf16[64,2176]{1,0:T(8,128)(2,1)}, bf16[64,2176]{1,0:T(8,128)(2,1)S(1)}, u32[]{:S(2)}, u32[]{:S(2)}) collective-permute-start(bf16[64,2176]{1,0:T(8,128)(2,1)} %get-tuple-element.26.refs_4_.refs_0_), channel_id=1, source_target_pairs={{0,2},{1,3},{2,0},{3,1},{4,6},{5,7},{6,4},{7,5},{12,14},{13,15},{1... | collective-permute-start | bytes 835592 | tf_op jit(solution)/shard_map/ppermute | solution.py:63
  7.0 2.8 %copy-done = bf16[1,2048,1536]{2,1,0:T(8,128)(2,1)S(1)} copy-done((bf16[1,2048,1536]{2,1,0:T(8,128)(2,1)S(1)}, bf16[1,2048,1536]{2,1,0:T(8,128)(2,1)}, u32[]{:S(2)}) %copy-start) | copy-done | bytes 6291480
  9.8 1.9 %copy-done.2 = bf16[1,768,2048]{2,1,0:T(8,128)(2,1)S(1)} copy-done((bf16[1,768,2048]{2,1,0:T(8,128)(2,1)S(1)}, bf16[1,768,2048]{2,1,0:T(8,128)(2,1)}, u32[]{:S(2)}) %copy-start.2) | copy-done | bytes 3145752
  11.7 0.8 %copy-done.6 = bf16[128,256]{1,0:T(8,128)(2,1)S(1)} copy-done((bf16[128,256]{1,0:T(8,128)(2,1)S(1)}, bf16[128,256]{1,0:T(8,128)(2,1)}, u32[]{:S(2)}) %copy-start.6) | copy-done | bytes 65560
  12.6 0.6 collective-permute-start.2
  13.2 2.3 %collective-permute-start.5 = (bf16[64,2176]{1,0:T(8,128)(2,1)}, bf16[64,2176]{1,0:T(8,128)(2,1)S(1)}, u32[]{:S(2)}, u32[]{:S(2)}) collective-permute-start(bf16[64,2176]{1,0:T(8,128)(2,1)} %get-tuple-element.26.refs_4_.refs_0_), channel_id=1, source_target_pairs={{0,8},{1,9},{2,10},{3,11},{4,0},{5,1},{6,2},{7,3},{12,4},{13,5},{1... | collective-permute-start | bytes 835592 | tf_op jit(solution)/shard_map/ppermute | solution.py:59
  15.4 0.0 collective-permute-done.refs_0_.refs_4_
  15.4 0.6 collective-permute-start.7
  16.0 0.9 %collective-permute-done.2 = bf16[128,256]{1,0:T(8,128)(2,1)S(1)} collective-permute-done((bf16[128,256]{1,0:T(8,128)(2,1)S(1)}, bf16[128,256]{1,0:T(8,128)(2,1)S(1)}, u32[]{:S(2)}, u32[]{:S(2)}) %collective-permute-start.2) | collective-permute-done | bytes 65568 | tf_op jit(solution)/shard_map/ppermute | solution.py:63
  16.9 3.3 %collective-permute-start.4 = (bf16[64,2176]{1,0:T(8,128)(2,1)S(1)}, bf16[64,2176]{1,0:T(8,128)(2,1)S(1)}, u32[]{:S(2)}, u32[]{:S(2)}) collective-permute-start(bf16[64,2176]{1,0:T(8,128)(2,1)S(1)} %collective-permute-done.refs_0_.refs_4_), channel_id=1, source_target_pairs={{0,4},{1,5},{2,6},{3,7},{4,12},{5,13},{6,14},{7,15},{12,8},{13,9},... | collective-permute-start | bytes 835592 | tf_op jit(solution)/shard_map/ppermute | solution.py:55
  20.3 2.6 %collective-permute-done.5.refs_4_.refs_12_ = bf16[64,2176]{1,0:T(8,128)(2,1)S(1)} collective-permute-done((bf16[64,2176]{1,0:T(8,128)(2,1)}, bf16[64,2176]{1,0:T(8,128)(2,1)S(1)}, u32[]{:S(2)}, u32[]{:S(2)}) %collective-permute-start.5) | collective-permute-done | bytes 278560 | tf_op jit(solution)/shard_map/ppermute | solution.py:59
  22.8 1.2 %collective-permute-start.6 = (bf16[64,2176]{1,0:T(8,128)(2,1)S(1)}, bf16[64,2176]{1,0:T(8,128)(2,1)S(1)}, u32[]{:S(2)}, u32[]{:S(2)}) collective-permute-start(bf16[64,2176]{1,0:T(8,128)(2,1)S(1)} %collective-permute-done.5.refs_4_.refs_12_), channel_id=1, source_target_pairs={{0,2},{1,3},{2,0},{3,1},{4,6},{5,7},{6,4},{7,5},{12,14},{13,15},{1... | collective-permute-start | bytes 835592 | tf_op jit(solution)/shard_map/ppermute | solution.py:63
  24.1 0.0 collective-permute-start.10
  24.1 0.5 collective-permute-start.8
  24.6 0.0 collective-permute-start.9
  24.6 5.9 %collective-permute-done.4.refs_0_.refs_8_ = bf16[64,2176]{1,0:T(8,128)(2,1)S(1)} collective-permute-done((bf16[64,2176]{1,0:T(8,128)(2,1)S(1)}, bf16[64,2176]{1,0:T(8,128)(2,1)S(1)}, u32[]{:S(2)}, u32[]{:S(2)}) %collective-permute-start.4) | collective-permute-done | bytes 278560 | tf_op jit(solution)/shard_map/ppermute | solution.py:55
  30.5 1.5 %collective-permute-start.11 = (bf16[64,2176]{1,0:T(8,128)(2,1)S(1)}, bf16[64,2176]{1,0:T(8,128)(2,1)S(1)}, u32[]{:S(2)}, u32[]{:S(2)}) collective-permute-start(bf16[64,2176]{1,0:T(8,128)(2,1)S(1)} %collective-permute-done.4.refs_0_.refs_8_), channel_id=1, source_target_pairs={{0,2},{1,3},{2,0},{3,1},{4,6},{5,7},{6,4},{7,5},{12,14},{13,15},{1... | collective-permute-start | bytes 835592 | tf_op jit(solution)/shard_map/ppermute | solution.py:63
  32.0 0.0 collective-permute-done.6.refs_5_.refs_13_
  32.0 0.7 collective-permute-start.13
  32.7 1.9 %collective-permute-start.12 = (bf16[256,256]{1,0:T(8,128)(2,1)S(1)}, bf16[256,256]{1,0:T(8,128)(2,1)S(1)}, u32[]{:S(2)}, u32[]{:S(2)}) collective-permute-start(bf16[256,256]{1,0:T(8,128)(2,1)S(1)} %pad_maximum_fusion), channel_id=1, source_target_pairs={{0,4},{1,5},{2,6},{3,7},{4,12},{5,13},{6,14},{7,15},{12,8},{13,9},... | collective-permute-start | bytes 393224 | tf_op jit(solution)/shard_map/ppermute | solution.py:55
  34.5 0.0 collective-permute-done.9.refs_3_.refs_7_
  34.6 3.2 %experts.2 = (bf16[128,2048]{1,0:T(8,128)(2,1)S(1)}, bf16[128,2048]{1,0:T(8,128)(2,1)S(1)}, bf16[256,2048]{1,0:T(8,128)(2,1)S(1)}) custom-call(bf16[64,2176]{1,0:T(8,128)(2,1)S(1)} %collective-permute-done.refs_0_.refs_4_, bf16[64,2176]{1,0:T(8,128)(2,1)S(1)} %collective-permute-done.7.refs_1_.refs_5_, ...), custom_call_target="tpu_custom_call" | custom-call | flops 1 | bytes 1 | tf_op jit(solution)/shard_map/experts/pallas_call | solution.py:290
  37.7 2.2 %collective-permute-done.13 = bf16[256,256]{1,0:T(8,128)(2,1)S(1)} collective-permute-done((bf16[256,256]{1,0:T(8,128)(2,1)S(1)}, bf16[256,256]{1,0:T(8,128)(2,1)S(1)}, u32[]{:S(2)}, u32[]{:S(2)}) %collective-permute-start.13) | collective-permute-done | bytes 131104 | tf_op jit(solution)/shard_map/ppermute | solution.py:59
  39.9 0.0 collective-permute-done.12
  40.0 0.0 collective-permute-done.11.refs_1_.refs_9_
  40.0 0.0 collective-permute-start.14
  40.0 0.5 collective-permute-start.17
  40.5 0.1 collective-permute-start.18
  40.5 0.4 collective-permute-start.15
  41.0 0.1 collective-permute-start.16
  41.1 1.6 %collective-permute-done.14 = bf16[256,2048]{1,0:T(8,128)(2,1)S(1)} collective-permute-done((bf16[256,2048]{1,0:T(8,128)(2,1)S(1)}, bf16[256,2048]{1,0:T(8,128)(2,1)S(1)}, u32[]{:S(2)}, u32[]{:S(2)}) %collective-permute-start.14) | collective-permute-done | bytes 1048608 | tf_op jit(solution)/shard_map/ppermute | solution.py:67
  42.6 0.1 add_convert_fusion.7
  42.8 0.7 collective-permute-start.19
  43.4 2.7 %collective-permute-start.20 = (bf16[256,256]{1,0:T(8,128)(2,1)S(1)}, bf16[256,256]{1,0:T(8,128)(2,1)S(1)}, u32[]{:S(2)}, u32[]{:S(2)}) collective-permute-start(bf16[256,256]{1,0:T(8,128)(2,1)S(1)} %collective-permute-done.12), channel_id=1, source_target_pairs={{0,4},{1,5},{2,6},{3,7},{4,12},{5,13},{6,14},{7,15},{12,8},{13,9},... | collective-permute-start | bytes 393224 | tf_op jit(solution)/shard_map/ppermute | solution.py:55
  46.1 3.2 %experts.3 = (bf16[128,2048]{1,0:T(8,128)(2,1)S(1)}, bf16[128,2048]{1,0:T(8,128)(2,1)S(1)}, bf16[256,2048]{1,0:T(8,128)(2,1)S(1)}) custom-call(bf16[64,2176]{1,0:T(8,128)(2,1)S(1)} %collective-permute-done.4.refs_0_.refs_8_, bf16[64,2176]{1,0:T(8,128)(2,1)S(1)} %collective-permute-done.11.refs_1_.refs_9_, ...), custom_call_target="tpu_custom_call" | custom-call | flops 1 | bytes 1 | tf_op jit(solution)/shard_map/experts/pallas_call | solution.py:290
  49.3 0.0 copy-start.4
  49.3 1.3 %collective-permute-done.20 = bf16[256,256]{1,0:T(8,128)(2,1)S(1)} collective-permute-done((bf16[256,256]{1,0:T(8,128)(2,1)S(1)}, bf16[256,256]{1,0:T(8,128)(2,1)S(1)}, u32[]{:S(2)}, u32[]{:S(2)}) %collective-permute-start.20) | collective-permute-done | bytes 131104 | tf_op jit(solution)/shard_map/ppermute | solution.py:55
  50.7 0.5 collective-permute-done.19
  51.3 1.6 %collective-permute-start.26 = (bf16[512,256]{1,0:T(8,128)(2,1)S(1)}, bf16[512,256]{1,0:T(8,128)(2,1)S(1)}, u32[]{:S(2)}, u32[]{:S(2)}) collective-permute-start(bf16[512,256]{1,0:T(8,128)(2,1)S(1)} %bitcast.31), channel_id=1, source_target_pairs={{0,16},{16,0},{1,17},{17,1},{2,18},{18,2},{3,19},{19,3},{4,20},{20... | collective-permute-start | bytes 786440 | tf_op jit(solution)/shard_map/ppermute | solution.py:511
  52.8 0.1 add_convert_fusion.3
  52.9 1.6 %collective-permute-start.24 = (bf16[64,2048]{1,0:T(8,128)(2,1)S(1)}, bf16[64,2048]{1,0:T(8,128)(2,1)S(1)}, u32[]{:S(2)}, u32[]{:S(2)}) collective-permute-start(bf16[64,2048]{1,0:T(8,128)(2,1)S(1)} %add_convert_fusion.3), channel_id=1, source_target_pairs={{0,4},{1,5},{2,6},{3,7},{4,12},{5,13},{6,14},{7,15},{12,8},{13,9},... | collective-permute-start | bytes 786440 | tf_op jit(solution)/shard_map/ppermute | solution.py:55
  54.5 0.1 add_convert_fusion.5
  54.7 1.8 %collective-permute-start.23 = (bf16[64,2048]{1,0:T(8,128)(2,1)S(1)}, bf16[64,2048]{1,0:T(8,128)(2,1)S(1)}, u32[]{:S(2)}, u32[]{:S(2)}) collective-permute-start(bf16[64,2048]{1,0:T(8,128)(2,1)S(1)} %get-tuple-element.51), channel_id=1, source_target_pairs={{0,2},{1,3},{2,0},{3,1},{4,6},{5,7},{6,4},{7,5},{12,14},{13,15},{1... | collective-permute-start | bytes 786440 | tf_op jit(solution)/shard_map/ppermute | solution.py:63
  56.5 3.6 %collective-permute-done.26.refs_17_ = bf16[512,256]{1,0:T(8,128)(2,1)S(1)} collective-permute-done((bf16[512,256]{1,0:T(8,128)(2,1)S(1)}, bf16[512,256]{1,0:T(8,128)(2,1)S(1)}, u32[]{:S(2)}, u32[]{:S(2)}) %collective-permute-start.26) | collective-permute-done | bytes 262176 | tf_op jit(solution)/shard_map/ppermute | solution.py:511
  60.1 2.3 %collective-permute-done.24 = bf16[64,2048]{1,0:T(8,128)(2,1)S(1)} collective-permute-done((bf16[64,2048]{1,0:T(8,128)(2,1)S(1)}, bf16[64,2048]{1,0:T(8,128)(2,1)S(1)}, u32[]{:S(2)}, u32[]{:S(2)}) %collective-permute-start.24) | collective-permute-done | bytes 262176 | tf_op jit(solution)/shard_map/ppermute | solution.py:55
  62.3 0.6 collective-permute-done.23
  62.9 0.1 add_convert_fusion.2
  63.0 2.6 %collective-permute-start.25 = (bf16[64,2048]{1,0:T(8,128)(2,1)S(1)}, bf16[64,2048]{1,0:T(8,128)(2,1)S(1)}, u32[]{:S(2)}, u32[]{:S(2)}) collective-permute-start(bf16[64,2048]{1,0:T(8,128)(2,1)S(1)} %add_convert_fusion.2), channel_id=1, source_target_pairs={{0,4},{1,5},{2,6},{3,7},{4,12},{5,13},{6,14},{7,15},{12,8},{13,9},... | collective-permute-start | bytes 786440 | tf_op jit(solution)/shard_map/ppermute | solution.py:55
  65.6 1.7 %collective-permute-start.22 = (bf16[64,2048]{1,0:T(8,128)(2,1)S(1)}, bf16[64,2048]{1,0:T(8,128)(2,1)S(1)}, u32[]{:S(2)}, u32[]{:S(2)}) collective-permute-start(bf16[64,2048]{1,0:T(8,128)(2,1)S(1)} %get-tuple-element.50), channel_id=1, source_target_pairs={{0,2},{1,3},{2,0},{3,1},{4,6},{5,7},{6,4},{7,5},{12,14},{13,15},{1... | collective-permute-start | bytes 786440 | tf_op jit(solution)/shard_map/ppermute | solution.py:63
  67.4 4.8 %values.1 = (bf16[1024,256]{1,0:T(8,128)(2,1)S(1)}, bf16[1024,256]{1,0:T(8,128)(2,1)S(1)}) custom-call(bf16[64,2176]{1,0:T(8,128)(2,1)S(1)} %copy-done.5, bf16[64,2176]{1,0:T(8,128)(2,1)S(1)} %collective-permute-done.3.refs_5_.refs_1_, bf16[64,2176]{1,0:T(8,128)(2,1)S(1)} %collective-permute-done.1.refs_6_.refs_2_, ...), custom_call_target="tpu_custom_call" | custom-call | flops 1 | bytes 1 | tf_op jit(solution)/shard_map/values/pallas_call | solution.py:339
  72.2 0.0 copy-start.7
  72.2 1.8 %attention.4.refs_0_ = bf16[64,4096]{1,0:T(8,128)(2,1)} custom-call(bf16[64,4096]{1,0:T(8,128)(2,1)S(1)} %bitcast.24, bf16[1024,256]{1,0:T(8,128)(2,1)S(1)} %get-tuple-element.44.k_ref, bf16[1024,256]{1,0:T(8,128)(2,1)S(1)} %get-tuple-element.45.v_ref), custom_call_target="tpu_custom_call" | custom-call | flops 1 | bytes 1 | tf_op jit(solution)/shard_map/attention/pallas_call | solution.py:425
  74.1 0.1 add_convert_fusion.1
  74.2 1.3 %collective-permute-start.30 = (bf16[64,2048]{1,0:T(8,128)(2,1)S(1)}, bf16[64,2048]{1,0:T(8,128)(2,1)S(1)}, u32[]{:S(2)}, u32[]{:S(2)}) collective-permute-start(bf16[64,2048]{1,0:T(8,128)(2,1)S(1)} %add_convert_fusion.1), channel_id=1, source_target_pairs={{0,4},{1,5},{2,6},{3,7},{4,12},{5,13},{6,14},{7,15},{12,8},{13,9},... | collective-permute-start | bytes 786440 | tf_op jit(solution)/shard_map/ppermute | solution.py:55
  75.5 0.6 collective-permute-start.29
  76.1 1.8 %attention.5.refs_0_ = bf16[64,4096]{1,0:T(8,128)(2,1)} custom-call(bf16[64,4096]{1,0:T(8,128)(2,1)S(1)} %bitcast.25, bf16[1024,256]{1,0:T(8,128)(2,1)S(1)} %get-tuple-element.44.k_ref, bf16[1024,256]{1,0:T(8,128)(2,1)S(1)} %get-tuple-element.45.v_ref, bf16[64,4096]{1,0:T(8,128)(2,1)} %attention.4.refs_0_), custom_call_target="tpu_custom_call", output_to_operand_aliasing={{}: (3, {})} | custom-call | flops 1 | bytes 1 | tf_op jit(solution)/shard_map/attention/pallas_call | solution.py:425
  77.9 1.8 %attention.6.refs_0_ = bf16[64,4096]{1,0:T(8,128)(2,1)} custom-call(bf16[64,4096]{1,0:T(8,128)(2,1)S(1)} %bitcast.26, bf16[1024,256]{1,0:T(8,128)(2,1)S(1)} %get-tuple-element.44.k_ref, bf16[1024,256]{1,0:T(8,128)(2,1)S(1)} %get-tuple-element.45.v_ref, bf16[64,4096]{1,0:T(8,128)(2,1)} %attention.5.refs_0_), custom_call_target="tpu_custom_call", output_to_operand_aliasing={{}: (3, {})} | custom-call | flops 1 | bytes 1 | tf_op jit(solution)/shard_map/attention/pallas_call | solution.py:425
  79.7 1.8 %attention.7 = bf16[64,4096]{1,0:T(8,128)(2,1)} custom-call(bf16[64,4096]{1,0:T(8,128)(2,1)S(1)} %bitcast.27, bf16[1024,256]{1,0:T(8,128)(2,1)S(1)} %get-tuple-element.44.k_ref, bf16[1024,256]{1,0:T(8,128)(2,1)S(1)} %get-tuple-element.45.v_ref, bf16[64,4096]{1,0:T(8,128)(2,1)} %attention.6.refs_0_), custom_call_target="tpu_custom_call", output_to_operand_aliasing={{}: (3, {})} | custom-call | flops 1 | bytes 1 | tf_op jit(solution)/shard_map/attention/pallas_call | solution.py:425
  81.6 0.5 collective-permute-done.30
  82.1 0.1 collective-permute-done.29
  82.2 0.9 %fusion = bf16[64,1,2048]{2,0,1:T(8,128)(2,1)} fusion(bf16[64,2048]{1,0:T(8,128)(2,1)S(1)} %collective-permute-done.30, bf16[64,2048]{1,0:T(8,128)(2,1)S(1)} %collective-permute-done.29, bf16[256,2048]{1,0:T(8,128)(2,1)S(1)} %collective-permute-done.14, bf16[128,2048]{1,0:T(8,128)(2,1)S(1)} %get-tuple-element.31, bf16[64,1,2048]{2,0,1:T(8,128)(2,1)S(1)} %copy-done.7), kind=kLoop, calls=%fused_computation.8 | loop fusion | flops 1310720 | bytes 1572864 | tf_op jit(solution)/shard_map/reshape | solution.py:579
  (35 shorter events, 0.1 us)
Async XLA Ops:
  2.5 4.6 %collective-permute-start.1 = (bf16[64,2176]{1,0:T(8,128)(2,1)}, bf16[64,2176]{1,0:T(8,128)(2,1)S(1)}, u32[]{:S(2)}, u32[]{:S(2)}) collective-permute-start(bf16[64,2176]{1,0:T(8,128)(2,1)} %get-tuple-element.26.refs_4_.refs_0_), channel_id=1, source_target_pairs={{0,1},{1,0},{2,3},{3,2},{4,5},{5,4},{6,7},{7,6},{12,13},{13,12},{1... | collective-permute-start | bytes 835592 | tf_op jit(solution)/shard_map/ppermute | solution.py:67
  2.9 12.5 %collective-permute-start = (bf16[64,2176]{1,0:T(8,128)(2,1)}, bf16[64,2176]{1,0:T(8,128)(2,1)S(1)}, u32[]{:S(2)}, u32[]{:S(2)}) collective-permute-start(bf16[64,2176]{1,0:T(8,128)(2,1)} %get-tuple-element.26.refs_4_.refs_0_), channel_id=1, source_target_pairs={{0,4},{1,5},{2,6},{3,7},{4,12},{5,13},{6,14},{7,15},{12,8},{13,9},... | collective-permute-start | bytes 835592 | tf_op jit(solution)/shard_map/ppermute | solution.py:55
  5.5 11.4 %collective-permute-start.3 = (bf16[64,2176]{1,0:T(8,128)(2,1)}, bf16[64,2176]{1,0:T(8,128)(2,1)S(1)}, u32[]{:S(2)}, u32[]{:S(2)}) collective-permute-start(bf16[64,2176]{1,0:T(8,128)(2,1)} %get-tuple-element.26.refs_4_.refs_0_), channel_id=1, source_target_pairs={{0,2},{1,3},{2,0},{3,1},{4,6},{5,7},{6,4},{7,5},{12,14},{13,15},{1... | collective-permute-start | bytes 835592 | tf_op jit(solution)/shard_map/ppermute | solution.py:63
  7.0 2.8 %copy-start = (bf16[1,2048,1536]{2,1,0:T(8,128)(2,1)S(1)}, bf16[1,2048,1536]{2,1,0:T(8,128)(2,1)}, u32[]{:S(2)}) copy-start(bf16[1,2048,1536]{2,1,0:T(8,128)(2,1)} %param.16) | copy-start | bytes 18874372
  9.8 1.9 %copy-start.2 = (bf16[1,768,2048]{2,1,0:T(8,128)(2,1)S(1)}, bf16[1,768,2048]{2,1,0:T(8,128)(2,1)}, u32[]{:S(2)}) copy-start(bf16[1,768,2048]{2,1,0:T(8,128)(2,1)} %param.17) | copy-start | bytes 9437188
  11.7 0.8 %copy-start.6 = (bf16[128,256]{1,0:T(8,128)(2,1)S(1)}, bf16[128,256]{1,0:T(8,128)(2,1)}, u32[]{:S(2)}) copy-start(bf16[128,256]{1,0:T(8,128)(2,1)} %get-tuple-element.28.small_ref) | copy-start | bytes 196612
  12.6 22.0 %copy-start.1 = (bf16[1,2048,1536]{2,1,0:T(8,128)(2,1)S(1)}, bf16[1,2048,1536]{2,1,0:T(8,128)(2,1)}, u32[]{:S(2)}) copy-start(bf16[1,2048,1536]{2,1,0:T(8,128)(2,1)} %param.16) | copy-start | bytes 18874372
  12.6 22.0 %copy-start.3 = (bf16[1,768,2048]{2,1,0:T(8,128)(2,1)S(1)}, bf16[1,768,2048]{2,1,0:T(8,128)(2,1)}, u32[]{:S(2)}) copy-start(bf16[1,768,2048]{2,1,0:T(8,128)(2,1)} %param.17) | copy-start | bytes 9437188
  12.6 22.0 %copy-start.5 = (bf16[64,2176]{1,0:T(8,128)(2,1)S(1)}, bf16[64,2176]{1,0:T(8,128)(2,1)}, u32[]{:S(2)}) copy-start(bf16[64,2176]{1,0:T(8,128)(2,1)} %get-tuple-element.26.refs_4_.refs_0_) | copy-start | bytes 835588
  12.6 4.3 %collective-permute-start.2 = (bf16[128,256]{1,0:T(8,128)(2,1)S(1)}, bf16[128,256]{1,0:T(8,128)(2,1)S(1)}, u32[]{:S(2)}, u32[]{:S(2)}) collective-permute-start(bf16[128,256]{1,0:T(8,128)(2,1)S(1)} %hold_weights.1), channel_id=1, source_target_pairs={{0,2},{1,3},{2,0},{3,1},{4,6},{5,7},{6,4},{7,5},{12,14},{13,15},{1... | collective-permute-start | bytes 196616 | tf_op jit(solution)/shard_map/ppermute | solution.py:63
  13.2 9.7 %collective-permute-start.5 = (bf16[64,2176]{1,0:T(8,128)(2,1)}, bf16[64,2176]{1,0:T(8,128)(2,1)S(1)}, u32[]{:S(2)}, u32[]{:S(2)}) collective-permute-start(bf16[64,2176]{1,0:T(8,128)(2,1)} %get-tuple-element.26.refs_4_.refs_0_), channel_id=1, source_target_pairs={{0,8},{1,9},{2,10},{3,11},{4,0},{5,1},{6,2},{7,3},{12,4},{13,5},{1... | collective-permute-start | bytes 835592 | tf_op jit(solution)/shard_map/ppermute | solution.py:59
  15.4 9.1 %collective-permute-start.7 = (bf16[64,2176]{1,0:T(8,128)(2,1)S(1)}, bf16[64,2176]{1,0:T(8,128)(2,1)S(1)}, u32[]{:S(2)}, u32[]{:S(2)}) collective-permute-start(bf16[64,2176]{1,0:T(8,128)(2,1)S(1)} %collective-permute-done.refs_0_.refs_4_), channel_id=1, source_target_pairs={{0,2},{1,3},{2,0},{3,1},{4,6},{5,7},{6,4},{7,5},{12,14},{13,15},{1... | collective-permute-start | bytes 835592 | tf_op jit(solution)/shard_map/ppermute | solution.py:63
  16.9 13.5 %collective-permute-start.4 = (bf16[64,2176]{1,0:T(8,128)(2,1)S(1)}, bf16[64,2176]{1,0:T(8,128)(2,1)S(1)}, u32[]{:S(2)}, u32[]{:S(2)}) collective-permute-start(bf16[64,2176]{1,0:T(8,128)(2,1)S(1)} %collective-permute-done.refs_0_.refs_4_), channel_id=1, source_target_pairs={{0,4},{1,5},{2,6},{3,7},{4,12},{5,13},{6,14},{7,15},{12,8},{13,9},... | collective-permute-start | bytes 835592 | tf_op jit(solution)/shard_map/ppermute | solution.py:55
  22.8 9.2 %collective-permute-start.6 = (bf16[64,2176]{1,0:T(8,128)(2,1)S(1)}, bf16[64,2176]{1,0:T(8,128)(2,1)S(1)}, u32[]{:S(2)}, u32[]{:S(2)}) collective-permute-start(bf16[64,2176]{1,0:T(8,128)(2,1)S(1)} %collective-permute-done.5.refs_4_.refs_12_), channel_id=1, source_target_pairs={{0,2},{1,3},{2,0},{3,1},{4,6},{5,7},{6,4},{7,5},{12,14},{13,15},{1... | collective-permute-start | bytes 835592 | tf_op jit(solution)/shard_map/ppermute | solution.py:63
  24.1 8.6 %collective-permute-start.10 = (bf16[64,2176]{1,0:T(8,128)(2,1)S(1)}, bf16[64,2176]{1,0:T(8,128)(2,1)S(1)}, u32[]{:S(2)}, u32[]{:S(2)}) collective-permute-start(bf16[64,2176]{1,0:T(8,128)(2,1)S(1)} %collective-permute-done.3.refs_5_.refs_1_), channel_id=1, source_target_pairs={{0,1},{1,0},{2,3},{3,2},{4,5},{5,4},{6,7},{7,6},{12,13},{13,12},{1... | collective-permute-start | bytes 835592 | tf_op jit(solution)/shard_map/ppermute | solution.py:67
  24.1 10.5 %collective-permute-start.8 = (bf16[64,2176]{1,0:T(8,128)(2,1)S(1)}, bf16[64,2176]{1,0:T(8,128)(2,1)S(1)}, u32[]{:S(2)}, u32[]{:S(2)}) collective-permute-start(bf16[64,2176]{1,0:T(8,128)(2,1)S(1)} %collective-permute-done.refs_0_.refs_4_), channel_id=1, source_target_pairs={{0,1},{1,0},{2,3},{3,2},{4,5},{5,4},{6,7},{7,6},{12,13},{13,12},{1... | collective-permute-start | bytes 835592 | tf_op jit(solution)/shard_map/ppermute | solution.py:67
  24.6 10.0 %collective-permute-start.9 = (bf16[64,2176]{1,0:T(8,128)(2,1)S(1)}, bf16[64,2176]{1,0:T(8,128)(2,1)S(1)}, u32[]{:S(2)}, u32[]{:S(2)}) collective-permute-start(bf16[64,2176]{1,0:T(8,128)(2,1)S(1)} %collective-permute-done.7.refs_1_.refs_5_), channel_id=1, source_target_pairs={{0,1},{1,0},{2,3},{3,2},{4,5},{5,4},{6,7},{7,6},{12,13},{13,12},{1... | collective-permute-start | bytes 835592 | tf_op jit(solution)/shard_map/ppermute | solution.py:67
  30.5 9.5 %collective-permute-start.11 = (bf16[64,2176]{1,0:T(8,128)(2,1)S(1)}, bf16[64,2176]{1,0:T(8,128)(2,1)S(1)}, u32[]{:S(2)}, u32[]{:S(2)}) collective-permute-start(bf16[64,2176]{1,0:T(8,128)(2,1)S(1)} %collective-permute-done.4.refs_0_.refs_8_), channel_id=1, source_target_pairs={{0,2},{1,3},{2,0},{3,1},{4,6},{5,7},{6,4},{7,5},{12,14},{13,15},{1... | collective-permute-start | bytes 835592 | tf_op jit(solution)/shard_map/ppermute | solution.py:63
  32.0 7.9 %collective-permute-start.13 = (bf16[256,256]{1,0:T(8,128)(2,1)S(1)}, bf16[256,256]{1,0:T(8,128)(2,1)S(1)}, u32[]{:S(2)}, u32[]{:S(2)}) collective-permute-start(bf16[256,256]{1,0:T(8,128)(2,1)S(1)} %pad_maximum_fusion), channel_id=1, source_target_pairs={{0,8},{1,9},{2,10},{3,11},{4,0},{5,1},{6,2},{7,3},{12,4},{13,5},{1... | collective-permute-start | bytes 393224 | tf_op jit(solution)/shard_map/ppermute | solution.py:59
  32.7 7.3 %collective-permute-start.12 = (bf16[256,256]{1,0:T(8,128)(2,1)S(1)}, bf16[256,256]{1,0:T(8,128)(2,1)S(1)}, u32[]{:S(2)}, u32[]{:S(2)}) collective-permute-start(bf16[256,256]{1,0:T(8,128)(2,1)S(1)} %pad_maximum_fusion), channel_id=1, source_target_pairs={{0,4},{1,5},{2,6},{3,7},{4,12},{5,13},{6,14},{7,15},{12,8},{13,9},... | collective-permute-start | bytes 393224 | tf_op jit(solution)/shard_map/ppermute | solution.py:55
  40.0 2.7 %collective-permute-start.14 = (bf16[256,2048]{1,0:T(8,128)(2,1)S(1)}, bf16[256,2048]{1,0:T(8,128)(2,1)S(1)}, u32[]{:S(2)}, u32[]{:S(2)}) collective-permute-start(bf16[256,2048]{1,0:T(8,128)(2,1)S(1)} %get-tuple-element.34), channel_id=1, source_target_pairs={{0,1},{1,0},{2,3},{3,2},{4,5},{5,4},{6,7},{7,6},{12,13},{13,12},{1... | collective-permute-start | bytes 3145736 | tf_op jit(solution)/shard_map/ppermute | solution.py:67
  40.0 3.5 %collective-permute-start.17 = (bf16[64,2176]{1,0:T(8,128)(2,1)S(1)}, bf16[64,2176]{1,0:T(8,128)(2,1)S(1)}, u32[]{:S(2)}, u32[]{:S(2)}) collective-permute-start(bf16[64,2176]{1,0:T(8,128)(2,1)S(1)} %collective-permute-done.5.refs_4_.refs_12_), channel_id=1, source_target_pairs={{0,1},{1,0},{2,3},{3,2},{4,5},{5,4},{6,7},{7,6},{12,13},{13,12},{1... | collective-permute-start | bytes 835592 | tf_op jit(solution)/shard_map/ppermute | solution.py:67
  40.5 5.6 %collective-permute-start.18 = (bf16[64,2176]{1,0:T(8,128)(2,1)S(1)}, bf16[64,2176]{1,0:T(8,128)(2,1)S(1)}, u32[]{:S(2)}, u32[]{:S(2)}) collective-permute-start(bf16[64,2176]{1,0:T(8,128)(2,1)S(1)} %collective-permute-done.6.refs_5_.refs_13_), channel_id=1, source_target_pairs={{0,1},{1,0},{2,3},{3,2},{4,5},{5,4},{6,7},{7,6},{12,13},{13,12},{1... | collective-permute-start | bytes 835592 | tf_op jit(solution)/shard_map/ppermute | solution.py:67
  40.5 5.6 %collective-permute-start.15 = (bf16[64,2176]{1,0:T(8,128)(2,1)S(1)}, bf16[64,2176]{1,0:T(8,128)(2,1)S(1)}, u32[]{:S(2)}, u32[]{:S(2)}) collective-permute-start(bf16[64,2176]{1,0:T(8,128)(2,1)S(1)} %collective-permute-done.4.refs_0_.refs_8_), channel_id=1, source_target_pairs={{0,1},{1,0},{2,3},{3,2},{4,5},{5,4},{6,7},{7,6},{12,13},{13,12},{1... | collective-permute-start | bytes 835592 | tf_op jit(solution)/shard_map/ppermute | solution.py:67
  41.0 5.1 %collective-permute-start.16 = (bf16[64,2176]{1,0:T(8,128)(2,1)S(1)}, bf16[64,2176]{1,0:T(8,128)(2,1)S(1)}, u32[]{:S(2)}, u32[]{:S(2)}) collective-permute-start(bf16[64,2176]{1,0:T(8,128)(2,1)S(1)} %collective-permute-done.11.refs_1_.refs_9_), channel_id=1, source_target_pairs={{0,1},{1,0},{2,3},{3,2},{4,5},{5,4},{6,7},{7,6},{12,13},{13,12},{1... | collective-permute-start | bytes 835592 | tf_op jit(solution)/shard_map/ppermute | solution.py:67
  42.8 8.4 %collective-permute-start.19 = (bf16[64,2048]{1,0:T(8,128)(2,1)S(1)}, bf16[64,2048]{1,0:T(8,128)(2,1)S(1)}, u32[]{:S(2)}, u32[]{:S(2)}) collective-permute-start(bf16[64,2048]{1,0:T(8,128)(2,1)S(1)} %get-tuple-element.53), channel_id=1, source_target_pairs={{0,2},{1,3},{2,0},{3,1},{4,6},{5,7},{6,4},{7,5},{12,14},{13,15},{1... | collective-permute-start | bytes 786440 | tf_op jit(solution)/shard_map/ppermute | solution.py:63
  43.4 7.2 %collective-permute-start.20 = (bf16[256,256]{1,0:T(8,128)(2,1)S(1)}, bf16[256,256]{1,0:T(8,128)(2,1)S(1)}, u32[]{:S(2)}, u32[]{:S(2)}) collective-permute-start(bf16[256,256]{1,0:T(8,128)(2,1)S(1)} %collective-permute-done.12), channel_id=1, source_target_pairs={{0,4},{1,5},{2,6},{3,7},{4,12},{5,13},{6,14},{7,15},{12,8},{13,9},... | collective-permute-start | bytes 393224 | tf_op jit(solution)/shard_map/ppermute | solution.py:55
  49.3 22.9 %copy-start.4 = (bf16[64,1,4096]{2,0,1:T(8,128)(2,1)S(1)}, bf16[64,1,4096]{2,0,1:T(8,128)(2,1)}, u32[]{:S(2)}) copy-start(bf16[64,1,4096]{2,0,1:T(8,128)(2,1)} %param.10) | copy-start | bytes 1572868
  51.2 3.4 %collective-permute-start.21 = (bf16[256,2048]{1,0:T(8,128)(2,1)S(1)}, bf16[256,2048]{1,0:T(8,128)(2,1)S(1)}, u32[]{:S(2)}, u32[]{:S(2)}) collective-permute-start(bf16[256,2048]{1,0:T(8,128)(2,1)S(1)} %get-tuple-element.39), channel_id=1, source_target_pairs={{0,1},{1,0},{2,3},{3,2},{4,5},{5,4},{6,7},{7,6},{12,13},{13,12},{1... | collective-permute-start | bytes 3145736 | tf_op jit(solution)/shard_map/ppermute | solution.py:67
  51.3 8.8 %collective-permute-start.26 = (bf16[512,256]{1,0:T(8,128)(2,1)S(1)}, bf16[512,256]{1,0:T(8,128)(2,1)S(1)}, u32[]{:S(2)}, u32[]{:S(2)}) collective-permute-start(bf16[512,256]{1,0:T(8,128)(2,1)S(1)} %bitcast.31), channel_id=1, source_target_pairs={{0,16},{16,0},{1,17},{17,1},{2,18},{18,2},{3,19},{19,3},{4,20},{20... | collective-permute-start | bytes 786440 | tf_op jit(solution)/shard_map/ppermute | solution.py:511
  52.9 9.4 %collective-permute-start.24 = (bf16[64,2048]{1,0:T(8,128)(2,1)S(1)}, bf16[64,2048]{1,0:T(8,128)(2,1)S(1)}, u32[]{:S(2)}, u32[]{:S(2)}) collective-permute-start(bf16[64,2048]{1,0:T(8,128)(2,1)S(1)} %add_convert_fusion.3), channel_id=1, source_target_pairs={{0,4},{1,5},{2,6},{3,7},{4,12},{5,13},{6,14},{7,15},{12,8},{13,9},... | collective-permute-start | bytes 786440 | tf_op jit(solution)/shard_map/ppermute | solution.py:55
  54.7 8.2 %collective-permute-start.23 = (bf16[64,2048]{1,0:T(8,128)(2,1)S(1)}, bf16[64,2048]{1,0:T(8,128)(2,1)S(1)}, u32[]{:S(2)}, u32[]{:S(2)}) collective-permute-start(bf16[64,2048]{1,0:T(8,128)(2,1)S(1)} %get-tuple-element.51), channel_id=1, source_target_pairs={{0,2},{1,3},{2,0},{3,1},{4,6},{5,7},{6,4},{7,5},{12,14},{13,15},{1... | collective-permute-start | bytes 786440 | tf_op jit(solution)/shard_map/ppermute | solution.py:63
  56.5 10.9 %collective-permute-start.27 = (bf16[1024,256]{1,0:T(8,128)(2,1)S(1)}, bf16[1024,256]{1,0:T(8,128)(2,1)S(1)}, u32[]{:S(2)}, u32[]{:S(2)}) collective-permute-start(bf16[1024,256]{1,0:T(8,128)(2,1)S(1)} %constant_dynamic-update-slice_fusion.refs_16_), channel_id=1, source_target_pairs={{0,1},{1,0},{2,3},{3,2},{4,5},{5,4},{6,7},{7,6},{12,13},{13,12},{1... | collective-permute-start | bytes 1572872 | tf_op jit(solution)/shard_map/ppermute | solution.py:67
  60.0 7.3 %collective-permute-start.28 = (bf16[512,256]{1,0:T(8,128)(2,1)S(1)}, bf16[512,256]{1,0:T(8,128)(2,1)S(1)}, u32[]{:S(2)}, u32[]{:S(2)}) collective-permute-start(bf16[512,256]{1,0:T(8,128)(2,1)S(1)} %collective-permute-done.26.refs_17_), channel_id=1, source_target_pairs={{0,1},{1,0},{2,3},{3,2},{4,5},{5,4},{6,7},{7,6},{12,13},{13,12},{1... | collective-permute-start | bytes 786440 | tf_op jit(solution)/shard_map/ppermute | solution.py:67
  63.0 11.1 %collective-permute-start.25 = (bf16[64,2048]{1,0:T(8,128)(2,1)S(1)}, bf16[64,2048]{1,0:T(8,128)(2,1)S(1)}, u32[]{:S(2)}, u32[]{:S(2)}) collective-permute-start(bf16[64,2048]{1,0:T(8,128)(2,1)S(1)} %add_convert_fusion.2), channel_id=1, source_target_pairs={{0,4},{1,5},{2,6},{3,7},{4,12},{5,13},{6,14},{7,15},{12,8},{13,9},... | collective-permute-start | bytes 786440 | tf_op jit(solution)/shard_map/ppermute | solution.py:55
  65.6 8.5 %collective-permute-start.22 = (bf16[64,2048]{1,0:T(8,128)(2,1)S(1)}, bf16[64,2048]{1,0:T(8,128)(2,1)S(1)}, u32[]{:S(2)}, u32[]{:S(2)}) collective-permute-start(bf16[64,2048]{1,0:T(8,128)(2,1)S(1)} %get-tuple-element.50), channel_id=1, source_target_pairs={{0,2},{1,3},{2,0},{3,1},{4,6},{5,7},{6,4},{7,5},{12,14},{13,15},{1... | collective-permute-start | bytes 786440 | tf_op jit(solution)/shard_map/ppermute | solution.py:63
  72.2 10.0 %copy-start.7 = (bf16[64,1,2048]{2,0,1:T(8,128)(2,1)S(1)}, bf16[64,1,2048]{2,0,1:T(8,128)(2,1)}, u32[]{:S(2)}) copy-start(bf16[64,1,2048]{2,0,1:T(8,128)(2,1)} %param.9) | copy-start | bytes 786436
  74.2 7.9 %collective-permute-start.30 = (bf16[64,2048]{1,0:T(8,128)(2,1)S(1)}, bf16[64,2048]{1,0:T(8,128)(2,1)S(1)}, u32[]{:S(2)}, u32[]{:S(2)}) collective-permute-start(bf16[64,2048]{1,0:T(8,128)(2,1)S(1)} %add_convert_fusion.1), channel_id=1, source_target_pairs={{0,4},{1,5},{2,6},{3,7},{4,12},{5,13},{6,14},{7,15},{12,8},{13,9},... | collective-permute-start | bytes 786440 | tf_op jit(solution)/shard_map/ppermute | solution.py:55
  75.5 6.7 %collective-permute-start.29 = (bf16[64,2048]{1,0:T(8,128)(2,1)S(1)}, bf16[64,2048]{1,0:T(8,128)(2,1)S(1)}, u32[]{:S(2)}, u32[]{:S(2)}) collective-permute-start(bf16[64,2048]{1,0:T(8,128)(2,1)S(1)} %get-tuple-element.48), channel_id=1, source_target_pairs={{0,2},{1,3},{2,0},{3,1},{4,6},{5,7},{6,4},{7,5},{12,14},{13,15},{1... | collective-permute-start | bytes 786440 | tf_op jit(solution)/shard_map/ppermute | solution.py:63

commit v14 on v13

--- a/solution.py
+++ b/solution.py
@@ -301,55 +301,45 @@
 
 def value_kernel(key_rows, blocks, *refs):
     count = len(blocks)
-    x_hbm, smalls = refs[:count], refs[count : count + 4]
-    key_ref, value_ref, x_buf, weight, sems = refs[count + 4 :]
-    width = x_buf.shape[1]
+    x_refs, smalls = refs[:count], refs[count : count + 6]
+    key_ref, value_ref, weight = refs[count + 6 :]
+    width = weight.shape[0]
     share = width // count // 2
     plane = lax.axis_index("grp")
-    copies = []
-    for number, (operand, at, device) in enumerate(blocks):
-        place = device()
-        own, other = smalls[number * 2 // count * 2 : number * 2 // count * 2 + 2]
-        below = at * (key_rows + share)
-        pairs = [
-            (x_hbm[operand].at[:, pl.ds(0, width)], x_buf.at[pl.ds(place * key_rows, key_rows)]),
-            (own.at[pl.ds(below, key_rows)], key_ref.at[pl.ds(place * key_rows, key_rows)]),
-            (
-                own.at[pl.ds(below + key_rows, share)],
-                weight.at[pl.ds((2 * place + plane) * share, share)],
-            ),
-            (
-                other.at[pl.ds(at * share, share)],
-                weight.at[pl.ds((2 * place + 1 - plane) * share, share)],
-            ),
-        ]
-        for kind, (source, target) in enumerate(pairs):
-            copies.append(pltpu.make_async_copy(source, target, sems.at[kind, number]))
-    for copy in copies:
-        copy.start()
-    for copy in copies:
-        copy.wait()
-    value_ref[...] = dot(x_buf[...], weight[...]).astype(BF16)
+    places = [device() for _, _, _, device in blocks]
+
+    def below(number, size):
+        return pl.ds(pl.multiple_of(number * size, size), size)
+
+    for (_, at, core, _), place in zip(blocks, places):
+        own, near, far = smalls[3 * core : 3 * core + 3]
+        other, there = (near, at) if at * share < near.shape[0] else (far, at - near.shape[0] // share)
+        first = at * (key_rows + share)
+        key_ref[below(place, key_rows)] = own[first : first + key_rows]
+        weight[below(2 * place + plane, share)] = own[first + key_rows : first + key_rows + share]
+        weight[below(2 * place + 1 - plane, share)] = other[there * share : (there + 1) * share]
+    for start in range(0, count, 4):
+        rows = [x_refs[operand][:, :width] for operand, _, _, _ in blocks[start : start + 4]]
+        values = dot(jnp.concatenate(rows, axis=0), weight[...]).astype(BF16)
+        for number in range(4):
+            value_ref[below(places[start + number], key_rows)] = values[
+                number * key_rows : (number + 1) * key_rows
+            ]
 
 
 def make_values(arrays, blocks, smalls, key_rows, width):
     kv_width = smalls[0].shape[1]
-    total = key_rows * len(blocks)
-    kv = jax.ShapeDtypeStruct((total, kv_width), BF16)
+    kv = jax.ShapeDtypeStruct((key_rows * len(blocks), kv_width), BF16)
     return pl.pallas_call(
         functools.partial(value_kernel, key_rows, blocks),
         out_shape=[kv, kv],
-        in_specs=[ANY] * (len(arrays) + len(smalls)),
+        in_specs=[IN_VMEM] * (len(arrays) + len(smalls)),
         out_specs=[IN_VMEM] * 2,
-        scratch_shapes=[
-            pltpu.VMEM((total, width), BF16),
-            pltpu.VMEM((width, kv_width), BF16),
-            pltpu.SemaphoreType.DMA((4, len(blocks))),
-        ],
+        scratch_shapes=[pltpu.VMEM((width, kv_width), BF16)],
         compiler_params=pltpu.CompilerParams(vmem_limit_bytes=VMEM_LIMIT),
         cost_estimate=SHORT,
         name="values",
-    )(*arrays, *smalls)
+    )(*in_vmem(*arrays, *smalls))
 
 
 def attention_kernel(chunk, q_ref, k_ref, v_ref, *refs):
@@ -466,12 +456,19 @@
         ]
         for step in range(LINE)
     ]
+    order = (0, 1, 3, 2)
     blocks = [
-        (4 * step + core * 2 + y, 2 * step + y, functools.partial(from_device, step, y, core))
+        (4 * step + core * 2 + y, 2 * at + y, core, functools.partial(from_device, step, y, core))
         for core in range(2)
-        for step in range(LINE)
+        for at, step in enumerate(order)
         for y in range(2)
     ]
+
+    def swap_planes(pieces):
+        both = jnp.concatenate(pieces, axis=0)
+        shares = both.reshape(-1, small.shape[0], both.shape[1])[:, rows:]
+        return lax.ppermute(shares.reshape(-1, both.shape[1]), "grp", [(0, 1), (1, 0)])
+
     pair = after(pair, line[3])
     pairs = [pair, forward(pair), None, backward(pair)]
     pairs[2] = forward(pairs[1])
@@ -502,24 +499,25 @@
     theirs = [None] * LINE
     experts(1, 0, [line[2], crossed[3]], [crossed[2], pairs[1], pairs[3]])
     theirs[1] = across(crossing[1])
-    send = experts(2, 3, [crossing[0], crossing[1]], [theirs[1], pairs[2]])
+    near = swap_planes([pairs[0], pairs[1], pairs[3]])
+    send = experts(2, 3, [crossing[0], crossing[1]], [theirs[1], pairs[2], near])
     total = summed(*mine[1], after(theirs[1], send))
     moving = forward(total)
     theirs[2], theirs[3] = across(crossing[2]), across(crossing[3])
-    own = jnp.concatenate(pairs, axis=0)
-    shares = own.reshape(2 * LINE, small.shape[0], -1)[:, rows:]
-    other = lax.ppermute(shares.reshape(-1, own.shape[1]), "grp", [(0, 1), (1, 0)])
-    total = summed(*mine[2], theirs[2], moving)
+    far = swap_planes([after(pairs[2], *crossing[2:], total)])
+    own = after(jnp.concatenate([pairs[step] for step in order], axis=0), crossing[3])
+    smalls = [own, near, far, other_core(own), other_core(after(near, crossing[3])), other_core(far)]
+    total = summed(*mine[2], theirs[2], after(moving, *smalls[3:]))
     moving = forward(total)
     theirs[0] = across(after(crossing[0], total))
-    smalls = [own, other, other_core(own), other_core(after(other, crossing[3]))]
     smalls[0] = after(own, total)
     new_keys, values = make_values(sum(arrays, []), blocks, smalls, rows, width)
     context = attend_part(queries, new_keys, values, 0, 4)
+    context = attend_part(queries, new_keys, values, 1, 4, context)
     total = summed(*mine[3], theirs[3], after(moving, context))
     moving = forward(total)
     queries = after(queries, total)
-    for part in range(1, 4):
+    for part in range(2, 4):
         context = attend_part(queries, new_keys, values, part, 4, context)
     layer_out = summed(acts, *mine[0], theirs[0], after(moving, context))
     return context, layer_out

time: 83.3 us -> 84.4 us (1.013)
  waiting for transfers between devices: 22.1 us -> 25.8 us
  Pallas kernels: 20.4 us -> 16.9 us
    pallas_call x1, Pallas kernels: 4.84 us -> 1.33 us  [make_values(): pl.pallas_call(functools.partial(value_kernel, key_rows, blocks), out_sha...]
    ppermute x12 -> x13, waiting for transfers between devices: 1.6 us -> 4.2 us  [other_core(): return lax.ppermute(x, 'seq', swaps(0, 1))]
    ppermute x9, starting transfers between devices: 10.2 us -> 8.66 us  [across(): return lax.ppermute(x, 'seq', swaps(1, 0))]
    ppermute x1 -> x2, starting transfers between devices: 1.56 us -> 3.11 us  [swap_planes(): lax.ppermute(shares.reshape(-1, both.shape[1]), 'grp', [(0, 1), (1, 0)])]
    ppermute x9, waiting for transfers between devices: 2.1 us -> 3.21 us  [across(): return lax.ppermute(x, 'seq', swaps(1, 0))]
    ppermute x1 -> x2, waiting for transfers between devices: 3.58 us -> 2.95 us  [swap_planes(): lax.ppermute(shares.reshape(-1, both.shape[1]), 'grp', [(0, 1), (1, 0)])]
    ppermute x12 -> x13, starting transfers between devices: 2.06 us -> 2.26 us  [other_core(): return lax.ppermute(x, 'seq', swaps(0, 1))]
    unnamed x19 -> x16, local copies, waits for them, and re-layouts: 5.57 us -> 5.54 us
  transfers between devices with their start and end apart: 31 -> 33, of which waited for: 12 -> 13; matrix products, arithmetic and copies ran while one was open for 1% -> 0% of each run, Pallas kernels for 22% -> 18%
where the time goes in v14:
time: 84.4 us; the launch traced here: 84.1 us
  starting transfers between devices  33.4 us (40%)
  waiting for transfers between devices  25.8 us (31%)
  Pallas kernels  16.9 us (20%)
  local copies, waits for them, and re-layouts  5.56 us (7%)
  other arithmetic  1.56 us (2%)
    ppermute x7, starting transfers between devices, forward(): return lax.ppermute(x, 'seq', ring_steps(1))  16.5 us
    ppermute x7, waiting for transfers between devices, forward(): return lax.ppermute(x, 'seq', ring_steps(1))  10.7 us
    ppermute x9, starting transfers between devices, across(): return lax.ppermute(x, 'seq', swaps(1, 0))  8.66 us
    pallas_call x4, Pallas kernels, attend_part(): pl.pallas_call(functools.partial(attention_kernel, chunk), grid=(1,), out...  7.34 us
    pallas_call x2, Pallas kernels, run_experts(): pl.pallas_call(functools.partial(expert_kernel, top, tok_rows, capacity,...  6.37 us
    unnamed x16, local copies, waits for them, and re-layouts  5.54 us
    ppermute x2, waiting for transfers between devices, backward(): return lax.ppermute(x, 'seq', ring_steps(LINE - 1))  4.77 us
    ppermute x13, waiting for transfers between devices, other_core(): return lax.ppermute(x, 'seq', swaps(0, 1))  4.2 us
  transfers between devices with their start and end apart: 33, of which 13 were waited for; matrix products, arithmetic and copies ran while one was open for 0% of the time, Pallas kernels for 18%

profile of v14, /device:TPU:0, one launch (start us, length us, event | category | flops | bytes accessed | tf_op | source)
XLA Modules:
  0.0 84.1 jit_solution(1770370289240323153)
XLA Ops:
  0.6 1.9 %normalize_and_pack.1 = (bf16[64,2176]{1,0:T(8,128)(2,1)}, bf16[128,256]{1,0:T(8,128)(2,1)}) custom-call(bf16[64,2048]{1,0:T(8,128)(2,1)} %bitcast.31, f32[1,2048]{1,0:T(1,128)} %bitcast.37, s32[4,64]{1,0:T(4,128)} %bitcast.38, f32[4,64]{1,0:T(4,128)} %bitcast.39, bf16[64,256]{1,0:T(8,128)(2,1)} %bitcast.36, bf16[128,256]{1,0:T(8,128)(2,1)} %weight_ref.1), custom_call_target="tpu_custom_call" | custom-call | flops 1 | bytes 1 | tf_op jit(solution)/shard_map/normalize_and_pack/pallas_call | solution.py:112
  2.5 0.5 collective-permute-start.1
  2.9 2.6 %collective-permute-start = (bf16[64,2176]{1,0:T(8,128)(2,1)}, bf16[64,2176]{1,0:T(8,128)(2,1)S(1)}, u32[]{:S(2)}, u32[]{:S(2)}) collective-permute-start(bf16[64,2176]{1,0:T(8,128)(2,1)} %get-tuple-element.29.refs_4_.refs_0_), channel_id=1, source_target_pairs={{0,4},{1,5},{2,6},{3,7},{4,12},{5,13},{6,14},{7,15},{12,8},{13,9},... | collective-permute-start | bytes 835592 | tf_op jit(solution)/shard_map/ppermute | solution.py:55
  5.5 1.5 %collective-permute-start.3 = (bf16[64,2176]{1,0:T(8,128)(2,1)}, bf16[64,2176]{1,0:T(8,128)(2,1)S(1)}, u32[]{:S(2)}, u32[]{:S(2)}) collective-permute-start(bf16[64,2176]{1,0:T(8,128)(2,1)} %get-tuple-element.29.refs_4_.refs_0_), channel_id=1, source_target_pairs={{0,2},{1,3},{2,0},{3,1},{4,6},{5,7},{6,4},{7,5},{12,14},{13,15},{1... | collective-permute-start | bytes 835592 | tf_op jit(solution)/shard_map/ppermute | solution.py:63
  7.0 0.0 collective-permute-done.1.refs_6_.refs_2_
  7.0 2.8 %copy-done = bf16[1,2048,1536]{2,1,0:T(8,128)(2,1)S(1)} copy-done((bf16[1,2048,1536]{2,1,0:T(8,128)(2,1)S(1)}, bf16[1,2048,1536]{2,1,0:T(8,128)(2,1)}, u32[]{:S(2)}) %copy-start) | copy-done | bytes 6291480
  9.8 1.9 %copy-done.2 = bf16[1,768,2048]{2,1,0:T(8,128)(2,1)S(1)} copy-done((bf16[1,768,2048]{2,1,0:T(8,128)(2,1)S(1)}, bf16[1,768,2048]{2,1,0:T(8,128)(2,1)}, u32[]{:S(2)}) %copy-start.2) | copy-done | bytes 3145752
  11.7 0.8 copy-done.6
  12.6 0.6 collective-permute-start.2
  13.2 2.3 %collective-permute-start.5 = (bf16[64,2176]{1,0:T(8,128)(2,1)}, bf16[64,2176]{1,0:T(8,128)(2,1)S(1)}, u32[]{:S(2)}, u32[]{:S(2)}) collective-permute-start(bf16[64,2176]{1,0:T(8,128)(2,1)} %get-tuple-element.29.refs_4_.refs_0_), channel_id=1, source_target_pairs={{0,8},{1,9},{2,10},{3,11},{4,0},{5,1},{6,2},{7,3},{12,4},{13,5},{1... | collective-permute-start | bytes 835592 | tf_op jit(solution)/shard_map/ppermute | solution.py:59
  15.4 0.0 collective-permute-done.refs_0_.refs_4_
  15.4 0.6 collective-permute-start.7
  16.0 0.9 %collective-permute-done.2 = bf16[128,256]{1,0:T(8,128)(2,1)S(1)} collective-permute-done((bf16[128,256]{1,0:T(8,128)(2,1)S(1)}, bf16[128,256]{1,0:T(8,128)(2,1)S(1)}, u32[]{:S(2)}, u32[]{:S(2)}) %collective-permute-start.2) | collective-permute-done | bytes 65568 | tf_op jit(solution)/shard_map/ppermute | solution.py:63
  16.9 0.0 collective-permute-done.3.refs_5_.refs_1_
  16.9 3.3 %collective-permute-start.4 = (bf16[64,2176]{1,0:T(8,128)(2,1)S(1)}, bf16[64,2176]{1,0:T(8,128)(2,1)S(1)}, u32[]{:S(2)}, u32[]{:S(2)}) collective-permute-start(bf16[64,2176]{1,0:T(8,128)(2,1)S(1)} %collective-permute-done.refs_0_.refs_4_), channel_id=1, source_target_pairs={{0,4},{1,5},{2,6},{3,7},{4,12},{5,13},{6,14},{7,15},{12,8},{13,9},... | collective-permute-start | bytes 835592 | tf_op jit(solution)/shard_map/ppermute | solution.py:55
  20.3 2.6 %collective-permute-done.5.refs_4_.refs_12_ = bf16[64,2176]{1,0:T(8,128)(2,1)S(1)} collective-permute-done((bf16[64,2176]{1,0:T(8,128)(2,1)}, bf16[64,2176]{1,0:T(8,128)(2,1)S(1)}, u32[]{:S(2)}, u32[]{:S(2)}) %collective-permute-start.5) | collective-permute-done | bytes 278560 | tf_op jit(solution)/shard_map/ppermute | solution.py:59
  22.8 1.2 %collective-permute-start.6 = (bf16[64,2176]{1,0:T(8,128)(2,1)S(1)}, bf16[64,2176]{1,0:T(8,128)(2,1)S(1)}, u32[]{:S(2)}, u32[]{:S(2)}) collective-permute-start(bf16[64,2176]{1,0:T(8,128)(2,1)S(1)} %collective-permute-done.5.refs_4_.refs_12_), channel_id=1, source_target_pairs={{0,2},{1,3},{2,0},{3,1},{4,6},{5,7},{6,4},{7,5},{12,14},{13,15},{1... | collective-permute-start | bytes 835592 | tf_op jit(solution)/shard_map/ppermute | solution.py:63
  24.1 0.5 collective-permute-start.8
  24.6 0.0 collective-permute-start.9
  24.6 5.9 %collective-permute-done.4.refs_0_.refs_8_ = bf16[64,2176]{1,0:T(8,128)(2,1)S(1)} collective-permute-done((bf16[64,2176]{1,0:T(8,128)(2,1)S(1)}, bf16[64,2176]{1,0:T(8,128)(2,1)S(1)}, u32[]{:S(2)}, u32[]{:S(2)}) %collective-permute-start.4) | collective-permute-done | bytes 278560 | tf_op jit(solution)/shard_map/ppermute | solution.py:55
  30.5 1.5 %collective-permute-start.11 = (bf16[64,2176]{1,0:T(8,128)(2,1)S(1)}, bf16[64,2176]{1,0:T(8,128)(2,1)S(1)}, u32[]{:S(2)}, u32[]{:S(2)}) collective-permute-start(bf16[64,2176]{1,0:T(8,128)(2,1)S(1)} %collective-permute-done.4.refs_0_.refs_8_), channel_id=1, source_target_pairs={{0,2},{1,3},{2,0},{3,1},{4,6},{5,7},{6,4},{7,5},{12,14},{13,15},{1... | collective-permute-start | bytes 835592 | tf_op jit(solution)/shard_map/ppermute | solution.py:63
  32.0 0.7 collective-permute-start.13
  32.7 1.9 %collective-permute-start.12 = (bf16[256,256]{1,0:T(8,128)(2,1)S(1)}, bf16[256,256]{1,0:T(8,128)(2,1)S(1)}, u32[]{:S(2)}, u32[]{:S(2)}) collective-permute-start(bf16[256,256]{1,0:T(8,128)(2,1)S(1)} %pad_maximum_fusion.2), channel_id=1, source_target_pairs={{0,4},{1,5},{2,6},{3,7},{4,12},{5,13},{6,14},{7,15},{12,8},{13,9},... | collective-permute-start | bytes 393224 | tf_op jit(solution)/shard_map/ppermute | solution.py:55
  34.6 3.2 %experts.2 = (bf16[128,2048]{1,0:T(8,128)(2,1)S(1)}, bf16[128,2048]{1,0:T(8,128)(2,1)S(1)}, bf16[256,2048]{1,0:T(8,128)(2,1)S(1)}) custom-call(bf16[64,2176]{1,0:T(8,128)(2,1)S(1)} %collective-permute-done.refs_0_.refs_4_, bf16[64,2176]{1,0:T(8,128)(2,1)S(1)} %collective-permute-done.7.refs_1_.refs_5_, ...), custom_call_target="tpu_custom_call" | custom-call | flops 1 | bytes 1 | tf_op jit(solution)/shard_map/experts/pallas_call | solution.py:290
  37.7 2.2 %collective-permute-done.13 = bf16[256,256]{1,0:T(8,128)(2,1)S(1)} collective-permute-done((bf16[256,256]{1,0:T(8,128)(2,1)S(1)}, bf16[256,256]{1,0:T(8,128)(2,1)S(1)}, u32[]{:S(2)}, u32[]{:S(2)}) %collective-permute-start.13) | collective-permute-done | bytes 131104 | tf_op jit(solution)/shard_map/ppermute | solution.py:59
  39.9 0.0 collective-permute-done.12
  40.0 0.5 collective-permute-start.17
  40.5 0.1 collective-permute-start.18
  40.5 0.4 collective-permute-start.15
  41.0 0.1 collective-permute-start.16
  41.1 1.6 %collective-permute-done.14 = bf16[256,2048]{1,0:T(8,128)(2,1)S(1)} collective-permute-done((bf16[256,2048]{1,0:T(8,128)(2,1)S(1)}, bf16[256,2048]{1,0:T(8,128)(2,1)S(1)}, u32[]{:S(2)}, u32[]{:S(2)}) %collective-permute-start.14) | collective-permute-done | bytes 1048608 | tf_op jit(solution)/shard_map/ppermute | solution.py:67
  42.6 0.1 add_convert_fusion.7
  42.8 0.7 collective-permute-start.19
  43.5 1.6 %collective-permute-start.21 = (bf16[384,256]{1,0:T(8,128)(2,1)S(1)}, bf16[384,256]{1,0:T(8,128)(2,1)S(1)}, u32[]{:S(2)}, u32[]{:S(2)}) collective-permute-start(bf16[384,256]{1,0:T(8,128)(2,1)S(1)} %bitcast.34), channel_id=1, source_target_pairs={{0,16},{16,0},{1,17},{17,1},{2,18},{18,2},{3,19},{19,3},{4,20},{20... | collective-permute-start | bytes 589832 | tf_op jit(solution)/shard_map/ppermute | solution.py:470
  45.1 2.7 %collective-permute-start.20 = (bf16[256,256]{1,0:T(8,128)(2,1)S(1)}, bf16[256,256]{1,0:T(8,128)(2,1)S(1)}, u32[]{:S(2)}, u32[]{:S(2)}) collective-permute-start(bf16[256,256]{1,0:T(8,128)(2,1)S(1)} %collective-permute-done.12), channel_id=1, source_target_pairs={{0,4},{1,5},{2,6},{3,7},{4,12},{5,13},{6,14},{7,15},{12,8},{13,9},... | collective-permute-start | bytes 393224 | tf_op jit(solution)/shard_map/ppermute | solution.py:55
  47.7 3.2 %experts.3 = (bf16[128,2048]{1,0:T(8,128)(2,1)S(1)}, bf16[128,2048]{1,0:T(8,128)(2,1)S(1)}, bf16[256,2048]{1,0:T(8,128)(2,1)S(1)}) custom-call(bf16[64,2176]{1,0:T(8,128)(2,1)S(1)} %collective-permute-done.4.refs_0_.refs_8_, bf16[64,2176]{1,0:T(8,128)(2,1)S(1)} %collective-permute-done.11.refs_1_.refs_9_, ...), custom_call_target="tpu_custom_call" | custom-call | flops 1 | bytes 1 | tf_op jit(solution)/shard_map/experts/pallas_call | solution.py:290
  50.9 0.0 copy-start.4
  50.9 1.1 %collective-permute-done.20 = bf16[256,256]{1,0:T(8,128)(2,1)S(1)} collective-permute-done((bf16[256,256]{1,0:T(8,128)(2,1)S(1)}, bf16[256,256]{1,0:T(8,128)(2,1)S(1)}, u32[]{:S(2)}, u32[]{:S(2)}) %collective-permute-start.20) | collective-permute-done | bytes 131104 | tf_op jit(solution)/shard_map/ppermute | solution.py:55
  52.1 2.6 %collective-permute-done.22 = bf16[256,2048]{1,0:T(8,128)(2,1)S(1)} collective-permute-done((bf16[256,2048]{1,0:T(8,128)(2,1)S(1)}, bf16[256,2048]{1,0:T(8,128)(2,1)S(1)}, u32[]{:S(2)}, u32[]{:S(2)}) %collective-permute-start.22) | collective-permute-done | bytes 1048608 | tf_op jit(solution)/shard_map/ppermute | solution.py:67
  54.7 0.1 add_convert_fusion.4
  54.8 0.2 collective-permute-start.26
  55.0 0.1 add_convert_fusion.3
  55.1 1.6 %collective-permute-start.25 = (bf16[64,2048]{1,0:T(8,128)(2,1)S(1)}, bf16[64,2048]{1,0:T(8,128)(2,1)S(1)}, u32[]{:S(2)}, u32[]{:S(2)}) collective-permute-start(bf16[64,2048]{1,0:T(8,128)(2,1)S(1)} %add_convert_fusion.3), channel_id=1, source_target_pairs={{0,4},{1,5},{2,6},{3,7},{4,12},{5,13},{6,14},{7,15},{12,8},{13,9},... | collective-permute-start | bytes 786440 | tf_op jit(solution)/shard_map/ppermute | solution.py:55
  56.7 0.9 %collective-permute-start.24 = (bf16[64,2048]{1,0:T(8,128)(2,1)S(1)}, bf16[64,2048]{1,0:T(8,128)(2,1)S(1)}, u32[]{:S(2)}, u32[]{:S(2)}) collective-permute-start(bf16[64,2048]{1,0:T(8,128)(2,1)S(1)} %get-tuple-element.56), channel_id=1, source_target_pairs={{0,2},{1,3},{2,0},{3,1},{4,6},{5,7},{6,4},{7,5},{12,14},{13,15},{1... | collective-permute-start | bytes 786440 | tf_op jit(solution)/shard_map/ppermute | solution.py:63
  57.6 1.6 %collective-permute-start.28 = (bf16[128,256]{1,0:T(8,128)(2,1)S(1)}, bf16[128,256]{1,0:T(8,128)(2,1)S(1)}, u32[]{:S(2)}, u32[]{:S(2)}) collective-permute-start(bf16[128,256]{1,0:T(8,128)(2,1)S(1)} %bitcast.35), channel_id=1, source_target_pairs={{0,16},{16,0},{1,17},{17,1},{2,18},{18,2},{3,19},{19,3},{4,20},{20... | collective-permute-start | bytes 196616 | tf_op jit(solution)/shard_map/ppermute | solution.py:470
  59.2 2.9 %collective-permute-done.28.refs_18_ = bf16[128,256]{1,0:T(8,128)(2,1)S(1)} collective-permute-done((bf16[128,256]{1,0:T(8,128)(2,1)S(1)}, bf16[128,256]{1,0:T(8,128)(2,1)S(1)}, u32[]{:S(2)}, u32[]{:S(2)}) %collective-permute-start.28) | collective-permute-done | bytes 65568 | tf_op jit(solution)/shard_map/ppermute | solution.py:470
  62.1 2.5 %collective-permute-done.25 = bf16[64,2048]{1,0:T(8,128)(2,1)S(1)} collective-permute-done((bf16[64,2048]{1,0:T(8,128)(2,1)S(1)}, bf16[64,2048]{1,0:T(8,128)(2,1)S(1)}, u32[]{:S(2)}, u32[]{:S(2)}) %collective-permute-start.25) | collective-permute-done | bytes 262176 | tf_op jit(solution)/shard_map/ppermute | solution.py:55
  64.6 0.4 collective-permute-done.24
  65.0 0.1 add_convert_fusion.2
  65.2 2.8 %collective-permute-start.30 = (bf16[64,2048]{1,0:T(8,128)(2,1)S(1)}, bf16[64,2048]{1,0:T(8,128)(2,1)S(1)}, u32[]{:S(2)}, u32[]{:S(2)}) collective-permute-start(bf16[64,2048]{1,0:T(8,128)(2,1)S(1)} %add_convert_fusion.2), channel_id=1, source_target_pairs={{0,4},{1,5},{2,6},{3,7},{4,12},{5,13},{6,14},{7,15},{12,8},{13,9},... | collective-permute-start | bytes 786440 | tf_op jit(solution)/shard_map/ppermute | solution.py:55
  68.0 0.8 collective-permute-start.23
  68.8 1.3 %values.1 = (bf16[1024,256]{1,0:T(8,128)(2,1)S(1)}, bf16[1024,256]{1,0:T(8,128)(2,1)S(1)}) custom-call(bf16[64,2176]{1,0:T(8,128)(2,1)S(1)} %copy-done.5, bf16[64,2176]{1,0:T(8,128)(2,1)S(1)} %collective-permute-done.3.refs_5_.refs_1_, bf16[64,2176]{1,0:T(8,128)(2,1)S(1)} %collective-permute-done.1.refs_6_.refs_2_, ...), custom_call_target="tpu_custom_call" | custom-call | flops 1 | bytes 1 | tf_op jit(solution)/shard_map/values/pallas_call | solution.py:333
  70.2 0.0 copy-start.7
  70.2 1.8 %attention.4.refs_0_ = bf16[64,4096]{1,0:T(8,128)(2,1)} custom-call(bf16[64,4096]{1,0:T(8,128)(2,1)S(1)} %bitcast.26, bf16[1024,256]{1,0:T(8,128)(2,1)S(1)} %get-tuple-element.50.k_ref, bf16[1024,256]{1,0:T(8,128)(2,1)S(1)} %get-tuple-element.51.v_ref), custom_call_target="tpu_custom_call" | custom-call | flops 1 | bytes 1 | tf_op jit(solution)/shard_map/attention/pallas_call | solution.py:415
  72.0 1.8 %attention.5.refs_0_ = bf16[64,4096]{1,0:T(8,128)(2,1)} custom-call(bf16[64,4096]{1,0:T(8,128)(2,1)S(1)} %bitcast.27, bf16[1024,256]{1,0:T(8,128)(2,1)S(1)} %get-tuple-element.50.k_ref, bf16[1024,256]{1,0:T(8,128)(2,1)S(1)} %get-tuple-element.51.v_ref, bf16[64,4096]{1,0:T(8,128)(2,1)} %attention.4.refs_0_), custom_call_target="tpu_custom_call", output_to_operand_aliasing={{}: (3, {})} | custom-call | flops 1 | bytes 1 | tf_op jit(solution)/shard_map/attention/pallas_call | solution.py:415
  73.9 1.3 %collective-permute-done.23 = bf16[64,2048]{1,0:T(8,128)(2,1)S(1)} collective-permute-done((bf16[64,2048]{1,0:T(8,128)(2,1)S(1)}, bf16[64,2048]{1,0:T(8,128)(2,1)S(1)}, u32[]{:S(2)}, u32[]{:S(2)}) %collective-permute-start.23) | collective-permute-done | bytes 262176 | tf_op jit(solution)/shard_map/ppermute | solution.py:63
  75.2 0.1 add_convert_fusion.1
  75.3 1.6 %collective-permute-start.32 = (bf16[64,2048]{1,0:T(8,128)(2,1)S(1)}, bf16[64,2048]{1,0:T(8,128)(2,1)S(1)}, u32[]{:S(2)}, u32[]{:S(2)}) collective-permute-start(bf16[64,2048]{1,0:T(8,128)(2,1)S(1)} %add_convert_fusion.1), channel_id=1, source_target_pairs={{0,4},{1,5},{2,6},{3,7},{4,12},{5,13},{6,14},{7,15},{12,8},{13,9},... | collective-permute-start | bytes 786440 | tf_op jit(solution)/shard_map/ppermute | solution.py:55
  76.9 0.8 collective-permute-start.31
  77.7 1.8 %attention.6.refs_0_ = bf16[64,4096]{1,0:T(8,128)(2,1)} custom-call(bf16[64,4096]{1,0:T(8,128)(2,1)S(1)} %bitcast.28, bf16[1024,256]{1,0:T(8,128)(2,1)S(1)} %get-tuple-element.50.k_ref, bf16[1024,256]{1,0:T(8,128)(2,1)S(1)} %get-tuple-element.51.v_ref, bf16[64,4096]{1,0:T(8,128)(2,1)} %attention.5.refs_0_), custom_call_target="tpu_custom_call", output_to_operand_aliasing={{}: (3, {})} | custom-call | flops 1 | bytes 1 | tf_op jit(solution)/shard_map/attention/pallas_call | solution.py:415
  79.5 1.8 %attention.7 = bf16[64,4096]{1,0:T(8,128)(2,1)} custom-call(bf16[64,4096]{1,0:T(8,128)(2,1)S(1)} %bitcast.29, bf16[1024,256]{1,0:T(8,128)(2,1)S(1)} %get-tuple-element.50.k_ref, bf16[1024,256]{1,0:T(8,128)(2,1)S(1)} %get-tuple-element.51.v_ref, bf16[64,4096]{1,0:T(8,128)(2,1)} %attention.6.refs_0_), custom_call_target="tpu_custom_call", output_to_operand_aliasing={{}: (3, {})} | custom-call | flops 1 | bytes 1 | tf_op jit(solution)/shard_map/attention/pallas_call | solution.py:415
  81.4 1.2 %collective-permute-done.32 = bf16[64,2048]{1,0:T(8,128)(2,1)S(1)} collective-permute-done((bf16[64,2048]{1,0:T(8,128)(2,1)S(1)}, bf16[64,2048]{1,0:T(8,128)(2,1)S(1)}, u32[]{:S(2)}, u32[]{:S(2)}) %collective-permute-start.32) | collective-permute-done | bytes 262176 | tf_op jit(solution)/shard_map/ppermute | solution.py:55
  82.6 0.6 collective-permute-done.31
  83.2 0.9 %fusion = bf16[64,1,2048]{2,0,1:T(8,128)(2,1)} fusion(bf16[64,2048]{1,0:T(8,128)(2,1)S(1)} %collective-permute-done.32, bf16[64,2048]{1,0:T(8,128)(2,1)S(1)} %collective-permute-done.31, bf16[256,2048]{1,0:T(8,128)(2,1)S(1)} %collective-permute-done.14, bf16[128,2048]{1,0:T(8,128)(2,1)S(1)} %get-tuple-element.34, bf16[64,1,2048]{2,0,1:T(8,128)(2,1)S(1)} %copy-done.7), kind=kLoop, calls=%fused_computation.10 | loop fusion | flops 1310720 | bytes 1572864 | tf_op jit(solution)/shard_map/reshape | solution.py:577
  (38 shorter events, 0.2 us)
Async XLA Ops:
  2.5 4.6 %collective-permute-start.1 = (bf16[64,2176]{1,0:T(8,128)(2,1)}, bf16[64,2176]{1,0:T(8,128)(2,1)S(1)}, u32[]{:S(2)}, u32[]{:S(2)}) collective-permute-start(bf16[64,2176]{1,0:T(8,128)(2,1)} %get-tuple-element.29.refs_4_.refs_0_), channel_id=1, source_target_pairs={{0,1},{1,0},{2,3},{3,2},{4,5},{5,4},{6,7},{7,6},{12,13},{13,12},{1... | collective-permute-start | bytes 835592 | tf_op jit(solution)/shard_map/ppermute | solution.py:67
  2.9 12.5 %collective-permute-start = (bf16[64,2176]{1,0:T(8,128)(2,1)}, bf16[64,2176]{1,0:T(8,128)(2,1)S(1)}, u32[]{:S(2)}, u32[]{:S(2)}) collective-permute-start(bf16[64,2176]{1,0:T(8,128)(2,1)} %get-tuple-element.29.refs_4_.refs_0_), channel_id=1, source_target_pairs={{0,4},{1,5},{2,6},{3,7},{4,12},{5,13},{6,14},{7,15},{12,8},{13,9},... | collective-permute-start | bytes 835592 | tf_op jit(solution)/shard_map/ppermute | solution.py:55
  5.5 11.4 %collective-permute-start.3 = (bf16[64,2176]{1,0:T(8,128)(2,1)}, bf16[64,2176]{1,0:T(8,128)(2,1)S(1)}, u32[]{:S(2)}, u32[]{:S(2)}) collective-permute-start(bf16[64,2176]{1,0:T(8,128)(2,1)} %get-tuple-element.29.refs_4_.refs_0_), channel_id=1, source_target_pairs={{0,2},{1,3},{2,0},{3,1},{4,6},{5,7},{6,4},{7,5},{12,14},{13,15},{1... | collective-permute-start | bytes 835592 | tf_op jit(solution)/shard_map/ppermute | solution.py:63
  7.0 2.8 %copy-start = (bf16[1,2048,1536]{2,1,0:T(8,128)(2,1)S(1)}, bf16[1,2048,1536]{2,1,0:T(8,128)(2,1)}, u32[]{:S(2)}) copy-start(bf16[1,2048,1536]{2,1,0:T(8,128)(2,1)} %param.16) | copy-start | bytes 18874372
  9.8 1.9 %copy-start.2 = (bf16[1,768,2048]{2,1,0:T(8,128)(2,1)S(1)}, bf16[1,768,2048]{2,1,0:T(8,128)(2,1)}, u32[]{:S(2)}) copy-start(bf16[1,768,2048]{2,1,0:T(8,128)(2,1)} %param.17) | copy-start | bytes 9437188
  11.7 0.8 copy-start.6
  12.6 22.0 %copy-start.1 = (bf16[1,2048,1536]{2,1,0:T(8,128)(2,1)S(1)}, bf16[1,2048,1536]{2,1,0:T(8,128)(2,1)}, u32[]{:S(2)}) copy-start(bf16[1,2048,1536]{2,1,0:T(8,128)(2,1)} %param.16) | copy-start | bytes 18874372
  12.6 22.0 %copy-start.3 = (bf16[1,768,2048]{2,1,0:T(8,128)(2,1)S(1)}, bf16[1,768,2048]{2,1,0:T(8,128)(2,1)}, u32[]{:S(2)}) copy-start(bf16[1,768,2048]{2,1,0:T(8,128)(2,1)} %param.17) | copy-start | bytes 9437188
  12.6 22.0 %copy-start.5 = (bf16[64,2176]{1,0:T(8,128)(2,1)S(1)}, bf16[64,2176]{1,0:T(8,128)(2,1)}, u32[]{:S(2)}) copy-start(bf16[64,2176]{1,0:T(8,128)(2,1)} %get-tuple-element.29.refs_4_.refs_0_) | copy-start | bytes 835588
  12.6 4.3 %collective-permute-start.2 = (bf16[128,256]{1,0:T(8,128)(2,1)S(1)}, bf16[128,256]{1,0:T(8,128)(2,1)S(1)}, u32[]{:S(2)}, u32[]{:S(2)}) collective-permute-start(bf16[128,256]{1,0:T(8,128)(2,1)S(1)} %hold_weights.1), channel_id=1, source_target_pairs={{0,2},{1,3},{2,0},{3,1},{4,6},{5,7},{6,4},{7,5},{12,14},{13,15},{1... | collective-permute-start | bytes 196616 | tf_op jit(solution)/shard_map/ppermute | solution.py:63
  13.2 9.7 %collective-permute-start.5 = (bf16[64,2176]{1,0:T(8,128)(2,1)}, bf16[64,2176]{1,0:T(8,128)(2,1)S(1)}, u32[]{:S(2)}, u32[]{:S(2)}) collective-permute-start(bf16[64,2176]{1,0:T(8,128)(2,1)} %get-tuple-element.29.refs_4_.refs_0_), channel_id=1, source_target_pairs={{0,8},{1,9},{2,10},{3,11},{4,0},{5,1},{6,2},{7,3},{12,4},{13,5},{1... | collective-permute-start | bytes 835592 | tf_op jit(solution)/shard_map/ppermute | solution.py:59
  15.4 9.1 %collective-permute-start.7 = (bf16[64,2176]{1,0:T(8,128)(2,1)S(1)}, bf16[64,2176]{1,0:T(8,128)(2,1)S(1)}, u32[]{:S(2)}, u32[]{:S(2)}) collective-permute-start(bf16[64,2176]{1,0:T(8,128)(2,1)S(1)} %collective-permute-done.refs_0_.refs_4_), channel_id=1, source_target_pairs={{0,2},{1,3},{2,0},{3,1},{4,6},{5,7},{6,4},{7,5},{12,14},{13,15},{1... | collective-permute-start | bytes 835592 | tf_op jit(solution)/shard_map/ppermute | solution.py:63
  16.9 13.5 %collective-permute-start.4 = (bf16[64,2176]{1,0:T(8,128)(2,1)S(1)}, bf16[64,2176]{1,0:T(8,128)(2,1)S(1)}, u32[]{:S(2)}, u32[]{:S(2)}) collective-permute-start(bf16[64,2176]{1,0:T(8,128)(2,1)S(1)} %collective-permute-done.refs_0_.refs_4_), channel_id=1, source_target_pairs={{0,4},{1,5},{2,6},{3,7},{4,12},{5,13},{6,14},{7,15},{12,8},{13,9},... | collective-permute-start | bytes 835592 | tf_op jit(solution)/shard_map/ppermute | solution.py:55
  22.8 9.2 %collective-permute-start.6 = (bf16[64,2176]{1,0:T(8,128)(2,1)S(1)}, bf16[64,2176]{1,0:T(8,128)(2,1)S(1)}, u32[]{:S(2)}, u32[]{:S(2)}) collective-permute-start(bf16[64,2176]{1,0:T(8,128)(2,1)S(1)} %collective-permute-done.5.refs_4_.refs_12_), channel_id=1, source_target_pairs={{0,2},{1,3},{2,0},{3,1},{4,6},{5,7},{6,4},{7,5},{12,14},{13,15},{1... | collective-permute-start | bytes 835592 | tf_op jit(solution)/shard_map/ppermute | solution.py:63
  24.1 8.6 %collective-permute-start.10 = (bf16[64,2176]{1,0:T(8,128)(2,1)S(1)}, bf16[64,2176]{1,0:T(8,128)(2,1)S(1)}, u32[]{:S(2)}, u32[]{:S(2)}) collective-permute-start(bf16[64,2176]{1,0:T(8,128)(2,1)S(1)} %collective-permute-done.3.refs_5_.refs_1_), channel_id=1, source_target_pairs={{0,1},{1,0},{2,3},{3,2},{4,5},{5,4},{6,7},{7,6},{12,13},{13,12},{1... | collective-permute-start | bytes 835592 | tf_op jit(solution)/shard_map/ppermute | solution.py:67
  24.1 10.5 %collective-permute-start.8 = (bf16[64,2176]{1,0:T(8,128)(2,1)S(1)}, bf16[64,2176]{1,0:T(8,128)(2,1)S(1)}, u32[]{:S(2)}, u32[]{:S(2)}) collective-permute-start(bf16[64,2176]{1,0:T(8,128)(2,1)S(1)} %collective-permute-done.refs_0_.refs_4_), channel_id=1, source_target_pairs={{0,1},{1,0},{2,3},{3,2},{4,5},{5,4},{6,7},{7,6},{12,13},{13,12},{1... | collective-permute-start | bytes 835592 | tf_op jit(solution)/shard_map/ppermute | solution.py:67
  24.6 10.0 %collective-permute-start.9 = (bf16[64,2176]{1,0:T(8,128)(2,1)S(1)}, bf16[64,2176]{1,0:T(8,128)(2,1)S(1)}, u32[]{:S(2)}, u32[]{:S(2)}) collective-permute-start(bf16[64,2176]{1,0:T(8,128)(2,1)S(1)} %collective-permute-done.7.refs_1_.refs_5_), channel_id=1, source_target_pairs={{0,1},{1,0},{2,3},{3,2},{4,5},{5,4},{6,7},{7,6},{12,13},{13,12},{1... | collective-permute-start | bytes 835592 | tf_op jit(solution)/shard_map/ppermute | solution.py:67
  30.5 9.5 %collective-permute-start.11 = (bf16[64,2176]{1,0:T(8,128)(2,1)S(1)}, bf16[64,2176]{1,0:T(8,128)(2,1)S(1)}, u32[]{:S(2)}, u32[]{:S(2)}) collective-permute-start(bf16[64,2176]{1,0:T(8,128)(2,1)S(1)} %collective-permute-done.4.refs_0_.refs_8_), channel_id=1, source_target_pairs={{0,2},{1,3},{2,0},{3,1},{4,6},{5,7},{6,4},{7,5},{12,14},{13,15},{1... | collective-permute-start | bytes 835592 | tf_op jit(solution)/shard_map/ppermute | solution.py:63
  32.0 7.9 %collective-permute-start.13 = (bf16[256,256]{1,0:T(8,128)(2,1)S(1)}, bf16[256,256]{1,0:T(8,128)(2,1)S(1)}, u32[]{:S(2)}, u32[]{:S(2)}) collective-permute-start(bf16[256,256]{1,0:T(8,128)(2,1)S(1)} %pad_maximum_fusion.2), channel_id=1, source_target_pairs={{0,8},{1,9},{2,10},{3,11},{4,0},{5,1},{6,2},{7,3},{12,4},{13,5},{1... | collective-permute-start | bytes 393224 | tf_op jit(solution)/shard_map/ppermute | solution.py:59
  32.7 7.3 %collective-permute-start.12 = (bf16[256,256]{1,0:T(8,128)(2,1)S(1)}, bf16[256,256]{1,0:T(8,128)(2,1)S(1)}, u32[]{:S(2)}, u32[]{:S(2)}) collective-permute-start(bf16[256,256]{1,0:T(8,128)(2,1)S(1)} %pad_maximum_fusion.2), channel_id=1, source_target_pairs={{0,4},{1,5},{2,6},{3,7},{4,12},{5,13},{6,14},{7,15},{12,8},{13,9},... | collective-permute-start | bytes 393224 | tf_op jit(solution)/shard_map/ppermute | solution.py:55
  40.0 2.7 %collective-permute-start.14 = (bf16[256,2048]{1,0:T(8,128)(2,1)S(1)}, bf16[256,2048]{1,0:T(8,128)(2,1)S(1)}, u32[]{:S(2)}, u32[]{:S(2)}) collective-permute-start(bf16[256,2048]{1,0:T(8,128)(2,1)S(1)} %get-tuple-element.37), channel_id=1, source_target_pairs={{0,1},{1,0},{2,3},{3,2},{4,5},{5,4},{6,7},{7,6},{12,13},{13,12},{1... | collective-permute-start | bytes 3145736 | tf_op jit(solution)/shard_map/ppermute | solution.py:67
  40.0 3.5 %collective-permute-start.17 = (bf16[64,2176]{1,0:T(8,128)(2,1)S(1)}, bf16[64,2176]{1,0:T(8,128)(2,1)S(1)}, u32[]{:S(2)}, u32[]{:S(2)}) collective-permute-start(bf16[64,2176]{1,0:T(8,128)(2,1)S(1)} %collective-permute-done.5.refs_4_.refs_12_), channel_id=1, source_target_pairs={{0,1},{1,0},{2,3},{3,2},{4,5},{5,4},{6,7},{7,6},{12,13},{13,12},{1... | collective-permute-start | bytes 835592 | tf_op jit(solution)/shard_map/ppermute | solution.py:67
  40.5 4.6 %collective-permute-start.18 = (bf16[64,2176]{1,0:T(8,128)(2,1)S(1)}, bf16[64,2176]{1,0:T(8,128)(2,1)S(1)}, u32[]{:S(2)}, u32[]{:S(2)}) collective-permute-start(bf16[64,2176]{1,0:T(8,128)(2,1)S(1)} %collective-permute-done.6.refs_5_.refs_13_), channel_id=1, source_target_pairs={{0,1},{1,0},{2,3},{3,2},{4,5},{5,4},{6,7},{7,6},{12,13},{13,12},{1... | collective-permute-start | bytes 835592 | tf_op jit(solution)/shard_map/ppermute | solution.py:67
  40.5 7.2 %collective-permute-start.15 = (bf16[64,2176]{1,0:T(8,128)(2,1)S(1)}, bf16[64,2176]{1,0:T(8,128)(2,1)S(1)}, u32[]{:S(2)}, u32[]{:S(2)}) collective-permute-start(bf16[64,2176]{1,0:T(8,128)(2,1)S(1)} %collective-permute-done.4.refs_0_.refs_8_), channel_id=1, source_target_pairs={{0,1},{1,0},{2,3},{3,2},{4,5},{5,4},{6,7},{7,6},{12,13},{13,12},{1... | collective-permute-start | bytes 835592 | tf_op jit(solution)/shard_map/ppermute | solution.py:67
  41.0 6.7 %collective-permute-start.16 = (bf16[64,2176]{1,0:T(8,128)(2,1)S(1)}, bf16[64,2176]{1,0:T(8,128)(2,1)S(1)}, u32[]{:S(2)}, u32[]{:S(2)}) collective-permute-start(bf16[64,2176]{1,0:T(8,128)(2,1)S(1)} %collective-permute-done.11.refs_1_.refs_9_), channel_id=1, source_target_pairs={{0,1},{1,0},{2,3},{3,2},{4,5},{5,4},{6,7},{7,6},{12,13},{13,12},{1... | collective-permute-start | bytes 835592 | tf_op jit(solution)/shard_map/ppermute | solution.py:67
  42.8 9.2 %collective-permute-start.19 = (bf16[64,2048]{1,0:T(8,128)(2,1)S(1)}, bf16[64,2048]{1,0:T(8,128)(2,1)S(1)}, u32[]{:S(2)}, u32[]{:S(2)}) collective-permute-start(bf16[64,2048]{1,0:T(8,128)(2,1)S(1)} %get-tuple-element.59), channel_id=1, source_target_pairs={{0,2},{1,3},{2,0},{3,1},{4,6},{5,7},{6,4},{7,5},{12,14},{13,15},{1... | collective-permute-start | bytes 786440 | tf_op jit(solution)/shard_map/ppermute | solution.py:63
  43.5 8.5 %collective-permute-start.21 = (bf16[384,256]{1,0:T(8,128)(2,1)S(1)}, bf16[384,256]{1,0:T(8,128)(2,1)S(1)}, u32[]{:S(2)}, u32[]{:S(2)}) collective-permute-start(bf16[384,256]{1,0:T(8,128)(2,1)S(1)} %bitcast.34), channel_id=1, source_target_pairs={{0,16},{16,0},{1,17},{17,1},{2,18},{18,2},{3,19},{19,3},{4,20},{20... | collective-permute-start | bytes 589832 | tf_op jit(solution)/shard_map/ppermute | solution.py:470
  45.1 6.9 %collective-permute-start.20 = (bf16[256,256]{1,0:T(8,128)(2,1)S(1)}, bf16[256,256]{1,0:T(8,128)(2,1)S(1)}, u32[]{:S(2)}, u32[]{:S(2)}) collective-permute-start(bf16[256,256]{1,0:T(8,128)(2,1)S(1)} %collective-permute-done.12), channel_id=1, source_target_pairs={{0,4},{1,5},{2,6},{3,7},{4,12},{5,13},{6,14},{7,15},{12,8},{13,9},... | collective-permute-start | bytes 393224 | tf_op jit(solution)/shard_map/ppermute | solution.py:55
  50.9 19.3 %copy-start.4 = (bf16[64,1,4096]{2,0,1:T(8,128)(2,1)S(1)}, bf16[64,1,4096]{2,0,1:T(8,128)(2,1)}, u32[]{:S(2)}) copy-start(bf16[64,1,4096]{2,0,1:T(8,128)(2,1)} %param.10) | copy-start | bytes 1572868
  52.0 2.7 %collective-permute-start.22 = (bf16[256,2048]{1,0:T(8,128)(2,1)S(1)}, bf16[256,2048]{1,0:T(8,128)(2,1)S(1)}, u32[]{:S(2)}, u32[]{:S(2)}) collective-permute-start(bf16[256,2048]{1,0:T(8,128)(2,1)S(1)} %get-tuple-element.42), channel_id=1, source_target_pairs={{0,1},{1,0},{2,3},{3,2},{4,5},{5,4},{6,7},{7,6},{12,13},{13,12},{1... | collective-permute-start | bytes 3145736 | tf_op jit(solution)/shard_map/ppermute | solution.py:67
  54.8 9.8 %collective-permute-start.26 = (bf16[1024,256]{1,0:T(8,128)(2,1)S(1)}, bf16[1024,256]{1,0:T(8,128)(2,1)S(1)}, u32[]{:S(2)}, u32[]{:S(2)}) collective-permute-start(bf16[1024,256]{1,0:T(8,128)(2,1)S(1)} %pad_maximum_fusion.refs_16_), channel_id=1, source_target_pairs={{0,1},{1,0},{2,3},{3,2},{4,5},{5,4},{6,7},{7,6},{12,13},{13,12},{1... | collective-permute-start | bytes 1572872 | tf_op jit(solution)/shard_map/ppermute | solution.py:67
  55.1 9.5 %collective-permute-start.25 = (bf16[64,2048]{1,0:T(8,128)(2,1)S(1)}, bf16[64,2048]{1,0:T(8,128)(2,1)S(1)}, u32[]{:S(2)}, u32[]{:S(2)}) collective-permute-start(bf16[64,2048]{1,0:T(8,128)(2,1)S(1)} %add_convert_fusion.3), channel_id=1, source_target_pairs={{0,4},{1,5},{2,6},{3,7},{4,12},{5,13},{6,14},{7,15},{12,8},{13,9},... | collective-permute-start | bytes 786440 | tf_op jit(solution)/shard_map/ppermute | solution.py:55
  56.7 8.3 %collective-permute-start.24 = (bf16[64,2048]{1,0:T(8,128)(2,1)S(1)}, bf16[64,2048]{1,0:T(8,128)(2,1)S(1)}, u32[]{:S(2)}, u32[]{:S(2)}) collective-permute-start(bf16[64,2048]{1,0:T(8,128)(2,1)S(1)} %get-tuple-element.56), channel_id=1, source_target_pairs={{0,2},{1,3},{2,0},{3,1},{4,6},{5,7},{6,4},{7,5},{12,14},{13,15},{1... | collective-permute-start | bytes 786440 | tf_op jit(solution)/shard_map/ppermute | solution.py:63
  57.6 7.0 %collective-permute-start.27 = (bf16[384,256]{1,0:T(8,128)(2,1)S(1)}, bf16[384,256]{1,0:T(8,128)(2,1)S(1)}, u32[]{:S(2)}, u32[]{:S(2)}) collective-permute-start(bf16[384,256]{1,0:T(8,128)(2,1)S(1)} %collective-permute-done.21.refs_17_), channel_id=1, source_target_pairs={{0,1},{1,0},{2,3},{3,2},{4,5},{5,4},{6,7},{7,6},{12,13},{13,12},{1... | collective-permute-start | bytes 589832 | tf_op jit(solution)/shard_map/ppermute | solution.py:67
  57.6 4.5 %collective-permute-start.28 = (bf16[128,256]{1,0:T(8,128)(2,1)S(1)}, bf16[128,256]{1,0:T(8,128)(2,1)S(1)}, u32[]{:S(2)}, u32[]{:S(2)}) collective-permute-start(bf16[128,256]{1,0:T(8,128)(2,1)S(1)} %bitcast.35), channel_id=1, source_target_pairs={{0,16},{16,0},{1,17},{17,1},{2,18},{18,2},{3,19},{19,3},{4,20},{20... | collective-permute-start | bytes 196616 | tf_op jit(solution)/shard_map/ppermute | solution.py:470
  62.1 2.5 %collective-permute-start.29 = (bf16[128,256]{1,0:T(8,128)(2,1)S(1)}, bf16[128,256]{1,0:T(8,128)(2,1)S(1)}, u32[]{:S(2)}, u32[]{:S(2)}) collective-permute-start(bf16[128,256]{1,0:T(8,128)(2,1)S(1)} %collective-permute-done.28.refs_18_), channel_id=1, source_target_pairs={{0,1},{1,0},{2,3},{3,2},{4,5},{5,4},{6,7},{7,6},{12,13},{13,12},{1... | collective-permute-start | bytes 196616 | tf_op jit(solution)/shard_map/ppermute | solution.py:67
  65.2 8.7 %collective-permute-start.30 = (bf16[64,2048]{1,0:T(8,128)(2,1)S(1)}, bf16[64,2048]{1,0:T(8,128)(2,1)S(1)}, u32[]{:S(2)}, u32[]{:S(2)}) collective-permute-start(bf16[64,2048]{1,0:T(8,128)(2,1)S(1)} %add_convert_fusion.2), channel_id=1, source_target_pairs={{0,4},{1,5},{2,6},{3,7},{4,12},{5,13},{6,14},{7,15},{12,8},{13,9},... | collective-permute-start | bytes 786440 | tf_op jit(solution)/shard_map/ppermute | solution.py:55
  68.0 7.2 %collective-permute-start.23 = (bf16[64,2048]{1,0:T(8,128)(2,1)S(1)}, bf16[64,2048]{1,0:T(8,128)(2,1)S(1)}, u32[]{:S(2)}, u32[]{:S(2)}) collective-permute-start(bf16[64,2048]{1,0:T(8,128)(2,1)S(1)} %get-tuple-element.57), channel_id=1, source_target_pairs={{0,2},{1,3},{2,0},{3,1},{4,6},{5,7},{6,4},{7,5},{12,14},{13,15},{1... | collective-permute-start | bytes 786440 | tf_op jit(solution)/shard_map/ppermute | solution.py:63
  70.2 13.1 %copy-start.7 = (bf16[64,1,2048]{2,0,1:T(8,128)(2,1)S(1)}, bf16[64,1,2048]{2,0,1:T(8,128)(2,1)}, u32[]{:S(2)}) copy-start(bf16[64,1,2048]{2,0,1:T(8,128)(2,1)} %param.9) | copy-start | bytes 786436
  75.3 7.3 %collective-permute-start.32 = (bf16[64,2048]{1,0:T(8,128)(2,1)S(1)}, bf16[64,2048]{1,0:T(8,128)(2,1)S(1)}, u32[]{:S(2)}, u32[]{:S(2)}) collective-permute-start(bf16[64,2048]{1,0:T(8,128)(2,1)S(1)} %add_convert_fusion.1), channel_id=1, source_target_pairs={{0,4},{1,5},{2,6},{3,7},{4,12},{5,13},{6,14},{7,15},{12,8},{13,9},... | collective-permute-start | bytes 786440 | tf_op jit(solution)/shard_map/ppermute | solution.py:55
  76.9 6.4 %collective-permute-start.31 = (bf16[64,2048]{1,0:T(8,128)(2,1)S(1)}, bf16[64,2048]{1,0:T(8,128)(2,1)S(1)}, u32[]{:S(2)}, u32[]{:S(2)}) collective-permute-start(bf16[64,2048]{1,0:T(8,128)(2,1)S(1)} %get-tuple-element.54), channel_id=1, source_target_pairs={{0,2},{1,3},{2,0},{3,1},{4,6},{5,7},{6,4},{7,5},{12,14},{13,15},{1... | collective-permute-start | bytes 786440 | tf_op jit(solution)/shard_map/ppermute | solution.py:63

commit v15 on v14

--- a/solution.py
+++ b/solution.py
@@ -474,16 +474,19 @@
     pairs[2] = forward(pairs[1])
     keep, mine, crossing = [None] * LINE, [None] * LINE, [None] * LINE
 
-    def experts(first, second, before, beside):
+    def experts(first, second, before, beside, split):
         ready = arrays[first] + arrays[second]
         ready = [after(ready[0], *before), *ready[1:]]
         sources = [[(4 * group + i, 0, rows) for i in range(4)] for group in range(2)]
-        targets = [[(group, 0, 2 * rows), (2, group * 2 * rows, 2 * rows)] for group in range(2)]
-        keep[first], keep[second], send = run_experts(
+        targets = [
+            [(group, 0, 2 * rows), (3, 0, 2 * rows) if group * split else (2, group * 2 * rows, 2 * rows)]
+            for group in range(2)
+        ]
+        keep[first], keep[second], send, *last = run_experts(
             ready,
             sources,
             targets,
-            [2 * rows, 2 * rows, 4 * rows],
+            [2 * rows] * 4 if split else [2 * rows, 2 * rows, 4 * rows],
             w_gate_up,
             w_down,
             top,
@@ -491,22 +494,27 @@
             capacity,
         )
         came = other_core(after(send, *beside))
-        for at, step in ((0, first), (2 * rows, second)):
-            mine[step] = (keep[step][:rows], came[at : at + rows])
-            crossing[step] = summed(keep[step][rows:], came[at + rows : at + 2 * rows])
+        mine[first] = (keep[first][:rows], came[:rows])
+        crossing[first] = summed(keep[first][rows:], came[rows : 2 * rows])
+        if split:
+            came = other_core(after(last[0], crossing[first]))
+        else:
+            came = came[2 * rows :]
+        mine[second] = (keep[second][:rows], came[:rows])
+        crossing[second] = summed(keep[second][rows:], came[rows:])
         return send
 
     theirs = [None] * LINE
-    experts(1, 0, [line[2], crossed[3]], [crossed[2], pairs[1], pairs[3]])
+    experts(1, 0, [line[2], crossed[3]], [crossed[2], pairs[1], pairs[3]], False)
     theirs[1] = across(crossing[1])
     near = swap_planes([pairs[0], pairs[1], pairs[3]])
-    send = experts(2, 3, [crossing[0], crossing[1]], [theirs[1], pairs[2], near])
+    send = experts(2, 3, [crossing[0], crossing[1]], [theirs[1], pairs[2], near], True)
     total = summed(*mine[1], after(theirs[1], send))
     moving = forward(total)
     theirs[2], theirs[3] = across(crossing[2]), across(crossing[3])
-    far = swap_planes([after(pairs[2], *crossing[2:], total)])
-    own = after(jnp.concatenate([pairs[step] for step in order], axis=0), crossing[3])
-    smalls = [own, near, far, other_core(own), other_core(after(near, crossing[3])), other_core(far)]
+    far = swap_planes([after(pairs[2], total)])
+    own = after(jnp.concatenate([pairs[step] for step in order], axis=0), total)
+    smalls = [own, near, far, other_core(own), other_core(after(near, total)), other_core(far)]
     total = summed(*mine[2], theirs[2], after(moving, *smalls[3:]))
     moving = forward(total)
     theirs[0] = across(after(crossing[0], total))

time: 84.4 us -> 82 us (0.972)
  waiting for transfers between devices: 25.8 us -> 23.6 us
    ppermute x13 -> x14, waiting for transfers between devices: 4.2 us -> 2.85 us  [other_core(): return lax.ppermute(x, 'seq', swaps(0, 1))]
    ppermute x7, waiting for transfers between devices: 10.7 us -> 9.6 us  [forward(): return lax.ppermute(x, 'seq', ring_steps(1))]
    ppermute x13 -> x14, starting transfers between devices: 2.26 us -> 2.43 us  [other_core(): return lax.ppermute(x, 'seq', swaps(0, 1))]
  transfers between devices with their start and end apart: 33 -> 34, of which waited for: 13 -> 13; matrix products, arithmetic and copies ran while one was open for 0% -> 1% of each run, Pallas kernels for 18% -> 18%
where the time goes in v15:
time: 82 us; the launch traced here: 81.7 us
  starting transfers between devices  33.3 us (41%)
  waiting for transfers between devices  23.6 us (29%)
  Pallas kernels  16.9 us (21%)
  local copies, waits for them, and re-layouts  5.56 us (7%)
  other arithmetic  1.57 us (2%)
    ppermute x7, starting transfers between devices, forward(): return lax.ppermute(x, 'seq', ring_steps(1))  16.1 us
    ppermute x7, waiting for transfers between devices, forward(): return lax.ppermute(x, 'seq', ring_steps(1))  9.6 us
    ppermute x9, starting transfers between devices, across(): return lax.ppermute(x, 'seq', swaps(1, 0))  8.78 us
    pallas_call x4, Pallas kernels, attend_part(): pl.pallas_call(functools.partial(attention_kernel, chunk), grid=(1,), out...  7.34 us
    pallas_call x2, Pallas kernels, run_experts(): pl.pallas_call(functools.partial(expert_kernel, top, tok_rows, capacity,...  6.37 us
    unnamed x16, local copies, waits for them, and re-layouts  5.54 us
    ppermute x2, waiting for transfers between devices, backward(): return lax.ppermute(x, 'seq', ring_steps(LINE - 1))  4.77 us
    ppermute x9, waiting for transfers between devices, across(): return lax.ppermute(x, 'seq', swaps(1, 0))  3.39 us
  transfers between devices with their start and end apart: 34, of which 13 were waited for; matrix products, arithmetic and copies ran while one was open for 1% of the time, Pallas kernels for 18%

profile of v15, /device:TPU:0, one launch (start us, length us, event | category | flops | bytes accessed | tf_op | source)
XLA Modules:
  0.0 81.7 jit_solution(2427615082797984684)
XLA Ops:
  0.6 1.9 %normalize_and_pack.1 = (bf16[64,2176]{1,0:T(8,128)(2,1)}, bf16[128,256]{1,0:T(8,128)(2,1)}) custom-call(bf16[64,2048]{1,0:T(8,128)(2,1)} %bitcast.31, f32[1,2048]{1,0:T(1,128)} %bitcast.37, s32[4,64]{1,0:T(4,128)} %bitcast.38, f32[4,64]{1,0:T(4,128)} %bitcast.39, bf16[64,256]{1,0:T(8,128)(2,1)} %bitcast.36, bf16[128,256]{1,0:T(8,128)(2,1)} %weight_ref.1), custom_call_target="tpu_custom_call" | custom-call | flops 1 | bytes 1 | tf_op jit(solution)/shard_map/normalize_and_pack/pallas_call | solution.py:112
  2.5 0.5 collective-permute-start.1
  2.9 2.6 %collective-permute-start = (bf16[64,2176]{1,0:T(8,128)(2,1)}, bf16[64,2176]{1,0:T(8,128)(2,1)S(1)}, u32[]{:S(2)}, u32[]{:S(2)}) collective-permute-start(bf16[64,2176]{1,0:T(8,128)(2,1)} %get-tuple-element.31.refs_4_.refs_0_), channel_id=1, source_target_pairs={{0,4},{1,5},{2,6},{3,7},{4,12},{5,13},{6,14},{7,15},{12,8},{13,9},... | collective-permute-start | bytes 835592 | tf_op jit(solution)/shard_map/ppermute | solution.py:55
  5.5 1.5 %collective-permute-start.3 = (bf16[64,2176]{1,0:T(8,128)(2,1)}, bf16[64,2176]{1,0:T(8,128)(2,1)S(1)}, u32[]{:S(2)}, u32[]{:S(2)}) collective-permute-start(bf16[64,2176]{1,0:T(8,128)(2,1)} %get-tuple-element.31.refs_4_.refs_0_), channel_id=1, source_target_pairs={{0,2},{1,3},{2,0},{3,1},{4,6},{5,7},{6,4},{7,5},{12,14},{13,15},{1... | collective-permute-start | bytes 835592 | tf_op jit(solution)/shard_map/ppermute | solution.py:63
  7.0 2.8 %copy-done = bf16[1,2048,1536]{2,1,0:T(8,128)(2,1)S(1)} copy-done((bf16[1,2048,1536]{2,1,0:T(8,128)(2,1)S(1)}, bf16[1,2048,1536]{2,1,0:T(8,128)(2,1)}, u32[]{:S(2)}) %copy-start) | copy-done | bytes 6291480
  9.8 1.9 %copy-done.2 = bf16[1,768,2048]{2,1,0:T(8,128)(2,1)S(1)} copy-done((bf16[1,768,2048]{2,1,0:T(8,128)(2,1)S(1)}, bf16[1,768,2048]{2,1,0:T(8,128)(2,1)}, u32[]{:S(2)}) %copy-start.2) | copy-done | bytes 3145752
  11.7 0.8 %copy-done.6 = bf16[128,256]{1,0:T(8,128)(2,1)S(1)} copy-done((bf16[128,256]{1,0:T(8,128)(2,1)S(1)}, bf16[128,256]{1,0:T(8,128)(2,1)}, u32[]{:S(2)}) %copy-start.6) | copy-done | bytes 65560
  12.6 0.6 collective-permute-start.2
  13.2 2.3 %collective-permute-start.5 = (bf16[64,2176]{1,0:T(8,128)(2,1)}, bf16[64,2176]{1,0:T(8,128)(2,1)S(1)}, u32[]{:S(2)}, u32[]{:S(2)}) collective-permute-start(bf16[64,2176]{1,0:T(8,128)(2,1)} %get-tuple-element.31.refs_4_.refs_0_), channel_id=1, source_target_pairs={{0,8},{1,9},{2,10},{3,11},{4,0},{5,1},{6,2},{7,3},{12,4},{13,5},{1... | collective-permute-start | bytes 835592 | tf_op jit(solution)/shard_map/ppermute | solution.py:59
  15.4 0.6 collective-permute-start.7
  16.0 0.9 %collective-permute-done.2 = bf16[128,256]{1,0:T(8,128)(2,1)S(1)} collective-permute-done((bf16[128,256]{1,0:T(8,128)(2,1)S(1)}, bf16[128,256]{1,0:T(8,128)(2,1)S(1)}, u32[]{:S(2)}, u32[]{:S(2)}) %collective-permute-start.2) | collective-permute-done | bytes 65568 | tf_op jit(solution)/shard_map/ppermute | solution.py:63
  16.9 3.3 %collective-permute-start.4 = (bf16[64,2176]{1,0:T(8,128)(2,1)S(1)}, bf16[64,2176]{1,0:T(8,128)(2,1)S(1)}, u32[]{:S(2)}, u32[]{:S(2)}) collective-permute-start(bf16[64,2176]{1,0:T(8,128)(2,1)S(1)} %collective-permute-done.refs_0_.refs_4_), channel_id=1, source_target_pairs={{0,4},{1,5},{2,6},{3,7},{4,12},{5,13},{6,14},{7,15},{12,8},{13,9},... | collective-permute-start | bytes 835592 | tf_op jit(solution)/shard_map/ppermute | solution.py:55
  20.3 2.6 %collective-permute-done.5.refs_4_.refs_12_ = bf16[64,2176]{1,0:T(8,128)(2,1)S(1)} collective-permute-done((bf16[64,2176]{1,0:T(8,128)(2,1)}, bf16[64,2176]{1,0:T(8,128)(2,1)S(1)}, u32[]{:S(2)}, u32[]{:S(2)}) %collective-permute-start.5) | collective-permute-done | bytes 278560 | tf_op jit(solution)/shard_map/ppermute | solution.py:59
  22.8 1.2 %collective-permute-start.6 = (bf16[64,2176]{1,0:T(8,128)(2,1)S(1)}, bf16[64,2176]{1,0:T(8,128)(2,1)S(1)}, u32[]{:S(2)}, u32[]{:S(2)}) collective-permute-start(bf16[64,2176]{1,0:T(8,128)(2,1)S(1)} %collective-permute-done.5.refs_4_.refs_12_), channel_id=1, source_target_pairs={{0,2},{1,3},{2,0},{3,1},{4,6},{5,7},{6,4},{7,5},{12,14},{13,15},{1... | collective-permute-start | bytes 835592 | tf_op jit(solution)/shard_map/ppermute | solution.py:63
  24.1 0.5 collective-permute-start.8
  24.6 0.0 collective-permute-start.9
  24.6 5.9 %collective-permute-done.4.refs_0_.refs_8_ = bf16[64,2176]{1,0:T(8,128)(2,1)S(1)} collective-permute-done((bf16[64,2176]{1,0:T(8,128)(2,1)S(1)}, bf16[64,2176]{1,0:T(8,128)(2,1)S(1)}, u32[]{:S(2)}, u32[]{:S(2)}) %collective-permute-start.4) | collective-permute-done | bytes 278560 | tf_op jit(solution)/shard_map/ppermute | solution.py:55
  30.5 1.5 %collective-permute-start.11 = (bf16[64,2176]{1,0:T(8,128)(2,1)S(1)}, bf16[64,2176]{1,0:T(8,128)(2,1)S(1)}, u32[]{:S(2)}, u32[]{:S(2)}) collective-permute-start(bf16[64,2176]{1,0:T(8,128)(2,1)S(1)} %collective-permute-done.4.refs_0_.refs_8_), channel_id=1, source_target_pairs={{0,2},{1,3},{2,0},{3,1},{4,6},{5,7},{6,4},{7,5},{12,14},{13,15},{1... | collective-permute-start | bytes 835592 | tf_op jit(solution)/shard_map/ppermute | solution.py:63
  32.0 0.7 collective-permute-start.13
  32.7 1.9 %collective-permute-start.12 = (bf16[256,256]{1,0:T(8,128)(2,1)S(1)}, bf16[256,256]{1,0:T(8,128)(2,1)S(1)}, u32[]{:S(2)}, u32[]{:S(2)}) collective-permute-start(bf16[256,256]{1,0:T(8,128)(2,1)S(1)} %pad_maximum_fusion.2), channel_id=1, source_target_pairs={{0,4},{1,5},{2,6},{3,7},{4,12},{5,13},{6,14},{7,15},{12,8},{13,9},... | collective-permute-start | bytes 393224 | tf_op jit(solution)/shard_map/ppermute | solution.py:55
  34.6 3.2 %experts.2 = (bf16[128,2048]{1,0:T(8,128)(2,1)S(1)}, bf16[128,2048]{1,0:T(8,128)(2,1)S(1)}, bf16[256,2048]{1,0:T(8,128)(2,1)S(1)}) custom-call(bf16[64,2176]{1,0:T(8,128)(2,1)S(1)} %collective-permute-done.refs_0_.refs_4_, bf16[64,2176]{1,0:T(8,128)(2,1)S(1)} %collective-permute-done.7.refs_1_.refs_5_, ...), custom_call_target="tpu_custom_call" | custom-call | flops 1 | bytes 1 | tf_op jit(solution)/shard_map/experts/pallas_call | solution.py:290
  37.7 2.2 %collective-permute-done.13 = bf16[256,256]{1,0:T(8,128)(2,1)S(1)} collective-permute-done((bf16[256,256]{1,0:T(8,128)(2,1)S(1)}, bf16[256,256]{1,0:T(8,128)(2,1)S(1)}, u32[]{:S(2)}, u32[]{:S(2)}) %collective-permute-start.13) | collective-permute-done | bytes 131104 | tf_op jit(solution)/shard_map/ppermute | solution.py:59
  39.9 0.0 collective-permute-done.12
  40.0 0.5 collective-permute-start.17
  40.5 0.1 collective-permute-start.18
  40.5 0.4 collective-permute-start.15
  41.0 0.1 collective-permute-start.16
  41.1 1.6 %collective-permute-done.14 = bf16[256,2048]{1,0:T(8,128)(2,1)S(1)} collective-permute-done((bf16[256,2048]{1,0:T(8,128)(2,1)S(1)}, bf16[256,2048]{1,0:T(8,128)(2,1)S(1)}, u32[]{:S(2)}, u32[]{:S(2)}) %collective-permute-start.14) | collective-permute-done | bytes 1048608 | tf_op jit(solution)/shard_map/ppermute | solution.py:67
  42.6 0.1 add_convert_fusion.7
  42.8 0.7 collective-permute-start.19
  43.5 1.6 %collective-permute-start.21 = (bf16[384,256]{1,0:T(8,128)(2,1)S(1)}, bf16[384,256]{1,0:T(8,128)(2,1)S(1)}, u32[]{:S(2)}, u32[]{:S(2)}) collective-permute-start(bf16[384,256]{1,0:T(8,128)(2,1)S(1)} %bitcast.34), channel_id=1, source_target_pairs={{0,16},{16,0},{1,17},{17,1},{2,18},{18,2},{3,19},{19,3},{4,20},{20... | collective-permute-start | bytes 589832 | tf_op jit(solution)/shard_map/ppermute | solution.py:470
  45.1 2.7 %collective-permute-start.20 = (bf16[256,256]{1,0:T(8,128)(2,1)S(1)}, bf16[256,256]{1,0:T(8,128)(2,1)S(1)}, u32[]{:S(2)}, u32[]{:S(2)}) collective-permute-start(bf16[256,256]{1,0:T(8,128)(2,1)S(1)} %collective-permute-done.12), channel_id=1, source_target_pairs={{0,4},{1,5},{2,6},{3,7},{4,12},{5,13},{6,14},{7,15},{12,8},{13,9},... | collective-permute-start | bytes 393224 | tf_op jit(solution)/shard_map/ppermute | solution.py:55
  47.7 3.2 %experts.3 = (bf16[128,2048]{1,0:T(8,128)(2,1)S(1)}, bf16[128,2048]{1,0:T(8,128)(2,1)S(1)}, bf16[128,2048]{1,0:T(8,128)(2,1)S(1)}, bf16[128,2048]{1,0:T(8,128)(2,1)S(1)}) custom-call(bf16[64,2176]{1,0:T(8,128)(2,1)S(1)} %collective-permute-done.4.refs_0_.refs_8_, bf16[64,2176]{1,0:T(8,128)(2,1)S(1)} %collective-permute-done.11.refs_1_.refs_9_, ...), custom_call_target="tpu_custom_call" | custom-call | flops 1 | bytes 1 | tf_op jit(solution)/shard_map/experts/pallas_call | solution.py:290
  50.9 0.0 copy-start.4
  50.9 1.1 %collective-permute-done.20 = bf16[256,256]{1,0:T(8,128)(2,1)S(1)} collective-permute-done((bf16[256,256]{1,0:T(8,128)(2,1)S(1)}, bf16[256,256]{1,0:T(8,128)(2,1)S(1)}, u32[]{:S(2)}, u32[]{:S(2)}) %collective-permute-start.20) | collective-permute-done | bytes 131104 | tf_op jit(solution)/shard_map/ppermute | solution.py:55
  52.1 0.1 add_convert_fusion.3
  52.2 1.6 %collective-permute-start.26 = (bf16[64,2048]{1,0:T(8,128)(2,1)S(1)}, bf16[64,2048]{1,0:T(8,128)(2,1)S(1)}, u32[]{:S(2)}, u32[]{:S(2)}) collective-permute-start(bf16[64,2048]{1,0:T(8,128)(2,1)S(1)} %add_convert_fusion.3), channel_id=1, source_target_pairs={{0,4},{1,5},{2,6},{3,7},{4,12},{5,13},{6,14},{7,15},{12,8},{13,9},... | collective-permute-start | bytes 786440 | tf_op jit(solution)/shard_map/ppermute | solution.py:55
  53.8 0.2 collective-permute-start.27
  54.0 0.1 add_convert_fusion.5
  54.1 0.9 %collective-permute-start.25 = (bf16[64,2048]{1,0:T(8,128)(2,1)S(1)}, bf16[64,2048]{1,0:T(8,128)(2,1)S(1)}, u32[]{:S(2)}, u32[]{:S(2)}) collective-permute-start(bf16[64,2048]{1,0:T(8,128)(2,1)S(1)} %add_convert_fusion.5), channel_id=1, source_target_pairs={{0,2},{1,3},{2,0},{3,1},{4,6},{5,7},{6,4},{7,5},{12,14},{13,15},{1... | collective-permute-start | bytes 786440 | tf_op jit(solution)/shard_map/ppermute | solution.py:63
  55.0 1.6 %collective-permute-start.29 = (bf16[128,256]{1,0:T(8,128)(2,1)S(1)}, bf16[128,256]{1,0:T(8,128)(2,1)S(1)}, u32[]{:S(2)}, u32[]{:S(2)}) collective-permute-start(bf16[128,256]{1,0:T(8,128)(2,1)S(1)} %bitcast.35), channel_id=1, source_target_pairs={{0,16},{16,0},{1,17},{17,1},{2,18},{18,2},{3,19},{19,3},{4,20},{20... | collective-permute-start | bytes 196616 | tf_op jit(solution)/shard_map/ppermute | solution.py:470
  56.6 2.9 %collective-permute-done.29.refs_18_ = bf16[128,256]{1,0:T(8,128)(2,1)S(1)} collective-permute-done((bf16[128,256]{1,0:T(8,128)(2,1)S(1)}, bf16[128,256]{1,0:T(8,128)(2,1)S(1)}, u32[]{:S(2)}, u32[]{:S(2)}) %collective-permute-start.29) | collective-permute-done | bytes 65568 | tf_op jit(solution)/shard_map/ppermute | solution.py:470
  59.5 1.3 %collective-permute-done.30.refs_21_ = bf16[128,256]{1,0:T(8,128)(2,1)S(1)} collective-permute-done((bf16[128,256]{1,0:T(8,128)(2,1)S(1)}, bf16[128,256]{1,0:T(8,128)(2,1)S(1)}, u32[]{:S(2)}, u32[]{:S(2)}) %collective-permute-start.30) | collective-permute-done | bytes 65568 | tf_op jit(solution)/shard_map/ppermute | solution.py:67
  60.8 0.2 collective-permute-start.23
  60.9 0.9 %collective-permute-done.26 = bf16[64,2048]{1,0:T(8,128)(2,1)S(1)} collective-permute-done((bf16[64,2048]{1,0:T(8,128)(2,1)S(1)}, bf16[64,2048]{1,0:T(8,128)(2,1)S(1)}, u32[]{:S(2)}, u32[]{:S(2)}) %collective-permute-start.26) | collective-permute-done | bytes 262176 | tf_op jit(solution)/shard_map/ppermute | solution.py:55
  61.8 0.8 %collective-permute-done.25 = bf16[64,2048]{1,0:T(8,128)(2,1)S(1)} collective-permute-done((bf16[64,2048]{1,0:T(8,128)(2,1)S(1)}, bf16[64,2048]{1,0:T(8,128)(2,1)S(1)}, u32[]{:S(2)}, u32[]{:S(2)}) %collective-permute-start.25) | collective-permute-done | bytes 262176 | tf_op jit(solution)/shard_map/ppermute | solution.py:63
  62.7 0.1 add_convert_fusion.2
  62.8 2.8 %collective-permute-start.31 = (bf16[64,2048]{1,0:T(8,128)(2,1)S(1)}, bf16[64,2048]{1,0:T(8,128)(2,1)S(1)}, u32[]{:S(2)}, u32[]{:S(2)}) collective-permute-start(bf16[64,2048]{1,0:T(8,128)(2,1)S(1)} %add_convert_fusion.2), channel_id=1, source_target_pairs={{0,4},{1,5},{2,6},{3,7},{4,12},{5,13},{6,14},{7,15},{12,8},{13,9},... | collective-permute-start | bytes 786440 | tf_op jit(solution)/shard_map/ppermute | solution.py:55
  65.6 0.1 add_convert_fusion.4
  65.7 0.9 %collective-permute-start.24 = (bf16[64,2048]{1,0:T(8,128)(2,1)S(1)}, bf16[64,2048]{1,0:T(8,128)(2,1)S(1)}, u32[]{:S(2)}, u32[]{:S(2)}) collective-permute-start(bf16[64,2048]{1,0:T(8,128)(2,1)S(1)} %add_convert_fusion.4), channel_id=1, source_target_pairs={{0,2},{1,3},{2,0},{3,1},{4,6},{5,7},{6,4},{7,5},{12,14},{13,15},{1... | collective-permute-start | bytes 786440 | tf_op jit(solution)/shard_map/ppermute | solution.py:63
  66.6 1.3 %values.1 = (bf16[1024,256]{1,0:T(8,128)(2,1)S(1)}, bf16[1024,256]{1,0:T(8,128)(2,1)S(1)}) custom-call(bf16[64,2176]{1,0:T(8,128)(2,1)S(1)} %copy-done.5, bf16[64,2176]{1,0:T(8,128)(2,1)S(1)} %collective-permute-done.3.refs_5_.refs_1_, bf16[64,2176]{1,0:T(8,128)(2,1)S(1)} %collective-permute-done.1.refs_6_.refs_2_, ...), custom_call_target="tpu_custom_call" | custom-call | flops 1 | bytes 1 | tf_op jit(solution)/shard_map/values/pallas_call | solution.py:333
  67.9 0.0 copy-start.7
  67.9 1.8 %attention.4.refs_0_ = bf16[64,4096]{1,0:T(8,128)(2,1)} custom-call(bf16[64,4096]{1,0:T(8,128)(2,1)S(1)} %bitcast.26, bf16[1024,256]{1,0:T(8,128)(2,1)S(1)} %get-tuple-element.54.k_ref, bf16[1024,256]{1,0:T(8,128)(2,1)S(1)} %get-tuple-element.55.v_ref), custom_call_target="tpu_custom_call" | custom-call | flops 1 | bytes 1 | tf_op jit(solution)/shard_map/attention/pallas_call | solution.py:415
  69.8 1.8 %attention.5.refs_0_ = bf16[64,4096]{1,0:T(8,128)(2,1)} custom-call(bf16[64,4096]{1,0:T(8,128)(2,1)S(1)} %bitcast.27, bf16[1024,256]{1,0:T(8,128)(2,1)S(1)} %get-tuple-element.54.k_ref, bf16[1024,256]{1,0:T(8,128)(2,1)S(1)} %get-tuple-element.55.v_ref, bf16[64,4096]{1,0:T(8,128)(2,1)} %attention.4.refs_0_), custom_call_target="tpu_custom_call", output_to_operand_aliasing={{}: (3, {})} | custom-call | flops 1 | bytes 1 | tf_op jit(solution)/shard_map/attention/pallas_call | solution.py:415
  71.6 0.0 collective-permute-done.31
  71.6 1.5 %collective-permute-done.24 = bf16[64,2048]{1,0:T(8,128)(2,1)S(1)} collective-permute-done((bf16[64,2048]{1,0:T(8,128)(2,1)S(1)}, bf16[64,2048]{1,0:T(8,128)(2,1)S(1)}, u32[]{:S(2)}, u32[]{:S(2)}) %collective-permute-start.24) | collective-permute-done | bytes 262176 | tf_op jit(solution)/shard_map/ppermute | solution.py:63
  73.2 0.1 add_convert_fusion.1
  73.3 1.2 %collective-permute-start.33 = (bf16[64,2048]{1,0:T(8,128)(2,1)S(1)}, bf16[64,2048]{1,0:T(8,128)(2,1)S(1)}, u32[]{:S(2)}, u32[]{:S(2)}) collective-permute-start(bf16[64,2048]{1,0:T(8,128)(2,1)S(1)} %add_convert_fusion.1), channel_id=1, source_target_pairs={{0,4},{1,5},{2,6},{3,7},{4,12},{5,13},{6,14},{7,15},{12,8},{13,9},... | collective-permute-start | bytes 786440 | tf_op jit(solution)/shard_map/ppermute | solution.py:55
  74.5 0.8 %collective-permute-start.32 = (bf16[64,2048]{1,0:T(8,128)(2,1)S(1)}, bf16[64,2048]{1,0:T(8,128)(2,1)S(1)}, u32[]{:S(2)}, u32[]{:S(2)}) collective-permute-start(bf16[64,2048]{1,0:T(8,128)(2,1)S(1)} %get-tuple-element.58), channel_id=1, source_target_pairs={{0,2},{1,3},{2,0},{3,1},{4,6},{5,7},{6,4},{7,5},{12,14},{13,15},{1... | collective-permute-start | bytes 786440 | tf_op jit(solution)/shard_map/ppermute | solution.py:63
  75.3 1.8 %attention.6.refs_0_ = bf16[64,4096]{1,0:T(8,128)(2,1)} custom-call(bf16[64,4096]{1,0:T(8,128)(2,1)S(1)} %bitcast.28, bf16[1024,256]{1,0:T(8,128)(2,1)S(1)} %get-tuple-element.54.k_ref, bf16[1024,256]{1,0:T(8,128)(2,1)S(1)} %get-tuple-element.55.v_ref, bf16[64,4096]{1,0:T(8,128)(2,1)} %attention.5.refs_0_), custom_call_target="tpu_custom_call", output_to_operand_aliasing={{}: (3, {})} | custom-call | flops 1 | bytes 1 | tf_op jit(solution)/shard_map/attention/pallas_call | solution.py:415
  77.2 1.8 %attention.7 = bf16[64,4096]{1,0:T(8,128)(2,1)} custom-call(bf16[64,4096]{1,0:T(8,128)(2,1)S(1)} %bitcast.29, bf16[1024,256]{1,0:T(8,128)(2,1)S(1)} %get-tuple-element.54.k_ref, bf16[1024,256]{1,0:T(8,128)(2,1)S(1)} %get-tuple-element.55.v_ref, bf16[64,4096]{1,0:T(8,128)(2,1)} %attention.6.refs_0_), custom_call_target="tpu_custom_call", output_to_operand_aliasing={{}: (3, {})} | custom-call | flops 1 | bytes 1 | tf_op jit(solution)/shard_map/attention/pallas_call | solution.py:415
  79.0 1.7 %collective-permute-done.33 = bf16[64,2048]{1,0:T(8,128)(2,1)S(1)} collective-permute-done((bf16[64,2048]{1,0:T(8,128)(2,1)S(1)}, bf16[64,2048]{1,0:T(8,128)(2,1)S(1)}, u32[]{:S(2)}, u32[]{:S(2)}) %collective-permute-start.33) | collective-permute-done | bytes 262176 | tf_op jit(solution)/shard_map/ppermute | solution.py:55
  80.7 0.1 collective-permute-done.32
  80.9 0.9 %fusion = bf16[64,1,2048]{2,0,1:T(8,128)(2,1)} fusion(bf16[64,2048]{1,0:T(8,128)(2,1)S(1)} %collective-permute-done.33, bf16[64,2048]{1,0:T(8,128)(2,1)S(1)} %collective-permute-done.32, bf16[256,2048]{1,0:T(8,128)(2,1)S(1)} %collective-permute-done.14, bf16[128,2048]{1,0:T(8,128)(2,1)S(1)} %get-tuple-element.36, bf16[64,1,2048]{2,0,1:T(8,128)(2,1)S(1)} %copy-done.7), kind=kLoop, calls=%fused_computation.10 | loop fusion | flops 1310720 | bytes 1572864 | tf_op jit(solution)/shard_map/reshape | solution.py:585
  (41 shorter events, 0.2 us)
Async XLA Ops:
  2.5 4.6 %collective-permute-start.1 = (bf16[64,2176]{1,0:T(8,128)(2,1)}, bf16[64,2176]{1,0:T(8,128)(2,1)S(1)}, u32[]{:S(2)}, u32[]{:S(2)}) collective-permute-start(bf16[64,2176]{1,0:T(8,128)(2,1)} %get-tuple-element.31.refs_4_.refs_0_), channel_id=1, source_target_pairs={{0,1},{1,0},{2,3},{3,2},{4,5},{5,4},{6,7},{7,6},{12,13},{13,12},{1... | collective-permute-start | bytes 835592 | tf_op jit(solution)/shard_map/ppermute | solution.py:67
  2.9 12.5 %collective-permute-start = (bf16[64,2176]{1,0:T(8,128)(2,1)}, bf16[64,2176]{1,0:T(8,128)(2,1)S(1)}, u32[]{:S(2)}, u32[]{:S(2)}) collective-permute-start(bf16[64,2176]{1,0:T(8,128)(2,1)} %get-tuple-element.31.refs_4_.refs_0_), channel_id=1, source_target_pairs={{0,4},{1,5},{2,6},{3,7},{4,12},{5,13},{6,14},{7,15},{12,8},{13,9},... | collective-permute-start | bytes 835592 | tf_op jit(solution)/shard_map/ppermute | solution.py:55
  5.5 11.4 %collective-permute-start.3 = (bf16[64,2176]{1,0:T(8,128)(2,1)}, bf16[64,2176]{1,0:T(8,128)(2,1)S(1)}, u32[]{:S(2)}, u32[]{:S(2)}) collective-permute-start(bf16[64,2176]{1,0:T(8,128)(2,1)} %get-tuple-element.31.refs_4_.refs_0_), channel_id=1, source_target_pairs={{0,2},{1,3},{2,0},{3,1},{4,6},{5,7},{6,4},{7,5},{12,14},{13,15},{1... | collective-permute-start | bytes 835592 | tf_op jit(solution)/shard_map/ppermute | solution.py:63
  7.0 2.8 %copy-start = (bf16[1,2048,1536]{2,1,0:T(8,128)(2,1)S(1)}, bf16[1,2048,1536]{2,1,0:T(8,128)(2,1)}, u32[]{:S(2)}) copy-start(bf16[1,2048,1536]{2,1,0:T(8,128)(2,1)} %param.16) | copy-start | bytes 18874372
  9.8 1.9 %copy-start.2 = (bf16[1,768,2048]{2,1,0:T(8,128)(2,1)S(1)}, bf16[1,768,2048]{2,1,0:T(8,128)(2,1)}, u32[]{:S(2)}) copy-start(bf16[1,768,2048]{2,1,0:T(8,128)(2,1)} %param.17) | copy-start | bytes 9437188
  11.7 0.8 %copy-start.6 = (bf16[128,256]{1,0:T(8,128)(2,1)S(1)}, bf16[128,256]{1,0:T(8,128)(2,1)}, u32[]{:S(2)}) copy-start(bf16[128,256]{1,0:T(8,128)(2,1)} %get-tuple-element.33.small_ref) | copy-start | bytes 196612
  12.6 22.0 %copy-start.1 = (bf16[1,2048,1536]{2,1,0:T(8,128)(2,1)S(1)}, bf16[1,2048,1536]{2,1,0:T(8,128)(2,1)}, u32[]{:S(2)}) copy-start(bf16[1,2048,1536]{2,1,0:T(8,128)(2,1)} %param.16) | copy-start | bytes 18874372
  12.6 22.0 %copy-start.3 = (bf16[1,768,2048]{2,1,0:T(8,128)(2,1)S(1)}, bf16[1,768,2048]{2,1,0:T(8,128)(2,1)}, u32[]{:S(2)}) copy-start(bf16[1,768,2048]{2,1,0:T(8,128)(2,1)} %param.17) | copy-start | bytes 9437188
  12.6 22.0 %copy-start.5 = (bf16[64,2176]{1,0:T(8,128)(2,1)S(1)}, bf16[64,2176]{1,0:T(8,128)(2,1)}, u32[]{:S(2)}) copy-start(bf16[64,2176]{1,0:T(8,128)(2,1)} %get-tuple-element.31.refs_4_.refs_0_) | copy-start | bytes 835588
  12.6 4.3 %collective-permute-start.2 = (bf16[128,256]{1,0:T(8,128)(2,1)S(1)}, bf16[128,256]{1,0:T(8,128)(2,1)S(1)}, u32[]{:S(2)}, u32[]{:S(2)}) collective-permute-start(bf16[128,256]{1,0:T(8,128)(2,1)S(1)} %hold_weights.1), channel_id=1, source_target_pairs={{0,2},{1,3},{2,0},{3,1},{4,6},{5,7},{6,4},{7,5},{12,14},{13,15},{1... | collective-permute-start | bytes 196616 | tf_op jit(solution)/shard_map/ppermute | solution.py:63
  13.2 9.7 %collective-permute-start.5 = (bf16[64,2176]{1,0:T(8,128)(2,1)}, bf16[64,2176]{1,0:T(8,128)(2,1)S(1)}, u32[]{:S(2)}, u32[]{:S(2)}) collective-permute-start(bf16[64,2176]{1,0:T(8,128)(2,1)} %get-tuple-element.31.refs_4_.refs_0_), channel_id=1, source_target_pairs={{0,8},{1,9},{2,10},{3,11},{4,0},{5,1},{6,2},{7,3},{12,4},{13,5},{1... | collective-permute-start | bytes 835592 | tf_op jit(solution)/shard_map/ppermute | solution.py:59
  15.4 9.1 %collective-permute-start.7 = (bf16[64,2176]{1,0:T(8,128)(2,1)S(1)}, bf16[64,2176]{1,0:T(8,128)(2,1)S(1)}, u32[]{:S(2)}, u32[]{:S(2)}) collective-permute-start(bf16[64,2176]{1,0:T(8,128)(2,1)S(1)} %collective-permute-done.refs_0_.refs_4_), channel_id=1, source_target_pairs={{0,2},{1,3},{2,0},{3,1},{4,6},{5,7},{6,4},{7,5},{12,14},{13,15},{1... | collective-permute-start | bytes 835592 | tf_op jit(solution)/shard_map/ppermute | solution.py:63
  16.9 13.5 %collective-permute-start.4 = (bf16[64,2176]{1,0:T(8,128)(2,1)S(1)}, bf16[64,2176]{1,0:T(8,128)(2,1)S(1)}, u32[]{:S(2)}, u32[]{:S(2)}) collective-permute-start(bf16[64,2176]{1,0:T(8,128)(2,1)S(1)} %collective-permute-done.refs_0_.refs_4_), channel_id=1, source_target_pairs={{0,4},{1,5},{2,6},{3,7},{4,12},{5,13},{6,14},{7,15},{12,8},{13,9},... | collective-permute-start | bytes 835592 | tf_op jit(solution)/shard_map/ppermute | solution.py:55
  22.8 9.2 %collective-permute-start.6 = (bf16[64,2176]{1,0:T(8,128)(2,1)S(1)}, bf16[64,2176]{1,0:T(8,128)(2,1)S(1)}, u32[]{:S(2)}, u32[]{:S(2)}) collective-permute-start(bf16[64,2176]{1,0:T(8,128)(2,1)S(1)} %collective-permute-done.5.refs_4_.refs_12_), channel_id=1, source_target_pairs={{0,2},{1,3},{2,0},{3,1},{4,6},{5,7},{6,4},{7,5},{12,14},{13,15},{1... | collective-permute-start | bytes 835592 | tf_op jit(solution)/shard_map/ppermute | solution.py:63
  24.1 8.6 %collective-permute-start.10 = (bf16[64,2176]{1,0:T(8,128)(2,1)S(1)}, bf16[64,2176]{1,0:T(8,128)(2,1)S(1)}, u32[]{:S(2)}, u32[]{:S(2)}) collective-permute-start(bf16[64,2176]{1,0:T(8,128)(2,1)S(1)} %collective-permute-done.3.refs_5_.refs_1_), channel_id=1, source_target_pairs={{0,1},{1,0},{2,3},{3,2},{4,5},{5,4},{6,7},{7,6},{12,13},{13,12},{1... | collective-permute-start | bytes 835592 | tf_op jit(solution)/shard_map/ppermute | solution.py:67
  24.1 10.5 %collective-permute-start.8 = (bf16[64,2176]{1,0:T(8,128)(2,1)S(1)}, bf16[64,2176]{1,0:T(8,128)(2,1)S(1)}, u32[]{:S(2)}, u32[]{:S(2)}) collective-permute-start(bf16[64,2176]{1,0:T(8,128)(2,1)S(1)} %collective-permute-done.refs_0_.refs_4_), channel_id=1, source_target_pairs={{0,1},{1,0},{2,3},{3,2},{4,5},{5,4},{6,7},{7,6},{12,13},{13,12},{1... | collective-permute-start | bytes 835592 | tf_op jit(solution)/shard_map/ppermute | solution.py:67
  24.6 10.0 %collective-permute-start.9 = (bf16[64,2176]{1,0:T(8,128)(2,1)S(1)}, bf16[64,2176]{1,0:T(8,128)(2,1)S(1)}, u32[]{:S(2)}, u32[]{:S(2)}) collective-permute-start(bf16[64,2176]{1,0:T(8,128)(2,1)S(1)} %collective-permute-done.7.refs_1_.refs_5_), channel_id=1, source_target_pairs={{0,1},{1,0},{2,3},{3,2},{4,5},{5,4},{6,7},{7,6},{12,13},{13,12},{1... | collective-permute-start | bytes 835592 | tf_op jit(solution)/shard_map/ppermute | solution.py:67
  30.5 9.5 %collective-permute-start.11 = (bf16[64,2176]{1,0:T(8,128)(2,1)S(1)}, bf16[64,2176]{1,0:T(8,128)(2,1)S(1)}, u32[]{:S(2)}, u32[]{:S(2)}) collective-permute-start(bf16[64,2176]{1,0:T(8,128)(2,1)S(1)} %collective-permute-done.4.refs_0_.refs_8_), channel_id=1, source_target_pairs={{0,2},{1,3},{2,0},{3,1},{4,6},{5,7},{6,4},{7,5},{12,14},{13,15},{1... | collective-permute-start | bytes 835592 | tf_op jit(solution)/shard_map/ppermute | solution.py:63
  32.0 7.9 %collective-permute-start.13 = (bf16[256,256]{1,0:T(8,128)(2,1)S(1)}, bf16[256,256]{1,0:T(8,128)(2,1)S(1)}, u32[]{:S(2)}, u32[]{:S(2)}) collective-permute-start(bf16[256,256]{1,0:T(8,128)(2,1)S(1)} %pad_maximum_fusion.2), channel_id=1, source_target_pairs={{0,8},{1,9},{2,10},{3,11},{4,0},{5,1},{6,2},{7,3},{12,4},{13,5},{1... | collective-permute-start | bytes 393224 | tf_op jit(solution)/shard_map/ppermute | solution.py:59
  32.7 7.3 %collective-permute-start.12 = (bf16[256,256]{1,0:T(8,128)(2,1)S(1)}, bf16[256,256]{1,0:T(8,128)(2,1)S(1)}, u32[]{:S(2)}, u32[]{:S(2)}) collective-permute-start(bf16[256,256]{1,0:T(8,128)(2,1)S(1)} %pad_maximum_fusion.2), channel_id=1, source_target_pairs={{0,4},{1,5},{2,6},{3,7},{4,12},{5,13},{6,14},{7,15},{12,8},{13,9},... | collective-permute-start | bytes 393224 | tf_op jit(solution)/shard_map/ppermute | solution.py:55
  40.0 2.7 %collective-permute-start.14 = (bf16[256,2048]{1,0:T(8,128)(2,1)S(1)}, bf16[256,2048]{1,0:T(8,128)(2,1)S(1)}, u32[]{:S(2)}, u32[]{:S(2)}) collective-permute-start(bf16[256,2048]{1,0:T(8,128)(2,1)S(1)} %get-tuple-element.39), channel_id=1, source_target_pairs={{0,1},{1,0},{2,3},{3,2},{4,5},{5,4},{6,7},{7,6},{12,13},{13,12},{1... | collective-permute-start | bytes 3145736 | tf_op jit(solution)/shard_map/ppermute | solution.py:67
  40.0 3.5 %collective-permute-start.17 = (bf16[64,2176]{1,0:T(8,128)(2,1)S(1)}, bf16[64,2176]{1,0:T(8,128)(2,1)S(1)}, u32[]{:S(2)}, u32[]{:S(2)}) collective-permute-start(bf16[64,2176]{1,0:T(8,128)(2,1)S(1)} %collective-permute-done.5.refs_4_.refs_12_), channel_id=1, source_target_pairs={{0,1},{1,0},{2,3},{3,2},{4,5},{5,4},{6,7},{7,6},{12,13},{13,12},{1... | collective-permute-start | bytes 835592 | tf_op jit(solution)/shard_map/ppermute | solution.py:67
  40.5 4.6 %collective-permute-start.18 = (bf16[64,2176]{1,0:T(8,128)(2,1)S(1)}, bf16[64,2176]{1,0:T(8,128)(2,1)S(1)}, u32[]{:S(2)}, u32[]{:S(2)}) collective-permute-start(bf16[64,2176]{1,0:T(8,128)(2,1)S(1)} %collective-permute-done.6.refs_5_.refs_13_), channel_id=1, source_target_pairs={{0,1},{1,0},{2,3},{3,2},{4,5},{5,4},{6,7},{7,6},{12,13},{13,12},{1... | collective-permute-start | bytes 835592 | tf_op jit(solution)/shard_map/ppermute | solution.py:67
  40.5 7.2 %collective-permute-start.15 = (bf16[64,2176]{1,0:T(8,128)(2,1)S(1)}, bf16[64,2176]{1,0:T(8,128)(2,1)S(1)}, u32[]{:S(2)}, u32[]{:S(2)}) collective-permute-start(bf16[64,2176]{1,0:T(8,128)(2,1)S(1)} %collective-permute-done.4.refs_0_.refs_8_), channel_id=1, source_target_pairs={{0,1},{1,0},{2,3},{3,2},{4,5},{5,4},{6,7},{7,6},{12,13},{13,12},{1... | collective-permute-start | bytes 835592 | tf_op jit(solution)/shard_map/ppermute | solution.py:67
  41.0 6.7 %collective-permute-start.16 = (bf16[64,2176]{1,0:T(8,128)(2,1)S(1)}, bf16[64,2176]{1,0:T(8,128)(2,1)S(1)}, u32[]{:S(2)}, u32[]{:S(2)}) collective-permute-start(bf16[64,2176]{1,0:T(8,128)(2,1)S(1)} %collective-permute-done.11.refs_1_.refs_9_), channel_id=1, source_target_pairs={{0,1},{1,0},{2,3},{3,2},{4,5},{5,4},{6,7},{7,6},{12,13},{13,12},{1... | collective-permute-start | bytes 835592 | tf_op jit(solution)/shard_map/ppermute | solution.py:67
  42.8 9.2 %collective-permute-start.19 = (bf16[64,2048]{1,0:T(8,128)(2,1)S(1)}, bf16[64,2048]{1,0:T(8,128)(2,1)S(1)}, u32[]{:S(2)}, u32[]{:S(2)}) collective-permute-start(bf16[64,2048]{1,0:T(8,128)(2,1)S(1)} %get-tuple-element.61), channel_id=1, source_target_pairs={{0,2},{1,3},{2,0},{3,1},{4,6},{5,7},{6,4},{7,5},{12,14},{13,15},{1... | collective-permute-start | bytes 786440 | tf_op jit(solution)/shard_map/ppermute | solution.py:63
  43.5 8.5 %collective-permute-start.21 = (bf16[384,256]{1,0:T(8,128)(2,1)S(1)}, bf16[384,256]{1,0:T(8,128)(2,1)S(1)}, u32[]{:S(2)}, u32[]{:S(2)}) collective-permute-start(bf16[384,256]{1,0:T(8,128)(2,1)S(1)} %bitcast.34), channel_id=1, source_target_pairs={{0,16},{16,0},{1,17},{17,1},{2,18},{18,2},{3,19},{19,3},{4,20},{20... | collective-permute-start | bytes 589832 | tf_op jit(solution)/shard_map/ppermute | solution.py:470
  45.1 6.9 %collective-permute-start.20 = (bf16[256,256]{1,0:T(8,128)(2,1)S(1)}, bf16[256,256]{1,0:T(8,128)(2,1)S(1)}, u32[]{:S(2)}, u32[]{:S(2)}) collective-permute-start(bf16[256,256]{1,0:T(8,128)(2,1)S(1)} %collective-permute-done.12), channel_id=1, source_target_pairs={{0,4},{1,5},{2,6},{3,7},{4,12},{5,13},{6,14},{7,15},{12,8},{13,9},... | collective-permute-start | bytes 393224 | tf_op jit(solution)/shard_map/ppermute | solution.py:55
  50.9 17.0 %copy-start.4 = (bf16[64,1,4096]{2,0,1:T(8,128)(2,1)S(1)}, bf16[64,1,4096]{2,0,1:T(8,128)(2,1)}, u32[]{:S(2)}) copy-start(bf16[64,1,4096]{2,0,1:T(8,128)(2,1)} %param.10) | copy-start | bytes 1572868
  52.0 2.0 %collective-permute-start.22 = (bf16[128,2048]{1,0:T(8,128)(2,1)S(1)}, bf16[128,2048]{1,0:T(8,128)(2,1)S(1)}, u32[]{:S(2)}, u32[]{:S(2)}) collective-permute-start(bf16[128,2048]{1,0:T(8,128)(2,1)S(1)} %get-tuple-element.46), channel_id=1, source_target_pairs={{0,1},{1,0},{2,3},{3,2},{4,5},{5,4},{6,7},{7,6},{12,13},{13,12},{1... | collective-permute-start | bytes 1572872 | tf_op jit(solution)/shard_map/ppermute | solution.py:67
  52.2 9.7 %collective-permute-start.26 = (bf16[64,2048]{1,0:T(8,128)(2,1)S(1)}, bf16[64,2048]{1,0:T(8,128)(2,1)S(1)}, u32[]{:S(2)}, u32[]{:S(2)}) collective-permute-start(bf16[64,2048]{1,0:T(8,128)(2,1)S(1)} %add_convert_fusion.3), channel_id=1, source_target_pairs={{0,4},{1,5},{2,6},{3,7},{4,12},{5,13},{6,14},{7,15},{12,8},{13,9},... | collective-permute-start | bytes 786440 | tf_op jit(solution)/shard_map/ppermute | solution.py:55
  53.8 8.0 %collective-permute-start.27 = (bf16[1024,256]{1,0:T(8,128)(2,1)S(1)}, bf16[1024,256]{1,0:T(8,128)(2,1)S(1)}, u32[]{:S(2)}, u32[]{:S(2)}) collective-permute-start(bf16[1024,256]{1,0:T(8,128)(2,1)S(1)} %pad_maximum_fusion.refs_16_), channel_id=1, source_target_pairs={{0,1},{1,0},{2,3},{3,2},{4,5},{5,4},{6,7},{7,6},{12,13},{13,12},{1... | collective-permute-start | bytes 1572872 | tf_op jit(solution)/shard_map/ppermute | solution.py:67
  54.1 8.6 %collective-permute-start.25 = (bf16[64,2048]{1,0:T(8,128)(2,1)S(1)}, bf16[64,2048]{1,0:T(8,128)(2,1)S(1)}, u32[]{:S(2)}, u32[]{:S(2)}) collective-permute-start(bf16[64,2048]{1,0:T(8,128)(2,1)S(1)} %add_convert_fusion.5), channel_id=1, source_target_pairs={{0,2},{1,3},{2,0},{3,1},{4,6},{5,7},{6,4},{7,5},{12,14},{13,15},{1... | collective-permute-start | bytes 786440 | tf_op jit(solution)/shard_map/ppermute | solution.py:63
  55.0 5.9 %collective-permute-start.28 = (bf16[384,256]{1,0:T(8,128)(2,1)S(1)}, bf16[384,256]{1,0:T(8,128)(2,1)S(1)}, u32[]{:S(2)}, u32[]{:S(2)}) collective-permute-start(bf16[384,256]{1,0:T(8,128)(2,1)S(1)} %collective-permute-done.21.refs_17_), channel_id=1, source_target_pairs={{0,1},{1,0},{2,3},{3,2},{4,5},{5,4},{6,7},{7,6},{12,13},{13,12},{1... | collective-permute-start | bytes 589832 | tf_op jit(solution)/shard_map/ppermute | solution.py:67
  55.0 4.5 %collective-permute-start.29 = (bf16[128,256]{1,0:T(8,128)(2,1)S(1)}, bf16[128,256]{1,0:T(8,128)(2,1)S(1)}, u32[]{:S(2)}, u32[]{:S(2)}) collective-permute-start(bf16[128,256]{1,0:T(8,128)(2,1)S(1)} %bitcast.35), channel_id=1, source_target_pairs={{0,16},{16,0},{1,17},{17,1},{2,18},{18,2},{3,19},{19,3},{4,20},{20... | collective-permute-start | bytes 196616 | tf_op jit(solution)/shard_map/ppermute | solution.py:470
  59.5 1.3 %collective-permute-start.30 = (bf16[128,256]{1,0:T(8,128)(2,1)S(1)}, bf16[128,256]{1,0:T(8,128)(2,1)S(1)}, u32[]{:S(2)}, u32[]{:S(2)}) collective-permute-start(bf16[128,256]{1,0:T(8,128)(2,1)S(1)} %collective-permute-done.29.refs_18_), channel_id=1, source_target_pairs={{0,1},{1,0},{2,3},{3,2},{4,5},{5,4},{6,7},{7,6},{12,13},{13,12},{1... | collective-permute-start | bytes 196616 | tf_op jit(solution)/shard_map/ppermute | solution.py:67
  60.8 4.8 %collective-permute-start.23 = (bf16[128,2048]{1,0:T(8,128)(2,1)S(1)}, bf16[128,2048]{1,0:T(8,128)(2,1)S(1)}, u32[]{:S(2)}, u32[]{:S(2)}) collective-permute-start(bf16[128,2048]{1,0:T(8,128)(2,1)S(1)} %get-tuple-element.47), channel_id=1, source_target_pairs={{0,1},{1,0},{2,3},{3,2},{4,5},{5,4},{6,7},{7,6},{12,13},{13,12},{1... | collective-permute-start | bytes 1572872 | tf_op jit(solution)/shard_map/ppermute | solution.py:67
  62.8 8.8 %collective-permute-start.31 = (bf16[64,2048]{1,0:T(8,128)(2,1)S(1)}, bf16[64,2048]{1,0:T(8,128)(2,1)S(1)}, u32[]{:S(2)}, u32[]{:S(2)}) collective-permute-start(bf16[64,2048]{1,0:T(8,128)(2,1)S(1)} %add_convert_fusion.2), channel_id=1, source_target_pairs={{0,4},{1,5},{2,6},{3,7},{4,12},{5,13},{6,14},{7,15},{12,8},{13,9},... | collective-permute-start | bytes 786440 | tf_op jit(solution)/shard_map/ppermute | solution.py:55
  65.7 7.5 %collective-permute-start.24 = (bf16[64,2048]{1,0:T(8,128)(2,1)S(1)}, bf16[64,2048]{1,0:T(8,128)(2,1)S(1)}, u32[]{:S(2)}, u32[]{:S(2)}) collective-permute-start(bf16[64,2048]{1,0:T(8,128)(2,1)S(1)} %add_convert_fusion.4), channel_id=1, source_target_pairs={{0,2},{1,3},{2,0},{3,1},{4,6},{5,7},{6,4},{7,5},{12,14},{13,15},{1... | collective-permute-start | bytes 786440 | tf_op jit(solution)/shard_map/ppermute | solution.py:63
  67.9 13.0 %copy-start.7 = (bf16[64,1,2048]{2,0,1:T(8,128)(2,1)S(1)}, bf16[64,1,2048]{2,0,1:T(8,128)(2,1)}, u32[]{:S(2)}) copy-start(bf16[64,1,2048]{2,0,1:T(8,128)(2,1)} %param.9) | copy-start | bytes 786436
  73.3 7.4 %collective-permute-start.33 = (bf16[64,2048]{1,0:T(8,128)(2,1)S(1)}, bf16[64,2048]{1,0:T(8,128)(2,1)S(1)}, u32[]{:S(2)}, u32[]{:S(2)}) collective-permute-start(bf16[64,2048]{1,0:T(8,128)(2,1)S(1)} %add_convert_fusion.1), channel_id=1, source_target_pairs={{0,4},{1,5},{2,6},{3,7},{4,12},{5,13},{6,14},{7,15},{12,8},{13,9},... | collective-permute-start | bytes 786440 | tf_op jit(solution)/shard_map/ppermute | solution.py:55
  74.5 6.4 %collective-permute-start.32 = (bf16[64,2048]{1,0:T(8,128)(2,1)S(1)}, bf16[64,2048]{1,0:T(8,128)(2,1)S(1)}, u32[]{:S(2)}, u32[]{:S(2)}) collective-permute-start(bf16[64,2048]{1,0:T(8,128)(2,1)S(1)} %get-tuple-element.58), channel_id=1, source_target_pairs={{0,2},{1,3},{2,0},{3,1},{4,6},{5,7},{6,4},{7,5},{12,14},{13,15},{1... | collective-permute-start | bytes 786440 | tf_op jit(solution)/shard_map/ppermute | solution.py:63

commit v16 on v15

--- a/solution.py
+++ b/solution.py
@@ -515,7 +515,7 @@
     far = swap_planes([after(pairs[2], total)])
     own = after(jnp.concatenate([pairs[step] for step in order], axis=0), total)
     smalls = [own, near, far, other_core(own), other_core(after(near, total)), other_core(far)]
-    total = summed(*mine[2], theirs[2], after(moving, *smalls[3:]))
+    total = summed(*mine[2], theirs[2], after(moving, far, *smalls[3:5]))
     moving = forward(total)
     theirs[0] = across(after(crossing[0], total))
     smalls[0] = after(own, total)

time: 82 us -> 82.8 us (level)
  waiting for transfers between devices: 23.6 us -> 27.3 us
  starting transfers between devices: 33.3 us -> 30.4 us
    ppermute x7, waiting for transfers between devices: 9.6 us -> 15.4 us  [forward(): return lax.ppermute(x, 'seq', ring_steps(1))]
    ppermute x7, starting transfers between devices: 16.1 us -> 12.1 us  [forward(): return lax.ppermute(x, 'seq', ring_steps(1))]
    ppermute x2, waiting for transfers between devices: 4.77 us -> 2.57 us  [backward(): return lax.ppermute(x, 'seq', ring_steps(LINE - 1))]
    ppermute x9, starting transfers between devices: 8.78 us -> 10.1 us  [across(): return lax.ppermute(x, 'seq', swaps(1, 0))]
    ppermute x14, waiting for transfers between devices: 2.85 us -> 3.97 us  [other_core(): return lax.ppermute(x, 'seq', swaps(0, 1))]
    ppermute x9, waiting for transfers between devices: 3.39 us -> 2.38 us  [across(): return lax.ppermute(x, 'seq', swaps(1, 0))]
  transfers between devices with their start and end apart: 34 -> 34, of which waited for: 13 -> 14; matrix products, arithmetic and copies ran while one was open for 1% -> 1% of each run, Pallas kernels for 18% -> 18%
where the time goes in v16:
time: 82.8 us; the launch traced here: 82.5 us
  starting transfers between devices  30.4 us (37%)
  waiting for transfers between devices  27.3 us (33%)
  Pallas kernels  16.9 us (20%)
  local copies, waits for them, and re-layouts  5.56 us (7%)
  other arithmetic  1.57 us (2%)
    ppermute x7, waiting for transfers between devices, forward(): return lax.ppermute(x, 'seq', ring_steps(1))  15.4 us
    ppermute x7, starting transfers between devices, forward(): return lax.ppermute(x, 'seq', ring_steps(1))  12.1 us
    ppermute x9, starting transfers between devices, across(): return lax.ppermute(x, 'seq', swaps(1, 0))  10.1 us
    pallas_call x4, Pallas kernels, attend_part(): pl.pallas_call(functools.partial(attention_kernel, chunk), grid=(1,), out...  7.33 us
    pallas_call x2, Pallas kernels, run_experts(): pl.pallas_call(functools.partial(expert_kernel, top, tok_rows, capacity,...  6.37 us
    unnamed x16, local copies, waits for them, and re-layouts  5.54 us
    ppermute x14, waiting for transfers between devices, other_core(): return lax.ppermute(x, 'seq', swaps(0, 1))  3.97 us
    ppermute x2, starting transfers between devices, swap_planes(): lax.ppermute(shares.reshape(-1, both.shape[1]), 'grp', [(0, 1), (1, 0)])  3.04 us
  transfers between devices with their start and end apart: 34, of which 14 were waited for; matrix products, arithmetic and copies ran while one was open for 1% of the time, Pallas kernels for 18%

profile of v16, /device:TPU:0, one launch (start us, length us, event | category | flops | bytes accessed | tf_op | source)
XLA Modules:
  0.0 82.5 jit_solution(6360304418080007713)
XLA Ops:
  0.6 1.9 %normalize_and_pack.1 = (bf16[64,2176]{1,0:T(8,128)(2,1)}, bf16[128,256]{1,0:T(8,128)(2,1)}) custom-call(bf16[64,2048]{1,0:T(8,128)(2,1)} %bitcast.31, f32[1,2048]{1,0:T(1,128)} %bitcast.37, s32[4,64]{1,0:T(4,128)} %bitcast.38, f32[4,64]{1,0:T(4,128)} %bitcast.39, bf16[64,256]{1,0:T(8,128)(2,1)} %bitcast.36, bf16[128,256]{1,0:T(8,128)(2,1)} %weight_ref.1), custom_call_target="tpu_custom_call" | custom-call | flops 1 | bytes 1 | tf_op jit(solution)/shard_map/normalize_and_pack/pallas_call | solution.py:112
  2.5 0.5 collective-permute-start.1
  2.9 2.6 %collective-permute-start = (bf16[64,2176]{1,0:T(8,128)(2,1)}, bf16[64,2176]{1,0:T(8,128)(2,1)S(1)}, u32[]{:S(2)}, u32[]{:S(2)}) collective-permute-start(bf16[64,2176]{1,0:T(8,128)(2,1)} %get-tuple-element.31.refs_4_.refs_0_), channel_id=1, source_target_pairs={{0,4},{1,5},{2,6},{3,7},{4,12},{5,13},{6,14},{7,15},{12,8},{13,9},... | collective-permute-start | bytes 835592 | tf_op jit(solution)/shard_map/ppermute | solution.py:55
  5.5 1.5 %collective-permute-start.3 = (bf16[64,2176]{1,0:T(8,128)(2,1)}, bf16[64,2176]{1,0:T(8,128)(2,1)S(1)}, u32[]{:S(2)}, u32[]{:S(2)}) collective-permute-start(bf16[64,2176]{1,0:T(8,128)(2,1)} %get-tuple-element.31.refs_4_.refs_0_), channel_id=1, source_target_pairs={{0,2},{1,3},{2,0},{3,1},{4,6},{5,7},{6,4},{7,5},{12,14},{13,15},{1... | collective-permute-start | bytes 835592 | tf_op jit(solution)/shard_map/ppermute | solution.py:63
  7.0 0.0 collective-permute-done.1.refs_6_.refs_2_
  7.0 2.8 %copy-done = bf16[1,2048,1536]{2,1,0:T(8,128)(2,1)S(1)} copy-done((bf16[1,2048,1536]{2,1,0:T(8,128)(2,1)S(1)}, bf16[1,2048,1536]{2,1,0:T(8,128)(2,1)}, u32[]{:S(2)}) %copy-start) | copy-done | bytes 6291480
  9.8 1.9 %copy-done.2 = bf16[1,768,2048]{2,1,0:T(8,128)(2,1)S(1)} copy-done((bf16[1,768,2048]{2,1,0:T(8,128)(2,1)S(1)}, bf16[1,768,2048]{2,1,0:T(8,128)(2,1)}, u32[]{:S(2)}) %copy-start.2) | copy-done | bytes 3145752
  11.7 0.8 %copy-done.6 = bf16[128,256]{1,0:T(8,128)(2,1)S(1)} copy-done((bf16[128,256]{1,0:T(8,128)(2,1)S(1)}, bf16[128,256]{1,0:T(8,128)(2,1)}, u32[]{:S(2)}) %copy-start.6) | copy-done | bytes 65560
  12.6 0.6 collective-permute-start.2
  13.2 2.3 %collective-permute-start.5 = (bf16[64,2176]{1,0:T(8,128)(2,1)}, bf16[64,2176]{1,0:T(8,128)(2,1)S(1)}, u32[]{:S(2)}, u32[]{:S(2)}) collective-permute-start(bf16[64,2176]{1,0:T(8,128)(2,1)} %get-tuple-element.31.refs_4_.refs_0_), channel_id=1, source_target_pairs={{0,8},{1,9},{2,10},{3,11},{4,0},{5,1},{6,2},{7,3},{12,4},{13,5},{1... | collective-permute-start | bytes 835592 | tf_op jit(solution)/shard_map/ppermute | solution.py:59
  15.4 0.6 collective-permute-start.7
  16.0 0.9 %collective-permute-done.2 = bf16[128,256]{1,0:T(8,128)(2,1)S(1)} collective-permute-done((bf16[128,256]{1,0:T(8,128)(2,1)S(1)}, bf16[128,256]{1,0:T(8,128)(2,1)S(1)}, u32[]{:S(2)}, u32[]{:S(2)}) %collective-permute-start.2) | collective-permute-done | bytes 65568 | tf_op jit(solution)/shard_map/ppermute | solution.py:63
  16.9 0.0 collective-permute-done.3.refs_5_.refs_1_
  16.9 3.3 %collective-permute-start.4 = (bf16[64,2176]{1,0:T(8,128)(2,1)S(1)}, bf16[64,2176]{1,0:T(8,128)(2,1)S(1)}, u32[]{:S(2)}, u32[]{:S(2)}) collective-permute-start(bf16[64,2176]{1,0:T(8,128)(2,1)S(1)} %collective-permute-done.refs_0_.refs_4_), channel_id=1, source_target_pairs={{0,4},{1,5},{2,6},{3,7},{4,12},{5,13},{6,14},{7,15},{12,8},{13,9},... | collective-permute-start | bytes 835592 | tf_op jit(solution)/shard_map/ppermute | solution.py:55
  20.3 2.6 %collective-permute-done.5.refs_4_.refs_12_ = bf16[64,2176]{1,0:T(8,128)(2,1)S(1)} collective-permute-done((bf16[64,2176]{1,0:T(8,128)(2,1)}, bf16[64,2176]{1,0:T(8,128)(2,1)S(1)}, u32[]{:S(2)}, u32[]{:S(2)}) %collective-permute-start.5) | collective-permute-done | bytes 278560 | tf_op jit(solution)/shard_map/ppermute | solution.py:59
  22.8 1.2 %collective-permute-start.6 = (bf16[64,2176]{1,0:T(8,128)(2,1)S(1)}, bf16[64,2176]{1,0:T(8,128)(2,1)S(1)}, u32[]{:S(2)}, u32[]{:S(2)}) collective-permute-start(bf16[64,2176]{1,0:T(8,128)(2,1)S(1)} %collective-permute-done.5.refs_4_.refs_12_), channel_id=1, source_target_pairs={{0,2},{1,3},{2,0},{3,1},{4,6},{5,7},{6,4},{7,5},{12,14},{13,15},{1... | collective-permute-start | bytes 835592 | tf_op jit(solution)/shard_map/ppermute | solution.py:63
  24.1 0.5 collective-permute-start.10
  24.6 0.0 collective-permute-start.9
  24.6 5.9 %collective-permute-done.4.refs_0_.refs_8_ = bf16[64,2176]{1,0:T(8,128)(2,1)S(1)} collective-permute-done((bf16[64,2176]{1,0:T(8,128)(2,1)S(1)}, bf16[64,2176]{1,0:T(8,128)(2,1)S(1)}, u32[]{:S(2)}, u32[]{:S(2)}) %collective-permute-start.4) | collective-permute-done | bytes 278560 | tf_op jit(solution)/shard_map/ppermute | solution.py:55
  30.5 1.5 %collective-permute-start.11 = (bf16[64,2176]{1,0:T(8,128)(2,1)S(1)}, bf16[64,2176]{1,0:T(8,128)(2,1)S(1)}, u32[]{:S(2)}, u32[]{:S(2)}) collective-permute-start(bf16[64,2176]{1,0:T(8,128)(2,1)S(1)} %collective-permute-done.4.refs_0_.refs_8_), channel_id=1, source_target_pairs={{0,2},{1,3},{2,0},{3,1},{4,6},{5,7},{6,4},{7,5},{12,14},{13,15},{1... | collective-permute-start | bytes 835592 | tf_op jit(solution)/shard_map/ppermute | solution.py:63
  32.0 2.5 %collective-permute-start.12 = (bf16[256,256]{1,0:T(8,128)(2,1)S(1)}, bf16[256,256]{1,0:T(8,128)(2,1)S(1)}, u32[]{:S(2)}, u32[]{:S(2)}) collective-permute-start(bf16[256,256]{1,0:T(8,128)(2,1)S(1)} %pad_maximum_fusion.2), channel_id=1, source_target_pairs={{0,4},{1,5},{2,6},{3,7},{4,12},{5,13},{6,14},{7,15},{12,8},{13,9},... | collective-permute-start | bytes 393224 | tf_op jit(solution)/shard_map/ppermute | solution.py:55
  34.5 0.4 collective-permute-start.13
  35.0 3.2 %experts.2 = (bf16[128,2048]{1,0:T(8,128)(2,1)S(1)}, bf16[128,2048]{1,0:T(8,128)(2,1)S(1)}, bf16[256,2048]{1,0:T(8,128)(2,1)S(1)}) custom-call(bf16[64,2176]{1,0:T(8,128)(2,1)S(1)} %collective-permute-done.refs_0_.refs_4_, bf16[64,2176]{1,0:T(8,128)(2,1)S(1)} %collective-permute-done.7.refs_1_.refs_5_, ...), custom_call_target="tpu_custom_call" | custom-call | flops 1 | bytes 1 | tf_op jit(solution)/shard_map/experts/pallas_call | solution.py:290
  38.2 2.7 %collective-permute-done.12 = bf16[256,256]{1,0:T(8,128)(2,1)S(1)} collective-permute-done((bf16[256,256]{1,0:T(8,128)(2,1)S(1)}, bf16[256,256]{1,0:T(8,128)(2,1)S(1)}, u32[]{:S(2)}, u32[]{:S(2)}) %collective-permute-start.12) | collective-permute-done | bytes 131104 | tf_op jit(solution)/shard_map/ppermute | solution.py:55
  40.9 0.5 collective-permute-start.17
  41.4 0.1 collective-permute-start.18
  41.4 0.4 collective-permute-start.15
  41.9 0.1 collective-permute-start.16
  42.0 1.6 %collective-permute-done.14 = bf16[256,2048]{1,0:T(8,128)(2,1)S(1)} collective-permute-done((bf16[256,2048]{1,0:T(8,128)(2,1)S(1)}, bf16[256,2048]{1,0:T(8,128)(2,1)S(1)}, u32[]{:S(2)}, u32[]{:S(2)}) %collective-permute-start.14) | collective-permute-done | bytes 1048608 | tf_op jit(solution)/shard_map/ppermute | solution.py:67
  43.5 0.1 add_convert_fusion.7
  43.7 1.2 %collective-permute-start.19 = (bf16[64,2048]{1,0:T(8,128)(2,1)S(1)}, bf16[64,2048]{1,0:T(8,128)(2,1)S(1)}, u32[]{:S(2)}, u32[]{:S(2)}) collective-permute-start(bf16[64,2048]{1,0:T(8,128)(2,1)S(1)} %get-tuple-element.61), channel_id=1, source_target_pairs={{0,2},{1,3},{2,0},{3,1},{4,6},{5,7},{6,4},{7,5},{12,14},{13,15},{1... | collective-permute-start | bytes 786440 | tf_op jit(solution)/shard_map/ppermute | solution.py:63
  44.9 1.6 %collective-permute-start.21 = (bf16[384,256]{1,0:T(8,128)(2,1)S(1)}, bf16[384,256]{1,0:T(8,128)(2,1)S(1)}, u32[]{:S(2)}, u32[]{:S(2)}) collective-permute-start(bf16[384,256]{1,0:T(8,128)(2,1)S(1)} %bitcast.34), channel_id=1, source_target_pairs={{0,16},{16,0},{1,17},{17,1},{2,18},{18,2},{3,19},{19,3},{4,20},{20... | collective-permute-start | bytes 589832 | tf_op jit(solution)/shard_map/ppermute | solution.py:470
  46.5 0.9 %collective-permute-start.20 = (bf16[256,256]{1,0:T(8,128)(2,1)S(1)}, bf16[256,256]{1,0:T(8,128)(2,1)S(1)}, u32[]{:S(2)}, u32[]{:S(2)}) collective-permute-start(bf16[256,256]{1,0:T(8,128)(2,1)S(1)} %collective-permute-done.12), channel_id=1, source_target_pairs={{0,4},{1,5},{2,6},{3,7},{4,12},{5,13},{6,14},{7,15},{12,8},{13,9},... | collective-permute-start | bytes 393224 | tf_op jit(solution)/shard_map/ppermute | solution.py:55
  47.4 3.2 %experts.3 = (bf16[128,2048]{1,0:T(8,128)(2,1)S(1)}, bf16[128,2048]{1,0:T(8,128)(2,1)S(1)}, bf16[128,2048]{1,0:T(8,128)(2,1)S(1)}, bf16[128,2048]{1,0:T(8,128)(2,1)S(1)}) custom-call(bf16[64,2176]{1,0:T(8,128)(2,1)S(1)} %collective-permute-done.4.refs_0_.refs_8_, bf16[64,2176]{1,0:T(8,128)(2,1)S(1)} %collective-permute-done.11.refs_1_.refs_9_, ...), custom_call_target="tpu_custom_call" | custom-call | flops 1 | bytes 1 | tf_op jit(solution)/shard_map/experts/pallas_call | solution.py:290
  50.6 0.0 copy-start.4
  50.6 1.8 %collective-permute-done.20 = bf16[256,256]{1,0:T(8,128)(2,1)S(1)} collective-permute-done((bf16[256,256]{1,0:T(8,128)(2,1)S(1)}, bf16[256,256]{1,0:T(8,128)(2,1)S(1)}, u32[]{:S(2)}, u32[]{:S(2)}) %collective-permute-start.20) | collective-permute-done | bytes 131104 | tf_op jit(solution)/shard_map/ppermute | solution.py:55
  52.4 0.1 add_convert_fusion.3
  52.5 0.2 collective-permute-start.26
  52.7 0.4 collective-permute-start.28
  53.1 1.1 %collective-permute-done.22 = bf16[128,2048]{1,0:T(8,128)(2,1)S(1)} collective-permute-done((bf16[128,2048]{1,0:T(8,128)(2,1)S(1)}, bf16[128,2048]{1,0:T(8,128)(2,1)S(1)}, u32[]{:S(2)}, u32[]{:S(2)}) %collective-permute-start.22) | collective-permute-done | bytes 524320 | tf_op jit(solution)/shard_map/ppermute | solution.py:67
  54.3 0.1 add_convert_fusion.5
  54.3 1.0 %collective-permute-start.25 = (bf16[64,2048]{1,0:T(8,128)(2,1)S(1)}, bf16[64,2048]{1,0:T(8,128)(2,1)S(1)}, u32[]{:S(2)}, u32[]{:S(2)}) collective-permute-start(bf16[64,2048]{1,0:T(8,128)(2,1)S(1)} %add_convert_fusion.5), channel_id=1, source_target_pairs={{0,2},{1,3},{2,0},{3,1},{4,6},{5,7},{6,4},{7,5},{12,14},{13,15},{1... | collective-permute-start | bytes 786440 | tf_op jit(solution)/shard_map/ppermute | solution.py:63
  55.3 1.5 %collective-permute-start.27 = (bf16[128,256]{1,0:T(8,128)(2,1)S(1)}, bf16[128,256]{1,0:T(8,128)(2,1)S(1)}, u32[]{:S(2)}, u32[]{:S(2)}) collective-permute-start(bf16[128,256]{1,0:T(8,128)(2,1)S(1)} %bitcast.35), channel_id=1, source_target_pairs={{0,16},{16,0},{1,17},{17,1},{2,18},{18,2},{3,19},{19,3},{4,20},{20... | collective-permute-start | bytes 196616 | tf_op jit(solution)/shard_map/ppermute | solution.py:470
  56.8 3.0 %collective-permute-done.27.refs_18_ = bf16[128,256]{1,0:T(8,128)(2,1)S(1)} collective-permute-done((bf16[128,256]{1,0:T(8,128)(2,1)S(1)}, bf16[128,256]{1,0:T(8,128)(2,1)S(1)}, u32[]{:S(2)}, u32[]{:S(2)}) %collective-permute-start.27) | collective-permute-done | bytes 65568 | tf_op jit(solution)/shard_map/ppermute | solution.py:470
  59.8 2.3 %collective-permute-done.26 = bf16[64,2048]{1,0:T(8,128)(2,1)S(1)} collective-permute-done((bf16[64,2048]{1,0:T(8,128)(2,1)S(1)}, bf16[64,2048]{1,0:T(8,128)(2,1)S(1)}, u32[]{:S(2)}, u32[]{:S(2)}) %collective-permute-start.26) | collective-permute-done | bytes 262176 | tf_op jit(solution)/shard_map/ppermute | solution.py:55
  62.2 0.6 collective-permute-done.25
  62.7 0.1 add_convert_fusion.2
  62.9 0.7 collective-permute-start.30
  63.5 0.1 add_convert_fusion.4
  63.6 1.4 %collective-permute-start.24 = (bf16[64,2048]{1,0:T(8,128)(2,1)S(1)}, bf16[64,2048]{1,0:T(8,128)(2,1)S(1)}, u32[]{:S(2)}, u32[]{:S(2)}) collective-permute-start(bf16[64,2048]{1,0:T(8,128)(2,1)S(1)} %add_convert_fusion.4), channel_id=1, source_target_pairs={{0,2},{1,3},{2,0},{3,1},{4,6},{5,7},{6,4},{7,5},{12,14},{13,15},{1... | collective-permute-start | bytes 786440 | tf_op jit(solution)/shard_map/ppermute | solution.py:63
  65.0 1.3 %collective-permute-done.31.refs_21_ = bf16[128,256]{1,0:T(8,128)(2,1)S(1)} collective-permute-done((bf16[128,256]{1,0:T(8,128)(2,1)S(1)}, bf16[128,256]{1,0:T(8,128)(2,1)S(1)}, u32[]{:S(2)}, u32[]{:S(2)}) %collective-permute-start.31) | collective-permute-done | bytes 65568 | tf_op jit(solution)/shard_map/ppermute | solution.py:67
  66.2 1.3 %values.1 = (bf16[1024,256]{1,0:T(8,128)(2,1)S(1)}, bf16[1024,256]{1,0:T(8,128)(2,1)S(1)}) custom-call(bf16[64,2176]{1,0:T(8,128)(2,1)S(1)} %copy-done.5, bf16[64,2176]{1,0:T(8,128)(2,1)S(1)} %collective-permute-done.3.refs_5_.refs_1_, bf16[64,2176]{1,0:T(8,128)(2,1)S(1)} %collective-permute-done.1.refs_6_.refs_2_, ...), custom_call_target="tpu_custom_call" | custom-call | flops 1 | bytes 1 | tf_op jit(solution)/shard_map/values/pallas_call | solution.py:333
  67.6 0.0 copy-start.7
  67.6 1.8 %attention.4.refs_0_ = bf16[64,4096]{1,0:T(8,128)(2,1)} custom-call(bf16[64,4096]{1,0:T(8,128)(2,1)S(1)} %bitcast.26, bf16[1024,256]{1,0:T(8,128)(2,1)S(1)} %get-tuple-element.54.k_ref, bf16[1024,256]{1,0:T(8,128)(2,1)S(1)} %get-tuple-element.55.v_ref), custom_call_target="tpu_custom_call" | custom-call | flops 1 | bytes 1 | tf_op jit(solution)/shard_map/attention/pallas_call | solution.py:415
  69.4 1.8 %attention.5.refs_0_ = bf16[64,4096]{1,0:T(8,128)(2,1)} custom-call(bf16[64,4096]{1,0:T(8,128)(2,1)S(1)} %bitcast.27, bf16[1024,256]{1,0:T(8,128)(2,1)S(1)} %get-tuple-element.54.k_ref, bf16[1024,256]{1,0:T(8,128)(2,1)S(1)} %get-tuple-element.55.v_ref, bf16[64,4096]{1,0:T(8,128)(2,1)} %attention.4.refs_0_), custom_call_target="tpu_custom_call", output_to_operand_aliasing={{}: (3, {})} | custom-call | flops 1 | bytes 1 | tf_op jit(solution)/shard_map/attention/pallas_call | solution.py:415
  71.3 0.3 collective-permute-done.30
  71.5 0.1 add_convert_fusion.1
  71.7 1.9 %collective-permute-start.33 = (bf16[64,2048]{1,0:T(8,128)(2,1)S(1)}, bf16[64,2048]{1,0:T(8,128)(2,1)S(1)}, u32[]{:S(2)}, u32[]{:S(2)}) collective-permute-start(bf16[64,2048]{1,0:T(8,128)(2,1)S(1)} %add_convert_fusion.1), channel_id=1, source_target_pairs={{0,4},{1,5},{2,6},{3,7},{4,12},{5,13},{6,14},{7,15},{12,8},{13,9},... | collective-permute-start | bytes 786440 | tf_op jit(solution)/shard_map/ppermute | solution.py:55
  73.5 1.1 %collective-permute-start.32 = (bf16[64,2048]{1,0:T(8,128)(2,1)S(1)}, bf16[64,2048]{1,0:T(8,128)(2,1)S(1)}, u32[]{:S(2)}, u32[]{:S(2)}) collective-permute-start(bf16[64,2048]{1,0:T(8,128)(2,1)S(1)} %get-tuple-element.58), channel_id=1, source_target_pairs={{0,2},{1,3},{2,0},{3,1},{4,6},{5,7},{6,4},{7,5},{12,14},{13,15},{1... | collective-permute-start | bytes 786440 | tf_op jit(solution)/shard_map/ppermute | solution.py:63
  74.7 1.8 %attention.6.refs_0_ = bf16[64,4096]{1,0:T(8,128)(2,1)} custom-call(bf16[64,4096]{1,0:T(8,128)(2,1)S(1)} %bitcast.28, bf16[1024,256]{1,0:T(8,128)(2,1)S(1)} %get-tuple-element.54.k_ref, bf16[1024,256]{1,0:T(8,128)(2,1)S(1)} %get-tuple-element.55.v_ref, bf16[64,4096]{1,0:T(8,128)(2,1)} %attention.5.refs_0_), custom_call_target="tpu_custom_call", output_to_operand_aliasing={{}: (3, {})} | custom-call | flops 1 | bytes 1 | tf_op jit(solution)/shard_map/attention/pallas_call | solution.py:415
  76.5 1.8 %attention.7 = bf16[64,4096]{1,0:T(8,128)(2,1)} custom-call(bf16[64,4096]{1,0:T(8,128)(2,1)S(1)} %bitcast.29, bf16[1024,256]{1,0:T(8,128)(2,1)S(1)} %get-tuple-element.54.k_ref, bf16[1024,256]{1,0:T(8,128)(2,1)S(1)} %get-tuple-element.55.v_ref, bf16[64,4096]{1,0:T(8,128)(2,1)} %attention.6.refs_0_), custom_call_target="tpu_custom_call", output_to_operand_aliasing={{}: (3, {})} | custom-call | flops 1 | bytes 1 | tf_op jit(solution)/shard_map/attention/pallas_call | solution.py:415
  78.3 2.4 %collective-permute-done.33 = bf16[64,2048]{1,0:T(8,128)(2,1)S(1)} collective-permute-done((bf16[64,2048]{1,0:T(8,128)(2,1)S(1)}, bf16[64,2048]{1,0:T(8,128)(2,1)S(1)}, u32[]{:S(2)}, u32[]{:S(2)}) %collective-permute-start.33) | collective-permute-done | bytes 262176 | tf_op jit(solution)/shard_map/ppermute | solution.py:55
  80.7 0.9 %collective-permute-done.32 = bf16[64,2048]{1,0:T(8,128)(2,1)S(1)} collective-permute-done((bf16[64,2048]{1,0:T(8,128)(2,1)S(1)}, bf16[64,2048]{1,0:T(8,128)(2,1)S(1)}, u32[]{:S(2)}, u32[]{:S(2)}) %collective-permute-start.32) | collective-permute-done | bytes 262176 | tf_op jit(solution)/shard_map/ppermute | solution.py:63
  81.6 0.9 %fusion = bf16[64,1,2048]{2,0,1:T(8,128)(2,1)} fusion(bf16[64,2048]{1,0:T(8,128)(2,1)S(1)} %collective-permute-done.33, bf16[64,2048]{1,0:T(8,128)(2,1)S(1)} %collective-permute-done.32, bf16[256,2048]{1,0:T(8,128)(2,1)S(1)} %collective-permute-done.14, bf16[128,2048]{1,0:T(8,128)(2,1)S(1)} %get-tuple-element.36, bf16[64,1,2048]{2,0,1:T(8,128)(2,1)S(1)} %copy-done.7), kind=kLoop, calls=%fused_computation.10 | loop fusion | flops 1310720 | bytes 1572864 | tf_op jit(solution)/shard_map/reshape | solution.py:585
  (41 shorter events, 0.2 us)
Async XLA Ops:
  2.5 4.6 %collective-permute-start.1 = (bf16[64,2176]{1,0:T(8,128)(2,1)}, bf16[64,2176]{1,0:T(8,128)(2,1)S(1)}, u32[]{:S(2)}, u32[]{:S(2)}) collective-permute-start(bf16[64,2176]{1,0:T(8,128)(2,1)} %get-tuple-element.31.refs_4_.refs_0_), channel_id=1, source_target_pairs={{0,1},{1,0},{2,3},{3,2},{4,5},{5,4},{6,7},{7,6},{12,13},{13,12},{1... | collective-permute-start | bytes 835592 | tf_op jit(solution)/shard_map/ppermute | solution.py:67
  2.9 12.5 %collective-permute-start = (bf16[64,2176]{1,0:T(8,128)(2,1)}, bf16[64,2176]{1,0:T(8,128)(2,1)S(1)}, u32[]{:S(2)}, u32[]{:S(2)}) collective-permute-start(bf16[64,2176]{1,0:T(8,128)(2,1)} %get-tuple-element.31.refs_4_.refs_0_), channel_id=1, source_target_pairs={{0,4},{1,5},{2,6},{3,7},{4,12},{5,13},{6,14},{7,15},{12,8},{13,9},... | collective-permute-start | bytes 835592 | tf_op jit(solution)/shard_map/ppermute | solution.py:55
  5.5 11.4 %collective-permute-start.3 = (bf16[64,2176]{1,0:T(8,128)(2,1)}, bf16[64,2176]{1,0:T(8,128)(2,1)S(1)}, u32[]{:S(2)}, u32[]{:S(2)}) collective-permute-start(bf16[64,2176]{1,0:T(8,128)(2,1)} %get-tuple-element.31.refs_4_.refs_0_), channel_id=1, source_target_pairs={{0,2},{1,3},{2,0},{3,1},{4,6},{5,7},{6,4},{7,5},{12,14},{13,15},{1... | collective-permute-start | bytes 835592 | tf_op jit(solution)/shard_map/ppermute | solution.py:63
  7.0 2.8 %copy-start = (bf16[1,2048,1536]{2,1,0:T(8,128)(2,1)S(1)}, bf16[1,2048,1536]{2,1,0:T(8,128)(2,1)}, u32[]{:S(2)}) copy-start(bf16[1,2048,1536]{2,1,0:T(8,128)(2,1)} %param.16) | copy-start | bytes 18874372
  9.8 1.9 %copy-start.2 = (bf16[1,768,2048]{2,1,0:T(8,128)(2,1)S(1)}, bf16[1,768,2048]{2,1,0:T(8,128)(2,1)}, u32[]{:S(2)}) copy-start(bf16[1,768,2048]{2,1,0:T(8,128)(2,1)} %param.17) | copy-start | bytes 9437188
  11.7 0.8 %copy-start.6 = (bf16[128,256]{1,0:T(8,128)(2,1)S(1)}, bf16[128,256]{1,0:T(8,128)(2,1)}, u32[]{:S(2)}) copy-start(bf16[128,256]{1,0:T(8,128)(2,1)} %get-tuple-element.33.small_ref) | copy-start | bytes 196612
  12.6 22.4 %copy-start.1 = (bf16[1,2048,1536]{2,1,0:T(8,128)(2,1)S(1)}, bf16[1,2048,1536]{2,1,0:T(8,128)(2,1)}, u32[]{:S(2)}) copy-start(bf16[1,2048,1536]{2,1,0:T(8,128)(2,1)} %param.16) | copy-start | bytes 18874372
  12.6 22.4 %copy-start.3 = (bf16[1,768,2048]{2,1,0:T(8,128)(2,1)S(1)}, bf16[1,768,2048]{2,1,0:T(8,128)(2,1)}, u32[]{:S(2)}) copy-start(bf16[1,768,2048]{2,1,0:T(8,128)(2,1)} %param.17) | copy-start | bytes 9437188
  12.6 22.4 %copy-start.5 = (bf16[64,2176]{1,0:T(8,128)(2,1)S(1)}, bf16[64,2176]{1,0:T(8,128)(2,1)}, u32[]{:S(2)}) copy-start(bf16[64,2176]{1,0:T(8,128)(2,1)} %get-tuple-element.31.refs_4_.refs_0_) | copy-start | bytes 835588
  12.6 4.3 %collective-permute-start.2 = (bf16[128,256]{1,0:T(8,128)(2,1)S(1)}, bf16[128,256]{1,0:T(8,128)(2,1)S(1)}, u32[]{:S(2)}, u32[]{:S(2)}) collective-permute-start(bf16[128,256]{1,0:T(8,128)(2,1)S(1)} %hold_weights.1), channel_id=1, source_target_pairs={{0,2},{1,3},{2,0},{3,1},{4,6},{5,7},{6,4},{7,5},{12,14},{13,15},{1... | collective-permute-start | bytes 196616 | tf_op jit(solution)/shard_map/ppermute | solution.py:63
  13.2 9.7 %collective-permute-start.5 = (bf16[64,2176]{1,0:T(8,128)(2,1)}, bf16[64,2176]{1,0:T(8,128)(2,1)S(1)}, u32[]{:S(2)}, u32[]{:S(2)}) collective-permute-start(bf16[64,2176]{1,0:T(8,128)(2,1)} %get-tuple-element.31.refs_4_.refs_0_), channel_id=1, source_target_pairs={{0,8},{1,9},{2,10},{3,11},{4,0},{5,1},{6,2},{7,3},{12,4},{13,5},{1... | collective-permute-start | bytes 835592 | tf_op jit(solution)/shard_map/ppermute | solution.py:59
  15.4 9.1 %collective-permute-start.7 = (bf16[64,2176]{1,0:T(8,128)(2,1)S(1)}, bf16[64,2176]{1,0:T(8,128)(2,1)S(1)}, u32[]{:S(2)}, u32[]{:S(2)}) collective-permute-start(bf16[64,2176]{1,0:T(8,128)(2,1)S(1)} %collective-permute-done.refs_0_.refs_4_), channel_id=1, source_target_pairs={{0,2},{1,3},{2,0},{3,1},{4,6},{5,7},{6,4},{7,5},{12,14},{13,15},{1... | collective-permute-start | bytes 835592 | tf_op jit(solution)/shard_map/ppermute | solution.py:63
  16.9 13.5 %collective-permute-start.4 = (bf16[64,2176]{1,0:T(8,128)(2,1)S(1)}, bf16[64,2176]{1,0:T(8,128)(2,1)S(1)}, u32[]{:S(2)}, u32[]{:S(2)}) collective-permute-start(bf16[64,2176]{1,0:T(8,128)(2,1)S(1)} %collective-permute-done.refs_0_.refs_4_), channel_id=1, source_target_pairs={{0,4},{1,5},{2,6},{3,7},{4,12},{5,13},{6,14},{7,15},{12,8},{13,9},... | collective-permute-start | bytes 835592 | tf_op jit(solution)/shard_map/ppermute | solution.py:55
  22.8 9.2 %collective-permute-start.6 = (bf16[64,2176]{1,0:T(8,128)(2,1)S(1)}, bf16[64,2176]{1,0:T(8,128)(2,1)S(1)}, u32[]{:S(2)}, u32[]{:S(2)}) collective-permute-start(bf16[64,2176]{1,0:T(8,128)(2,1)S(1)} %collective-permute-done.5.refs_4_.refs_12_), channel_id=1, source_target_pairs={{0,2},{1,3},{2,0},{3,1},{4,6},{5,7},{6,4},{7,5},{12,14},{13,15},{1... | collective-permute-start | bytes 835592 | tf_op jit(solution)/shard_map/ppermute | solution.py:63
  24.1 10.5 %collective-permute-start.8 = (bf16[64,2176]{1,0:T(8,128)(2,1)S(1)}, bf16[64,2176]{1,0:T(8,128)(2,1)S(1)}, u32[]{:S(2)}, u32[]{:S(2)}) collective-permute-start(bf16[64,2176]{1,0:T(8,128)(2,1)S(1)} %collective-permute-done.refs_0_.refs_4_), channel_id=1, source_target_pairs={{0,1},{1,0},{2,3},{3,2},{4,5},{5,4},{6,7},{7,6},{12,13},{13,12},{1... | collective-permute-start | bytes 835592 | tf_op jit(solution)/shard_map/ppermute | solution.py:67
  24.1 10.9 %collective-permute-start.10 = (bf16[64,2176]{1,0:T(8,128)(2,1)S(1)}, bf16[64,2176]{1,0:T(8,128)(2,1)S(1)}, u32[]{:S(2)}, u32[]{:S(2)}) collective-permute-start(bf16[64,2176]{1,0:T(8,128)(2,1)S(1)} %collective-permute-done.3.refs_5_.refs_1_), channel_id=1, source_target_pairs={{0,1},{1,0},{2,3},{3,2},{4,5},{5,4},{6,7},{7,6},{12,13},{13,12},{1... | collective-permute-start | bytes 835592 | tf_op jit(solution)/shard_map/ppermute | solution.py:67
  24.6 10.4 %collective-permute-start.9 = (bf16[64,2176]{1,0:T(8,128)(2,1)S(1)}, bf16[64,2176]{1,0:T(8,128)(2,1)S(1)}, u32[]{:S(2)}, u32[]{:S(2)}) collective-permute-start(bf16[64,2176]{1,0:T(8,128)(2,1)S(1)} %collective-permute-done.7.refs_1_.refs_5_), channel_id=1, source_target_pairs={{0,1},{1,0},{2,3},{3,2},{4,5},{5,4},{6,7},{7,6},{12,13},{13,12},{1... | collective-permute-start | bytes 835592 | tf_op jit(solution)/shard_map/ppermute | solution.py:67
  30.5 10.4 %collective-permute-start.11 = (bf16[64,2176]{1,0:T(8,128)(2,1)S(1)}, bf16[64,2176]{1,0:T(8,128)(2,1)S(1)}, u32[]{:S(2)}, u32[]{:S(2)}) collective-permute-start(bf16[64,2176]{1,0:T(8,128)(2,1)S(1)} %collective-permute-done.4.refs_0_.refs_8_), channel_id=1, source_target_pairs={{0,2},{1,3},{2,0},{3,1},{4,6},{5,7},{6,4},{7,5},{12,14},{13,15},{1... | collective-permute-start | bytes 835592 | tf_op jit(solution)/shard_map/ppermute | solution.py:63
  32.0 8.8 %collective-permute-start.12 = (bf16[256,256]{1,0:T(8,128)(2,1)S(1)}, bf16[256,256]{1,0:T(8,128)(2,1)S(1)}, u32[]{:S(2)}, u32[]{:S(2)}) collective-permute-start(bf16[256,256]{1,0:T(8,128)(2,1)S(1)} %pad_maximum_fusion.2), channel_id=1, source_target_pairs={{0,4},{1,5},{2,6},{3,7},{4,12},{5,13},{6,14},{7,15},{12,8},{13,9},... | collective-permute-start | bytes 393224 | tf_op jit(solution)/shard_map/ppermute | solution.py:55
  34.5 6.3 %collective-permute-start.13 = (bf16[256,256]{1,0:T(8,128)(2,1)S(1)}, bf16[256,256]{1,0:T(8,128)(2,1)S(1)}, u32[]{:S(2)}, u32[]{:S(2)}) collective-permute-start(bf16[256,256]{1,0:T(8,128)(2,1)S(1)} %pad_maximum_fusion.2), channel_id=1, source_target_pairs={{0,8},{1,9},{2,10},{3,11},{4,0},{5,1},{6,2},{7,3},{12,4},{13,5},{1... | collective-permute-start | bytes 393224 | tf_op jit(solution)/shard_map/ppermute | solution.py:59
  40.9 2.7 %collective-permute-start.14 = (bf16[256,2048]{1,0:T(8,128)(2,1)S(1)}, bf16[256,2048]{1,0:T(8,128)(2,1)S(1)}, u32[]{:S(2)}, u32[]{:S(2)}) collective-permute-start(bf16[256,2048]{1,0:T(8,128)(2,1)S(1)} %get-tuple-element.39), channel_id=1, source_target_pairs={{0,1},{1,0},{2,3},{3,2},{4,5},{5,4},{6,7},{7,6},{12,13},{13,12},{1... | collective-permute-start | bytes 3145736 | tf_op jit(solution)/shard_map/ppermute | solution.py:67
  40.9 4.0 %collective-permute-start.17 = (bf16[64,2176]{1,0:T(8,128)(2,1)S(1)}, bf16[64,2176]{1,0:T(8,128)(2,1)S(1)}, u32[]{:S(2)}, u32[]{:S(2)}) collective-permute-start(bf16[64,2176]{1,0:T(8,128)(2,1)S(1)} %collective-permute-done.5.refs_4_.refs_12_), channel_id=1, source_target_pairs={{0,1},{1,0},{2,3},{3,2},{4,5},{5,4},{6,7},{7,6},{12,13},{13,12},{1... | collective-permute-start | bytes 835592 | tf_op jit(solution)/shard_map/ppermute | solution.py:67
  41.4 5.1 %collective-permute-start.18 = (bf16[64,2176]{1,0:T(8,128)(2,1)S(1)}, bf16[64,2176]{1,0:T(8,128)(2,1)S(1)}, u32[]{:S(2)}, u32[]{:S(2)}) collective-permute-start(bf16[64,2176]{1,0:T(8,128)(2,1)S(1)} %collective-permute-done.6.refs_5_.refs_13_), channel_id=1, source_target_pairs={{0,1},{1,0},{2,3},{3,2},{4,5},{5,4},{6,7},{7,6},{12,13},{13,12},{1... | collective-permute-start | bytes 835592 | tf_op jit(solution)/shard_map/ppermute | solution.py:67
  41.4 5.9 %collective-permute-start.15 = (bf16[64,2176]{1,0:T(8,128)(2,1)S(1)}, bf16[64,2176]{1,0:T(8,128)(2,1)S(1)}, u32[]{:S(2)}, u32[]{:S(2)}) collective-permute-start(bf16[64,2176]{1,0:T(8,128)(2,1)S(1)} %collective-permute-done.4.refs_0_.refs_8_), channel_id=1, source_target_pairs={{0,1},{1,0},{2,3},{3,2},{4,5},{5,4},{6,7},{7,6},{12,13},{13,12},{1... | collective-permute-start | bytes 835592 | tf_op jit(solution)/shard_map/ppermute | solution.py:67
  41.9 5.5 %collective-permute-start.16 = (bf16[64,2176]{1,0:T(8,128)(2,1)S(1)}, bf16[64,2176]{1,0:T(8,128)(2,1)S(1)}, u32[]{:S(2)}, u32[]{:S(2)}) collective-permute-start(bf16[64,2176]{1,0:T(8,128)(2,1)S(1)} %collective-permute-done.11.refs_1_.refs_9_), channel_id=1, source_target_pairs={{0,1},{1,0},{2,3},{3,2},{4,5},{5,4},{6,7},{7,6},{12,13},{13,12},{1... | collective-permute-start | bytes 835592 | tf_op jit(solution)/shard_map/ppermute | solution.py:67
  43.7 8.7 %collective-permute-start.19 = (bf16[64,2048]{1,0:T(8,128)(2,1)S(1)}, bf16[64,2048]{1,0:T(8,128)(2,1)S(1)}, u32[]{:S(2)}, u32[]{:S(2)}) collective-permute-start(bf16[64,2048]{1,0:T(8,128)(2,1)S(1)} %get-tuple-element.61), channel_id=1, source_target_pairs={{0,2},{1,3},{2,0},{3,1},{4,6},{5,7},{6,4},{7,5},{12,14},{13,15},{1... | collective-permute-start | bytes 786440 | tf_op jit(solution)/shard_map/ppermute | solution.py:63
  44.9 7.4 %collective-permute-start.21 = (bf16[384,256]{1,0:T(8,128)(2,1)S(1)}, bf16[384,256]{1,0:T(8,128)(2,1)S(1)}, u32[]{:S(2)}, u32[]{:S(2)}) collective-permute-start(bf16[384,256]{1,0:T(8,128)(2,1)S(1)} %bitcast.34), channel_id=1, source_target_pairs={{0,16},{16,0},{1,17},{17,1},{2,18},{18,2},{3,19},{19,3},{4,20},{20... | collective-permute-start | bytes 589832 | tf_op jit(solution)/shard_map/ppermute | solution.py:470
  46.5 5.9 %collective-permute-start.20 = (bf16[256,256]{1,0:T(8,128)(2,1)S(1)}, bf16[256,256]{1,0:T(8,128)(2,1)S(1)}, u32[]{:S(2)}, u32[]{:S(2)}) collective-permute-start(bf16[256,256]{1,0:T(8,128)(2,1)S(1)} %collective-permute-done.12), channel_id=1, source_target_pairs={{0,4},{1,5},{2,6},{3,7},{4,12},{5,13},{6,14},{7,15},{12,8},{13,9},... | collective-permute-start | bytes 393224 | tf_op jit(solution)/shard_map/ppermute | solution.py:55
  50.6 17.0 %copy-start.4 = (bf16[64,1,4096]{2,0,1:T(8,128)(2,1)S(1)}, bf16[64,1,4096]{2,0,1:T(8,128)(2,1)}, u32[]{:S(2)}) copy-start(bf16[64,1,4096]{2,0,1:T(8,128)(2,1)} %param.10) | copy-start | bytes 1572868
  52.3 1.9 %collective-permute-start.22 = (bf16[128,2048]{1,0:T(8,128)(2,1)S(1)}, bf16[128,2048]{1,0:T(8,128)(2,1)S(1)}, u32[]{:S(2)}, u32[]{:S(2)}) collective-permute-start(bf16[128,2048]{1,0:T(8,128)(2,1)S(1)} %get-tuple-element.46), channel_id=1, source_target_pairs={{0,1},{1,0},{2,3},{3,2},{4,5},{5,4},{6,7},{7,6},{12,13},{13,12},{1... | collective-permute-start | bytes 1572872 | tf_op jit(solution)/shard_map/ppermute | solution.py:67
  52.5 9.7 %collective-permute-start.26 = (bf16[64,2048]{1,0:T(8,128)(2,1)S(1)}, bf16[64,2048]{1,0:T(8,128)(2,1)S(1)}, u32[]{:S(2)}, u32[]{:S(2)}) collective-permute-start(bf16[64,2048]{1,0:T(8,128)(2,1)S(1)} %add_convert_fusion.3), channel_id=1, source_target_pairs={{0,4},{1,5},{2,6},{3,7},{4,12},{5,13},{6,14},{7,15},{12,8},{13,9},... | collective-permute-start | bytes 786440 | tf_op jit(solution)/shard_map/ppermute | solution.py:55
  52.7 9.4 %collective-permute-start.28 = (bf16[1024,256]{1,0:T(8,128)(2,1)S(1)}, bf16[1024,256]{1,0:T(8,128)(2,1)S(1)}, u32[]{:S(2)}, u32[]{:S(2)}) collective-permute-start(bf16[1024,256]{1,0:T(8,128)(2,1)S(1)} %pad_maximum_fusion.refs_16_), channel_id=1, source_target_pairs={{0,1},{1,0},{2,3},{3,2},{4,5},{5,4},{6,7},{7,6},{12,13},{13,12},{1... | collective-permute-start | bytes 1572872 | tf_op jit(solution)/shard_map/ppermute | solution.py:67
  54.3 8.4 %collective-permute-start.25 = (bf16[64,2048]{1,0:T(8,128)(2,1)S(1)}, bf16[64,2048]{1,0:T(8,128)(2,1)S(1)}, u32[]{:S(2)}, u32[]{:S(2)}) collective-permute-start(bf16[64,2048]{1,0:T(8,128)(2,1)S(1)} %add_convert_fusion.5), channel_id=1, source_target_pairs={{0,2},{1,3},{2,0},{3,1},{4,6},{5,7},{6,4},{7,5},{12,14},{13,15},{1... | collective-permute-start | bytes 786440 | tf_op jit(solution)/shard_map/ppermute | solution.py:63
  55.3 4.5 %collective-permute-start.29 = (bf16[384,256]{1,0:T(8,128)(2,1)S(1)}, bf16[384,256]{1,0:T(8,128)(2,1)S(1)}, u32[]{:S(2)}, u32[]{:S(2)}) collective-permute-start(bf16[384,256]{1,0:T(8,128)(2,1)S(1)} %collective-permute-done.21.refs_17_), channel_id=1, source_target_pairs={{0,1},{1,0},{2,3},{3,2},{4,5},{5,4},{6,7},{7,6},{12,13},{13,12},{1... | collective-permute-start | bytes 589832 | tf_op jit(solution)/shard_map/ppermute | solution.py:67
  55.3 4.5 %collective-permute-start.27 = (bf16[128,256]{1,0:T(8,128)(2,1)S(1)}, bf16[128,256]{1,0:T(8,128)(2,1)S(1)}, u32[]{:S(2)}, u32[]{:S(2)}) collective-permute-start(bf16[128,256]{1,0:T(8,128)(2,1)S(1)} %bitcast.35), channel_id=1, source_target_pairs={{0,16},{16,0},{1,17},{17,1},{2,18},{18,2},{3,19},{19,3},{4,20},{20... | collective-permute-start | bytes 196616 | tf_op jit(solution)/shard_map/ppermute | solution.py:470
  59.8 3.7 %collective-permute-start.23 = (bf16[128,2048]{1,0:T(8,128)(2,1)S(1)}, bf16[128,2048]{1,0:T(8,128)(2,1)S(1)}, u32[]{:S(2)}, u32[]{:S(2)}) collective-permute-start(bf16[128,2048]{1,0:T(8,128)(2,1)S(1)} %get-tuple-element.47), channel_id=1, source_target_pairs={{0,1},{1,0},{2,3},{3,2},{4,5},{5,4},{6,7},{7,6},{12,13},{13,12},{1... | collective-permute-start | bytes 1572872 | tf_op jit(solution)/shard_map/ppermute | solution.py:67
  62.9 8.7 %collective-permute-start.30 = (bf16[64,2048]{1,0:T(8,128)(2,1)S(1)}, bf16[64,2048]{1,0:T(8,128)(2,1)S(1)}, u32[]{:S(2)}, u32[]{:S(2)}) collective-permute-start(bf16[64,2048]{1,0:T(8,128)(2,1)S(1)} %add_convert_fusion.2), channel_id=1, source_target_pairs={{0,4},{1,5},{2,6},{3,7},{4,12},{5,13},{6,14},{7,15},{12,8},{13,9},... | collective-permute-start | bytes 786440 | tf_op jit(solution)/shard_map/ppermute | solution.py:55
  63.6 7.9 %collective-permute-start.24 = (bf16[64,2048]{1,0:T(8,128)(2,1)S(1)}, bf16[64,2048]{1,0:T(8,128)(2,1)S(1)}, u32[]{:S(2)}, u32[]{:S(2)}) collective-permute-start(bf16[64,2048]{1,0:T(8,128)(2,1)S(1)} %add_convert_fusion.4), channel_id=1, source_target_pairs={{0,2},{1,3},{2,0},{3,1},{4,6},{5,7},{6,4},{7,5},{12,14},{13,15},{1... | collective-permute-start | bytes 786440 | tf_op jit(solution)/shard_map/ppermute | solution.py:63
  65.0 1.3 %collective-permute-start.31 = (bf16[128,256]{1,0:T(8,128)(2,1)S(1)}, bf16[128,256]{1,0:T(8,128)(2,1)S(1)}, u32[]{:S(2)}, u32[]{:S(2)}) collective-permute-start(bf16[128,256]{1,0:T(8,128)(2,1)S(1)} %collective-permute-done.27.refs_18_), channel_id=1, source_target_pairs={{0,1},{1,0},{2,3},{3,2},{4,5},{5,4},{6,7},{7,6},{12,13},{13,12},{1... | collective-permute-start | bytes 196616 | tf_op jit(solution)/shard_map/ppermute | solution.py:67
  67.6 14.1 %copy-start.7 = (bf16[64,1,2048]{2,0,1:T(8,128)(2,1)S(1)}, bf16[64,1,2048]{2,0,1:T(8,128)(2,1)}, u32[]{:S(2)}) copy-start(bf16[64,1,2048]{2,0,1:T(8,128)(2,1)} %param.9) | copy-start | bytes 786436
  71.7 9.1 %collective-permute-start.33 = (bf16[64,2048]{1,0:T(8,128)(2,1)S(1)}, bf16[64,2048]{1,0:T(8,128)(2,1)S(1)}, u32[]{:S(2)}, u32[]{:S(2)}) collective-permute-start(bf16[64,2048]{1,0:T(8,128)(2,1)S(1)} %add_convert_fusion.1), channel_id=1, source_target_pairs={{0,4},{1,5},{2,6},{3,7},{4,12},{5,13},{6,14},{7,15},{12,8},{13,9},... | collective-permute-start | bytes 786440 | tf_op jit(solution)/shard_map/ppermute | solution.py:55
  73.5 8.1 %collective-permute-start.32 = (bf16[64,2048]{1,0:T(8,128)(2,1)S(1)}, bf16[64,2048]{1,0:T(8,128)(2,1)S(1)}, u32[]{:S(2)}, u32[]{:S(2)}) collective-permute-start(bf16[64,2048]{1,0:T(8,128)(2,1)S(1)} %get-tuple-element.58), channel_id=1, source_target_pairs={{0,2},{1,3},{2,0},{3,1},{4,6},{5,7},{6,4},{7,5},{12,14},{13,15},{1... | collective-permute-start | bytes 786440 | tf_op jit(solution)/shard_map/ppermute | solution.py:63

commit v17 on v16

--- a/solution.py
+++ b/solution.py
@@ -507,15 +507,15 @@
     theirs = [None] * LINE
     experts(1, 0, [line[2], crossed[3]], [crossed[2], pairs[1], pairs[3]], False)
     theirs[1] = across(crossing[1])
-    near = swap_planes([pairs[0], pairs[1], pairs[3]])
-    send = experts(2, 3, [crossing[0], crossing[1]], [theirs[1], pairs[2], near], True)
+    send = experts(2, 3, [crossing[0], crossing[1]], [theirs[1], pairs[2]], True)
     total = summed(*mine[1], after(theirs[1], send))
     moving = forward(total)
     theirs[2], theirs[3] = across(crossing[2]), across(crossing[3])
-    far = swap_planes([after(pairs[2], total)])
-    own = after(jnp.concatenate([pairs[step] for step in order], axis=0), total)
-    smalls = [own, near, far, other_core(own), other_core(after(near, total)), other_core(far)]
-    total = summed(*mine[2], theirs[2], after(moving, far, *smalls[3:5]))
+    own = after(jnp.concatenate([pairs[step] for step in order], axis=0), crossing[2], total)
+    other = swap_planes([own])
+    swapped = other_core(other)
+    smalls = [own, other, other, other_core(own), swapped, swapped]
+    total = summed(*mine[2], theirs[2], after(moving, other, smalls[3]))
     moving = forward(total)
     theirs[0] = across(after(crossing[0], total))
     smalls[0] = after(own, total)

time: 82.8 us -> 82.6 us (level)
  starting transfers between devices: 30.4 us -> 28.9 us
  waiting for transfers between devices: 27.3 us -> 28.7 us
    ppermute x2 -> x1, waiting for transfers between devices: 3.02 us -> 5.06 us  [swap_planes(): lax.ppermute(shares.reshape(-1, both.shape[1]), 'grp', [(0, 1), (1, 0)])]
    ppermute x2 -> x1, starting transfers between devices: 3.04 us -> 1.57 us  [swap_planes(): lax.ppermute(shares.reshape(-1, both.shape[1]), 'grp', [(0, 1), (1, 0)])]
    ppermute x9, starting transfers between devices: 10.1 us -> 11.3 us  [across(): return lax.ppermute(x, 'seq', swaps(1, 0))]
    ppermute x7, starting transfers between devices: 12.1 us -> 11 us  [forward(): return lax.ppermute(x, 'seq', ring_steps(1))]
    ppermute x14 -> x13, waiting for transfers between devices: 3.97 us -> 3.36 us  [other_core(): return lax.ppermute(x, 'seq', swaps(0, 1))]
    ppermute x14 -> x13, starting transfers between devices: 2.46 us -> 2.26 us  [other_core(): return lax.ppermute(x, 'seq', swaps(0, 1))]
  transfers between devices with their start and end apart: 34 -> 32, of which waited for: 14 -> 13; matrix products, arithmetic and copies ran while one was open for 1% -> 1% of each run, Pallas kernels for 18% -> 18%
where the time goes in v17:
time: 82.6 us; the launch traced here: 82.3 us
  starting transfers between devices  28.9 us (35%)
  waiting for transfers between devices  28.7 us (35%)
  Pallas kernels  16.9 us (20%)
  local copies, waits for them, and re-layouts  5.55 us (7%)
  other arithmetic  1.54 us (2%)
    ppermute x7, waiting for transfers between devices, forward(): return lax.ppermute(x, 'seq', ring_steps(1))  15.6 us
    ppermute x9, starting transfers between devices, across(): return lax.ppermute(x, 'seq', swaps(1, 0))  11.3 us
    ppermute x7, starting transfers between devices, forward(): return lax.ppermute(x, 'seq', ring_steps(1))  11 us
    pallas_call x4, Pallas kernels, attend_part(): pl.pallas_call(functools.partial(attention_kernel, chunk), grid=(1,), out...  7.33 us
    pallas_call x2, Pallas kernels, run_experts(): pl.pallas_call(functools.partial(expert_kernel, top, tok_rows, capacity,...  6.36 us
    unnamed x16, local copies, waits for them, and re-layouts  5.54 us
    ppermute x1, waiting for transfers between devices, swap_planes(): lax.ppermute(shares.reshape(-1, both.shape[1]), 'grp', [(0, 1), (1, 0)])  5.06 us
    ppermute x13, waiting for transfers between devices, other_core(): return lax.ppermute(x, 'seq', swaps(0, 1))  3.36 us
  transfers between devices with their start and end apart: 32, of which 13 were waited for; matrix products, arithmetic and copies ran while one was open for 1% of the time, Pallas kernels for 18%

profile of v17, /device:TPU:0, one launch (start us, length us, event | category | flops | bytes accessed | tf_op | source)
XLA Modules:
  0.0 82.3 jit_solution(3295840522412227050)
XLA Ops:
  0.6 1.9 %normalize_and_pack.1 = (bf16[64,2176]{1,0:T(8,128)(2,1)}, bf16[128,256]{1,0:T(8,128)(2,1)}) custom-call(bf16[64,2048]{1,0:T(8,128)(2,1)} %bitcast.30, f32[1,2048]{1,0:T(1,128)} %bitcast.33, s32[4,64]{1,0:T(4,128)} %bitcast.34, f32[4,64]{1,0:T(4,128)} %bitcast.35, bf16[64,256]{1,0:T(8,128)(2,1)} %bitcast.32, bf16[128,256]{1,0:T(8,128)(2,1)} %weight_ref.1), custom_call_target="tpu_custom_call" | custom-call | flops 1 | bytes 1 | tf_op jit(solution)/shard_map/normalize_and_pack/pallas_call | solution.py:112
  2.5 0.5 collective-permute-start.1
  2.9 2.6 %collective-permute-start = (bf16[64,2176]{1,0:T(8,128)(2,1)}, bf16[64,2176]{1,0:T(8,128)(2,1)S(1)}, u32[]{:S(2)}, u32[]{:S(2)}) collective-permute-start(bf16[64,2176]{1,0:T(8,128)(2,1)} %get-tuple-element.29.refs_4_.refs_0_), channel_id=1, source_target_pairs={{0,4},{1,5},{2,6},{3,7},{4,12},{5,13},{6,14},{7,15},{12,8},{13,9},... | collective-permute-start | bytes 835592 | tf_op jit(solution)/shard_map/ppermute | solution.py:55
  5.5 1.5 %collective-permute-start.3 = (bf16[64,2176]{1,0:T(8,128)(2,1)}, bf16[64,2176]{1,0:T(8,128)(2,1)S(1)}, u32[]{:S(2)}, u32[]{:S(2)}) collective-permute-start(bf16[64,2176]{1,0:T(8,128)(2,1)} %get-tuple-element.29.refs_4_.refs_0_), channel_id=1, source_target_pairs={{0,2},{1,3},{2,0},{3,1},{4,6},{5,7},{6,4},{7,5},{12,14},{13,15},{1... | collective-permute-start | bytes 835592 | tf_op jit(solution)/shard_map/ppermute | solution.py:63
  7.0 0.0 collective-permute-done.1.refs_6_.refs_2_
  7.0 2.8 %copy-done = bf16[1,2048,1536]{2,1,0:T(8,128)(2,1)S(1)} copy-done((bf16[1,2048,1536]{2,1,0:T(8,128)(2,1)S(1)}, bf16[1,2048,1536]{2,1,0:T(8,128)(2,1)}, u32[]{:S(2)}) %copy-start) | copy-done | bytes 6291480
  9.8 1.9 %copy-done.2 = bf16[1,768,2048]{2,1,0:T(8,128)(2,1)S(1)} copy-done((bf16[1,768,2048]{2,1,0:T(8,128)(2,1)S(1)}, bf16[1,768,2048]{2,1,0:T(8,128)(2,1)}, u32[]{:S(2)}) %copy-start.2) | copy-done | bytes 3145752
  11.7 0.8 %copy-done.6 = bf16[128,256]{1,0:T(8,128)(2,1)S(1)} copy-done((bf16[128,256]{1,0:T(8,128)(2,1)S(1)}, bf16[128,256]{1,0:T(8,128)(2,1)}, u32[]{:S(2)}) %copy-start.6) | copy-done | bytes 65560
  12.6 0.6 collective-permute-start.2
  13.2 2.3 %collective-permute-start.5 = (bf16[64,2176]{1,0:T(8,128)(2,1)}, bf16[64,2176]{1,0:T(8,128)(2,1)S(1)}, u32[]{:S(2)}, u32[]{:S(2)}) collective-permute-start(bf16[64,2176]{1,0:T(8,128)(2,1)} %get-tuple-element.29.refs_4_.refs_0_), channel_id=1, source_target_pairs={{0,8},{1,9},{2,10},{3,11},{4,0},{5,1},{6,2},{7,3},{12,4},{13,5},{1... | collective-permute-start | bytes 835592 | tf_op jit(solution)/shard_map/ppermute | solution.py:59
  15.4 0.0 collective-permute-done.refs_0_.refs_4_
  15.4 0.6 collective-permute-start.7
  16.0 0.9 %collective-permute-done.2 = bf16[128,256]{1,0:T(8,128)(2,1)S(1)} collective-permute-done((bf16[128,256]{1,0:T(8,128)(2,1)S(1)}, bf16[128,256]{1,0:T(8,128)(2,1)S(1)}, u32[]{:S(2)}, u32[]{:S(2)}) %collective-permute-start.2) | collective-permute-done | bytes 65568 | tf_op jit(solution)/shard_map/ppermute | solution.py:63
  16.9 3.3 %collective-permute-start.4 = (bf16[64,2176]{1,0:T(8,128)(2,1)S(1)}, bf16[64,2176]{1,0:T(8,128)(2,1)S(1)}, u32[]{:S(2)}, u32[]{:S(2)}) collective-permute-start(bf16[64,2176]{1,0:T(8,128)(2,1)S(1)} %collective-permute-done.refs_0_.refs_4_), channel_id=1, source_target_pairs={{0,4},{1,5},{2,6},{3,7},{4,12},{5,13},{6,14},{7,15},{12,8},{13,9},... | collective-permute-start | bytes 835592 | tf_op jit(solution)/shard_map/ppermute | solution.py:55
  20.3 2.6 %collective-permute-done.5.refs_4_.refs_12_ = bf16[64,2176]{1,0:T(8,128)(2,1)S(1)} collective-permute-done((bf16[64,2176]{1,0:T(8,128)(2,1)}, bf16[64,2176]{1,0:T(8,128)(2,1)S(1)}, u32[]{:S(2)}, u32[]{:S(2)}) %collective-permute-start.5) | collective-permute-done | bytes 278560 | tf_op jit(solution)/shard_map/ppermute | solution.py:59
  22.8 1.2 %collective-permute-start.6 = (bf16[64,2176]{1,0:T(8,128)(2,1)S(1)}, bf16[64,2176]{1,0:T(8,128)(2,1)S(1)}, u32[]{:S(2)}, u32[]{:S(2)}) collective-permute-start(bf16[64,2176]{1,0:T(8,128)(2,1)S(1)} %collective-permute-done.5.refs_4_.refs_12_), channel_id=1, source_target_pairs={{0,2},{1,3},{2,0},{3,1},{4,6},{5,7},{6,4},{7,5},{12,14},{13,15},{1... | collective-permute-start | bytes 835592 | tf_op jit(solution)/shard_map/ppermute | solution.py:63
  24.1 0.5 collective-permute-start.10
  24.6 0.0 collective-permute-start.9
  24.6 5.9 %collective-permute-done.4.refs_0_.refs_8_ = bf16[64,2176]{1,0:T(8,128)(2,1)S(1)} collective-permute-done((bf16[64,2176]{1,0:T(8,128)(2,1)S(1)}, bf16[64,2176]{1,0:T(8,128)(2,1)S(1)}, u32[]{:S(2)}, u32[]{:S(2)}) %collective-permute-start.4) | collective-permute-done | bytes 278560 | tf_op jit(solution)/shard_map/ppermute | solution.py:55
  30.5 1.5 %collective-permute-start.11 = (bf16[64,2176]{1,0:T(8,128)(2,1)S(1)}, bf16[64,2176]{1,0:T(8,128)(2,1)S(1)}, u32[]{:S(2)}, u32[]{:S(2)}) collective-permute-start(bf16[64,2176]{1,0:T(8,128)(2,1)S(1)} %collective-permute-done.4.refs_0_.refs_8_), channel_id=1, source_target_pairs={{0,2},{1,3},{2,0},{3,1},{4,6},{5,7},{6,4},{7,5},{12,14},{13,15},{1... | collective-permute-start | bytes 835592 | tf_op jit(solution)/shard_map/ppermute | solution.py:63
  32.0 0.0 collective-permute-done.6.refs_5_.refs_13_
  32.0 2.5 %collective-permute-start.12 = (bf16[256,256]{1,0:T(8,128)(2,1)S(1)}, bf16[256,256]{1,0:T(8,128)(2,1)S(1)}, u32[]{:S(2)}, u32[]{:S(2)}) collective-permute-start(bf16[256,256]{1,0:T(8,128)(2,1)S(1)} %pad_maximum_fusion.1), channel_id=1, source_target_pairs={{0,4},{1,5},{2,6},{3,7},{4,12},{5,13},{6,14},{7,15},{12,8},{13,9},... | collective-permute-start | bytes 393224 | tf_op jit(solution)/shard_map/ppermute | solution.py:55
  34.5 0.4 collective-permute-start.13
  35.0 3.2 %experts.2 = (bf16[128,2048]{1,0:T(8,128)(2,1)S(1)}, bf16[128,2048]{1,0:T(8,128)(2,1)S(1)}, bf16[256,2048]{1,0:T(8,128)(2,1)S(1)}) custom-call(bf16[64,2176]{1,0:T(8,128)(2,1)S(1)} %collective-permute-done.refs_0_.refs_4_, bf16[64,2176]{1,0:T(8,128)(2,1)S(1)} %collective-permute-done.7.refs_1_.refs_5_, ...), custom_call_target="tpu_custom_call" | custom-call | flops 1 | bytes 1 | tf_op jit(solution)/shard_map/experts/pallas_call | solution.py:290
  38.2 2.7 %collective-permute-done.12 = bf16[256,256]{1,0:T(8,128)(2,1)S(1)} collective-permute-done((bf16[256,256]{1,0:T(8,128)(2,1)S(1)}, bf16[256,256]{1,0:T(8,128)(2,1)S(1)}, u32[]{:S(2)}, u32[]{:S(2)}) %collective-permute-start.12) | collective-permute-done | bytes 131104 | tf_op jit(solution)/shard_map/ppermute | solution.py:55
  40.9 0.0 collective-permute-done.13
  40.9 0.5 collective-permute-start.17
  41.4 0.1 collective-permute-start.18
  41.4 0.4 collective-permute-start.15
  41.9 0.1 collective-permute-start.16
  42.0 1.6 %collective-permute-done.14 = bf16[256,2048]{1,0:T(8,128)(2,1)S(1)} collective-permute-done((bf16[256,2048]{1,0:T(8,128)(2,1)S(1)}, bf16[256,2048]{1,0:T(8,128)(2,1)S(1)}, u32[]{:S(2)}, u32[]{:S(2)}) %collective-permute-start.14) | collective-permute-done | bytes 1048608 | tf_op jit(solution)/shard_map/ppermute | solution.py:67
  43.5 0.1 add_convert_fusion.7
  43.7 1.2 %collective-permute-start.19 = (bf16[64,2048]{1,0:T(8,128)(2,1)S(1)}, bf16[64,2048]{1,0:T(8,128)(2,1)S(1)}, u32[]{:S(2)}, u32[]{:S(2)}) collective-permute-start(bf16[64,2048]{1,0:T(8,128)(2,1)S(1)} %get-tuple-element.57), channel_id=1, source_target_pairs={{0,2},{1,3},{2,0},{3,1},{4,6},{5,7},{6,4},{7,5},{12,14},{13,15},{1... | collective-permute-start | bytes 786440 | tf_op jit(solution)/shard_map/ppermute | solution.py:63
  44.8 0.9 %collective-permute-start.20 = (bf16[256,256]{1,0:T(8,128)(2,1)S(1)}, bf16[256,256]{1,0:T(8,128)(2,1)S(1)}, u32[]{:S(2)}, u32[]{:S(2)}) collective-permute-start(bf16[256,256]{1,0:T(8,128)(2,1)S(1)} %collective-permute-done.12), channel_id=1, source_target_pairs={{0,4},{1,5},{2,6},{3,7},{4,12},{5,13},{6,14},{7,15},{12,8},{13,9},... | collective-permute-start | bytes 393224 | tf_op jit(solution)/shard_map/ppermute | solution.py:55
  45.8 3.2 %experts.3 = (bf16[128,2048]{1,0:T(8,128)(2,1)S(1)}, bf16[128,2048]{1,0:T(8,128)(2,1)S(1)}, bf16[128,2048]{1,0:T(8,128)(2,1)S(1)}, bf16[128,2048]{1,0:T(8,128)(2,1)S(1)}) custom-call(bf16[64,2176]{1,0:T(8,128)(2,1)S(1)} %collective-permute-done.4.refs_0_.refs_8_, bf16[64,2176]{1,0:T(8,128)(2,1)S(1)} %collective-permute-done.11.refs_1_.refs_9_, ...), custom_call_target="tpu_custom_call" | custom-call | flops 1 | bytes 1 | tf_op jit(solution)/shard_map/experts/pallas_call | solution.py:290
  48.9 0.0 copy-start.4
  48.9 2.0 %collective-permute-done.20 = bf16[256,256]{1,0:T(8,128)(2,1)S(1)} collective-permute-done((bf16[256,256]{1,0:T(8,128)(2,1)S(1)}, bf16[256,256]{1,0:T(8,128)(2,1)S(1)}, u32[]{:S(2)}, u32[]{:S(2)}) %collective-permute-start.20) | collective-permute-done | bytes 131104 | tf_op jit(solution)/shard_map/ppermute | solution.py:55
  51.0 1.1 %collective-permute-done.19 = bf16[64,2048]{1,0:T(8,128)(2,1)S(1)} collective-permute-done((bf16[64,2048]{1,0:T(8,128)(2,1)S(1)}, bf16[64,2048]{1,0:T(8,128)(2,1)S(1)}, u32[]{:S(2)}, u32[]{:S(2)}) %collective-permute-start.19) | collective-permute-done | bytes 262176 | tf_op jit(solution)/shard_map/ppermute | solution.py:63
  52.1 0.1 add_convert_fusion.3
  52.2 1.8 %collective-permute-done.21 = bf16[128,2048]{1,0:T(8,128)(2,1)S(1)} collective-permute-done((bf16[128,2048]{1,0:T(8,128)(2,1)S(1)}, bf16[128,2048]{1,0:T(8,128)(2,1)S(1)}, u32[]{:S(2)}, u32[]{:S(2)}) %collective-permute-start.21) | collective-permute-done | bytes 524320 | tf_op jit(solution)/shard_map/ppermute | solution.py:67
  54.0 0.1 add_convert_fusion.5
  54.0 0.2 collective-permute-start.27
  54.3 1.6 %collective-permute-start.26 = (bf16[512,256]{1,0:T(8,128)(2,1)S(1)}, bf16[512,256]{1,0:T(8,128)(2,1)S(1)}, u32[]{:S(2)}, u32[]{:S(2)}) collective-permute-start(bf16[512,256]{1,0:T(8,128)(2,1)S(1)} %bitcast.31), channel_id=1, source_target_pairs={{0,16},{16,0},{1,17},{17,1},{2,18},{18,2},{3,19},{19,3},{4,20},{20... | collective-permute-start | bytes 786440 | tf_op jit(solution)/shard_map/ppermute | solution.py:470
  55.8 0.3 collective-permute-start.25
  56.1 1.7 %collective-permute-start.24 = (bf16[64,2048]{1,0:T(8,128)(2,1)S(1)}, bf16[64,2048]{1,0:T(8,128)(2,1)S(1)}, u32[]{:S(2)}, u32[]{:S(2)}) collective-permute-start(bf16[64,2048]{1,0:T(8,128)(2,1)S(1)} %add_convert_fusion.5), channel_id=1, source_target_pairs={{0,2},{1,3},{2,0},{3,1},{4,6},{5,7},{6,4},{7,5},{12,14},{13,15},{1... | collective-permute-start | bytes 786440 | tf_op jit(solution)/shard_map/ppermute | solution.py:63
  57.9 5.1 %collective-permute-done.26.refs_17_.refs_18_ = bf16[512,256]{1,0:T(8,128)(2,1)S(1)} collective-permute-done((bf16[512,256]{1,0:T(8,128)(2,1)S(1)}, bf16[512,256]{1,0:T(8,128)(2,1)S(1)}, u32[]{:S(2)}, u32[]{:S(2)}) %collective-permute-start.26) | collective-permute-done | bytes 262176 | tf_op jit(solution)/shard_map/ppermute | solution.py:470
  62.9 2.1 %collective-permute-done.25 = bf16[64,2048]{1,0:T(8,128)(2,1)S(1)} collective-permute-done((bf16[64,2048]{1,0:T(8,128)(2,1)S(1)}, bf16[64,2048]{1,0:T(8,128)(2,1)S(1)}, u32[]{:S(2)}, u32[]{:S(2)}) %collective-permute-start.25) | collective-permute-done | bytes 262176 | tf_op jit(solution)/shard_map/ppermute | solution.py:55
  65.0 0.1 add_convert_fusion.2
  65.2 0.2 collective-permute-start.28
  65.4 0.1 add_convert_fusion.4
  65.5 1.2 %collective-permute-start.23 = (bf16[64,2048]{1,0:T(8,128)(2,1)S(1)}, bf16[64,2048]{1,0:T(8,128)(2,1)S(1)}, u32[]{:S(2)}, u32[]{:S(2)}) collective-permute-start(bf16[64,2048]{1,0:T(8,128)(2,1)S(1)} %add_convert_fusion.4), channel_id=1, source_target_pairs={{0,2},{1,3},{2,0},{3,1},{4,6},{5,7},{6,4},{7,5},{12,14},{13,15},{1... | collective-permute-start | bytes 786440 | tf_op jit(solution)/shard_map/ppermute | solution.py:63
  66.8 1.3 %values.1 = (bf16[1024,256]{1,0:T(8,128)(2,1)S(1)}, bf16[1024,256]{1,0:T(8,128)(2,1)S(1)}) custom-call(bf16[64,2176]{1,0:T(8,128)(2,1)S(1)} %copy-done.5, bf16[64,2176]{1,0:T(8,128)(2,1)S(1)} %collective-permute-done.3.refs_5_.refs_1_, bf16[64,2176]{1,0:T(8,128)(2,1)S(1)} %collective-permute-done.1.refs_6_.refs_2_, ...), custom_call_target="tpu_custom_call" | custom-call | flops 1 | bytes 1 | tf_op jit(solution)/shard_map/values/pallas_call | solution.py:333
  68.1 0.0 copy-start.7
  68.1 1.8 %attention.4.refs_0_ = bf16[64,4096]{1,0:T(8,128)(2,1)} custom-call(bf16[64,4096]{1,0:T(8,128)(2,1)S(1)} %bitcast.24, bf16[1024,256]{1,0:T(8,128)(2,1)S(1)} %get-tuple-element.50.k_ref, bf16[1024,256]{1,0:T(8,128)(2,1)S(1)} %get-tuple-element.51.v_ref), custom_call_target="tpu_custom_call" | custom-call | flops 1 | bytes 1 | tf_op jit(solution)/shard_map/attention/pallas_call | solution.py:415
  70.0 1.8 %attention.5.refs_0_ = bf16[64,4096]{1,0:T(8,128)(2,1)} custom-call(bf16[64,4096]{1,0:T(8,128)(2,1)S(1)} %bitcast.25, bf16[1024,256]{1,0:T(8,128)(2,1)S(1)} %get-tuple-element.50.k_ref, bf16[1024,256]{1,0:T(8,128)(2,1)S(1)} %get-tuple-element.51.v_ref, bf16[64,4096]{1,0:T(8,128)(2,1)} %attention.4.refs_0_), custom_call_target="tpu_custom_call", output_to_operand_aliasing={{}: (3, {})} | custom-call | flops 1 | bytes 1 | tf_op jit(solution)/shard_map/attention/pallas_call | solution.py:415
  71.8 2.0 %collective-permute-done.28 = bf16[64,2048]{1,0:T(8,128)(2,1)S(1)} collective-permute-done((bf16[64,2048]{1,0:T(8,128)(2,1)S(1)}, bf16[64,2048]{1,0:T(8,128)(2,1)S(1)}, u32[]{:S(2)}, u32[]{:S(2)}) %collective-permute-start.28) | collective-permute-done | bytes 262176 | tf_op jit(solution)/shard_map/ppermute | solution.py:55
  73.8 0.1 add_convert_fusion.1
  73.9 1.2 %collective-permute-start.31 = (bf16[64,2048]{1,0:T(8,128)(2,1)S(1)}, bf16[64,2048]{1,0:T(8,128)(2,1)S(1)}, u32[]{:S(2)}, u32[]{:S(2)}) collective-permute-start(bf16[64,2048]{1,0:T(8,128)(2,1)S(1)} %add_convert_fusion.1), channel_id=1, source_target_pairs={{0,4},{1,5},{2,6},{3,7},{4,12},{5,13},{6,14},{7,15},{12,8},{13,9},... | collective-permute-start | bytes 786440 | tf_op jit(solution)/shard_map/ppermute | solution.py:55
  75.1 1.7 %collective-permute-start.30 = (bf16[64,2048]{1,0:T(8,128)(2,1)S(1)}, bf16[64,2048]{1,0:T(8,128)(2,1)S(1)}, u32[]{:S(2)}, u32[]{:S(2)}) collective-permute-start(bf16[64,2048]{1,0:T(8,128)(2,1)S(1)} %get-tuple-element.54), channel_id=1, source_target_pairs={{0,2},{1,3},{2,0},{3,1},{4,6},{5,7},{6,4},{7,5},{12,14},{13,15},{1... | collective-permute-start | bytes 786440 | tf_op jit(solution)/shard_map/ppermute | solution.py:63
  76.8 1.8 %attention.6.refs_0_ = bf16[64,4096]{1,0:T(8,128)(2,1)} custom-call(bf16[64,4096]{1,0:T(8,128)(2,1)S(1)} %bitcast.26, bf16[1024,256]{1,0:T(8,128)(2,1)S(1)} %get-tuple-element.50.k_ref, bf16[1024,256]{1,0:T(8,128)(2,1)S(1)} %get-tuple-element.51.v_ref, bf16[64,4096]{1,0:T(8,128)(2,1)} %attention.5.refs_0_), custom_call_target="tpu_custom_call", output_to_operand_aliasing={{}: (3, {})} | custom-call | flops 1 | bytes 1 | tf_op jit(solution)/shard_map/attention/pallas_call | solution.py:415
  78.7 1.8 %attention.7 = bf16[64,4096]{1,0:T(8,128)(2,1)} custom-call(bf16[64,4096]{1,0:T(8,128)(2,1)S(1)} %bitcast.27, bf16[1024,256]{1,0:T(8,128)(2,1)S(1)} %get-tuple-element.50.k_ref, bf16[1024,256]{1,0:T(8,128)(2,1)S(1)} %get-tuple-element.51.v_ref, bf16[64,4096]{1,0:T(8,128)(2,1)} %attention.6.refs_0_), custom_call_target="tpu_custom_call", output_to_operand_aliasing={{}: (3, {})} | custom-call | flops 1 | bytes 1 | tf_op jit(solution)/shard_map/attention/pallas_call | solution.py:415
  80.5 0.9 %collective-permute-done.31 = bf16[64,2048]{1,0:T(8,128)(2,1)S(1)} collective-permute-done((bf16[64,2048]{1,0:T(8,128)(2,1)S(1)}, bf16[64,2048]{1,0:T(8,128)(2,1)S(1)}, u32[]{:S(2)}, u32[]{:S(2)}) %collective-permute-start.31) | collective-permute-done | bytes 262176 | tf_op jit(solution)/shard_map/ppermute | solution.py:55
  81.4 0.1 collective-permute-done.30
  81.5 0.9 %fusion = bf16[64,1,2048]{2,0,1:T(8,128)(2,1)} fusion(bf16[64,2048]{1,0:T(8,128)(2,1)S(1)} %collective-permute-done.31, bf16[64,2048]{1,0:T(8,128)(2,1)S(1)} %collective-permute-done.30, bf16[256,2048]{1,0:T(8,128)(2,1)S(1)} %collective-permute-done.14, bf16[128,2048]{1,0:T(8,128)(2,1)S(1)} %get-tuple-element.34, bf16[64,1,2048]{2,0,1:T(8,128)(2,1)S(1)} %copy-done.7), kind=kLoop, calls=%fused_computation.9 | loop fusion | flops 1310720 | bytes 1572864 | tf_op jit(solution)/shard_map/reshape | solution.py:585
  (35 shorter events, 0.1 us)
Async XLA Ops:
  2.5 4.6 %collective-permute-start.1 = (bf16[64,2176]{1,0:T(8,128)(2,1)}, bf16[64,2176]{1,0:T(8,128)(2,1)S(1)}, u32[]{:S(2)}, u32[]{:S(2)}) collective-permute-start(bf16[64,2176]{1,0:T(8,128)(2,1)} %get-tuple-element.29.refs_4_.refs_0_), channel_id=1, source_target_pairs={{0,1},{1,0},{2,3},{3,2},{4,5},{5,4},{6,7},{7,6},{12,13},{13,12},{1... | collective-permute-start | bytes 835592 | tf_op jit(solution)/shard_map/ppermute | solution.py:67
  2.9 12.5 %collective-permute-start = (bf16[64,2176]{1,0:T(8,128)(2,1)}, bf16[64,2176]{1,0:T(8,128)(2,1)S(1)}, u32[]{:S(2)}, u32[]{:S(2)}) collective-permute-start(bf16[64,2176]{1,0:T(8,128)(2,1)} %get-tuple-element.29.refs_4_.refs_0_), channel_id=1, source_target_pairs={{0,4},{1,5},{2,6},{3,7},{4,12},{5,13},{6,14},{7,15},{12,8},{13,9},... | collective-permute-start | bytes 835592 | tf_op jit(solution)/shard_map/ppermute | solution.py:55
  5.5 11.4 %collective-permute-start.3 = (bf16[64,2176]{1,0:T(8,128)(2,1)}, bf16[64,2176]{1,0:T(8,128)(2,1)S(1)}, u32[]{:S(2)}, u32[]{:S(2)}) collective-permute-start(bf16[64,2176]{1,0:T(8,128)(2,1)} %get-tuple-element.29.refs_4_.refs_0_), channel_id=1, source_target_pairs={{0,2},{1,3},{2,0},{3,1},{4,6},{5,7},{6,4},{7,5},{12,14},{13,15},{1... | collective-permute-start | bytes 835592 | tf_op jit(solution)/shard_map/ppermute | solution.py:63
  7.0 2.8 %copy-start = (bf16[1,2048,1536]{2,1,0:T(8,128)(2,1)S(1)}, bf16[1,2048,1536]{2,1,0:T(8,128)(2,1)}, u32[]{:S(2)}) copy-start(bf16[1,2048,1536]{2,1,0:T(8,128)(2,1)} %param.16) | copy-start | bytes 18874372
  9.8 1.9 %copy-start.2 = (bf16[1,768,2048]{2,1,0:T(8,128)(2,1)S(1)}, bf16[1,768,2048]{2,1,0:T(8,128)(2,1)}, u32[]{:S(2)}) copy-start(bf16[1,768,2048]{2,1,0:T(8,128)(2,1)} %param.17) | copy-start | bytes 9437188
  11.7 0.8 %copy-start.6 = (bf16[128,256]{1,0:T(8,128)(2,1)S(1)}, bf16[128,256]{1,0:T(8,128)(2,1)}, u32[]{:S(2)}) copy-start(bf16[128,256]{1,0:T(8,128)(2,1)} %get-tuple-element.31.small_ref) | copy-start | bytes 196612
  12.6 22.4 %copy-start.1 = (bf16[1,2048,1536]{2,1,0:T(8,128)(2,1)S(1)}, bf16[1,2048,1536]{2,1,0:T(8,128)(2,1)}, u32[]{:S(2)}) copy-start(bf16[1,2048,1536]{2,1,0:T(8,128)(2,1)} %param.16) | copy-start | bytes 18874372
  12.6 22.4 %copy-start.3 = (bf16[1,768,2048]{2,1,0:T(8,128)(2,1)S(1)}, bf16[1,768,2048]{2,1,0:T(8,128)(2,1)}, u32[]{:S(2)}) copy-start(bf16[1,768,2048]{2,1,0:T(8,128)(2,1)} %param.17) | copy-start | bytes 9437188
  12.6 22.4 %copy-start.5 = (bf16[64,2176]{1,0:T(8,128)(2,1)S(1)}, bf16[64,2176]{1,0:T(8,128)(2,1)}, u32[]{:S(2)}) copy-start(bf16[64,2176]{1,0:T(8,128)(2,1)} %get-tuple-element.29.refs_4_.refs_0_) | copy-start | bytes 835588
  12.6 4.3 %collective-permute-start.2 = (bf16[128,256]{1,0:T(8,128)(2,1)S(1)}, bf16[128,256]{1,0:T(8,128)(2,1)S(1)}, u32[]{:S(2)}, u32[]{:S(2)}) collective-permute-start(bf16[128,256]{1,0:T(8,128)(2,1)S(1)} %hold_weights.1), channel_id=1, source_target_pairs={{0,2},{1,3},{2,0},{3,1},{4,6},{5,7},{6,4},{7,5},{12,14},{13,15},{1... | collective-permute-start | bytes 196616 | tf_op jit(solution)/shard_map/ppermute | solution.py:63
  13.2 9.7 %collective-permute-start.5 = (bf16[64,2176]{1,0:T(8,128)(2,1)}, bf16[64,2176]{1,0:T(8,128)(2,1)S(1)}, u32[]{:S(2)}, u32[]{:S(2)}) collective-permute-start(bf16[64,2176]{1,0:T(8,128)(2,1)} %get-tuple-element.29.refs_4_.refs_0_), channel_id=1, source_target_pairs={{0,8},{1,9},{2,10},{3,11},{4,0},{5,1},{6,2},{7,3},{12,4},{13,5},{1... | collective-permute-start | bytes 835592 | tf_op jit(solution)/shard_map/ppermute | solution.py:59
  15.4 9.1 %collective-permute-start.7 = (bf16[64,2176]{1,0:T(8,128)(2,1)S(1)}, bf16[64,2176]{1,0:T(8,128)(2,1)S(1)}, u32[]{:S(2)}, u32[]{:S(2)}) collective-permute-start(bf16[64,2176]{1,0:T(8,128)(2,1)S(1)} %collective-permute-done.refs_0_.refs_4_), channel_id=1, source_target_pairs={{0,2},{1,3},{2,0},{3,1},{4,6},{5,7},{6,4},{7,5},{12,14},{13,15},{1... | collective-permute-start | bytes 835592 | tf_op jit(solution)/shard_map/ppermute | solution.py:63
  16.9 13.5 %collective-permute-start.4 = (bf16[64,2176]{1,0:T(8,128)(2,1)S(1)}, bf16[64,2176]{1,0:T(8,128)(2,1)S(1)}, u32[]{:S(2)}, u32[]{:S(2)}) collective-permute-start(bf16[64,2176]{1,0:T(8,128)(2,1)S(1)} %collective-permute-done.refs_0_.refs_4_), channel_id=1, source_target_pairs={{0,4},{1,5},{2,6},{3,7},{4,12},{5,13},{6,14},{7,15},{12,8},{13,9},... | collective-permute-start | bytes 835592 | tf_op jit(solution)/shard_map/ppermute | solution.py:55
  22.8 9.2 %collective-permute-start.6 = (bf16[64,2176]{1,0:T(8,128)(2,1)S(1)}, bf16[64,2176]{1,0:T(8,128)(2,1)S(1)}, u32[]{:S(2)}, u32[]{:S(2)}) collective-permute-start(bf16[64,2176]{1,0:T(8,128)(2,1)S(1)} %collective-permute-done.5.refs_4_.refs_12_), channel_id=1, source_target_pairs={{0,2},{1,3},{2,0},{3,1},{4,6},{5,7},{6,4},{7,5},{12,14},{13,15},{1... | collective-permute-start | bytes 835592 | tf_op jit(solution)/shard_map/ppermute | solution.py:63
  24.1 10.5 %collective-permute-start.8 = (bf16[64,2176]{1,0:T(8,128)(2,1)S(1)}, bf16[64,2176]{1,0:T(8,128)(2,1)S(1)}, u32[]{:S(2)}, u32[]{:S(2)}) collective-permute-start(bf16[64,2176]{1,0:T(8,128)(2,1)S(1)} %collective-permute-done.refs_0_.refs_4_), channel_id=1, source_target_pairs={{0,1},{1,0},{2,3},{3,2},{4,5},{5,4},{6,7},{7,6},{12,13},{13,12},{1... | collective-permute-start | bytes 835592 | tf_op jit(solution)/shard_map/ppermute | solution.py:67
  24.1 10.9 %collective-permute-start.10 = (bf16[64,2176]{1,0:T(8,128)(2,1)S(1)}, bf16[64,2176]{1,0:T(8,128)(2,1)S(1)}, u32[]{:S(2)}, u32[]{:S(2)}) collective-permute-start(bf16[64,2176]{1,0:T(8,128)(2,1)S(1)} %collective-permute-done.3.refs_5_.refs_1_), channel_id=1, source_target_pairs={{0,1},{1,0},{2,3},{3,2},{4,5},{5,4},{6,7},{7,6},{12,13},{13,12},{1... | collective-permute-start | bytes 835592 | tf_op jit(solution)/shard_map/ppermute | solution.py:67
  24.6 10.4 %collective-permute-start.9 = (bf16[64,2176]{1,0:T(8,128)(2,1)S(1)}, bf16[64,2176]{1,0:T(8,128)(2,1)S(1)}, u32[]{:S(2)}, u32[]{:S(2)}) collective-permute-start(bf16[64,2176]{1,0:T(8,128)(2,1)S(1)} %collective-permute-done.7.refs_1_.refs_5_), channel_id=1, source_target_pairs={{0,1},{1,0},{2,3},{3,2},{4,5},{5,4},{6,7},{7,6},{12,13},{13,12},{1... | collective-permute-start | bytes 835592 | tf_op jit(solution)/shard_map/ppermute | solution.py:67
  30.5 10.4 %collective-permute-start.11 = (bf16[64,2176]{1,0:T(8,128)(2,1)S(1)}, bf16[64,2176]{1,0:T(8,128)(2,1)S(1)}, u32[]{:S(2)}, u32[]{:S(2)}) collective-permute-start(bf16[64,2176]{1,0:T(8,128)(2,1)S(1)} %collective-permute-done.4.refs_0_.refs_8_), channel_id=1, source_target_pairs={{0,2},{1,3},{2,0},{3,1},{4,6},{5,7},{6,4},{7,5},{12,14},{13,15},{1... | collective-permute-start | bytes 835592 | tf_op jit(solution)/shard_map/ppermute | solution.py:63
  32.0 8.8 %collective-permute-start.12 = (bf16[256,256]{1,0:T(8,128)(2,1)S(1)}, bf16[256,256]{1,0:T(8,128)(2,1)S(1)}, u32[]{:S(2)}, u32[]{:S(2)}) collective-permute-start(bf16[256,256]{1,0:T(8,128)(2,1)S(1)} %pad_maximum_fusion.1), channel_id=1, source_target_pairs={{0,4},{1,5},{2,6},{3,7},{4,12},{5,13},{6,14},{7,15},{12,8},{13,9},... | collective-permute-start | bytes 393224 | tf_op jit(solution)/shard_map/ppermute | solution.py:55
  34.5 6.3 %collective-permute-start.13 = (bf16[256,256]{1,0:T(8,128)(2,1)S(1)}, bf16[256,256]{1,0:T(8,128)(2,1)S(1)}, u32[]{:S(2)}, u32[]{:S(2)}) collective-permute-start(bf16[256,256]{1,0:T(8,128)(2,1)S(1)} %pad_maximum_fusion.1), channel_id=1, source_target_pairs={{0,8},{1,9},{2,10},{3,11},{4,0},{5,1},{6,2},{7,3},{12,4},{13,5},{1... | collective-permute-start | bytes 393224 | tf_op jit(solution)/shard_map/ppermute | solution.py:59
  40.9 2.7 %collective-permute-start.14 = (bf16[256,2048]{1,0:T(8,128)(2,1)S(1)}, bf16[256,2048]{1,0:T(8,128)(2,1)S(1)}, u32[]{:S(2)}, u32[]{:S(2)}) collective-permute-start(bf16[256,2048]{1,0:T(8,128)(2,1)S(1)} %get-tuple-element.37), channel_id=1, source_target_pairs={{0,1},{1,0},{2,3},{3,2},{4,5},{5,4},{6,7},{7,6},{12,13},{13,12},{1... | collective-permute-start | bytes 3145736 | tf_op jit(solution)/shard_map/ppermute | solution.py:67
  40.9 4.0 %collective-permute-start.17 = (bf16[64,2176]{1,0:T(8,128)(2,1)S(1)}, bf16[64,2176]{1,0:T(8,128)(2,1)S(1)}, u32[]{:S(2)}, u32[]{:S(2)}) collective-permute-start(bf16[64,2176]{1,0:T(8,128)(2,1)S(1)} %collective-permute-done.5.refs_4_.refs_12_), channel_id=1, source_target_pairs={{0,1},{1,0},{2,3},{3,2},{4,5},{5,4},{6,7},{7,6},{12,13},{13,12},{1... | collective-permute-start | bytes 835592 | tf_op jit(solution)/shard_map/ppermute | solution.py:67
  41.4 4.4 %collective-permute-start.18 = (bf16[64,2176]{1,0:T(8,128)(2,1)S(1)}, bf16[64,2176]{1,0:T(8,128)(2,1)S(1)}, u32[]{:S(2)}, u32[]{:S(2)}) collective-permute-start(bf16[64,2176]{1,0:T(8,128)(2,1)S(1)} %collective-permute-done.6.refs_5_.refs_13_), channel_id=1, source_target_pairs={{0,1},{1,0},{2,3},{3,2},{4,5},{5,4},{6,7},{7,6},{12,13},{13,12},{1... | collective-permute-start | bytes 835592 | tf_op jit(solution)/shard_map/ppermute | solution.py:67
  41.4 4.3 %collective-permute-start.15 = (bf16[64,2176]{1,0:T(8,128)(2,1)S(1)}, bf16[64,2176]{1,0:T(8,128)(2,1)S(1)}, u32[]{:S(2)}, u32[]{:S(2)}) collective-permute-start(bf16[64,2176]{1,0:T(8,128)(2,1)S(1)} %collective-permute-done.4.refs_0_.refs_8_), channel_id=1, source_target_pairs={{0,1},{1,0},{2,3},{3,2},{4,5},{5,4},{6,7},{7,6},{12,13},{13,12},{1... | collective-permute-start | bytes 835592 | tf_op jit(solution)/shard_map/ppermute | solution.py:67
  41.9 3.9 %collective-permute-start.16 = (bf16[64,2176]{1,0:T(8,128)(2,1)S(1)}, bf16[64,2176]{1,0:T(8,128)(2,1)S(1)}, u32[]{:S(2)}, u32[]{:S(2)}) collective-permute-start(bf16[64,2176]{1,0:T(8,128)(2,1)S(1)} %collective-permute-done.11.refs_1_.refs_9_), channel_id=1, source_target_pairs={{0,1},{1,0},{2,3},{3,2},{4,5},{5,4},{6,7},{7,6},{12,13},{13,12},{1... | collective-permute-start | bytes 835592 | tf_op jit(solution)/shard_map/ppermute | solution.py:67
  43.7 8.4 %collective-permute-start.19 = (bf16[64,2048]{1,0:T(8,128)(2,1)S(1)}, bf16[64,2048]{1,0:T(8,128)(2,1)S(1)}, u32[]{:S(2)}, u32[]{:S(2)}) collective-permute-start(bf16[64,2048]{1,0:T(8,128)(2,1)S(1)} %get-tuple-element.57), channel_id=1, source_target_pairs={{0,2},{1,3},{2,0},{3,1},{4,6},{5,7},{6,4},{7,5},{12,14},{13,15},{1... | collective-permute-start | bytes 786440 | tf_op jit(solution)/shard_map/ppermute | solution.py:63
  44.8 6.2 %collective-permute-start.20 = (bf16[256,256]{1,0:T(8,128)(2,1)S(1)}, bf16[256,256]{1,0:T(8,128)(2,1)S(1)}, u32[]{:S(2)}, u32[]{:S(2)}) collective-permute-start(bf16[256,256]{1,0:T(8,128)(2,1)S(1)} %collective-permute-done.12), channel_id=1, source_target_pairs={{0,4},{1,5},{2,6},{3,7},{4,12},{5,13},{6,14},{7,15},{12,8},{13,9},... | collective-permute-start | bytes 393224 | tf_op jit(solution)/shard_map/ppermute | solution.py:55
  48.9 19.2 %copy-start.4 = (bf16[64,1,4096]{2,0,1:T(8,128)(2,1)S(1)}, bf16[64,1,4096]{2,0,1:T(8,128)(2,1)}, u32[]{:S(2)}) copy-start(bf16[64,1,4096]{2,0,1:T(8,128)(2,1)} %param.10) | copy-start | bytes 1572868
  52.1 1.9 %collective-permute-start.21 = (bf16[128,2048]{1,0:T(8,128)(2,1)S(1)}, bf16[128,2048]{1,0:T(8,128)(2,1)S(1)}, u32[]{:S(2)}, u32[]{:S(2)}) collective-permute-start(bf16[128,2048]{1,0:T(8,128)(2,1)S(1)} %get-tuple-element.44), channel_id=1, source_target_pairs={{0,1},{1,0},{2,3},{3,2},{4,5},{5,4},{6,7},{7,6},{12,13},{13,12},{1... | collective-permute-start | bytes 1572872 | tf_op jit(solution)/shard_map/ppermute | solution.py:67
  54.0 11.0 %collective-permute-start.27 = (bf16[1024,256]{1,0:T(8,128)(2,1)S(1)}, bf16[1024,256]{1,0:T(8,128)(2,1)S(1)}, u32[]{:S(2)}, u32[]{:S(2)}) collective-permute-start(bf16[1024,256]{1,0:T(8,128)(2,1)S(1)} %pad_maximum_fusion.refs_16_), channel_id=1, source_target_pairs={{0,1},{1,0},{2,3},{3,2},{4,5},{5,4},{6,7},{7,6},{12,13},{13,12},{1... | collective-permute-start | bytes 1572872 | tf_op jit(solution)/shard_map/ppermute | solution.py:67
  54.3 8.7 %collective-permute-start.26 = (bf16[512,256]{1,0:T(8,128)(2,1)S(1)}, bf16[512,256]{1,0:T(8,128)(2,1)S(1)}, u32[]{:S(2)}, u32[]{:S(2)}) collective-permute-start(bf16[512,256]{1,0:T(8,128)(2,1)S(1)} %bitcast.31), channel_id=1, source_target_pairs={{0,16},{16,0},{1,17},{17,1},{2,18},{18,2},{3,19},{19,3},{4,20},{20... | collective-permute-start | bytes 786440 | tf_op jit(solution)/shard_map/ppermute | solution.py:470
  55.8 9.2 %collective-permute-start.25 = (bf16[64,2048]{1,0:T(8,128)(2,1)S(1)}, bf16[64,2048]{1,0:T(8,128)(2,1)S(1)}, u32[]{:S(2)}, u32[]{:S(2)}) collective-permute-start(bf16[64,2048]{1,0:T(8,128)(2,1)S(1)} %add_convert_fusion.3), channel_id=1, source_target_pairs={{0,4},{1,5},{2,6},{3,7},{4,12},{5,13},{6,14},{7,15},{12,8},{13,9},... | collective-permute-start | bytes 786440 | tf_op jit(solution)/shard_map/ppermute | solution.py:55
  56.1 8.9 %collective-permute-start.24 = (bf16[64,2048]{1,0:T(8,128)(2,1)S(1)}, bf16[64,2048]{1,0:T(8,128)(2,1)S(1)}, u32[]{:S(2)}, u32[]{:S(2)}) collective-permute-start(bf16[64,2048]{1,0:T(8,128)(2,1)S(1)} %add_convert_fusion.5), channel_id=1, source_target_pairs={{0,2},{1,3},{2,0},{3,1},{4,6},{5,7},{6,4},{7,5},{12,14},{13,15},{1... | collective-permute-start | bytes 786440 | tf_op jit(solution)/shard_map/ppermute | solution.py:63
  57.9 7.6 %collective-permute-start.22 = (bf16[128,2048]{1,0:T(8,128)(2,1)S(1)}, bf16[128,2048]{1,0:T(8,128)(2,1)S(1)}, u32[]{:S(2)}, u32[]{:S(2)}) collective-permute-start(bf16[128,2048]{1,0:T(8,128)(2,1)S(1)} %get-tuple-element.45), channel_id=1, source_target_pairs={{0,1},{1,0},{2,3},{3,2},{4,5},{5,4},{6,7},{7,6},{12,13},{13,12},{1... | collective-permute-start | bytes 1572872 | tf_op jit(solution)/shard_map/ppermute | solution.py:67
  62.9 3.8 %collective-permute-start.29 = (bf16[512,256]{1,0:T(8,128)(2,1)S(1)}, bf16[512,256]{1,0:T(8,128)(2,1)S(1)}, u32[]{:S(2)}, u32[]{:S(2)}) collective-permute-start(bf16[512,256]{1,0:T(8,128)(2,1)S(1)} %collective-permute-done.26.refs_17_.refs_18_), channel_id=1, source_target_pairs={{0,1},{1,0},{2,3},{3,2},{4,5},{5,4},{6,7},{7,6},{12,13},{13,12},{1... | collective-permute-start | bytes 786440 | tf_op jit(solution)/shard_map/ppermute | solution.py:67
  65.2 8.6 %collective-permute-start.28 = (bf16[64,2048]{1,0:T(8,128)(2,1)S(1)}, bf16[64,2048]{1,0:T(8,128)(2,1)S(1)}, u32[]{:S(2)}, u32[]{:S(2)}) collective-permute-start(bf16[64,2048]{1,0:T(8,128)(2,1)S(1)} %add_convert_fusion.2), channel_id=1, source_target_pairs={{0,4},{1,5},{2,6},{3,7},{4,12},{5,13},{6,14},{7,15},{12,8},{13,9},... | collective-permute-start | bytes 786440 | tf_op jit(solution)/shard_map/ppermute | solution.py:55
  65.5 8.3 %collective-permute-start.23 = (bf16[64,2048]{1,0:T(8,128)(2,1)S(1)}, bf16[64,2048]{1,0:T(8,128)(2,1)S(1)}, u32[]{:S(2)}, u32[]{:S(2)}) collective-permute-start(bf16[64,2048]{1,0:T(8,128)(2,1)S(1)} %add_convert_fusion.4), channel_id=1, source_target_pairs={{0,2},{1,3},{2,0},{3,1},{4,6},{5,7},{6,4},{7,5},{12,14},{13,15},{1... | collective-permute-start | bytes 786440 | tf_op jit(solution)/shard_map/ppermute | solution.py:63
  68.1 13.4 %copy-start.7 = (bf16[64,1,2048]{2,0,1:T(8,128)(2,1)S(1)}, bf16[64,1,2048]{2,0,1:T(8,128)(2,1)}, u32[]{:S(2)}) copy-start(bf16[64,1,2048]{2,0,1:T(8,128)(2,1)} %param.9) | copy-start | bytes 786436
  73.9 7.5 %collective-permute-start.31 = (bf16[64,2048]{1,0:T(8,128)(2,1)S(1)}, bf16[64,2048]{1,0:T(8,128)(2,1)S(1)}, u32[]{:S(2)}, u32[]{:S(2)}) collective-permute-start(bf16[64,2048]{1,0:T(8,128)(2,1)S(1)} %add_convert_fusion.1), channel_id=1, source_target_pairs={{0,4},{1,5},{2,6},{3,7},{4,12},{5,13},{6,14},{7,15},{12,8},{13,9},... | collective-permute-start | bytes 786440 | tf_op jit(solution)/shard_map/ppermute | solution.py:55
  75.1 6.4 %collective-permute-start.30 = (bf16[64,2048]{1,0:T(8,128)(2,1)S(1)}, bf16[64,2048]{1,0:T(8,128)(2,1)S(1)}, u32[]{:S(2)}, u32[]{:S(2)}) collective-permute-start(bf16[64,2048]{1,0:T(8,128)(2,1)S(1)} %get-tuple-element.54), channel_id=1, source_target_pairs={{0,2},{1,3},{2,0},{3,1},{4,6},{5,7},{6,4},{7,5},{12,14},{13,15},{1... | collective-permute-start | bytes 786440 | tf_op jit(solution)/shard_map/ppermute | solution.py:63
